TPU v7x, 32 devices: a whole 2x2x4 slice. The times are simulated.
32 devices in a mesh: grp: 2 (over x), dev: 16 (over z, y, core).
Axes of the slice: x: 2, y: 2, z: 4, core: 2. Of those that a mesh axis runs over, the one named last changes fastest.
Arguments:
- pair_ft: bfloat16 [4096, 2, 1024], P('dev', None, 'grp'), may hold values from -6 to 6
- aux_ft: bfloat16 [4096, 2, 1024], P('dev', None, 'grp'), may hold values from -0.125 to 0.125
- coul_weight: float32 [1024], P('grp'), may hold values from 0.2 to 5
- aux_basis: bfloat16 [128, 4096], replicated, may hold values from -0.5 to 0.5
- aux_decay: float32 [4096], replicated, may hold values from 0.05 to 1
- image_dist: float32 [125], replicated, may hold values from 0 to 3
- image_phase: float32 [125], replicated, may hold values from -3.140625 to 3.140625
- item_pair: bfloat16 [512, 128, 128], P(('grp', 'dev')), may hold values from -4 to 4
- item_image: int32 [512], P(('grp', 'dev')), may hold values from 0 to 124
- item_sub: int32 [512], P(('grp', 'dev')), may hold values from 0 to 1
- item_count: int32 [32], P(('grp', 'dev')), may hold values from 0 to 16, as said below
Outputs:
- j3c: bfloat16 [4096, 2, 4096], P('grp', None, 'dev')
Inputs may be any that keep to these rules, and one draw needn't show every extreme that they name: `item_count`: in every index of dev one of the 2 devices holds exactly 16 live slots. The counts of the 2 devices that share an index of dev sum to at most 24, and in every draw some index of dev reaches 24.
All inputs are finite; a program needn't handle non-finite values.
Results may differ from a plain program's by a relative error of at most 0.0047.
Values may be sent and summed in bfloat16 or wider, within the bound.
No kernel may reach another device: no remote copies, remote signals or barrier semaphores. Data moves between devices by JAX's collectives and lax.ppermute only.
A program may use at most 64 MiB of HBM per device.

v0:
```python
import math

import jax
import jax.numpy as jnp
from jax import lax
from jax.sharding import PartitionSpec as P


def stacked_pairs(weighted):
    real_part = weighted[:, 0, :].T
    imag_part = weighted[:, 1, :].T
    real_cols = jnp.concatenate([real_part, imag_part], axis=0)
    imag_cols = jnp.concatenate([imag_part, -real_part], axis=0)
    return jnp.concatenate([real_cols, imag_cols], axis=1)


def short_range(
    aux_basis,
    aux_decay,
    image_dist,
    image_phase,
    first_row,
    row_count,
    blocks,
    images,
    sub_ids,
    usable,
    sub_count,
):
    basis_cols = lax.dynamic_slice_in_dim(aux_basis, first_row, row_count, 1)
    decay_rows = lax.dynamic_slice_in_dim(aux_decay, first_row, row_count, 0)
    products = jnp.einsum("kp,ikr->pir", basis_cols, blocks, preferred_element_type=jnp.float32)
    lookup = (images[:, None] == jnp.arange(image_dist.shape[0], dtype=jnp.int32)[None, :]).astype(
        jnp.float32
    )
    distance = jnp.dot(lookup, image_dist, precision=lax.Precision.HIGHEST)
    phase_value = jnp.dot(lookup, image_phase, precision=lax.Precision.HIGHEST)
    damping = jnp.exp(-decay_rows[:, None] * distance[None, :])
    factors = jnp.stack([jnp.cos(phase_value) * usable, jnp.sin(phase_value) * usable], axis=0)
    weights = damping[:, None, :] * factors[None, :, :]
    placing = (sub_ids[:, None] == jnp.arange(sub_count, dtype=jnp.int32)[None, :]).astype(
        jnp.float32
    )
    placed = jnp.einsum(
        "pir,pci,is->pcsr", products, weights, placing, precision=lax.Precision.HIGHEST
    )
    return placed.reshape(row_count, 2, sub_count * products.shape[2])


def body(
    pair_ft,
    aux_ft,
    coul_weight,
    aux_basis,
    aux_decay,
    image_dist,
    image_phase,
    item_pair,
    item_image,
    item_sub,
    item_count,
):
    group_count = lax.axis_size("grp")
    member_count = lax.axis_size("dev")
    capacity = item_image.shape[0]
    local_rows = pair_ft.shape[0]
    sub_rows = item_pair.shape[2]
    sub_count = local_rows // sub_rows
    aux_share = aux_ft.shape[0] * member_count // group_count
    weighted = (pair_ft.astype(jnp.float32) * coul_weight[None, None, :]).astype(jnp.bfloat16)

    def make_term(factors, factor_offset, pair_matrix, blocks, images, sub_ids, usable):

        def term_rows(first_row, row_count):
            block_rows = math.gcd(row_count, 512)

            def one_block(block_index):
                block_start = block_index * block_rows
                local_factors = lax.dynamic_slice_in_dim(
                    factors, block_start - factor_offset, block_rows, 0
                )
                factor_rows = local_factors.reshape(block_rows, -1)
                long_part = jnp.dot(factor_rows, pair_matrix, preferred_element_type=jnp.float32)
                long_part = long_part.reshape(block_rows, 2, local_rows)
                return long_part + short_range(
                    aux_basis,
                    aux_decay,
                    image_dist,
                    image_phase,
                    block_start,
                    block_rows,
                    blocks,
                    images,
                    sub_ids,
                    usable,
                    sub_count,
                )

            pieces = lax.map(one_block, jnp.arange(row_count // block_rows, dtype=jnp.int32))
            return pieces.reshape(row_count, 2, local_rows)

        return term_rows

    gathered = lax.all_gather(aux_ft, "dev", axis=0, tiled=True)
    blocks = item_pair
    images = item_image
    sub_ids = item_sub
    usable = jnp.arange(capacity, dtype=jnp.int32) < item_count[0]
    term_rows = make_term(
        gathered, 0, stacked_pairs(weighted), blocks, images, sub_ids, usable.astype(jnp.float32)
    )
    summed = lax.psum_scatter(
        term_rows(jnp.int32(0), aux_share * lax.axis_size("grp")),
        "grp",
        scatter_dimension=0,
        tiled=True,
    )
    return summed.astype(jnp.bfloat16)


def solution(mesh):
    return jax.shard_map(
        body,
        mesh=mesh,
        in_specs=(
            P("dev", None, "grp"),
            P("dev", None, "grp"),
            P("grp"),
            P(),
            P(),
            P(),
            P(),
            P(("grp", "dev"), None, None),
            P(("grp", "dev")),
            P(("grp", "dev")),
            P(("grp", "dev")),
        ),
        out_specs=P("grp", None, "dev"),
        check_vma=False,
    )
```

profile of v0, /device:TPU:0, one launch (start us, length us, event | category | flops | bytes accessed | tf_op | source)
XLA Modules:
  0.0 455.4 jit_solution(14320613396010505270)
XLA Ops:
  13.8 73.3 %all-gather.2.cloned.1.call-done = bf16[4096,2,512]{2,1,0:T(2,128)(2,1)} async-done(((bf16[256,2,512]{2,1,0:T(2,128)(2,1)}), bf16[4096,2,512]{2,1,0:T(2,128)(2,1)}) %all-gather.2.cloned.1.call-update) | async-done | bytes 8388624 | tf_op jit(solution)/shard_map/all_gather | solution.py:104
  87.2 161.1 %while.14 = (s32[]{:T(128)}, f32[8,512,2,256]{3,2,1,0:T(2,128)}, s32[8]{0:T(128)S(1)}, bf16[4096,2,512]{2,1,0:T(2,128)(2,1)}, bf16[1024,512]{0,1:T(8,128)(2,1)},...) while((s32[]{:T(128)}, f32[8,512,2,256]{3,2,1,0:T(2,128)}, ...), condition=%wide.region_1.2_spmd, body=%wide.region_0.1_spmd.sunk | while | flops 855958080 | bytes 25042132 | solution.py:99
  91.3 8.0 %fusion.38 = f32[512,2,2,128]{3,1,2,0:T(2,128)S(1)} fusion(f32[512,16,128,1]{2,0,1,3:T(8,128)S(1)} %convolution_bitcast_fusion.4, f32[16,512,2]{0,2,1:T(2,128)S(1)} %multiply_bitcast_fusion.2, f32[16,2]{0,1:T(2,128)S(1)} %compare_convert_fusion.2), kind=kOutput, calls=%fused_computation.3.clone.1 | convolution fusion | flops 50364416 | bytes 5308544 | tf_op jit(solution)/shard_map/while/body/eval_jaxpr/pir,pci,is->pcsr/dot_general | solution.py:44
  100.8 2.0 constant_dynamic-slice_fusion.2
  103.5 2.0 fusion.39
  111.5 8.0 %fusion.38 = f32[512,2,2,128]{3,1,2,0:T(2,128)S(1)} fusion(f32[512,16,128,1]{2,0,1,3:T(8,128)S(1)} %convolution_bitcast_fusion.4, f32[16,512,2]{0,2,1:T(2,128)S(1)} %multiply_bitcast_fusion.2, f32[16,2]{0,1:T(2,128)S(1)} %compare_convert_fusion.2), kind=kOutput, calls=%fused_computation.3.clone.1 | convolution fusion | flops 50364416 | bytes 5308544 | tf_op jit(solution)/shard_map/while/body/eval_jaxpr/pir,pci,is->pcsr/dot_general | solution.py:44
  121.0 2.0 constant_dynamic-slice_fusion.2
  123.7 2.0 fusion.39
  131.6 8.0 %fusion.38 = f32[512,2,2,128]{3,1,2,0:T(2,128)S(1)} fusion(f32[512,16,128,1]{2,0,1,3:T(8,128)S(1)} %convolution_bitcast_fusion.4, f32[16,512,2]{0,2,1:T(2,128)S(1)} %multiply_bitcast_fusion.2, f32[16,2]{0,1:T(2,128)S(1)} %compare_convert_fusion.2), kind=kOutput, calls=%fused_computation.3.clone.1 | convolution fusion | flops 50364416 | bytes 5308544 | tf_op jit(solution)/shard_map/while/body/eval_jaxpr/pir,pci,is->pcsr/dot_general | solution.py:44
  141.1 2.0 constant_dynamic-slice_fusion.2
  143.8 2.0 fusion.39
  151.7 8.0 %fusion.38 = f32[512,2,2,128]{3,1,2,0:T(2,128)S(1)} fusion(f32[512,16,128,1]{2,0,1,3:T(8,128)S(1)} %convolution_bitcast_fusion.4, f32[16,512,2]{0,2,1:T(2,128)S(1)} %multiply_bitcast_fusion.2, f32[16,2]{0,1:T(2,128)S(1)} %compare_convert_fusion.2), kind=kOutput, calls=%fused_computation.3.clone.1 | convolution fusion | flops 50364416 | bytes 5308544 | tf_op jit(solution)/shard_map/while/body/eval_jaxpr/pir,pci,is->pcsr/dot_general | solution.py:44
  161.2 2.0 constant_dynamic-slice_fusion.2
  163.9 2.0 fusion.39
  171.9 8.0 %fusion.38 = f32[512,2,2,128]{3,1,2,0:T(2,128)S(1)} fusion(f32[512,16,128,1]{2,0,1,3:T(8,128)S(1)} %convolution_bitcast_fusion.4, f32[16,512,2]{0,2,1:T(2,128)S(1)} %multiply_bitcast_fusion.2, f32[16,2]{0,1:T(2,128)S(1)} %compare_convert_fusion.2), kind=kOutput, calls=%fused_computation.3.clone.1 | convolution fusion | flops 50364416 | bytes 5308544 | tf_op jit(solution)/shard_map/while/body/eval_jaxpr/pir,pci,is->pcsr/dot_general | solution.py:44
  184.0 2.0 fusion.39
  192.0 8.0 %fusion.38 = f32[512,2,2,128]{3,1,2,0:T(2,128)S(1)} fusion(f32[512,16,128,1]{2,0,1,3:T(8,128)S(1)} %convolution_bitcast_fusion.4, f32[16,512,2]{0,2,1:T(2,128)S(1)} %multiply_bitcast_fusion.2, f32[16,2]{0,1:T(2,128)S(1)} %compare_convert_fusion.2), kind=kOutput, calls=%fused_computation.3.clone.1 | convolution fusion | flops 50364416 | bytes 5308544 | tf_op jit(solution)/shard_map/while/body/eval_jaxpr/pir,pci,is->pcsr/dot_general | solution.py:44
  204.2 2.0 fusion.39
  212.1 8.0 %fusion.38 = f32[512,2,2,128]{3,1,2,0:T(2,128)S(1)} fusion(f32[512,16,128,1]{2,0,1,3:T(8,128)S(1)} %convolution_bitcast_fusion.4, f32[16,512,2]{0,2,1:T(2,128)S(1)} %multiply_bitcast_fusion.2, f32[16,2]{0,1:T(2,128)S(1)} %compare_convert_fusion.2), kind=kOutput, calls=%fused_computation.3.clone.1 | convolution fusion | flops 50364416 | bytes 5308544 | tf_op jit(solution)/shard_map/while/body/eval_jaxpr/pir,pci,is->pcsr/dot_general | solution.py:44
  224.3 2.0 fusion.39
  232.3 8.0 %fusion.38 = f32[512,2,2,128]{3,1,2,0:T(2,128)S(1)} fusion(f32[512,16,128,1]{2,0,1,3:T(8,128)S(1)} %convolution_bitcast_fusion.4, f32[16,512,2]{0,2,1:T(2,128)S(1)} %multiply_bitcast_fusion.2, f32[16,2]{0,1:T(2,128)S(1)} %compare_convert_fusion.2), kind=kOutput, calls=%fused_computation.3.clone.1 | convolution fusion | flops 50364416 | bytes 5308544 | tf_op jit(solution)/shard_map/while/body/eval_jaxpr/pir,pci,is->pcsr/dot_general | solution.py:44
  244.4 2.0 fusion.39
  248.2 196.0 %all-reduce.2 = bf16[4096,2,256]{2,1,0:T(2,128)(2,1)} all-reduce(f32[4096,2,256]{2,1,0:T(2,128)} %bitcast.74), channel_id=2, replica_groups=mesh['grp'=2,'dev'=16] {'grp'}, use_global_device_ids=true, to_apply=%region_2.3.clone | all-reduce | flops 2097152 | bytes 12582912
  444.2 4.4 dynamic-slice_convert_fusion
  (108 shorter events, 74.1 us)
Async XLA Ops:
  6.5 3.2 copy-start
  6.5 80.6 %copy-start.1 = (s32[16]{0:T(128)S(1)}, s32[16]{0:T(128)}, u32[]{:S(2)}) copy-start(s32[16]{0:T(128)} %param.22) | copy-start | bytes 196
  6.5 80.6 %all-gather.2.cloned.1.call-start = ((), (), s32[]{:S(2)}) async-start(), calls=%async_computation | async-start | bytes 8912896 | tf_op jit(solution)/shard_map/all_gather | solution.py:104
Sparse Core Ops, SparseCore 0:
  9.5 77.5 all-gather.1
where the time goes:
time: 457 us; the launch traced here: 455 us
  blocking collectives  196 us (43%)
  matrix products  96.5 us (21%)
  waiting for transfers between devices  74.1 us (16%)
  local copies, waits for them, and re-layouts  58.6 us (13%)
  between operations  14.7 us (3%)
  other arithmetic  10.5 us (2%)
  loops' own time  5.18 us (1%)
    unnamed x1, blocking collectives  196 us
    all_gather x1, waiting for transfers between devices, body(): gathered = lax.all_gather(aux_ft, 'dev', axis=0, tiled=True)  73.3 us
    dot_general x8, matrix products, short_range(): jnp.einsum('pir,pci,is->pcsr', products, weights, placing, precision=lax....  64.2 us
    dot_general x8, matrix products, one_block(): jnp.dot(factor_rows, pair_matrix, preferred_element_type=jnp.float32)  15.8 us
    dynamic_slice x8, local copies, waits for them, and re-layouts, one_block(): lax.dynamic_slice_in_dim(factors, block_start - factor_offset, block_rows...  15.6 us
    dot_general x8, matrix products, short_range(): jnp.einsum('kp,ikr->pir', basis_cols, blocks, preferred_element_type=jnp....  14.8 us
    dynamic_update_slice x8, local copies, waits for them, and re-layouts, term_rows(): lax.map(one_block, jnp.arange(row_count // block_rows, dtype=jnp.int32))  14.5 us
  transfers between devices with their start and end apart: 1, of which 1 were waited for; matrix products, arithmetic and copies ran while one was open for 1% of the time, Pallas kernels for 0%

commit v1 on v0

v1 whole, which is shorter than its diff:
```python
import functools

import jax
import jax.numpy as jnp
from jax import lax
from jax.experimental import pallas as pl
from jax.experimental.pallas import tpu as pltpu
from jax.sharding import PartitionSpec as P

AXES = ("grp", "dev")
CORES = 2
GROUP_ITEMS = 4
VMEM_BYTES = 48 * 1024 * 1024


def short_kernel(
    half_ref, live_ref, sub_ref, meta_ref, basis_ref, decay_ref, items_ref, out_ref,
    basis_f32, left, acc, dists, group_sub, cursor, *, slots, subs, depth, width,
):
    step = pl.program_id(0)

    @pl.when(step == 0)
    def _():
        left[...] = jnp.zeros_like(left)
        for s in range(subs):
            cursor[s] = 0

        def count(i, carry):
            cursor[sub_ref[i]] = cursor[sub_ref[i]] + live_ref[i]
            return carry

        lax.fori_loop(0, slots, count, 0)
        first = jnp.int32(0)
        for s in range(subs):
            groups = (cursor[s] + GROUP_ITEMS - 1) // GROUP_ITEMS

            def mark(i, carry, s=s):
                group_sub[i] = s
                return carry

            lax.fori_loop(first, first + groups, mark, 0)
            cursor[s] = first * GROUP_ITEMS
            first = first + groups
        cursor[subs] = first

        def clear(i, carry):
            dists[i] = 0.0
            return carry

        lax.fori_loop(0, first * GROUP_ITEMS, clear, 0)

        def place(i, carry):
            @pl.when(live_ref[i] > 0)
            def _():
                s = sub_ref[i]
                at = cursor[s]
                cursor[s] = at + 1
                dists[at] = meta_ref[0, i]
                turned = items_ref[i].astype(jnp.float32).T
                lanes = pl.ds(pl.multiple_of((at % GROUP_ITEMS) * depth, depth), depth)
                left[at // GROUP_ITEMS, 0:width, lanes] = (turned * meta_ref[1, i]).astype(left.dtype)
                left[at // GROUP_ITEMS, width:, lanes] = (turned * meta_ref[2, i]).astype(left.dtype)

            return carry

        lax.fori_loop(0, slots, place, 0)

    basis_f32[...] = basis_ref[...].astype(jnp.float32)
    acc[...] = jnp.zeros_like(acc)
    decay = decay_ref[...]

    def one_group(group, carry):
        parts = []
        for k in range(GROUP_ITEMS):
            damping = jnp.exp(decay * -dists[group * GROUP_ITEMS + k])
            parts.append((basis_f32[...] * damping).astype(jnp.bfloat16))
        right = jnp.concatenate(parts, axis=0)
        s = group_sub[group]
        acc[s] += jnp.dot(left[group], right, preferred_element_type=jnp.float32)
        return carry

    lax.fori_loop(0, cursor[subs], one_group, 0)
    for s in range(subs):
        for c in range(2):
            column = (c * subs + s) * width
            out_ref[:, column : column + width] = acc[s, c * width : (c + 1) * width, :].T


def short_range(half, live, sub_ids, meta, aux_basis, aux_decay, items, row_count, subs):
    slots, depth, width = items.shape
    tile = min(row_count, 512)
    steps = row_count // tile
    groups = slots // GROUP_ITEMS + subs
    kernel = functools.partial(short_kernel, slots=slots, subs=subs, depth=depth, width=width)
    return pl.pallas_call(
        kernel,
        out_shape=jax.ShapeDtypeStruct((row_count, 2 * subs * width), jnp.float32),
        grid_spec=pltpu.PrefetchScalarGridSpec(
            num_scalar_prefetch=4,
            grid=(steps,),
            in_specs=[
                pl.BlockSpec((depth, tile), lambda t, half, *_: (0, half[0] * steps + t)),
                pl.BlockSpec((1, tile), lambda t, half, *_: (0, half[0] * steps + t)),
                pl.BlockSpec((slots, depth, width), lambda t, *_: (0, 0, 0)),
            ],
            out_specs=pl.BlockSpec((tile, 2 * subs * width), lambda t, *_: (t, 0)),
            scratch_shapes=[
                pltpu.VMEM((depth, tile), jnp.float32),
                pltpu.VMEM((groups, 2 * width, GROUP_ITEMS * depth), jnp.bfloat16),
                pltpu.VMEM((subs, 2 * width, tile), jnp.float32),
                pltpu.SMEM((groups * GROUP_ITEMS,), jnp.float32),
                pltpu.SMEM((groups,), jnp.int32),
                pltpu.SMEM((subs + 1,), jnp.int32),
            ],
        ),
        compiler_params=pltpu.CompilerParams(vmem_limit_bytes=VMEM_BYTES),
        cost_estimate=pl.CostEstimate(
            flops=2 * row_count * slots * depth * width * 2,
            bytes_accessed=row_count * 2 * subs * width * 4 + slots * depth * width * 2,
            transcendentals=0,
        ),
        name="short_range",
    )(half, live, sub_ids, meta, aux_basis, aux_decay.reshape(1, -1), items)


def long_kernel(place_ref, *refs, chains, pieces, rows, depth):
    names = []
    at = 0
    for count in chains:
        names.append(refs[at : at + count])
        at += count
    factors = refs[at : at + pieces * len(chains)]
    at += pieces * len(chains)
    outs = refs[at : at + pieces]
    at += pieces
    block, left, right, block_sem, right_sem = refs[at:]
    for chain, candidates in enumerate(names):
        for k, ref in enumerate(candidates):

            @pl.when(place_ref[0] == k)
            def _(ref=ref, chain=chain):
                pltpu.make_async_copy(ref, block.at[chain], block_sem.at[chain]).start()

    for n, ref in enumerate(factors):
        pltpu.make_async_copy(ref, right.at[n], right_sem.at[n]).start()
    half = depth // 2
    for chain, candidates in enumerate(names):
        pltpu.make_async_copy(candidates[0], block.at[chain], block_sem.at[chain]).wait()
        left[chain, 0:rows, :] = block[chain]
        left[chain, rows:, 0:half] = -block[chain, :, half:]
        left[chain, rows:, half:] = block[chain, :, 0:half]
    for piece in range(pieces):
        total = None
        for chain in range(len(chains)):
            n = piece * len(chains) + chain
            pltpu.make_async_copy(factors[n], right.at[n], right_sem.at[n]).wait()
            part = jnp.dot(left[chain], right[n], preferred_element_type=jnp.float32)
            total = part if total is None else total + part
        width = total.shape[1]
        outs[piece][:, 0:width] = total[0:rows].astype(outs[piece].dtype)
        outs[piece][:, width:] = total[rows:].astype(outs[piece].dtype)


def long_range(place, chains, factors, out_dtypes):
    rows, depth = chains[0][0].shape
    width = factors[0][0].shape[1]
    pieces = len(factors)
    count = pieces * len(chains)
    blocks = [block for candidates in chains for block in candidates]
    flat = [factor for per_piece in factors for factor in per_piece]
    kernel = functools.partial(
        long_kernel, chains=[len(c) for c in chains], pieces=pieces, rows=rows, depth=depth
    )
    return pl.pallas_call(
        kernel,
        out_shape=[jax.ShapeDtypeStruct((rows, 2 * width), dtype) for dtype in out_dtypes],
        in_specs=[pl.BlockSpec(memory_space=pltpu.SMEM)]
        + [pl.BlockSpec(memory_space=pl.ANY)] * (len(blocks) + len(flat)),
        out_specs=[pl.BlockSpec(memory_space=pltpu.VMEM)] * pieces,
        scratch_shapes=[
            pltpu.VMEM((len(chains), rows, depth), jnp.bfloat16),
            pltpu.VMEM((len(chains), 2 * rows, depth), jnp.bfloat16),
            pltpu.VMEM((count, depth, width), jnp.bfloat16),
            pltpu.SemaphoreType.DMA((len(chains),)),
            pltpu.SemaphoreType.DMA((count,)),
        ],
        compiler_params=pltpu.CompilerParams(vmem_limit_bytes=VMEM_BYTES),
        cost_estimate=pl.CostEstimate(
            flops=2 * 2 * rows * depth * width * count,
            bytes_accessed=2 * (count * depth * width + len(chains) * rows * depth + pieces * rows * 2 * width),
            transcendentals=0,
        ),
        name="long_range",
    )(place, *blocks, *flat)


def final_kernel(offset_ref, *refs, pieces, rows):
    short_ref = refs[pieces]
    out_ref = refs[pieces + 1]
    for n in range(pieces):
        window = pl.ds(pl.multiple_of(offset_ref[n], rows), rows)
        total = (refs[n][...].astype(jnp.float32) + short_ref[window, :]).astype(out_ref.dtype)
        width = total.shape[1] // 2
        out_ref[window, 0, :] = total[:, 0:width]
        out_ref[window, 1, :] = total[:, width:]


def final_sum(offsets, pieces, short):
    rows, columns = pieces[0].shape
    row_count = short.shape[0]
    return pl.pallas_call(
        functools.partial(final_kernel, pieces=len(pieces), rows=rows),
        out_shape=jax.ShapeDtypeStruct((row_count, 2, columns // 2), jnp.bfloat16),
        in_specs=[pl.BlockSpec(memory_space=pltpu.SMEM)]
        + [pl.BlockSpec(memory_space=pltpu.VMEM)] * (len(pieces) + 1),
        out_specs=pl.BlockSpec(memory_space=pltpu.VMEM),
        compiler_params=pltpu.CompilerParams(vmem_limit_bytes=VMEM_BYTES),
        cost_estimate=pl.CostEstimate(
            flops=row_count * columns, bytes_accessed=row_count * columns * 8, transcendentals=0
        ),
        name="final_sum",
    )(offsets, *pieces, short)


def slot_table(image_dist, image_phase, item_image, item_sub, item_count):
    chosen = item_image[None, :] == jnp.arange(image_dist.shape[0], dtype=jnp.int32)[:, None]
    distance = jnp.sum(jnp.where(chosen, image_dist[:, None], 0.0), axis=0)
    cosine = jnp.sum(jnp.where(chosen, jnp.cos(image_phase)[:, None], 0.0), axis=0)
    sine = jnp.sum(jnp.where(chosen, jnp.sin(image_phase)[:, None], 0.0), axis=0)
    live = jnp.arange(item_image.shape[0], dtype=jnp.int32) < item_count[0]
    return jnp.stack(
        [distance, cosine, sine, item_sub.astype(jnp.float32), live.astype(jnp.float32)]
    )


def split_table(table):
    return table[4].astype(jnp.int32), table[3].astype(jnp.int32), table[0:3]


def body(
    pair_ft,
    aux_ft,
    coul_weight,
    aux_basis,
    aux_decay,
    image_dist,
    image_phase,
    item_pair,
    item_image,
    item_sub,
    item_count,
):
    group_count = lax.axis_size("grp")
    member_count = lax.axis_size("dev")
    group = lax.axis_index("grp")
    member = lax.axis_index("dev")
    local_rows, _, local_g = pair_ft.shape
    subs = local_rows // item_pair.shape[2]
    rows = aux_ft.shape[0]
    row_count = rows * member_count // group_count
    half = jnp.reshape(group, (1,)).astype(jnp.int32)

    chips = member_count // CORES
    breadth = max(n for n in range(1, chips + 1) if chips % n == 0 and n * n <= chips)
    length = chips // breadth

    aux_flat = aux_ft.reshape(rows, 2 * local_g)
    weighted = (pair_ft.astype(jnp.float32) * coul_weight[None, None, :]).astype(jnp.bfloat16)
    turned = weighted.reshape(local_rows, 2 * local_g).T
    table = slot_table(image_dist, image_phase, item_image, item_sub, item_count)

    if group_count != 2 or length % 2:
        everything = lax.all_gather(aux_flat, "dev", axis=0, tiled=True)
        mine = lax.all_to_all(everything, "grp", split_axis=0, concat_axis=1, tiled=True)
        factor = lax.all_gather(turned, "grp", axis=0, tiled=True)
        parts = factor.reshape(group_count, 2, local_g, local_rows)
        other = jnp.stack([parts[:, 1], -parts[:, 0]], axis=1).reshape(factor.shape)
        long_part = jnp.concatenate(
            [
                jnp.dot(mine, factor, preferred_element_type=jnp.float32),
                jnp.dot(mine, other, preferred_element_type=jnp.float32),
            ],
            axis=1,
        )
        items = lax.all_gather(item_pair, "grp", axis=0, tiled=True)
        live, sub_ids, meta = split_table(lax.all_gather(table, "grp", axis=1, tiled=True))
        short = short_range(
            half, live, sub_ids, meta, aux_basis, aux_decay, items, row_count, subs
        )
        return (long_part + short).astype(jnp.bfloat16).reshape(row_count, 2, local_rows)

    home = length // 2
    up = member // (breadth * CORES)
    across = member // CORES % breadth
    core = member % CORES
    logical = jnp.where(group == 0, up, length - 1 - up)

    def send(value, route):
        def index(g, u, y, c):
            z = u if g == 0 else length - 1 - u
            return g * member_count + (z * breadth + y) * CORES + c

        pairs = []
        for g in range(group_count):
            for u in range(length):
                for y in range(breadth):
                    for c in range(CORES):
                        target = route(g, u, y, c)
                        if target is not None:
                            pairs.append((index(g, u, y, c), index(*target)))
        return lax.ppermute(value, AXES, pairs)

    def mirrored(g, u, y, c):
        return 1 - g, length - 1 - u, y, c

    crossed = send(aux_flat, lambda g, u, y, c: mirrored(g, u, y, c) if u >= home else None)

    def chain_of(head):
        rising = {0: head}
        for s in range(1, length):
            rising[s] = send(
                rising[s - 1],
                lambda g, u, y, c, s=s: (g, u + 1, y, c)
                if u + 1 < length and 0 <= u - (s - 1) < home
                else None,
            )
        falling = {0: head}
        for s in range(1, home):
            falling[s] = send(
                falling[s - 1],
                lambda g, u, y, c, s=s: (g, u - 1, y, c)
                if u >= 1 and u + s - 1 < home
                else None,
            )
        return [
            [rising[u - j] if u >= j else falling[j - u] for u in range(length)]
            for j in range(home)
        ]

    turned_x = send(turned, mirrored)
    items_x = send(item_pair, mirrored)
    table_x = send(table, mirrored)
    chains = [chain_of(aux_flat), chain_of(crossed)]

    factors = []
    partners = [(s, t) for s in range(breadth) for t in range(CORES)]
    over_y = {0: [turned, turned_x]}
    for s in range(1, breadth):
        over_y[s] = [
            send(v, lambda g, u, y, c, s=s: (g, u, (y - s) % breadth, c)) for v in over_y[0]
        ]
    for s, t in partners:
        if t == 0:
            factors.append(over_y[s])
        else:
            factors.append(
                [send(v, lambda g, u, y, c, t=t: (g, u, y, (c - t) % CORES)) for v in over_y[s]]
            )

    live, sub_ids, meta = split_table(jnp.concatenate([table, table_x], axis=1))
    items = jnp.concatenate([item_pair, items_x], axis=0)
    short = short_range(half, live, sub_ids, meta, aux_basis, aux_decay, items, row_count, subs)

    place = jnp.reshape(logical, (1,)).astype(jnp.int32)
    results = []
    offsets = []
    for j in reversed(range(home)):
        made = long_range(
            place,
            [chain[j] for chain in chains],
            factors,
            [jnp.float32 if n == 0 else jnp.bfloat16 for n in range(len(partners))],
        )
        slab = jnp.where(group == 0, j, home - 1 - j)
        for (s, t), piece in zip(partners, made):
            if (s, t) != (0, 0):
                piece = send(
                    piece,
                    lambda g, u, y, c, s=s, t=t: (g, u, (y + s) % breadth, (c + t) % CORES),
                )
            results.append(piece)
            offsets.append(
                ((slab * breadth + (across - s) % breadth) * CORES + (core - t) % CORES) * rows
            )
    return final_sum(jnp.stack(offsets).astype(jnp.int32), results, short)


def solution(mesh):
    return jax.shard_map(
        body,
        mesh=mesh,
        in_specs=(
            P("dev", None, "grp"),
            P("dev", None, "grp"),
            P("grp"),
            P(),
            P(),
            P(),
            P(),
            P(("grp", "dev"), None, None),
            P(("grp", "dev")),
            P(("grp", "dev")),
            P(("grp", "dev")),
        ),
        out_specs=P("grp", None, "dev"),
        check_vma=False,
    )
```

time: 457 us -> 122 us (0.27)
  the two profiles are of different devices: /device:TPU:0 before, /device:TPU:2 now
where the time goes in v1:
time: 122 us; the launch traced here: 120 us
  waiting for transfers between devices  51.5 us (42%)
  Pallas kernels  34.7 us (28%)
  starting transfers between devices  25.6 us (21%)
  local copies, waits for them, and re-layouts  4.3 us (4%)
  other arithmetic  3.19 us (3%)
    ppermute x24, waiting for transfers between devices, send(): return lax.ppermute(value, AXES, pairs)  51.5 us
    ppermute x24, starting transfers between devices, send(): return lax.ppermute(value, AXES, pairs)  25.6 us
    pallas_call x1, Pallas kernels, short_range(): pl.pallas_call(kernel, out_shape=jax.ShapeDtypeStruct((row_count, 2 * sub...  14 us
    pallas_call x2, Pallas kernels, long_range(): pl.pallas_call(kernel, out_shape=[jax.ShapeDtypeStruct((rows, 2 * width),...  12.9 us
    pallas_call x1, Pallas kernels, final_sum(): pl.pallas_call(functools.partial(final_kernel, pieces=len(pieces), rows=r...  7.84 us
    unnamed x13, local copies, waits for them, and re-layouts  2.95 us
  transfers between devices with their start and end apart: 24, of which 7 were waited for; matrix products, arithmetic and copies ran while one was open for 4% of the time, Pallas kernels for 22%

profile of v1, /device:TPU:2, one launch (start us, length us, event | category | flops | bytes accessed | tf_op | source)
XLA Modules:
  0.0 120.2 jit_solution(10146730121388081961)
XLA Ops:
  0.0 1.1 copy.14
  2.5 5.9 %collective-permute-start.3 = (bf16[256,1024]{1,0:T(8,128)(2,1)S(1)}, bf16[256,1024]{1,0:T(8,128)(2,1)S(1)}, u32[]{:S(2)}, u32[]{:S(2)}) collective-permute-start(bf16[256,1024]{1,0:T(8,128)(2,1)S(1)} %bitcast.29), channel_id=1, source_target_pairs={{8,24},{9,25},{10,26},{11,27},{12,28},{13,29},{14,30},{15,31},{20,... | collective-permute-start | bytes 1572872 | tf_op jit(solution)/shard_map/ppermute | solution.py:311
  8.4 1.5 %multiply_convert_fusion = bf16[256,2,512]{2,1,0:T(2,128)(2,1)S(1)} fusion(bf16[256,2,512]{2,1,0:T(2,128)(2,1)} %param.11, f32[512]{0:T(512)} %param.13), kind=kLoop, calls=%fused_computation.1 | loop fusion | flops 786432 | bytes 1050624 | tf_op jit(solution)/shard_map/convert_element_type | solution.py:268
  13.5 2.1 %collective-permute-start.22 = (f32[5,16]{1,0:T(8,128)S(1)}, f32[5,16]{1,0:T(8,128)S(1)}, u32[]{:S(2)}, u32[]{:S(2)}) collective-permute-start(f32[5,16]{1,0:T(8,128)S(1)} %stack.56), channel_id=1, source_target_pairs={{0,16},{1,17},{2,18},{3,19},{4,20},{5,21},{6,22},{7,23},{8,24},{9,... | collective-permute-start | bytes 968 | tf_op jit(solution)/shard_map/ppermute | solution.py:311
  15.5 15.1 %collective-permute-done.22 = f32[5,16]{1,0:T(8,128)S(1)} collective-permute-done((f32[5,16]{1,0:T(8,128)S(1)}, f32[5,16]{1,0:T(8,128)S(1)}, u32[]{:S(2)}, u32[]{:S(2)}) %collective-permute-start.22) | collective-permute-done | bytes 352 | tf_op jit(solution)/shard_map/ppermute | solution.py:311
  31.4 2.3 %collective-permute-start.10 = (bf16[1024,256]{1,0:T(8,128)(2,1)S(1)}, bf16[1024,256]{1,0:T(8,128)(2,1)}, u32[]{:S(2)}, u32[]{:S(2)}) collective-permute-start(bf16[1024,256]{1,0:T(8,128)(2,1)S(1)} %bitcast.34), channel_id=1, source_target_pairs={{0,2},{1,3},{2,0},{3,1},{4,6},{5,7},{6,4},{7,5},{8,10},{9,11},{10,... | collective-permute-start | bytes 1572872 | tf_op jit(solution)/shard_map/ppermute | solution.py:311
  34.4 1.3 %collective-permute-start.2 = (bf16[256,1024]{1,0:T(8,128)(2,1)S(1)}, bf16[256,1024]{1,0:T(8,128)(2,1)S(1)}, u32[]{:S(2)}, u32[]{:S(2)}) collective-permute-start(bf16[256,1024]{1,0:T(8,128)(2,1)S(1)} %collective-permute-done.1.refs_2_.refs_1_), channel_id=1, source_target_pairs={{4,8},{5,9},{6,10},{7,11},{8,12},{9,13},{10,14},{11,15},{24,20},{2... | collective-permute-start | bytes 1572872 | tf_op jit(solution)/shard_map/ppermute | solution.py:311
  35.8 1.5 %collective-permute-start.4 = (bf16[256,1024]{1,0:T(8,128)(2,1)S(1)}, bf16[256,1024]{1,0:T(8,128)(2,1)}, u32[]{:S(2)}, u32[]{:S(2)}) collective-permute-start(bf16[256,1024]{1,0:T(8,128)(2,1)S(1)} %collective-permute-done.3.refs_5_.refs_4_), channel_id=1, source_target_pairs={{4,0},{5,1},{6,2},{7,3},{24,28},{25,29},{26,30},{27,31}} | collective-permute-start | bytes 1572872 | tf_op jit(solution)/shard_map/ppermute | solution.py:311
  37.3 9.3 %collective-permute-done.10.refs_12_ = bf16[1024,256]{1,0:T(8,128)(2,1)} collective-permute-done((bf16[1024,256]{1,0:T(8,128)(2,1)S(1)}, bf16[1024,256]{1,0:T(8,128)(2,1)}, u32[]{:S(2)}, u32[]{:S(2)}) %collective-permute-start.10) | collective-permute-done | bytes 524320 | tf_op jit(solution)/shard_map/ppermute | solution.py:311
  46.6 1.3 %collective-permute-start.6 = (bf16[256,1024]{1,0:T(8,128)(2,1)S(1)}, bf16[256,1024]{1,0:T(8,128)(2,1)}, u32[]{:S(2)}, u32[]{:S(2)}) collective-permute-start(bf16[256,1024]{1,0:T(8,128)(2,1)S(1)} %collective-permute-done.5.refs_6_.refs_5_), channel_id=1, source_target_pairs={{4,8},{5,9},{6,10},{7,11},{8,12},{9,13},{10,14},{11,15},{24,20},{2... | collective-permute-start | bytes 1572872 | tf_op jit(solution)/shard_map/ppermute | solution.py:311
  47.9 2.5 %collective-permute-done.2.refs_3_.refs_2_ = bf16[256,1024]{1,0:T(8,128)(2,1)S(1)} collective-permute-done((bf16[256,1024]{1,0:T(8,128)(2,1)S(1)}, bf16[256,1024]{1,0:T(8,128)(2,1)S(1)}, u32[]{:S(2)}, u32[]{:S(2)}) %collective-permute-start.2) | collective-permute-done | bytes 524320 | tf_op jit(solution)/shard_map/ppermute | solution.py:311
  50.4 7.3 %collective-permute-done.11.refs_13_ = bf16[1024,256]{1,0:T(8,128)(2,1)} collective-permute-done((bf16[1024,256]{1,0:T(8,128)(2,1)}, bf16[1024,256]{1,0:T(8,128)(2,1)}, u32[]{:S(2)}, u32[]{:S(2)}) %collective-permute-start.11) | collective-permute-done | bytes 524320 | tf_op jit(solution)/shard_map/ppermute | solution.py:311
  57.7 2.6 %collective-permute-start.23 = (bf16[16,128,128]{2,1,0:T(8,128)(2,1)}, bf16[16,128,128]{2,1,0:T(8,128)(2,1)S(1)}, u32[]{:S(2)}, u32[]{:S(2)}) collective-permute-start(bf16[16,128,128]{2,1,0:T(8,128)(2,1)} %param.18), channel_id=1, source_target_pairs={{0,16},{1,17},{2,18},{3,19},{4,20},{5,21},{6,22},{7,23},{8,24},{9,... | collective-permute-start | bytes 1572872 | tf_op jit(solution)/shard_map/ppermute | solution.py:311
  60.4 1.3 %collective-permute-start.17 = (bf16[256,1024]{1,0:T(8,128)(2,1)S(1)}, bf16[256,1024]{1,0:T(8,128)(2,1)S(1)}, u32[]{:S(2)}, u32[]{:S(2)}) collective-permute-start(bf16[256,1024]{1,0:T(8,128)(2,1)S(1)} %collective-permute-done.2.refs_3_.refs_2_), channel_id=1, source_target_pairs={{8,12},{9,13},{10,14},{11,15},{20,16},{21,17},{22,18},{23,19}} | collective-permute-start | bytes 1572872 | tf_op jit(solution)/shard_map/ppermute | solution.py:311
  61.7 5.1 %collective-permute-done.6.refs_7_.refs_6_ = bf16[256,1024]{1,0:T(8,128)(2,1)} collective-permute-done((bf16[256,1024]{1,0:T(8,128)(2,1)S(1)}, bf16[256,1024]{1,0:T(8,128)(2,1)}, u32[]{:S(2)}, u32[]{:S(2)}) %collective-permute-start.6) | collective-permute-done | bytes 524320 | tf_op jit(solution)/shard_map/ppermute | solution.py:311
  66.8 1.3 %collective-permute-start.18 = (bf16[256,1024]{1,0:T(8,128)(2,1)}, bf16[256,1024]{1,0:T(8,128)(2,1)S(1)}, u32[]{:S(2)}, u32[]{:S(2)}) collective-permute-start(bf16[256,1024]{1,0:T(8,128)(2,1)} %collective-permute-done.6.refs_7_.refs_6_), channel_id=1, source_target_pairs={{8,12},{9,13},{10,14},{11,15},{20,16},{21,17},{22,18},{23,19}} | collective-permute-start | bytes 1572872 | tf_op jit(solution)/shard_map/ppermute | solution.py:311
  69.2 6.4 %long_range.2 = (f32[256,512]{1,0:T(8,128)S(1)}, bf16[256,512]{1,0:T(8,128)(2,1)S(1)}, bf16[256,512]{1,0:T(8,128)(2,1)S(1)}, bf16[256,512]{1,0:T(8,128)(2,1)S(1)}) custom-call(s32[1]{0:T(128)} %bitcast.8.place_ref, bf16[256,1024]{1,0:T(8,128)(2,1)S(1)} %copy-done.1, bf16[256,1024]{1,0:T(8,128)(2,1)S(1)} %bitcast.30, ...), custom_call_target="tpu_custom_call" | custom-call | flops 2147483648 | bytes 6291456 | tf_op jit(solution)/shard_map/long_range/pallas_call | solution.py:174
  76.4 1.3 %collective-permute-start.16 = (bf16[256,512]{1,0:T(8,128)(2,1)S(1)}, bf16[256,512]{1,0:T(8,128)(2,1)S(1)}, u32[]{:S(2)}, u32[]{:S(2)}) collective-permute-start(bf16[256,512]{1,0:T(8,128)(2,1)S(1)} %get-tuple-element.16), channel_id=1, source_target_pairs={{0,3},{1,2},{2,1},{3,0},{4,7},{5,6},{6,5},{7,4},{8,11},{9,10},{10,... | collective-permute-start | bytes 786440 | tf_op jit(solution)/shard_map/ppermute | solution.py:311
  77.7 1.6 %collective-permute-done.17.refs_3_ = bf16[256,1024]{1,0:T(8,128)(2,1)S(1)} collective-permute-done((bf16[256,1024]{1,0:T(8,128)(2,1)S(1)}, bf16[256,1024]{1,0:T(8,128)(2,1)S(1)}, u32[]{:S(2)}, u32[]{:S(2)}) %collective-permute-start.17) | collective-permute-done | bytes 524320 | tf_op jit(solution)/shard_map/ppermute | solution.py:311
  79.3 10.7 %collective-permute-done.18.refs_7_ = bf16[256,1024]{1,0:T(8,128)(2,1)S(1)} collective-permute-done((bf16[256,1024]{1,0:T(8,128)(2,1)}, bf16[256,1024]{1,0:T(8,128)(2,1)S(1)}, u32[]{:S(2)}, u32[]{:S(2)}) %collective-permute-start.18) | collective-permute-done | bytes 524320 | tf_op jit(solution)/shard_map/ppermute | solution.py:311
  90.0 6.5 %long_range.3 = (f32[256,512]{1,0:T(8,128)S(1)}, bf16[256,512]{1,0:T(8,128)(2,1)S(1)}, bf16[256,512]{1,0:T(8,128)(2,1)S(1)}, bf16[256,512]{1,0:T(8,128)(2,1)S(1)}) custom-call(s32[1]{0:T(128)} %bitcast.8.place_ref, bf16[256,1024]{1,0:T(8,128)(2,1)S(1)} %bitcast.31, bf16[256,1024]{1,0:T(8,128)(2,1)S(1)} %collective-permute-done.1.refs_2_.refs_1_, ...), custom_call_target="tpu_custom_call" | custom-call | flops 2147483648 | bytes 6291456 | tf_op jit(solution)/shard_map/long_range/pallas_call | solution.py:174
  97.1 1.3 %collective-permute-start.21 = (bf16[256,512]{1,0:T(8,128)(2,1)S(1)}, bf16[256,512]{1,0:T(8,128)(2,1)S(1)}, u32[]{:S(2)}, u32[]{:S(2)}) collective-permute-start(bf16[256,512]{1,0:T(8,128)(2,1)S(1)} %get-tuple-element.20), channel_id=1, source_target_pairs={{0,3},{1,2},{2,1},{3,0},{4,7},{5,6},{6,5},{7,4},{8,11},{9,10},{10,... | collective-permute-start | bytes 786440 | tf_op jit(solution)/shard_map/ppermute | solution.py:311
  98.4 14.0 %short_range.1.refs_8_ = f32[2048,512]{1,0:T(8,128)} custom-call(s32[1]{0:T(128)} %bitcast.12.half_ref, s32[32]{0:T(128)S(1)} %get-tuple-element.25.live_ref, s32[32]{0:T(128)S(1)} %get-tuple-element.24.sub_ref, f32[3,32]{1,0:T(4,128)S(1)} %slice.11.meta_ref, bf16[128,4096]{1,0:T(8,128)(2,1)S(1)} %copy-done.2, f32[1,4096]{1,0:T(1,128)S(1)} %bitcast.37, ...), custom_call_target="tpu_custom_call" | custom-call | flops 4294967296 | bytes 5242880 | tf_op jit(solution)/shard_map/short_range/pallas_call | solution.py:95
  112.4 7.8 %final_sum.1 = bf16[2048,2,256]{2,1,0:T(2,128)(2,1)} custom-call(s32[8]{0:T(128)S(1)} %stack.51.offset_ref, f32[256,512]{1,0:T(8,128)S(1)} %get-tuple-element.13.refs_0_, bf16[256,512]{1,0:T(8,128)(2,1)S(1)} %collective-permute-done.14.refs_1_, bf16[256,512]{1,0:T(8,128)(2,1)S(1)} %collective-permute-done.15.refs_2_, ...), custom_call_target="tpu_custom_call" | custom-call | flops 1048576 | bytes 8388608 | tf_op jit(solution)/shard_map/final_sum/pallas_call | solution.py:211
  (53 shorter events, 8.5 us)
Async XLA Ops:
  1.1 29.5 %collective-permute-start = (bf16[256,1024]{1,0:T(8,128)(2,1)S(1)}, bf16[256,1024]{1,0:T(8,128)(2,1)S(1)}, u32[]{:S(2)}, u32[]{:S(2)}) collective-permute-start(bf16[256,1024]{1,0:T(8,128)(2,1)S(1)} %bitcast.27), channel_id=1, source_target_pairs={{4,0},{5,1},{6,2},{7,3},{24,28},{25,29},{26,30},{27,31}} | collective-permute-start | bytes 1572872 | tf_op jit(solution)/shard_map/ppermute | solution.py:311
  1.8 32.6 %collective-permute-start.1 = (bf16[256,1024]{1,0:T(8,128)(2,1)S(1)}, bf16[256,1024]{1,0:T(8,128)(2,1)S(1)}, u32[]{:S(2)}, u32[]{:S(2)}) collective-permute-start(bf16[256,1024]{1,0:T(8,128)(2,1)S(1)} %bitcast.28), channel_id=1, source_target_pairs={{0,4},{1,5},{2,6},{3,7},{4,8},{5,9},{6,10},{7,11},{28,24},{29,25},... | collective-permute-start | bytes 1572872 | tf_op jit(solution)/shard_map/ppermute | solution.py:311
  2.5 31.2 %collective-permute-start.3 = (bf16[256,1024]{1,0:T(8,128)(2,1)S(1)}, bf16[256,1024]{1,0:T(8,128)(2,1)S(1)}, u32[]{:S(2)}, u32[]{:S(2)}) collective-permute-start(bf16[256,1024]{1,0:T(8,128)(2,1)S(1)} %bitcast.29), channel_id=1, source_target_pairs={{8,24},{9,25},{10,26},{11,27},{12,28},{13,29},{14,30},{15,31},{20,... | collective-permute-start | bytes 1572872 | tf_op jit(solution)/shard_map/ppermute | solution.py:311
  10.5 25.3 %collective-permute-start.7 = (bf16[1024,256]{1,0:T(8,128)(2,1)S(1)}, bf16[1024,256]{1,0:T(8,128)(2,1)}, u32[]{:S(2)}, u32[]{:S(2)}) collective-permute-start(bf16[1024,256]{1,0:T(8,128)(2,1)S(1)} %bitcast.32), channel_id=1, source_target_pairs={{0,16},{1,17},{2,18},{3,19},{4,20},{5,21},{6,22},{7,23},{8,24},{9,... | collective-permute-start | bytes 1572872 | tf_op jit(solution)/shard_map/ppermute | solution.py:311
  13.5 17.1 %collective-permute-start.22 = (f32[5,16]{1,0:T(8,128)S(1)}, f32[5,16]{1,0:T(8,128)S(1)}, u32[]{:S(2)}, u32[]{:S(2)}) collective-permute-start(f32[5,16]{1,0:T(8,128)S(1)} %stack.56), channel_id=1, source_target_pairs={{0,16},{1,17},{2,18},{3,19},{4,20},{5,21},{6,22},{7,23},{8,24},{9,... | collective-permute-start | bytes 968 | tf_op jit(solution)/shard_map/ppermute | solution.py:311
  30.6 5.2 %collective-permute-start.8 = (bf16[1024,256]{1,0:T(8,128)(2,1)S(1)}, bf16[1024,256]{1,0:T(8,128)(2,1)S(1)}, u32[]{:S(2)}, u32[]{:S(2)}) collective-permute-start(bf16[1024,256]{1,0:T(8,128)(2,1)S(1)} %bitcast.33), channel_id=1, source_target_pairs={{0,1},{1,0},{2,3},{3,2},{4,5},{5,4},{6,7},{7,6},{8,9},{9,8},{10,11... | collective-permute-start | bytes 1572872 | tf_op jit(solution)/shard_map/ppermute | solution.py:311
  31.4 15.2 %collective-permute-start.10 = (bf16[1024,256]{1,0:T(8,128)(2,1)S(1)}, bf16[1024,256]{1,0:T(8,128)(2,1)}, u32[]{:S(2)}, u32[]{:S(2)}) collective-permute-start(bf16[1024,256]{1,0:T(8,128)(2,1)S(1)} %bitcast.34), channel_id=1, source_target_pairs={{0,2},{1,3},{2,0},{3,1},{4,6},{5,7},{6,4},{7,5},{8,10},{9,11},{10,... | collective-permute-start | bytes 1572872 | tf_op jit(solution)/shard_map/ppermute | solution.py:311
  33.7 12.9 %collective-permute-start.5 = (bf16[256,1024]{1,0:T(8,128)(2,1)S(1)}, bf16[256,1024]{1,0:T(8,128)(2,1)S(1)}, u32[]{:S(2)}, u32[]{:S(2)}) collective-permute-start(bf16[256,1024]{1,0:T(8,128)(2,1)S(1)} %collective-permute-done.3.refs_5_.refs_4_), channel_id=1, source_target_pairs={{0,4},{1,5},{2,6},{3,7},{4,8},{5,9},{6,10},{7,11},{28,24},{29,25},... | collective-permute-start | bytes 1572872 | tf_op jit(solution)/shard_map/ppermute | solution.py:311
  34.4 15.9 %collective-permute-start.2 = (bf16[256,1024]{1,0:T(8,128)(2,1)S(1)}, bf16[256,1024]{1,0:T(8,128)(2,1)S(1)}, u32[]{:S(2)}, u32[]{:S(2)}) collective-permute-start(bf16[256,1024]{1,0:T(8,128)(2,1)S(1)} %collective-permute-done.1.refs_2_.refs_1_), channel_id=1, source_target_pairs={{4,8},{5,9},{6,10},{7,11},{8,12},{9,13},{10,14},{11,15},{24,20},{2... | collective-permute-start | bytes 1572872 | tf_op jit(solution)/shard_map/ppermute | solution.py:311
  35.7 21.9 %collective-permute-start.11 = (bf16[1024,256]{1,0:T(8,128)(2,1)}, bf16[1024,256]{1,0:T(8,128)(2,1)}, u32[]{:S(2)}, u32[]{:S(2)}) collective-permute-start(bf16[1024,256]{1,0:T(8,128)(2,1)} %collective-permute-done.7.refs_9_), channel_id=1, source_target_pairs={{0,2},{1,3},{2,0},{3,1},{4,6},{5,7},{6,4},{7,5},{8,10},{9,11},{10,... | collective-permute-start | bytes 1572872 | tf_op jit(solution)/shard_map/ppermute | solution.py:311
  35.8 21.9 %collective-permute-start.4 = (bf16[256,1024]{1,0:T(8,128)(2,1)S(1)}, bf16[256,1024]{1,0:T(8,128)(2,1)}, u32[]{:S(2)}, u32[]{:S(2)}) collective-permute-start(bf16[256,1024]{1,0:T(8,128)(2,1)S(1)} %collective-permute-done.3.refs_5_.refs_4_), channel_id=1, source_target_pairs={{4,0},{5,1},{6,2},{7,3},{24,28},{25,29},{26,30},{27,31}} | collective-permute-start | bytes 1572872 | tf_op jit(solution)/shard_map/ppermute | solution.py:311
  46.6 13.8 %collective-permute-start.9 = (bf16[1024,256]{1,0:T(8,128)(2,1)}, bf16[1024,256]{1,0:T(8,128)(2,1)}, u32[]{:S(2)}, u32[]{:S(2)}) collective-permute-start(bf16[1024,256]{1,0:T(8,128)(2,1)} %collective-permute-done.7.refs_9_), channel_id=1, source_target_pairs={{0,1},{1,0},{2,3},{3,2},{4,5},{5,4},{6,7},{7,6},{8,9},{9,8},{10,11... | collective-permute-start | bytes 1572872 | tf_op jit(solution)/shard_map/ppermute | solution.py:311
  46.6 20.2 %collective-permute-start.6 = (bf16[256,1024]{1,0:T(8,128)(2,1)S(1)}, bf16[256,1024]{1,0:T(8,128)(2,1)}, u32[]{:S(2)}, u32[]{:S(2)}) collective-permute-start(bf16[256,1024]{1,0:T(8,128)(2,1)S(1)} %collective-permute-done.5.refs_6_.refs_5_), channel_id=1, source_target_pairs={{4,8},{5,9},{6,10},{7,11},{8,12},{9,13},{10,14},{11,15},{24,20},{2... | collective-permute-start | bytes 1572872 | tf_op jit(solution)/shard_map/ppermute | solution.py:311
  50.4 17.7 %collective-permute-start.12 = (bf16[1024,256]{1,0:T(8,128)(2,1)}, bf16[1024,256]{1,0:T(8,128)(2,1)}, u32[]{:S(2)}, u32[]{:S(2)}) collective-permute-start(bf16[1024,256]{1,0:T(8,128)(2,1)} %collective-permute-done.10.refs_12_), channel_id=1, source_target_pairs={{0,1},{1,0},{2,3},{3,2},{4,5},{5,4},{6,7},{7,6},{8,9},{9,8},{10,11... | collective-permute-start | bytes 1572872 | tf_op jit(solution)/shard_map/ppermute | solution.py:311
  57.7 10.5 %collective-permute-start.13 = (bf16[1024,256]{1,0:T(8,128)(2,1)}, bf16[1024,256]{1,0:T(8,128)(2,1)}, u32[]{:S(2)}, u32[]{:S(2)}) collective-permute-start(bf16[1024,256]{1,0:T(8,128)(2,1)} %collective-permute-done.11.refs_13_), channel_id=1, source_target_pairs={{0,1},{1,0},{2,3},{3,2},{4,5},{5,4},{6,7},{7,6},{8,9},{9,8},{10,11... | collective-permute-start | bytes 1572872 | tf_op jit(solution)/shard_map/ppermute | solution.py:311
  57.7 18.0 %collective-permute-start.23 = (bf16[16,128,128]{2,1,0:T(8,128)(2,1)}, bf16[16,128,128]{2,1,0:T(8,128)(2,1)S(1)}, u32[]{:S(2)}, u32[]{:S(2)}) collective-permute-start(bf16[16,128,128]{2,1,0:T(8,128)(2,1)} %param.18), channel_id=1, source_target_pairs={{0,16},{1,17},{2,18},{3,19},{4,20},{5,21},{6,22},{7,23},{8,24},{9,... | collective-permute-start | bytes 1572872 | tf_op jit(solution)/shard_map/ppermute | solution.py:311
  60.4 18.8 %collective-permute-start.17 = (bf16[256,1024]{1,0:T(8,128)(2,1)S(1)}, bf16[256,1024]{1,0:T(8,128)(2,1)S(1)}, u32[]{:S(2)}, u32[]{:S(2)}) collective-permute-start(bf16[256,1024]{1,0:T(8,128)(2,1)S(1)} %collective-permute-done.2.refs_3_.refs_2_), channel_id=1, source_target_pairs={{8,12},{9,13},{10,14},{11,15},{20,16},{21,17},{22,18},{23,19}} | collective-permute-start | bytes 1572872 | tf_op jit(solution)/shard_map/ppermute | solution.py:311
  66.8 23.1 %collective-permute-start.18 = (bf16[256,1024]{1,0:T(8,128)(2,1)}, bf16[256,1024]{1,0:T(8,128)(2,1)S(1)}, u32[]{:S(2)}, u32[]{:S(2)}) collective-permute-start(bf16[256,1024]{1,0:T(8,128)(2,1)} %collective-permute-done.6.refs_7_.refs_6_), channel_id=1, source_target_pairs={{8,12},{9,13},{10,14},{11,15},{20,16},{21,17},{22,18},{23,19}} | collective-permute-start | bytes 1572872 | tf_op jit(solution)/shard_map/ppermute | solution.py:311
  75.6 21.5 %collective-permute-start.14 = (bf16[256,512]{1,0:T(8,128)(2,1)S(1)}, bf16[256,512]{1,0:T(8,128)(2,1)S(1)}, u32[]{:S(2)}, u32[]{:S(2)}) collective-permute-start(bf16[256,512]{1,0:T(8,128)(2,1)S(1)} %get-tuple-element.14), channel_id=1, source_target_pairs={{0,1},{1,0},{2,3},{3,2},{4,5},{5,4},{6,7},{7,6},{8,9},{9,8},{10,11... | collective-permute-start | bytes 786440 | tf_op jit(solution)/shard_map/ppermute | solution.py:311
  75.8 36.5 %collective-permute-start.15 = (bf16[256,512]{1,0:T(8,128)(2,1)S(1)}, bf16[256,512]{1,0:T(8,128)(2,1)S(1)}, u32[]{:S(2)}, u32[]{:S(2)}) collective-permute-start(bf16[256,512]{1,0:T(8,128)(2,1)S(1)} %get-tuple-element.15), channel_id=1, source_target_pairs={{0,2},{1,3},{2,0},{3,1},{4,6},{5,7},{6,4},{7,5},{8,10},{9,11},{10,... | collective-permute-start | bytes 786440 | tf_op jit(solution)/shard_map/ppermute | solution.py:311
  76.4 36.0 %collective-permute-start.16 = (bf16[256,512]{1,0:T(8,128)(2,1)S(1)}, bf16[256,512]{1,0:T(8,128)(2,1)S(1)}, u32[]{:S(2)}, u32[]{:S(2)}) collective-permute-start(bf16[256,512]{1,0:T(8,128)(2,1)S(1)} %get-tuple-element.16), channel_id=1, source_target_pairs={{0,3},{1,2},{2,1},{3,0},{4,7},{5,6},{6,5},{7,4},{8,11},{9,10},{10,... | collective-permute-start | bytes 786440 | tf_op jit(solution)/shard_map/ppermute | solution.py:311
  96.4 15.9 %collective-permute-start.19 = (bf16[256,512]{1,0:T(8,128)(2,1)S(1)}, bf16[256,512]{1,0:T(8,128)(2,1)S(1)}, u32[]{:S(2)}, u32[]{:S(2)}) collective-permute-start(bf16[256,512]{1,0:T(8,128)(2,1)S(1)} %get-tuple-element.18), channel_id=1, source_target_pairs={{0,1},{1,0},{2,3},{3,2},{4,5},{5,4},{6,7},{7,6},{8,9},{9,8},{10,11... | collective-permute-start | bytes 786440 | tf_op jit(solution)/shard_map/ppermute | solution.py:311
  96.5 15.9 %collective-permute-start.20 = (bf16[256,512]{1,0:T(8,128)(2,1)S(1)}, bf16[256,512]{1,0:T(8,128)(2,1)S(1)}, u32[]{:S(2)}, u32[]{:S(2)}) collective-permute-start(bf16[256,512]{1,0:T(8,128)(2,1)S(1)} %get-tuple-element.19), channel_id=1, source_target_pairs={{0,2},{1,3},{2,0},{3,1},{4,6},{5,7},{6,4},{7,5},{8,10},{9,11},{10,... | collective-permute-start | bytes 786440 | tf_op jit(solution)/shard_map/ppermute | solution.py:311
  97.1 15.3 %collective-permute-start.21 = (bf16[256,512]{1,0:T(8,128)(2,1)S(1)}, bf16[256,512]{1,0:T(8,128)(2,1)S(1)}, u32[]{:S(2)}, u32[]{:S(2)}) collective-permute-start(bf16[256,512]{1,0:T(8,128)(2,1)S(1)} %get-tuple-element.20), channel_id=1, source_target_pairs={{0,3},{1,2},{2,1},{3,0},{4,7},{5,6},{6,5},{7,4},{8,11},{9,10},{10,... | collective-permute-start | bytes 786440 | tf_op jit(solution)/shard_map/ppermute | solution.py:311
  (6 other events, 66.9 us)

commit v2 on v1

v2 whole, which is shorter than its diff:
```python
import functools

import jax
import jax.numpy as jnp
from jax import lax
from jax.experimental import pallas as pl
from jax.experimental.pallas import tpu as pltpu
from jax.sharding import PartitionSpec as P

AXES = ("grp", "dev")
CORES = 2
GROUP_ITEMS = 4
VMEM_BYTES = 32 * 1024 * 1024


def short_kernel(
    half_ref, live_ref, sub_ref, meta_ref, basis_ref, decay_ref, *refs, share, subs, depth, width
):
    items, (out_ref, basis_f32, left, acc, dists, group_sub, cursor) = refs[:-7], refs[-7:]
    slots = share * len(items)
    step = pl.program_id(0)

    @pl.when(step == 0)
    def _():
        left[...] = jnp.zeros_like(left)
        for s in range(subs):
            cursor[s] = 0

        def count(i, carry):
            cursor[sub_ref[i]] = cursor[sub_ref[i]] + live_ref[i]
            return carry

        lax.fori_loop(0, slots, count, 0)
        first = jnp.int32(0)
        for s in range(subs):
            groups = (cursor[s] + GROUP_ITEMS - 1) // GROUP_ITEMS

            def mark(i, carry, s=s):
                group_sub[i] = s
                return carry

            lax.fori_loop(first, first + groups, mark, 0)
            cursor[s] = first * GROUP_ITEMS
            first = first + groups
        cursor[subs] = first

        def clear(i, carry):
            dists[i] = 0.0
            return carry

        lax.fori_loop(0, first * GROUP_ITEMS, clear, 0)

        for n, items_ref in enumerate(items):

            def place(k, carry, first=n * share, items_ref=items_ref):
                i = first + k

                @pl.when(live_ref[i] > 0)
                def _():
                    s = sub_ref[i]
                    at = cursor[s]
                    cursor[s] = at + 1
                    dists[at] = meta_ref[0, i]
                    turned = items_ref[k].astype(jnp.float32)
                    lanes = pl.ds(pl.multiple_of((at % GROUP_ITEMS) * depth, depth), depth)
                    group = at // GROUP_ITEMS
                    left[group, 0:width, lanes] = (turned * meta_ref[1, i]).astype(left.dtype)
                    left[group, width:, lanes] = (turned * meta_ref[2, i]).astype(left.dtype)

                return carry

            lax.fori_loop(0, share, place, 0)

    basis_f32[...] = basis_ref[...].astype(jnp.float32)
    acc[...] = jnp.zeros_like(acc)
    decay = decay_ref[...]

    def one_group(group, carry):
        parts = []
        for k in range(GROUP_ITEMS):
            damping = jnp.exp(decay * -dists[group * GROUP_ITEMS + k])
            parts.append((basis_f32[...] * damping).astype(jnp.bfloat16))
        right = jnp.concatenate(parts, axis=0)
        s = group_sub[group]
        acc[s] += jnp.dot(left[group], right, preferred_element_type=jnp.float32)
        return carry

    lax.fori_loop(0, cursor[subs], one_group, 0)
    for s in range(subs):
        for c in range(2):
            column = (c * subs + s) * width
            out_ref[:, column : column + width] = acc[s, c * width : (c + 1) * width, :].T


def short_range(half, live, sub_ids, meta, aux_basis, aux_decay, items, row_count, subs):
    _, width, depth = items[0].shape
    slots = live.shape[0]
    share = slots // len(items)
    tile = min(row_count, 512)
    steps = row_count // tile
    groups = slots // GROUP_ITEMS + subs
    kernel = functools.partial(short_kernel, share=share, subs=subs, depth=depth, width=width)
    return pl.pallas_call(
        kernel,
        out_shape=jax.ShapeDtypeStruct((row_count, 2 * subs * width), jnp.float32),
        grid_spec=pltpu.PrefetchScalarGridSpec(
            num_scalar_prefetch=4,
            grid=(steps,),
            in_specs=[
                pl.BlockSpec((depth, tile), lambda t, half, *_: (0, half[0] * steps + t)),
                pl.BlockSpec((1, tile), lambda t, half, *_: (0, half[0] * steps + t)),
            ]
            + [pl.BlockSpec((share, width, depth), lambda t, *_: (0, 0, 0))] * len(items),
            out_specs=pl.BlockSpec((tile, 2 * subs * width), lambda t, *_: (t, 0)),
            scratch_shapes=[
                pltpu.VMEM((depth, tile), jnp.float32),
                pltpu.VMEM((groups, 2 * width, GROUP_ITEMS * depth), jnp.bfloat16),
                pltpu.VMEM((subs, 2 * width, tile), jnp.float32),
                pltpu.SMEM((groups * GROUP_ITEMS,), jnp.float32),
                pltpu.SMEM((groups,), jnp.int32),
                pltpu.SMEM((subs + 1,), jnp.int32),
            ],
        ),
        compiler_params=pltpu.CompilerParams(vmem_limit_bytes=VMEM_BYTES),
        cost_estimate=pl.CostEstimate(
            flops=2 * row_count * slots * depth * width * 2,
            bytes_accessed=row_count * 2 * subs * width * 4 + slots * depth * width * 2,
            transcendentals=0,
        ),
        name="short_range",
    )(half, live, sub_ids, meta, aux_basis, aux_decay.reshape(1, -1), *items)


def long_kernel(place_ref, *refs, chains, pieces, rows, depth):
    names = []
    at = 0
    for count in chains:
        names.append(refs[at : at + count])
        at += count
    factors = refs[at : at + pieces * len(chains)]
    at += pieces * len(chains)
    outs = refs[at : at + pieces]
    block, left, right, block_sem, right_sem = refs[at + pieces :]
    for chain, candidates in enumerate(names):
        for k, ref in enumerate(candidates):

            @pl.when(place_ref[0] == k)
            def _(ref=ref, chain=chain):
                pltpu.make_async_copy(ref, block.at[chain], block_sem.at[chain]).start()

    copies = {}
    for piece in reversed(range(pieces)):
        for chain in range(len(chains)):
            copies[piece, chain] = pltpu.make_async_copy(
                factors[piece * len(chains) + chain],
                right.at[piece, pl.ds(chain * depth, depth), :],
                right_sem.at[piece, chain],
            )
            copies[piece, chain].start()
    half = depth // 2
    for chain, candidates in enumerate(names):
        pltpu.make_async_copy(candidates[0], block.at[chain], block_sem.at[chain]).wait()
        at = chain * depth
        left[0:rows, at : at + depth] = block[chain]
        left[rows:, at : at + half] = -block[chain, :, half:]
        left[rows:, at + half : at + depth] = block[chain, :, 0:half]
    for piece in reversed(range(pieces)):
        for chain in range(len(chains)):
            copies[piece, chain].wait()
        total = jnp.dot(left[...], right[piece], preferred_element_type=jnp.float32)
        width = total.shape[1]
        outs[piece][:, 0:width] = total[0:rows].astype(outs[piece].dtype)
        outs[piece][:, width:] = total[rows:].astype(outs[piece].dtype)


def long_range(place, chains, factors, out_dtypes):
    rows, depth = chains[0][0].shape
    width = factors[0][0].shape[1]
    pieces = len(factors)
    count = pieces * len(chains)
    blocks = [block for candidates in chains for block in candidates]
    flat = [factor for per_piece in factors for factor in per_piece]
    kernel = functools.partial(
        long_kernel, chains=[len(c) for c in chains], pieces=pieces, rows=rows, depth=depth
    )
    return pl.pallas_call(
        kernel,
        out_shape=[jax.ShapeDtypeStruct((rows, 2 * width), dtype) for dtype in out_dtypes],
        in_specs=[pl.BlockSpec(memory_space=pltpu.SMEM)]
        + [pl.BlockSpec(memory_space=pl.ANY)] * (len(blocks) + len(flat)),
        out_specs=[pl.BlockSpec(memory_space=pltpu.VMEM)] * pieces,
        scratch_shapes=[
            pltpu.VMEM((len(chains), rows, depth), jnp.bfloat16),
            pltpu.VMEM((2 * rows, len(chains) * depth), jnp.bfloat16),
            pltpu.VMEM((pieces, len(chains) * depth, width), jnp.bfloat16),
            pltpu.SemaphoreType.DMA((len(chains),)),
            pltpu.SemaphoreType.DMA((pieces, len(chains))),
        ],
        compiler_params=pltpu.CompilerParams(vmem_limit_bytes=VMEM_BYTES),
        cost_estimate=pl.CostEstimate(
            flops=2 * 2 * rows * depth * width * count,
            bytes_accessed=2 * (count * depth * width + len(chains) * rows * depth + pieces * rows * 2 * width),
            transcendentals=0,
        ),
        name="long_range",
    )(place, *blocks, *flat)


def final_kernel(order_ref, *refs, pieces):
    short_ref, out_ref = refs[pieces], refs[-1]
    width = out_ref.shape[2]
    for n in range(pieces):

        @pl.when(pl.program_id(0) == n)
        def _(n=n):
            total = (refs[n][...].astype(jnp.float32) + short_ref[...]).astype(out_ref.dtype)
            out_ref[:, 0, :] = total[:, 0:width]
            out_ref[:, 1, :] = total[:, width:]


def final_sum(order, pieces, short, earlier):
    rows, columns = pieces[0].shape
    row_count = short.shape[0]
    count = len(pieces)
    return pl.pallas_call(
        functools.partial(final_kernel, pieces=count),
        out_shape=jax.ShapeDtypeStruct((row_count, 2, columns // 2), jnp.bfloat16),
        grid_spec=pltpu.PrefetchScalarGridSpec(
            num_scalar_prefetch=1,
            grid=(count,),
            in_specs=[pl.BlockSpec((rows, columns), lambda n, order: (0, 0))] * count
            + [pl.BlockSpec((rows, columns), lambda n, order: (order[n], 0))]
            + [pl.BlockSpec(memory_space=pl.ANY)] * (earlier is not None),
            out_specs=pl.BlockSpec((rows, 2, columns // 2), lambda n, order: (order[n], 0, 0)),
        ),
        input_output_aliases={count + 2: 0} if earlier is not None else {},
        compiler_params=pltpu.CompilerParams(vmem_limit_bytes=VMEM_BYTES),
        cost_estimate=pl.CostEstimate(
            flops=count * rows * columns, bytes_accessed=count * rows * columns * 8, transcendentals=0
        ),
        name="final_sum",
    )(order, *pieces, short, *([earlier] if earlier is not None else []))


def slot_table(image_dist, image_phase, images):
    chosen = images[None, :] == jnp.arange(image_dist.shape[0], dtype=jnp.int32)[:, None]
    distance = jnp.sum(jnp.where(chosen, image_dist[:, None], 0.0), axis=0)
    phase = jnp.sum(jnp.where(chosen, image_phase[:, None], 0.0), axis=0)
    return jnp.stack([distance, jnp.cos(phase), jnp.sin(phase)])


def slot_block(slots, items):
    digits = jnp.concatenate([slots // 128, slots % 128], axis=0).astype(items.dtype)
    fill = [(0, full - used) for full, used in zip(items.shape[1:], digits.shape)]
    return jnp.pad(digits, fill)[None]


def read_slots(packed, slots):
    count, share = slots.shape
    digits = packed[-1, 0 : 2 * count, 0:share].astype(jnp.int32)
    return digits[0:count] * 128 + digits[count:]


def after(value, *earlier):
    return lax.optimization_barrier((value, *earlier))[0] if earlier else value


def body(
    pair_ft,
    aux_ft,
    coul_weight,
    aux_basis,
    aux_decay,
    image_dist,
    image_phase,
    item_pair,
    item_image,
    item_sub,
    item_count,
):
    group_count = lax.axis_size("grp")
    member_count = lax.axis_size("dev")
    group = lax.axis_index("grp")
    member = lax.axis_index("dev")
    local_rows, _, local_g = pair_ft.shape
    subs = local_rows // item_pair.shape[2]
    rows = aux_ft.shape[0]
    row_count = rows * member_count // group_count
    half = jnp.reshape(group, (1,)).astype(jnp.int32)

    chips = member_count // CORES
    breadth = max(n for n in range(1, chips + 1) if chips % n == 0 and n * n <= chips)
    length = chips // breadth

    aux_flat = aux_ft.reshape(rows, 2 * local_g)
    weighted = (pair_ft.astype(jnp.float32) * coul_weight[None, None, :]).astype(jnp.bfloat16)
    turned = weighted.reshape(local_rows, 2 * local_g).T
    item_rows = jnp.swapaxes(item_pair, 1, 2)
    live = (jnp.arange(item_image.shape[0], dtype=jnp.int32) < item_count[0]).astype(jnp.int32)
    slots = jnp.stack([item_image, item_sub, live])

    if group_count != 2 or length % 2:
        everything = lax.all_gather(aux_flat, "dev", axis=0, tiled=True)
        mine = lax.all_to_all(everything, "grp", split_axis=0, concat_axis=1, tiled=True)
        factor = lax.all_gather(turned, "grp", axis=0, tiled=True)
        parts = factor.reshape(group_count, 2, local_g, local_rows)
        other = jnp.stack([parts[:, 1], -parts[:, 0]], axis=1).reshape(factor.shape)
        long_part = jnp.concatenate(
            [
                jnp.dot(mine, factor, preferred_element_type=jnp.float32),
                jnp.dot(mine, other, preferred_element_type=jnp.float32),
            ],
            axis=1,
        )
        items = lax.all_gather(item_rows, "grp", axis=0, tiled=True)
        images, sub_ids, live = lax.all_gather(slots, "grp", axis=1, tiled=True)
        table = slot_table(image_dist, image_phase, images)
        short = short_range(
            half, live, sub_ids, table, aux_basis, aux_decay, [items], row_count, subs
        )
        return (long_part + short).astype(jnp.bfloat16).reshape(row_count, 2, local_rows)

    home = length // 2
    up = member // (breadth * CORES)
    across = member // CORES % breadth
    core = member % CORES
    logical = jnp.where(group == 0, up, length - 1 - up)

    def send(value, route):
        def index(g, u, y, c):
            z = u if g == 0 else length - 1 - u
            return g * member_count + (z * breadth + y) * CORES + c

        pairs = []
        for g in range(group_count):
            for u in range(length):
                for y in range(breadth):
                    for c in range(CORES):
                        target = route(g, u, y, c)
                        if target is not None:
                            pairs.append((index(g, u, y, c), index(*target)))
        return lax.ppermute(value, AXES, pairs)

    def mirrored(g, u, y, c):
        return 1 - g, length - 1 - u, y, c

    outward = {0: aux_flat}
    inward = {0: aux_flat}
    across_x = {}

    def hop(s):
        outward[s] = send(
            outward[s - 1],
            lambda g, u, y, c: (g, u + 1, y, c) if u + 1 < length and u - (s - 1) >= 0 else None,
        )
        inward[s] = send(
            inward[s - 1],
            lambda g, u, y, c: (g, u - 1, y, c) if u >= 1 and u + (s - 1) < length else None,
        )

    def cross(s, *earlier):
        block = after(outward[s] if s >= 0 else inward[-s], *earlier)
        across_x[s] = send(
            block, lambda g, u, y, c: mirrored(g, u, y, c) if home <= u - s < length else None
        )

    def over_y(value, s):
        return send(value, lambda g, u, y, c: (g, u, (y - s) % breadth, c))

    def over_core(value, t):
        return send(value, lambda g, u, y, c: (g, u, y, (c - t) % CORES))

    hop(1)
    turned_x = send(turned, mirrored)
    packed = jnp.concatenate([item_rows, slot_block(slots, item_rows)], axis=0)
    items_x = send(after(packed, turned_x, outward[1], inward[1]), mirrored)
    for s in range(2, length):
        hop(s)

    shifts = [s for s in range(1 - length, home)]
    early = [s for s in shifts if s % 2 == 0]
    late = [s for s in shifts if s % 2]
    for s in early:
        cross(s, items_x)

    images, sub_ids, live = jnp.concatenate([slots, read_slots(items_x, slots)], axis=1)
    table = slot_table(image_dist, image_phase, images)
    short = short_range(
        half, live, sub_ids, table, aux_basis, aux_decay, [packed, items_x], row_count, subs
    )
    for s in late:
        cross(s, items_x, inward[length - 1], short)

    partners = [(s, t) for s in range(breadth) for t in range(CORES)]
    factors = []
    for s, t in partners:
        pair = [turned, turned_x]
        if s:
            pair = [over_y(v, s) for v in pair]
        if t:
            pair = [over_core(v, t) for v in pair]
        factors.append(pair)

    place = jnp.reshape(logical, (1,)).astype(jnp.int32)
    out = None
    for k in range(home):
        mine = [sorted(range(home), key=lambda j: ((j - u) % 2, abs(u - j)))[k] for u in range(length)]
        own = [outward[u - j] if u >= j else inward[j - u] for u, j in enumerate(mine)]
        other = [across_x[j - u] for u, j in enumerate(mine)]
        made = long_range(
            place,
            [own, other],
            factors,
            [jnp.float32 if n == 0 else jnp.bfloat16 for n in range(len(partners))],
        )
        block = sum(jnp.where(logical == u, j, 0) for u, j in enumerate(mine))
        slab = jnp.where(group == 0, block, home - 1 - block)
        results = []
        order = []
        for (s, t), piece in zip(partners, made):
            if (s, t) != (0, 0):
                piece = send(
                    piece,
                    lambda g, u, y, c, s=s, t=t: (g, u, (y + s) % breadth, (c + t) % CORES),
                )
            results.append(piece)
            order.append((slab * breadth + (across - s) % breadth) * CORES + (core - t) % CORES)
        out = final_sum(jnp.stack(order).astype(jnp.int32), results, short, out)
    return out


def solution(mesh):
    return jax.shard_map(
        body,
        mesh=mesh,
        in_specs=(
            P("dev", None, "grp"),
            P("dev", None, "grp"),
            P("grp"),
            P(),
            P(),
            P(),
            P(),
            P(("grp", "dev"), None, None),
            P(("grp", "dev")),
            P(("grp", "dev")),
            P(("grp", "dev")),
        ),
        out_specs=P("grp", None, "dev"),
        check_vma=False,
    )
```

time: 122 us -> 129 us (1.057)
  the two profiles are of different devices: /device:TPU:2 before, /device:TPU:0 now
where the time goes in v2:
time: 129 us; the launch traced here: 127 us
  starting transfers between devices  38.8 us (30%)
  waiting for transfers between devices  34.1 us (26%)
  Pallas kernels  33.2 us (26%)
  local copies, waits for them, and re-layouts  16.9 us (13%)
  other arithmetic  3.45 us (3%)
    ppermute x25, starting transfers between devices, send(): return lax.ppermute(value, AXES, pairs)  38.8 us
    ppermute x25, waiting for transfers between devices, send(): return lax.ppermute(value, AXES, pairs)  34.1 us
    unnamed x50, local copies, waits for them, and re-layouts  16.3 us
    pallas_call x1, Pallas kernels, short_range(): pl.pallas_call(kernel, out_shape=jax.ShapeDtypeStruct((row_count, 2 * sub...  12.7 us
    pallas_call x2, Pallas kernels, long_range(): pl.pallas_call(kernel, out_shape=[jax.ShapeDtypeStruct((rows, 2 * width),...  11.8 us
    pallas_call x2, Pallas kernels, final_sum(): pl.pallas_call(functools.partial(final_kernel, pieces=count), out_shape=j...  8.62 us
  transfers between devices with their start and end apart: 25, of which 8 were waited for; matrix products, arithmetic and copies ran while one was open for 3% of the time, Pallas kernels for 23%

profile of v2, /device:TPU:0, one launch (start us, length us, event | category | flops | bytes accessed | tf_op | source)
XLA Modules:
  0.0 127.3 jit_solution(5039352788260235775)
XLA Ops:
  1.2 5.1 %collective-permute-start.1 = (bf16[256,1024]{1,0:T(8,128)(2,1)S(1)}, bf16[256,1024]{1,0:T(8,128)(2,1)S(1)}, u32[]{:S(2)}, u32[]{:S(2)}) collective-permute-start(bf16[256,1024]{1,0:T(8,128)(2,1)S(1)} %bitcast.41), channel_id=1, source_target_pairs={{0,4},{1,5},{2,6},{3,7},{4,8},{5,9},{6,10},{7,11},{8,12},{9,13},{1... | collective-permute-start | bytes 1572872 | tf_op jit(solution)/shard_map/ppermute | solution.py:342
  9.6 3.4 %collective-permute-start.4 = (bf16[1024,256]{1,0:T(8,128)(2,1)S(1)}, bf16[1024,256]{1,0:T(8,128)(2,1)S(1)}, u32[]{:S(2)}, u32[]{:S(2)}) collective-permute-start(bf16[1024,256]{1,0:T(8,128)(2,1)S(1)} %bitcast.36), channel_id=1, source_target_pairs={{0,16},{1,17},{2,18},{3,19},{4,20},{5,21},{6,22},{7,23},{8,24},{9,... | collective-permute-start | bytes 1572872 | tf_op jit(solution)/shard_map/ppermute | solution.py:342
  14.9 2.5 %collective-permute-done.1.refs_1_.refs_2_ = bf16[256,1024]{1,0:T(8,128)(2,1)S(1)} collective-permute-done((bf16[256,1024]{1,0:T(8,128)(2,1)S(1)}, bf16[256,1024]{1,0:T(8,128)(2,1)S(1)}, u32[]{:S(2)}, u32[]{:S(2)}) %collective-permute-start.1) | collective-permute-done | bytes 524320 | tf_op jit(solution)/shard_map/ppermute | solution.py:342
  17.4 4.3 %collective-permute-done.refs_0_ = bf16[256,1024]{1,0:T(8,128)(2,1)} collective-permute-done((bf16[256,1024]{1,0:T(8,128)(2,1)S(1)}, bf16[256,1024]{1,0:T(8,128)(2,1)}, u32[]{:S(2)}, u32[]{:S(2)}) %collective-permute-start) | collective-permute-done | bytes 524320 | tf_op jit(solution)/shard_map/ppermute | solution.py:342
  21.7 2.7 %collective-permute-done.4.refs_9_ = bf16[1024,256]{1,0:T(8,128)(2,1)S(1)} collective-permute-done((bf16[1024,256]{1,0:T(8,128)(2,1)S(1)}, bf16[1024,256]{1,0:T(8,128)(2,1)S(1)}, u32[]{:S(2)}, u32[]{:S(2)}) %collective-permute-start.4) | collective-permute-done | bytes 524320 | tf_op jit(solution)/shard_map/ppermute | solution.py:342
  24.4 1.7 %collective-permute-start.5 = (bf16[17,128,128]{2,1,0:T(8,128)(2,1)}, bf16[17,128,128]{2,1,0:T(8,128)(2,1)}, u32[]{:S(2)}, u32[]{:S(2)}) collective-permute-start(bf16[17,128,128]{2,1,0:T(8,128)(2,1)} %pad_maximum_fusion.refs_0_), channel_id=1, source_target_pairs={{0,16},{1,17},{2,18},{3,19},{4,20},{5,21},{6,22},{7,23},{8,24},{9,... | collective-permute-start | bytes 1671176 | tf_op jit(solution)/shard_map/ppermute | solution.py:342
  27.4 1.6 %collective-permute-start.13 = (bf16[1024,256]{1,0:T(8,128)(2,1)S(1)}, bf16[1024,256]{1,0:T(8,128)(2,1)S(1)}, u32[]{:S(2)}, u32[]{:S(2)}) collective-permute-start(bf16[1024,256]{1,0:T(8,128)(2,1)S(1)} %bitcast.37), channel_id=1, source_target_pairs={{0,2},{1,3},{2,0},{3,1},{4,6},{5,7},{6,4},{7,5},{8,10},{9,11},{10,... | collective-permute-start | bytes 1572872 | tf_op jit(solution)/shard_map/ppermute | solution.py:342
  30.5 9.7 %collective-permute-done.6 = bf16[256,1024]{1,0:T(8,128)(2,1)} collective-permute-done((bf16[256,1024]{1,0:T(8,128)(2,1)}, bf16[256,1024]{1,0:T(8,128)(2,1)}, u32[]{:S(2)}, u32[]{:S(2)}) %collective-permute-start.6) | collective-permute-done | bytes 524320 | tf_op jit(solution)/shard_map/ppermute | solution.py:342
  40.2 1.5 %collective-permute-start.14 = (bf16[1024,256]{1,0:T(8,128)(2,1)S(1)}, bf16[1024,256]{1,0:T(8,128)(2,1)S(1)}, u32[]{:S(2)}, u32[]{:S(2)}) collective-permute-start(bf16[1024,256]{1,0:T(8,128)(2,1)S(1)} %collective-permute-done.4.refs_9_), channel_id=1, source_target_pairs={{0,2},{1,3},{2,0},{3,1},{4,6},{5,7},{6,4},{7,5},{8,10},{9,11},{10,... | collective-permute-start | bytes 1572872 | tf_op jit(solution)/shard_map/ppermute | solution.py:342
  44.6 6.6 %collective-permute-done.14.refs_13_ = bf16[1024,256]{1,0:T(8,128)(2,1)S(1)} collective-permute-done((bf16[1024,256]{1,0:T(8,128)(2,1)S(1)}, bf16[1024,256]{1,0:T(8,128)(2,1)S(1)}, u32[]{:S(2)}, u32[]{:S(2)}) %collective-permute-start.14) | collective-permute-done | bytes 524320 | tf_op jit(solution)/shard_map/ppermute | solution.py:342
  52.6 2.1 %collective-permute-done.7 = bf16[256,1024]{1,0:T(8,128)(2,1)} collective-permute-done((bf16[256,1024]{1,0:T(8,128)(2,1)}, bf16[256,1024]{1,0:T(8,128)(2,1)}, u32[]{:S(2)}, u32[]{:S(2)}) %collective-permute-start.7) | collective-permute-done | bytes 524320 | tf_op jit(solution)/shard_map/ppermute | solution.py:342
  54.6 3.4 %collective-permute-start.21 = (bf16[256,1024]{1,0:T(8,128)(2,1)}, bf16[256,1024]{1,0:T(8,128)(2,1)}, u32[]{:S(2)}, u32[]{:S(2)}) collective-permute-start(bf16[256,1024]{1,0:T(8,128)(2,1)} %collective-permute-done.6), channel_id=1, source_target_pairs={{0,16},{1,17},{2,18},{3,19},{4,20},{5,21},{6,22},{7,23},{28,12},{2... | collective-permute-start | bytes 1572872 | tf_op jit(solution)/shard_map/ppermute | solution.py:342
  59.2 12.7 %short_range.1.refs_4_ = f32[2048,512]{1,0:T(8,128)S(1)} custom-call(s32[1]{0:T(128)} %bitcast.12.half_ref, s32[32]{0:T(128)S(1)} %get-tuple-element.37.live_ref, s32[32]{0:T(128)S(1)} %get-tuple-element.36.sub_ref, f32[3,32]{1,0:T(4,128)S(1)} %pad_maximum_fusion.1.meta_ref, bf16[128,4096]{1,0:T(8,128)(2,1)S(1)} %copy-done.17, f32[1,4096]{1,0:T(1,128)S(1)} %bitcast.46, ...), custom_call_target="tpu_custom_call" | custom-call | flops 4294967296 | bytes 5242880 | tf_op jit(solution)/shard_map/short_range/pallas_call | solution.py:103
  72.0 1.9 %copy-done = f32[2048,512]{1,0:T(8,128)} copy-done((f32[2048,512]{1,0:T(8,128)}, f32[2048,512]{1,0:T(8,128)S(1)}, u32[]{:S(2)}) %copy-start) | copy-done | bytes 4194328
  81.4 6.2 %collective-permute-start.10 = (bf16[256,1024]{1,0:T(8,128)(2,1)}, bf16[256,1024]{1,0:T(8,128)(2,1)}, u32[]{:S(2)}, u32[]{:S(2)}) collective-permute-start(bf16[256,1024]{1,0:T(8,128)(2,1)} %collective-permute-done.7), channel_id=1, source_target_pairs={{0,16},{1,17},{2,18},{3,19},{28,12},{29,13},{30,14},{31,15}} | collective-permute-start | bytes 1572872 | tf_op jit(solution)/shard_map/ppermute | solution.py:342
  92.8 5.5 %long_range.3 = (f32[256,512]{1,0:T(8,128)S(1)}, bf16[256,512]{1,0:T(8,128)(2,1)S(1)}, bf16[256,512]{1,0:T(8,128)(2,1)}, bf16[256,512]{1,0:T(8,128)(2,1)}) custom-call(s32[1]{0:T(128)} %bitcast.4.place_ref, bf16[256,1024]{1,0:T(8,128)(2,1)S(1)} %bitcast.44, bf16[256,1024]{1,0:T(8,128)(2,1)S(1)} %bitcast.45, ...), custom_call_target="tpu_custom_call" | custom-call | flops 2147483648 | bytes 6291456 | tf_op jit(solution)/shard_map/long_range/pallas_call | solution.py:186
  98.4 2.2 %collective-permute-start.23 = (bf16[256,512]{1,0:T(8,128)(2,1)}, bf16[256,512]{1,0:T(8,128)(2,1)}, u32[]{:S(2)}, u32[]{:S(2)}) collective-permute-start(bf16[256,512]{1,0:T(8,128)(2,1)} %get-tuple-element.31), channel_id=1, source_target_pairs={{0,2},{1,3},{2,0},{3,1},{4,6},{5,7},{6,4},{7,5},{8,10},{9,11},{10,... | collective-permute-start | bytes 786440 | tf_op jit(solution)/shard_map/ppermute | solution.py:342
  100.6 6.4 %long_range.2 = (f32[256,512]{1,0:T(8,128)S(1)}, bf16[256,512]{1,0:T(8,128)(2,1)}, bf16[256,512]{1,0:T(8,128)(2,1)}, bf16[256,512]{1,0:T(8,128)(2,1)}) custom-call(s32[1]{0:T(128)} %bitcast.4.place_ref, bf16[256,1024]{1,0:T(8,128)(2,1)} %collective-permute-done.refs_0_, bf16[256,1024]{1,0:T(8,128)(2,1)S(1)} %collective-permute-done.1.refs_1_.refs_2_, ...), custom_call_target="tpu_custom_call" | custom-call | flops 2147483648 | bytes 6291456 | tf_op jit(solution)/shard_map/long_range/pallas_call | solution.py:186
  107.2 2.0 %collective-permute-start.18 = (bf16[256,512]{1,0:T(8,128)(2,1)}, bf16[256,512]{1,0:T(8,128)(2,1)S(1)}, u32[]{:S(2)}, u32[]{:S(2)}) collective-permute-start(bf16[256,512]{1,0:T(8,128)(2,1)} %get-tuple-element.25), channel_id=1, source_target_pairs={{0,2},{1,3},{2,0},{3,1},{4,6},{5,7},{6,4},{7,5},{8,10},{9,11},{10,... | collective-permute-start | bytes 786440 | tf_op jit(solution)/shard_map/ppermute | solution.py:342
  109.3 3.8 %collective-permute-done.24.refs_3_ = bf16[256,512]{1,0:T(8,128)(2,1)} collective-permute-done((bf16[256,512]{1,0:T(8,128)(2,1)}, bf16[256,512]{1,0:T(8,128)(2,1)}, u32[]{:S(2)}, u32[]{:S(2)}) %collective-permute-start.24) | collective-permute-done | bytes 262176 | tf_op jit(solution)/shard_map/ppermute | solution.py:342
  113.2 2.2 %copy-done.1 = f32[2048,512]{1,0:T(8,128)S(1)} copy-done((f32[2048,512]{1,0:T(8,128)S(1)}, f32[2048,512]{1,0:T(8,128)}, u32[]{:S(2)}) %copy-start.1) | copy-done | bytes 4194328
  116.4 5.0 %final_sum.2.refs_5_ = bf16[2048,2,256]{2,1,0:T(2,128)(2,1)} custom-call(s32[4]{0:T(128)S(1)} %pad_add_fusion.3.order_ref, f32[256,512]{1,0:T(8,128)S(1)} %copy-done.16, bf16[256,512]{1,0:T(8,128)(2,1)S(1)} %collective-permute-done.22.refs_1_, bf16[256,512]{1,0:T(8,128)(2,1)} %collective-permute-done.23.refs_2_, ...), custom_call_target="tpu_custom_call" | custom-call | flops 524288 | bytes 4194304 | tf_op jit(solution)/shard_map/final_sum/pallas_call | solution.py:225
  121.4 2.3 %collective-permute-done.19.refs_3_ = bf16[256,512]{1,0:T(8,128)(2,1)S(1)} collective-permute-done((bf16[256,512]{1,0:T(8,128)(2,1)}, bf16[256,512]{1,0:T(8,128)(2,1)S(1)}, u32[]{:S(2)}, u32[]{:S(2)}) %collective-permute-start.19) | collective-permute-done | bytes 262176 | tf_op jit(solution)/shard_map/ppermute | solution.py:342
  123.7 3.7 %final_sum.3 = bf16[2048,2,256]{2,1,0:T(2,128)(2,1)} custom-call(s32[4]{0:T(128)S(1)} %pad_add_fusion.2.order_ref, f32[256,512]{1,0:T(8,128)S(1)} %get-tuple-element.23.refs_0_, bf16[256,512]{1,0:T(8,128)(2,1)S(1)} %collective-permute-done.17.refs_1_, bf16[256,512]{1,0:T(8,128)(2,1)S(1)} %collective-permute-done.18.refs_2_, ...), custom_call_target="tpu_custom_call", output_to_operand_aliasing={{}: (6, {})} | custom-call | flops 524288 | bytes 4194304 | tf_op jit(solution)/shard_map/final_sum/pallas_call | solution.py:225
  (96 shorter events, 28.0 us)
Async XLA Ops:
  1.2 16.2 %collective-permute-start.1 = (bf16[256,1024]{1,0:T(8,128)(2,1)S(1)}, bf16[256,1024]{1,0:T(8,128)(2,1)S(1)}, u32[]{:S(2)}, u32[]{:S(2)}) collective-permute-start(bf16[256,1024]{1,0:T(8,128)(2,1)S(1)} %bitcast.41), channel_id=1, source_target_pairs={{0,4},{1,5},{2,6},{3,7},{4,8},{5,9},{6,10},{7,11},{8,12},{9,13},{1... | collective-permute-start | bytes 1572872 | tf_op jit(solution)/shard_map/ppermute | solution.py:342
  6.3 15.4 %collective-permute-start = (bf16[256,1024]{1,0:T(8,128)(2,1)S(1)}, bf16[256,1024]{1,0:T(8,128)(2,1)}, u32[]{:S(2)}, u32[]{:S(2)}) collective-permute-start(bf16[256,1024]{1,0:T(8,128)(2,1)S(1)} %bitcast.42), channel_id=1, source_target_pairs={{4,0},{5,1},{6,2},{7,3},{8,4},{9,5},{10,6},{11,7},{12,8},{13,9},{1... | collective-permute-start | bytes 1572872 | tf_op jit(solution)/shard_map/ppermute | solution.py:342
  9.6 14.8 %collective-permute-start.4 = (bf16[1024,256]{1,0:T(8,128)(2,1)S(1)}, bf16[1024,256]{1,0:T(8,128)(2,1)S(1)}, u32[]{:S(2)}, u32[]{:S(2)}) collective-permute-start(bf16[1024,256]{1,0:T(8,128)(2,1)S(1)} %bitcast.36), channel_id=1, source_target_pairs={{0,16},{1,17},{2,18},{3,19},{4,20},{5,21},{6,22},{7,23},{8,24},{9,... | collective-permute-start | bytes 1572872 | tf_op jit(solution)/shard_map/ppermute | solution.py:342
  24.4 17.4 %collective-permute-start.5 = (bf16[17,128,128]{2,1,0:T(8,128)(2,1)}, bf16[17,128,128]{2,1,0:T(8,128)(2,1)}, u32[]{:S(2)}, u32[]{:S(2)}) collective-permute-start(bf16[17,128,128]{2,1,0:T(8,128)(2,1)} %pad_maximum_fusion.refs_0_), channel_id=1, source_target_pairs={{0,16},{1,17},{2,18},{3,19},{4,20},{5,21},{6,22},{7,23},{8,24},{9,... | collective-permute-start | bytes 1671176 | tf_op jit(solution)/shard_map/ppermute | solution.py:342
  26.1 14.1 %collective-permute-start.6 = (bf16[256,1024]{1,0:T(8,128)(2,1)}, bf16[256,1024]{1,0:T(8,128)(2,1)}, u32[]{:S(2)}, u32[]{:S(2)}) collective-permute-start(bf16[256,1024]{1,0:T(8,128)(2,1)} %collective-permute-done.refs_0_), channel_id=1, source_target_pairs={{4,0},{5,1},{6,2},{7,3},{8,4},{9,5},{10,6},{11,7},{24,28},{25,29},... | collective-permute-start | bytes 1572872 | tf_op jit(solution)/shard_map/ppermute | solution.py:342
  27.4 16.6 %collective-permute-start.13 = (bf16[1024,256]{1,0:T(8,128)(2,1)S(1)}, bf16[1024,256]{1,0:T(8,128)(2,1)S(1)}, u32[]{:S(2)}, u32[]{:S(2)}) collective-permute-start(bf16[1024,256]{1,0:T(8,128)(2,1)S(1)} %bitcast.37), channel_id=1, source_target_pairs={{0,2},{1,3},{2,0},{3,1},{4,6},{5,7},{6,4},{7,5},{8,10},{9,11},{10,... | collective-permute-start | bytes 1572872 | tf_op jit(solution)/shard_map/ppermute | solution.py:342
  29.0 15.1 %collective-permute-start.11 = (bf16[1024,256]{1,0:T(8,128)(2,1)S(1)}, bf16[1024,256]{1,0:T(8,128)(2,1)S(1)}, u32[]{:S(2)}, u32[]{:S(2)}) collective-permute-start(bf16[1024,256]{1,0:T(8,128)(2,1)S(1)} %bitcast.38), channel_id=1, source_target_pairs={{0,1},{1,0},{2,3},{3,2},{4,5},{5,4},{6,7},{7,6},{8,9},{9,8},{10,11... | collective-permute-start | bytes 1572872 | tf_op jit(solution)/shard_map/ppermute | solution.py:342
  29.0 22.2 %collective-permute-start.2 = (bf16[256,1024]{1,0:T(8,128)(2,1)S(1)}, bf16[256,1024]{1,0:T(8,128)(2,1)}, u32[]{:S(2)}, u32[]{:S(2)}) collective-permute-start(bf16[256,1024]{1,0:T(8,128)(2,1)S(1)} %collective-permute-done.1.refs_1_.refs_2_), channel_id=1, source_target_pairs={{4,8},{5,9},{6,10},{7,11},{8,12},{9,13},{10,14},{11,15},{24,20},{2... | collective-permute-start | bytes 1572872 | tf_op jit(solution)/shard_map/ppermute | solution.py:342
  40.2 11.0 %collective-permute-start.14 = (bf16[1024,256]{1,0:T(8,128)(2,1)S(1)}, bf16[1024,256]{1,0:T(8,128)(2,1)S(1)}, u32[]{:S(2)}, u32[]{:S(2)}) collective-permute-start(bf16[1024,256]{1,0:T(8,128)(2,1)S(1)} %collective-permute-done.4.refs_9_), channel_id=1, source_target_pairs={{0,2},{1,3},{2,0},{3,1},{4,6},{5,7},{6,4},{7,5},{8,10},{9,11},{10,... | collective-permute-start | bytes 1572872 | tf_op jit(solution)/shard_map/ppermute | solution.py:342
  41.7 12.9 %collective-permute-start.7 = (bf16[256,1024]{1,0:T(8,128)(2,1)}, bf16[256,1024]{1,0:T(8,128)(2,1)}, u32[]{:S(2)}, u32[]{:S(2)}) collective-permute-start(bf16[256,1024]{1,0:T(8,128)(2,1)} %collective-permute-done.6), channel_id=1, source_target_pairs={{4,0},{5,1},{6,2},{7,3},{24,28},{25,29},{26,30},{27,31}} | collective-permute-start | bytes 1572872 | tf_op jit(solution)/shard_map/ppermute | solution.py:342
  44.0 32.2 %collective-permute-start.12 = (bf16[1024,256]{1,0:T(8,128)(2,1)S(1)}, bf16[1024,256]{1,0:T(8,128)(2,1)S(1)}, u32[]{:S(2)}, u32[]{:S(2)}) collective-permute-start(bf16[1024,256]{1,0:T(8,128)(2,1)S(1)} %collective-permute-done.4.refs_9_), channel_id=1, source_target_pairs={{0,1},{1,0},{2,3},{3,2},{4,5},{5,4},{6,7},{7,6},{8,9},{9,8},{10,11... | collective-permute-start | bytes 1572872 | tf_op jit(solution)/shard_map/ppermute | solution.py:342
  44.1 29.9 %collective-permute-start.15 = (bf16[1024,256]{1,0:T(8,128)(2,1)S(1)}, bf16[1024,256]{1,0:T(8,128)(2,1)S(1)}, u32[]{:S(2)}, u32[]{:S(2)}) collective-permute-start(bf16[1024,256]{1,0:T(8,128)(2,1)S(1)} %collective-permute-done.13.refs_12_), channel_id=1, source_target_pairs={{0,1},{1,0},{2,3},{3,2},{4,5},{5,4},{6,7},{7,6},{8,9},{9,8},{10,11... | collective-permute-start | bytes 1572872 | tf_op jit(solution)/shard_map/ppermute | solution.py:342
  51.2 27.1 %collective-permute-start.16 = (bf16[1024,256]{1,0:T(8,128)(2,1)S(1)}, bf16[1024,256]{1,0:T(8,128)(2,1)S(1)}, u32[]{:S(2)}, u32[]{:S(2)}) collective-permute-start(bf16[1024,256]{1,0:T(8,128)(2,1)S(1)} %collective-permute-done.14.refs_13_), channel_id=1, source_target_pairs={{0,1},{1,0},{2,3},{3,2},{4,5},{5,4},{6,7},{7,6},{8,9},{9,8},{10,11... | collective-permute-start | bytes 1572872 | tf_op jit(solution)/shard_map/ppermute | solution.py:342
  51.2 29.4 %collective-permute-start.20 = (bf16[256,1024]{1,0:T(8,128)(2,1)S(1)}, bf16[256,1024]{1,0:T(8,128)(2,1)S(1)}, u32[]{:S(2)}, u32[]{:S(2)}) collective-permute-start(bf16[256,1024]{1,0:T(8,128)(2,1)S(1)} %bitcast.43), channel_id=1, source_target_pairs={{8,24},{9,25},{10,26},{11,27},{12,28},{13,29},{14,30},{15,31},{20,... | collective-permute-start | bytes 1572872 | tf_op jit(solution)/shard_map/ppermute | solution.py:342
  54.6 32.9 %collective-permute-start.21 = (bf16[256,1024]{1,0:T(8,128)(2,1)}, bf16[256,1024]{1,0:T(8,128)(2,1)}, u32[]{:S(2)}, u32[]{:S(2)}) collective-permute-start(bf16[256,1024]{1,0:T(8,128)(2,1)} %collective-permute-done.6), channel_id=1, source_target_pairs={{0,16},{1,17},{2,18},{3,19},{4,20},{5,21},{6,22},{7,23},{28,12},{2... | collective-permute-start | bytes 1572872 | tf_op jit(solution)/shard_map/ppermute | solution.py:342
  74.8 23.6 %collective-permute-start.3 = (bf16[256,1024]{1,0:T(8,128)(2,1)}, bf16[256,1024]{1,0:T(8,128)(2,1)}, u32[]{:S(2)}, u32[]{:S(2)}) collective-permute-start(bf16[256,1024]{1,0:T(8,128)(2,1)} %collective-permute-done.2.refs_2_.refs_3_), channel_id=1, source_target_pairs={{8,12},{9,13},{10,14},{11,15},{20,16},{21,17},{22,18},{23,19}} | collective-permute-start | bytes 1572872 | tf_op jit(solution)/shard_map/ppermute | solution.py:342
  77.0 23.6 %collective-permute-start.8 = (bf16[256,1024]{1,0:T(8,128)(2,1)S(1)}, bf16[256,1024]{1,0:T(8,128)(2,1)}, u32[]{:S(2)}, u32[]{:S(2)}) collective-permute-start(bf16[256,1024]{1,0:T(8,128)(2,1)S(1)} %collective-permute-done.1.refs_1_.refs_2_), channel_id=1, source_target_pairs={{12,28},{13,29},{14,30},{15,31},{16,0},{17,1},{18,2},{19,3}} | collective-permute-start | bytes 1572872 | tf_op jit(solution)/shard_map/ppermute | solution.py:342
  79.1 21.5 %collective-permute-start.9 = (bf16[256,1024]{1,0:T(8,128)(2,1)}, bf16[256,1024]{1,0:T(8,128)(2,1)}, u32[]{:S(2)}, u32[]{:S(2)}) collective-permute-start(bf16[256,1024]{1,0:T(8,128)(2,1)} %collective-permute-done.refs_0_), channel_id=1, source_target_pairs={{4,20},{5,21},{6,22},{7,23},{8,24},{9,25},{10,26},{11,27},{24,8},{... | collective-permute-start | bytes 1572872 | tf_op jit(solution)/shard_map/ppermute | solution.py:342
  81.4 19.2 %collective-permute-start.10 = (bf16[256,1024]{1,0:T(8,128)(2,1)}, bf16[256,1024]{1,0:T(8,128)(2,1)}, u32[]{:S(2)}, u32[]{:S(2)}) collective-permute-start(bf16[256,1024]{1,0:T(8,128)(2,1)} %collective-permute-done.7), channel_id=1, source_target_pairs={{0,16},{1,17},{2,18},{3,19},{28,12},{29,13},{30,14},{31,15}} | collective-permute-start | bytes 1572872 | tf_op jit(solution)/shard_map/ppermute | solution.py:342
  98.4 11.0 %collective-permute-start.23 = (bf16[256,512]{1,0:T(8,128)(2,1)}, bf16[256,512]{1,0:T(8,128)(2,1)}, u32[]{:S(2)}, u32[]{:S(2)}) collective-permute-start(bf16[256,512]{1,0:T(8,128)(2,1)} %get-tuple-element.31), channel_id=1, source_target_pairs={{0,2},{1,3},{2,0},{3,1},{4,6},{5,7},{6,4},{7,5},{8,10},{9,11},{10,... | collective-permute-start | bytes 786440 | tf_op jit(solution)/shard_map/ppermute | solution.py:342
  100.6 12.6 %collective-permute-start.24 = (bf16[256,512]{1,0:T(8,128)(2,1)}, bf16[256,512]{1,0:T(8,128)(2,1)}, u32[]{:S(2)}, u32[]{:S(2)}) collective-permute-start(bf16[256,512]{1,0:T(8,128)(2,1)} %get-tuple-element.32), channel_id=1, source_target_pairs={{0,3},{1,2},{2,1},{3,0},{4,7},{5,6},{6,5},{7,4},{8,11},{9,10},{10,... | collective-permute-start | bytes 786440 | tf_op jit(solution)/shard_map/ppermute | solution.py:342
  107.0 14.4 %collective-permute-start.17 = (bf16[256,512]{1,0:T(8,128)(2,1)}, bf16[256,512]{1,0:T(8,128)(2,1)S(1)}, u32[]{:S(2)}, u32[]{:S(2)}) collective-permute-start(bf16[256,512]{1,0:T(8,128)(2,1)} %get-tuple-element.24), channel_id=1, source_target_pairs={{0,1},{1,0},{2,3},{3,2},{4,5},{5,4},{6,7},{7,6},{8,9},{9,8},{10,11... | collective-permute-start | bytes 786440 | tf_op jit(solution)/shard_map/ppermute | solution.py:342
  107.2 14.2 %collective-permute-start.18 = (bf16[256,512]{1,0:T(8,128)(2,1)}, bf16[256,512]{1,0:T(8,128)(2,1)S(1)}, u32[]{:S(2)}, u32[]{:S(2)}) collective-permute-start(bf16[256,512]{1,0:T(8,128)(2,1)} %get-tuple-element.25), channel_id=1, source_target_pairs={{0,2},{1,3},{2,0},{3,1},{4,6},{5,7},{6,4},{7,5},{8,10},{9,11},{10,... | collective-permute-start | bytes 786440 | tf_op jit(solution)/shard_map/ppermute | solution.py:342
  109.2 14.5 %collective-permute-start.19 = (bf16[256,512]{1,0:T(8,128)(2,1)}, bf16[256,512]{1,0:T(8,128)(2,1)S(1)}, u32[]{:S(2)}, u32[]{:S(2)}) collective-permute-start(bf16[256,512]{1,0:T(8,128)(2,1)} %get-tuple-element.26), channel_id=1, source_target_pairs={{0,3},{1,2},{2,1},{3,0},{4,7},{5,6},{6,5},{7,4},{8,11},{9,10},{10,... | collective-permute-start | bytes 786440 | tf_op jit(solution)/shard_map/ppermute | solution.py:342
  (25 other events, 261.9 us)

commit v3 on v2

v3 whole, which is shorter than its diff:
```python
import functools

import jax
import jax.numpy as jnp
from jax import lax
from jax.experimental import pallas as pl
from jax.experimental.pallas import tpu as pltpu
from jax.sharding import PartitionSpec as P

AXES = ("grp", "dev")
CORES = 2
GROUP_ITEMS = 4
VMEM_BYTES = 20 * 1024 * 1024


def short_kernel(
    half_ref, live_ref, sub_ref, meta_ref, basis_ref, decay_ref, *refs, share, subs, depth, width
):
    items, (out_ref, basis_f32, left, acc, dists, group_sub, cursor) = refs[:-7], refs[-7:]
    slots = share * len(items)
    row_count = out_ref.shape[0]
    left[...] = jnp.zeros_like(left)
    acc[...] = jnp.zeros_like(acc)
    mine = pl.ds(pl.multiple_of(half_ref[0] * row_count, row_count), row_count)
    basis_f32[...] = basis_ref[:, mine].astype(jnp.float32)

    for s in range(subs):
        cursor[s] = 0

    def count(i, carry):
        cursor[sub_ref[i]] = cursor[sub_ref[i]] + live_ref[i]
        return carry

    lax.fori_loop(0, slots, count, 0)
    first = jnp.int32(0)
    for s in range(subs):
        groups = (cursor[s] + GROUP_ITEMS - 1) // GROUP_ITEMS

        def mark(i, carry, s=s):
            group_sub[i] = s
            return carry

        lax.fori_loop(first, first + groups, mark, 0)
        cursor[s] = first * GROUP_ITEMS
        first = first + groups

    def clear(i, carry):
        dists[i] = 0.0
        return carry

    lax.fori_loop(0, first * GROUP_ITEMS, clear, 0)

    for n, items_ref in enumerate(items):

        def place(k, carry, first=n * share, items_ref=items_ref):
            i = first + k

            @pl.when(live_ref[i] > 0)
            def _():
                s = sub_ref[i]
                at = cursor[s]
                cursor[s] = at + 1
                dists[at] = meta_ref[0, i]
                turned = items_ref[k].astype(jnp.float32)
                lanes = pl.ds(pl.multiple_of((at % GROUP_ITEMS) * depth, depth), depth)
                group = at // GROUP_ITEMS
                left[group, 0:width, lanes] = (turned * meta_ref[1, i]).astype(left.dtype)
                left[group, width:, lanes] = (turned * meta_ref[2, i]).astype(left.dtype)

            return carry

        lax.fori_loop(0, share, place, 0)

    tile = min(row_count, 512)
    decay = decay_ref[:, mine]

    def one_group(group, carry):
        s = group_sub[group]
        damping = [jnp.exp(decay * -dists[group * GROUP_ITEMS + k]) for k in range(GROUP_ITEMS)]
        for t in range(0, row_count, tile):
            right = jnp.concatenate(
                [
                    (basis_f32[:, t : t + tile] * damping[k][:, t : t + tile]).astype(jnp.bfloat16)
                    for k in range(GROUP_ITEMS)
                ],
                axis=0,
            )
            acc[s, :, t : t + tile] += jnp.dot(
                left[group], right, preferred_element_type=jnp.float32
            )
        return carry

    lax.fori_loop(0, first, one_group, 0)
    for s in range(subs):
        for c in range(2):
            column = (c * subs + s) * width
            for t in range(0, row_count, tile):
                out_ref[t : t + tile, column : column + width] = acc[
                    s, c * width : (c + 1) * width, t : t + tile
                ].T


def short_range(half, live, sub_ids, meta, aux_basis, aux_decay, items, row_count, subs):
    _, width, depth = items[0].shape
    slots = live.shape[0]
    share = slots // len(items)
    groups = slots // GROUP_ITEMS + subs
    kernel = functools.partial(short_kernel, share=share, subs=subs, depth=depth, width=width)
    return pl.pallas_call(
        kernel,
        out_shape=jax.ShapeDtypeStruct((row_count, 2 * subs * width), jnp.float32),
        in_specs=[pl.BlockSpec(memory_space=pltpu.SMEM)] * 4
        + [pl.BlockSpec(memory_space=pltpu.VMEM)] * (2 + len(items)),
        out_specs=pl.BlockSpec(memory_space=pltpu.VMEM),
        scratch_shapes=[
            pltpu.VMEM((depth, row_count), jnp.float32),
            pltpu.VMEM((groups, 2 * width, GROUP_ITEMS * depth), jnp.bfloat16),
            pltpu.VMEM((subs, 2 * width, row_count), jnp.float32),
            pltpu.SMEM((groups * GROUP_ITEMS,), jnp.float32),
            pltpu.SMEM((groups,), jnp.int32),
            pltpu.SMEM((subs,), jnp.int32),
        ],
        compiler_params=pltpu.CompilerParams(vmem_limit_bytes=VMEM_BYTES),
        cost_estimate=pl.CostEstimate(
            flops=2 * row_count * slots * depth * width * 2,
            bytes_accessed=row_count * 2 * subs * width * 4 + slots * depth * width * 2,
            transcendentals=0,
        ),
        name="short_range",
    )(half, live, sub_ids, meta, aux_basis, aux_decay.reshape(1, -1), *items)


def long_kernel(*refs, blocks, chains, pieces):
    parts = refs[: blocks * chains]
    factors = refs[blocks * chains : (blocks + pieces) * chains]
    outs = refs[(blocks + pieces) * chains : -1]
    left = refs[-1]
    rows, depth = parts[0].shape
    half = depth // 2
    for block in range(blocks):
        top = block * rows
        low = (blocks + block) * rows
        for chain in range(chains):
            part = parts[block * chains + chain]
            at = chain * depth
            left[top : top + rows, at : at + depth] = part[...]
            left[low : low + rows, at : at + half] = -part[:, half:]
            left[low : low + rows, at + half : at + depth] = part[:, 0:half]
    for piece in reversed(range(pieces)):
        total = None
        for chain in range(chains):
            term = jnp.dot(
                left[:, chain * depth : (chain + 1) * depth],
                factors[piece * chains + chain][...],
                preferred_element_type=jnp.float32,
            )
            total = term if total is None else total + term
        width = total.shape[1]
        outs[piece][:, 0:width] = total[0 : blocks * rows].astype(outs[piece].dtype)
        outs[piece][:, width:] = total[blocks * rows :].astype(outs[piece].dtype)


def long_range(blocks, factors, out_dtypes):
    rows, depth = blocks[0][0].shape
    width = factors[0][0].shape[1]
    chains = len(blocks[0])
    pieces = len(factors)
    all_rows = len(blocks) * rows
    flat = [v for group in blocks + factors for v in group]
    return pl.pallas_call(
        functools.partial(long_kernel, blocks=len(blocks), chains=chains, pieces=pieces),
        out_shape=[jax.ShapeDtypeStruct((all_rows, 2 * width), dtype) for dtype in out_dtypes],
        in_specs=[pl.BlockSpec(memory_space=pltpu.VMEM)] * len(flat),
        out_specs=[pl.BlockSpec(memory_space=pltpu.VMEM)] * pieces,
        scratch_shapes=[pltpu.VMEM((2 * all_rows, chains * depth), jnp.bfloat16)],
        compiler_params=pltpu.CompilerParams(vmem_limit_bytes=VMEM_BYTES),
        cost_estimate=pl.CostEstimate(
            flops=2 * 2 * all_rows * depth * chains * width * pieces,
            bytes_accessed=2 * len(flat) * rows * depth + 6 * all_rows * 2 * width,
            transcendentals=0,
        ),
        name="long_range",
    )(*flat)


def final_kernel(order_ref, *refs, pieces, blocks):
    short_ref, out_ref = refs[pieces], refs[-1]
    rows, _, width = out_ref.shape
    for n in range(pieces * blocks):

        @pl.when(pl.program_id(0) == n)
        def _(n=n):
            top = n % blocks * rows
            window = pl.ds(pl.multiple_of(order_ref[n] * rows, rows), rows)
            piece = refs[n // blocks][top : top + rows, :].astype(jnp.float32)
            total = (piece + short_ref[window, :]).astype(out_ref.dtype)
            out_ref[:, 0, :] = total[:, 0:width]
            out_ref[:, 1, :] = total[:, width:]


def final_sum(order, pieces, short, earlier, rows):
    columns = pieces[0].shape[1]
    row_count = short.shape[0]
    count = len(pieces)
    blocks = pieces[0].shape[0] // rows
    steps = count * blocks
    whole = pl.BlockSpec(memory_space=pltpu.VMEM)
    return pl.pallas_call(
        functools.partial(final_kernel, pieces=count, blocks=blocks),
        out_shape=jax.ShapeDtypeStruct((row_count, 2, columns // 2), jnp.bfloat16),
        grid_spec=pltpu.PrefetchScalarGridSpec(
            num_scalar_prefetch=1,
            grid=(steps,),
            in_specs=[whole] * (count + 1)
            + [pl.BlockSpec(memory_space=pl.ANY)] * (earlier is not None),
            out_specs=pl.BlockSpec((rows, 2, columns // 2), lambda n, order: (order[n], 0, 0)),
        ),
        input_output_aliases={count + 2: 0} if earlier is not None else {},
        compiler_params=pltpu.CompilerParams(vmem_limit_bytes=VMEM_BYTES),
        cost_estimate=pl.CostEstimate(
            flops=steps * rows * columns, bytes_accessed=steps * rows * columns * 8, transcendentals=0
        ),
        name="final_sum",
    )(order, *pieces, short, *([earlier] if earlier is not None else []))


def slot_table(image_dist, image_phase, images):
    chosen = images[None, :] == jnp.arange(image_dist.shape[0], dtype=jnp.int32)[:, None]
    distance = jnp.sum(jnp.where(chosen, image_dist[:, None], 0.0), axis=0)
    phase = jnp.sum(jnp.where(chosen, image_phase[:, None], 0.0), axis=0)
    return jnp.stack([distance, jnp.cos(phase), jnp.sin(phase)])


def slot_block(slots, items):
    digits = jnp.concatenate([slots // 128, slots % 128], axis=0).astype(items.dtype)
    fill = [(0, full - used) for full, used in zip(items.shape[1:], digits.shape)]
    return jnp.pad(digits, fill)[None]


def read_slots(packed, slots):
    count, share = slots.shape
    digits = packed[-1, 0 : 2 * count, 0:share].astype(jnp.int32)
    return digits[0:count] * 128 + digits[count:]


def after(value, *earlier):
    return lax.optimization_barrier((value, *earlier))[0] if earlier else value


def body(
    pair_ft,
    aux_ft,
    coul_weight,
    aux_basis,
    aux_decay,
    image_dist,
    image_phase,
    item_pair,
    item_image,
    item_sub,
    item_count,
):
    group_count = lax.axis_size("grp")
    member_count = lax.axis_size("dev")
    group = lax.axis_index("grp")
    member = lax.axis_index("dev")
    local_rows, _, local_g = pair_ft.shape
    subs = local_rows // item_pair.shape[2]
    rows = aux_ft.shape[0]
    row_count = rows * member_count // group_count
    half = jnp.reshape(group, (1,)).astype(jnp.int32)

    chips = member_count // CORES
    breadth = max(n for n in range(1, chips + 1) if chips % n == 0 and n * n <= chips)
    length = chips // breadth

    aux_flat = aux_ft.reshape(rows, 2 * local_g)
    weighted = (pair_ft.astype(jnp.float32) * coul_weight[None, None, :]).astype(jnp.bfloat16)
    turned = weighted.reshape(local_rows, 2 * local_g).T
    item_rows = jnp.swapaxes(item_pair, 1, 2)
    live = (jnp.arange(item_image.shape[0], dtype=jnp.int32) < item_count[0]).astype(jnp.int32)
    slots = jnp.stack([item_image, item_sub, live])

    if group_count != 2 or length % 2:
        everything = lax.all_gather(aux_flat, "dev", axis=0, tiled=True)
        mine = lax.all_to_all(everything, "grp", split_axis=0, concat_axis=1, tiled=True)
        factor = lax.all_gather(turned, "grp", axis=0, tiled=True)
        parts = factor.reshape(group_count, 2, local_g, local_rows)
        other = jnp.stack([parts[:, 1], -parts[:, 0]], axis=1).reshape(factor.shape)
        long_part = jnp.concatenate(
            [
                jnp.dot(mine, factor, preferred_element_type=jnp.float32),
                jnp.dot(mine, other, preferred_element_type=jnp.float32),
            ],
            axis=1,
        )
        items = lax.all_gather(item_rows, "grp", axis=0, tiled=True)
        images, sub_ids, live = lax.all_gather(slots, "grp", axis=1, tiled=True)
        table = slot_table(image_dist, image_phase, images)
        short = short_range(
            half, live, sub_ids, table, aux_basis, aux_decay, [items], row_count, subs
        )
        return (long_part + short).astype(jnp.bfloat16).reshape(row_count, 2, local_rows)

    home = length // 2
    place = member // (breadth * CORES)
    across = member // CORES % breadth
    core = member % CORES

    def send(value, route):
        def index(g, z, y, c):
            return g * member_count + (z * breadth + y) * CORES + c

        pairs = []
        for g in range(group_count):
            for z in range(length):
                for y in range(breadth):
                    for c in range(CORES):
                        pairs.append((index(g, z, y, c), index(*route(g, z, y, c))))
        return lax.ppermute(value, AXES, pairs)

    def to_plane(value):
        return send(value, lambda g, z, y, c: (1 - g, z, y, c))

    def along(value):
        return send(value, lambda g, z, y, c: (g, (z + 1) % length, y, c))

    def over_y(value, s):
        return send(value, lambda g, z, y, c: (g, z, (y + s) % breadth, c))

    def over_core(value, t):
        return send(value, lambda g, z, y, c: (g, z, y, (c + t) % CORES))

    def hops_of(g, z):
        return sorted((z - j) % length for j in range(g * home, (g + 1) * home))

    def pick(held, g_of, n):
        wanted = sum(
            jnp.where((group == g) & (place == z), hops_of(g_of(g), z)[n], 0)
            for g in range(group_count)
            for z in range(length)
        )
        possible = sorted({hops_of(g, z)[n] for g in range(group_count) for z in range(length)})
        value = held[possible[-1]]
        for k in reversed(possible[:-1]):
            value = jnp.where(wanted == k, held[k], value)
        return value, wanted

    held = [aux_flat]
    held.append(along(held[0]))
    turned_x = to_plane(turned)
    factors = [[turned, turned_x]] + [[over_y(turned, s)] for s in range(1, breadth)]
    packed = jnp.concatenate([item_rows, slot_block(slots, item_rows)], axis=0)
    items_x = to_plane(after(packed, turned_x, held[1], *(pair[0] for pair in factors[1:])))
    for s in range(1, breadth):
        factors[s].append(over_y(turned_x, s))
    for k in range(2, length):
        held.append(along(held[-1]))

    images, sub_ids, live = jnp.concatenate([slots, read_slots(items_x, slots)], axis=1)
    table = slot_table(image_dist, image_phase, images)
    short = short_range(
        half, live, sub_ids, table, aux_basis, aux_decay, [packed, items_x], row_count, subs
    )

    ready = []
    order = []
    out = None
    latest = [items_x] + [pair[1] for pair in factors[1:]]
    for n in range(home):
        if n:
            held = lax.optimization_barrier((*held, *latest, short))[:length]
        mine, hops = pick(held, lambda g: g, n)
        theirs, _ = pick(held, lambda g: 1 - g, n)
        crossed = to_plane(after(theirs, *latest))
        latest = [crossed]
        blocks = [[after(mine, short), crossed]]
        for t in range(1, CORES):
            blocks.append([over_core(v, t) for v in blocks[0]])
        made = long_range(
            blocks, factors, [jnp.float32 if s == 0 else jnp.bfloat16 for s in range(breadth)]
        )
        slab = (place - hops) % length - group * home
        for s in range(breadth):
            piece = over_y(made[s], s) if s else made[s]
            numbers = [
                (slab * breadth + (across - s) % breadth) * CORES + (core - t) % CORES
                for t in range(CORES)
            ]
            ready.append(piece)
            order.append(numbers)
    last = breadth - 1
    for chosen in (slice(0, len(ready) - last), slice(len(ready) - last, None)):
        numbers = jnp.stack([v for group_of in order[chosen] for v in group_of]).astype(jnp.int32)
        out = final_sum(numbers, ready[chosen], short, out, rows)
    return out


def solution(mesh):
    return jax.shard_map(
        body,
        mesh=mesh,
        in_specs=(
            P("dev", None, "grp"),
            P("dev", None, "grp"),
            P("grp"),
            P(),
            P(),
            P(),
            P(),
            P(("grp", "dev"), None, None),
            P(("grp", "dev")),
            P(("grp", "dev")),
            P(("grp", "dev")),
        ),
        out_specs=P("grp", None, "dev"),
        check_vma=False,
    )
```

time: 129 us -> 93.8 us (0.73)
  starting transfers between devices: 38.8 us -> 13.6 us
  Pallas kernels: 33.2 us -> 23.8 us
  local copies, waits for them, and re-layouts: 16.9 us -> 9.3 us
  waiting for transfers between devices: 34.1 us -> 41.5 us
    ppermute x25 -> x15, starting transfers between devices: 38.8 us -> 13.6 us  [send(): return lax.ppermute(value, AXES, pairs)]
    unnamed x50 -> x24, local copies, waits for them, and re-layouts: 16.3 us -> 8.62 us
    ppermute x25 -> x15, waiting for transfers between devices: 34.1 us -> 41.5 us  [send(): return lax.ppermute(value, AXES, pairs)]
    pallas_call x4, Pallas kernels: 20.4 us -> 15.7 us  [the longest x2 8.34 us: long_range(): pl.pallas_call(functools.partial(long_kernel, blocks=len(blocks), chains=...]
    pallas_call x1, Pallas kernels: 12.7 us -> 8.14 us  [short_range(): pl.pallas_call(kernel, out_shape=jax.ShapeDtypeStruct((row_count, 2 * sub...]
    select_n x0 -> x2, other arithmetic: none -> 2.34 us  [pick(): value = jnp.where(wanted == k, held[k], value)]
  transfers between devices with their start and end apart: 25 -> 15, of which waited for: 8 -> 7; matrix products, arithmetic and copies ran while one was open for 3% -> 5% of each run, Pallas kernels for 23% -> 23%
where the time goes in v3:
time: 93.8 us; the launch traced here: 93.2 us
  waiting for transfers between devices  41.5 us (44%)
  Pallas kernels  23.8 us (25%)
  starting transfers between devices  13.6 us (14%)
  local copies, waits for them, and re-layouts  9.3 us (10%)
  other arithmetic  4.23 us (5%)
    ppermute x15, waiting for transfers between devices, send(): return lax.ppermute(value, AXES, pairs)  41.5 us
    ppermute x15, starting transfers between devices, send(): return lax.ppermute(value, AXES, pairs)  13.6 us
    unnamed x24, local copies, waits for them, and re-layouts  8.62 us
    pallas_call x2, Pallas kernels, long_range(): pl.pallas_call(functools.partial(long_kernel, blocks=len(blocks), chains=...  8.34 us
    pallas_call x1, Pallas kernels, short_range(): pl.pallas_call(kernel, out_shape=jax.ShapeDtypeStruct((row_count, 2 * sub...  8.14 us
    pallas_call x2, Pallas kernels, final_sum(): pl.pallas_call(functools.partial(final_kernel, pieces=count, blocks=block...  7.33 us
    select_n x2, other arithmetic, pick(): value = jnp.where(wanted == k, held[k], value)  2.34 us
  transfers between devices with their start and end apart: 15, of which 7 were waited for; matrix products, arithmetic and copies ran while one was open for 5% of the time, Pallas kernels for 23%

profile of v3, /device:TPU:0, one launch (start us, length us, event | category | flops | bytes accessed | tf_op | source)
XLA Modules:
  0.0 93.2 jit_solution(13674945539574568206)
XLA Ops:
  0.0 1.1 %copy.17 = bf16[32,8,2,512]{3,1,2,0:T(8,128)(2,1)S(1)} copy(bf16[32,8,2,512]{3,2,1,0:T(2,128)(2,1)} %bitcast.43) | data formatting | bytes 1048576
  1.1 3.1 %collective-permute-start = (bf16[256,1024]{1,0:T(8,128)(2,1)S(1)}, bf16[256,1024]{1,0:T(8,128)(2,1)S(1)}, u32[]{:S(2)}, u32[]{:S(2)}) collective-permute-start(bf16[256,1024]{1,0:T(8,128)(2,1)S(1)} %bitcast.41), channel_id=1, source_target_pairs={{0,4},{1,5},{2,6},{3,7},{4,8},{5,9},{6,10},{7,11},{8,12},{9,13},{1... | collective-permute-start | bytes 1572872 | tf_op jit(solution)/shard_map/ppermute | solution.py:320
  4.2 1.5 %multiply_convert_fusion = bf16[256,2,512]{2,1,0:T(2,128)(2,1)S(1)} fusion(bf16[256,2,512]{2,1,0:T(2,128)(2,1)} %param.11, f32[512]{0:T(512)} %param.13), kind=kLoop, calls=%fused_computation | loop fusion | flops 786432 | bytes 1050624 | tf_op jit(solution)/shard_map/convert_element_type | solution.py:278
  6.2 1.6 %collective-permute-start.4 = (bf16[1024,256]{1,0:T(8,128)(2,1)S(1)}, bf16[1024,256]{1,0:T(8,128)(2,1)S(1)}, u32[]{:S(2)}, u32[]{:S(2)}) collective-permute-start(bf16[1024,256]{1,0:T(8,128)(2,1)S(1)} %bitcast.35), channel_id=1, source_target_pairs={{0,2},{1,3},{2,0},{3,1},{4,6},{5,7},{6,4},{7,5},{8,10},{9,11},{10,... | collective-permute-start | bytes 1572872 | tf_op jit(solution)/shard_map/ppermute | solution.py:320
  7.8 1.5 %collective-permute-start.3 = (bf16[1024,256]{1,0:T(8,128)(2,1)S(1)}, bf16[1024,256]{1,0:T(8,128)(2,1)}, u32[]{:S(2)}, u32[]{:S(2)}) collective-permute-start(bf16[1024,256]{1,0:T(8,128)(2,1)S(1)} %bitcast.36), channel_id=1, source_target_pairs={{0,16},{1,17},{2,18},{3,19},{4,20},{5,21},{6,22},{7,23},{8,24},{9,... | collective-permute-start | bytes 1572872 | tf_op jit(solution)/shard_map/ppermute | solution.py:320
  10.0 8.2 %collective-permute-done = bf16[256,1024]{1,0:T(8,128)(2,1)S(1)} collective-permute-done((bf16[256,1024]{1,0:T(8,128)(2,1)S(1)}, bf16[256,1024]{1,0:T(8,128)(2,1)S(1)}, u32[]{:S(2)}, u32[]{:S(2)}) %collective-permute-start) | collective-permute-done | bytes 524320 | tf_op jit(solution)/shard_map/ppermute | solution.py:320
  18.2 1.3 %copy.15 = bf16[16,128,128]{1,2,0:T(8,128)(2,1)S(1)} copy(bf16[16,128,128]{2,1,0:T(8,128)(2,1)} %param.18) | data formatting | bytes 1048576 | tf_op args[7]
  21.0 1.5 %collective-permute-start.5 = (bf16[17,128,128]{2,1,0:T(8,128)(2,1)S(1)}, bf16[17,128,128]{2,1,0:T(8,128)(2,1)S(1)}, u32[]{:S(2)}, u32[]{:S(2)}) collective-permute-start(bf16[17,128,128]{2,1,0:T(8,128)(2,1)S(1)} %pad_maximum_fusion.refs_0_), channel_id=1, source_target_pairs={{0,16},{1,17},{2,18},{3,19},{4,20},{5,21},{6,22},{7,23},{8,24},{9,... | collective-permute-start | bytes 1671176 | tf_op jit(solution)/shard_map/ppermute | solution.py:320
  23.5 9.7 %collective-permute-done.1 = bf16[256,1024]{1,0:T(8,128)(2,1)} collective-permute-done((bf16[256,1024]{1,0:T(8,128)(2,1)S(1)}, bf16[256,1024]{1,0:T(8,128)(2,1)}, u32[]{:S(2)}, u32[]{:S(2)}) %collective-permute-start.1) | collective-permute-done | bytes 524320 | tf_op jit(solution)/shard_map/ppermute | solution.py:320
  33.2 1.2 %select_select_fusion = (bf16[256,1024]{1,0:T(8,128)(2,1)S(1)}, bf16[256,1024]{1,0:T(8,128)(2,1)S(1)}) fusion(bf16[256,1024]{1,0:T(8,128)(2,1)S(1)} %bitcast.42, bf16[256,1024]{1,0:T(8,128)(2,1)S(1)} %collective-permute-done, bf16[256,1024]{1,0:T(8,128)(2,1)} %collective-permute-done.1, pred[]{:T(512)S(6)} %eq.76, pred[]{:T(512)S(6)} %eq.75, pred[]{:T(512)S(6)} %eq.67, ...), kind=kLoop, calls=%fused_computation.2 | loop fusion | flops 1048576 | bytes 2621444 | tf_op jit(solution)/shard_map/jit(_where)/select_n | solution.py:346
  36.0 1.2 %copy-done.3 = bf16[128,4096]{1,0:T(8,128)(2,1)S(1)} copy-done((bf16[128,4096]{1,0:T(8,128)(2,1)S(1)}, bf16[128,4096]{1,0:T(8,128)(2,1)}, u32[]{:S(2)}) %copy-start.3) | copy-done | bytes 1048600
  37.2 8.1 %short_range.1.refs_3_.refs_1_ = f32[2048,512]{1,0:T(8,128)S(1)} custom-call(s32[1]{0:T(128)} %bitcast.10.half_ref, s32[32]{0:T(128)S(1)} %get-tuple-element.37.live_ref, s32[32]{0:T(128)S(1)} %get-tuple-element.36.sub_ref, f32[3,32]{1,0:T(4,128)S(1)} %pad_maximum_fusion.1.meta_ref, bf16[128,4096]{1,0:T(8,128)(2,1)S(1)} %copy-done.3, ...), custom_call_target="tpu_custom_call" | custom-call | flops 4294967296 | bytes 5242880 | tf_op jit(solution)/shard_map/short_range/pallas_call | solution.py:109
  45.4 1.9 %copy-done = f32[2048,512]{1,0:T(8,128)} copy-done((f32[2048,512]{1,0:T(8,128)}, f32[2048,512]{1,0:T(8,128)S(1)}, u32[]{:S(2)}) %copy-start) | copy-done | bytes 4194328
  47.4 1.2 %select_select_fusion.1 = (bf16[256,1024]{1,0:T(8,128)(2,1)S(1)}, bf16[256,1024]{1,0:T(8,128)(2,1)S(1)}) fusion(bf16[256,1024]{1,0:T(8,128)(2,1)S(1)} %collective-permute-done, bf16[256,1024]{1,0:T(8,128)(2,1)} %collective-permute-done.1, bf16[256,1024]{1,0:T(8,128)(2,1)S(1)} %collective-permute-done.2, pred[]{:T(512)S(6)} %eq.74, pred[]{:T(512)S(6)} %eq.73, ...), kind=kLoop, calls=%fused_computation.3 | loop fusion | flops 1048576 | bytes 2621444 | tf_op jit(solution)/shard_map/jit(_where)/select_n | solution.py:346
  48.6 1.1 %collective-permute-start.8 = (bf16[256,1024]{1,0:T(8,128)(2,1)S(1)}, bf16[256,1024]{1,0:T(8,128)(2,1)S(1)}, u32[]{:S(2)}, u32[]{:S(2)}) collective-permute-start(bf16[256,1024]{1,0:T(8,128)(2,1)S(1)} %get-tuple-element.23), channel_id=1, source_target_pairs={{0,16},{1,17},{2,18},{3,19},{4,20},{5,21},{6,22},{7,23},{8,24},{9,... | collective-permute-start | bytes 1572872 | tf_op jit(solution)/shard_map/ppermute | solution.py:320
  50.1 10.1 %collective-permute-done.8.refs_1_ = bf16[256,1024]{1,0:T(8,128)(2,1)S(1)} collective-permute-done((bf16[256,1024]{1,0:T(8,128)(2,1)S(1)}, bf16[256,1024]{1,0:T(8,128)(2,1)S(1)}, u32[]{:S(2)}, u32[]{:S(2)}) %collective-permute-start.8) | collective-permute-done | bytes 524320 | tf_op jit(solution)/shard_map/ppermute | solution.py:320
  60.3 4.2 %long_range.3 = (f32[512,512]{1,0:T(8,128)S(1)}, bf16[512,512]{1,0:T(8,128)(2,1)}) custom-call(bf16[256,1024]{1,0:T(8,128)(2,1)S(1)} %get-tuple-element.25.refs_0_, bf16[256,1024]{1,0:T(8,128)(2,1)S(1)} %collective-permute-done.7.refs_1_, bf16[256,1024]{1,0:T(8,128)(2,1)S(1)} %collective-permute-done.12.refs_2_, ...), custom_call_target="tpu_custom_call" | custom-call | flops 2147483648 | bytes 5767168 | tf_op jit(solution)/shard_map/long_range/pallas_call | solution.py:170
  64.5 2.3 %collective-permute-start.14 = (bf16[512,512]{1,0:T(8,128)(2,1)}, bf16[512,512]{1,0:T(8,128)(2,1)S(1)}, u32[]{:S(2)}, u32[]{:S(2)}) collective-permute-start(bf16[512,512]{1,0:T(8,128)(2,1)} %get-tuple-element.27), channel_id=1, source_target_pairs={{0,2},{1,3},{2,0},{3,1},{4,6},{5,7},{6,4},{7,5},{8,10},{9,11},{10,... | collective-permute-start | bytes 1572872 | tf_op jit(solution)/shard_map/ppermute | solution.py:320
  66.8 4.2 %long_range.2 = (f32[512,512]{1,0:T(8,128)S(1)}, bf16[512,512]{1,0:T(8,128)(2,1)}) custom-call(bf16[256,1024]{1,0:T(8,128)(2,1)S(1)} %get-tuple-element.22.refs_0_, bf16[256,1024]{1,0:T(8,128)(2,1)S(1)} %collective-permute-done.8.refs_1_, bf16[256,1024]{1,0:T(8,128)(2,1)S(1)} %collective-permute-done.9.refs_2_, ...), custom_call_target="tpu_custom_call" | custom-call | flops 2147483648 | bytes 5767168 | tf_op jit(solution)/shard_map/long_range/pallas_call | solution.py:170
  71.2 8.6 %collective-permute-done.14.refs_1_ = bf16[512,512]{1,0:T(8,128)(2,1)S(1)} collective-permute-done((bf16[512,512]{1,0:T(8,128)(2,1)}, bf16[512,512]{1,0:T(8,128)(2,1)S(1)}, u32[]{:S(2)}, u32[]{:S(2)}) %collective-permute-start.14) | collective-permute-done | bytes 524320 | tf_op jit(solution)/shard_map/ppermute | solution.py:320
  79.8 2.2 %copy-done.1 = f32[2048,512]{1,0:T(8,128)S(1)} copy-done((f32[2048,512]{1,0:T(8,128)S(1)}, f32[2048,512]{1,0:T(8,128)}, u32[]{:S(2)}) %copy-start.1) | copy-done | bytes 4194328
  82.0 4.9 %final_sum.2.refs_2_ = bf16[2048,2,256]{2,1,0:T(2,128)(2,1)} custom-call(s32[6]{0:T(128)S(1)} %stack.62.order_ref, f32[512,512]{1,0:T(8,128)S(1)} %get-tuple-element.26.refs_0_, bf16[512,512]{1,0:T(8,128)(2,1)S(1)} %collective-permute-done.14.refs_1_, f32[512,512]{1,0:T(8,128)S(1)} %get-tuple-element.28.refs_2_, f32[2048,512]{1,0:T(8,128)S(1)} %copy-done.1), custom_call_target="tpu_custom_call" | custom-call | flops 786432 | bytes 6291456 | tf_op jit(solution)/shard_map/final_sum/pallas_call | solution.py:208
  86.9 3.9 %collective-permute-done.11.refs_0_ = bf16[512,512]{1,0:T(8,128)(2,1)S(1)} collective-permute-done((bf16[512,512]{1,0:T(8,128)(2,1)}, bf16[512,512]{1,0:T(8,128)(2,1)S(1)}, u32[]{:S(2)}, u32[]{:S(2)}) %collective-permute-start.11) | collective-permute-done | bytes 524320 | tf_op jit(solution)/shard_map/ppermute | solution.py:320
  90.8 2.4 %final_sum.3 = bf16[2048,2,256]{2,1,0:T(2,128)(2,1)} custom-call(s32[2]{0:T(128)S(1)} %pad_add_fusion.2.order_ref, bf16[512,512]{1,0:T(8,128)(2,1)S(1)} %collective-permute-done.11.refs_0_, f32[2048,512]{1,0:T(8,128)S(1)} %copy-done.2, bf16[2048,2,256]{2,1,0:T(2,128)(2,1)} %final_sum.2.refs_2_), custom_call_target="tpu_custom_call", output_to_operand_aliasing={{}: (3, {})} | custom-call | flops 262144 | bytes 2097152 | tf_op jit(solution)/shard_map/final_sum/pallas_call | solution.py:208
  (52 shorter events, 5.4 us)
Async XLA Ops:
  0.0 18.2 %copy-start.7 = (s32[16]{0:T(128)S(1)}, s32[16]{0:T(128)}, u32[]{:S(2)}) copy-start(s32[16]{0:T(128)} %param.20) | copy-start | bytes 196
  0.0 18.2 %copy-start.8 = (s32[16]{0:T(128)S(1)}, s32[16]{0:T(128)}, u32[]{:S(2)}) copy-start(s32[16]{0:T(128)} %param.19) | copy-start | bytes 196
  1.1 17.0 %collective-permute-start = (bf16[256,1024]{1,0:T(8,128)(2,1)S(1)}, bf16[256,1024]{1,0:T(8,128)(2,1)S(1)}, u32[]{:S(2)}, u32[]{:S(2)}) collective-permute-start(bf16[256,1024]{1,0:T(8,128)(2,1)S(1)} %bitcast.41), channel_id=1, source_target_pairs={{0,4},{1,5},{2,6},{3,7},{4,8},{5,9},{6,10},{7,11},{8,12},{9,13},{1... | collective-permute-start | bytes 1572872 | tf_op jit(solution)/shard_map/ppermute | solution.py:320
  6.2 13.4 %collective-permute-start.4 = (bf16[1024,256]{1,0:T(8,128)(2,1)S(1)}, bf16[1024,256]{1,0:T(8,128)(2,1)S(1)}, u32[]{:S(2)}, u32[]{:S(2)}) collective-permute-start(bf16[1024,256]{1,0:T(8,128)(2,1)S(1)} %bitcast.35), channel_id=1, source_target_pairs={{0,2},{1,3},{2,0},{3,1},{4,6},{5,7},{6,4},{7,5},{8,10},{9,11},{10,... | collective-permute-start | bytes 1572872 | tf_op jit(solution)/shard_map/ppermute | solution.py:320
  7.8 13.2 %collective-permute-start.3 = (bf16[1024,256]{1,0:T(8,128)(2,1)S(1)}, bf16[1024,256]{1,0:T(8,128)(2,1)}, u32[]{:S(2)}, u32[]{:S(2)}) collective-permute-start(bf16[1024,256]{1,0:T(8,128)(2,1)S(1)} %bitcast.36), channel_id=1, source_target_pairs={{0,16},{1,17},{2,18},{3,19},{4,20},{5,21},{6,22},{7,23},{8,24},{9,... | collective-permute-start | bytes 1572872 | tf_op jit(solution)/shard_map/ppermute | solution.py:320
  18.2 15.0 %collective-permute-start.1 = (bf16[256,1024]{1,0:T(8,128)(2,1)S(1)}, bf16[256,1024]{1,0:T(8,128)(2,1)}, u32[]{:S(2)}, u32[]{:S(2)}) collective-permute-start(bf16[256,1024]{1,0:T(8,128)(2,1)S(1)} %collective-permute-done), channel_id=1, source_target_pairs={{0,4},{1,5},{2,6},{3,7},{4,8},{5,9},{6,10},{7,11},{8,12},{9,13},{1... | collective-permute-start | bytes 1572872 | tf_op jit(solution)/shard_map/ppermute | solution.py:320
  19.5 16.2 %copy-start.9 = (f32[125]{0:T(128)S(1)}, f32[125]{0:T(128)}, u32[]{:S(2)}) copy-start(f32[125]{0:T(128)} %param.16) | copy-start | bytes 1504
  19.5 16.2 %copy-start.10 = (f32[125]{0:T(128)S(1)}, f32[125]{0:T(128)}, u32[]{:S(2)}) copy-start(f32[125]{0:T(128)} %param.17) | copy-start | bytes 1504
  19.6 16.5 %copy-start.6 = (f32[4096]{0:T(1024)S(1)}, f32[4096]{0:T(1024)}, u32[]{:S(2)}) copy-start(f32[4096]{0:T(1024)} %param.15) | copy-start | bytes 49156
  21.0 13.3 %collective-permute-start.5 = (bf16[17,128,128]{2,1,0:T(8,128)(2,1)S(1)}, bf16[17,128,128]{2,1,0:T(8,128)(2,1)S(1)}, u32[]{:S(2)}, u32[]{:S(2)}) collective-permute-start(bf16[17,128,128]{2,1,0:T(8,128)(2,1)S(1)} %pad_maximum_fusion.refs_0_), channel_id=1, source_target_pairs={{0,16},{1,17},{2,18},{3,19},{4,20},{5,21},{6,22},{7,23},{8,24},{9,... | collective-permute-start | bytes 1671176 | tf_op jit(solution)/shard_map/ppermute | solution.py:320
  22.5 12.2 %collective-permute-start.6 = (bf16[1024,256]{1,0:T(8,128)(2,1)}, bf16[1024,256]{1,0:T(8,128)(2,1)S(1)}, u32[]{:S(2)}, u32[]{:S(2)}) collective-permute-start(bf16[1024,256]{1,0:T(8,128)(2,1)} %collective-permute-done.3.refs_5_), channel_id=1, source_target_pairs={{0,2},{1,3},{2,0},{3,1},{4,6},{5,7},{6,4},{7,5},{8,10},{9,11},{10,... | collective-permute-start | bytes 1572872 | tf_op jit(solution)/shard_map/ppermute | solution.py:320
  33.2 14.2 %collective-permute-start.2 = (bf16[256,1024]{1,0:T(8,128)(2,1)}, bf16[256,1024]{1,0:T(8,128)(2,1)S(1)}, u32[]{:S(2)}, u32[]{:S(2)}) collective-permute-start(bf16[256,1024]{1,0:T(8,128)(2,1)} %collective-permute-done.1), channel_id=1, source_target_pairs={{0,4},{1,5},{2,6},{3,7},{4,8},{5,9},{6,10},{7,11},{8,12},{9,13},{1... | collective-permute-start | bytes 1572872 | tf_op jit(solution)/shard_map/ppermute | solution.py:320
  34.7 12.6 %collective-permute-start.7 = (bf16[256,1024]{1,0:T(8,128)(2,1)S(1)}, bf16[256,1024]{1,0:T(8,128)(2,1)S(1)}, u32[]{:S(2)}, u32[]{:S(2)}) collective-permute-start(bf16[256,1024]{1,0:T(8,128)(2,1)S(1)} %get-tuple-element.18), channel_id=1, source_target_pairs={{0,16},{1,17},{2,18},{3,19},{4,20},{5,21},{6,22},{7,23},{8,24},{9,... | collective-permute-start | bytes 1572872 | tf_op jit(solution)/shard_map/ppermute | solution.py:320
  45.4 2.0 %copy-start = (f32[2048,512]{1,0:T(8,128)}, f32[2048,512]{1,0:T(8,128)S(1)}, u32[]{:S(2)}) copy-start(f32[2048,512]{1,0:T(8,128)S(1)} %short_range.1.refs_3_.refs_1_) | copy-start | bytes 12582916
  47.3 13.0 %copy-start.5 = (bf16[1024,256]{1,0:T(8,128)(2,1)S(1)}, bf16[1024,256]{1,0:T(8,128)(2,1)}, u32[]{:S(2)}) copy-start(bf16[1024,256]{1,0:T(8,128)(2,1)} %copy-done.4) | copy-start | bytes 1572868
  48.6 11.7 %collective-permute-start.8 = (bf16[256,1024]{1,0:T(8,128)(2,1)S(1)}, bf16[256,1024]{1,0:T(8,128)(2,1)S(1)}, u32[]{:S(2)}, u32[]{:S(2)}) collective-permute-start(bf16[256,1024]{1,0:T(8,128)(2,1)S(1)} %get-tuple-element.23), channel_id=1, source_target_pairs={{0,16},{1,17},{2,18},{3,19},{4,20},{5,21},{6,22},{7,23},{8,24},{9,... | collective-permute-start | bytes 1572872 | tf_op jit(solution)/shard_map/ppermute | solution.py:320
  49.6 10.7 %collective-permute-start.12 = (bf16[256,1024]{1,0:T(8,128)(2,1)S(1)}, bf16[256,1024]{1,0:T(8,128)(2,1)S(1)}, u32[]{:S(2)}, u32[]{:S(2)}) collective-permute-start(bf16[256,1024]{1,0:T(8,128)(2,1)S(1)} %get-tuple-element.25.refs_0_), channel_id=1, source_target_pairs={{0,1},{1,0},{2,3},{3,2},{4,5},{5,4},{6,7},{7,6},{8,9},{9,8},{10,11... | collective-permute-start | bytes 1572872 | tf_op jit(solution)/shard_map/ppermute | solution.py:320
  49.6 10.7 %collective-permute-start.13 = (bf16[256,1024]{1,0:T(8,128)(2,1)S(1)}, bf16[256,1024]{1,0:T(8,128)(2,1)S(1)}, u32[]{:S(2)}, u32[]{:S(2)}) collective-permute-start(bf16[256,1024]{1,0:T(8,128)(2,1)S(1)} %collective-permute-done.7.refs_1_), channel_id=1, source_target_pairs={{0,1},{1,0},{2,3},{3,2},{4,5},{5,4},{6,7},{7,6},{8,9},{9,8},{10,11... | collective-permute-start | bytes 1572872 | tf_op jit(solution)/shard_map/ppermute | solution.py:320
  50.1 16.7 %collective-permute-start.9 = (bf16[256,1024]{1,0:T(8,128)(2,1)S(1)}, bf16[256,1024]{1,0:T(8,128)(2,1)S(1)}, u32[]{:S(2)}, u32[]{:S(2)}) collective-permute-start(bf16[256,1024]{1,0:T(8,128)(2,1)S(1)} %get-tuple-element.22.refs_0_), channel_id=1, source_target_pairs={{0,1},{1,0},{2,3},{3,2},{4,5},{5,4},{6,7},{7,6},{8,9},{9,8},{10,11... | collective-permute-start | bytes 1572872 | tf_op jit(solution)/shard_map/ppermute | solution.py:320
  60.3 6.5 %collective-permute-start.10 = (bf16[256,1024]{1,0:T(8,128)(2,1)S(1)}, bf16[256,1024]{1,0:T(8,128)(2,1)S(1)}, u32[]{:S(2)}, u32[]{:S(2)}) collective-permute-start(bf16[256,1024]{1,0:T(8,128)(2,1)S(1)} %collective-permute-done.8.refs_1_), channel_id=1, source_target_pairs={{0,1},{1,0},{2,3},{3,2},{4,5},{5,4},{6,7},{7,6},{8,9},{9,8},{10,11... | collective-permute-start | bytes 1572872 | tf_op jit(solution)/shard_map/ppermute | solution.py:320
  64.5 15.3 %collective-permute-start.14 = (bf16[512,512]{1,0:T(8,128)(2,1)}, bf16[512,512]{1,0:T(8,128)(2,1)S(1)}, u32[]{:S(2)}, u32[]{:S(2)}) collective-permute-start(bf16[512,512]{1,0:T(8,128)(2,1)} %get-tuple-element.27), channel_id=1, source_target_pairs={{0,2},{1,3},{2,0},{3,1},{4,6},{5,7},{6,4},{7,5},{8,10},{9,11},{10,... | collective-permute-start | bytes 1572872 | tf_op jit(solution)/shard_map/ppermute | solution.py:320
  71.0 19.8 %collective-permute-start.11 = (bf16[512,512]{1,0:T(8,128)(2,1)}, bf16[512,512]{1,0:T(8,128)(2,1)S(1)}, u32[]{:S(2)}, u32[]{:S(2)}) collective-permute-start(bf16[512,512]{1,0:T(8,128)(2,1)} %get-tuple-element.24), channel_id=1, source_target_pairs={{0,2},{1,3},{2,0},{3,1},{4,6},{5,7},{6,4},{7,5},{8,10},{9,11},{10,... | collective-permute-start | bytes 1572872 | tf_op jit(solution)/shard_map/ppermute | solution.py:320
  79.8 2.2 %copy-start.1 = (f32[2048,512]{1,0:T(8,128)S(1)}, f32[2048,512]{1,0:T(8,128)}, u32[]{:S(2)}) copy-start(f32[2048,512]{1,0:T(8,128)} %copy-done) | copy-start | bytes 12582916
  82.0 8.9 %copy-start.2 = (f32[2048,512]{1,0:T(8,128)S(1)}, f32[2048,512]{1,0:T(8,128)}, u32[]{:S(2)}) copy-start(f32[2048,512]{1,0:T(8,128)} %copy-done) | copy-start | bytes 12582916
  (2 other events, 2.0 us)

commit v4 on v3

--- a/solution.py
+++ b/solution.py
@@ -10,19 +10,22 @@
 AXES = ("grp", "dev")
 CORES = 2
 GROUP_ITEMS = 4
-VMEM_BYTES = 20 * 1024 * 1024
+SHORT_VMEM_BYTES = 28 * 1024 * 1024
+VMEM_BYTES = 16 * 1024 * 1024
 
 
 def short_kernel(
     half_ref, live_ref, sub_ref, meta_ref, basis_ref, decay_ref, *refs, share, subs, depth, width
 ):
-    items, (out_ref, basis_f32, left, acc, dists, group_sub, cursor) = refs[:-7], refs[-7:]
+    items, scratch = refs[:-11], refs[-11:]
+    out_ref, basis, basis_f32, left, acc, made, dists, group_sub, cursor, basis_sem, out_sem = scratch
     slots = share * len(items)
     row_count = out_ref.shape[0]
+    mine = pl.ds(pl.multiple_of(half_ref[0] * row_count, row_count), row_count)
+    basis_copy = pltpu.make_async_copy(basis_ref.at[:, mine], basis, basis_sem)
+    basis_copy.start()
     left[...] = jnp.zeros_like(left)
     acc[...] = jnp.zeros_like(acc)
-    mine = pl.ds(pl.multiple_of(half_ref[0] * row_count, row_count), row_count)
-    basis_f32[...] = basis_ref[:, mine].astype(jnp.float32)
 
     for s in range(subs):
         cursor[s] = 0
@@ -71,8 +74,10 @@
 
         lax.fori_loop(0, share, place, 0)
 
-    tile = min(row_count, 512)
+    tile = min(row_count, made.shape[1])
     decay = decay_ref[:, mine]
+    basis_copy.wait()
+    basis_f32[...] = basis[...].astype(jnp.float32)
 
     def one_group(group, carry):
         s = group_sub[group]
@@ -91,13 +96,18 @@
         return carry
 
     lax.fori_loop(0, first, one_group, 0)
-    for s in range(subs):
-        for c in range(2):
-            column = (c * subs + s) * width
-            for t in range(0, row_count, tile):
-                out_ref[t : t + tile, column : column + width] = acc[
+    copies = []
+    for n, t in enumerate(range(0, row_count, tile)):
+        for s in range(subs):
+            for c in range(2):
+                column = (c * subs + s) * width
+                made[n, :, column : column + width] = acc[
                     s, c * width : (c + 1) * width, t : t + tile
                 ].T
+        copies.append(pltpu.make_async_copy(made.at[n], out_ref.at[pl.ds(t, tile), :], out_sem.at[n]))
+        copies[-1].start()
+    for copy in copies:
+        copy.wait()
 
 
 def short_range(half, live, sub_ids, meta, aux_basis, aux_decay, items, row_count, subs):
@@ -105,22 +115,28 @@
     slots = live.shape[0]
     share = slots // len(items)
     groups = slots // GROUP_ITEMS + subs
+    tile = min(row_count, 512)
     kernel = functools.partial(short_kernel, share=share, subs=subs, depth=depth, width=width)
     return pl.pallas_call(
         kernel,
         out_shape=jax.ShapeDtypeStruct((row_count, 2 * subs * width), jnp.float32),
         in_specs=[pl.BlockSpec(memory_space=pltpu.SMEM)] * 4
-        + [pl.BlockSpec(memory_space=pltpu.VMEM)] * (2 + len(items)),
-        out_specs=pl.BlockSpec(memory_space=pltpu.VMEM),
+        + [pl.BlockSpec(memory_space=pltpu.HBM)]
+        + [pl.BlockSpec(memory_space=pltpu.VMEM)] * (1 + len(items)),
+        out_specs=pl.BlockSpec(memory_space=pltpu.HBM),
         scratch_shapes=[
+            pltpu.VMEM((depth, row_count), jnp.bfloat16),
             pltpu.VMEM((depth, row_count), jnp.float32),
             pltpu.VMEM((groups, 2 * width, GROUP_ITEMS * depth), jnp.bfloat16),
             pltpu.VMEM((subs, 2 * width, row_count), jnp.float32),
+            pltpu.VMEM((row_count // tile, tile, 2 * subs * width), jnp.float32),
             pltpu.SMEM((groups * GROUP_ITEMS,), jnp.float32),
             pltpu.SMEM((groups,), jnp.int32),
             pltpu.SMEM((subs,), jnp.int32),
+            pltpu.SemaphoreType.DMA,
+            pltpu.SemaphoreType.DMA((row_count // tile,)),
         ],
-        compiler_params=pltpu.CompilerParams(vmem_limit_bytes=VMEM_BYTES),
+        compiler_params=pltpu.CompilerParams(vmem_limit_bytes=SHORT_VMEM_BYTES),
         cost_estimate=pl.CostEstimate(
             flops=2 * row_count * slots * depth * width * 2,
             bytes_accessed=row_count * 2 * subs * width * 4 + slots * depth * width * 2,
@@ -130,72 +146,75 @@
     )(half, live, sub_ids, meta, aux_basis, aux_decay.reshape(1, -1), *items)
 
 
-def long_kernel(*refs, blocks, chains, pieces):
+def long_kernel(*refs, blocks, chains, window):
     parts = refs[: blocks * chains]
-    factors = refs[blocks * chains : (blocks + pieces) * chains]
-    outs = refs[(blocks + pieces) * chains : -1]
-    left = refs[-1]
-    rows, depth = parts[0].shape
+    factors = refs[blocks * chains : (blocks + 1) * chains]
+    out_ref, right = refs[-2:]
+    depth, width = factors[0].shape
     half = depth // 2
-    for block in range(blocks):
-        top = block * rows
-        low = (blocks + block) * rows
-        for chain in range(chains):
-            part = parts[block * chains + chain]
-            at = chain * depth
-            left[top : top + rows, at : at + depth] = part[...]
-            left[low : low + rows, at : at + half] = -part[:, half:]
-            left[low : low + rows, at + half : at + depth] = part[:, 0:half]
-    for piece in reversed(range(pieces)):
-        total = None
-        for chain in range(chains):
-            term = jnp.dot(
-                left[:, chain * depth : (chain + 1) * depth],
-                factors[piece * chains + chain][...],
-                preferred_element_type=jnp.float32,
+    for chain, factor in enumerate(factors):
+        top = chain * depth
+        right[top : top + depth, 0:width] = factor[...]
+        right[top : top + half, width:] = factor[half:, :]
+        right[top + half : top + depth, width:] = -factor[0:half, :]
+    left = jnp.concatenate(
+        [
+            jnp.concatenate(
+                [
+                    parts[block * chains + chain][pl.ds(window[chain], window[-1]), :]
+                    for block in range(blocks)
+                ],
+                axis=0,
             )
-            total = term if total is None else total + term
-        width = total.shape[1]
-        outs[piece][:, 0:width] = total[0 : blocks * rows].astype(outs[piece].dtype)
-        outs[piece][:, width:] = total[blocks * rows :].astype(outs[piece].dtype)
-
-
-def long_range(blocks, factors, out_dtypes):
-    rows, depth = blocks[0][0].shape
-    width = factors[0][0].shape[1]
-    chains = len(blocks[0])
-    pieces = len(factors)
-    all_rows = len(blocks) * rows
-    flat = [v for group in blocks + factors for v in group]
+            for chain in range(chains)
+        ],
+        axis=1,
+    )
+    out_ref[...] = jnp.dot(left, right[...], preferred_element_type=jnp.float32).astype(out_ref.dtype)
+
+
+def long_range(blocks, factors, window, dtype):
+    depth, width = factors[0].shape
+    chains = len(factors)
+    all_rows = len(blocks) * window[-1]
+    flat = [v for group in blocks for v in group] + list(factors)
     return pl.pallas_call(
-        functools.partial(long_kernel, blocks=len(blocks), chains=chains, pieces=pieces),
-        out_shape=[jax.ShapeDtypeStruct((all_rows, 2 * width), dtype) for dtype in out_dtypes],
+        functools.partial(long_kernel, blocks=len(blocks), chains=chains, window=window),
+        out_shape=jax.ShapeDtypeStruct((all_rows, 2 * width), dtype),
         in_specs=[pl.BlockSpec(memory_space=pltpu.VMEM)] * len(flat),
-        out_specs=[pl.BlockSpec(memory_space=pltpu.VMEM)] * pieces,
-        scratch_shapes=[pltpu.VMEM((2 * all_rows, chains * depth), jnp.bfloat16)],
+        out_specs=pl.BlockSpec(memory_space=pltpu.VMEM),
+        scratch_shapes=[pltpu.VMEM((chains * depth, 2 * width), jnp.bfloat16)],
         compiler_params=pltpu.CompilerParams(vmem_limit_bytes=VMEM_BYTES),
         cost_estimate=pl.CostEstimate(
-            flops=2 * 2 * all_rows * depth * chains * width * pieces,
-            bytes_accessed=2 * len(flat) * rows * depth + 6 * all_rows * 2 * width,
+            flops=2 * all_rows * depth * chains * 2 * width,
+            bytes_accessed=2 * chains * depth * (all_rows + width) + 4 * all_rows * width,
             transcendentals=0,
         ),
         name="long_range",
     )(*flat)
 
 
-def final_kernel(order_ref, *refs, pieces, blocks):
-    short_ref, out_ref = refs[pieces], refs[-1]
-    rows, _, width = out_ref.shape
-    for n in range(pieces * blocks):
-
-        @pl.when(pl.program_id(0) == n)
-        def _(n=n):
-            top = n % blocks * rows
-            window = pl.ds(pl.multiple_of(order_ref[n] * rows, rows), rows)
-            piece = refs[n // blocks][top : top + rows, :].astype(jnp.float32)
-            total = (piece + short_ref[window, :]).astype(out_ref.dtype)
-            out_ref[:, 0, :] = total[:, 0:width]
-            out_ref[:, 1, :] = total[:, width:]
+def final_kernel(order_ref, *refs, pieces, blocks, rows, aliased):
+    short_ref = refs[pieces]
+    out_ref, terms, made, term_sem, out_sem = refs[pieces + 1 + aliased :]
+    steps = pieces * blocks
+    windows = [pl.ds(pl.multiple_of(order_ref[n] * rows, rows), rows) for n in range(steps)]
+    arriving = []
+    for n, window in enumerate(windows):
+        arriving.append(
+            pltpu.make_async_copy(short_ref.at[window, :], terms.at[n], term_sem.at[n])
+        )
+        arriving[-1].start()
+    leaving = []
+    for n, window in enumerate(windows):
+        arriving[n].wait()
+        top = n % blocks * rows
+        total = refs[n // blocks][top : top + rows, :].astype(jnp.float32) + terms[n]
+        made[n] = total.astype(made.dtype).reshape(made.shape[1:])
+        leaving.append(pltpu.make_async_copy(made.at[n], out_ref.at[window], out_sem.at[n]))
+        leaving[-1].start()
+    for copy in leaving:
+        copy.wait()
 
 
 def final_sum(order, pieces, short, earlier, rows):
@@ -204,24 +223,27 @@
     count = len(pieces)
     blocks = pieces[0].shape[0] // rows
     steps = count * blocks
-    whole = pl.BlockSpec(memory_space=pltpu.VMEM)
+    aliased = earlier is not None
     return pl.pallas_call(
-        functools.partial(final_kernel, pieces=count, blocks=blocks),
+        functools.partial(final_kernel, pieces=count, blocks=blocks, rows=rows, aliased=aliased),
         out_shape=jax.ShapeDtypeStruct((row_count, 2, columns // 2), jnp.bfloat16),
-        grid_spec=pltpu.PrefetchScalarGridSpec(
-            num_scalar_prefetch=1,
-            grid=(steps,),
-            in_specs=[whole] * (count + 1)
-            + [pl.BlockSpec(memory_space=pl.ANY)] * (earlier is not None),
-            out_specs=pl.BlockSpec((rows, 2, columns // 2), lambda n, order: (order[n], 0, 0)),
-        ),
-        input_output_aliases={count + 2: 0} if earlier is not None else {},
+        in_specs=[pl.BlockSpec(memory_space=pltpu.SMEM)]
+        + [pl.BlockSpec(memory_space=pltpu.VMEM)] * count
+        + [pl.BlockSpec(memory_space=pltpu.HBM)] * (1 + aliased),
+        out_specs=pl.BlockSpec(memory_space=pltpu.HBM),
+        scratch_shapes=[
+            pltpu.VMEM((steps, rows, columns), jnp.float32),
+            pltpu.VMEM((steps, rows, 2, columns // 2), jnp.bfloat16),
+            pltpu.SemaphoreType.DMA((steps,)),
+            pltpu.SemaphoreType.DMA((steps,)),
+        ],
+        input_output_aliases={count + 2: 0} if aliased else {},
         compiler_params=pltpu.CompilerParams(vmem_limit_bytes=VMEM_BYTES),
         cost_estimate=pl.CostEstimate(
             flops=steps * rows * columns, bytes_accessed=steps * rows * columns * 8, transcendentals=0
         ),
         name="final_sum",
-    )(order, *pieces, short, *([earlier] if earlier is not None else []))
+    )(order, *pieces, short, *([earlier] if aliased else []))
 
 
 def slot_table(image_dist, image_phase, images):
@@ -322,8 +344,11 @@
     def to_plane(value):
         return send(value, lambda g, z, y, c: (1 - g, z, y, c))
 
+    ring = [*range(0, length, 2), *reversed(range(1, length, 2))]
+    turn = {z: n for n, z in enumerate(ring)}
+
     def along(value):
-        return send(value, lambda g, z, y, c: (g, (z + 1) % length, y, c))
+        return send(value, lambda g, z, y, c: (g, ring[(turn[z] + 1) % length], y, c))
 
     def over_y(value, s):
         return send(value, lambda g, z, y, c: (g, z, (y + s) % breadth, c))
@@ -332,19 +357,33 @@
         return send(value, lambda g, z, y, c: (g, z, y, (c + t) % CORES))
 
     def hops_of(g, z):
-        return sorted((z - j) % length for j in range(g * home, (g + 1) * home))
-
-    def pick(held, g_of, n):
-        wanted = sum(
-            jnp.where((group == g) & (place == z), hops_of(g_of(g), z)[n], 0)
+        return sorted((turn[z] - turn[j]) % length for j in range(g * home, (g + 1) * home))
+
+    def here(number):
+        return sum(
+            jnp.where((group == g) & (place == z), number(g, z), 0)
             for g in range(group_count)
             for z in range(length)
         )
+
+    def pick(other, n, window, *earlier):
+        wanted = here(lambda g, z: hops_of(g ^ other, z)[n])
         possible = sorted({hops_of(g, z)[n] for g in range(group_count) for z in range(length)})
-        value = held[possible[-1]]
-        for k in reversed(possible[:-1]):
-            value = jnp.where(wanted == k, held[k], value)
-        return value, wanted
+        blocks = lax.optimization_barrier((*(held[k] for k in possible), *earlier))
+        value = blocks[len(possible) - 1][window]
+        for k, block in reversed(list(zip(possible[:-1], blocks))):
+            value = jnp.where(wanted == k, block[window], value)
+        return value
+
+    def numbers_of(n, s):
+        slab = here(lambda g, z: ring[(turn[z] - hops_of(g, z)[n]) % length] - g * home)
+        return [
+            (slab * breadth + (across - s) % breadth) * CORES + (core - t) % CORES
+            for t in range(CORES)
+        ]
+
+    def with_cores(value):
+        return [value] + [over_core(value, t) for t in range(1, CORES)]
 
     held = [aux_flat]
     held.append(along(held[0]))
@@ -363,36 +402,64 @@
         half, live, sub_ids, table, aux_basis, aux_decay, [packed, items_x], row_count, subs
     )
 
-    ready = []
-    order = []
+    parts = 2 if rows % 32 == 0 else 1
+    units = [(n, 0, rows) for n in range(home - 1)]
+    units += [(home - 1, k * (rows // parts), rows // parts) for k in range(parts)]
+    mine = {}
+    theirs = []
+    crossed = []
+    away = []
+    arriving = []
+    own = []
+
+    def product(i, s, *earlier):
+        n, first, count = units[i]
+        blocks = list(zip(mine[n], [after(crossed[i][0], *earlier), *crossed[i][1:]]))
+        return long_range(blocks, factors[s], (first, 0, count), jnp.bfloat16 if s else jnp.float32)
+
+    def multiply(i, *earlier):
+        away.append([product(i, s, *earlier) for s in range(1, breadth)])
+        arriving.append([over_y(v, s) for s, v in enumerate(away[i], 1)])
+
+    for i, (n, first, count) in enumerate(units):
+        if i == 0:
+            gate = [items_x, *(pair[1] for pair in factors[1:])]
+        elif i == 1:
+            gate = [crossed[0][0], short]
+        else:
+            gate = away[i - 2]
+        theirs.append(pick(True, n, slice(first, first + count), *gate))
+        moved = to_plane(theirs[i])
+        if first + count == rows:
+            mine[n] = with_cores(pick(False, n, slice(None), theirs[i]))
+        if i:
+            multiply(i - 1)
+        crossed.append(with_cores(after(moved, *away[i - 1] if i else [short])))
+        if i > 1:
+            own.append(product(i - 2, 0, theirs[i]))
+    last = len(units) - 1
+    multiply(last, *(arriving[0] if last > 1 else []))
+    if last:
+        own.append(product(last - 1, 0, crossed[last][0]))
+    own.append(product(last, 0))
+
+    def place_of(piece, i, s):
+        n, first, count = units[i]
+        return piece, [v * (rows // count) + first // count for v in numbers_of(n, s)]
+
+    calls = []
+    for i, (_, _, count) in enumerate(units):
+        here_now = [place_of(own[i], i, 0)]
+        arrived = [place_of(v, i, s) for s, v in enumerate(arriving[i], 1)]
+        for entries in [here_now + arrived] if i < last else [here_now, arrived]:
+            if calls and calls[-1][0] == count and entries is not arrived:
+                calls[-1][1].extend(entries)
+            elif entries:
+                calls.append((count, entries))
     out = None
-    latest = [items_x] + [pair[1] for pair in factors[1:]]
-    for n in range(home):
-        if n:
-            held = lax.optimization_barrier((*held, *latest, short))[:length]
-        mine, hops = pick(held, lambda g: g, n)
-        theirs, _ = pick(held, lambda g: 1 - g, n)
-        crossed = to_plane(after(theirs, *latest))
-        latest = [crossed]
-        blocks = [[after(mine, short), crossed]]
-        for t in range(1, CORES):
-            blocks.append([over_core(v, t) for v in blocks[0]])
-        made = long_range(
-            blocks, factors, [jnp.float32 if s == 0 else jnp.bfloat16 for s in range(breadth)]
-        )
-        slab = (place - hops) % length - group * home
-        for s in range(breadth):
-            piece = over_y(made[s], s) if s else made[s]
-            numbers = [
-                (slab * breadth + (across - s) % breadth) * CORES + (core - t) % CORES
-                for t in range(CORES)
-            ]
-            ready.append(piece)
-            order.append(numbers)
-    last = breadth - 1
-    for chosen in (slice(0, len(ready) - last), slice(len(ready) - last, None)):
-        numbers = jnp.stack([v for group_of in order[chosen] for v in group_of]).astype(jnp.int32)
-        out = final_sum(numbers, ready[chosen], short, out, rows)
+    for count, entries in calls:
+        numbers = jnp.stack([v for _, each in entries for v in each]).astype(jnp.int32)
+        out = final_sum(numbers, [piece for piece, _ in entries], short, out, count)
     return out
 
 

time: 93.8 us -> 93.3 us (level)
  waiting for transfers between devices: 41.5 us -> 31 us
  starting transfers between devices: 13.6 us -> 21.4 us
  other arithmetic: 4.23 us -> 8.1 us
  local copies, waits for them, and re-layouts: 9.3 us -> 5.6 us
  Pallas kernels: 23.8 us -> 24.9 us
    ppermute x15 -> x18, waiting for transfers between devices: 41.5 us -> 31 us  [send(): return lax.ppermute(value, AXES, pairs)]
    ppermute x15 -> x18, starting transfers between devices: 13.6 us -> 21.4 us  [send(): return lax.ppermute(value, AXES, pairs)]
    select_n x2 -> x5, other arithmetic: 2.34 us -> 6.13 us  [pick(): value = jnp.where(wanted == k, block[window], value)]
    unnamed x24 -> x46, local copies, waits for them, and re-layouts: 8.62 us -> 4.92 us
    pallas_call x2 -> x6, Pallas kernels: 8.34 us -> 10.7 us  [long_range(): pl.pallas_call(functools.partial(long_kernel, blocks=len(blocks), chains=...]
    pallas_call x2 -> x3, Pallas kernels: 7.33 us -> 6.42 us  [final_sum(): pl.pallas_call(functools.partial(final_kernel, pieces=count, blocks=block...]
  transfers between devices with their start and end apart: 15 -> 18, of which waited for: 7 -> 8; matrix products, arithmetic and copies ran while one was open for 5% -> 10% of each run, Pallas kernels for 23% -> 25%
where the time goes in v4:
time: 93.3 us; the launch traced here: 92.1 us
  waiting for transfers between devices  31 us (33%)
  Pallas kernels  24.9 us (27%)
  starting transfers between devices  21.4 us (23%)
  other arithmetic  8.1 us (9%)
  local copies, waits for them, and re-layouts  5.6 us (6%)
  between operations  1.03 us (1%)
    ppermute x18, waiting for transfers between devices, send(): return lax.ppermute(value, AXES, pairs)  31 us
    ppermute x18, starting transfers between devices, send(): return lax.ppermute(value, AXES, pairs)  21.4 us
    pallas_call x6, Pallas kernels, long_range(): pl.pallas_call(functools.partial(long_kernel, blocks=len(blocks), chains=...  10.7 us
    pallas_call x1, Pallas kernels, short_range(): pl.pallas_call(kernel, out_shape=jax.ShapeDtypeStruct((row_count, 2 * sub...  7.76 us
    pallas_call x3, Pallas kernels, final_sum(): pl.pallas_call(functools.partial(final_kernel, pieces=count, blocks=block...  6.42 us
    select_n x5, other arithmetic, pick(): value = jnp.where(wanted == k, block[window], value)  6.13 us
    unnamed x46, local copies, waits for them, and re-layouts  4.92 us
  transfers between devices with their start and end apart: 18, of which 8 were waited for; matrix products, arithmetic and copies ran while one was open for 10% of the time, Pallas kernels for 25%

profile of v4, /device:TPU:0, one launch (start us, length us, event | category | flops | bytes accessed | tf_op | source)
XLA Modules:
  0.0 92.1 jit_solution(2025964753127508794)
XLA Ops:
  1.2 4.1 %collective-permute-start = (bf16[256,1024]{1,0:T(8,128)(2,1)S(1)}, bf16[256,1024]{1,0:T(8,128)(2,1)}, u32[]{:S(2)}, u32[]{:S(2)}) collective-permute-start(bf16[256,1024]{1,0:T(8,128)(2,1)S(1)} %bitcast.45), channel_id=1, source_target_pairs={{0,8},{1,9},{2,10},{3,11},{4,0},{5,1},{6,2},{7,3},{8,12},{9,13},{1... | collective-permute-start | bytes 1572872 | tf_op jit(solution)/shard_map/ppermute | solution.py:342
  7.3 1.6 %collective-permute-start.3 = (bf16[1024,256]{1,0:T(8,128)(2,1)S(1)}, bf16[1024,256]{1,0:T(8,128)(2,1)S(1)}, u32[]{:S(2)}, u32[]{:S(2)}) collective-permute-start(bf16[1024,256]{1,0:T(8,128)(2,1)S(1)} %bitcast.39), channel_id=1, source_target_pairs={{0,16},{1,17},{2,18},{3,19},{4,20},{5,21},{6,22},{7,23},{8,24},{9,... | collective-permute-start | bytes 1572872 | tf_op jit(solution)/shard_map/ppermute | solution.py:342
  8.8 1.5 %collective-permute-start.4 = (bf16[1024,256]{1,0:T(8,128)(2,1)S(1)}, bf16[1024,256]{1,0:T(8,128)(2,1)S(1)}, u32[]{:S(2)}, u32[]{:S(2)}) collective-permute-start(bf16[1024,256]{1,0:T(8,128)(2,1)S(1)} %bitcast.40), channel_id=1, source_target_pairs={{0,2},{1,3},{2,0},{3,1},{4,6},{5,7},{6,4},{7,5},{8,10},{9,11},{10,... | collective-permute-start | bytes 1572872 | tf_op jit(solution)/shard_map/ppermute | solution.py:342
  11.5 5.0 %collective-permute-done = bf16[256,1024]{1,0:T(8,128)(2,1)} collective-permute-done((bf16[256,1024]{1,0:T(8,128)(2,1)S(1)}, bf16[256,1024]{1,0:T(8,128)(2,1)}, u32[]{:S(2)}, u32[]{:S(2)}) %collective-permute-start) | collective-permute-done | bytes 524320 | tf_op jit(solution)/shard_map/ppermute | solution.py:342
  16.5 4.3 %collective-permute-done.3.refs_5_ = bf16[1024,256]{1,0:T(8,128)(2,1)S(1)} collective-permute-done((bf16[1024,256]{1,0:T(8,128)(2,1)S(1)}, bf16[1024,256]{1,0:T(8,128)(2,1)S(1)}, u32[]{:S(2)}, u32[]{:S(2)}) %collective-permute-start.3) | collective-permute-done | bytes 524320 | tf_op jit(solution)/shard_map/ppermute | solution.py:342
  22.5 1.6 %collective-permute-start.1 = (bf16[256,1024]{1,0:T(8,128)(2,1)}, bf16[256,1024]{1,0:T(8,128)(2,1)}, u32[]{:S(2)}, u32[]{:S(2)}) collective-permute-start(bf16[256,1024]{1,0:T(8,128)(2,1)} %collective-permute-done), channel_id=1, source_target_pairs={{0,8},{1,9},{2,10},{3,11},{4,0},{5,1},{6,2},{7,3},{8,12},{9,13},{1... | collective-permute-start | bytes 1572872 | tf_op jit(solution)/shard_map/ppermute | solution.py:342
  24.1 1.5 %collective-permute-start.6 = (bf16[1024,256]{1,0:T(8,128)(2,1)S(1)}, bf16[1024,256]{1,0:T(8,128)(2,1)S(1)}, u32[]{:S(2)}, u32[]{:S(2)}) collective-permute-start(bf16[1024,256]{1,0:T(8,128)(2,1)S(1)} %collective-permute-done.3.refs_5_), channel_id=1, source_target_pairs={{0,2},{1,3},{2,0},{3,1},{4,6},{5,7},{6,4},{7,5},{8,10},{9,11},{10,... | collective-permute-start | bytes 1572872 | tf_op jit(solution)/shard_map/ppermute | solution.py:342
  25.6 9.2 %collective-permute-done.1 = bf16[256,1024]{1,0:T(8,128)(2,1)} collective-permute-done((bf16[256,1024]{1,0:T(8,128)(2,1)}, bf16[256,1024]{1,0:T(8,128)(2,1)}, u32[]{:S(2)}, u32[]{:S(2)}) %collective-permute-start.1) | collective-permute-done | bytes 524320 | tf_op jit(solution)/shard_map/ppermute | solution.py:342
  34.7 2.5 %collective-permute-start.2 = (bf16[256,1024]{1,0:T(8,128)(2,1)}, bf16[256,1024]{1,0:T(8,128)(2,1)}, u32[]{:S(2)}, u32[]{:S(2)}) collective-permute-start(bf16[256,1024]{1,0:T(8,128)(2,1)} %collective-permute-done.1), channel_id=1, source_target_pairs={{0,8},{1,9},{2,10},{3,11},{4,0},{5,1},{6,2},{7,3},{8,12},{9,13},{1... | collective-permute-start | bytes 1572872 | tf_op jit(solution)/shard_map/ppermute | solution.py:342
  38.6 1.7 %collective-permute-start.7 = (bf16[256,1024]{1,0:T(8,128)(2,1)S(1)}, bf16[256,1024]{1,0:T(8,128)(2,1)}, u32[]{:S(2)}, u32[]{:S(2)}) collective-permute-start(bf16[256,1024]{1,0:T(8,128)(2,1)S(1)} %select_select_fusion.2), channel_id=1, source_target_pairs={{0,16},{1,17},{2,18},{3,19},{4,20},{5,21},{6,22},{7,23},{8,24},{9,... | collective-permute-start | bytes 1572872 | tf_op jit(solution)/shard_map/ppermute | solution.py:342
  42.0 7.8 %short_range.1.refs_2_.refs_3_.refs_1_ = f32[2048,512]{1,0:T(8,128)S(1)} custom-call(s32[1]{0:T(128)} %bitcast.10.half_ref, s32[32]{0:T(128)S(1)} %get-tuple-element.53.live_ref, s32[32]{0:T(128)S(1)} %get-tuple-element.52.sub_ref, f32[3,32]{1,0:T(4,128)S(1)} %pad_maximum_fusion.1.meta_ref, bf16[128,4096]{1,0:T(8,128)(2,1)S(1)} %copy-done.13, ...), custom_call_target="tpu_custom_call" | custom-call | flops 4294967296 | bytes 5242880 | tf_op jit(solution)/shard_map/short_range/pallas_call | solution.py:120
  49.7 2.0 %copy-done = f32[2048,512]{1,0:T(8,128)} copy-done((f32[2048,512]{1,0:T(8,128)}, f32[2048,512]{1,0:T(8,128)S(1)}, u32[]{:S(2)}) %copy-start) | copy-done | bytes 4194328
  54.0 3.3 %long_range.6 = bf16[512,512]{1,0:T(8,128)(2,1)} custom-call(bf16[256,1024]{1,0:T(8,128)(2,1)S(1)} %select_select_fusion.1.refs_0_, bf16[256,1024]{1,0:T(8,128)(2,1)} %collective-permute-done.7.refs_1_, bf16[256,1024]{1,0:T(8,128)(2,1)S(1)} %collective-permute-done.8.refs_2_, bf16[256,1024]{1,0:T(8,128)(2,1)} %collective-permute-done.9.refs_3_, ...), custom_call_target="tpu_custom_call" | custom-call | flops 1073741824 | bytes 3670016 | tf_op jit(solution)/shard_map/long_range/pallas_call | solution.py:181
  62.1 1.5 %collective-permute-start.14 = (bf16[512,512]{1,0:T(8,128)(2,1)}, bf16[512,512]{1,0:T(8,128)(2,1)}, u32[]{:S(2)}, u32[]{:S(2)}) collective-permute-start(bf16[512,512]{1,0:T(8,128)(2,1)} %long_range.6), channel_id=1, source_target_pairs={{0,2},{1,3},{2,0},{3,1},{4,6},{5,7},{6,4},{7,5},{8,10},{9,11},{10,... | collective-permute-start | bytes 1572872 | tf_op jit(solution)/shard_map/ppermute | solution.py:342
  65.8 4.7 %collective-permute-done.10.refs_1_ = bf16[128,1024]{1,0:T(8,128)(2,1)} collective-permute-done((bf16[128,1024]{1,0:T(8,128)(2,1)S(1)}, bf16[128,1024]{1,0:T(8,128)(2,1)}, u32[]{:S(2)}, u32[]{:S(2)}) %collective-permute-start.10) | collective-permute-done | bytes 262176 | tf_op jit(solution)/shard_map/ppermute | solution.py:342
  70.6 1.5 %collective-permute-start.17 = (bf16[256,512]{1,0:T(8,128)(2,1)}, bf16[256,512]{1,0:T(8,128)(2,1)S(1)}, u32[]{:S(2)}, u32[]{:S(2)}) collective-permute-start(bf16[256,512]{1,0:T(8,128)(2,1)} %copy-done.10), channel_id=1, source_target_pairs={{0,2},{1,3},{2,0},{3,1},{4,6},{5,7},{6,4},{7,5},{8,10},{9,11},{10,... | collective-permute-start | bytes 786440 | tf_op jit(solution)/shard_map/ppermute | solution.py:342
  72.2 5.0 %collective-permute-done.14.refs_1_ = bf16[512,512]{1,0:T(8,128)(2,1)} collective-permute-done((bf16[512,512]{1,0:T(8,128)(2,1)}, bf16[512,512]{1,0:T(8,128)(2,1)}, u32[]{:S(2)}, u32[]{:S(2)}) %collective-permute-start.14) | collective-permute-done | bytes 524320 | tf_op jit(solution)/shard_map/ppermute | solution.py:342
  77.2 1.7 %long_range.8 = bf16[256,512]{1,0:T(8,128)(2,1)S(1)} custom-call(bf16[256,1024]{1,0:T(8,128)(2,1)S(1)} %select_select_fusion.refs_0_, bf16[128,1024]{1,0:T(8,128)(2,1)} %collective-permute-done.10.refs_1_, bf16[256,1024]{1,0:T(8,128)(2,1)S(1)} %collective-permute-done.12.refs_2_, bf16[128,1024]{1,0:T(8,128)(2,1)} %collective-permute-done.15.refs_3_, ...), custom_call_target="tpu_custom_call" | custom-call | flops 536870912 | bytes 2359296 | tf_op jit(solution)/shard_map/long_range/pallas_call | solution.py:181
  78.9 1.6 %collective-permute-start.16 = (bf16[256,512]{1,0:T(8,128)(2,1)S(1)}, bf16[256,512]{1,0:T(8,128)(2,1)S(1)}, u32[]{:S(2)}, u32[]{:S(2)}) collective-permute-start(bf16[256,512]{1,0:T(8,128)(2,1)S(1)} %long_range.8), channel_id=1, source_target_pairs={{0,2},{1,3},{2,0},{3,1},{4,6},{5,7},{6,4},{7,5},{8,10},{9,11},{10,... | collective-permute-start | bytes 786440 | tf_op jit(solution)/shard_map/ppermute | solution.py:342
  80.6 2.6 %long_range.11.refs_0_ = f32[512,512]{1,0:T(8,128)S(1)} custom-call(bf16[256,1024]{1,0:T(8,128)(2,1)S(1)} %copy-done.3, bf16[256,1024]{1,0:T(8,128)(2,1)} %collective-permute-done.7.refs_1_, bf16[256,1024]{1,0:T(8,128)(2,1)S(1)} %copy-done.9, bf16[256,1024]{1,0:T(8,128)(2,1)} %collective-permute-done.9.refs_3_, bf16[1024,256]{1,0:T(8,128)(2,1)S(1)} %bitcast.41, ...), custom_call_target="tpu_custom_call" | custom-call | flops 1073741824 | bytes 3670016 | tf_op jit(solution)/shard_map/long_range/pallas_call | solution.py:181
  83.2 2.9 %final_sum.3.refs_4_ = bf16[2048,2,256]{2,1,0:T(2,128)(2,1)} custom-call(s32[4]{0:T(128)S(1)} %pad_add_fusion.3.order_ref, f32[512,512]{1,0:T(8,128)S(1)} %long_range.11.refs_0_, bf16[512,512]{1,0:T(8,128)(2,1)} %collective-permute-done.14.refs_1_, f32[2048,512]{1,0:T(8,128)S(1)} %copy-done.1), custom_call_target="tpu_custom_call" | custom-call | flops 524288 | bytes 4194304 | tf_op jit(solution)/shard_map/final_sum/pallas_call | solution.py:227
  86.8 1.7 %long_range.10.refs_2_ = f32[256,512]{1,0:T(8,128)S(1)} custom-call(bf16[256,1024]{1,0:T(8,128)(2,1)S(1)} %select_select_fusion.refs_0_, bf16[128,1024]{1,0:T(8,128)(2,1)} %collective-permute-done.10.refs_1_, bf16[256,1024]{1,0:T(8,128)(2,1)S(1)} %collective-permute-done.12.refs_2_, bf16[128,1024]{1,0:T(8,128)(2,1)} %collective-permute-done.15.refs_3_, ...), custom_call_target="tpu_custom_call" | custom-call | flops 536870912 | bytes 2359296 | tf_op jit(solution)/shard_map/long_range/pallas_call | solution.py:181
  88.5 2.1 %final_sum.4.refs_2_ = bf16[2048,2,256]{2,1,0:T(2,128)(2,1)} custom-call(s32[6]{0:T(128)S(1)} %stack.77.order_ref, f32[256,512]{1,0:T(8,128)S(1)} %long_range.9.refs_0_, bf16[256,512]{1,0:T(8,128)(2,1)S(1)} %collective-permute-done.17.refs_1_, f32[256,512]{1,0:T(8,128)S(1)} %long_range.10.refs_2_, ...), custom_call_target="tpu_custom_call", output_to_operand_aliasing={{}: (5, {})} | custom-call | flops 393216 | bytes 3145728 | tf_op jit(solution)/shard_map/final_sum/pallas_call | solution.py:227
  90.6 1.5 %final_sum.5 = bf16[2048,2,256]{2,1,0:T(2,128)(2,1)} custom-call(s32[2]{0:T(128)S(1)} %pad_add_fusion.2.order_ref, bf16[256,512]{1,0:T(8,128)(2,1)S(1)} %collective-permute-done.16.refs_0_, f32[2048,512]{1,0:T(8,128)S(1)} %copy-done.1, bf16[2048,2,256]{2,1,0:T(2,128)(2,1)} %final_sum.4.refs_2_), custom_call_target="tpu_custom_call", output_to_operand_aliasing={{}: (3, {})} | custom-call | flops 131072 | bytes 1048576 | tf_op jit(solution)/shard_map/final_sum/pallas_call | solution.py:227
  (89 shorter events, 18.5 us)
Async XLA Ops:
  1.2 15.3 %collective-permute-start = (bf16[256,1024]{1,0:T(8,128)(2,1)S(1)}, bf16[256,1024]{1,0:T(8,128)(2,1)}, u32[]{:S(2)}, u32[]{:S(2)}) collective-permute-start(bf16[256,1024]{1,0:T(8,128)(2,1)S(1)} %bitcast.45), channel_id=1, source_target_pairs={{0,8},{1,9},{2,10},{3,11},{4,0},{5,1},{6,2},{7,3},{8,12},{9,13},{1... | collective-permute-start | bytes 1572872 | tf_op jit(solution)/shard_map/ppermute | solution.py:342
  7.3 13.4 %collective-permute-start.3 = (bf16[1024,256]{1,0:T(8,128)(2,1)S(1)}, bf16[1024,256]{1,0:T(8,128)(2,1)S(1)}, u32[]{:S(2)}, u32[]{:S(2)}) collective-permute-start(bf16[1024,256]{1,0:T(8,128)(2,1)S(1)} %bitcast.39), channel_id=1, source_target_pairs={{0,16},{1,17},{2,18},{3,19},{4,20},{5,21},{6,22},{7,23},{8,24},{9,... | collective-permute-start | bytes 1572872 | tf_op jit(solution)/shard_map/ppermute | solution.py:342
  8.8 13.1 %collective-permute-start.4 = (bf16[1024,256]{1,0:T(8,128)(2,1)S(1)}, bf16[1024,256]{1,0:T(8,128)(2,1)S(1)}, u32[]{:S(2)}, u32[]{:S(2)}) collective-permute-start(bf16[1024,256]{1,0:T(8,128)(2,1)S(1)} %bitcast.40), channel_id=1, source_target_pairs={{0,2},{1,3},{2,0},{3,1},{4,6},{5,7},{6,4},{7,5},{8,10},{9,11},{10,... | collective-permute-start | bytes 1572872 | tf_op jit(solution)/shard_map/ppermute | solution.py:342
  11.0 29.3 %copy-start.20 = (f32[125]{0:T(128)S(1)}, f32[125]{0:T(128)}, u32[]{:S(2)}) copy-start(f32[125]{0:T(128)} %param.16) | copy-start | bytes 1504
  11.0 29.3 %copy-start.21 = (f32[125]{0:T(128)S(1)}, f32[125]{0:T(128)}, u32[]{:S(2)}) copy-start(f32[125]{0:T(128)} %param.17) | copy-start | bytes 1504
  11.5 28.8 %copy-start.6 = (bf16[17,128,128]{2,1,0:T(8,128)(2,1)}, bf16[17,128,128]{2,1,0:T(8,128)(2,1)S(1)}, u32[]{:S(2)}) copy-start(bf16[17,128,128]{2,1,0:T(8,128)(2,1)S(1)} %pad_maximum_fusion.refs_0_) | copy-start | bytes 1671172
  21.9 15.3 %collective-permute-start.5 = (bf16[17,128,128]{2,1,0:T(8,128)(2,1)S(1)}, bf16[17,128,128]{2,1,0:T(8,128)(2,1)S(1)}, u32[]{:S(2)}, u32[]{:S(2)}) collective-permute-start(bf16[17,128,128]{2,1,0:T(8,128)(2,1)S(1)} %pad_maximum_fusion.refs_0_), channel_id=1, source_target_pairs={{0,16},{1,17},{2,18},{3,19},{4,20},{5,21},{6,22},{7,23},{8,24},{9,... | collective-permute-start | bytes 1671176 | tf_op jit(solution)/shard_map/ppermute | solution.py:342
  22.5 12.3 %collective-permute-start.1 = (bf16[256,1024]{1,0:T(8,128)(2,1)}, bf16[256,1024]{1,0:T(8,128)(2,1)}, u32[]{:S(2)}, u32[]{:S(2)}) collective-permute-start(bf16[256,1024]{1,0:T(8,128)(2,1)} %collective-permute-done), channel_id=1, source_target_pairs={{0,8},{1,9},{2,10},{3,11},{4,0},{5,1},{6,2},{7,3},{8,12},{9,13},{1... | collective-permute-start | bytes 1572872 | tf_op jit(solution)/shard_map/ppermute | solution.py:342
  24.1 13.2 %collective-permute-start.6 = (bf16[1024,256]{1,0:T(8,128)(2,1)S(1)}, bf16[1024,256]{1,0:T(8,128)(2,1)S(1)}, u32[]{:S(2)}, u32[]{:S(2)}) collective-permute-start(bf16[1024,256]{1,0:T(8,128)(2,1)S(1)} %collective-permute-done.3.refs_5_), channel_id=1, source_target_pairs={{0,2},{1,3},{2,0},{3,1},{4,6},{5,7},{6,4},{7,5},{8,10},{9,11},{10,... | collective-permute-start | bytes 1572872 | tf_op jit(solution)/shard_map/ppermute | solution.py:342
  25.6 14.9 %copy-start.16 = (bf16[32,8,2,512]{3,1,2,0:T(8,128)(2,1)S(1)}, bf16[32,8,2,512]{3,1,2,0:T(8,128)(2,1)}, u32[]{:S(2)}) copy-start(bf16[32,8,2,512]{3,1,2,0:T(8,128)(2,1)} %copy-done.15) | copy-start | bytes 1572868
  25.6 16.3 %copy-start.13 = (bf16[128,4096]{1,0:T(8,128)(2,1)S(1)}, bf16[128,4096]{1,0:T(8,128)(2,1)}, u32[]{:S(2)}) copy-start(bf16[128,4096]{1,0:T(8,128)(2,1)} %basis_ref.1) | copy-start | bytes 3145732
  25.6 16.3 %copy-start.14 = (f32[4096]{0:T(1024)S(1)}, f32[4096]{0:T(1024)}, u32[]{:S(2)}) copy-start(f32[4096]{0:T(1024)} %param.15) | copy-start | bytes 49156
  34.7 17.4 %collective-permute-start.2 = (bf16[256,1024]{1,0:T(8,128)(2,1)}, bf16[256,1024]{1,0:T(8,128)(2,1)}, u32[]{:S(2)}, u32[]{:S(2)}) collective-permute-start(bf16[256,1024]{1,0:T(8,128)(2,1)} %collective-permute-done.1), channel_id=1, source_target_pairs={{0,8},{1,9},{2,10},{3,11},{4,0},{5,1},{6,2},{7,3},{8,12},{9,13},{1... | collective-permute-start | bytes 1572872 | tf_op jit(solution)/shard_map/ppermute | solution.py:342
  38.6 13.1 %collective-permute-start.7 = (bf16[256,1024]{1,0:T(8,128)(2,1)S(1)}, bf16[256,1024]{1,0:T(8,128)(2,1)}, u32[]{:S(2)}, u32[]{:S(2)}) collective-permute-start(bf16[256,1024]{1,0:T(8,128)(2,1)S(1)} %select_select_fusion.2), channel_id=1, source_target_pairs={{0,16},{1,17},{2,18},{3,19},{4,20},{5,21},{6,22},{7,23},{8,24},{9,... | collective-permute-start | bytes 1572872 | tf_op jit(solution)/shard_map/ppermute | solution.py:342
  41.8 12.0 %collective-permute-start.8 = (bf16[256,1024]{1,0:T(8,128)(2,1)S(1)}, bf16[256,1024]{1,0:T(8,128)(2,1)S(1)}, u32[]{:S(2)}, u32[]{:S(2)}) collective-permute-start(bf16[256,1024]{1,0:T(8,128)(2,1)S(1)} %select_select_fusion.1.refs_0_), channel_id=1, source_target_pairs={{0,1},{1,0},{2,3},{3,2},{4,5},{5,4},{6,7},{7,6},{8,9},{9,8},{10,11... | collective-permute-start | bytes 1572872 | tf_op jit(solution)/shard_map/ppermute | solution.py:342
  51.7 2.3 %collective-permute-start.9 = (bf16[256,1024]{1,0:T(8,128)(2,1)}, bf16[256,1024]{1,0:T(8,128)(2,1)}, u32[]{:S(2)}, u32[]{:S(2)}) collective-permute-start(bf16[256,1024]{1,0:T(8,128)(2,1)} %collective-permute-done.7.refs_1_), channel_id=1, source_target_pairs={{0,1},{1,0},{2,3},{3,2},{4,5},{5,4},{6,7},{7,6},{8,9},{9,8},{10,11... | collective-permute-start | bytes 1572872 | tf_op jit(solution)/shard_map/ppermute | solution.py:342
  53.3 8.4 %collective-permute-start.11 = (bf16[128,1024]{1,0:T(8,128)(2,1)S(1)}, bf16[128,1024]{1,0:T(8,128)(2,1)S(1)}, u32[]{:S(2)}, u32[]{:S(2)}) collective-permute-start(bf16[128,1024]{1,0:T(8,128)(2,1)S(1)} %select_select_fusion.3), channel_id=1, source_target_pairs={{0,16},{1,17},{2,18},{3,19},{4,20},{5,21},{6,22},{7,23},{8,24},{9,... | collective-permute-start | bytes 786440 | tf_op jit(solution)/shard_map/ppermute | solution.py:342
  59.7 3.9 %collective-permute-start.12 = (bf16[256,1024]{1,0:T(8,128)(2,1)S(1)}, bf16[256,1024]{1,0:T(8,128)(2,1)S(1)}, u32[]{:S(2)}, u32[]{:S(2)}) collective-permute-start(bf16[256,1024]{1,0:T(8,128)(2,1)S(1)} %select_select_fusion.refs_0_), channel_id=1, source_target_pairs={{0,1},{1,0},{2,3},{3,2},{4,5},{5,4},{6,7},{7,6},{8,9},{9,8},{10,11... | collective-permute-start | bytes 1572872 | tf_op jit(solution)/shard_map/ppermute | solution.py:342
  61.6 2.0 %collective-permute-start.13 = (bf16[128,1024]{1,0:T(8,128)(2,1)S(1)}, bf16[128,1024]{1,0:T(8,128)(2,1)S(1)}, u32[]{:S(2)}, u32[]{:S(2)}) collective-permute-start(bf16[128,1024]{1,0:T(8,128)(2,1)S(1)} %collective-permute-done.11.refs_1_), channel_id=1, source_target_pairs={{0,1},{1,0},{2,3},{3,2},{4,5},{5,4},{6,7},{7,6},{8,9},{9,8},{10,11... | collective-permute-start | bytes 786440 | tf_op jit(solution)/shard_map/ppermute | solution.py:342
  61.6 8.8 %collective-permute-start.10 = (bf16[128,1024]{1,0:T(8,128)(2,1)S(1)}, bf16[128,1024]{1,0:T(8,128)(2,1)}, u32[]{:S(2)}, u32[]{:S(2)}) collective-permute-start(bf16[128,1024]{1,0:T(8,128)(2,1)S(1)} %select_select_fusion.4), channel_id=1, source_target_pairs={{0,16},{1,17},{2,18},{3,19},{4,20},{5,21},{6,22},{7,23},{8,24},{9,... | collective-permute-start | bytes 786440 | tf_op jit(solution)/shard_map/ppermute | solution.py:342
  62.1 15.1 %collective-permute-start.14 = (bf16[512,512]{1,0:T(8,128)(2,1)}, bf16[512,512]{1,0:T(8,128)(2,1)}, u32[]{:S(2)}, u32[]{:S(2)}) collective-permute-start(bf16[512,512]{1,0:T(8,128)(2,1)} %long_range.6), channel_id=1, source_target_pairs={{0,2},{1,3},{2,0},{3,1},{4,6},{5,7},{6,4},{7,5},{8,10},{9,11},{10,... | collective-permute-start | bytes 1572872 | tf_op jit(solution)/shard_map/ppermute | solution.py:342
  70.5 6.7 %collective-permute-start.15 = (bf16[128,1024]{1,0:T(8,128)(2,1)}, bf16[128,1024]{1,0:T(8,128)(2,1)}, u32[]{:S(2)}, u32[]{:S(2)}) collective-permute-start(bf16[128,1024]{1,0:T(8,128)(2,1)} %collective-permute-done.10.refs_1_), channel_id=1, source_target_pairs={{0,1},{1,0},{2,3},{3,2},{4,5},{5,4},{6,7},{7,6},{8,9},{9,8},{10,11... | collective-permute-start | bytes 786440 | tf_op jit(solution)/shard_map/ppermute | solution.py:342
  70.6 17.9 %collective-permute-start.17 = (bf16[256,512]{1,0:T(8,128)(2,1)}, bf16[256,512]{1,0:T(8,128)(2,1)S(1)}, u32[]{:S(2)}, u32[]{:S(2)}) collective-permute-start(bf16[256,512]{1,0:T(8,128)(2,1)} %copy-done.10), channel_id=1, source_target_pairs={{0,2},{1,3},{2,0},{3,1},{4,6},{5,7},{6,4},{7,5},{8,10},{9,11},{10,... | collective-permute-start | bytes 786440 | tf_op jit(solution)/shard_map/ppermute | solution.py:342
  78.9 11.7 %collective-permute-start.16 = (bf16[256,512]{1,0:T(8,128)(2,1)S(1)}, bf16[256,512]{1,0:T(8,128)(2,1)S(1)}, u32[]{:S(2)}, u32[]{:S(2)}) collective-permute-start(bf16[256,512]{1,0:T(8,128)(2,1)S(1)} %long_range.8), channel_id=1, source_target_pairs={{0,2},{1,3},{2,0},{3,1},{4,6},{5,7},{6,4},{7,5},{8,10},{9,11},{10,... | collective-permute-start | bytes 786440 | tf_op jit(solution)/shard_map/ppermute | solution.py:342
  (16 other events, 95.7 us)

commit v5 on v4

--- a/solution.py
+++ b/solution.py
@@ -9,9 +9,10 @@
 
 AXES = ("grp", "dev")
 CORES = 2
+SMALL_COST = pl.CostEstimate(flops=1, bytes_accessed=1, transcendentals=0)
 GROUP_ITEMS = 4
-SHORT_VMEM_BYTES = 28 * 1024 * 1024
-VMEM_BYTES = 16 * 1024 * 1024
+SHORT_VMEM_BYTES = 20 * 1024 * 1024
+VMEM_BYTES = 10 * 1024 * 1024
 
 
 def short_kernel(
@@ -138,9 +139,7 @@
         ],
         compiler_params=pltpu.CompilerParams(vmem_limit_bytes=SHORT_VMEM_BYTES),
         cost_estimate=pl.CostEstimate(
-            flops=2 * row_count * slots * depth * width * 2,
-            bytes_accessed=row_count * 2 * subs * width * 4 + slots * depth * width * 2,
-            transcendentals=0,
+            flops=4 * row_count * slots * depth * width, bytes_accessed=1, transcendentals=0
         ),
         name="short_range",
     )(half, live, sub_ids, meta, aux_basis, aux_decay.reshape(1, -1), *items)
@@ -157,20 +156,17 @@
         right[top : top + depth, 0:width] = factor[...]
         right[top : top + half, width:] = factor[half:, :]
         right[top + half : top + depth, width:] = -factor[0:half, :]
-    left = jnp.concatenate(
-        [
-            jnp.concatenate(
-                [
-                    parts[block * chains + chain][pl.ds(window[chain], window[-1]), :]
-                    for block in range(blocks)
-                ],
-                axis=0,
-            )
-            for chain in range(chains)
-        ],
-        axis=1,
-    )
-    out_ref[...] = jnp.dot(left, right[...], preferred_element_type=jnp.float32).astype(out_ref.dtype)
+    count = window[-1]
+    for block in range(blocks):
+        left = jnp.concatenate(
+            [
+                parts[block * chains + chain][pl.ds(window[chain], count), :]
+                for chain in range(chains)
+            ],
+            axis=1,
+        )
+        made = jnp.dot(left, right[...], preferred_element_type=jnp.float32)
+        out_ref[block * count : (block + 1) * count, :] = made.astype(out_ref.dtype)
 
 
 def long_range(blocks, factors, window, dtype):
@@ -185,11 +181,7 @@
         out_specs=pl.BlockSpec(memory_space=pltpu.VMEM),
         scratch_shapes=[pltpu.VMEM((chains * depth, 2 * width), jnp.bfloat16)],
         compiler_params=pltpu.CompilerParams(vmem_limit_bytes=VMEM_BYTES),
-        cost_estimate=pl.CostEstimate(
-            flops=2 * all_rows * depth * chains * 2 * width,
-            bytes_accessed=2 * chains * depth * (all_rows + width) + 4 * all_rows * width,
-            transcendentals=0,
-        ),
+        cost_estimate=SMALL_COST,
         name="long_range",
     )(*flat)
 
@@ -239,9 +231,7 @@
         ],
         input_output_aliases={count + 2: 0} if aliased else {},
         compiler_params=pltpu.CompilerParams(vmem_limit_bytes=VMEM_BYTES),
-        cost_estimate=pl.CostEstimate(
-            flops=steps * rows * columns, bytes_accessed=steps * rows * columns * 8, transcendentals=0
-        ),
+        cost_estimate=SMALL_COST,
         name="final_sum",
     )(order, *pieces, short, *([earlier] if aliased else []))
 
@@ -297,7 +287,8 @@
     length = chips // breadth
 
     aux_flat = aux_ft.reshape(rows, 2 * local_g)
-    weighted = (pair_ft.astype(jnp.float32) * coul_weight[None, None, :]).astype(jnp.bfloat16)
+    pairs = after(pair_ft, aux_flat).astype(jnp.float32)
+    weighted = (pairs * coul_weight[None, None, :]).astype(jnp.bfloat16)
     turned = weighted.reshape(local_rows, 2 * local_g).T
     item_rows = jnp.swapaxes(item_pair, 1, 2)
     live = (jnp.arange(item_image.shape[0], dtype=jnp.int32) < item_count[0]).astype(jnp.int32)
@@ -386,15 +377,15 @@
         return [value] + [over_core(value, t) for t in range(1, CORES)]
 
     held = [aux_flat]
-    held.append(along(held[0]))
+    held.append(along(after(aux_flat, turned)))
     turned_x = to_plane(turned)
     factors = [[turned, turned_x]] + [[over_y(turned, s)] for s in range(1, breadth)]
     packed = jnp.concatenate([item_rows, slot_block(slots, item_rows)], axis=0)
-    items_x = to_plane(after(packed, turned_x, held[1], *(pair[0] for pair in factors[1:])))
+    items_x = to_plane(after(packed, held[1], turned_x, *(pair[0] for pair in factors[1:])))
     for s in range(1, breadth):
         factors[s].append(over_y(turned_x, s))
     for k in range(2, length):
-        held.append(along(held[-1]))
+        held.append(along(after(held[-1], turned_x)))
 
     images, sub_ids, live = jnp.concatenate([slots, read_slots(items_x, slots)], axis=1)
     table = slot_table(image_dist, image_phase, images)
@@ -434,13 +425,14 @@
             mine[n] = with_cores(pick(False, n, slice(None), theirs[i]))
         if i:
             multiply(i - 1)
-        crossed.append(with_cores(after(moved, *away[i - 1] if i else [short])))
+        earlier = [short] if i == 0 else away[i - 1] + (arriving[i - 2] if i > 1 else [])
+        crossed.append(with_cores(after(moved, *earlier)))
         if i > 1:
             own.append(product(i - 2, 0, theirs[i]))
     last = len(units) - 1
-    multiply(last, *(arriving[0] if last > 1 else []))
     if last:
-        own.append(product(last - 1, 0, crossed[last][0]))
+        own.append(product(last - 1, 0))
+    multiply(last, *own)
     own.append(product(last, 0))
 
     def place_of(piece, i, s):

time: 93.3 us -> 96.7 us (1.036)
  local copies, waits for them, and re-layouts: 5.6 us -> 9.48 us
  starting transfers between devices: 21.4 us -> 18.9 us
  waiting for transfers between devices: 31 us -> 32.2 us
  other arithmetic: 8.1 us -> 9.18 us
    unnamed x46 -> x54, local copies, waits for them, and re-layouts: 4.92 us -> 8.81 us
    ppermute x18, starting transfers between devices: 21.4 us -> 18.9 us  [send(): return lax.ppermute(value, AXES, pairs)]
    pallas_call x1, Pallas kernels: 7.76 us -> 10.1 us  [short_range(): pl.pallas_call(kernel, out_shape=jax.ShapeDtypeStruct((row_count, 2 * sub...]
    pallas_call x6, Pallas kernels: 10.7 us -> 9.06 us  [long_range(): pl.pallas_call(functools.partial(long_kernel, blocks=len(blocks), chains=...]
    ppermute x18, waiting for transfers between devices: 31 us -> 32.2 us  [send(): return lax.ppermute(value, AXES, pairs)]
  transfers between devices with their start and end apart: 18 -> 18, of which waited for: 8 -> 9; matrix products, arithmetic and copies ran while one was open for 10% -> 8% of each run, Pallas kernels for 25% -> 25%
where the time goes in v5:
time: 96.7 us; the launch traced here: 96.5 us
  waiting for transfers between devices  32.2 us (33%)
  Pallas kernels  25.4 us (26%)
  starting transfers between devices  18.9 us (20%)
  local copies, waits for them, and re-layouts  9.48 us (10%)
  other arithmetic  9.18 us (9%)
  between operations  1.31 us (1%)
    ppermute x18, waiting for transfers between devices, send(): return lax.ppermute(value, AXES, pairs)  32.2 us
    ppermute x18, starting transfers between devices, send(): return lax.ppermute(value, AXES, pairs)  18.9 us
    pallas_call x1, Pallas kernels, short_range(): pl.pallas_call(kernel, out_shape=jax.ShapeDtypeStruct((row_count, 2 * sub...  10.1 us
    pallas_call x6, Pallas kernels, long_range(): pl.pallas_call(functools.partial(long_kernel, blocks=len(blocks), chains=...  9.06 us
    unnamed x54, local copies, waits for them, and re-layouts  8.81 us
    select_n x5, other arithmetic, pick(): value = jnp.where(wanted == k, block[window], value)  6.34 us
    pallas_call x3, Pallas kernels, final_sum(): pl.pallas_call(functools.partial(final_kernel, pieces=count, blocks=block...  6.24 us
  transfers between devices with their start and end apart: 18, of which 9 were waited for; matrix products, arithmetic and copies ran while one was open for 8% of the time, Pallas kernels for 25%

profile of v5, /device:TPU:0, one launch (start us, length us, event | category | flops | bytes accessed | tf_op | source)
XLA Modules:
  0.0 96.5 jit_solution(18261515748484829518)
XLA Ops:
  1.2 1.6 %multiply_convert_fusion = bf16[256,2,512]{2,1,0:T(2,128)(2,1)S(1)} fusion(bf16[256,2,512]{2,1,0:T(2,128)(2,1)} %param.11, f32[512]{0:T(512)} %param.13), kind=kLoop, calls=%fused_computation | loop fusion | flops 786432 | bytes 1050624 | tf_op jit(solution)/shard_map/convert_element_type | solution.py:291
  3.4 4.1 %collective-permute-start = (bf16[256,1024]{1,0:T(8,128)(2,1)S(1)}, bf16[256,1024]{1,0:T(8,128)(2,1)}, u32[]{:S(2)}, u32[]{:S(2)}) collective-permute-start(bf16[256,1024]{1,0:T(8,128)(2,1)S(1)} %bitcast.45), channel_id=1, source_target_pairs={{0,8},{1,9},{2,10},{3,11},{4,0},{5,1},{6,2},{7,3},{8,12},{9,13},{1... | collective-permute-start | bytes 1572872 | tf_op jit(solution)/shard_map/ppermute | solution.py:333
  7.5 1.5 %collective-permute-start.4 = (bf16[1024,256]{1,0:T(8,128)(2,1)S(1)}, bf16[1024,256]{1,0:T(8,128)(2,1)S(1)}, u32[]{:S(2)}, u32[]{:S(2)}) collective-permute-start(bf16[1024,256]{1,0:T(8,128)(2,1)S(1)} %bitcast.39), channel_id=1, source_target_pairs={{0,2},{1,3},{2,0},{3,1},{4,6},{5,7},{6,4},{7,5},{8,10},{9,11},{10,... | collective-permute-start | bytes 1572872 | tf_op jit(solution)/shard_map/ppermute | solution.py:333
  9.0 1.5 %collective-permute-start.1 = (bf16[1024,256]{1,0:T(8,128)(2,1)S(1)}, bf16[1024,256]{1,0:T(8,128)(2,1)S(1)}, u32[]{:S(2)}, u32[]{:S(2)}) collective-permute-start(bf16[1024,256]{1,0:T(8,128)(2,1)S(1)} %bitcast.40), channel_id=1, source_target_pairs={{0,16},{1,17},{2,18},{3,19},{4,20},{5,21},{6,22},{7,23},{8,24},{9,... | collective-permute-start | bytes 1572872 | tf_op jit(solution)/shard_map/ppermute | solution.py:333
  11.6 7.1 %collective-permute-done = bf16[256,1024]{1,0:T(8,128)(2,1)} collective-permute-done((bf16[256,1024]{1,0:T(8,128)(2,1)S(1)}, bf16[256,1024]{1,0:T(8,128)(2,1)}, u32[]{:S(2)}, u32[]{:S(2)}) %collective-permute-start) | collective-permute-done | bytes 524320 | tf_op jit(solution)/shard_map/ppermute | solution.py:333
  18.7 2.2 %collective-permute-done.4.refs_4_ = bf16[1024,256]{1,0:T(8,128)(2,1)S(1)} collective-permute-done((bf16[1024,256]{1,0:T(8,128)(2,1)S(1)}, bf16[1024,256]{1,0:T(8,128)(2,1)S(1)}, u32[]{:S(2)}, u32[]{:S(2)}) %collective-permute-start.4) | collective-permute-done | bytes 524320 | tf_op jit(solution)/shard_map/ppermute | solution.py:333
  22.1 1.5 %collective-permute-start.5 = (bf16[17,128,128]{2,1,0:T(8,128)(2,1)S(1)}, bf16[17,128,128]{2,1,0:T(8,128)(2,1)}, u32[]{:S(2)}, u32[]{:S(2)}) collective-permute-start(bf16[17,128,128]{2,1,0:T(8,128)(2,1)S(1)} %pad_maximum_fusion.refs_0_), channel_id=1, source_target_pairs={{0,16},{1,17},{2,18},{3,19},{4,20},{5,21},{6,22},{7,23},{8,24},{9,... | collective-permute-start | bytes 1671176 | tf_op jit(solution)/shard_map/ppermute | solution.py:333
  23.6 1.6 %collective-permute-start.2 = (bf16[256,1024]{1,0:T(8,128)(2,1)}, bf16[256,1024]{1,0:T(8,128)(2,1)}, u32[]{:S(2)}, u32[]{:S(2)}) collective-permute-start(bf16[256,1024]{1,0:T(8,128)(2,1)} %collective-permute-done), channel_id=1, source_target_pairs={{0,8},{1,9},{2,10},{3,11},{4,0},{5,1},{6,2},{7,3},{8,12},{9,13},{1... | collective-permute-start | bytes 1572872 | tf_op jit(solution)/shard_map/ppermute | solution.py:333
  25.7 10.1 %collective-permute-done.2 = bf16[256,1024]{1,0:T(8,128)(2,1)} collective-permute-done((bf16[256,1024]{1,0:T(8,128)(2,1)}, bf16[256,1024]{1,0:T(8,128)(2,1)}, u32[]{:S(2)}, u32[]{:S(2)}) %collective-permute-start.2) | collective-permute-done | bytes 524320 | tf_op jit(solution)/shard_map/ppermute | solution.py:333
  35.8 2.6 %collective-permute-start.3 = (bf16[256,1024]{1,0:T(8,128)(2,1)}, bf16[256,1024]{1,0:T(8,128)(2,1)}, u32[]{:S(2)}, u32[]{:S(2)}) collective-permute-start(bf16[256,1024]{1,0:T(8,128)(2,1)} %collective-permute-done.2), channel_id=1, source_target_pairs={{0,8},{1,9},{2,10},{3,11},{4,0},{5,1},{6,2},{7,3},{8,12},{9,13},{1... | collective-permute-start | bytes 1572872 | tf_op jit(solution)/shard_map/ppermute | solution.py:333
  42.7 10.1 %short_range.1.refs_2_.refs_3_.refs_1_ = f32[2048,512]{1,0:T(8,128)S(1)} custom-call(s32[1]{0:T(128)} %bitcast.10.half_ref, s32[32]{0:T(128)S(1)} %get-tuple-element.59.live_ref, s32[32]{0:T(128)S(1)} %get-tuple-element.58.sub_ref, f32[3,32]{1,0:T(4,128)S(1)} %pad_maximum_fusion.1.meta_ref, bf16[128,4096]{1,0:T(8,128)(2,1)S(1)} %copy-done.18, ...), custom_call_target="tpu_custom_call" | custom-call | flops 4294967296 | bytes 1 | tf_op jit(solution)/shard_map/short_range/pallas_call | solution.py:121
  52.8 2.0 %copy-done = f32[2048,512]{1,0:T(8,128)} copy-done((f32[2048,512]{1,0:T(8,128)}, f32[2048,512]{1,0:T(8,128)S(1)}, u32[]{:S(2)}) %copy-start) | copy-done | bytes 4194328
  57.5 2.5 %long_range.6 = bf16[512,512]{1,0:T(8,128)(2,1)S(1)} custom-call(bf16[256,1024]{1,0:T(8,128)(2,1)S(1)} %select_select_fusion.1.refs_0_, bf16[256,1024]{1,0:T(8,128)(2,1)S(1)} %collective-permute-done.7.refs_1_, bf16[256,1024]{1,0:T(8,128)(2,1)S(1)} %collective-permute-done.8.refs_2_, bf16[256,1024]{1,0:T(8,128)(2,1)} %collective-permute-done.9.refs_3_, ...), custom_call_target="tpu_custom_call" | custom-call | flops 1 | bytes 1 | tf_op jit(solution)/shard_map/long_range/pallas_call | solution.py:177
  62.8 1.9 %collective-permute-done.11.refs_1_ = bf16[128,1024]{1,0:T(8,128)(2,1)S(1)} collective-permute-done((bf16[128,1024]{1,0:T(8,128)(2,1)S(1)}, bf16[128,1024]{1,0:T(8,128)(2,1)S(1)}, u32[]{:S(2)}, u32[]{:S(2)}) %collective-permute-start.11) | collective-permute-done | bytes 262176 | tf_op jit(solution)/shard_map/ppermute | solution.py:333
  66.3 1.4 %long_range.7 = bf16[256,512]{1,0:T(8,128)(2,1)} custom-call(bf16[256,1024]{1,0:T(8,128)(2,1)S(1)} %select_select_fusion.refs_0_, bf16[128,1024]{1,0:T(8,128)(2,1)S(1)} %collective-permute-done.11.refs_1_, bf16[256,1024]{1,0:T(8,128)(2,1)S(1)} %collective-permute-done.12.refs_2_, bf16[128,1024]{1,0:T(8,128)(2,1)S(1)} %collective-permute-done.13.refs_3_, ...), custom_call_target="tpu_custom_call" | custom-call | flops 1 | bytes 1 | tf_op jit(solution)/shard_map/long_range/pallas_call | solution.py:177
  67.7 5.8 %collective-permute-done.10.refs_1_ = bf16[128,1024]{1,0:T(8,128)(2,1)S(1)} collective-permute-done((bf16[128,1024]{1,0:T(8,128)(2,1)S(1)}, bf16[128,1024]{1,0:T(8,128)(2,1)S(1)}, u32[]{:S(2)}, u32[]{:S(2)}) %collective-permute-start.10) | collective-permute-done | bytes 262176 | tf_op jit(solution)/shard_map/ppermute | solution.py:333
  73.4 3.6 %collective-permute-done.14.refs_1_ = bf16[512,512]{1,0:T(8,128)(2,1)S(1)} collective-permute-done((bf16[512,512]{1,0:T(8,128)(2,1)S(1)}, bf16[512,512]{1,0:T(8,128)(2,1)S(1)}, u32[]{:S(2)}, u32[]{:S(2)}) %collective-permute-start.14) | collective-permute-done | bytes 524320 | tf_op jit(solution)/shard_map/ppermute | solution.py:333
  77.9 2.3 %long_range.8.refs_0_ = f32[512,512]{1,0:T(8,128)S(1)} custom-call(bf16[256,1024]{1,0:T(8,128)(2,1)S(1)} %select_select_fusion.1.refs_0_, bf16[256,1024]{1,0:T(8,128)(2,1)S(1)} %copy-done.9, bf16[256,1024]{1,0:T(8,128)(2,1)S(1)} %copy-done.11, bf16[256,1024]{1,0:T(8,128)(2,1)} %collective-permute-done.9.refs_3_, bf16[1024,256]{1,0:T(8,128)(2,1)S(1)} %bitcast.41, ...), custom_call_target="tpu_custom_call" | custom-call | flops 1 | bytes 1 | tf_op jit(solution)/shard_map/long_range/pallas_call | solution.py:177
  81.3 1.4 %long_range.10 = bf16[256,512]{1,0:T(8,128)(2,1)} custom-call(bf16[256,1024]{1,0:T(8,128)(2,1)S(1)} %select_select_fusion.refs_0_, bf16[128,1024]{1,0:T(8,128)(2,1)S(1)} %collective-permute-done.10.refs_1_, bf16[256,1024]{1,0:T(8,128)(2,1)S(1)} %collective-permute-done.12.refs_2_, bf16[128,1024]{1,0:T(8,128)(2,1)S(1)} %collective-permute-done.15.refs_3_, ...), custom_call_target="tpu_custom_call" | custom-call | flops 1 | bytes 1 | tf_op jit(solution)/shard_map/long_range/pallas_call | solution.py:177
  82.7 1.8 %collective-permute-start.16 = (bf16[256,512]{1,0:T(8,128)(2,1)}, bf16[256,512]{1,0:T(8,128)(2,1)S(1)}, u32[]{:S(2)}, u32[]{:S(2)}) collective-permute-start(bf16[256,512]{1,0:T(8,128)(2,1)} %long_range.10), channel_id=1, source_target_pairs={{0,2},{1,3},{2,0},{3,1},{4,6},{5,7},{6,4},{7,5},{8,10},{9,11},{10,... | collective-permute-start | bytes 786440 | tf_op jit(solution)/shard_map/ppermute | solution.py:333
  84.7 2.2 %copy-done.1 = f32[2048,512]{1,0:T(8,128)S(1)} copy-done((f32[2048,512]{1,0:T(8,128)S(1)}, f32[2048,512]{1,0:T(8,128)}, u32[]{:S(2)}) %copy-start.1) | copy-done | bytes 4194328
  89.2 2.3 %final_sum.3.refs_4_ = bf16[2048,2,256]{2,1,0:T(2,128)(2,1)} custom-call(s32[4]{0:T(128)S(1)} %pad_add_fusion.3.order_ref, f32[512,512]{1,0:T(8,128)S(1)} %copy-done.7, bf16[512,512]{1,0:T(8,128)(2,1)S(1)} %copy-done.17, f32[2048,512]{1,0:T(8,128)S(1)} %copy-done.1), custom_call_target="tpu_custom_call" | custom-call | flops 1 | bytes 1 | tf_op jit(solution)/shard_map/final_sum/pallas_call | solution.py:219
  92.3 2.5 %final_sum.4.refs_2_ = bf16[2048,2,256]{2,1,0:T(2,128)(2,1)} custom-call(s32[6]{0:T(128)S(1)} %stack.77.order_ref, f32[256,512]{1,0:T(8,128)S(1)} %long_range.9.refs_0_, bf16[256,512]{1,0:T(8,128)(2,1)} %collective-permute-done.17.refs_1_, f32[256,512]{1,0:T(8,128)S(1)} %long_range.11.refs_2_, ...), custom_call_target="tpu_custom_call", output_to_operand_aliasing={{}: (5, {})} | custom-call | flops 1 | bytes 1 | tf_op jit(solution)/shard_map/final_sum/pallas_call | solution.py:219
  94.8 1.5 %final_sum.5 = bf16[2048,2,256]{2,1,0:T(2,128)(2,1)} custom-call(s32[2]{0:T(128)S(1)} %pad_add_fusion.2.order_ref, bf16[256,512]{1,0:T(8,128)(2,1)S(1)} %collective-permute-done.16.refs_0_, f32[2048,512]{1,0:T(8,128)S(1)} %copy-done.2, bf16[2048,2,256]{2,1,0:T(2,128)(2,1)} %final_sum.4.refs_2_), custom_call_target="tpu_custom_call", output_to_operand_aliasing={{}: (3, {})} | custom-call | flops 1 | bytes 1 | tf_op jit(solution)/shard_map/final_sum/pallas_call | solution.py:219
  (97 shorter events, 20.3 us)
Async XLA Ops:
  1.2 38.0 %copy-start.20 = (bf16[32,8,2,512]{3,1,2,0:T(8,128)(2,1)}, bf16[32,8,2,512]{3,1,2,0:T(8,128)(2,1)S(1)}, u32[]{:S(2)}) copy-start(bf16[32,8,2,512]{3,1,2,0:T(8,128)(2,1)S(1)} %copy.18) | copy-start | bytes 1572868
  3.4 15.3 %collective-permute-start = (bf16[256,1024]{1,0:T(8,128)(2,1)S(1)}, bf16[256,1024]{1,0:T(8,128)(2,1)}, u32[]{:S(2)}, u32[]{:S(2)}) collective-permute-start(bf16[256,1024]{1,0:T(8,128)(2,1)S(1)} %bitcast.45), channel_id=1, source_target_pairs={{0,8},{1,9},{2,10},{3,11},{4,0},{5,1},{6,2},{7,3},{8,12},{9,13},{1... | collective-permute-start | bytes 1572872 | tf_op jit(solution)/shard_map/ppermute | solution.py:333
  7.5 13.4 %collective-permute-start.4 = (bf16[1024,256]{1,0:T(8,128)(2,1)S(1)}, bf16[1024,256]{1,0:T(8,128)(2,1)S(1)}, u32[]{:S(2)}, u32[]{:S(2)}) collective-permute-start(bf16[1024,256]{1,0:T(8,128)(2,1)S(1)} %bitcast.39), channel_id=1, source_target_pairs={{0,2},{1,3},{2,0},{3,1},{4,6},{5,7},{6,4},{7,5},{8,10},{9,11},{10,... | collective-permute-start | bytes 1572872 | tf_op jit(solution)/shard_map/ppermute | solution.py:333
  9.0 13.1 %collective-permute-start.1 = (bf16[1024,256]{1,0:T(8,128)(2,1)S(1)}, bf16[1024,256]{1,0:T(8,128)(2,1)S(1)}, u32[]{:S(2)}, u32[]{:S(2)}) collective-permute-start(bf16[1024,256]{1,0:T(8,128)(2,1)S(1)} %bitcast.40), channel_id=1, source_target_pairs={{0,16},{1,17},{2,18},{3,19},{4,20},{5,21},{6,22},{7,23},{8,24},{9,... | collective-permute-start | bytes 1572872 | tf_op jit(solution)/shard_map/ppermute | solution.py:333
  11.2 29.9 %copy-start.24 = (f32[125]{0:T(128)S(1)}, f32[125]{0:T(128)}, u32[]{:S(2)}) copy-start(f32[125]{0:T(128)} %param.16) | copy-start | bytes 1504
  11.2 29.8 %copy-start.25 = (f32[125]{0:T(128)S(1)}, f32[125]{0:T(128)}, u32[]{:S(2)}) copy-start(f32[125]{0:T(128)} %param.17) | copy-start | bytes 1504
  11.6 29.4 %copy-start.14 = (bf16[17,128,128]{2,1,0:T(8,128)(2,1)}, bf16[17,128,128]{2,1,0:T(8,128)(2,1)S(1)}, u32[]{:S(2)}) copy-start(bf16[17,128,128]{2,1,0:T(8,128)(2,1)S(1)} %pad_maximum_fusion.refs_0_) | copy-start | bytes 1671172
  22.1 20.4 %copy-start.3 = (bf16[1024,256]{1,0:T(8,128)(2,1)}, bf16[1024,256]{1,0:T(8,128)(2,1)S(1)}, u32[]{:S(2)}) copy-start(bf16[1024,256]{1,0:T(8,128)(2,1)S(1)} %collective-permute-done.1.refs_5_) | copy-start | bytes 1572868
  22.1 16.3 %collective-permute-start.5 = (bf16[17,128,128]{2,1,0:T(8,128)(2,1)S(1)}, bf16[17,128,128]{2,1,0:T(8,128)(2,1)}, u32[]{:S(2)}, u32[]{:S(2)}) collective-permute-start(bf16[17,128,128]{2,1,0:T(8,128)(2,1)S(1)} %pad_maximum_fusion.refs_0_), channel_id=1, source_target_pairs={{0,16},{1,17},{2,18},{3,19},{4,20},{5,21},{6,22},{7,23},{8,24},{9,... | collective-permute-start | bytes 1671176 | tf_op jit(solution)/shard_map/ppermute | solution.py:333
  23.6 12.2 %collective-permute-start.2 = (bf16[256,1024]{1,0:T(8,128)(2,1)}, bf16[256,1024]{1,0:T(8,128)(2,1)}, u32[]{:S(2)}, u32[]{:S(2)}) collective-permute-start(bf16[256,1024]{1,0:T(8,128)(2,1)} %collective-permute-done), channel_id=1, source_target_pairs={{0,8},{1,9},{2,10},{3,11},{4,0},{5,1},{6,2},{7,3},{8,12},{9,13},{1... | collective-permute-start | bytes 1572872 | tf_op jit(solution)/shard_map/ppermute | solution.py:333
  25.2 13.2 %collective-permute-start.6 = (bf16[1024,256]{1,0:T(8,128)(2,1)S(1)}, bf16[1024,256]{1,0:T(8,128)(2,1)S(1)}, u32[]{:S(2)}, u32[]{:S(2)}) collective-permute-start(bf16[1024,256]{1,0:T(8,128)(2,1)S(1)} %collective-permute-done.1.refs_5_), channel_id=1, source_target_pairs={{0,2},{1,3},{2,0},{3,1},{4,6},{5,7},{6,4},{7,5},{8,10},{9,11},{10,... | collective-permute-start | bytes 1572872 | tf_op jit(solution)/shard_map/ppermute | solution.py:333
  35.8 19.1 %collective-permute-start.3 = (bf16[256,1024]{1,0:T(8,128)(2,1)}, bf16[256,1024]{1,0:T(8,128)(2,1)}, u32[]{:S(2)}, u32[]{:S(2)}) collective-permute-start(bf16[256,1024]{1,0:T(8,128)(2,1)} %collective-permute-done.2), channel_id=1, source_target_pairs={{0,8},{1,9},{2,10},{3,11},{4,0},{5,1},{6,2},{7,3},{8,12},{9,13},{1... | collective-permute-start | bytes 1572872 | tf_op jit(solution)/shard_map/ppermute | solution.py:333
  40.4 14.4 %collective-permute-start.7 = (bf16[256,1024]{1,0:T(8,128)(2,1)S(1)}, bf16[256,1024]{1,0:T(8,128)(2,1)S(1)}, u32[]{:S(2)}, u32[]{:S(2)}) collective-permute-start(bf16[256,1024]{1,0:T(8,128)(2,1)S(1)} %select_select_fusion.2), channel_id=1, source_target_pairs={{0,16},{1,17},{2,18},{3,19},{4,20},{5,21},{6,22},{7,23},{8,24},{9,... | collective-permute-start | bytes 1572872 | tf_op jit(solution)/shard_map/ppermute | solution.py:333
  42.6 14.9 %collective-permute-start.8 = (bf16[256,1024]{1,0:T(8,128)(2,1)S(1)}, bf16[256,1024]{1,0:T(8,128)(2,1)S(1)}, u32[]{:S(2)}, u32[]{:S(2)}) collective-permute-start(bf16[256,1024]{1,0:T(8,128)(2,1)S(1)} %select_select_fusion.1.refs_0_), channel_id=1, source_target_pairs={{0,1},{1,0},{2,3},{3,2},{4,5},{5,4},{6,7},{7,6},{8,9},{9,8},{10,11... | collective-permute-start | bytes 1572872 | tf_op jit(solution)/shard_map/ppermute | solution.py:333
  54.8 2.8 %collective-permute-start.9 = (bf16[256,1024]{1,0:T(8,128)(2,1)S(1)}, bf16[256,1024]{1,0:T(8,128)(2,1)}, u32[]{:S(2)}, u32[]{:S(2)}) collective-permute-start(bf16[256,1024]{1,0:T(8,128)(2,1)S(1)} %collective-permute-done.7.refs_1_), channel_id=1, source_target_pairs={{0,1},{1,0},{2,3},{3,2},{4,5},{5,4},{6,7},{7,6},{8,9},{9,8},{10,11... | collective-permute-start | bytes 1572872 | tf_op jit(solution)/shard_map/ppermute | solution.py:333
  56.1 8.6 %collective-permute-start.11 = (bf16[128,1024]{1,0:T(8,128)(2,1)S(1)}, bf16[128,1024]{1,0:T(8,128)(2,1)S(1)}, u32[]{:S(2)}, u32[]{:S(2)}) collective-permute-start(bf16[128,1024]{1,0:T(8,128)(2,1)S(1)} %select_select_fusion.3), channel_id=1, source_target_pairs={{0,16},{1,17},{2,18},{3,19},{4,20},{5,21},{6,22},{7,23},{8,24},{9,... | collective-permute-start | bytes 786440 | tf_op jit(solution)/shard_map/ppermute | solution.py:333
  61.2 16.7 %copy-start.4 = (bf16[1024,256]{1,0:T(8,128)(2,1)S(1)}, bf16[1024,256]{1,0:T(8,128)(2,1)}, u32[]{:S(2)}) copy-start(bf16[1024,256]{1,0:T(8,128)(2,1)} %copy-done.3) | copy-start | bytes 1572868
  62.6 3.6 %collective-permute-start.12 = (bf16[256,1024]{1,0:T(8,128)(2,1)S(1)}, bf16[256,1024]{1,0:T(8,128)(2,1)S(1)}, u32[]{:S(2)}, u32[]{:S(2)}) collective-permute-start(bf16[256,1024]{1,0:T(8,128)(2,1)S(1)} %select_select_fusion.refs_0_), channel_id=1, source_target_pairs={{0,1},{1,0},{2,3},{3,2},{4,5},{5,4},{6,7},{7,6},{8,9},{9,8},{10,11... | collective-permute-start | bytes 1572872 | tf_op jit(solution)/shard_map/ppermute | solution.py:333
  62.7 14.3 %collective-permute-start.14 = (bf16[512,512]{1,0:T(8,128)(2,1)S(1)}, bf16[512,512]{1,0:T(8,128)(2,1)S(1)}, u32[]{:S(2)}, u32[]{:S(2)}) collective-permute-start(bf16[512,512]{1,0:T(8,128)(2,1)S(1)} %long_range.6), channel_id=1, source_target_pairs={{0,2},{1,3},{2,0},{3,1},{4,6},{5,7},{6,4},{7,5},{8,10},{9,11},{10,... | collective-permute-start | bytes 1572872 | tf_op jit(solution)/shard_map/ppermute | solution.py:333
  64.7 1.5 %collective-permute-start.13 = (bf16[128,1024]{1,0:T(8,128)(2,1)S(1)}, bf16[128,1024]{1,0:T(8,128)(2,1)S(1)}, u32[]{:S(2)}, u32[]{:S(2)}) collective-permute-start(bf16[128,1024]{1,0:T(8,128)(2,1)S(1)} %collective-permute-done.11.refs_1_), channel_id=1, source_target_pairs={{0,1},{1,0},{2,3},{3,2},{4,5},{5,4},{6,7},{7,6},{8,9},{9,8},{10,11... | collective-permute-start | bytes 786440 | tf_op jit(solution)/shard_map/ppermute | solution.py:333
  64.7 8.7 %collective-permute-start.10 = (bf16[128,1024]{1,0:T(8,128)(2,1)S(1)}, bf16[128,1024]{1,0:T(8,128)(2,1)S(1)}, u32[]{:S(2)}, u32[]{:S(2)}) collective-permute-start(bf16[128,1024]{1,0:T(8,128)(2,1)S(1)} %select_select_fusion.4), channel_id=1, source_target_pairs={{0,16},{1,17},{2,18},{3,19},{4,20},{5,21},{6,22},{7,23},{8,24},{9,... | collective-permute-start | bytes 786440 | tf_op jit(solution)/shard_map/ppermute | solution.py:333
  77.9 3.4 %collective-permute-start.15 = (bf16[128,1024]{1,0:T(8,128)(2,1)S(1)}, bf16[128,1024]{1,0:T(8,128)(2,1)S(1)}, u32[]{:S(2)}, u32[]{:S(2)}) collective-permute-start(bf16[128,1024]{1,0:T(8,128)(2,1)S(1)} %collective-permute-done.10.refs_1_), channel_id=1, source_target_pairs={{0,1},{1,0},{2,3},{3,2},{4,5},{5,4},{6,7},{7,6},{8,9},{9,8},{10,11... | collective-permute-start | bytes 786440 | tf_op jit(solution)/shard_map/ppermute | solution.py:333
  80.2 12.0 %collective-permute-start.17 = (bf16[256,512]{1,0:T(8,128)(2,1)}, bf16[256,512]{1,0:T(8,128)(2,1)}, u32[]{:S(2)}, u32[]{:S(2)}) collective-permute-start(bf16[256,512]{1,0:T(8,128)(2,1)} %long_range.7), channel_id=1, source_target_pairs={{0,2},{1,3},{2,0},{3,1},{4,6},{5,7},{6,4},{7,5},{8,10},{9,11},{10,... | collective-permute-start | bytes 786440 | tf_op jit(solution)/shard_map/ppermute | solution.py:333
  82.7 12.1 %collective-permute-start.16 = (bf16[256,512]{1,0:T(8,128)(2,1)}, bf16[256,512]{1,0:T(8,128)(2,1)S(1)}, u32[]{:S(2)}, u32[]{:S(2)}) collective-permute-start(bf16[256,512]{1,0:T(8,128)(2,1)} %long_range.10), channel_id=1, source_target_pairs={{0,2},{1,3},{2,0},{3,1},{4,6},{5,7},{6,4},{7,5},{8,10},{9,11},{10,... | collective-permute-start | bytes 786440 | tf_op jit(solution)/shard_map/ppermute | solution.py:333
  (20 other events, 101.2 us)

commit v6 on v5

--- a/solution.py
+++ b/solution.py
@@ -13,6 +13,10 @@
 GROUP_ITEMS = 4
 SHORT_VMEM_BYTES = 20 * 1024 * 1024
 VMEM_BYTES = 10 * 1024 * 1024
+
+
+def in_hbm(value):
+    return pltpu.with_memory_space_constraint(value, pltpu.HBM)
 
 
 def short_kernel(
@@ -120,7 +124,7 @@
     kernel = functools.partial(short_kernel, share=share, subs=subs, depth=depth, width=width)
     return pl.pallas_call(
         kernel,
-        out_shape=jax.ShapeDtypeStruct((row_count, 2 * subs * width), jnp.float32),
+        out_shape=pltpu.HBM((row_count, 2 * subs * width), jnp.float32),
         in_specs=[pl.BlockSpec(memory_space=pltpu.SMEM)] * 4
         + [pl.BlockSpec(memory_space=pltpu.HBM)]
         + [pl.BlockSpec(memory_space=pltpu.VMEM)] * (1 + len(items)),
@@ -142,7 +146,7 @@
             flops=4 * row_count * slots * depth * width, bytes_accessed=1, transcendentals=0
         ),
         name="short_range",
-    )(half, live, sub_ids, meta, aux_basis, aux_decay.reshape(1, -1), *items)
+    )(half, live, sub_ids, meta, in_hbm(aux_basis), aux_decay.reshape(1, -1), *items)
 
 
 def long_kernel(*refs, blocks, chains, window):
@@ -233,7 +237,7 @@
         compiler_params=pltpu.CompilerParams(vmem_limit_bytes=VMEM_BYTES),
         cost_estimate=SMALL_COST,
         name="final_sum",
-    )(order, *pieces, short, *([earlier] if aliased else []))
+    )(order, *pieces, in_hbm(short), *([earlier] if aliased else []))
 
 
 def slot_table(image_dist, image_phase, images):
@@ -338,8 +342,8 @@
     ring = [*range(0, length, 2), *reversed(range(1, length, 2))]
     turn = {z: n for n, z in enumerate(ring)}
 
-    def along(value):
-        return send(value, lambda g, z, y, c: (g, ring[(turn[z] + 1) % length], y, c))
+    def along(value, step):
+        return send(value, lambda g, z, y, c: (g, ring[(turn[z] + step) % length], y, c))
 
     def over_y(value, s):
         return send(value, lambda g, z, y, c: (g, z, (y + s) % breadth, c))
@@ -348,7 +352,8 @@
         return send(value, lambda g, z, y, c: (g, z, y, (c + t) % CORES))
 
     def hops_of(g, z):
-        return sorted((turn[z] - turn[j]) % length for j in range(g * home, (g + 1) * home))
+        hops = [(turn[z] - turn[j]) % length for j in range(g * home, (g + 1) * home)]
+        return sorted(hops, key=lambda k: (min(k, length - k), k))
 
     def here(number):
         return sum(
@@ -376,16 +381,17 @@
     def with_cores(value):
         return [value] + [over_core(value, t) for t in range(1, CORES)]
 
-    held = [aux_flat]
-    held.append(along(after(aux_flat, turned)))
+    held = {0: aux_flat, 1: along(aux_flat, 1), length - 1: along(aux_flat, -1)}
     turned_x = to_plane(turned)
     factors = [[turned, turned_x]] + [[over_y(turned, s)] for s in range(1, breadth)]
     packed = jnp.concatenate([item_rows, slot_block(slots, item_rows)], axis=0)
-    items_x = to_plane(after(packed, held[1], turned_x, *(pair[0] for pair in factors[1:])))
+    items_x = to_plane(after(packed, turned_x, held[1], *(pair[0] for pair in factors[1:])))
     for s in range(1, breadth):
         factors[s].append(over_y(turned_x, s))
-    for k in range(2, length):
-        held.append(along(after(held[-1], turned_x)))
+    for k in range(2, length // 2 + 1):
+        held[k] = along(after(held[k - 1], turned_x), 1)
+    for k in range(2, (length + 1) // 2):
+        held[length - k] = along(after(held[length - k + 1], turned_x), -1)
 
     images, sub_ids, live = jnp.concatenate([slots, read_slots(items_x, slots)], axis=1)
     table = slot_table(image_dist, image_phase, images)
@@ -423,35 +429,43 @@
         moved = to_plane(theirs[i])
         if first + count == rows:
             mine[n] = with_cores(pick(False, n, slice(None), theirs[i]))
-        if i:
-            multiply(i - 1)
-        earlier = [short] if i == 0 else away[i - 1] + (arriving[i - 2] if i > 1 else [])
-        crossed.append(with_cores(after(moved, *earlier)))
         if i > 1:
             own.append(product(i - 2, 0, theirs[i]))
+        if i:
+            multiply(i - 1, *own[-1:])
+        crossed.append(with_cores(after(moved, *away[i - 1] if i else [short])))
     last = len(units) - 1
     if last:
         own.append(product(last - 1, 0))
-    multiply(last, *own)
-    own.append(product(last, 0))
 
     def place_of(piece, i, s):
         n, first, count = units[i]
         return piece, [v * (rows // count) + first // count for v in numbers_of(n, s)]
 
     calls = []
-    for i, (_, _, count) in enumerate(units):
-        here_now = [place_of(own[i], i, 0)]
-        arrived = [place_of(v, i, s) for s, v in enumerate(arriving[i], 1)]
-        for entries in [here_now + arrived] if i < last else [here_now, arrived]:
-            if calls and calls[-1][0] == count and entries is not arrived:
-                calls[-1][1].extend(entries)
-            elif entries:
-                calls.append((count, entries))
-    out = None
-    for count, entries in calls:
+    for i, (_, _, count) in enumerate(units[:-1]):
+        entries = [place_of(v, i, s) for s, v in enumerate([own[i], *arriving[i]])]
+        if calls and calls[-1][0] == count:
+            calls[-1][1].extend(entries)
+        else:
+            calls.append((count, entries))
+
+    def add_up(out, count, entries):
         numbers = jnp.stack([v for _, each in entries for v in each]).astype(jnp.int32)
-        out = final_sum(numbers, [piece for piece, _ in entries], short, out, count)
+        return final_sum(numbers, [piece for piece, _ in entries], short, out, count)
+
+    out = add_up(None, *calls.pop(0)) if calls else None
+    multiply(last, *own, *([] if out is None else [out]))
+    own.append(product(last, 0))
+    count = units[last][2]
+    calls.append((count, [place_of(own[last], last, 0)]))
+    if len(calls) > 1 and calls[-2][0] == count:
+        entries = calls.pop()[1]
+        calls[-1][1].extend(entries)
+    if breadth > 1:
+        calls.append((count, [place_of(v, last, s) for s, v in enumerate(arriving[last], 1)]))
+    for call in calls:
+        out = add_up(out, *call)
     return out
 
 

time: 96.7 us -> 101 us (1.044)
  the two profiles are of different devices: /device:TPU:0 before, /device:TPU:24 now
where the time goes in v6:
time: 101 us
  waiting for transfers between devices  42.6 us (42%)
  Pallas kernels  30 us (30%)
  starting transfers between devices  13 us (13%)
  other arithmetic  8.73 us (9%)
  local copies, waits for them, and re-layouts  5.08 us (5%)
  between operations  1.15 us (1%)
    ppermute x18, waiting for transfers between devices, send(): return lax.ppermute(value, AXES, pairs)  42.6 us
    ppermute x18, starting transfers between devices, send(): return lax.ppermute(value, AXES, pairs)  13 us
    pallas_call x6, Pallas kernels, long_range(): pl.pallas_call(functools.partial(long_kernel, blocks=len(blocks), chains=...  11 us
    pallas_call x1, Pallas kernels, short_range(): pl.pallas_call(kernel, out_shape=pltpu.HBM((row_count, 2 * subs * width),...  9.65 us
    pallas_call x3, Pallas kernels, final_sum(): pl.pallas_call(functools.partial(final_kernel, pieces=count, blocks=block...  9.38 us
    select_n x5, other arithmetic, pick(): value = jnp.where(wanted == k, block[window], value)  5.88 us
    unnamed x52, local copies, waits for them, and re-layouts  4.41 us
  transfers between devices with their start and end apart: 18, of which 8 were waited for; matrix products, arithmetic and copies ran while one was open for 7% of the time, Pallas kernels for 27%

profile of v6, /device:TPU:24, one launch (start us, length us, event | category | flops | bytes accessed | tf_op | source)
XLA Modules:
  0.0 100.7 jit_solution(6977988943094902591)
XLA Ops:
  1.2 1.6 %multiply_convert_fusion = bf16[256,2,512]{2,1,0:T(2,128)(2,1)S(1)} fusion(bf16[256,2,512]{2,1,0:T(2,128)(2,1)} %param.11, f32[512]{0:T(512)} %param.13), kind=kLoop, calls=%fused_computation | loop fusion | flops 786432 | bytes 1050624 | tf_op jit(solution)/shard_map/convert_element_type | solution.py:295
  3.4 1.6 %collective-permute-start.4 = (bf16[1024,256]{1,0:T(8,128)(2,1)S(1)}, bf16[1024,256]{1,0:T(8,128)(2,1)S(1)}, u32[]{:S(2)}, u32[]{:S(2)}) collective-permute-start(bf16[1024,256]{1,0:T(8,128)(2,1)S(1)} %bitcast.39), channel_id=1, source_target_pairs={{0,2},{1,3},{2,0},{3,1},{4,6},{5,7},{6,4},{7,5},{8,10},{9,11},{10,... | collective-permute-start | bytes 1572872 | tf_op jit(solution)/shard_map/ppermute | solution.py:337
  5.0 1.5 %collective-permute-start.1 = (bf16[1024,256]{1,0:T(8,128)(2,1)S(1)}, bf16[1024,256]{1,0:T(8,128)(2,1)S(1)}, u32[]{:S(2)}, u32[]{:S(2)}) collective-permute-start(bf16[1024,256]{1,0:T(8,128)(2,1)S(1)} %bitcast.40), channel_id=1, source_target_pairs={{0,16},{1,17},{2,18},{3,19},{4,20},{5,21},{6,22},{7,23},{8,24},{9,... | collective-permute-start | bytes 1572872 | tf_op jit(solution)/shard_map/ppermute | solution.py:337
  7.9 9.2 %collective-permute-done.4.refs_4_ = bf16[1024,256]{1,0:T(8,128)(2,1)S(1)} collective-permute-done((bf16[1024,256]{1,0:T(8,128)(2,1)S(1)}, bf16[1024,256]{1,0:T(8,128)(2,1)S(1)}, u32[]{:S(2)}, u32[]{:S(2)}) %collective-permute-start.4) | collective-permute-done | bytes 524320 | tf_op jit(solution)/shard_map/ppermute | solution.py:337
  17.1 1.2 %collective-permute-done.1.refs_5_ = bf16[1024,256]{1,0:T(8,128)(2,1)S(1)} collective-permute-done((bf16[1024,256]{1,0:T(8,128)(2,1)S(1)}, bf16[1024,256]{1,0:T(8,128)(2,1)S(1)}, u32[]{:S(2)}, u32[]{:S(2)}) %collective-permute-start.1) | collective-permute-done | bytes 524320 | tf_op jit(solution)/shard_map/ppermute | solution.py:337
  18.4 1.3 %collective-permute-done = bf16[256,1024]{1,0:T(8,128)(2,1)} collective-permute-done((bf16[256,1024]{1,0:T(8,128)(2,1)S(1)}, bf16[256,1024]{1,0:T(8,128)(2,1)}, u32[]{:S(2)}, u32[]{:S(2)}) %collective-permute-start) | collective-permute-done | bytes 524320 | tf_op jit(solution)/shard_map/ppermute | solution.py:337
  20.2 1.3 %collective-permute-start.3 = (bf16[256,1024]{1,0:T(8,128)(2,1)S(1)}, bf16[256,1024]{1,0:T(8,128)(2,1)}, u32[]{:S(2)}, u32[]{:S(2)}) collective-permute-start(bf16[256,1024]{1,0:T(8,128)(2,1)S(1)} %bitcast.46), channel_id=1, source_target_pairs={{0,4},{1,5},{2,6},{3,7},{4,12},{5,13},{6,14},{7,15},{8,0},{9,1},{1... | collective-permute-start | bytes 1572872 | tf_op jit(solution)/shard_map/ppermute | solution.py:337
  22.1 1.6 %collective-permute-start.2 = (bf16[256,1024]{1,0:T(8,128)(2,1)}, bf16[256,1024]{1,0:T(8,128)(2,1)}, u32[]{:S(2)}, u32[]{:S(2)}) collective-permute-start(bf16[256,1024]{1,0:T(8,128)(2,1)} %collective-permute-done), channel_id=1, source_target_pairs={{0,8},{1,9},{2,10},{3,11},{4,0},{5,1},{6,2},{7,3},{8,12},{9,13},{1... | collective-permute-start | bytes 1572872 | tf_op jit(solution)/shard_map/ppermute | solution.py:337
  23.6 20.8 %collective-permute-done.3 = bf16[256,1024]{1,0:T(8,128)(2,1)} collective-permute-done((bf16[256,1024]{1,0:T(8,128)(2,1)S(1)}, bf16[256,1024]{1,0:T(8,128)(2,1)}, u32[]{:S(2)}, u32[]{:S(2)}) %collective-permute-start.3) | collective-permute-done | bytes 524320 | tf_op jit(solution)/shard_map/ppermute | solution.py:337
  46.4 1.5 %collective-permute-start.7 = (bf16[256,1024]{1,0:T(8,128)(2,1)S(1)}, bf16[256,1024]{1,0:T(8,128)(2,1)S(1)}, u32[]{:S(2)}, u32[]{:S(2)}) collective-permute-start(bf16[256,1024]{1,0:T(8,128)(2,1)S(1)} %select_select_fusion.2), channel_id=1, source_target_pairs={{0,16},{1,17},{2,18},{3,19},{4,20},{5,21},{6,22},{7,23},{8,24},{9,... | collective-permute-start | bytes 1572872 | tf_op jit(solution)/shard_map/ppermute | solution.py:337
  49.4 9.7 %short_range.1.refs_2_.refs_3_.refs_1_ = f32[2048,512]{1,0:T(8,128)} custom-call(s32[1]{0:T(128)} %bitcast.10.half_ref, s32[32]{0:T(128)S(1)} %get-tuple-element.57.live_ref, s32[32]{0:T(128)S(1)} %get-tuple-element.56.sub_ref, f32[3,32]{1,0:T(4,128)S(1)} %pad_maximum_fusion.1.meta_ref, bf16[128,4096]{1,0:T(8,128)(2,1)} %basis_ref.1, ...), custom_call_target="tpu_custom_call" | custom-call | flops 4294967296 | bytes 1 | tf_op jit(solution)/shard_map/short_range/pallas_call | solution.py:125
  61.7 3.3 %long_range.6 = bf16[512,512]{1,0:T(8,128)(2,1)} custom-call(bf16[256,1024]{1,0:T(8,128)(2,1)S(1)} %select_select_fusion.1.refs_0_, bf16[256,1024]{1,0:T(8,128)(2,1)S(1)} %collective-permute-done.7.refs_1_, bf16[256,1024]{1,0:T(8,128)(2,1)S(1)} %collective-permute-done.8.refs_2_, bf16[256,1024]{1,0:T(8,128)(2,1)} %collective-permute-done.9.refs_3_, ...), custom_call_target="tpu_custom_call" | custom-call | flops 1 | bytes 1 | tf_op jit(solution)/shard_map/long_range/pallas_call | solution.py:181
  64.9 1.2 %select_select_fusion.4 = bf16[128,1024]{1,0:T(8,128)(2,1)S(1)} fusion(bf16[256,1024]{1,0:T(8,128)(2,1)} %collective-permute-done.3, bf16[256,1024]{1,0:T(8,128)(2,1)} %collective-permute-done.2, bf16[256,1024]{1,0:T(8,128)(2,1)} %collective-permute-done, pred[]{:T(512)S(6)} %eq.81, pred[]{:T(512)S(6)} %eq.72), kind=kLoop, calls=%fused_computation.6 | loop fusion | flops 262144 | bytes 1048578 | tf_op jit(solution)/shard_map/jit(_where)/select_n | solution.py:371
  66.2 1.2 %select_select_fusion.refs_0_ = bf16[256,1024]{1,0:T(8,128)(2,1)S(1)} fusion(bf16[256,1024]{1,0:T(8,128)(2,1)} %collective-permute-done, bf16[256,1024]{1,0:T(8,128)(2,1)} %collective-permute-done.2, bf16[256,1024]{1,0:T(8,128)(2,1)} %collective-permute-done.3, pred[]{:T(512)S(6)} %eq.82, pred[]{:T(512)S(6)} %eq.71), kind=kLoop, calls=%fused_computation.2 | loop fusion | flops 524288 | bytes 2097154 | tf_op jit(solution)/shard_map/jit(_where)/select_n | solution.py:371
  67.5 1.8 %collective-permute-done.11.refs_1_ = bf16[128,1024]{1,0:T(8,128)(2,1)S(1)} collective-permute-done((bf16[128,1024]{1,0:T(8,128)(2,1)S(1)}, bf16[128,1024]{1,0:T(8,128)(2,1)S(1)}, u32[]{:S(2)}, u32[]{:S(2)}) %collective-permute-start.11) | collective-permute-done | bytes 262176 | tf_op jit(solution)/shard_map/ppermute | solution.py:337
  70.6 2.3 %long_range.7.refs_0_ = f32[512,512]{1,0:T(8,128)S(1)} custom-call(bf16[256,1024]{1,0:T(8,128)(2,1)S(1)} %select_select_fusion.1.refs_0_, bf16[256,1024]{1,0:T(8,128)(2,1)S(1)} %copy-done.8, bf16[256,1024]{1,0:T(8,128)(2,1)S(1)} %copy-done.10, bf16[256,1024]{1,0:T(8,128)(2,1)} %collective-permute-done.9.refs_3_, bf16[1024,256]{1,0:T(8,128)(2,1)S(1)} %bitcast.41, ...), custom_call_target="tpu_custom_call" | custom-call | flops 1 | bytes 1 | tf_op jit(solution)/shard_map/long_range/pallas_call | solution.py:181
  74.7 3.3 %collective-permute-done.10.refs_1_ = bf16[128,1024]{1,0:T(8,128)(2,1)S(1)} collective-permute-done((bf16[128,1024]{1,0:T(8,128)(2,1)S(1)}, bf16[128,1024]{1,0:T(8,128)(2,1)S(1)}, u32[]{:S(2)}, u32[]{:S(2)}) %collective-permute-start.10) | collective-permute-done | bytes 262176 | tf_op jit(solution)/shard_map/ppermute | solution.py:337
  81.3 3.7 %collective-permute-done.14.refs_1_ = bf16[512,512]{1,0:T(8,128)(2,1)} collective-permute-done((bf16[512,512]{1,0:T(8,128)(2,1)}, bf16[512,512]{1,0:T(8,128)(2,1)}, u32[]{:S(2)}, u32[]{:S(2)}) %collective-permute-start.14) | collective-permute-done | bytes 524320 | tf_op jit(solution)/shard_map/ppermute | solution.py:337
  85.0 3.7 %final_sum.3.refs_4_ = bf16[2048,2,256]{2,1,0:T(2,128)(2,1)} custom-call(s32[4]{0:T(128)S(1)} %pad_add_fusion.3.order_ref, f32[512,512]{1,0:T(8,128)S(1)} %copy-done.4, bf16[512,512]{1,0:T(8,128)(2,1)} %collective-permute-done.14.refs_1_, f32[2048,512]{1,0:T(8,128)} %short_range.1.refs_2_.refs_3_.refs_1_), custom_call_target="tpu_custom_call" | custom-call | flops 1 | bytes 1 | tf_op jit(solution)/shard_map/final_sum/pallas_call | solution.py:223
  88.8 2.4 %long_range.10 = bf16[256,512]{1,0:T(8,128)(2,1)} custom-call(bf16[256,1024]{1,0:T(8,128)(2,1)S(1)} %select_select_fusion.refs_0_, bf16[128,1024]{1,0:T(8,128)(2,1)S(1)} %collective-permute-done.10.refs_1_, bf16[256,1024]{1,0:T(8,128)(2,1)S(1)} %collective-permute-done.12.refs_2_, bf16[128,1024]{1,0:T(8,128)(2,1)} %collective-permute-done.15.refs_3_, ...), custom_call_target="tpu_custom_call" | custom-call | flops 1 | bytes 1 | tf_op jit(solution)/shard_map/long_range/pallas_call | solution.py:181
  92.0 1.7 %long_range.11.refs_2_ = f32[256,512]{1,0:T(8,128)S(1)} custom-call(bf16[256,1024]{1,0:T(8,128)(2,1)S(1)} %select_select_fusion.refs_0_, bf16[128,1024]{1,0:T(8,128)(2,1)S(1)} %collective-permute-done.10.refs_1_, bf16[256,1024]{1,0:T(8,128)(2,1)S(1)} %collective-permute-done.12.refs_2_, bf16[128,1024]{1,0:T(8,128)(2,1)} %collective-permute-done.15.refs_3_, ...), custom_call_target="tpu_custom_call" | custom-call | flops 1 | bytes 1 | tf_op jit(solution)/shard_map/long_range/pallas_call | solution.py:181
  93.6 3.3 %final_sum.4.refs_2_ = bf16[2048,2,256]{2,1,0:T(2,128)(2,1)} custom-call(s32[6]{0:T(128)S(1)} %stack.82.order_ref, f32[256,512]{1,0:T(8,128)S(1)} %copy-done.6, bf16[256,512]{1,0:T(8,128)(2,1)} %collective-permute-done.17.refs_1_, f32[256,512]{1,0:T(8,128)S(1)} %long_range.11.refs_2_, ...), custom_call_target="tpu_custom_call", output_to_operand_aliasing={{}: (5, {})} | custom-call | flops 1 | bytes 1 | tf_op jit(solution)/shard_map/final_sum/pallas_call | solution.py:223
  97.0 1.3 %collective-permute-done.16.refs_0_ = bf16[256,512]{1,0:T(8,128)(2,1)S(1)} collective-permute-done((bf16[256,512]{1,0:T(8,128)(2,1)}, bf16[256,512]{1,0:T(8,128)(2,1)S(1)}, u32[]{:S(2)}, u32[]{:S(2)}) %collective-permute-start.16) | collective-permute-done | bytes 262176 | tf_op jit(solution)/shard_map/ppermute | solution.py:337
  98.3 2.4 %final_sum.5 = bf16[2048,2,256]{2,1,0:T(2,128)(2,1)} custom-call(s32[2]{0:T(128)S(1)} %pad_add_fusion.2.order_ref, bf16[256,512]{1,0:T(8,128)(2,1)S(1)} %collective-permute-done.16.refs_0_, f32[2048,512]{1,0:T(8,128)} %short_range.1.refs_2_.refs_3_.refs_1_, bf16[2048,2,256]{2,1,0:T(2,128)(2,1)} %final_sum.4.refs_2_), custom_call_target="tpu_custom_call", output_to_operand_aliasing={{}: (3, {})} | custom-call | flops 1 | bytes 1 | tf_op jit(solution)/shard_map/final_sum/pallas_call | solution.py:223
  (95 shorter events, 16.7 us)
Async XLA Ops:
  0.0 7.8 %copy-start.22 = (s32[16]{0:T(128)S(1)}, s32[16]{0:T(128)}, u32[]{:S(2)}) copy-start(s32[16]{0:T(128)} %param.19) | copy-start | bytes 196
  1.2 44.0 %copy-start.19 = (bf16[32,8,2,512]{3,1,2,0:T(8,128)(2,1)}, bf16[32,8,2,512]{3,1,2,0:T(8,128)(2,1)S(1)}, u32[]{:S(2)}) copy-start(bf16[32,8,2,512]{3,1,2,0:T(8,128)(2,1)S(1)} %copy.18) | copy-start | bytes 1572868
  3.4 13.7 %collective-permute-start.4 = (bf16[1024,256]{1,0:T(8,128)(2,1)S(1)}, bf16[1024,256]{1,0:T(8,128)(2,1)S(1)}, u32[]{:S(2)}, u32[]{:S(2)}) collective-permute-start(bf16[1024,256]{1,0:T(8,128)(2,1)S(1)} %bitcast.39), channel_id=1, source_target_pairs={{0,2},{1,3},{2,0},{3,1},{4,6},{5,7},{6,4},{7,5},{8,10},{9,11},{10,... | collective-permute-start | bytes 1572872 | tf_op jit(solution)/shard_map/ppermute | solution.py:337
  5.0 13.4 %collective-permute-start.1 = (bf16[1024,256]{1,0:T(8,128)(2,1)S(1)}, bf16[1024,256]{1,0:T(8,128)(2,1)S(1)}, u32[]{:S(2)}, u32[]{:S(2)}) collective-permute-start(bf16[1024,256]{1,0:T(8,128)(2,1)S(1)} %bitcast.40), channel_id=1, source_target_pairs={{0,16},{1,17},{2,18},{3,19},{4,20},{5,21},{6,22},{7,23},{8,24},{9,... | collective-permute-start | bytes 1572872 | tf_op jit(solution)/shard_map/ppermute | solution.py:337
  6.5 13.2 %collective-permute-start = (bf16[256,1024]{1,0:T(8,128)(2,1)S(1)}, bf16[256,1024]{1,0:T(8,128)(2,1)}, u32[]{:S(2)}, u32[]{:S(2)}) collective-permute-start(bf16[256,1024]{1,0:T(8,128)(2,1)S(1)} %bitcast.45), channel_id=1, source_target_pairs={{0,8},{1,9},{2,10},{3,11},{4,0},{5,1},{6,2},{7,3},{8,12},{9,13},{1... | collective-permute-start | bytes 1572872 | tf_op jit(solution)/shard_map/ppermute | solution.py:337
  7.5 40.4 %copy-start.23 = (f32[125]{0:T(128)S(1)}, f32[125]{0:T(128)}, u32[]{:S(2)}) copy-start(f32[125]{0:T(128)} %param.16) | copy-start | bytes 1504
  7.5 40.4 %copy-start.24 = (f32[125]{0:T(128)S(1)}, f32[125]{0:T(128)}, u32[]{:S(2)}) copy-start(f32[125]{0:T(128)} %param.17) | copy-start | bytes 1504
  7.9 40.0 %copy-start.15 = (bf16[17,128,128]{2,1,0:T(8,128)(2,1)}, bf16[17,128,128]{2,1,0:T(8,128)(2,1)S(1)}, u32[]{:S(2)}) copy-start(bf16[17,128,128]{2,1,0:T(8,128)(2,1)S(1)} %pad_maximum_fusion.refs_0_) | copy-start | bytes 1671172
  18.4 30.9 %copy-start = (bf16[1024,256]{1,0:T(8,128)(2,1)}, bf16[1024,256]{1,0:T(8,128)(2,1)S(1)}, u32[]{:S(2)}) copy-start(bf16[1024,256]{1,0:T(8,128)(2,1)S(1)} %collective-permute-done.1.refs_5_) | copy-start | bytes 1572868
  19.7 24.8 %collective-permute-start.5 = (bf16[17,128,128]{2,1,0:T(8,128)(2,1)S(1)}, bf16[17,128,128]{2,1,0:T(8,128)(2,1)}, u32[]{:S(2)}, u32[]{:S(2)}) collective-permute-start(bf16[17,128,128]{2,1,0:T(8,128)(2,1)S(1)} %pad_maximum_fusion.refs_0_), channel_id=1, source_target_pairs={{0,16},{1,17},{2,18},{3,19},{4,20},{5,21},{6,22},{7,23},{8,24},{9,... | collective-permute-start | bytes 1671176 | tf_op jit(solution)/shard_map/ppermute | solution.py:337
  20.2 24.2 %collective-permute-start.3 = (bf16[256,1024]{1,0:T(8,128)(2,1)S(1)}, bf16[256,1024]{1,0:T(8,128)(2,1)}, u32[]{:S(2)}, u32[]{:S(2)}) collective-permute-start(bf16[256,1024]{1,0:T(8,128)(2,1)S(1)} %bitcast.46), channel_id=1, source_target_pairs={{0,4},{1,5},{2,6},{3,7},{4,12},{5,13},{6,14},{7,15},{8,0},{9,1},{1... | collective-permute-start | bytes 1572872 | tf_op jit(solution)/shard_map/ppermute | solution.py:337
  21.6 22.9 %collective-permute-start.6 = (bf16[1024,256]{1,0:T(8,128)(2,1)S(1)}, bf16[1024,256]{1,0:T(8,128)(2,1)S(1)}, u32[]{:S(2)}, u32[]{:S(2)}) collective-permute-start(bf16[1024,256]{1,0:T(8,128)(2,1)S(1)} %collective-permute-done.1.refs_5_), channel_id=1, source_target_pairs={{0,2},{1,3},{2,0},{3,1},{4,6},{5,7},{6,4},{7,5},{8,10},{9,11},{10,... | collective-permute-start | bytes 1572872 | tf_op jit(solution)/shard_map/ppermute | solution.py:337
  22.1 37.6 %collective-permute-start.2 = (bf16[256,1024]{1,0:T(8,128)(2,1)}, bf16[256,1024]{1,0:T(8,128)(2,1)}, u32[]{:S(2)}, u32[]{:S(2)}) collective-permute-start(bf16[256,1024]{1,0:T(8,128)(2,1)} %collective-permute-done), channel_id=1, source_target_pairs={{0,8},{1,9},{2,10},{3,11},{4,0},{5,1},{6,2},{7,3},{8,12},{9,13},{1... | collective-permute-start | bytes 1572872 | tf_op jit(solution)/shard_map/ppermute | solution.py:337
  46.4 12.7 %collective-permute-start.7 = (bf16[256,1024]{1,0:T(8,128)(2,1)S(1)}, bf16[256,1024]{1,0:T(8,128)(2,1)S(1)}, u32[]{:S(2)}, u32[]{:S(2)}) collective-permute-start(bf16[256,1024]{1,0:T(8,128)(2,1)S(1)} %select_select_fusion.2), channel_id=1, source_target_pairs={{0,16},{1,17},{2,18},{3,19},{4,20},{5,21},{6,22},{7,23},{8,24},{9,... | collective-permute-start | bytes 1572872 | tf_op jit(solution)/shard_map/ppermute | solution.py:337
  49.3 12.3 %collective-permute-start.8 = (bf16[256,1024]{1,0:T(8,128)(2,1)S(1)}, bf16[256,1024]{1,0:T(8,128)(2,1)S(1)}, u32[]{:S(2)}, u32[]{:S(2)}) collective-permute-start(bf16[256,1024]{1,0:T(8,128)(2,1)S(1)} %select_select_fusion.1.refs_0_), channel_id=1, source_target_pairs={{0,1},{1,0},{2,3},{3,2},{4,5},{5,4},{6,7},{7,6},{8,9},{9,8},{10,11... | collective-permute-start | bytes 1572872 | tf_op jit(solution)/shard_map/ppermute | solution.py:337
  59.1 2.5 %collective-permute-start.9 = (bf16[256,1024]{1,0:T(8,128)(2,1)S(1)}, bf16[256,1024]{1,0:T(8,128)(2,1)}, u32[]{:S(2)}, u32[]{:S(2)}) collective-permute-start(bf16[256,1024]{1,0:T(8,128)(2,1)S(1)} %collective-permute-done.7.refs_1_), channel_id=1, source_target_pairs={{0,1},{1,0},{2,3},{3,2},{4,5},{5,4},{6,7},{7,6},{8,9},{9,8},{10,11... | collective-permute-start | bytes 1572872 | tf_op jit(solution)/shard_map/ppermute | solution.py:337
  60.8 8.4 %collective-permute-start.11 = (bf16[128,1024]{1,0:T(8,128)(2,1)S(1)}, bf16[128,1024]{1,0:T(8,128)(2,1)S(1)}, u32[]{:S(2)}, u32[]{:S(2)}) collective-permute-start(bf16[128,1024]{1,0:T(8,128)(2,1)S(1)} %select_select_fusion.3), channel_id=1, source_target_pairs={{0,16},{1,17},{2,18},{3,19},{4,20},{5,21},{6,22},{7,23},{8,24},{9,... | collective-permute-start | bytes 786440 | tf_op jit(solution)/shard_map/ppermute | solution.py:337
  67.4 6.5 %collective-permute-start.12 = (bf16[256,1024]{1,0:T(8,128)(2,1)S(1)}, bf16[256,1024]{1,0:T(8,128)(2,1)S(1)}, u32[]{:S(2)}, u32[]{:S(2)}) collective-permute-start(bf16[256,1024]{1,0:T(8,128)(2,1)S(1)} %select_select_fusion.refs_0_), channel_id=1, source_target_pairs={{0,1},{1,0},{2,3},{3,2},{4,5},{5,4},{6,7},{7,6},{8,9},{9,8},{10,11... | collective-permute-start | bytes 1572872 | tf_op jit(solution)/shard_map/ppermute | solution.py:337
  69.2 4.7 %collective-permute-start.13 = (bf16[128,1024]{1,0:T(8,128)(2,1)S(1)}, bf16[128,1024]{1,0:T(8,128)(2,1)S(1)}, u32[]{:S(2)}, u32[]{:S(2)}) collective-permute-start(bf16[128,1024]{1,0:T(8,128)(2,1)S(1)} %collective-permute-done.11.refs_1_), channel_id=1, source_target_pairs={{0,1},{1,0},{2,3},{3,2},{4,5},{5,4},{6,7},{7,6},{8,9},{9,8},{10,11... | collective-permute-start | bytes 786440 | tf_op jit(solution)/shard_map/ppermute | solution.py:337
  69.2 8.7 %collective-permute-start.10 = (bf16[128,1024]{1,0:T(8,128)(2,1)S(1)}, bf16[128,1024]{1,0:T(8,128)(2,1)S(1)}, u32[]{:S(2)}, u32[]{:S(2)}) collective-permute-start(bf16[128,1024]{1,0:T(8,128)(2,1)S(1)} %select_select_fusion.4), channel_id=1, source_target_pairs={{0,16},{1,17},{2,18},{3,19},{4,20},{5,21},{6,22},{7,23},{8,24},{9,... | collective-permute-start | bytes 786440 | tf_op jit(solution)/shard_map/ppermute | solution.py:337
  70.0 15.1 %collective-permute-start.14 = (bf16[512,512]{1,0:T(8,128)(2,1)}, bf16[512,512]{1,0:T(8,128)(2,1)}, u32[]{:S(2)}, u32[]{:S(2)}) collective-permute-start(bf16[512,512]{1,0:T(8,128)(2,1)} %long_range.6), channel_id=1, source_target_pairs={{0,2},{1,3},{2,0},{3,1},{4,6},{5,7},{6,4},{7,5},{8,10},{9,11},{10,... | collective-permute-start | bytes 1572872 | tf_op jit(solution)/shard_map/ppermute | solution.py:337
  78.0 10.8 %collective-permute-start.15 = (bf16[128,1024]{1,0:T(8,128)(2,1)S(1)}, bf16[128,1024]{1,0:T(8,128)(2,1)}, u32[]{:S(2)}, u32[]{:S(2)}) collective-permute-start(bf16[128,1024]{1,0:T(8,128)(2,1)S(1)} %collective-permute-done.10.refs_1_), channel_id=1, source_target_pairs={{0,1},{1,0},{2,3},{3,2},{4,5},{5,4},{6,7},{7,6},{8,9},{9,8},{10,11... | collective-permute-start | bytes 786440 | tf_op jit(solution)/shard_map/ppermute | solution.py:337
  78.2 15.4 %collective-permute-start.17 = (bf16[256,512]{1,0:T(8,128)(2,1)}, bf16[256,512]{1,0:T(8,128)(2,1)}, u32[]{:S(2)}, u32[]{:S(2)}) collective-permute-start(bf16[256,512]{1,0:T(8,128)(2,1)} %copy-done.17), channel_id=1, source_target_pairs={{0,2},{1,3},{2,0},{3,1},{4,6},{5,7},{6,4},{7,5},{8,10},{9,11},{10,... | collective-permute-start | bytes 786440 | tf_op jit(solution)/shard_map/ppermute | solution.py:337
  91.1 7.1 %collective-permute-start.16 = (bf16[256,512]{1,0:T(8,128)(2,1)}, bf16[256,512]{1,0:T(8,128)(2,1)S(1)}, u32[]{:S(2)}, u32[]{:S(2)}) collective-permute-start(bf16[256,512]{1,0:T(8,128)(2,1)} %long_range.10), channel_id=1, source_target_pairs={{0,2},{1,3},{2,0},{3,1},{4,6},{5,7},{6,4},{7,5},{8,10},{9,11},{10,... | collective-permute-start | bytes 786440 | tf_op jit(solution)/shard_map/ppermute | solution.py:337
  (19 other events, 81.2 us)

commit v7 on v6

--- a/solution.py
+++ b/solution.py
@@ -149,50 +149,74 @@
     )(half, live, sub_ids, meta, in_hbm(aux_basis), aux_decay.reshape(1, -1), *items)
 
 
-def long_kernel(*refs, blocks, chains, window):
+def long_kernel(*refs, blocks, chains, pieces, window):
     parts = refs[: blocks * chains]
-    factors = refs[blocks * chains : (blocks + 1) * chains]
-    out_ref, right = refs[-2:]
+    factors = refs[blocks * chains : (blocks + pieces) * chains]
+    outs = refs[(blocks + pieces) * chains : -3]
+    right, own, own_sem = refs[-3:]
     depth, width = factors[0].shape
     half = depth // 2
-    for chain, factor in enumerate(factors):
-        top = chain * depth
-        right[top : top + depth, 0:width] = factor[...]
-        right[top : top + half, width:] = factor[half:, :]
-        right[top + half : top + depth, width:] = -factor[0:half, :]
     count = window[-1]
-    for block in range(blocks):
-        left = jnp.concatenate(
-            [
-                parts[block * chains + chain][pl.ds(window[chain], count), :]
-                for chain in range(chains)
-            ],
-            axis=1,
-        )
-        made = jnp.dot(left, right[...], preferred_element_type=jnp.float32)
-        out_ref[block * count : (block + 1) * count, :] = made.astype(out_ref.dtype)
-
-
-def long_range(blocks, factors, window, dtype):
-    depth, width = factors[0].shape
-    chains = len(factors)
-    all_rows = len(blocks) * window[-1]
-    flat = [v for group in blocks for v in group] + list(factors)
+    copies = []
+    for piece in reversed(range(pieces)):
+        for chain in range(chains):
+            factor = factors[piece * chains + chain]
+            top = chain * depth
+            right[top : top + depth, 0:width] = factor[...]
+            right[top : top + half, width:] = factor[half:, :]
+            right[top + half : top + depth, width:] = -factor[0:half, :]
+        for block in range(blocks):
+            left = jnp.concatenate(
+                [
+                    parts[block * chains + chain][pl.ds(window[chain], count), :]
+                    for chain in range(chains)
+                ],
+                axis=1,
+            )
+            total = jnp.dot(left, right[...], preferred_element_type=jnp.float32)
+            if piece:
+                outs[piece][block * count : (block + 1) * count, :] = total.astype(outs[piece].dtype)
+                continue
+            own[block] = total
+            target = outs[0].at[pl.ds(block * count, count), :]
+            copies.append(pltpu.make_async_copy(own.at[block], target, own_sem.at[block]))
+            copies[-1].start()
+    for copy in copies:
+        copy.wait()
+
+
+def long_range(blocks, factors, window):
+    depth, width = factors[0][0].shape
+    chains = len(factors[0])
+    pieces = len(factors)
+    count = window[-1]
+    shape = (len(blocks) * count, 2 * width)
+    flat = [v for group in [*blocks, *factors] for v in group]
     return pl.pallas_call(
-        functools.partial(long_kernel, blocks=len(blocks), chains=chains, window=window),
-        out_shape=jax.ShapeDtypeStruct((all_rows, 2 * width), dtype),
+        functools.partial(
+            long_kernel, blocks=len(blocks), chains=chains, pieces=pieces, window=window
+        ),
+        out_shape=[pltpu.HBM(shape, jnp.float32)]
+        + [jax.ShapeDtypeStruct(shape, jnp.bfloat16)] * (pieces - 1),
         in_specs=[pl.BlockSpec(memory_space=pltpu.VMEM)] * len(flat),
-        out_specs=pl.BlockSpec(memory_space=pltpu.VMEM),
-        scratch_shapes=[pltpu.VMEM((chains * depth, 2 * width), jnp.bfloat16)],
+        out_specs=[pl.BlockSpec(memory_space=pltpu.HBM)]
+        + [pl.BlockSpec(memory_space=pltpu.VMEM)] * (pieces - 1),
+        scratch_shapes=[
+            pltpu.VMEM((chains * depth, 2 * width), jnp.bfloat16),
+            pltpu.VMEM((len(blocks), count, 2 * width), jnp.float32),
+            pltpu.SemaphoreType.DMA((len(blocks),)),
+        ],
         compiler_params=pltpu.CompilerParams(vmem_limit_bytes=VMEM_BYTES),
         cost_estimate=SMALL_COST,
         name="long_range",
     )(*flat)
 
 
-def final_kernel(order_ref, *refs, pieces, blocks, rows, aliased):
+def final_kernel(order_ref, *refs, pieces, blocks, rows, aliased, stay):
     short_ref = refs[pieces]
-    out_ref, terms, made, term_sem, out_sem = refs[pieces + 1 + aliased :]
+    out_ref, *scratch = refs[pieces + 1 + aliased :]
+    parts, (terms, made, part_sem, term_sem, out_sem) = scratch[:-5], scratch[-5:]
+    parts = [parts.pop(0) if held else ref for held, ref in zip(stay, refs)]
     steps = pieces * blocks
     windows = [pl.ds(pl.multiple_of(order_ref[n] * rows, rows), rows) for n in range(steps)]
     arriving = []
@@ -201,11 +225,19 @@
             pltpu.make_async_copy(short_ref.at[window, :], terms.at[n], term_sem.at[n])
         )
         arriving[-1].start()
+        piece = n // blocks
+        if n % blocks == 0 and stay[piece]:
+            part = pltpu.make_async_copy(refs[piece], parts[piece], part_sem.at[piece])
+            part.start()
+            arriving[-1] = (part, arriving[-1])
+        else:
+            arriving[-1] = (arriving[-1],)
     leaving = []
     for n, window in enumerate(windows):
-        arriving[n].wait()
+        for copy in arriving[n]:
+            copy.wait()
         top = n % blocks * rows
-        total = refs[n // blocks][top : top + rows, :].astype(jnp.float32) + terms[n]
+        total = parts[n // blocks][top : top + rows, :].astype(jnp.float32) + terms[n]
         made[n] = total.astype(made.dtype).reshape(made.shape[1:])
         leaving.append(pltpu.make_async_copy(made.at[n], out_ref.at[window], out_sem.at[n]))
         leaving[-1].start()
@@ -220,16 +252,21 @@
     blocks = pieces[0].shape[0] // rows
     steps = count * blocks
     aliased = earlier is not None
+    stay = [piece.dtype == jnp.float32 for piece in pieces]
     return pl.pallas_call(
-        functools.partial(final_kernel, pieces=count, blocks=blocks, rows=rows, aliased=aliased),
-        out_shape=jax.ShapeDtypeStruct((row_count, 2, columns // 2), jnp.bfloat16),
+        functools.partial(
+            final_kernel, pieces=count, blocks=blocks, rows=rows, aliased=aliased, stay=stay
+        ),
+        out_shape=pltpu.HBM((row_count, 2, columns // 2), jnp.bfloat16),
         in_specs=[pl.BlockSpec(memory_space=pltpu.SMEM)]
-        + [pl.BlockSpec(memory_space=pltpu.VMEM)] * count
+        + [pl.BlockSpec(memory_space=pltpu.HBM if held else pltpu.VMEM) for held in stay]
         + [pl.BlockSpec(memory_space=pltpu.HBM)] * (1 + aliased),
         out_specs=pl.BlockSpec(memory_space=pltpu.HBM),
-        scratch_shapes=[
+        scratch_shapes=[pltpu.VMEM(piece.shape, piece.dtype) for piece, held in zip(pieces, stay) if held]
+        + [
             pltpu.VMEM((steps, rows, columns), jnp.float32),
             pltpu.VMEM((steps, rows, 2, columns // 2), jnp.bfloat16),
+            pltpu.SemaphoreType.DMA((count,)),
             pltpu.SemaphoreType.DMA((steps,)),
             pltpu.SemaphoreType.DMA((steps,)),
         ],
@@ -237,7 +274,12 @@
         compiler_params=pltpu.CompilerParams(vmem_limit_bytes=VMEM_BYTES),
         cost_estimate=SMALL_COST,
         name="final_sum",
-    )(order, *pieces, in_hbm(short), *([earlier] if aliased else []))
+    )(
+        order,
+        *(in_hbm(piece) if held else piece for piece, held in zip(pieces, stay)),
+        in_hbm(short),
+        *([earlier] if aliased else []),
+    )
 
 
 def slot_table(image_dist, image_phase, images):
@@ -385,13 +427,14 @@
     turned_x = to_plane(turned)
     factors = [[turned, turned_x]] + [[over_y(turned, s)] for s in range(1, breadth)]
     packed = jnp.concatenate([item_rows, slot_block(slots, item_rows)], axis=0)
-    items_x = to_plane(after(packed, turned_x, held[1], *(pair[0] for pair in factors[1:])))
+    items_x = to_plane(packed)
+    begun = [items_x, turned_x, *(pair[0] for pair in factors[1:]), held[1], held[length - 1]]
     for s in range(1, breadth):
-        factors[s].append(over_y(turned_x, s))
+        factors[s].append(over_y(after(turned_x, *begun), s))
     for k in range(2, length // 2 + 1):
-        held[k] = along(after(held[k - 1], turned_x), 1)
+        held[k] = along(after(held[k - 1], *begun), 1)
     for k in range(2, (length + 1) // 2):
-        held[length - k] = along(after(held[length - k + 1], turned_x), -1)
+        held[length - k] = along(after(held[length - k + 1], *begun), -1)
 
     images, sub_ids, live = jnp.concatenate([slots, read_slots(items_x, slots)], axis=1)
     table = slot_table(image_dist, image_phase, images)
@@ -409,34 +452,24 @@
     arriving = []
     own = []
 
-    def product(i, s, *earlier):
+    def multiply(i, *earlier):
         n, first, count = units[i]
         blocks = list(zip(mine[n], [after(crossed[i][0], *earlier), *crossed[i][1:]]))
-        return long_range(blocks, factors[s], (first, 0, count), jnp.bfloat16 if s else jnp.float32)
-
-    def multiply(i, *earlier):
-        away.append([product(i, s, *earlier) for s in range(1, breadth)])
-        arriving.append([over_y(v, s) for s, v in enumerate(away[i], 1)])
+        made = long_range(blocks, factors, (first, 0, count))
+        own.append(made[0])
+        away.append(made[1:])
+        arriving.append([over_y(v, s) for s, v in enumerate(made[1:], 1)])
 
     for i, (n, first, count) in enumerate(units):
-        if i == 0:
-            gate = [items_x, *(pair[1] for pair in factors[1:])]
-        elif i == 1:
-            gate = [crossed[0][0], short]
-        else:
-            gate = away[i - 2]
+        gate = begun if i == 0 else [crossed[0][0], short] if i == 1 else away[i - 2]
         theirs.append(pick(True, n, slice(first, first + count), *gate))
         moved = to_plane(theirs[i])
         if first + count == rows:
             mine[n] = with_cores(pick(False, n, slice(None), theirs[i]))
-        if i > 1:
-            own.append(product(i - 2, 0, theirs[i]))
         if i:
-            multiply(i - 1, *own[-1:])
+            multiply(i - 1)
         crossed.append(with_cores(after(moved, *away[i - 1] if i else [short])))
     last = len(units) - 1
-    if last:
-        own.append(product(last - 1, 0))
 
     def place_of(piece, i, s):
         n, first, count = units[i]
@@ -455,8 +488,7 @@
         return final_sum(numbers, [piece for piece, _ in entries], short, out, count)
 
     out = add_up(None, *calls.pop(0)) if calls else None
-    multiply(last, *own, *([] if out is None else [out]))
-    own.append(product(last, 0))
+    multiply(last, *([] if out is None else [out]))
     count = units[last][2]
     calls.append((count, [place_of(own[last], last, 0)]))
     if len(calls) > 1 and calls[-2][0] == count:

time: 101 us -> 93.8 us (0.929)
  the two profiles are of different devices: /device:TPU:24 before, /device:TPU:0 now
where the time goes in v7:
time: 93.8 us; the launch traced here: 93.3 us
  waiting for transfers between devices  33.7 us (36%)
  Pallas kernels  31 us (33%)
  starting transfers between devices  17.6 us (19%)
  other arithmetic  6.13 us (7%)
  local copies, waits for them, and re-layouts  3.91 us (4%)
  between operations  0.94 us (1%)
    ppermute x18, waiting for transfers between devices, send(): return lax.ppermute(value, AXES, pairs)  33.7 us
    ppermute x18, starting transfers between devices, send(): return lax.ppermute(value, AXES, pairs)  17.6 us
    pallas_call x3, Pallas kernels, long_range(): pl.pallas_call(functools.partial(long_kernel, blocks=len(blocks), chains=...  10.8 us
    pallas_call x3, Pallas kernels, final_sum(): pl.pallas_call(functools.partial(final_kernel, pieces=count, blocks=block...  10.5 us
    pallas_call x1, Pallas kernels, short_range(): pl.pallas_call(kernel, out_shape=pltpu.HBM((row_count, 2 * subs * width),...  9.66 us
    select_n x5, other arithmetic, pick(): value = jnp.where(wanted == k, block[window], value)  4.54 us
    unnamed x24, local copies, waits for them, and re-layouts  3.24 us
  transfers between devices with their start and end apart: 18, of which 7 were waited for; matrix products, arithmetic and copies ran while one was open for 9% of the time, Pallas kernels for 31%

profile of v7, /device:TPU:0, one launch (start us, length us, event | category | flops | bytes accessed | tf_op | source)
XLA Modules:
  0.0 93.3 jit_solution(3560929242769694288)
XLA Ops:
  0.0 1.2 %copy.18 = bf16[32,8,2,512]{3,1,2,0:T(8,128)(2,1)S(1)} copy(bf16[32,8,2,512]{3,2,1,0:T(2,128)(2,1)} %bitcast.50) | data formatting | bytes 1048576
  1.2 4.1 %collective-permute-start = (bf16[256,1024]{1,0:T(8,128)(2,1)S(1)}, bf16[256,1024]{1,0:T(8,128)(2,1)}, u32[]{:S(2)}, u32[]{:S(2)}) collective-permute-start(bf16[256,1024]{1,0:T(8,128)(2,1)S(1)} %bitcast.45), channel_id=1, source_target_pairs={{0,8},{1,9},{2,10},{3,11},{4,0},{5,1},{6,2},{7,3},{8,12},{9,13},{1... | collective-permute-start | bytes 1572872 | tf_op jit(solution)/shard_map/ppermute | solution.py:379
  6.0 1.3 %copy.16 = bf16[16,128,128]{1,2,0:T(8,128)(2,1)S(1)} copy(bf16[16,128,128]{2,1,0:T(8,128)(2,1)} %param.18) | data formatting | bytes 1048576 | tf_op args[7]
  7.4 1.6 %collective-permute-start.1 = (bf16[17,128,128]{2,1,0:T(8,128)(2,1)S(1)}, bf16[17,128,128]{2,1,0:T(8,128)(2,1)}, u32[]{:S(2)}, u32[]{:S(2)}) collective-permute-start(bf16[17,128,128]{2,1,0:T(8,128)(2,1)S(1)} %pad_maximum_fusion.refs_0_), channel_id=1, source_target_pairs={{0,16},{1,17},{2,18},{3,19},{4,20},{5,21},{6,22},{7,23},{8,24},{9,... | collective-permute-start | bytes 1671176 | tf_op jit(solution)/shard_map/ppermute | solution.py:379
  10.5 1.5 %collective-permute-start.3 = (bf16[1024,256]{1,0:T(8,128)(2,1)S(1)}, bf16[1024,256]{1,0:T(8,128)(2,1)S(1)}, u32[]{:S(2)}, u32[]{:S(2)}) collective-permute-start(bf16[1024,256]{1,0:T(8,128)(2,1)S(1)} %bitcast.40), channel_id=1, source_target_pairs={{0,2},{1,3},{2,0},{3,1},{4,6},{5,7},{6,4},{7,5},{8,10},{9,11},{10,... | collective-permute-start | bytes 1572872 | tf_op jit(solution)/shard_map/ppermute | solution.py:379
  12.1 5.6 %collective-permute-done = bf16[256,1024]{1,0:T(8,128)(2,1)} collective-permute-done((bf16[256,1024]{1,0:T(8,128)(2,1)S(1)}, bf16[256,1024]{1,0:T(8,128)(2,1)}, u32[]{:S(2)}, u32[]{:S(2)}) %collective-permute-start) | collective-permute-done | bytes 524320 | tf_op jit(solution)/shard_map/ppermute | solution.py:379
  17.7 15.1 %collective-permute-done.2.refs_5_ = bf16[1024,256]{1,0:T(8,128)(2,1)S(1)} collective-permute-done((bf16[1024,256]{1,0:T(8,128)(2,1)S(1)}, bf16[1024,256]{1,0:T(8,128)(2,1)S(1)}, u32[]{:S(2)}, u32[]{:S(2)}) %collective-permute-start.2) | collective-permute-done | bytes 524320 | tf_op jit(solution)/shard_map/ppermute | solution.py:379
  32.8 1.6 %collective-permute-start.5 = (bf16[256,1024]{1,0:T(8,128)(2,1)}, bf16[256,1024]{1,0:T(8,128)(2,1)}, u32[]{:S(2)}, u32[]{:S(2)}) collective-permute-start(bf16[256,1024]{1,0:T(8,128)(2,1)} %collective-permute-done), channel_id=1, source_target_pairs={{0,8},{1,9},{2,10},{3,11},{4,0},{5,1},{6,2},{7,3},{8,12},{9,13},{1... | collective-permute-start | bytes 1572872 | tf_op jit(solution)/shard_map/ppermute | solution.py:379
  34.5 1.6 %collective-permute-start.6 = (bf16[256,1024]{1,0:T(8,128)(2,1)S(1)}, bf16[256,1024]{1,0:T(8,128)(2,1)}, u32[]{:S(2)}, u32[]{:S(2)}) collective-permute-start(bf16[256,1024]{1,0:T(8,128)(2,1)S(1)} %select_select_fusion.2), channel_id=1, source_target_pairs={{0,16},{1,17},{2,18},{3,19},{4,20},{5,21},{6,22},{7,23},{8,24},{9,... | collective-permute-start | bytes 1572872 | tf_op jit(solution)/shard_map/ppermute | solution.py:379
  38.3 1.6 %collective-permute-start.9 = (bf16[1024,256]{1,0:T(8,128)(2,1)S(1)}, bf16[1024,256]{1,0:T(8,128)(2,1)S(1)}, u32[]{:S(2)}, u32[]{:S(2)}) collective-permute-start(bf16[1024,256]{1,0:T(8,128)(2,1)S(1)} %collective-permute-done.2.refs_5_), channel_id=1, source_target_pairs={{0,2},{1,3},{2,0},{3,1},{4,6},{5,7},{6,4},{7,5},{8,10},{9,11},{10,... | collective-permute-start | bytes 1572872 | tf_op jit(solution)/shard_map/ppermute | solution.py:379
  39.9 9.7 %short_range.1.refs_2_.refs_3_.refs_1_ = f32[2048,512]{1,0:T(8,128)} custom-call(s32[1]{0:T(128)} %bitcast.10.half_ref, s32[32]{0:T(128)S(1)} %get-tuple-element.65.live_ref, s32[32]{0:T(128)S(1)} %get-tuple-element.64.sub_ref, f32[3,32]{1,0:T(4,128)S(1)} %pad_maximum_fusion.1.meta_ref, bf16[128,4096]{1,0:T(8,128)(2,1)} %basis_ref.1, ...), custom_call_target="tpu_custom_call" | custom-call | flops 4294967296 | bytes 1 | tf_op jit(solution)/shard_map/short_range/pallas_call | solution.py:125
  49.8 1.1 %select_select_fusion.3 = bf16[128,1024]{1,0:T(8,128)(2,1)S(1)} fusion(bf16[256,1024]{1,0:T(8,128)(2,1)} %copy-done.2, bf16[256,1024]{1,0:T(8,128)(2,1)} %collective-permute-done.5, bf16[256,1024]{1,0:T(8,128)(2,1)} %collective-permute-done, pred[]{:T(512)S(6)} %eq.81, pred[]{:T(512)S(6)} %eq.72), kind=kLoop, calls=%fused_computation.5 | loop fusion | flops 262144 | bytes 1048578 | tf_op jit(solution)/shard_map/jit(_where)/select_n | solution.py:413
  51.1 1.5 %collective-permute-done.9.refs_7_ = bf16[1024,256]{1,0:T(8,128)(2,1)S(1)} collective-permute-done((bf16[1024,256]{1,0:T(8,128)(2,1)S(1)}, bf16[1024,256]{1,0:T(8,128)(2,1)S(1)}, u32[]{:S(2)}, u32[]{:S(2)}) %collective-permute-start.9) | collective-permute-done | bytes 524320 | tf_op jit(solution)/shard_map/ppermute | solution.py:379
  52.6 5.2 %long_range.3 = (f32[512,512]{1,0:T(8,128)}, bf16[512,512]{1,0:T(8,128)(2,1)}) custom-call(bf16[256,1024]{1,0:T(8,128)(2,1)S(1)} %select_select_fusion.1.refs_0_, bf16[256,1024]{1,0:T(8,128)(2,1)} %collective-permute-done.6.refs_1_, bf16[256,1024]{1,0:T(8,128)(2,1)} %collective-permute-done.7.refs_2_, bf16[256,1024]{1,0:T(8,128)(2,1)S(1)} %collective-permute-done.8.refs_3_, ...), custom_call_target="tpu_custom_call" | custom-call | flops 1 | bytes 1 | tf_op jit(solution)/shard_map/long_range/pallas_call | solution.py:195
  58.9 1.1 %select_select_fusion.refs_0_ = bf16[256,1024]{1,0:T(8,128)(2,1)S(1)} fusion(bf16[256,1024]{1,0:T(8,128)(2,1)} %collective-permute-done, bf16[256,1024]{1,0:T(8,128)(2,1)} %collective-permute-done.5, bf16[256,1024]{1,0:T(8,128)(2,1)S(1)} %copy-done.3, pred[]{:T(512)S(6)} %eq.82, pred[]{:T(512)S(6)} %eq.71), kind=kLoop, calls=%fused_computation.2 | loop fusion | flops 524288 | bytes 2097154 | tf_op jit(solution)/shard_map/jit(_where)/select_n | solution.py:413
  62.4 2.0 %long_range.4 = (f32[256,512]{1,0:T(8,128)}, bf16[256,512]{1,0:T(8,128)(2,1)S(1)}) custom-call(bf16[256,1024]{1,0:T(8,128)(2,1)S(1)} %select_select_fusion.refs_0_, bf16[128,1024]{1,0:T(8,128)(2,1)S(1)} %collective-permute-done.11.refs_1_, bf16[256,1024]{1,0:T(8,128)(2,1)S(1)} %collective-permute-done.12.refs_2_, ...), custom_call_target="tpu_custom_call" | custom-call | flops 1 | bytes 1 | tf_op jit(solution)/shard_map/long_range/pallas_call | solution.py:195
  65.1 3.8 %collective-permute-done.10.refs_1_ = bf16[128,1024]{1,0:T(8,128)(2,1)S(1)} collective-permute-done((bf16[128,1024]{1,0:T(8,128)(2,1)S(1)}, bf16[128,1024]{1,0:T(8,128)(2,1)S(1)}, u32[]{:S(2)}, u32[]{:S(2)}) %collective-permute-start.10) | collective-permute-done | bytes 262176 | tf_op jit(solution)/shard_map/ppermute | solution.py:379
  69.0 1.5 %collective-permute-start.17 = (bf16[256,512]{1,0:T(8,128)(2,1)}, bf16[256,512]{1,0:T(8,128)(2,1)}, u32[]{:S(2)}, u32[]{:S(2)}) collective-permute-start(bf16[256,512]{1,0:T(8,128)(2,1)} %copy-done), channel_id=1, source_target_pairs={{0,2},{1,3},{2,0},{3,1},{4,6},{5,7},{6,4},{7,5},{8,10},{9,11},{10,... | collective-permute-start | bytes 786440 | tf_op jit(solution)/shard_map/ppermute | solution.py:379
  70.5 5.7 %collective-permute-done.14.refs_1_ = bf16[512,512]{1,0:T(8,128)(2,1)} collective-permute-done((bf16[512,512]{1,0:T(8,128)(2,1)}, bf16[512,512]{1,0:T(8,128)(2,1)}, u32[]{:S(2)}, u32[]{:S(2)}) %collective-permute-start.14) | collective-permute-done | bytes 524320 | tf_op jit(solution)/shard_map/ppermute | solution.py:379
  76.2 4.4 %final_sum.3.refs_4_ = bf16[2048,2,256]{2,1,0:T(2,128)(2,1)} custom-call(s32[4]{0:T(128)S(1)} %pad_add_fusion.3.order_ref, f32[512,512]{1,0:T(8,128)} %get-tuple-element.56.refs_0_, bf16[512,512]{1,0:T(8,128)(2,1)} %collective-permute-done.14.refs_1_, f32[2048,512]{1,0:T(8,128)} %short_range.1.refs_2_.refs_3_.refs_1_), custom_call_target="tpu_custom_call" | custom-call | flops 1 | bytes 1 | tf_op jit(solution)/shard_map/final_sum/pallas_call | solution.py:256
  80.6 3.7 %long_range.5 = (f32[256,512]{1,0:T(8,128)}, bf16[256,512]{1,0:T(8,128)(2,1)}) custom-call(bf16[256,1024]{1,0:T(8,128)(2,1)S(1)} %select_select_fusion.refs_0_, bf16[128,1024]{1,0:T(8,128)(2,1)S(1)} %collective-permute-done.10.refs_1_, bf16[256,1024]{1,0:T(8,128)(2,1)S(1)} %collective-permute-done.12.refs_2_, ...), custom_call_target="tpu_custom_call" | custom-call | flops 1 | bytes 1 | tf_op jit(solution)/shard_map/long_range/pallas_call | solution.py:195
  85.5 3.7 %final_sum.4.refs_2_ = bf16[2048,2,256]{2,1,0:T(2,128)(2,1)} custom-call(s32[6]{0:T(128)S(1)} %stack.82.order_ref, f32[256,512]{1,0:T(8,128)} %get-tuple-element.59.refs_0_, bf16[256,512]{1,0:T(8,128)(2,1)} %collective-permute-done.17.refs_1_, f32[256,512]{1,0:T(8,128)} %get-tuple-element.60.refs_2_, ...), custom_call_target="tpu_custom_call", output_to_operand_aliasing={{}: (5, {})} | custom-call | flops 1 | bytes 1 | tf_op jit(solution)/shard_map/final_sum/pallas_call | solution.py:256
  89.3 1.7 %collective-permute-done.16.refs_0_ = bf16[256,512]{1,0:T(8,128)(2,1)S(1)} collective-permute-done((bf16[256,512]{1,0:T(8,128)(2,1)}, bf16[256,512]{1,0:T(8,128)(2,1)S(1)}, u32[]{:S(2)}, u32[]{:S(2)}) %collective-permute-start.16) | collective-permute-done | bytes 262176 | tf_op jit(solution)/shard_map/ppermute | solution.py:379
  90.9 2.4 %final_sum.5 = bf16[2048,2,256]{2,1,0:T(2,128)(2,1)} custom-call(s32[2]{0:T(128)S(1)} %pad_add_fusion.2.order_ref, bf16[256,512]{1,0:T(8,128)(2,1)S(1)} %collective-permute-done.16.refs_0_, f32[2048,512]{1,0:T(8,128)} %short_range.1.refs_2_.refs_3_.refs_1_, bf16[2048,2,256]{2,1,0:T(2,128)(2,1)} %final_sum.4.refs_2_), custom_call_target="tpu_custom_call", output_to_operand_aliasing={{}: (3, {})} | custom-call | flops 1 | bytes 1 | tf_op jit(solution)/shard_map/final_sum/pallas_call | solution.py:256
  (64 shorter events, 9.7 us)
Async XLA Ops:
  0.0 9.0 %copy-start.5 = (bf16[256,2,512]{2,1,0:T(2,128)(2,1)S(1)}, bf16[256,2,512]{2,1,0:T(2,128)(2,1)}, u32[]{:S(2)}) copy-start(bf16[256,2,512]{2,1,0:T(2,128)(2,1)} %param.11) | copy-start | bytes 1572868
  0.0 9.0 %copy-start.6 = (f32[512]{0:T(512)S(1)}, f32[512]{0:T(512)}, u32[]{:S(2)}) copy-start(f32[512]{0:T(512)} %param.13) | copy-start | bytes 6148
  1.2 33.3 %copy-start.4 = (bf16[32,8,2,512]{3,1,2,0:T(8,128)(2,1)}, bf16[32,8,2,512]{3,1,2,0:T(8,128)(2,1)S(1)}, u32[]{:S(2)}) copy-start(bf16[32,8,2,512]{3,1,2,0:T(8,128)(2,1)S(1)} %copy.18) | copy-start | bytes 1572868
  1.2 16.5 %collective-permute-start = (bf16[256,1024]{1,0:T(8,128)(2,1)S(1)}, bf16[256,1024]{1,0:T(8,128)(2,1)}, u32[]{:S(2)}, u32[]{:S(2)}) collective-permute-start(bf16[256,1024]{1,0:T(8,128)(2,1)S(1)} %bitcast.45), channel_id=1, source_target_pairs={{0,8},{1,9},{2,10},{3,11},{4,0},{5,1},{6,2},{7,3},{8,12},{9,13},{1... | collective-permute-start | bytes 1572872 | tf_op jit(solution)/shard_map/ppermute | solution.py:379
  7.4 29.5 %copy-start.9 = (f32[125]{0:T(128)S(1)}, f32[125]{0:T(128)}, u32[]{:S(2)}) copy-start(f32[125]{0:T(128)} %param.16) | copy-start | bytes 1504
  7.4 29.5 %copy-start.10 = (f32[125]{0:T(128)S(1)}, f32[125]{0:T(128)}, u32[]{:S(2)}) copy-start(f32[125]{0:T(128)} %param.17) | copy-start | bytes 1504
  7.4 25.4 %collective-permute-start.1 = (bf16[17,128,128]{2,1,0:T(8,128)(2,1)S(1)}, bf16[17,128,128]{2,1,0:T(8,128)(2,1)}, u32[]{:S(2)}, u32[]{:S(2)}) collective-permute-start(bf16[17,128,128]{2,1,0:T(8,128)(2,1)S(1)} %pad_maximum_fusion.refs_0_), channel_id=1, source_target_pairs={{0,16},{1,17},{2,18},{3,19},{4,20},{5,21},{6,22},{7,23},{8,24},{9,... | collective-permute-start | bytes 1671176 | tf_op jit(solution)/shard_map/ppermute | solution.py:379
  9.9 22.9 %collective-permute-start.2 = (bf16[1024,256]{1,0:T(8,128)(2,1)S(1)}, bf16[1024,256]{1,0:T(8,128)(2,1)S(1)}, u32[]{:S(2)}, u32[]{:S(2)}) collective-permute-start(bf16[1024,256]{1,0:T(8,128)(2,1)S(1)} %bitcast.39), channel_id=1, source_target_pairs={{0,16},{1,17},{2,18},{3,19},{4,20},{5,21},{6,22},{7,23},{8,24},{9,... | collective-permute-start | bytes 1572872 | tf_op jit(solution)/shard_map/ppermute | solution.py:379
  10.5 22.3 %collective-permute-start.3 = (bf16[1024,256]{1,0:T(8,128)(2,1)S(1)}, bf16[1024,256]{1,0:T(8,128)(2,1)S(1)}, u32[]{:S(2)}, u32[]{:S(2)}) collective-permute-start(bf16[1024,256]{1,0:T(8,128)(2,1)S(1)} %bitcast.40), channel_id=1, source_target_pairs={{0,2},{1,3},{2,0},{3,1},{4,6},{5,7},{6,4},{7,5},{8,10},{9,11},{10,... | collective-permute-start | bytes 1572872 | tf_op jit(solution)/shard_map/ppermute | solution.py:379
  12.1 20.7 %collective-permute-start.4 = (bf16[256,1024]{1,0:T(8,128)(2,1)S(1)}, bf16[256,1024]{1,0:T(8,128)(2,1)S(1)}, u32[]{:S(2)}, u32[]{:S(2)}) collective-permute-start(bf16[256,1024]{1,0:T(8,128)(2,1)S(1)} %bitcast.46), channel_id=1, source_target_pairs={{0,4},{1,5},{2,6},{3,7},{4,12},{5,13},{6,14},{7,15},{8,0},{9,1},{1... | collective-permute-start | bytes 1572872 | tf_op jit(solution)/shard_map/ppermute | solution.py:379
  12.1 27.8 %copy-start.1 = (f32[4096]{0:T(1024)S(1)}, f32[4096]{0:T(1024)}, u32[]{:S(2)}) copy-start(f32[4096]{0:T(1024)} %param.15) | copy-start | bytes 49156
  32.8 17.0 %collective-permute-start.5 = (bf16[256,1024]{1,0:T(8,128)(2,1)}, bf16[256,1024]{1,0:T(8,128)(2,1)}, u32[]{:S(2)}, u32[]{:S(2)}) collective-permute-start(bf16[256,1024]{1,0:T(8,128)(2,1)} %collective-permute-done), channel_id=1, source_target_pairs={{0,8},{1,9},{2,10},{3,11},{4,0},{5,1},{6,2},{7,3},{8,12},{9,13},{1... | collective-permute-start | bytes 1572872 | tf_op jit(solution)/shard_map/ppermute | solution.py:379
  34.5 15.0 %collective-permute-start.6 = (bf16[256,1024]{1,0:T(8,128)(2,1)S(1)}, bf16[256,1024]{1,0:T(8,128)(2,1)}, u32[]{:S(2)}, u32[]{:S(2)}) collective-permute-start(bf16[256,1024]{1,0:T(8,128)(2,1)S(1)} %select_select_fusion.2), channel_id=1, source_target_pairs={{0,16},{1,17},{2,18},{3,19},{4,20},{5,21},{6,22},{7,23},{8,24},{9,... | collective-permute-start | bytes 1572872 | tf_op jit(solution)/shard_map/ppermute | solution.py:379
  38.2 12.9 %collective-permute-start.7 = (bf16[256,1024]{1,0:T(8,128)(2,1)S(1)}, bf16[256,1024]{1,0:T(8,128)(2,1)}, u32[]{:S(2)}, u32[]{:S(2)}) collective-permute-start(bf16[256,1024]{1,0:T(8,128)(2,1)S(1)} %select_select_fusion.1.refs_0_), channel_id=1, source_target_pairs={{0,1},{1,0},{2,3},{3,2},{4,5},{5,4},{6,7},{7,6},{8,9},{9,8},{10,11... | collective-permute-start | bytes 1572872 | tf_op jit(solution)/shard_map/ppermute | solution.py:379
  38.3 14.3 %collective-permute-start.9 = (bf16[1024,256]{1,0:T(8,128)(2,1)S(1)}, bf16[1024,256]{1,0:T(8,128)(2,1)S(1)}, u32[]{:S(2)}, u32[]{:S(2)}) collective-permute-start(bf16[1024,256]{1,0:T(8,128)(2,1)S(1)} %collective-permute-done.2.refs_5_), channel_id=1, source_target_pairs={{0,2},{1,3},{2,0},{3,1},{4,6},{5,7},{6,4},{7,5},{8,10},{9,11},{10,... | collective-permute-start | bytes 1572872 | tf_op jit(solution)/shard_map/ppermute | solution.py:379
  49.6 3.1 %collective-permute-start.8 = (bf16[256,1024]{1,0:T(8,128)(2,1)}, bf16[256,1024]{1,0:T(8,128)(2,1)S(1)}, u32[]{:S(2)}, u32[]{:S(2)}) collective-permute-start(bf16[256,1024]{1,0:T(8,128)(2,1)} %collective-permute-done.6.refs_1_), channel_id=1, source_target_pairs={{0,1},{1,0},{2,3},{3,2},{4,5},{5,4},{6,7},{7,6},{8,9},{9,8},{10,11... | collective-permute-start | bytes 1572872 | tf_op jit(solution)/shard_map/ppermute | solution.py:379
  51.0 9.1 %collective-permute-start.11 = (bf16[128,1024]{1,0:T(8,128)(2,1)S(1)}, bf16[128,1024]{1,0:T(8,128)(2,1)S(1)}, u32[]{:S(2)}, u32[]{:S(2)}) collective-permute-start(bf16[128,1024]{1,0:T(8,128)(2,1)S(1)} %select_select_fusion.3), channel_id=1, source_target_pairs={{0,16},{1,17},{2,18},{3,19},{4,20},{5,21},{6,22},{7,23},{8,24},{9,... | collective-permute-start | bytes 786440 | tf_op jit(solution)/shard_map/ppermute | solution.py:379
  60.0 2.4 %collective-permute-start.12 = (bf16[256,1024]{1,0:T(8,128)(2,1)S(1)}, bf16[256,1024]{1,0:T(8,128)(2,1)S(1)}, u32[]{:S(2)}, u32[]{:S(2)}) collective-permute-start(bf16[256,1024]{1,0:T(8,128)(2,1)S(1)} %select_select_fusion.refs_0_), channel_id=1, source_target_pairs={{0,1},{1,0},{2,3},{3,2},{4,5},{5,4},{6,7},{7,6},{8,9},{9,8},{10,11... | collective-permute-start | bytes 1572872 | tf_op jit(solution)/shard_map/ppermute | solution.py:379
  60.1 2.3 %collective-permute-start.13 = (bf16[128,1024]{1,0:T(8,128)(2,1)S(1)}, bf16[128,1024]{1,0:T(8,128)(2,1)S(1)}, u32[]{:S(2)}, u32[]{:S(2)}) collective-permute-start(bf16[128,1024]{1,0:T(8,128)(2,1)S(1)} %collective-permute-done.11.refs_1_), channel_id=1, source_target_pairs={{0,1},{1,0},{2,3},{3,2},{4,5},{5,4},{6,7},{7,6},{8,9},{9,8},{10,11... | collective-permute-start | bytes 786440 | tf_op jit(solution)/shard_map/ppermute | solution.py:379
  60.6 8.3 %collective-permute-start.10 = (bf16[128,1024]{1,0:T(8,128)(2,1)S(1)}, bf16[128,1024]{1,0:T(8,128)(2,1)S(1)}, u32[]{:S(2)}, u32[]{:S(2)}) collective-permute-start(bf16[128,1024]{1,0:T(8,128)(2,1)S(1)} %select_select_fusion.4), channel_id=1, source_target_pairs={{0,16},{1,17},{2,18},{3,19},{4,20},{5,21},{6,22},{7,23},{8,24},{9,... | collective-permute-start | bytes 786440 | tf_op jit(solution)/shard_map/ppermute | solution.py:379
  61.1 15.1 %collective-permute-start.14 = (bf16[512,512]{1,0:T(8,128)(2,1)}, bf16[512,512]{1,0:T(8,128)(2,1)}, u32[]{:S(2)}, u32[]{:S(2)}) collective-permute-start(bf16[512,512]{1,0:T(8,128)(2,1)} %get-tuple-element.43), channel_id=1, source_target_pairs={{0,2},{1,3},{2,0},{3,1},{4,6},{5,7},{6,4},{7,5},{8,10},{9,11},{10,... | collective-permute-start | bytes 1572872 | tf_op jit(solution)/shard_map/ppermute | solution.py:379
  68.9 11.7 %collective-permute-start.15 = (bf16[128,1024]{1,0:T(8,128)(2,1)S(1)}, bf16[128,1024]{1,0:T(8,128)(2,1)}, u32[]{:S(2)}, u32[]{:S(2)}) collective-permute-start(bf16[128,1024]{1,0:T(8,128)(2,1)S(1)} %collective-permute-done.10.refs_1_), channel_id=1, source_target_pairs={{0,1},{1,0},{2,3},{3,2},{4,5},{5,4},{6,7},{7,6},{8,9},{9,8},{10,11... | collective-permute-start | bytes 786440 | tf_op jit(solution)/shard_map/ppermute | solution.py:379
  69.0 16.5 %collective-permute-start.17 = (bf16[256,512]{1,0:T(8,128)(2,1)}, bf16[256,512]{1,0:T(8,128)(2,1)}, u32[]{:S(2)}, u32[]{:S(2)}) collective-permute-start(bf16[256,512]{1,0:T(8,128)(2,1)} %copy-done), channel_id=1, source_target_pairs={{0,2},{1,3},{2,0},{3,1},{4,6},{5,7},{6,4},{7,5},{8,10},{9,11},{10,... | collective-permute-start | bytes 786440 | tf_op jit(solution)/shard_map/ppermute | solution.py:379
  84.3 6.6 %collective-permute-start.16 = (bf16[256,512]{1,0:T(8,128)(2,1)}, bf16[256,512]{1,0:T(8,128)(2,1)S(1)}, u32[]{:S(2)}, u32[]{:S(2)}) collective-permute-start(bf16[256,512]{1,0:T(8,128)(2,1)} %get-tuple-element.58), channel_id=1, source_target_pairs={{0,2},{1,3},{2,0},{3,1},{4,6},{5,7},{6,4},{7,5},{8,10},{9,11},{10,... | collective-permute-start | bytes 786440 | tf_op jit(solution)/shard_map/ppermute | solution.py:379
  (5 other events, 27.5 us)

commit v8 on v7

--- a/solution.py
+++ b/solution.py
@@ -152,8 +152,8 @@
 def long_kernel(*refs, blocks, chains, pieces, window):
     parts = refs[: blocks * chains]
     factors = refs[blocks * chains : (blocks + pieces) * chains]
-    outs = refs[(blocks + pieces) * chains : -3]
-    right, own, own_sem = refs[-3:]
+    outs, scratch = refs[(blocks + pieces) * chains :][:pieces], refs[-pieces - 2 :]
+    right, made, out_sem = scratch[0], scratch[1:-1], scratch[-1]
     depth, width = factors[0].shape
     half = depth // 2
     count = window[-1]
@@ -174,12 +174,11 @@
                 axis=1,
             )
             total = jnp.dot(left, right[...], preferred_element_type=jnp.float32)
-            if piece:
-                outs[piece][block * count : (block + 1) * count, :] = total.astype(outs[piece].dtype)
-                continue
-            own[block] = total
-            target = outs[0].at[pl.ds(block * count, count), :]
-            copies.append(pltpu.make_async_copy(own.at[block], target, own_sem.at[block]))
+            made[piece][block] = total.astype(outs[piece].dtype)
+            target = outs[piece].at[pl.ds(block * count, count), :]
+            copies.append(
+                pltpu.make_async_copy(made[piece].at[block], target, out_sem.at[piece, block])
+            )
             copies[-1].start()
     for copy in copies:
         copy.wait()
@@ -191,21 +190,18 @@
     pieces = len(factors)
     count = window[-1]
     shape = (len(blocks) * count, 2 * width)
+    dtypes = [jnp.bfloat16 if piece else jnp.float32 for piece in range(pieces)]
     flat = [v for group in [*blocks, *factors] for v in group]
     return pl.pallas_call(
         functools.partial(
             long_kernel, blocks=len(blocks), chains=chains, pieces=pieces, window=window
         ),
-        out_shape=[pltpu.HBM(shape, jnp.float32)]
-        + [jax.ShapeDtypeStruct(shape, jnp.bfloat16)] * (pieces - 1),
+        out_shape=[pltpu.HBM(shape, dtype) for dtype in dtypes],
         in_specs=[pl.BlockSpec(memory_space=pltpu.VMEM)] * len(flat),
-        out_specs=[pl.BlockSpec(memory_space=pltpu.HBM)]
-        + [pl.BlockSpec(memory_space=pltpu.VMEM)] * (pieces - 1),
-        scratch_shapes=[
-            pltpu.VMEM((chains * depth, 2 * width), jnp.bfloat16),
-            pltpu.VMEM((len(blocks), count, 2 * width), jnp.float32),
-            pltpu.SemaphoreType.DMA((len(blocks),)),
-        ],
+        out_specs=[pl.BlockSpec(memory_space=pltpu.HBM)] * pieces,
+        scratch_shapes=[pltpu.VMEM((chains * depth, 2 * width), jnp.bfloat16)]
+        + [pltpu.VMEM((len(blocks), count, 2 * width), dtype) for dtype in dtypes]
+        + [pltpu.SemaphoreType.DMA((pieces, len(blocks)))],
         compiler_params=pltpu.CompilerParams(vmem_limit_bytes=VMEM_BYTES),
         cost_estimate=SMALL_COST,
         name="long_range",
@@ -424,11 +420,11 @@
         return [value] + [over_core(value, t) for t in range(1, CORES)]
 
     held = {0: aux_flat, 1: along(aux_flat, 1), length - 1: along(aux_flat, -1)}
-    turned_x = to_plane(turned)
-    factors = [[turned, turned_x]] + [[over_y(turned, s)] for s in range(1, breadth)]
     packed = jnp.concatenate([item_rows, slot_block(slots, item_rows)], axis=0)
     items_x = to_plane(packed)
-    begun = [items_x, turned_x, *(pair[0] for pair in factors[1:]), held[1], held[length - 1]]
+    turned_x = to_plane(after(turned, items_x))
+    factors = [[turned, turned_x]] + [[over_y(turned, s)] for s in range(1, breadth)]
+    begun = [turned_x, *(pair[0] for pair in factors[1:]), held[1], held[length - 1]]
     for s in range(1, breadth):
         factors[s].append(over_y(after(turned_x, *begun), s))
     for k in range(2, length // 2 + 1):
@@ -461,14 +457,14 @@
         arriving.append([over_y(v, s) for s, v in enumerate(made[1:], 1)])
 
     for i, (n, first, count) in enumerate(units):
-        gate = begun if i == 0 else [crossed[0][0], short] if i == 1 else away[i - 2]
+        gate = [*begun, short] if i == 0 else [moved, *(away[i - 2] if i > 1 else [])]
         theirs.append(pick(True, n, slice(first, first + count), *gate))
         moved = to_plane(theirs[i])
-        if first + count == rows:
+        if n not in mine:
             mine[n] = with_cores(pick(False, n, slice(None), theirs[i]))
         if i:
             multiply(i - 1)
-        crossed.append(with_cores(after(moved, *away[i - 1] if i else [short])))
+        crossed.append(with_cores(after(moved, *away[i - 1] if i else [])))
     last = len(units) - 1
 
     def place_of(piece, i, s):
@@ -488,7 +484,7 @@
         return final_sum(numbers, [piece for piece, _ in entries], short, out, count)
 
     out = add_up(None, *calls.pop(0)) if calls else None
-    multiply(last, *([] if out is None else [out]))
+    multiply(last)
     count = units[last][2]
     calls.append((count, [place_of(own[last], last, 0)]))
     if len(calls) > 1 and calls[-2][0] == count:

time: 93.8 us -> 89.5 us (0.954)
  Pallas kernels: 31 us -> 25.9 us
  other arithmetic: 6.13 us -> 7.88 us
  starting transfers between devices: 17.6 us -> 19.2 us
  waiting for transfers between devices: 33.7 us -> 32.2 us
  local copies, waits for them, and re-layouts: 3.91 us -> 2.9 us
    pallas_call x3, Pallas kernels: 10.8 us -> 7.2 us  [long_range(): pl.pallas_call(functools.partial(long_kernel, blocks=len(blocks), chains=...]
    select_n x5, other arithmetic: 4.54 us -> 6.28 us  [pick(): value = jnp.where(wanted == k, block[window], value)]
    ppermute x18, starting transfers between devices: 17.6 us -> 19.2 us  [send(): return lax.ppermute(value, AXES, pairs)]
    ppermute x18, waiting for transfers between devices: 33.7 us -> 32.2 us  [send(): return lax.ppermute(value, AXES, pairs)]
    unnamed x24 -> x18, local copies, waits for them, and re-layouts: 3.24 us -> 2.23 us
  transfers between devices with their start and end apart: 18 -> 18, of which waited for: 7 -> 10; matrix products, arithmetic and copies ran while one was open for 9% -> 10% of each run, Pallas kernels for 31% -> 26%
where the time goes in v8:
time: 89.5 us; the launch traced here: 89.1 us
  waiting for transfers between devices  32.2 us (36%)
  Pallas kernels  25.9 us (29%)
  starting transfers between devices  19.2 us (21%)
  other arithmetic  7.88 us (9%)
  local copies, waits for them, and re-layouts  2.9 us (3%)
  between operations  0.96 us (1%)
    ppermute x18, waiting for transfers between devices, send(): return lax.ppermute(value, AXES, pairs)  32.2 us
    ppermute x18, starting transfers between devices, send(): return lax.ppermute(value, AXES, pairs)  19.2 us
    pallas_call x3, Pallas kernels, final_sum(): pl.pallas_call(functools.partial(final_kernel, pieces=count, blocks=block...  9.57 us
    pallas_call x1, Pallas kernels, short_range(): pl.pallas_call(kernel, out_shape=pltpu.HBM((row_count, 2 * subs * width),...  9.14 us
    pallas_call x3, Pallas kernels, long_range(): pl.pallas_call(functools.partial(long_kernel, blocks=len(blocks), chains=...  7.2 us
    select_n x5, other arithmetic, pick(): value = jnp.where(wanted == k, block[window], value)  6.28 us
    unnamed x18, local copies, waits for them, and re-layouts  2.23 us
  transfers between devices with their start and end apart: 18, of which 10 were waited for; matrix products, arithmetic and copies ran while one was open for 10% of the time, Pallas kernels for 26%

profile of v8, /device:TPU:0, one launch (start us, length us, event | category | flops | bytes accessed | tf_op | source)
XLA Modules:
  0.0 89.1 jit_solution(12774269720951957185)
XLA Ops:
  2.9 3.0 %collective-permute-start.1 = (bf16[17,128,128]{2,1,0:T(8,128)(2,1)S(1)}, bf16[17,128,128]{2,1,0:T(8,128)(2,1)S(1)}, u32[]{:S(2)}, u32[]{:S(2)}) collective-permute-start(bf16[17,128,128]{2,1,0:T(8,128)(2,1)S(1)} %pad_maximum_fusion.refs_0_), channel_id=1, source_target_pairs={{0,16},{1,17},{2,18},{3,19},{4,20},{5,21},{6,22},{7,23},{8,24},{9,... | collective-permute-start | bytes 1671176 | tf_op jit(solution)/shard_map/ppermute | solution.py:375
  6.8 2.6 %collective-permute-start = (bf16[256,1024]{1,0:T(8,128)(2,1)}, bf16[256,1024]{1,0:T(8,128)(2,1)S(1)}, u32[]{:S(2)}, u32[]{:S(2)}) collective-permute-start(bf16[256,1024]{1,0:T(8,128)(2,1)} %bitcast.30), channel_id=1, source_target_pairs={{0,8},{1,9},{2,10},{3,11},{4,0},{5,1},{6,2},{7,3},{8,12},{9,13},{1... | collective-permute-start | bytes 1572872 | tf_op jit(solution)/shard_map/ppermute | solution.py:375
  10.4 1.6 %collective-permute-start.3 = (bf16[1024,256]{1,0:T(8,128)(2,1)S(1)}, bf16[1024,256]{1,0:T(8,128)(2,1)S(1)}, u32[]{:S(2)}, u32[]{:S(2)}) collective-permute-start(bf16[1024,256]{1,0:T(8,128)(2,1)S(1)} %bitcast.39), channel_id=1, source_target_pairs={{0,2},{1,3},{2,0},{3,1},{4,6},{5,7},{6,4},{7,5},{8,10},{9,11},{10,... | collective-permute-start | bytes 1572872 | tf_op jit(solution)/shard_map/ppermute | solution.py:375
  11.9 6.6 %collective-permute-done.1.refs_1_ = bf16[17,128,128]{2,1,0:T(8,128)(2,1)S(1)} collective-permute-done((bf16[17,128,128]{2,1,0:T(8,128)(2,1)S(1)}, bf16[17,128,128]{2,1,0:T(8,128)(2,1)S(1)}, u32[]{:S(2)}, u32[]{:S(2)}) %collective-permute-start.1) | collective-permute-done | bytes 557088 | tf_op jit(solution)/shard_map/ppermute | solution.py:375
  18.5 1.7 %collective-permute-start.2 = (bf16[1024,256]{1,0:T(8,128)(2,1)S(1)}, bf16[1024,256]{1,0:T(8,128)(2,1)S(1)}, u32[]{:S(2)}, u32[]{:S(2)}) collective-permute-start(bf16[1024,256]{1,0:T(8,128)(2,1)S(1)} %bitcast.40), channel_id=1, source_target_pairs={{0,16},{1,17},{2,18},{3,19},{4,20},{5,21},{6,22},{7,23},{8,24},{9,... | collective-permute-start | bytes 1572872 | tf_op jit(solution)/shard_map/ppermute | solution.py:375
  20.6 9.1 %short_range.1.refs_2_.refs_3_.refs_1_ = f32[2048,512]{1,0:T(8,128)} custom-call(s32[1]{0:T(128)} %bitcast.10.half_ref, s32[32]{0:T(128)S(1)} %get-tuple-element.63.live_ref, s32[32]{0:T(128)S(1)} %get-tuple-element.62.sub_ref, f32[3,32]{1,0:T(4,128)S(1)} %pad_maximum_fusion.1.meta_ref, bf16[128,4096]{1,0:T(8,128)(2,1)} %basis_ref.1, ...), custom_call_target="tpu_custom_call" | custom-call | flops 4294967296 | bytes 1 | tf_op jit(solution)/shard_map/short_range/pallas_call | solution.py:125
  29.8 3.8 %collective-permute-done.4 = bf16[256,1024]{1,0:T(8,128)(2,1)} collective-permute-done((bf16[256,1024]{1,0:T(8,128)(2,1)}, bf16[256,1024]{1,0:T(8,128)(2,1)}, u32[]{:S(2)}, u32[]{:S(2)}) %collective-permute-start.4) | collective-permute-done | bytes 524320 | tf_op jit(solution)/shard_map/ppermute | solution.py:375
  34.2 1.9 %select_select_fusion.2 = bf16[256,1024]{1,0:T(8,128)(2,1)} fusion(bf16[256,1024]{1,0:T(8,128)(2,1)} %bitcast.30, bf16[256,1024]{1,0:T(8,128)(2,1)S(1)} %collective-permute-done, bf16[256,1024]{1,0:T(8,128)(2,1)} %collective-permute-done.4, pred[]{:T(512)S(6)} %eq.78, pred[]{:T(512)S(6)} %eq.73), kind=kLoop, calls=%fused_computation.4 | loop fusion | flops 524288 | bytes 2097154 | tf_op jit(solution)/shard_map/jit(_where)/select_n | solution.py:409
  36.2 1.6 %collective-permute-start.6 = (bf16[256,1024]{1,0:T(8,128)(2,1)}, bf16[256,1024]{1,0:T(8,128)(2,1)S(1)}, u32[]{:S(2)}, u32[]{:S(2)}) collective-permute-start(bf16[256,1024]{1,0:T(8,128)(2,1)} %select_select_fusion.2), channel_id=1, source_target_pairs={{0,16},{1,17},{2,18},{3,19},{4,20},{5,21},{6,22},{7,23},{8,24},{9,... | collective-permute-start | bytes 1572872 | tf_op jit(solution)/shard_map/ppermute | solution.py:375
  39.1 1.6 %collective-permute-start.10 = (bf16[1024,256]{1,0:T(8,128)(2,1)S(1)}, bf16[1024,256]{1,0:T(8,128)(2,1)S(1)}, u32[]{:S(2)}, u32[]{:S(2)}) collective-permute-start(bf16[1024,256]{1,0:T(8,128)(2,1)S(1)} %collective-permute-done.2.refs_5_), channel_id=1, source_target_pairs={{0,2},{1,3},{2,0},{3,1},{4,6},{5,7},{6,4},{7,5},{8,10},{9,11},{10,... | collective-permute-start | bytes 1572872 | tf_op jit(solution)/shard_map/ppermute | solution.py:375
  40.7 6.8 %collective-permute-done.5 = bf16[256,1024]{1,0:T(8,128)(2,1)S(1)} collective-permute-done((bf16[256,1024]{1,0:T(8,128)(2,1)S(1)}, bf16[256,1024]{1,0:T(8,128)(2,1)S(1)}, u32[]{:S(2)}, u32[]{:S(2)}) %collective-permute-start.5) | collective-permute-done | bytes 524320 | tf_op jit(solution)/shard_map/ppermute | solution.py:375
  47.5 2.1 %collective-permute-done.6.refs_1_ = bf16[256,1024]{1,0:T(8,128)(2,1)S(1)} collective-permute-done((bf16[256,1024]{1,0:T(8,128)(2,1)}, bf16[256,1024]{1,0:T(8,128)(2,1)S(1)}, u32[]{:S(2)}, u32[]{:S(2)}) %collective-permute-start.6) | collective-permute-done | bytes 524320 | tf_op jit(solution)/shard_map/ppermute | solution.py:375
  53.4 3.2 %long_range.3 = (f32[512,512]{1,0:T(8,128)}, bf16[512,512]{1,0:T(8,128)(2,1)}) custom-call(bf16[256,1024]{1,0:T(8,128)(2,1)S(1)} %select_select_fusion.refs_0_, bf16[256,1024]{1,0:T(8,128)(2,1)S(1)} %collective-permute-done.6.refs_1_, bf16[256,1024]{1,0:T(8,128)(2,1)S(1)} %collective-permute-done.8.refs_2_, ...), custom_call_target="tpu_custom_call" | custom-call | flops 1 | bytes 1 | tf_op jit(solution)/shard_map/long_range/pallas_call | solution.py:195
  56.6 2.8 %collective-permute-done.7.refs_1_ = bf16[128,1024]{1,0:T(8,128)(2,1)S(1)} collective-permute-done((bf16[128,1024]{1,0:T(8,128)(2,1)S(1)}, bf16[128,1024]{1,0:T(8,128)(2,1)S(1)}, u32[]{:S(2)}, u32[]{:S(2)}) %collective-permute-start.7) | collective-permute-done | bytes 262176 | tf_op jit(solution)/shard_map/ppermute | solution.py:375
  62.7 2.0 %long_range.4 = (f32[256,512]{1,0:T(8,128)}, bf16[256,512]{1,0:T(8,128)(2,1)}) custom-call(bf16[256,1024]{1,0:T(8,128)(2,1)S(1)} %select_select_fusion.1.refs_0_, bf16[128,1024]{1,0:T(8,128)(2,1)S(1)} %collective-permute-done.7.refs_1_, bf16[256,1024]{1,0:T(8,128)(2,1)S(1)} %collective-permute-done.12.refs_2_, ...), custom_call_target="tpu_custom_call" | custom-call | flops 1 | bytes 1 | tf_op jit(solution)/shard_map/long_range/pallas_call | solution.py:195
  64.7 4.5 %collective-permute-done.11.refs_1_ = bf16[128,1024]{1,0:T(8,128)(2,1)S(1)} collective-permute-done((bf16[128,1024]{1,0:T(8,128)(2,1)S(1)}, bf16[128,1024]{1,0:T(8,128)(2,1)S(1)}, u32[]{:S(2)}, u32[]{:S(2)}) %collective-permute-start.11) | collective-permute-done | bytes 262176 | tf_op jit(solution)/shard_map/ppermute | solution.py:375
  70.7 2.0 %long_range.5 = (f32[256,512]{1,0:T(8,128)}, bf16[256,512]{1,0:T(8,128)(2,1)}) custom-call(bf16[256,1024]{1,0:T(8,128)(2,1)S(1)} %select_select_fusion.1.refs_0_, bf16[128,1024]{1,0:T(8,128)(2,1)S(1)} %collective-permute-done.11.refs_1_, bf16[256,1024]{1,0:T(8,128)(2,1)S(1)} %collective-permute-done.12.refs_2_, ...), custom_call_target="tpu_custom_call" | custom-call | flops 1 | bytes 1 | tf_op jit(solution)/shard_map/long_range/pallas_call | solution.py:195
  72.7 1.6 %collective-permute-start.15 = (bf16[256,512]{1,0:T(8,128)(2,1)}, bf16[256,512]{1,0:T(8,128)(2,1)S(1)}, u32[]{:S(2)}, u32[]{:S(2)}) collective-permute-start(bf16[256,512]{1,0:T(8,128)(2,1)} %get-tuple-element.55), channel_id=1, source_target_pairs={{0,2},{1,3},{2,0},{3,1},{4,6},{5,7},{6,4},{7,5},{8,10},{9,11},{10,... | collective-permute-start | bytes 786440 | tf_op jit(solution)/shard_map/ppermute | solution.py:375
  74.5 1.6 %collective-permute-done.17.refs_1_ = bf16[512,512]{1,0:T(8,128)(2,1)S(1)} collective-permute-done((bf16[512,512]{1,0:T(8,128)(2,1)}, bf16[512,512]{1,0:T(8,128)(2,1)S(1)}, u32[]{:S(2)}, u32[]{:S(2)}) %collective-permute-start.17) | collective-permute-done | bytes 524320 | tf_op jit(solution)/shard_map/ppermute | solution.py:375
  76.1 3.8 %final_sum.3.refs_4_ = bf16[2048,2,256]{2,1,0:T(2,128)(2,1)} custom-call(s32[4]{0:T(128)S(1)} %pad_add_fusion.3.order_ref, f32[512,512]{1,0:T(8,128)} %get-tuple-element.58.refs_0_, bf16[512,512]{1,0:T(8,128)(2,1)S(1)} %collective-permute-done.17.refs_1_, f32[2048,512]{1,0:T(8,128)} %short_range.1.refs_2_.refs_3_.refs_1_), custom_call_target="tpu_custom_call" | custom-call | flops 1 | bytes 1 | tf_op jit(solution)/shard_map/final_sum/pallas_call | solution.py:252
  80.0 1.8 %collective-permute-done.16.refs_1_ = bf16[256,512]{1,0:T(8,128)(2,1)S(1)} collective-permute-done((bf16[256,512]{1,0:T(8,128)(2,1)}, bf16[256,512]{1,0:T(8,128)(2,1)S(1)}, u32[]{:S(2)}, u32[]{:S(2)}) %collective-permute-start.16) | collective-permute-done | bytes 262176 | tf_op jit(solution)/shard_map/ppermute | solution.py:375
  81.7 3.3 %final_sum.4.refs_2_ = bf16[2048,2,256]{2,1,0:T(2,128)(2,1)} custom-call(s32[6]{0:T(128)S(1)} %stack.77.order_ref, f32[256,512]{1,0:T(8,128)} %get-tuple-element.56.refs_0_, bf16[256,512]{1,0:T(8,128)(2,1)S(1)} %collective-permute-done.16.refs_1_, f32[256,512]{1,0:T(8,128)} %get-tuple-element.57.refs_2_, ...), custom_call_target="tpu_custom_call", output_to_operand_aliasing={{}: (5, {})} | custom-call | flops 1 | bytes 1 | tf_op jit(solution)/shard_map/final_sum/pallas_call | solution.py:252
  85.1 1.6 %collective-permute-done.15.refs_0_ = bf16[256,512]{1,0:T(8,128)(2,1)S(1)} collective-permute-done((bf16[256,512]{1,0:T(8,128)(2,1)}, bf16[256,512]{1,0:T(8,128)(2,1)S(1)}, u32[]{:S(2)}, u32[]{:S(2)}) %collective-permute-start.15) | collective-permute-done | bytes 262176 | tf_op jit(solution)/shard_map/ppermute | solution.py:375
  86.7 2.4 %final_sum.5 = bf16[2048,2,256]{2,1,0:T(2,128)(2,1)} custom-call(s32[2]{0:T(128)S(1)} %pad_add_fusion.2.order_ref, bf16[256,512]{1,0:T(8,128)(2,1)S(1)} %collective-permute-done.15.refs_0_, f32[2048,512]{1,0:T(8,128)} %short_range.1.refs_2_.refs_3_.refs_1_, bf16[2048,2,256]{2,1,0:T(2,128)(2,1)} %final_sum.4.refs_2_), custom_call_target="tpu_custom_call", output_to_operand_aliasing={{}: (3, {})} | custom-call | flops 1 | bytes 1 | tf_op jit(solution)/shard_map/final_sum/pallas_call | solution.py:252
  (58 shorter events, 15.1 us)
Async XLA Ops:
  0.0 9.4 %copy-start.3 = (f32[512]{0:T(512)S(1)}, f32[512]{0:T(512)}, u32[]{:S(2)}) copy-start(f32[512]{0:T(512)} %param.13) | copy-start | bytes 6148
  2.8 17.5 %copy-start.4 = (s32[16]{0:T(128)S(1)}, s32[16]{0:T(128)}, u32[]{:S(2)}) copy-start(s32[16]{0:T(128)} %param.20) | copy-start | bytes 196
  2.8 17.5 %copy-start.5 = (s32[16]{0:T(128)S(1)}, s32[16]{0:T(128)}, u32[]{:S(2)}) copy-start(s32[16]{0:T(128)} %param.19) | copy-start | bytes 196
  2.8 17.6 %copy-start.6 = (f32[125]{0:T(128)S(1)}, f32[125]{0:T(128)}, u32[]{:S(2)}) copy-start(f32[125]{0:T(128)} %param.16) | copy-start | bytes 1504
  2.8 17.6 %copy-start.7 = (f32[125]{0:T(128)S(1)}, f32[125]{0:T(128)}, u32[]{:S(2)}) copy-start(f32[125]{0:T(128)} %param.17) | copy-start | bytes 1504
  2.8 17.8 %copy-start = (f32[4096]{0:T(1024)S(1)}, f32[4096]{0:T(1024)}, u32[]{:S(2)}) copy-start(f32[4096]{0:T(1024)} %param.15) | copy-start | bytes 49156
  2.9 15.6 %collective-permute-start.1 = (bf16[17,128,128]{2,1,0:T(8,128)(2,1)S(1)}, bf16[17,128,128]{2,1,0:T(8,128)(2,1)S(1)}, u32[]{:S(2)}, u32[]{:S(2)}) collective-permute-start(bf16[17,128,128]{2,1,0:T(8,128)(2,1)S(1)} %pad_maximum_fusion.refs_0_), channel_id=1, source_target_pairs={{0,16},{1,17},{2,18},{3,19},{4,20},{5,21},{6,22},{7,23},{8,24},{9,... | collective-permute-start | bytes 1671176 | tf_op jit(solution)/shard_map/ppermute | solution.py:375
  6.8 23.0 %collective-permute-start = (bf16[256,1024]{1,0:T(8,128)(2,1)}, bf16[256,1024]{1,0:T(8,128)(2,1)S(1)}, u32[]{:S(2)}, u32[]{:S(2)}) collective-permute-start(bf16[256,1024]{1,0:T(8,128)(2,1)} %bitcast.30), channel_id=1, source_target_pairs={{0,8},{1,9},{2,10},{3,11},{4,0},{5,1},{6,2},{7,3},{8,12},{9,13},{1... | collective-permute-start | bytes 1572872 | tf_op jit(solution)/shard_map/ppermute | solution.py:375
  9.4 24.3 %collective-permute-start.4 = (bf16[256,1024]{1,0:T(8,128)(2,1)}, bf16[256,1024]{1,0:T(8,128)(2,1)}, u32[]{:S(2)}, u32[]{:S(2)}) collective-permute-start(bf16[256,1024]{1,0:T(8,128)(2,1)} %bitcast.30), channel_id=1, source_target_pairs={{0,4},{1,5},{2,6},{3,7},{4,12},{5,13},{6,14},{7,15},{8,0},{9,1},{1... | collective-permute-start | bytes 1572872 | tf_op jit(solution)/shard_map/ppermute | solution.py:375
  10.4 19.5 %collective-permute-start.3 = (bf16[1024,256]{1,0:T(8,128)(2,1)S(1)}, bf16[1024,256]{1,0:T(8,128)(2,1)S(1)}, u32[]{:S(2)}, u32[]{:S(2)}) collective-permute-start(bf16[1024,256]{1,0:T(8,128)(2,1)S(1)} %bitcast.39), channel_id=1, source_target_pairs={{0,2},{1,3},{2,0},{3,1},{4,6},{5,7},{6,4},{7,5},{8,10},{9,11},{10,... | collective-permute-start | bytes 1572872 | tf_op jit(solution)/shard_map/ppermute | solution.py:375
  18.5 15.1 %collective-permute-start.2 = (bf16[1024,256]{1,0:T(8,128)(2,1)S(1)}, bf16[1024,256]{1,0:T(8,128)(2,1)S(1)}, u32[]{:S(2)}, u32[]{:S(2)}) collective-permute-start(bf16[1024,256]{1,0:T(8,128)(2,1)S(1)} %bitcast.40), channel_id=1, source_target_pairs={{0,16},{1,17},{2,18},{3,19},{4,20},{5,21},{6,22},{7,23},{8,24},{9,... | collective-permute-start | bytes 1572872 | tf_op jit(solution)/shard_map/ppermute | solution.py:375
  33.6 13.8 %collective-permute-start.5 = (bf16[256,1024]{1,0:T(8,128)(2,1)S(1)}, bf16[256,1024]{1,0:T(8,128)(2,1)S(1)}, u32[]{:S(2)}, u32[]{:S(2)}) collective-permute-start(bf16[256,1024]{1,0:T(8,128)(2,1)S(1)} %collective-permute-done), channel_id=1, source_target_pairs={{0,8},{1,9},{2,10},{3,11},{4,0},{5,1},{6,2},{7,3},{8,12},{9,13},{1... | collective-permute-start | bytes 1572872 | tf_op jit(solution)/shard_map/ppermute | solution.py:375
  36.2 13.5 %collective-permute-start.6 = (bf16[256,1024]{1,0:T(8,128)(2,1)}, bf16[256,1024]{1,0:T(8,128)(2,1)S(1)}, u32[]{:S(2)}, u32[]{:S(2)}) collective-permute-start(bf16[256,1024]{1,0:T(8,128)(2,1)} %select_select_fusion.2), channel_id=1, source_target_pairs={{0,16},{1,17},{2,18},{3,19},{4,20},{5,21},{6,22},{7,23},{8,24},{9,... | collective-permute-start | bytes 1572872 | tf_op jit(solution)/shard_map/ppermute | solution.py:375
  39.0 13.8 %collective-permute-start.8 = (bf16[256,1024]{1,0:T(8,128)(2,1)S(1)}, bf16[256,1024]{1,0:T(8,128)(2,1)S(1)}, u32[]{:S(2)}, u32[]{:S(2)}) collective-permute-start(bf16[256,1024]{1,0:T(8,128)(2,1)S(1)} %select_select_fusion.refs_0_), channel_id=1, source_target_pairs={{0,1},{1,0},{2,3},{3,2},{4,5},{5,4},{6,7},{7,6},{8,9},{9,8},{10,11... | collective-permute-start | bytes 1572872 | tf_op jit(solution)/shard_map/ppermute | solution.py:375
  39.1 14.3 %collective-permute-start.10 = (bf16[1024,256]{1,0:T(8,128)(2,1)S(1)}, bf16[1024,256]{1,0:T(8,128)(2,1)S(1)}, u32[]{:S(2)}, u32[]{:S(2)}) collective-permute-start(bf16[1024,256]{1,0:T(8,128)(2,1)S(1)} %collective-permute-done.2.refs_5_), channel_id=1, source_target_pairs={{0,2},{1,3},{2,0},{3,1},{4,6},{5,7},{6,4},{7,5},{8,10},{9,11},{10,... | collective-permute-start | bytes 1572872 | tf_op jit(solution)/shard_map/ppermute | solution.py:375
  49.6 3.8 %collective-permute-start.9 = (bf16[256,1024]{1,0:T(8,128)(2,1)S(1)}, bf16[256,1024]{1,0:T(8,128)(2,1)S(1)}, u32[]{:S(2)}, u32[]{:S(2)}) collective-permute-start(bf16[256,1024]{1,0:T(8,128)(2,1)S(1)} %collective-permute-done.6.refs_1_), channel_id=1, source_target_pairs={{0,1},{1,0},{2,3},{3,2},{4,5},{5,4},{6,7},{7,6},{8,9},{9,8},{10,11... | collective-permute-start | bytes 1572872 | tf_op jit(solution)/shard_map/ppermute | solution.py:375
  50.6 8.8 %collective-permute-start.7 = (bf16[128,1024]{1,0:T(8,128)(2,1)S(1)}, bf16[128,1024]{1,0:T(8,128)(2,1)S(1)}, u32[]{:S(2)}, u32[]{:S(2)}) collective-permute-start(bf16[128,1024]{1,0:T(8,128)(2,1)S(1)} %select_select_fusion.4), channel_id=1, source_target_pairs={{0,16},{1,17},{2,18},{3,19},{4,20},{5,21},{6,22},{7,23},{8,24},{9,... | collective-permute-start | bytes 786440 | tf_op jit(solution)/shard_map/ppermute | solution.py:375
  52.5 10.2 %collective-permute-start.12 = (bf16[256,1024]{1,0:T(8,128)(2,1)S(1)}, bf16[256,1024]{1,0:T(8,128)(2,1)S(1)}, u32[]{:S(2)}, u32[]{:S(2)}) collective-permute-start(bf16[256,1024]{1,0:T(8,128)(2,1)S(1)} %select_select_fusion.1.refs_0_), channel_id=1, source_target_pairs={{0,1},{1,0},{2,3},{3,2},{4,5},{5,4},{6,7},{7,6},{8,9},{9,8},{10,11... | collective-permute-start | bytes 1572872 | tf_op jit(solution)/shard_map/ppermute | solution.py:375
  59.4 3.3 %collective-permute-start.13 = (bf16[128,1024]{1,0:T(8,128)(2,1)S(1)}, bf16[128,1024]{1,0:T(8,128)(2,1)S(1)}, u32[]{:S(2)}, u32[]{:S(2)}) collective-permute-start(bf16[128,1024]{1,0:T(8,128)(2,1)S(1)} %collective-permute-done.7.refs_1_), channel_id=1, source_target_pairs={{0,1},{1,0},{2,3},{3,2},{4,5},{5,4},{6,7},{7,6},{8,9},{9,8},{10,11... | collective-permute-start | bytes 786440 | tf_op jit(solution)/shard_map/ppermute | solution.py:375
  60.4 8.8 %collective-permute-start.11 = (bf16[128,1024]{1,0:T(8,128)(2,1)S(1)}, bf16[128,1024]{1,0:T(8,128)(2,1)S(1)}, u32[]{:S(2)}, u32[]{:S(2)}) collective-permute-start(bf16[128,1024]{1,0:T(8,128)(2,1)S(1)} %select_select_fusion.3), channel_id=1, source_target_pairs={{0,16},{1,17},{2,18},{3,19},{4,20},{5,21},{6,22},{7,23},{8,24},{9,... | collective-permute-start | bytes 786440 | tf_op jit(solution)/shard_map/ppermute | solution.py:375
  61.2 15.0 %collective-permute-start.17 = (bf16[512,512]{1,0:T(8,128)(2,1)}, bf16[512,512]{1,0:T(8,128)(2,1)S(1)}, u32[]{:S(2)}, u32[]{:S(2)}) collective-permute-start(bf16[512,512]{1,0:T(8,128)(2,1)} %get-tuple-element.48), channel_id=1, source_target_pairs={{0,2},{1,3},{2,0},{3,1},{4,6},{5,7},{6,4},{7,5},{8,10},{9,11},{10,... | collective-permute-start | bytes 1572872 | tf_op jit(solution)/shard_map/ppermute | solution.py:375
  69.2 1.5 %collective-permute-start.14 = (bf16[128,1024]{1,0:T(8,128)(2,1)S(1)}, bf16[128,1024]{1,0:T(8,128)(2,1)S(1)}, u32[]{:S(2)}, u32[]{:S(2)}) collective-permute-start(bf16[128,1024]{1,0:T(8,128)(2,1)S(1)} %collective-permute-done.11.refs_1_), channel_id=1, source_target_pairs={{0,1},{1,0},{2,3},{3,2},{4,5},{5,4},{6,7},{7,6},{8,9},{9,8},{10,11... | collective-permute-start | bytes 786440 | tf_op jit(solution)/shard_map/ppermute | solution.py:375
  69.2 12.6 %collective-permute-start.16 = (bf16[256,512]{1,0:T(8,128)(2,1)}, bf16[256,512]{1,0:T(8,128)(2,1)S(1)}, u32[]{:S(2)}, u32[]{:S(2)}) collective-permute-start(bf16[256,512]{1,0:T(8,128)(2,1)} %get-tuple-element.53), channel_id=1, source_target_pairs={{0,2},{1,3},{2,0},{3,1},{4,6},{5,7},{6,4},{7,5},{8,10},{9,11},{10,... | collective-permute-start | bytes 786440 | tf_op jit(solution)/shard_map/ppermute | solution.py:375
  72.7 13.9 %collective-permute-start.15 = (bf16[256,512]{1,0:T(8,128)(2,1)}, bf16[256,512]{1,0:T(8,128)(2,1)S(1)}, u32[]{:S(2)}, u32[]{:S(2)}) collective-permute-start(bf16[256,512]{1,0:T(8,128)(2,1)} %get-tuple-element.55), channel_id=1, source_target_pairs={{0,2},{1,3},{2,0},{3,1},{4,6},{5,7},{6,4},{7,5},{8,10},{9,11},{10,... | collective-permute-start | bytes 786440 | tf_op jit(solution)/shard_map/ppermute | solution.py:375
  (2 other events, 15.3 us)

commit v9 on v8

--- a/solution.py
+++ b/solution.py
@@ -422,22 +422,8 @@
     held = {0: aux_flat, 1: along(aux_flat, 1), length - 1: along(aux_flat, -1)}
     packed = jnp.concatenate([item_rows, slot_block(slots, item_rows)], axis=0)
     items_x = to_plane(packed)
-    turned_x = to_plane(after(turned, items_x))
+    turned_x = to_plane(turned)
     factors = [[turned, turned_x]] + [[over_y(turned, s)] for s in range(1, breadth)]
-    begun = [turned_x, *(pair[0] for pair in factors[1:]), held[1], held[length - 1]]
-    for s in range(1, breadth):
-        factors[s].append(over_y(after(turned_x, *begun), s))
-    for k in range(2, length // 2 + 1):
-        held[k] = along(after(held[k - 1], *begun), 1)
-    for k in range(2, (length + 1) // 2):
-        held[length - k] = along(after(held[length - k + 1], *begun), -1)
-
-    images, sub_ids, live = jnp.concatenate([slots, read_slots(items_x, slots)], axis=1)
-    table = slot_table(image_dist, image_phase, images)
-    short = short_range(
-        half, live, sub_ids, table, aux_basis, aux_decay, [packed, items_x], row_count, subs
-    )
-
     parts = 2 if rows % 32 == 0 else 1
     units = [(n, 0, rows) for n in range(home - 1)]
     units += [(home - 1, k * (rows // parts), rows // parts) for k in range(parts)]
@@ -456,15 +442,33 @@
         away.append(made[1:])
         arriving.append([over_y(v, s) for s, v in enumerate(made[1:], 1)])
 
+    def foreign(i, *earlier):
+        n, first, count = units[i]
+        theirs.append(pick(True, n, slice(first, first + count), *earlier))
+        return to_plane(theirs[i])
+
+    moved = foreign(0)
+    begun = [items_x, turned_x, *(pair[0] for pair in factors[1:]), held[1], held[length - 1]]
+    begun = [theirs[0], *begun]
+    for k in range(2, length // 2 + 1):
+        held[k] = along(after(held[k - 1], *begun), 1)
+    for k in range(2, (length + 1) // 2):
+        held[length - k] = along(after(held[length - k + 1], *begun), -1)
+    for s in range(1, breadth):
+        factors[s].append(over_y(after(turned_x, *begun), s))
+    seen, sub_ids, live = jnp.concatenate([slots, read_slots(after(items_x, *begun), slots)], axis=1)
+    table = slot_table(image_dist, image_phase, seen)
+    short = short_range(
+        half, live, sub_ids, table, aux_basis, aux_decay, [packed, items_x], row_count, subs
+    )
     for i, (n, first, count) in enumerate(units):
-        gate = [*begun, short] if i == 0 else [moved, *(away[i - 2] if i > 1 else [])]
-        theirs.append(pick(True, n, slice(first, first + count), *gate))
-        moved = to_plane(theirs[i])
+        if i:
+            moved = foreign(i, theirs[i - 1], *(away[i - 2] if i > 1 else [short]))
         if n not in mine:
             mine[n] = with_cores(pick(False, n, slice(None), theirs[i]))
         if i:
             multiply(i - 1)
-        crossed.append(with_cores(after(moved, *away[i - 1] if i else [])))
+        crossed.append(with_cores(after(moved, *away[i - 1] if i else [short])))
     last = len(units) - 1
 
     def place_of(piece, i, s):

time: 89.5 us -> 89.7 us (level)
    convert_element_type x1, other arithmetic: 0.41 us -> 1.45 us  [body(): weighted = (pairs * coul_weight[None, None, :]).astype(jnp.bfloat16)]
    unnamed x18 -> x14, local copies, waits for them, and re-layouts: 2.23 us -> 2.27 us
  transfers between devices with their start and end apart: 18 -> 18, of which waited for: 10 -> 9; matrix products, arithmetic and copies ran while one was open for 10% -> 9% of each run, Pallas kernels for 26% -> 26%
where the time goes in v9:
time: 89.7 us; the launch traced here: 89.3 us
  waiting for transfers between devices  32.5 us (36%)
  Pallas kernels  26 us (29%)
  starting transfers between devices  19.6 us (22%)
  other arithmetic  7.45 us (8%)
  local copies, waits for them, and re-layouts  2.95 us (3%)
    ppermute x18, waiting for transfers between devices, send(): return lax.ppermute(value, AXES, pairs)  32.5 us
    ppermute x18, starting transfers between devices, send(): return lax.ppermute(value, AXES, pairs)  19.6 us
    pallas_call x3, Pallas kernels, final_sum(): pl.pallas_call(functools.partial(final_kernel, pieces=count, blocks=block...  9.57 us
    pallas_call x1, Pallas kernels, short_range(): pl.pallas_call(kernel, out_shape=pltpu.HBM((row_count, 2 * subs * width),...  9.22 us
    pallas_call x3, Pallas kernels, long_range(): pl.pallas_call(functools.partial(long_kernel, blocks=len(blocks), chains=...  7.2 us
    select_n x5, other arithmetic, pick(): value = jnp.where(wanted == k, block[window], value)  5.48 us
    unnamed x14, local copies, waits for them, and re-layouts  2.27 us
  transfers between devices with their start and end apart: 18, of which 9 were waited for; matrix products, arithmetic and copies ran while one was open for 9% of the time, Pallas kernels for 26%

profile of v9, /device:TPU:0, one launch (start us, length us, event | category | flops | bytes accessed | tf_op | source)
XLA Modules:
  0.0 89.3 jit_solution(1013874639010659552)
XLA Ops:
  0.0 2.0 %copy.18 = bf16[32,8,2,512]{3,1,2,0:T(8,128)(2,1)} copy(bf16[32,8,2,512]{3,2,1,0:T(2,128)(2,1)} %bitcast.46) | data formatting | bytes 1048576
  2.0 4.0 %collective-permute-start = (bf16[256,1024]{1,0:T(8,128)(2,1)}, bf16[256,1024]{1,0:T(8,128)(2,1)S(1)}, u32[]{:S(2)}, u32[]{:S(2)}) collective-permute-start(bf16[256,1024]{1,0:T(8,128)(2,1)} %bitcast.30), channel_id=1, source_target_pairs={{0,8},{1,9},{2,10},{3,11},{4,0},{5,1},{6,2},{7,3},{8,12},{9,13},{1... | collective-permute-start | bytes 1572872 | tf_op jit(solution)/shard_map/ppermute | solution.py:375
  6.0 1.5 %multiply_convert_fusion = bf16[256,2,512]{2,1,0:T(2,128)(2,1)S(1)} fusion(bf16[256,2,512]{2,1,0:T(2,128)(2,1)} %param.11, f32[512]{0:T(512)} %param.13), kind=kLoop, calls=%fused_computation | loop fusion | flops 786432 | bytes 1050624 | tf_op jit(solution)/shard_map/convert_element_type | solution.py:333
  8.0 1.6 %collective-permute-start.3 = (bf16[1024,256]{1,0:T(8,128)(2,1)S(1)}, bf16[1024,256]{1,0:T(8,128)(2,1)S(1)}, u32[]{:S(2)}, u32[]{:S(2)}) collective-permute-start(bf16[1024,256]{1,0:T(8,128)(2,1)S(1)} %bitcast.39), channel_id=1, source_target_pairs={{0,16},{1,17},{2,18},{3,19},{4,20},{5,21},{6,22},{7,23},{8,24},{9,... | collective-permute-start | bytes 1572872 | tf_op jit(solution)/shard_map/ppermute | solution.py:375
  9.6 1.5 %collective-permute-start.4 = (bf16[1024,256]{1,0:T(8,128)(2,1)S(1)}, bf16[1024,256]{1,0:T(8,128)(2,1)S(1)}, u32[]{:S(2)}, u32[]{:S(2)}) collective-permute-start(bf16[1024,256]{1,0:T(8,128)(2,1)S(1)} %bitcast.40), channel_id=1, source_target_pairs={{0,2},{1,3},{2,0},{3,1},{4,6},{5,7},{6,4},{7,5},{8,10},{9,11},{10,... | collective-permute-start | bytes 1572872 | tf_op jit(solution)/shard_map/ppermute | solution.py:375
  12.8 5.9 %collective-permute-done = bf16[256,1024]{1,0:T(8,128)(2,1)S(1)} collective-permute-done((bf16[256,1024]{1,0:T(8,128)(2,1)}, bf16[256,1024]{1,0:T(8,128)(2,1)S(1)}, u32[]{:S(2)}, u32[]{:S(2)}) %collective-permute-start) | collective-permute-done | bytes 524320 | tf_op jit(solution)/shard_map/ppermute | solution.py:375
  18.7 11.8 %collective-permute-done.1 = bf16[256,1024]{1,0:T(8,128)(2,1)} collective-permute-done((bf16[256,1024]{1,0:T(8,128)(2,1)}, bf16[256,1024]{1,0:T(8,128)(2,1)}, u32[]{:S(2)}, u32[]{:S(2)}) %collective-permute-start.1) | collective-permute-done | bytes 524320 | tf_op jit(solution)/shard_map/ppermute | solution.py:375
  31.7 1.7 %collective-permute-start.6 = (bf16[256,1024]{1,0:T(8,128)(2,1)S(1)}, bf16[256,1024]{1,0:T(8,128)(2,1)S(1)}, u32[]{:S(2)}, u32[]{:S(2)}) collective-permute-start(bf16[256,1024]{1,0:T(8,128)(2,1)S(1)} %select_select_fusion.2), channel_id=1, source_target_pairs={{0,16},{1,17},{2,18},{3,19},{4,20},{5,21},{6,22},{7,23},{8,24},{9,... | collective-permute-start | bytes 1572872 | tf_op jit(solution)/shard_map/ppermute | solution.py:375
  34.8 3.0 %collective-permute-start.5 = (bf16[256,1024]{1,0:T(8,128)(2,1)S(1)}, bf16[256,1024]{1,0:T(8,128)(2,1)S(1)}, u32[]{:S(2)}, u32[]{:S(2)}) collective-permute-start(bf16[256,1024]{1,0:T(8,128)(2,1)S(1)} %collective-permute-done), channel_id=1, source_target_pairs={{0,8},{1,9},{2,10},{3,11},{4,0},{5,1},{6,2},{7,3},{8,12},{9,13},{1... | collective-permute-start | bytes 1572872 | tf_op jit(solution)/shard_map/ppermute | solution.py:375
  38.1 1.6 %collective-permute-start.9 = (bf16[1024,256]{1,0:T(8,128)(2,1)S(1)}, bf16[1024,256]{1,0:T(8,128)(2,1)S(1)}, u32[]{:S(2)}, u32[]{:S(2)}) collective-permute-start(bf16[1024,256]{1,0:T(8,128)(2,1)S(1)} %collective-permute-done.3.refs_5_), channel_id=1, source_target_pairs={{0,2},{1,3},{2,0},{3,1},{4,6},{5,7},{6,4},{7,5},{8,10},{9,11},{10,... | collective-permute-start | bytes 1572872 | tf_op jit(solution)/shard_map/ppermute | solution.py:375
  39.8 9.2 %short_range.1.refs_2_.refs_3_.refs_1_ = f32[2048,512]{1,0:T(8,128)} custom-call(s32[1]{0:T(128)} %bitcast.10.half_ref, s32[32]{0:T(128)S(1)} %get-tuple-element.65.live_ref, s32[32]{0:T(128)S(1)} %get-tuple-element.64.sub_ref, f32[3,32]{1,0:T(4,128)S(1)} %pad_maximum_fusion.1.meta_ref, bf16[128,4096]{1,0:T(8,128)(2,1)} %basis_ref.1, ...), custom_call_target="tpu_custom_call" | custom-call | flops 4294967296 | bytes 1 | tf_op jit(solution)/shard_map/short_range/pallas_call | solution.py:125
  50.1 1.5 %collective-permute-start.11 = (bf16[128,1024]{1,0:T(8,128)(2,1)S(1)}, bf16[128,1024]{1,0:T(8,128)(2,1)S(1)}, u32[]{:S(2)}, u32[]{:S(2)}) collective-permute-start(bf16[128,1024]{1,0:T(8,128)(2,1)S(1)} %select_select_fusion.4), channel_id=1, source_target_pairs={{0,16},{1,17},{2,18},{3,19},{4,20},{5,21},{6,22},{7,23},{8,24},{9,... | collective-permute-start | bytes 786440 | tf_op jit(solution)/shard_map/ppermute | solution.py:375
  53.0 3.2 %long_range.3 = (f32[512,512]{1,0:T(8,128)}, bf16[512,512]{1,0:T(8,128)(2,1)}) custom-call(bf16[256,1024]{1,0:T(8,128)(2,1)S(1)} %select_select_fusion.refs_0_, bf16[256,1024]{1,0:T(8,128)(2,1)S(1)} %collective-permute-done.6.refs_1_, bf16[256,1024]{1,0:T(8,128)(2,1)S(1)} %collective-permute-done.7.refs_2_, ...), custom_call_target="tpu_custom_call" | custom-call | flops 1 | bytes 1 | tf_op jit(solution)/shard_map/long_range/pallas_call | solution.py:195
  56.2 2.6 %collective-permute-done.11.refs_1_ = bf16[128,1024]{1,0:T(8,128)(2,1)S(1)} collective-permute-done((bf16[128,1024]{1,0:T(8,128)(2,1)S(1)}, bf16[128,1024]{1,0:T(8,128)(2,1)S(1)}, u32[]{:S(2)}, u32[]{:S(2)}) %collective-permute-start.11) | collective-permute-done | bytes 262176 | tf_op jit(solution)/shard_map/ppermute | solution.py:375
  59.8 1.6 %collective-permute-start.10 = (bf16[128,1024]{1,0:T(8,128)(2,1)S(1)}, bf16[128,1024]{1,0:T(8,128)(2,1)S(1)}, u32[]{:S(2)}, u32[]{:S(2)}) collective-permute-start(bf16[128,1024]{1,0:T(8,128)(2,1)S(1)} %select_select_fusion.3), channel_id=1, source_target_pairs={{0,16},{1,17},{2,18},{3,19},{4,20},{5,21},{6,22},{7,23},{8,24},{9,... | collective-permute-start | bytes 786440 | tf_op jit(solution)/shard_map/ppermute | solution.py:375
  61.8 2.0 %long_range.4 = (f32[256,512]{1,0:T(8,128)}, bf16[256,512]{1,0:T(8,128)(2,1)}) custom-call(bf16[256,1024]{1,0:T(8,128)(2,1)S(1)} %select_select_fusion.1.refs_0_, bf16[128,1024]{1,0:T(8,128)(2,1)S(1)} %collective-permute-done.11.refs_1_, bf16[256,1024]{1,0:T(8,128)(2,1)S(1)} %collective-permute-done.12.refs_2_, ...), custom_call_target="tpu_custom_call" | custom-call | flops 1 | bytes 1 | tf_op jit(solution)/shard_map/long_range/pallas_call | solution.py:195
  63.8 4.8 %collective-permute-done.10.refs_1_ = bf16[128,1024]{1,0:T(8,128)(2,1)S(1)} collective-permute-done((bf16[128,1024]{1,0:T(8,128)(2,1)S(1)}, bf16[128,1024]{1,0:T(8,128)(2,1)S(1)}, u32[]{:S(2)}, u32[]{:S(2)}) %collective-permute-start.10) | collective-permute-done | bytes 262176 | tf_op jit(solution)/shard_map/ppermute | solution.py:375
  70.2 2.0 %long_range.5 = (f32[256,512]{1,0:T(8,128)}, bf16[256,512]{1,0:T(8,128)(2,1)}) custom-call(bf16[256,1024]{1,0:T(8,128)(2,1)S(1)} %select_select_fusion.1.refs_0_, bf16[128,1024]{1,0:T(8,128)(2,1)S(1)} %collective-permute-done.10.refs_1_, bf16[256,1024]{1,0:T(8,128)(2,1)S(1)} %collective-permute-done.12.refs_2_, ...), custom_call_target="tpu_custom_call" | custom-call | flops 1 | bytes 1 | tf_op jit(solution)/shard_map/long_range/pallas_call | solution.py:195
  73.2 3.1 %collective-permute-done.17.refs_1_ = bf16[512,512]{1,0:T(8,128)(2,1)S(1)} collective-permute-done((bf16[512,512]{1,0:T(8,128)(2,1)}, bf16[512,512]{1,0:T(8,128)(2,1)S(1)}, u32[]{:S(2)}, u32[]{:S(2)}) %collective-permute-start.17) | collective-permute-done | bytes 524320 | tf_op jit(solution)/shard_map/ppermute | solution.py:375
  76.4 3.8 %final_sum.3.refs_4_ = bf16[2048,2,256]{2,1,0:T(2,128)(2,1)} custom-call(s32[4]{0:T(128)S(1)} %pad_add_fusion.3.order_ref, f32[512,512]{1,0:T(8,128)} %get-tuple-element.60.refs_0_, bf16[512,512]{1,0:T(8,128)(2,1)S(1)} %collective-permute-done.17.refs_1_, f32[2048,512]{1,0:T(8,128)} %short_range.1.refs_2_.refs_3_.refs_1_), custom_call_target="tpu_custom_call" | custom-call | flops 1 | bytes 1 | tf_op jit(solution)/shard_map/final_sum/pallas_call | solution.py:252
  80.2 1.8 %collective-permute-done.16.refs_1_ = bf16[256,512]{1,0:T(8,128)(2,1)S(1)} collective-permute-done((bf16[256,512]{1,0:T(8,128)(2,1)}, bf16[256,512]{1,0:T(8,128)(2,1)S(1)}, u32[]{:S(2)}, u32[]{:S(2)}) %collective-permute-start.16) | collective-permute-done | bytes 262176 | tf_op jit(solution)/shard_map/ppermute | solution.py:375
  82.0 3.3 %final_sum.4.refs_2_ = bf16[2048,2,256]{2,1,0:T(2,128)(2,1)} custom-call(s32[6]{0:T(128)S(1)} %stack.77.order_ref, f32[256,512]{1,0:T(8,128)} %get-tuple-element.58.refs_0_, bf16[256,512]{1,0:T(8,128)(2,1)S(1)} %collective-permute-done.16.refs_1_, f32[256,512]{1,0:T(8,128)} %get-tuple-element.59.refs_2_, ...), custom_call_target="tpu_custom_call", output_to_operand_aliasing={{}: (5, {})} | custom-call | flops 1 | bytes 1 | tf_op jit(solution)/shard_map/final_sum/pallas_call | solution.py:252
  85.3 1.6 %collective-permute-done.15.refs_0_ = bf16[256,512]{1,0:T(8,128)(2,1)S(1)} collective-permute-done((bf16[256,512]{1,0:T(8,128)(2,1)}, bf16[256,512]{1,0:T(8,128)(2,1)S(1)}, u32[]{:S(2)}, u32[]{:S(2)}) %collective-permute-start.15) | collective-permute-done | bytes 262176 | tf_op jit(solution)/shard_map/ppermute | solution.py:375
  86.9 2.4 %final_sum.5 = bf16[2048,2,256]{2,1,0:T(2,128)(2,1)} custom-call(s32[2]{0:T(128)S(1)} %pad_add_fusion.2.order_ref, bf16[256,512]{1,0:T(8,128)(2,1)S(1)} %collective-permute-done.15.refs_0_, f32[2048,512]{1,0:T(8,128)} %short_range.1.refs_2_.refs_3_.refs_1_, bf16[2048,2,256]{2,1,0:T(2,128)(2,1)} %final_sum.4.refs_2_), custom_call_target="tpu_custom_call", output_to_operand_aliasing={{}: (3, {})} | custom-call | flops 1 | bytes 1 | tf_op jit(solution)/shard_map/final_sum/pallas_call | solution.py:252
  (54 shorter events, 10.9 us)
Async XLA Ops:
  0.0 11.8 %copy-start.1 = (bf16[16,128,128]{2,1,0:T(8,128)(2,1)S(1)}, bf16[16,128,128]{2,1,0:T(8,128)(2,1)}, u32[]{:S(2)}) copy-start(bf16[16,128,128]{2,1,0:T(8,128)(2,1)} %param.18) | copy-start | bytes 1572868
  0.0 12.1 %copy-start.2 = (s32[16]{0:T(128)S(1)}, s32[16]{0:T(128)}, u32[]{:S(2)}) copy-start(s32[16]{0:T(128)} %param.20) | copy-start | bytes 196
  0.0 12.1 %copy-start.3 = (s32[16]{0:T(128)S(1)}, s32[16]{0:T(128)}, u32[]{:S(2)}) copy-start(s32[16]{0:T(128)} %param.19) | copy-start | bytes 196
  2.0 16.7 %collective-permute-start = (bf16[256,1024]{1,0:T(8,128)(2,1)}, bf16[256,1024]{1,0:T(8,128)(2,1)S(1)}, u32[]{:S(2)}, u32[]{:S(2)}) collective-permute-start(bf16[256,1024]{1,0:T(8,128)(2,1)} %bitcast.30), channel_id=1, source_target_pairs={{0,8},{1,9},{2,10},{3,11},{4,0},{5,1},{6,2},{7,3},{8,12},{9,13},{1... | collective-permute-start | bytes 1572872 | tf_op jit(solution)/shard_map/ppermute | solution.py:375
  6.0 24.5 %collective-permute-start.1 = (bf16[256,1024]{1,0:T(8,128)(2,1)}, bf16[256,1024]{1,0:T(8,128)(2,1)}, u32[]{:S(2)}, u32[]{:S(2)}) collective-permute-start(bf16[256,1024]{1,0:T(8,128)(2,1)} %bitcast.30), channel_id=1, source_target_pairs={{0,4},{1,5},{2,6},{3,7},{4,12},{5,13},{6,14},{7,15},{8,0},{9,1},{1... | collective-permute-start | bytes 1572872 | tf_op jit(solution)/shard_map/ppermute | solution.py:375
  8.0 26.7 %collective-permute-start.3 = (bf16[1024,256]{1,0:T(8,128)(2,1)S(1)}, bf16[1024,256]{1,0:T(8,128)(2,1)S(1)}, u32[]{:S(2)}, u32[]{:S(2)}) collective-permute-start(bf16[1024,256]{1,0:T(8,128)(2,1)S(1)} %bitcast.39), channel_id=1, source_target_pairs={{0,16},{1,17},{2,18},{3,19},{4,20},{5,21},{6,22},{7,23},{8,24},{9,... | collective-permute-start | bytes 1572872 | tf_op jit(solution)/shard_map/ppermute | solution.py:375
  9.6 25.2 %collective-permute-start.4 = (bf16[1024,256]{1,0:T(8,128)(2,1)S(1)}, bf16[1024,256]{1,0:T(8,128)(2,1)S(1)}, u32[]{:S(2)}, u32[]{:S(2)}) collective-permute-start(bf16[1024,256]{1,0:T(8,128)(2,1)S(1)} %bitcast.40), channel_id=1, source_target_pairs={{0,2},{1,3},{2,0},{3,1},{4,6},{5,7},{6,4},{7,5},{8,10},{9,11},{10,... | collective-permute-start | bytes 1572872 | tf_op jit(solution)/shard_map/ppermute | solution.py:375
  12.2 22.6 %collective-permute-start.2 = (bf16[17,128,128]{2,1,0:T(8,128)(2,1)S(1)}, bf16[17,128,128]{2,1,0:T(8,128)(2,1)S(1)}, u32[]{:S(2)}, u32[]{:S(2)}) collective-permute-start(bf16[17,128,128]{2,1,0:T(8,128)(2,1)S(1)} %pad_maximum_fusion.refs_0_), channel_id=1, source_target_pairs={{0,16},{1,17},{2,18},{3,19},{4,20},{5,21},{6,22},{7,23},{8,24},{9,... | collective-permute-start | bytes 1671176 | tf_op jit(solution)/shard_map/ppermute | solution.py:375
  12.8 25.1 %copy-start.4 = (f32[125]{0:T(128)S(1)}, f32[125]{0:T(128)}, u32[]{:S(2)}) copy-start(f32[125]{0:T(128)} %param.16) | copy-start | bytes 1504
  12.8 25.1 %copy-start.5 = (f32[125]{0:T(128)S(1)}, f32[125]{0:T(128)}, u32[]{:S(2)}) copy-start(f32[125]{0:T(128)} %param.17) | copy-start | bytes 1504
  12.8 27.0 %copy-start = (f32[4096]{0:T(1024)S(1)}, f32[4096]{0:T(1024)}, u32[]{:S(2)}) copy-start(f32[4096]{0:T(1024)} %param.15) | copy-start | bytes 49156
  31.7 17.3 %collective-permute-start.6 = (bf16[256,1024]{1,0:T(8,128)(2,1)S(1)}, bf16[256,1024]{1,0:T(8,128)(2,1)S(1)}, u32[]{:S(2)}, u32[]{:S(2)}) collective-permute-start(bf16[256,1024]{1,0:T(8,128)(2,1)S(1)} %select_select_fusion.2), channel_id=1, source_target_pairs={{0,16},{1,17},{2,18},{3,19},{4,20},{5,21},{6,22},{7,23},{8,24},{9,... | collective-permute-start | bytes 1572872 | tf_op jit(solution)/shard_map/ppermute | solution.py:375
  34.7 18.4 %collective-permute-start.7 = (bf16[256,1024]{1,0:T(8,128)(2,1)S(1)}, bf16[256,1024]{1,0:T(8,128)(2,1)S(1)}, u32[]{:S(2)}, u32[]{:S(2)}) collective-permute-start(bf16[256,1024]{1,0:T(8,128)(2,1)S(1)} %select_select_fusion.refs_0_), channel_id=1, source_target_pairs={{0,1},{1,0},{2,3},{3,2},{4,5},{5,4},{6,7},{7,6},{8,9},{9,8},{10,11... | collective-permute-start | bytes 1572872 | tf_op jit(solution)/shard_map/ppermute | solution.py:375
  34.8 14.4 %collective-permute-start.5 = (bf16[256,1024]{1,0:T(8,128)(2,1)S(1)}, bf16[256,1024]{1,0:T(8,128)(2,1)S(1)}, u32[]{:S(2)}, u32[]{:S(2)}) collective-permute-start(bf16[256,1024]{1,0:T(8,128)(2,1)S(1)} %collective-permute-done), channel_id=1, source_target_pairs={{0,8},{1,9},{2,10},{3,11},{4,0},{5,1},{6,2},{7,3},{8,12},{9,13},{1... | collective-permute-start | bytes 1572872 | tf_op jit(solution)/shard_map/ppermute | solution.py:375
  38.1 14.9 %collective-permute-start.9 = (bf16[1024,256]{1,0:T(8,128)(2,1)S(1)}, bf16[1024,256]{1,0:T(8,128)(2,1)S(1)}, u32[]{:S(2)}, u32[]{:S(2)}) collective-permute-start(bf16[1024,256]{1,0:T(8,128)(2,1)S(1)} %collective-permute-done.3.refs_5_), channel_id=1, source_target_pairs={{0,2},{1,3},{2,0},{3,1},{4,6},{5,7},{6,4},{7,5},{8,10},{9,11},{10,... | collective-permute-start | bytes 1572872 | tf_op jit(solution)/shard_map/ppermute | solution.py:375
  49.0 4.0 %collective-permute-start.8 = (bf16[256,1024]{1,0:T(8,128)(2,1)S(1)}, bf16[256,1024]{1,0:T(8,128)(2,1)S(1)}, u32[]{:S(2)}, u32[]{:S(2)}) collective-permute-start(bf16[256,1024]{1,0:T(8,128)(2,1)S(1)} %collective-permute-done.6.refs_1_), channel_id=1, source_target_pairs={{0,1},{1,0},{2,3},{3,2},{4,5},{5,4},{6,7},{7,6},{8,9},{9,8},{10,11... | collective-permute-start | bytes 1572872 | tf_op jit(solution)/shard_map/ppermute | solution.py:375
  50.1 8.7 %collective-permute-start.11 = (bf16[128,1024]{1,0:T(8,128)(2,1)S(1)}, bf16[128,1024]{1,0:T(8,128)(2,1)S(1)}, u32[]{:S(2)}, u32[]{:S(2)}) collective-permute-start(bf16[128,1024]{1,0:T(8,128)(2,1)S(1)} %select_select_fusion.4), channel_id=1, source_target_pairs={{0,16},{1,17},{2,18},{3,19},{4,20},{5,21},{6,22},{7,23},{8,24},{9,... | collective-permute-start | bytes 786440 | tf_op jit(solution)/shard_map/ppermute | solution.py:375
  52.7 9.1 %collective-permute-start.12 = (bf16[256,1024]{1,0:T(8,128)(2,1)S(1)}, bf16[256,1024]{1,0:T(8,128)(2,1)S(1)}, u32[]{:S(2)}, u32[]{:S(2)}) collective-permute-start(bf16[256,1024]{1,0:T(8,128)(2,1)S(1)} %select_select_fusion.1.refs_0_), channel_id=1, source_target_pairs={{0,1},{1,0},{2,3},{3,2},{4,5},{5,4},{6,7},{7,6},{8,9},{9,8},{10,11... | collective-permute-start | bytes 1572872 | tf_op jit(solution)/shard_map/ppermute | solution.py:375
  58.8 3.0 %collective-permute-start.13 = (bf16[128,1024]{1,0:T(8,128)(2,1)S(1)}, bf16[128,1024]{1,0:T(8,128)(2,1)S(1)}, u32[]{:S(2)}, u32[]{:S(2)}) collective-permute-start(bf16[128,1024]{1,0:T(8,128)(2,1)S(1)} %collective-permute-done.11.refs_1_), channel_id=1, source_target_pairs={{0,1},{1,0},{2,3},{3,2},{4,5},{5,4},{6,7},{7,6},{8,9},{9,8},{10,11... | collective-permute-start | bytes 786440 | tf_op jit(solution)/shard_map/ppermute | solution.py:375
  59.8 8.8 %collective-permute-start.10 = (bf16[128,1024]{1,0:T(8,128)(2,1)S(1)}, bf16[128,1024]{1,0:T(8,128)(2,1)S(1)}, u32[]{:S(2)}, u32[]{:S(2)}) collective-permute-start(bf16[128,1024]{1,0:T(8,128)(2,1)S(1)} %select_select_fusion.3), channel_id=1, source_target_pairs={{0,16},{1,17},{2,18},{3,19},{4,20},{5,21},{6,22},{7,23},{8,24},{9,... | collective-permute-start | bytes 786440 | tf_op jit(solution)/shard_map/ppermute | solution.py:375
  61.4 15.0 %collective-permute-start.17 = (bf16[512,512]{1,0:T(8,128)(2,1)}, bf16[512,512]{1,0:T(8,128)(2,1)S(1)}, u32[]{:S(2)}, u32[]{:S(2)}) collective-permute-start(bf16[512,512]{1,0:T(8,128)(2,1)} %get-tuple-element.50), channel_id=1, source_target_pairs={{0,2},{1,3},{2,0},{3,1},{4,6},{5,7},{6,4},{7,5},{8,10},{9,11},{10,... | collective-permute-start | bytes 1572872 | tf_op jit(solution)/shard_map/ppermute | solution.py:375
  68.6 1.5 %collective-permute-start.14 = (bf16[128,1024]{1,0:T(8,128)(2,1)S(1)}, bf16[128,1024]{1,0:T(8,128)(2,1)S(1)}, u32[]{:S(2)}, u32[]{:S(2)}) collective-permute-start(bf16[128,1024]{1,0:T(8,128)(2,1)S(1)} %collective-permute-done.10.refs_1_), channel_id=1, source_target_pairs={{0,1},{1,0},{2,3},{3,2},{4,5},{5,4},{6,7},{7,6},{8,9},{9,8},{10,11... | collective-permute-start | bytes 786440 | tf_op jit(solution)/shard_map/ppermute | solution.py:375
  68.6 13.4 %collective-permute-start.16 = (bf16[256,512]{1,0:T(8,128)(2,1)}, bf16[256,512]{1,0:T(8,128)(2,1)S(1)}, u32[]{:S(2)}, u32[]{:S(2)}) collective-permute-start(bf16[256,512]{1,0:T(8,128)(2,1)} %get-tuple-element.55), channel_id=1, source_target_pairs={{0,2},{1,3},{2,0},{3,1},{4,6},{5,7},{6,4},{7,5},{8,10},{9,11},{10,... | collective-permute-start | bytes 786440 | tf_op jit(solution)/shard_map/ppermute | solution.py:375
  72.2 14.7 %collective-permute-start.15 = (bf16[256,512]{1,0:T(8,128)(2,1)}, bf16[256,512]{1,0:T(8,128)(2,1)S(1)}, u32[]{:S(2)}, u32[]{:S(2)}) collective-permute-start(bf16[256,512]{1,0:T(8,128)(2,1)} %get-tuple-element.57), channel_id=1, source_target_pairs={{0,2},{1,3},{2,0},{3,1},{4,6},{5,7},{6,4},{7,5},{8,10},{9,11},{10,... | collective-permute-start | bytes 786440 | tf_op jit(solution)/shard_map/ppermute | solution.py:375

commit v10 on v9

--- a/solution.py
+++ b/solution.py
@@ -421,12 +421,12 @@
 
     held = {0: aux_flat, 1: along(aux_flat, 1), length - 1: along(aux_flat, -1)}
     packed = jnp.concatenate([item_rows, slot_block(slots, item_rows)], axis=0)
-    items_x = to_plane(packed)
     turned_x = to_plane(turned)
     factors = [[turned, turned_x]] + [[over_y(turned, s)] for s in range(1, breadth)]
-    parts = 2 if rows % 32 == 0 else 1
-    units = [(n, 0, rows) for n in range(home - 1)]
-    units += [(home - 1, k * (rows // parts), rows // parts) for k in range(parts)]
+    items_x = to_plane(after(packed, *(pair[0] for pair in factors[1:]), turned_x, held[1]))
+    for s in range(1, breadth):
+        factors[s].append(over_y(turned_x, s))
+    units = [(n, 0, rows) for n in range(home)]
     mine = {}
     theirs = []
     crossed = []
@@ -447,28 +447,25 @@
         theirs.append(pick(True, n, slice(first, first + count), *earlier))
         return to_plane(theirs[i])
 
-    moved = foreign(0)
-    begun = [items_x, turned_x, *(pair[0] for pair in factors[1:]), held[1], held[length - 1]]
-    begun = [theirs[0], *begun]
+    moved = foreign(0, items_x, *(pair[1] for pair in factors[1:]))
+    begun = [theirs[0], held[1], held[length - 1]]
     for k in range(2, length // 2 + 1):
         held[k] = along(after(held[k - 1], *begun), 1)
     for k in range(2, (length + 1) // 2):
         held[length - k] = along(after(held[length - k + 1], *begun), -1)
-    for s in range(1, breadth):
-        factors[s].append(over_y(after(turned_x, *begun), s))
-    seen, sub_ids, live = jnp.concatenate([slots, read_slots(after(items_x, *begun), slots)], axis=1)
+    for i, (n, _, _) in enumerate(units):
+        if i:
+            moved = foreign(i, theirs[i - 1], *(away[i - 2] if i > 1 else []))
+        mine[n] = with_cores(pick(False, n, slice(None), theirs[i]))
+        if i:
+            multiply(i - 1)
+        crossed.append(with_cores(after(moved, *away[i - 1] if i else [])))
+    slots_x = read_slots(after(items_x, *(away[0] if away else [])), slots)
+    seen, sub_ids, live = jnp.concatenate([slots, slots_x], axis=1)
     table = slot_table(image_dist, image_phase, seen)
     short = short_range(
         half, live, sub_ids, table, aux_basis, aux_decay, [packed, items_x], row_count, subs
     )
-    for i, (n, first, count) in enumerate(units):
-        if i:
-            moved = foreign(i, theirs[i - 1], *(away[i - 2] if i > 1 else [short]))
-        if n not in mine:
-            mine[n] = with_cores(pick(False, n, slice(None), theirs[i]))
-        if i:
-            multiply(i - 1)
-        crossed.append(with_cores(after(moved, *away[i - 1] if i else [short])))
     last = len(units) - 1
 
     def place_of(piece, i, s):

time: 89.7 us -> 90.8 us (1.012)
  Pallas kernels: 26 us -> 28.1 us
  starting transfers between devices: 19.6 us -> 18.5 us
  waiting for transfers between devices: 32.5 us -> 31.5 us
    pallas_call x3 -> x2, Pallas kernels: 7.2 us -> 8.79 us  [long_range(): pl.pallas_call(functools.partial(long_kernel, blocks=len(blocks), chains=...]
    ppermute x18 -> x15, starting transfers between devices: 19.6 us -> 18.5 us  [send(): return lax.ppermute(value, AXES, pairs)]
    ppermute x18 -> x15, waiting for transfers between devices: 32.5 us -> 31.5 us  [send(): return lax.ppermute(value, AXES, pairs)]
    select_n x5 -> x4, other arithmetic: 5.48 us -> 5.37 us  [pick(): value = jnp.where(wanted == k, block[window], value)]
    unnamed x14 -> x18, local copies, waits for them, and re-layouts: 2.27 us -> 2.28 us
  transfers between devices with their start and end apart: 18 -> 15, of which waited for: 9 -> 9; matrix products, arithmetic and copies ran while one was open for 9% -> 7% of each run, Pallas kernels for 26% -> 28%
where the time goes in v10:
time: 90.8 us; the launch traced here: 89.9 us
  waiting for transfers between devices  31.5 us (35%)
  Pallas kernels  28.1 us (31%)
  starting transfers between devices  18.5 us (20%)
  other arithmetic  8.09 us (9%)
  local copies, waits for them, and re-layouts  2.87 us (3%)
    ppermute x15, waiting for transfers between devices, send(): return lax.ppermute(value, AXES, pairs)  31.5 us
    ppermute x15, starting transfers between devices, send(): return lax.ppermute(value, AXES, pairs)  18.5 us
    pallas_call x1, Pallas kernels, short_range(): pl.pallas_call(kernel, out_shape=pltpu.HBM((row_count, 2 * subs * width),...  9.68 us
    pallas_call x3, Pallas kernels, final_sum(): pl.pallas_call(functools.partial(final_kernel, pieces=count, blocks=block...  9.65 us
    pallas_call x2, Pallas kernels, long_range(): pl.pallas_call(functools.partial(long_kernel, blocks=len(blocks), chains=...  8.79 us
    select_n x4, other arithmetic, pick(): value = jnp.where(wanted == k, block[window], value)  5.37 us
    unnamed x18, local copies, waits for them, and re-layouts  2.28 us
  transfers between devices with their start and end apart: 15, of which 9 were waited for; matrix products, arithmetic and copies ran while one was open for 7% of the time, Pallas kernels for 28%

profile of v10, /device:TPU:0, one launch (start us, length us, event | category | flops | bytes accessed | tf_op | source)
XLA Modules:
  0.0 89.9 jit_solution(3788740491384880510)
XLA Ops:
  0.0 2.0 %copy.18 = bf16[32,8,2,512]{3,1,2,0:T(8,128)(2,1)} copy(bf16[32,8,2,512]{3,2,1,0:T(2,128)(2,1)} %bitcast.41) | data formatting | bytes 1048576
  2.0 1.5 %multiply_convert_fusion = bf16[256,2,512]{2,1,0:T(2,128)(2,1)S(1)} fusion(bf16[256,2,512]{2,1,0:T(2,128)(2,1)} %param.11, f32[512]{0:T(512)} %param.13), kind=kLoop, calls=%fused_computation | loop fusion | flops 786432 | bytes 1050624 | tf_op jit(solution)/shard_map/convert_element_type | solution.py:333
  4.0 3.0 %collective-permute-start.3 = (bf16[1024,256]{1,0:T(8,128)(2,1)S(1)}, bf16[1024,256]{1,0:T(8,128)(2,1)S(1)}, u32[]{:S(2)}, u32[]{:S(2)}) collective-permute-start(bf16[1024,256]{1,0:T(8,128)(2,1)S(1)} %bitcast.35), channel_id=1, source_target_pairs={{0,16},{1,17},{2,18},{3,19},{4,20},{5,21},{6,22},{7,23},{8,24},{9,... | collective-permute-start | bytes 1572872 | tf_op jit(solution)/shard_map/ppermute | solution.py:375
  7.0 1.5 %collective-permute-start.2 = (bf16[1024,256]{1,0:T(8,128)(2,1)S(1)}, bf16[1024,256]{1,0:T(8,128)(2,1)S(1)}, u32[]{:S(2)}, u32[]{:S(2)}) collective-permute-start(bf16[1024,256]{1,0:T(8,128)(2,1)S(1)} %bitcast.36), channel_id=1, source_target_pairs={{0,2},{1,3},{2,0},{3,1},{4,6},{5,7},{6,4},{7,5},{8,10},{9,11},{10,... | collective-permute-start | bytes 1572872 | tf_op jit(solution)/shard_map/ppermute | solution.py:375
  8.5 2.6 %collective-permute-start = (bf16[256,1024]{1,0:T(8,128)(2,1)}, bf16[256,1024]{1,0:T(8,128)(2,1)}, u32[]{:S(2)}, u32[]{:S(2)}) collective-permute-start(bf16[256,1024]{1,0:T(8,128)(2,1)} %bitcast.26), channel_id=1, source_target_pairs={{0,8},{1,9},{2,10},{3,11},{4,0},{5,1},{6,2},{7,3},{8,12},{9,13},{1... | collective-permute-start | bytes 1572872 | tf_op jit(solution)/shard_map/ppermute | solution.py:375
  12.2 6.7 %collective-permute-done.3.refs_5_ = bf16[1024,256]{1,0:T(8,128)(2,1)S(1)} collective-permute-done((bf16[1024,256]{1,0:T(8,128)(2,1)S(1)}, bf16[1024,256]{1,0:T(8,128)(2,1)S(1)}, u32[]{:S(2)}, u32[]{:S(2)}) %collective-permute-start.3) | collective-permute-done | bytes 524320 | tf_op jit(solution)/shard_map/ppermute | solution.py:375
  18.9 1.5 %collective-permute-done.2.refs_6_ = bf16[1024,256]{1,0:T(8,128)(2,1)S(1)} collective-permute-done((bf16[1024,256]{1,0:T(8,128)(2,1)S(1)}, bf16[1024,256]{1,0:T(8,128)(2,1)S(1)}, u32[]{:S(2)}, u32[]{:S(2)}) %collective-permute-start.2) | collective-permute-done | bytes 524320 | tf_op jit(solution)/shard_map/ppermute | solution.py:375
  20.4 1.7 %collective-permute-done = bf16[256,1024]{1,0:T(8,128)(2,1)} collective-permute-done((bf16[256,1024]{1,0:T(8,128)(2,1)}, bf16[256,1024]{1,0:T(8,128)(2,1)}, u32[]{:S(2)}, u32[]{:S(2)}) %collective-permute-start) | collective-permute-done | bytes 524320 | tf_op jit(solution)/shard_map/ppermute | solution.py:375
  22.6 2.4 %collective-permute-start.1 = (bf16[256,1024]{1,0:T(8,128)(2,1)}, bf16[256,1024]{1,0:T(8,128)(2,1)S(1)}, u32[]{:S(2)}, u32[]{:S(2)}) collective-permute-start(bf16[256,1024]{1,0:T(8,128)(2,1)} %bitcast.26), channel_id=1, source_target_pairs={{0,4},{1,5},{2,6},{3,7},{4,12},{5,13},{6,14},{7,15},{8,0},{9,1},{1... | collective-permute-start | bytes 1572872 | tf_op jit(solution)/shard_map/ppermute | solution.py:375
  25.4 10.9 %collective-permute-done.1 = bf16[256,1024]{1,0:T(8,128)(2,1)S(1)} collective-permute-done((bf16[256,1024]{1,0:T(8,128)(2,1)}, bf16[256,1024]{1,0:T(8,128)(2,1)S(1)}, u32[]{:S(2)}, u32[]{:S(2)}) %collective-permute-start.1) | collective-permute-done | bytes 524320 | tf_op jit(solution)/shard_map/ppermute | solution.py:375
  37.4 2.9 %collective-permute-start.6 = (bf16[256,1024]{1,0:T(8,128)(2,1)}, bf16[256,1024]{1,0:T(8,128)(2,1)}, u32[]{:S(2)}, u32[]{:S(2)}) collective-permute-start(bf16[256,1024]{1,0:T(8,128)(2,1)} %collective-permute-done), channel_id=1, source_target_pairs={{0,8},{1,9},{2,10},{3,11},{4,0},{5,1},{6,2},{7,3},{8,12},{9,13},{1... | collective-permute-start | bytes 1572872 | tf_op jit(solution)/shard_map/ppermute | solution.py:375
  40.3 1.4 %collective-permute-start.8 = (bf16[256,1024]{1,0:T(8,128)(2,1)}, bf16[256,1024]{1,0:T(8,128)(2,1)}, u32[]{:S(2)}, u32[]{:S(2)}) collective-permute-start(bf16[256,1024]{1,0:T(8,128)(2,1)} %select_select_fusion.3), channel_id=1, source_target_pairs={{0,16},{1,17},{2,18},{3,19},{4,20},{5,21},{6,22},{7,23},{8,24},{9,... | collective-permute-start | bytes 1572872 | tf_op jit(solution)/shard_map/ppermute | solution.py:375
  41.7 1.3 %select_select_fusion.refs_0_ = bf16[256,1024]{1,0:T(8,128)(2,1)S(1)} fusion(bf16[256,1024]{1,0:T(8,128)(2,1)} %bitcast.26, bf16[256,1024]{1,0:T(8,128)(2,1)} %collective-permute-done, bf16[256,1024]{1,0:T(8,128)(2,1)} %copy-done.1, pred[]{:T(512)S(6)} %eq.70, pred[]{:T(512)S(6)} %eq.69), kind=kLoop, calls=%fused_computation.2 | loop fusion | flops 524288 | bytes 2097154 | tf_op jit(solution)/shard_map/jit(_where)/select_n | solution.py:409
  43.1 6.5 %collective-permute-done.6 = bf16[256,1024]{1,0:T(8,128)(2,1)} collective-permute-done((bf16[256,1024]{1,0:T(8,128)(2,1)}, bf16[256,1024]{1,0:T(8,128)(2,1)}, u32[]{:S(2)}, u32[]{:S(2)}) %collective-permute-start.6) | collective-permute-done | bytes 524320 | tf_op jit(solution)/shard_map/ppermute | solution.py:375
  49.5 1.9 %select_select_fusion.2 = bf16[256,1024]{1,0:T(8,128)(2,1)} fusion(bf16[256,1024]{1,0:T(8,128)(2,1)} %collective-permute-done, bf16[256,1024]{1,0:T(8,128)(2,1)} %collective-permute-done.6, bf16[256,1024]{1,0:T(8,128)(2,1)S(1)} %copy-done.2, pred[]{:T(512)S(6)} %eq.67, pred[]{:T(512)S(6)} %eq.66), kind=kLoop, calls=%fused_computation.4 | loop fusion | flops 524288 | bytes 2097154 | tf_op jit(solution)/shard_map/jit(_where)/select_n | solution.py:409
  51.4 2.0 %collective-permute-start.7 = (bf16[256,1024]{1,0:T(8,128)(2,1)}, bf16[256,1024]{1,0:T(8,128)(2,1)}, u32[]{:S(2)}, u32[]{:S(2)}) collective-permute-start(bf16[256,1024]{1,0:T(8,128)(2,1)} %select_select_fusion.2), channel_id=1, source_target_pairs={{0,16},{1,17},{2,18},{3,19},{4,20},{5,21},{6,22},{7,23},{8,24},{9,... | collective-permute-start | bytes 1572872 | tf_op jit(solution)/shard_map/ppermute | solution.py:375
  55.7 4.5 %long_range.2 = (f32[512,512]{1,0:T(8,128)}, bf16[512,512]{1,0:T(8,128)(2,1)}) custom-call(bf16[256,1024]{1,0:T(8,128)(2,1)S(1)} %select_select_fusion.refs_0_, bf16[256,1024]{1,0:T(8,128)(2,1)} %collective-permute-done.8.refs_1_, bf16[256,1024]{1,0:T(8,128)(2,1)} %collective-permute-done.9.refs_2_, bf16[256,1024]{1,0:T(8,128)(2,1)} %collective-permute-done.10.refs_3_, ...), custom_call_target="tpu_custom_call" | custom-call | flops 1 | bytes 1 | tf_op jit(solution)/shard_map/long_range/pallas_call | solution.py:195
  60.8 2.1 %collective-permute-done.7.refs_1_ = bf16[256,1024]{1,0:T(8,128)(2,1)} collective-permute-done((bf16[256,1024]{1,0:T(8,128)(2,1)}, bf16[256,1024]{1,0:T(8,128)(2,1)}, u32[]{:S(2)}, u32[]{:S(2)}) %collective-permute-start.7) | collective-permute-done | bytes 524320 | tf_op jit(solution)/shard_map/ppermute | solution.py:375
  63.8 1.8 %collective-permute-done.12.refs_3_ = bf16[256,1024]{1,0:T(8,128)(2,1)S(1)} collective-permute-done((bf16[256,1024]{1,0:T(8,128)(2,1)}, bf16[256,1024]{1,0:T(8,128)(2,1)S(1)}, u32[]{:S(2)}, u32[]{:S(2)}) %collective-permute-start.12) | collective-permute-done | bytes 524320 | tf_op jit(solution)/shard_map/ppermute | solution.py:375
  65.6 4.3 %long_range.3 = (f32[512,512]{1,0:T(8,128)}, bf16[512,512]{1,0:T(8,128)(2,1)}) custom-call(bf16[256,1024]{1,0:T(8,128)(2,1)S(1)} %select_select_fusion.1.refs_0_, bf16[256,1024]{1,0:T(8,128)(2,1)} %collective-permute-done.7.refs_1_, bf16[256,1024]{1,0:T(8,128)(2,1)S(1)} %collective-permute-done.11.refs_2_, ...), custom_call_target="tpu_custom_call" | custom-call | flops 1 | bytes 1 | tf_op jit(solution)/shard_map/long_range/pallas_call | solution.py:195
  70.5 9.7 %short_range.1.refs_2_.refs_1_ = f32[2048,512]{1,0:T(8,128)} custom-call(s32[1]{0:T(128)} %bitcast.10.half_ref, s32[32]{0:T(128)S(1)} %get-tuple-element.51.live_ref, s32[32]{0:T(128)S(1)} %get-tuple-element.50.sub_ref, f32[3,32]{1,0:T(4,128)S(1)} %pad_maximum_fusion.1.meta_ref, bf16[128,4096]{1,0:T(8,128)(2,1)} %basis_ref.1, f32[1,4096]{1,0:T(1,128)S(1)} %bitcast.39, ...), custom_call_target="tpu_custom_call" | custom-call | flops 4294967296 | bytes 1 | tf_op jit(solution)/shard_map/short_range/pallas_call | solution.py:125
  80.2 3.9 %final_sum.3.refs_2_ = bf16[2048,2,256]{2,1,0:T(2,128)(2,1)} custom-call(s32[4]{0:T(128)S(1)} %pad_add_fusion.4.order_ref, f32[512,512]{1,0:T(8,128)} %get-tuple-element.46.refs_0_, bf16[512,512]{1,0:T(8,128)(2,1)S(1)} %collective-permute-done.14.refs_1_, f32[2048,512]{1,0:T(8,128)} %short_range.1.refs_2_.refs_1_), custom_call_target="tpu_custom_call" | custom-call | flops 1 | bytes 1 | tf_op jit(solution)/shard_map/final_sum/pallas_call | solution.py:252
  84.1 3.0 %final_sum.4.refs_2_ = bf16[2048,2,256]{2,1,0:T(2,128)(2,1)} custom-call(s32[2]{0:T(128)S(1)} %pad_add_fusion.3.order_ref, f32[512,512]{1,0:T(8,128)} %get-tuple-element.45.refs_0_, f32[2048,512]{1,0:T(8,128)} %short_range.1.refs_2_.refs_1_, bf16[2048,2,256]{2,1,0:T(2,128)(2,1)} %final_sum.3.refs_2_), custom_call_target="tpu_custom_call", output_to_operand_aliasing={{}: (3, {})} | custom-call | flops 1 | bytes 1 | tf_op jit(solution)/shard_map/final_sum/pallas_call | solution.py:252
  87.2 2.8 %final_sum.5 = bf16[2048,2,256]{2,1,0:T(2,128)(2,1)} custom-call(s32[2]{0:T(128)S(1)} %pad_add_fusion.2.order_ref, bf16[512,512]{1,0:T(8,128)(2,1)S(1)} %collective-permute-done.13.refs_0_, f32[2048,512]{1,0:T(8,128)} %short_range.1.refs_2_.refs_1_, bf16[2048,2,256]{2,1,0:T(2,128)(2,1)} %final_sum.4.refs_2_), custom_call_target="tpu_custom_call", output_to_operand_aliasing={{}: (3, {})} | custom-call | flops 1 | bytes 1 | tf_op jit(solution)/shard_map/final_sum/pallas_call | solution.py:252
  (50 shorter events, 7.5 us)
Async XLA Ops:
  0.0 11.7 %copy-start.3 = (bf16[16,128,128]{2,1,0:T(8,128)(2,1)S(1)}, bf16[16,128,128]{2,1,0:T(8,128)(2,1)}, u32[]{:S(2)}) copy-start(bf16[16,128,128]{2,1,0:T(8,128)(2,1)} %param.18) | copy-start | bytes 1572868
  0.0 12.1 %copy-start.4 = (s32[16]{0:T(128)S(1)}, s32[16]{0:T(128)}, u32[]{:S(2)}) copy-start(s32[16]{0:T(128)} %param.20) | copy-start | bytes 196
  0.0 12.1 %copy-start.5 = (s32[16]{0:T(128)S(1)}, s32[16]{0:T(128)}, u32[]{:S(2)}) copy-start(s32[16]{0:T(128)} %param.19) | copy-start | bytes 196
  4.0 14.9 %collective-permute-start.3 = (bf16[1024,256]{1,0:T(8,128)(2,1)S(1)}, bf16[1024,256]{1,0:T(8,128)(2,1)S(1)}, u32[]{:S(2)}, u32[]{:S(2)}) collective-permute-start(bf16[1024,256]{1,0:T(8,128)(2,1)S(1)} %bitcast.35), channel_id=1, source_target_pairs={{0,16},{1,17},{2,18},{3,19},{4,20},{5,21},{6,22},{7,23},{8,24},{9,... | collective-permute-start | bytes 1572872 | tf_op jit(solution)/shard_map/ppermute | solution.py:375
  7.0 13.4 %collective-permute-start.2 = (bf16[1024,256]{1,0:T(8,128)(2,1)S(1)}, bf16[1024,256]{1,0:T(8,128)(2,1)S(1)}, u32[]{:S(2)}, u32[]{:S(2)}) collective-permute-start(bf16[1024,256]{1,0:T(8,128)(2,1)S(1)} %bitcast.36), channel_id=1, source_target_pairs={{0,2},{1,3},{2,0},{3,1},{4,6},{5,7},{6,4},{7,5},{8,10},{9,11},{10,... | collective-permute-start | bytes 1572872 | tf_op jit(solution)/shard_map/ppermute | solution.py:375
  8.5 13.5 %collective-permute-start = (bf16[256,1024]{1,0:T(8,128)(2,1)}, bf16[256,1024]{1,0:T(8,128)(2,1)}, u32[]{:S(2)}, u32[]{:S(2)}) collective-permute-start(bf16[256,1024]{1,0:T(8,128)(2,1)} %bitcast.26), channel_id=1, source_target_pairs={{0,8},{1,9},{2,10},{3,11},{4,0},{5,1},{6,2},{7,3},{8,12},{9,13},{1... | collective-permute-start | bytes 1572872 | tf_op jit(solution)/shard_map/ppermute | solution.py:375
  22.0 14.5 %collective-permute-start.4 = (bf16[17,128,128]{2,1,0:T(8,128)(2,1)S(1)}, bf16[17,128,128]{2,1,0:T(8,128)(2,1)}, u32[]{:S(2)}, u32[]{:S(2)}) collective-permute-start(bf16[17,128,128]{2,1,0:T(8,128)(2,1)S(1)} %pad_maximum_fusion.refs_0_), channel_id=1, source_target_pairs={{0,16},{1,17},{2,18},{3,19},{4,20},{5,21},{6,22},{7,23},{8,24},{9,... | collective-permute-start | bytes 1671176 | tf_op jit(solution)/shard_map/ppermute | solution.py:375
  22.6 13.7 %collective-permute-start.1 = (bf16[256,1024]{1,0:T(8,128)(2,1)}, bf16[256,1024]{1,0:T(8,128)(2,1)S(1)}, u32[]{:S(2)}, u32[]{:S(2)}) collective-permute-start(bf16[256,1024]{1,0:T(8,128)(2,1)} %bitcast.26), channel_id=1, source_target_pairs={{0,4},{1,5},{2,6},{3,7},{4,12},{5,13},{6,14},{7,15},{8,0},{9,1},{1... | collective-permute-start | bytes 1572872 | tf_op jit(solution)/shard_map/ppermute | solution.py:375
  24.9 11.6 %collective-permute-start.5 = (bf16[1024,256]{1,0:T(8,128)(2,1)S(1)}, bf16[1024,256]{1,0:T(8,128)(2,1)S(1)}, u32[]{:S(2)}, u32[]{:S(2)}) collective-permute-start(bf16[1024,256]{1,0:T(8,128)(2,1)S(1)} %collective-permute-done.3.refs_5_), channel_id=1, source_target_pairs={{0,2},{1,3},{2,0},{3,1},{4,6},{5,7},{6,4},{7,5},{8,10},{9,11},{10,... | collective-permute-start | bytes 1572872 | tf_op jit(solution)/shard_map/ppermute | solution.py:375
  36.3 4.0 %copy-start.1 = (bf16[256,1024]{1,0:T(8,128)(2,1)}, bf16[256,1024]{1,0:T(8,128)(2,1)S(1)}, u32[]{:S(2)}) copy-start(bf16[256,1024]{1,0:T(8,128)(2,1)S(1)} %collective-permute-done.1) | copy-start | bytes 1572868
  37.4 12.1 %collective-permute-start.6 = (bf16[256,1024]{1,0:T(8,128)(2,1)}, bf16[256,1024]{1,0:T(8,128)(2,1)}, u32[]{:S(2)}, u32[]{:S(2)}) collective-permute-start(bf16[256,1024]{1,0:T(8,128)(2,1)} %collective-permute-done), channel_id=1, source_target_pairs={{0,8},{1,9},{2,10},{3,11},{4,0},{5,1},{6,2},{7,3},{8,12},{9,13},{1... | collective-permute-start | bytes 1572872 | tf_op jit(solution)/shard_map/ppermute | solution.py:375
  40.3 13.1 %collective-permute-start.8 = (bf16[256,1024]{1,0:T(8,128)(2,1)}, bf16[256,1024]{1,0:T(8,128)(2,1)}, u32[]{:S(2)}, u32[]{:S(2)}) collective-permute-start(bf16[256,1024]{1,0:T(8,128)(2,1)} %select_select_fusion.3), channel_id=1, source_target_pairs={{0,16},{1,17},{2,18},{3,19},{4,20},{5,21},{6,22},{7,23},{8,24},{9,... | collective-permute-start | bytes 1572872 | tf_op jit(solution)/shard_map/ppermute | solution.py:375
  41.7 7.9 %copy-start.2 = (bf16[256,1024]{1,0:T(8,128)(2,1)S(1)}, bf16[256,1024]{1,0:T(8,128)(2,1)}, u32[]{:S(2)}) copy-start(bf16[256,1024]{1,0:T(8,128)(2,1)} %copy-done.1) | copy-start | bytes 1572868
  43.0 12.5 %collective-permute-start.9 = (bf16[256,1024]{1,0:T(8,128)(2,1)S(1)}, bf16[256,1024]{1,0:T(8,128)(2,1)}, u32[]{:S(2)}, u32[]{:S(2)}) collective-permute-start(bf16[256,1024]{1,0:T(8,128)(2,1)S(1)} %select_select_fusion.refs_0_), channel_id=1, source_target_pairs={{0,1},{1,0},{2,3},{3,2},{4,5},{5,4},{6,7},{7,6},{8,9},{9,8},{10,11... | collective-permute-start | bytes 1572872 | tf_op jit(solution)/shard_map/ppermute | solution.py:375
  51.4 11.4 %collective-permute-start.7 = (bf16[256,1024]{1,0:T(8,128)(2,1)}, bf16[256,1024]{1,0:T(8,128)(2,1)}, u32[]{:S(2)}, u32[]{:S(2)}) collective-permute-start(bf16[256,1024]{1,0:T(8,128)(2,1)} %select_select_fusion.2), channel_id=1, source_target_pairs={{0,16},{1,17},{2,18},{3,19},{4,20},{5,21},{6,22},{7,23},{8,24},{9,... | collective-permute-start | bytes 1572872 | tf_op jit(solution)/shard_map/ppermute | solution.py:375
  53.4 2.3 %collective-permute-start.10 = (bf16[256,1024]{1,0:T(8,128)(2,1)}, bf16[256,1024]{1,0:T(8,128)(2,1)}, u32[]{:S(2)}, u32[]{:S(2)}) collective-permute-start(bf16[256,1024]{1,0:T(8,128)(2,1)} %collective-permute-done.8.refs_1_), channel_id=1, source_target_pairs={{0,1},{1,0},{2,3},{3,2},{4,5},{5,4},{6,7},{7,6},{8,9},{9,8},{10,11... | collective-permute-start | bytes 1572872 | tf_op jit(solution)/shard_map/ppermute | solution.py:375
  54.9 8.7 %copy-start.6 = (f32[125]{0:T(128)S(1)}, f32[125]{0:T(128)}, u32[]{:S(2)}) copy-start(f32[125]{0:T(128)} %param.16) | copy-start | bytes 1504
  54.9 8.7 %copy-start.7 = (f32[125]{0:T(128)S(1)}, f32[125]{0:T(128)}, u32[]{:S(2)}) copy-start(f32[125]{0:T(128)} %param.17) | copy-start | bytes 1504
  55.0 8.8 %collective-permute-start.11 = (bf16[256,1024]{1,0:T(8,128)(2,1)S(1)}, bf16[256,1024]{1,0:T(8,128)(2,1)S(1)}, u32[]{:S(2)}, u32[]{:S(2)}) collective-permute-start(bf16[256,1024]{1,0:T(8,128)(2,1)S(1)} %select_select_fusion.1.refs_0_), channel_id=1, source_target_pairs={{0,1},{1,0},{2,3},{3,2},{4,5},{5,4},{6,7},{7,6},{8,9},{9,8},{10,11... | collective-permute-start | bytes 1572872 | tf_op jit(solution)/shard_map/ppermute | solution.py:375
  60.2 20.1 %collective-permute-start.14 = (bf16[512,512]{1,0:T(8,128)(2,1)}, bf16[512,512]{1,0:T(8,128)(2,1)S(1)}, u32[]{:S(2)}, u32[]{:S(2)}) collective-permute-start(bf16[512,512]{1,0:T(8,128)(2,1)} %get-tuple-element.41), channel_id=1, source_target_pairs={{0,2},{1,3},{2,0},{3,1},{4,6},{5,7},{6,4},{7,5},{8,10},{9,11},{10,... | collective-permute-start | bytes 1572872 | tf_op jit(solution)/shard_map/ppermute | solution.py:375
  63.5 2.1 %collective-permute-start.12 = (bf16[256,1024]{1,0:T(8,128)(2,1)}, bf16[256,1024]{1,0:T(8,128)(2,1)S(1)}, u32[]{:S(2)}, u32[]{:S(2)}) collective-permute-start(bf16[256,1024]{1,0:T(8,128)(2,1)} %collective-permute-done.7.refs_1_), channel_id=1, source_target_pairs={{0,1},{1,0},{2,3},{3,2},{4,5},{5,4},{6,7},{7,6},{8,9},{9,8},{10,11... | collective-permute-start | bytes 1572872 | tf_op jit(solution)/shard_map/ppermute | solution.py:375
  63.8 6.8 %copy-start = (f32[4096]{0:T(1024)S(1)}, f32[4096]{0:T(1024)}, u32[]{:S(2)}) copy-start(f32[4096]{0:T(1024)} %param.15) | copy-start | bytes 49156
  69.9 17.2 %collective-permute-start.13 = (bf16[512,512]{1,0:T(8,128)(2,1)}, bf16[512,512]{1,0:T(8,128)(2,1)S(1)}, u32[]{:S(2)}, u32[]{:S(2)}) collective-permute-start(bf16[512,512]{1,0:T(8,128)(2,1)} %get-tuple-element.43), channel_id=1, source_target_pairs={{0,2},{1,3},{2,0},{3,1},{4,6},{5,7},{6,4},{7,5},{8,10},{9,11},{10,... | collective-permute-start | bytes 1572872 | tf_op jit(solution)/shard_map/ppermute | solution.py:375

commit v11 on v9

--- a/solution.py
+++ b/solution.py
@@ -149,14 +149,14 @@
     )(half, live, sub_ids, meta, in_hbm(aux_basis), aux_decay.reshape(1, -1), *items)
 
 
-def long_kernel(*refs, blocks, chains, pieces, window):
+def long_kernel(*refs, blocks, chains, pieces):
     parts = refs[: blocks * chains]
     factors = refs[blocks * chains : (blocks + pieces) * chains]
     outs, scratch = refs[(blocks + pieces) * chains :][:pieces], refs[-pieces - 2 :]
     right, made, out_sem = scratch[0], scratch[1:-1], scratch[-1]
     depth, width = factors[0].shape
     half = depth // 2
-    count = window[-1]
+    count = parts[0].shape[0]
     copies = []
     for piece in reversed(range(pieces)):
         for chain in range(chains):
@@ -167,11 +167,7 @@
             right[top + half : top + depth, width:] = -factor[0:half, :]
         for block in range(blocks):
             left = jnp.concatenate(
-                [
-                    parts[block * chains + chain][pl.ds(window[chain], count), :]
-                    for chain in range(chains)
-                ],
-                axis=1,
+                [parts[block * chains + chain][...] for chain in range(chains)], axis=1
             )
             total = jnp.dot(left, right[...], preferred_element_type=jnp.float32)
             made[piece][block] = total.astype(outs[piece].dtype)
@@ -184,18 +180,16 @@
         copy.wait()
 
 
-def long_range(blocks, factors, window):
+def long_range(blocks, factors):
     depth, width = factors[0][0].shape
     chains = len(factors[0])
     pieces = len(factors)
-    count = window[-1]
+    count = blocks[0][0].shape[0]
     shape = (len(blocks) * count, 2 * width)
-    dtypes = [jnp.bfloat16 if piece else jnp.float32 for piece in range(pieces)]
+    dtypes = [jnp.bfloat16] * pieces
     flat = [v for group in [*blocks, *factors] for v in group]
     return pl.pallas_call(
-        functools.partial(
-            long_kernel, blocks=len(blocks), chains=chains, pieces=pieces, window=window
-        ),
+        functools.partial(long_kernel, blocks=len(blocks), chains=chains, pieces=pieces),
         out_shape=[pltpu.HBM(shape, dtype) for dtype in dtypes],
         in_specs=[pl.BlockSpec(memory_space=pltpu.VMEM)] * len(flat),
         out_specs=[pl.BlockSpec(memory_space=pltpu.HBM)] * pieces,
@@ -208,12 +202,71 @@
     )(*flat)
 
 
-def final_kernel(order_ref, *refs, pieces, blocks, rows, aliased, stay):
+def own_kernel(order_ref, *refs, blocks, chains, aliased):
+    parts = refs[: blocks * chains]
+    factors = refs[blocks * chains : (blocks + 1) * chains]
+    short_ref = refs[(blocks + 1) * chains]
+    out_ref, right, terms, made, term_sem, out_sem = refs[(blocks + 1) * chains + 1 + aliased :]
+    rows = terms.shape[1]
+    depth, width = factors[0].shape
+    half = depth // 2
+    windows = [pl.ds(pl.multiple_of(order_ref[n] * rows, rows), rows) for n in range(blocks)]
+    arriving = []
+    for n, window in enumerate(windows):
+        arriving.append(
+            pltpu.make_async_copy(short_ref.at[window, :], terms.at[n], term_sem.at[n])
+        )
+        arriving[-1].start()
+    for chain, factor in enumerate(factors):
+        top = chain * depth
+        right[top : top + depth, 0:width] = factor[...]
+        right[top : top + half, width:] = factor[half:, :]
+        right[top + half : top + depth, width:] = -factor[0:half, :]
+    leaving = []
+    for n, window in enumerate(windows):
+        left = jnp.concatenate([parts[n * chains + chain][...] for chain in range(chains)], axis=1)
+        total = jnp.dot(left, right[...], preferred_element_type=jnp.float32)
+        arriving[n].wait()
+        made[n] = (total + terms[n]).astype(made.dtype).reshape(made.shape[1:])
+        leaving.append(pltpu.make_async_copy(made.at[n], out_ref.at[window], out_sem.at[n]))
+        leaving[-1].start()
+    for copy in leaving:
+        copy.wait()
+
+
+def own_sum(order, blocks, factors, short, earlier):
+    rows, depth = blocks[0][0].shape
+    width = factors[0].shape[1]
+    row_count, columns = short.shape
+    chains = len(factors)
+    count = len(blocks)
+    aliased = earlier is not None
+    flat = [v for group in [*blocks, factors] for v in group]
+    return pl.pallas_call(
+        functools.partial(own_kernel, blocks=count, chains=chains, aliased=aliased),
+        out_shape=pltpu.HBM((row_count, 2, width), jnp.bfloat16),
+        in_specs=[pl.BlockSpec(memory_space=pltpu.SMEM)]
+        + [pl.BlockSpec(memory_space=pltpu.VMEM)] * len(flat)
+        + [pl.BlockSpec(memory_space=pltpu.HBM)] * (1 + aliased),
+        out_specs=pl.BlockSpec(memory_space=pltpu.HBM),
+        scratch_shapes=[
+            pltpu.VMEM((chains * depth, 2 * width), jnp.bfloat16),
+            pltpu.VMEM((count, rows, columns), jnp.float32),
+            pltpu.VMEM((count, rows, 2, width), jnp.bfloat16),
+            pltpu.SemaphoreType.DMA((count,)),
+            pltpu.SemaphoreType.DMA((count,)),
+        ],
+        input_output_aliases={len(flat) + 2: 0} if aliased else {},
+        compiler_params=pltpu.CompilerParams(vmem_limit_bytes=VMEM_BYTES),
+        cost_estimate=SMALL_COST,
+        name="own_sum",
+    )(order, *flat, in_hbm(short), *([earlier] if aliased else []))
+
+
+def final_kernel(order_ref, *refs, pieces, blocks, aliased):
     short_ref = refs[pieces]
-    out_ref, *scratch = refs[pieces + 1 + aliased :]
-    parts, (terms, made, part_sem, term_sem, out_sem) = scratch[:-5], scratch[-5:]
-    parts = [parts.pop(0) if held else ref for held, ref in zip(stay, refs)]
-    steps = pieces * blocks
+    out_ref, terms, made, term_sem, out_sem = refs[pieces + 1 + aliased :]
+    steps, rows = terms.shape[:2]
     windows = [pl.ds(pl.multiple_of(order_ref[n] * rows, rows), rows) for n in range(steps)]
     arriving = []
     for n, window in enumerate(windows):
@@ -221,19 +274,11 @@
             pltpu.make_async_copy(short_ref.at[window, :], terms.at[n], term_sem.at[n])
         )
         arriving[-1].start()
-        piece = n // blocks
-        if n % blocks == 0 and stay[piece]:
-            part = pltpu.make_async_copy(refs[piece], parts[piece], part_sem.at[piece])
-            part.start()
-            arriving[-1] = (part, arriving[-1])
-        else:
-            arriving[-1] = (arriving[-1],)
     leaving = []
     for n, window in enumerate(windows):
-        for copy in arriving[n]:
-            copy.wait()
+        arriving[n].wait()
         top = n % blocks * rows
-        total = parts[n // blocks][top : top + rows, :].astype(jnp.float32) + terms[n]
+        total = refs[n // blocks][top : top + rows, :].astype(jnp.float32) + terms[n]
         made[n] = total.astype(made.dtype).reshape(made.shape[1:])
         leaving.append(pltpu.make_async_copy(made.at[n], out_ref.at[window], out_sem.at[n]))
         leaving[-1].start()
@@ -247,35 +292,24 @@
     count = len(pieces)
     blocks = pieces[0].shape[0] // rows
     steps = count * blocks
-    aliased = earlier is not None
-    stay = [piece.dtype == jnp.float32 for piece in pieces]
     return pl.pallas_call(
-        functools.partial(
-            final_kernel, pieces=count, blocks=blocks, rows=rows, aliased=aliased, stay=stay
-        ),
+        functools.partial(final_kernel, pieces=count, blocks=blocks, aliased=True),
         out_shape=pltpu.HBM((row_count, 2, columns // 2), jnp.bfloat16),
         in_specs=[pl.BlockSpec(memory_space=pltpu.SMEM)]
-        + [pl.BlockSpec(memory_space=pltpu.HBM if held else pltpu.VMEM) for held in stay]
-        + [pl.BlockSpec(memory_space=pltpu.HBM)] * (1 + aliased),
+        + [pl.BlockSpec(memory_space=pltpu.VMEM)] * count
+        + [pl.BlockSpec(memory_space=pltpu.HBM)] * 2,
         out_specs=pl.BlockSpec(memory_space=pltpu.HBM),
-        scratch_shapes=[pltpu.VMEM(piece.shape, piece.dtype) for piece, held in zip(pieces, stay) if held]
-        + [
+        scratch_shapes=[
             pltpu.VMEM((steps, rows, columns), jnp.float32),
             pltpu.VMEM((steps, rows, 2, columns // 2), jnp.bfloat16),
-            pltpu.SemaphoreType.DMA((count,)),
             pltpu.SemaphoreType.DMA((steps,)),
             pltpu.SemaphoreType.DMA((steps,)),
         ],
-        input_output_aliases={count + 2: 0} if aliased else {},
+        input_output_aliases={count + 2: 0},
         compiler_params=pltpu.CompilerParams(vmem_limit_bytes=VMEM_BYTES),
         cost_estimate=SMALL_COST,
         name="final_sum",
-    )(
-        order,
-        *(in_hbm(piece) if held else piece for piece, held in zip(pieces, stay)),
-        in_hbm(short),
-        *([earlier] if aliased else []),
-    )
+    )(order, *pieces, in_hbm(short), earlier)
 
 
 def slot_table(image_dist, image_phase, images):
@@ -400,13 +434,13 @@
             for z in range(length)
         )
 
-    def pick(other, n, window, *earlier):
+    def pick(other, n, *earlier):
         wanted = here(lambda g, z: hops_of(g ^ other, z)[n])
         possible = sorted({hops_of(g, z)[n] for g in range(group_count) for z in range(length)})
         blocks = lax.optimization_barrier((*(held[k] for k in possible), *earlier))
-        value = blocks[len(possible) - 1][window]
+        value = blocks[len(possible) - 1]
         for k, block in reversed(list(zip(possible[:-1], blocks))):
-            value = jnp.where(wanted == k, block[window], value)
+            value = jnp.where(wanted == k, block, value)
         return value
 
     def numbers_of(n, s):
@@ -421,83 +455,66 @@
 
     held = {0: aux_flat, 1: along(aux_flat, 1), length - 1: along(aux_flat, -1)}
     packed = jnp.concatenate([item_rows, slot_block(slots, item_rows)], axis=0)
-    items_x = to_plane(packed)
     turned_x = to_plane(turned)
     factors = [[turned, turned_x]] + [[over_y(turned, s)] for s in range(1, breadth)]
-    parts = 2 if rows % 32 == 0 else 1
-    units = [(n, 0, rows) for n in range(home - 1)]
-    units += [(home - 1, k * (rows // parts), rows // parts) for k in range(parts)]
+    items_x = to_plane(packed)
     mine = {}
     theirs = []
     crossed = []
     away = []
     arriving = []
-    own = []
-
-    def multiply(i, *earlier):
-        n, first, count = units[i]
-        blocks = list(zip(mine[n], [after(crossed[i][0], *earlier), *crossed[i][1:]]))
-        made = long_range(blocks, factors, (first, 0, count))
-        own.append(made[0])
-        away.append(made[1:])
-        arriving.append([over_y(v, s) for s, v in enumerate(made[1:], 1)])
-
-    def foreign(i, *earlier):
-        n, first, count = units[i]
-        theirs.append(pick(True, n, slice(first, first + count), *earlier))
-        return to_plane(theirs[i])
+
+    def blocks_of(i, *earlier):
+        return list(zip(mine[i], [after(crossed[i][0], *earlier), *crossed[i][1:]]))
+
+    def multiply(i):
+        earlier = arriving[i - 1] if i else []
+        away.append(long_range(blocks_of(i, *earlier), factors[1:]) if breadth > 1 else [])
+        arriving.append([over_y(v, s) for s, v in enumerate(away[i], 1)])
+
+    def shorts(*earlier):
+        slots_x = read_slots(after(items_x, *earlier), slots)
+        seen, sub_ids, live = jnp.concatenate([slots, slots_x], axis=1)
+        table = slot_table(image_dist, image_phase, seen)
+        all_items = [packed, items_x]
+        return short_range(
+            half, live, sub_ids, table, aux_basis, aux_decay, all_items, row_count, subs
+        )
+
+    def foreign(n, *earlier):
+        theirs.append(pick(True, n, *earlier))
+        return to_plane(theirs[n])
 
     moved = foreign(0)
-    begun = [items_x, turned_x, *(pair[0] for pair in factors[1:]), held[1], held[length - 1]]
-    begun = [theirs[0], *begun]
+    begun = [turned_x, items_x, *(pair[0] for pair in factors[1:])]
     for k in range(2, length // 2 + 1):
-        held[k] = along(after(held[k - 1], *begun), 1)
+        held[k] = along(after(held[k - 1], held[1], held[length - 1]), 1)
     for k in range(2, (length + 1) // 2):
-        held[length - k] = along(after(held[length - k + 1], *begun), -1)
+        held[length - k] = along(after(held[length - k + 1], held[1], held[length - 1]), -1)
     for s in range(1, breadth):
-        factors[s].append(over_y(after(turned_x, *begun), s))
-    seen, sub_ids, live = jnp.concatenate([slots, read_slots(after(items_x, *begun), slots)], axis=1)
-    table = slot_table(image_dist, image_phase, seen)
-    short = short_range(
-        half, live, sub_ids, table, aux_basis, aux_decay, [packed, items_x], row_count, subs
-    )
-    for i, (n, first, count) in enumerate(units):
-        if i:
-            moved = foreign(i, theirs[i - 1], *(away[i - 2] if i > 1 else [short]))
-        if n not in mine:
-            mine[n] = with_cores(pick(False, n, slice(None), theirs[i]))
-        if i:
-            multiply(i - 1)
-        crossed.append(with_cores(after(moved, *away[i - 1] if i else [short])))
-    last = len(units) - 1
-
-    def place_of(piece, i, s):
-        n, first, count = units[i]
-        return piece, [v * (rows // count) + first // count for v in numbers_of(n, s)]
-
-    calls = []
-    for i, (_, _, count) in enumerate(units[:-1]):
-        entries = [place_of(v, i, s) for s, v in enumerate([own[i], *arriving[i]])]
-        if calls and calls[-1][0] == count:
-            calls[-1][1].extend(entries)
-        else:
-            calls.append((count, entries))
-
-    def add_up(out, count, entries):
-        numbers = jnp.stack([v for _, each in entries for v in each]).astype(jnp.int32)
-        return final_sum(numbers, [piece for piece, _ in entries], short, out, count)
-
-    out = add_up(None, *calls.pop(0)) if calls else None
+        factors[s].append(over_y(after(turned_x, theirs[0], *begun), s))
+    short = shorts(theirs[0], *begun)
+
+    for n in range(home):
+        if n:
+            moved = foreign(n, theirs[n - 1], *(away[n - 2] if n > 1 else [short]))
+        mine[n] = with_cores(pick(False, n, theirs[n], *begun))
+        if n:
+            multiply(n - 1)
+        crossed.append(with_cores(after(moved, *away[n - 1] if n else [short])))
+    last = home - 1
     multiply(last)
-    count = units[last][2]
-    calls.append((count, [place_of(own[last], last, 0)]))
-    if len(calls) > 1 and calls[-2][0] == count:
-        entries = calls.pop()[1]
-        calls[-1][1].extend(entries)
-    if breadth > 1:
-        calls.append((count, [place_of(v, last, s) for s, v in enumerate(arriving[last], 1)]))
-    for call in calls:
-        out = add_up(out, *call)
+
+    def order_of(n, places):
+        return jnp.stack([v for s in places for v in numbers_of(n, s)]).astype(jnp.int32)
+
+    out = None
+    for n in range(home):
+        blocks = blocks_of(n, *away[last])
+        out = own_sum(order_of(n, [0]), blocks, factors[0], short, out)
+    for n in range(home):
+        if breadth > 1:
+            out = final_sum(order_of(n, range(1, breadth)), arriving[n], short, out, rows)
     return out
 
 

time: 89.7 us -> 93.9 us (1.047)
  Pallas kernels: 26 us -> 32.4 us
  local copies, waits for them, and re-layouts: 2.95 us -> 6.58 us
  starting transfers between devices: 19.6 us -> 16.3 us
  other arithmetic: 7.45 us -> 5.34 us
    pallas_call x0 -> x2, Pallas kernels: none -> 9.22 us  [own_sum(): pl.pallas_call(functools.partial(own_kernel, blocks=count, chains=chains,...]
    unnamed x14 -> x42, local copies, waits for them, and re-layouts: 2.27 us -> 5.99 us
    pallas_call x3 -> x2, Pallas kernels: 9.57 us -> 5.99 us  [final_sum(): pl.pallas_call(functools.partial(final_kernel, pieces=count, blocks=block...]
    ppermute x18 -> x15, starting transfers between devices: 19.6 us -> 16.3 us  [send(): return lax.ppermute(value, AXES, pairs)]
    select_n x5 -> x4, other arithmetic: 5.48 us -> 3.58 us  [pick(): value = jnp.where(wanted == k, block, value)]
    pallas_call x1, Pallas kernels: 9.22 us -> 10.5 us  [short_range(): pl.pallas_call(kernel, out_shape=pltpu.HBM((row_count, 2 * subs * width),...]
    convert_element_type x1, other arithmetic: 1.45 us -> 0.41 us  [body(): weighted = (pairs * coul_weight[None, None, :]).astype(jnp.bfloat16)]
    ppermute x18 -> x15, waiting for transfers between devices: 32.5 us -> 32 us  [send(): return lax.ppermute(value, AXES, pairs)]
  transfers between devices with their start and end apart: 18 -> 15, of which waited for: 9 -> 5; matrix products, arithmetic and copies ran while one was open for 9% -> 8% of each run, Pallas kernels for 26% -> 27%
where the time goes in v11:
time: 93.9 us; the launch traced here: 93.6 us
  Pallas kernels  32.4 us (35%)
  waiting for transfers between devices  32 us (34%)
  starting transfers between devices  16.3 us (17%)
  local copies, waits for them, and re-layouts  6.58 us (7%)
  other arithmetic  5.34 us (6%)
  between operations  0.96 us (1%)
    ppermute x15, waiting for transfers between devices, send(): return lax.ppermute(value, AXES, pairs)  32 us
    ppermute x15, starting transfers between devices, send(): return lax.ppermute(value, AXES, pairs)  16.3 us
    pallas_call x1, Pallas kernels, short_range(): pl.pallas_call(kernel, out_shape=pltpu.HBM((row_count, 2 * subs * width),...  10.5 us
    pallas_call x2, Pallas kernels, own_sum(): pl.pallas_call(functools.partial(own_kernel, blocks=count, chains=chains,...  9.22 us
    pallas_call x2, Pallas kernels, long_range(): pl.pallas_call(functools.partial(long_kernel, blocks=len(blocks), chains=...  6.71 us
    pallas_call x2, Pallas kernels, final_sum(): pl.pallas_call(functools.partial(final_kernel, pieces=count, blocks=block...  5.99 us
    unnamed x42, local copies, waits for them, and re-layouts  5.99 us
    select_n x4, other arithmetic, pick(): value = jnp.where(wanted == k, block, value)  3.58 us
  transfers between devices with their start and end apart: 15, of which 5 were waited for; matrix products, arithmetic and copies ran while one was open for 8% of the time, Pallas kernels for 27%

profile of v11, /device:TPU:0, one launch (start us, length us, event | category | flops | bytes accessed | tf_op | source)
XLA Modules:
  0.0 93.6 jit_solution(15308786361355549359)
XLA Ops:
  0.0 2.0 %copy.19 = bf16[32,8,2,512]{3,1,2,0:T(8,128)(2,1)} copy(bf16[32,8,2,512]{3,2,1,0:T(2,128)(2,1)} %bitcast.41) | data formatting | bytes 1048576
  2.0 3.0 %collective-permute-start.1 = (bf16[256,1024]{1,0:T(8,128)(2,1)}, bf16[256,1024]{1,0:T(8,128)(2,1)S(1)}, u32[]{:S(2)}, u32[]{:S(2)}) collective-permute-start(bf16[256,1024]{1,0:T(8,128)(2,1)} %bitcast.26), channel_id=1, source_target_pairs={{0,4},{1,5},{2,6},{3,7},{4,12},{5,13},{6,14},{7,15},{8,0},{9,1},{1... | collective-permute-start | bytes 1572872 | tf_op jit(solution)/shard_map/ppermute | solution.py:409
  6.7 1.3 %copy.17 = bf16[16,128,128]{1,2,0:T(8,128)(2,1)S(1)} copy(bf16[16,128,128]{2,1,0:T(8,128)(2,1)} %param.18) | data formatting | bytes 1048576 | tf_op args[7]
  8.2 1.9 %collective-permute-start.3 = (bf16[17,128,128]{2,1,0:T(8,128)(2,1)S(1)}, bf16[17,128,128]{2,1,0:T(8,128)(2,1)}, u32[]{:S(2)}, u32[]{:S(2)}) collective-permute-start(bf16[17,128,128]{2,1,0:T(8,128)(2,1)S(1)} %pad_maximum_fusion.refs_0_), channel_id=1, source_target_pairs={{0,16},{1,17},{2,18},{3,19},{4,20},{5,21},{6,22},{7,23},{8,24},{9,... | collective-permute-start | bytes 1671176 | tf_op jit(solution)/shard_map/ppermute | solution.py:409
  11.0 1.6 %collective-permute-start.5 = (bf16[1024,256]{1,0:T(8,128)(2,1)S(1)}, bf16[1024,256]{1,0:T(8,128)(2,1)S(1)}, u32[]{:S(2)}, u32[]{:S(2)}) collective-permute-start(bf16[1024,256]{1,0:T(8,128)(2,1)S(1)} %bitcast.35), channel_id=1, source_target_pairs={{0,2},{1,3},{2,0},{3,1},{4,6},{5,7},{6,4},{7,5},{8,10},{9,11},{10,... | collective-permute-start | bytes 1572872 | tf_op jit(solution)/shard_map/ppermute | solution.py:409
  13.2 5.1 %collective-permute-done.1 = bf16[256,1024]{1,0:T(8,128)(2,1)S(1)} collective-permute-done((bf16[256,1024]{1,0:T(8,128)(2,1)}, bf16[256,1024]{1,0:T(8,128)(2,1)S(1)}, u32[]{:S(2)}, u32[]{:S(2)}) %collective-permute-start.1) | collective-permute-done | bytes 524320 | tf_op jit(solution)/shard_map/ppermute | solution.py:409
  18.3 11.2 %collective-permute-done = bf16[256,1024]{1,0:T(8,128)(2,1)} collective-permute-done((bf16[256,1024]{1,0:T(8,128)(2,1)}, bf16[256,1024]{1,0:T(8,128)(2,1)}, u32[]{:S(2)}, u32[]{:S(2)}) %collective-permute-start) | collective-permute-done | bytes 524320 | tf_op jit(solution)/shard_map/ppermute | solution.py:409
  29.6 2.6 %collective-permute-start.7 = (bf16[256,1024]{1,0:T(8,128)(2,1)S(1)}, bf16[256,1024]{1,0:T(8,128)(2,1)S(1)}, u32[]{:S(2)}, u32[]{:S(2)}) collective-permute-start(bf16[256,1024]{1,0:T(8,128)(2,1)S(1)} %select_select_fusion.3), channel_id=1, source_target_pairs={{0,16},{1,17},{2,18},{3,19},{4,20},{5,21},{6,22},{7,23},{8,24},{9,... | collective-permute-start | bytes 1572872 | tf_op jit(solution)/shard_map/ppermute | solution.py:409
  32.3 1.7 %collective-permute-start.2 = (bf16[256,1024]{1,0:T(8,128)(2,1)}, bf16[256,1024]{1,0:T(8,128)(2,1)S(1)}, u32[]{:S(2)}, u32[]{:S(2)}) collective-permute-start(bf16[256,1024]{1,0:T(8,128)(2,1)} %collective-permute-done), channel_id=1, source_target_pairs={{0,8},{1,9},{2,10},{3,11},{4,0},{5,1},{6,2},{7,3},{8,12},{9,13},{1... | collective-permute-start | bytes 1572872 | tf_op jit(solution)/shard_map/ppermute | solution.py:409
  35.7 1.3 %select_select_fusion.refs_0_ = bf16[256,1024]{1,0:T(8,128)(2,1)S(1)} fusion(bf16[256,1024]{1,0:T(8,128)(2,1)} %bitcast.26, bf16[256,1024]{1,0:T(8,128)(2,1)} %collective-permute-done, bf16[256,1024]{1,0:T(8,128)(2,1)} %copy-done.11, pred[]{:T(512)S(6)} %eq.74, pred[]{:T(512)S(6)} %eq.73), kind=kLoop, calls=%fused_computation.2 | loop fusion | flops 524288 | bytes 2097154 | tf_op jit(solution)/shard_map/jit(_where)/select_n | solution.py:443
  37.1 1.6 %collective-permute-start.10 = (bf16[1024,256]{1,0:T(8,128)(2,1)S(1)}, bf16[1024,256]{1,0:T(8,128)(2,1)}, u32[]{:S(2)}, u32[]{:S(2)}) collective-permute-start(bf16[1024,256]{1,0:T(8,128)(2,1)S(1)} %collective-permute-done.4.refs_5_), channel_id=1, source_target_pairs={{0,2},{1,3},{2,0},{3,1},{4,6},{5,7},{6,4},{7,5},{8,10},{9,11},{10,... | collective-permute-start | bytes 1572872 | tf_op jit(solution)/shard_map/ppermute | solution.py:409
  38.7 10.5 %short_range.1.refs_6_.refs_1_ = f32[2048,512]{1,0:T(8,128)} custom-call(s32[1]{0:T(128)} %bitcast.2.half_ref, s32[32]{0:T(128)S(1)} %get-tuple-element.51.live_ref, s32[32]{0:T(128)S(1)} %get-tuple-element.50.sub_ref, f32[3,32]{1,0:T(4,128)S(1)} %pad_maximum_fusion.1.meta_ref, bf16[128,4096]{1,0:T(8,128)(2,1)} %basis_ref.1, f32[1,4096]{1,0:T(1,128)S(1)} %bitcast.39, ...), custom_call_target="tpu_custom_call" | custom-call | flops 4294967296 | bytes 1 | tf_op jit(solution)/shard_map/short_range/pallas_call | solution.py:125
  50.4 1.5 %collective-permute-start.6 = (bf16[256,1024]{1,0:T(8,128)(2,1)}, bf16[256,1024]{1,0:T(8,128)(2,1)}, u32[]{:S(2)}, u32[]{:S(2)}) collective-permute-start(bf16[256,1024]{1,0:T(8,128)(2,1)} %select_select_fusion.2), channel_id=1, source_target_pairs={{0,16},{1,17},{2,18},{3,19},{4,20},{5,21},{6,22},{7,23},{8,24},{9,... | collective-permute-start | bytes 1572872 | tf_op jit(solution)/shard_map/ppermute | solution.py:409
  51.9 1.3 %select_select_fusion.1.refs_0_ = bf16[256,1024]{1,0:T(8,128)(2,1)S(1)} fusion(bf16[256,1024]{1,0:T(8,128)(2,1)} %collective-permute-done, bf16[256,1024]{1,0:T(8,128)(2,1)} %copy-done.13, bf16[256,1024]{1,0:T(8,128)(2,1)} %copy-done.11, pred[]{:T(512)S(6)} %eq.72, pred[]{:T(512)S(6)} %eq.63), kind=kLoop, calls=%fused_computation.3 | loop fusion | flops 524288 | bytes 2097154 | tf_op jit(solution)/shard_map/jit(_where)/select_n | solution.py:443
  53.4 1.0 %copy-done.1 = bf16[1024,256]{1,0:T(8,128)(2,1)S(1)} copy-done((bf16[1024,256]{1,0:T(8,128)(2,1)S(1)}, bf16[1024,256]{1,0:T(8,128)(2,1)}, u32[]{:S(2)}) %copy-start.1) | copy-done | bytes 524312
  54.4 3.2 %long_range.2 = bf16[512,512]{1,0:T(8,128)(2,1)} custom-call(bf16[256,1024]{1,0:T(8,128)(2,1)S(1)} %select_select_fusion.refs_0_, bf16[256,1024]{1,0:T(8,128)(2,1)S(1)} %collective-permute-done.7.refs_1_, bf16[256,1024]{1,0:T(8,128)(2,1)S(1)} %collective-permute-done.8.refs_2_, bf16[256,1024]{1,0:T(8,128)(2,1)} %collective-permute-done.9.refs_3_, ...), custom_call_target="tpu_custom_call" | custom-call | flops 1 | bytes 1 | tf_op jit(solution)/shard_map/long_range/pallas_call | solution.py:191
  57.7 7.3 %collective-permute-done.6.refs_1_ = bf16[256,1024]{1,0:T(8,128)(2,1)} collective-permute-done((bf16[256,1024]{1,0:T(8,128)(2,1)}, bf16[256,1024]{1,0:T(8,128)(2,1)}, u32[]{:S(2)}, u32[]{:S(2)}) %collective-permute-start.6) | collective-permute-done | bytes 524320 | tf_op jit(solution)/shard_map/ppermute | solution.py:409
  65.0 7.2 %collective-permute-done.11.refs_0_ = bf16[512,512]{1,0:T(8,128)(2,1)S(1)} collective-permute-done((bf16[512,512]{1,0:T(8,128)(2,1)}, bf16[512,512]{1,0:T(8,128)(2,1)S(1)}, u32[]{:S(2)}, u32[]{:S(2)}) %collective-permute-start.11) | collective-permute-done | bytes 524320 | tf_op jit(solution)/shard_map/ppermute | solution.py:409
  72.9 3.5 %long_range.3 = bf16[512,512]{1,0:T(8,128)(2,1)} custom-call(bf16[256,1024]{1,0:T(8,128)(2,1)S(1)} %select_select_fusion.1.refs_0_, bf16[256,1024]{1,0:T(8,128)(2,1)} %collective-permute-done.6.refs_1_, bf16[256,1024]{1,0:T(8,128)(2,1)S(1)} %collective-permute-done.12.refs_2_, bf16[256,1024]{1,0:T(8,128)(2,1)S(1)} %collective-permute-done.13.refs_3_, ...), custom_call_target="tpu_custom_call" | custom-call | flops 1 | bytes 1 | tf_op jit(solution)/shard_map/long_range/pallas_call | solution.py:191
  77.1 4.6 %own_sum.2.refs_7_ = bf16[2048,2,256]{2,1,0:T(2,128)(2,1)} custom-call(s32[2]{0:T(128)S(1)} %pad_add_fusion.5.order_ref, bf16[256,1024]{1,0:T(8,128)(2,1)S(1)} %select_select_fusion.refs_0_, bf16[256,1024]{1,0:T(8,128)(2,1)S(1)} %collective-permute-done.7.refs_1_, bf16[256,1024]{1,0:T(8,128)(2,1)S(1)} %collective-permute-done.8.refs_2_, ...), custom_call_target="tpu_custom_call" | custom-call | flops 1 | bytes 1 | tf_op jit(solution)/shard_map/own_sum/pallas_call | solution.py:245
  81.8 4.6 %own_sum.3.refs_2_ = bf16[2048,2,256]{2,1,0:T(2,128)(2,1)} custom-call(s32[2]{0:T(128)S(1)} %pad_add_fusion.4.order_ref, bf16[256,1024]{1,0:T(8,128)(2,1)S(1)} %select_select_fusion.1.refs_0_, bf16[256,1024]{1,0:T(8,128)(2,1)} %collective-permute-done.6.refs_1_, bf16[256,1024]{1,0:T(8,128)(2,1)S(1)} %copy-done.3, ...), custom_call_target="tpu_custom_call", output_to_operand_aliasing={{}: (8, {})} | custom-call | flops 1 | bytes 1 | tf_op jit(solution)/shard_map/own_sum/pallas_call | solution.py:245
  86.4 2.7 %final_sum.2.refs_2_ = bf16[2048,2,256]{2,1,0:T(2,128)(2,1)} custom-call(s32[2]{0:T(128)S(1)} %pad_add_fusion.3.order_ref, bf16[512,512]{1,0:T(8,128)(2,1)S(1)} %copy-done.9, f32[2048,512]{1,0:T(8,128)} %short_range.1.refs_6_.refs_1_, bf16[2048,2,256]{2,1,0:T(2,128)(2,1)} %own_sum.3.refs_2_), custom_call_target="tpu_custom_call", output_to_operand_aliasing={{}: (3, {})} | custom-call | flops 1 | bytes 1 | tf_op jit(solution)/shard_map/final_sum/pallas_call | solution.py:295
  89.2 1.2 %collective-permute-done.14.refs_0_ = bf16[512,512]{1,0:T(8,128)(2,1)} collective-permute-done((bf16[512,512]{1,0:T(8,128)(2,1)}, bf16[512,512]{1,0:T(8,128)(2,1)}, u32[]{:S(2)}, u32[]{:S(2)}) %collective-permute-start.14) | collective-permute-done | bytes 524320 | tf_op jit(solution)/shard_map/ppermute | solution.py:409
  90.4 3.2 %final_sum.3 = bf16[2048,2,256]{2,1,0:T(2,128)(2,1)} custom-call(s32[2]{0:T(128)S(1)} %pad_add_fusion.2.order_ref, bf16[512,512]{1,0:T(8,128)(2,1)} %collective-permute-done.14.refs_0_, f32[2048,512]{1,0:T(8,128)} %short_range.1.refs_6_.refs_1_, bf16[2048,2,256]{2,1,0:T(2,128)(2,1)} %final_sum.2.refs_2_), custom_call_target="tpu_custom_call", output_to_operand_aliasing={{}: (3, {})} | custom-call | flops 1 | bytes 1 | tf_op jit(solution)/shard_map/final_sum/pallas_call | solution.py:295
  (76 shorter events, 7.4 us)
Async XLA Ops:
  0.0 8.0 %copy-start.17 = (s32[16]{0:T(128)S(1)}, s32[16]{0:T(128)}, u32[]{:S(2)}) copy-start(s32[16]{0:T(128)} %param.19) | copy-start | bytes 196
  0.0 10.1 %copy-start.14 = (bf16[256,2,512]{2,1,0:T(2,128)(2,1)S(1)}, bf16[256,2,512]{2,1,0:T(2,128)(2,1)}, u32[]{:S(2)}) copy-start(bf16[256,2,512]{2,1,0:T(2,128)(2,1)} %param.11) | copy-start | bytes 1572868
  0.0 10.1 %copy-start.15 = (f32[512]{0:T(512)S(1)}, f32[512]{0:T(512)}, u32[]{:S(2)}) copy-start(f32[512]{0:T(512)} %param.13) | copy-start | bytes 6148
  2.0 16.3 %collective-permute-start.1 = (bf16[256,1024]{1,0:T(8,128)(2,1)}, bf16[256,1024]{1,0:T(8,128)(2,1)S(1)}, u32[]{:S(2)}, u32[]{:S(2)}) collective-permute-start(bf16[256,1024]{1,0:T(8,128)(2,1)} %bitcast.26), channel_id=1, source_target_pairs={{0,4},{1,5},{2,6},{3,7},{4,12},{5,13},{6,14},{7,15},{8,0},{9,1},{1... | collective-permute-start | bytes 1572872 | tf_op jit(solution)/shard_map/ppermute | solution.py:409
  5.0 24.5 %collective-permute-start = (bf16[256,1024]{1,0:T(8,128)(2,1)}, bf16[256,1024]{1,0:T(8,128)(2,1)}, u32[]{:S(2)}, u32[]{:S(2)}) collective-permute-start(bf16[256,1024]{1,0:T(8,128)(2,1)} %bitcast.26), channel_id=1, source_target_pairs={{0,8},{1,9},{2,10},{3,11},{4,0},{5,1},{6,2},{7,3},{8,12},{9,13},{1... | collective-permute-start | bytes 1572872 | tf_op jit(solution)/shard_map/ppermute | solution.py:409
  8.2 21.4 %copy-start.6 = (bf16[17,128,128]{2,1,0:T(8,128)(2,1)}, bf16[17,128,128]{2,1,0:T(8,128)(2,1)S(1)}, u32[]{:S(2)}) copy-start(bf16[17,128,128]{2,1,0:T(8,128)(2,1)S(1)} %pad_maximum_fusion.refs_0_) | copy-start | bytes 1671172
  8.2 27.3 %copy-start.18 = (f32[125]{0:T(128)S(1)}, f32[125]{0:T(128)}, u32[]{:S(2)}) copy-start(f32[125]{0:T(128)} %param.16) | copy-start | bytes 1504
  8.2 27.3 %copy-start.19 = (f32[125]{0:T(128)S(1)}, f32[125]{0:T(128)}, u32[]{:S(2)}) copy-start(f32[125]{0:T(128)} %param.17) | copy-start | bytes 1504
  8.2 26.5 %collective-permute-start.3 = (bf16[17,128,128]{2,1,0:T(8,128)(2,1)S(1)}, bf16[17,128,128]{2,1,0:T(8,128)(2,1)}, u32[]{:S(2)}, u32[]{:S(2)}) collective-permute-start(bf16[17,128,128]{2,1,0:T(8,128)(2,1)S(1)} %pad_maximum_fusion.refs_0_), channel_id=1, source_target_pairs={{0,16},{1,17},{2,18},{3,19},{4,20},{5,21},{6,22},{7,23},{8,24},{9,... | collective-permute-start | bytes 1671176 | tf_op jit(solution)/shard_map/ppermute | solution.py:409
  11.0 22.9 %collective-permute-start.5 = (bf16[1024,256]{1,0:T(8,128)(2,1)S(1)}, bf16[1024,256]{1,0:T(8,128)(2,1)S(1)}, u32[]{:S(2)}, u32[]{:S(2)}) collective-permute-start(bf16[1024,256]{1,0:T(8,128)(2,1)S(1)} %bitcast.35), channel_id=1, source_target_pairs={{0,2},{1,3},{2,0},{3,1},{4,6},{5,7},{6,4},{7,5},{8,10},{9,11},{10,... | collective-permute-start | bytes 1572872 | tf_op jit(solution)/shard_map/ppermute | solution.py:409
  12.6 22.1 %collective-permute-start.4 = (bf16[1024,256]{1,0:T(8,128)(2,1)S(1)}, bf16[1024,256]{1,0:T(8,128)(2,1)S(1)}, u32[]{:S(2)}, u32[]{:S(2)}) collective-permute-start(bf16[1024,256]{1,0:T(8,128)(2,1)S(1)} %bitcast.36), channel_id=1, source_target_pairs={{0,16},{1,17},{2,18},{3,19},{4,20},{5,21},{6,22},{7,23},{8,24},{9,... | collective-permute-start | bytes 1572872 | tf_op jit(solution)/shard_map/ppermute | solution.py:409
  13.2 25.5 %copy-start.10 = (f32[4096]{0:T(1024)S(1)}, f32[4096]{0:T(1024)}, u32[]{:S(2)}) copy-start(f32[4096]{0:T(1024)} %param.15) | copy-start | bytes 49156
  18.3 11.2 %copy-start.11 = (bf16[256,1024]{1,0:T(8,128)(2,1)}, bf16[256,1024]{1,0:T(8,128)(2,1)S(1)}, u32[]{:S(2)}) copy-start(bf16[256,1024]{1,0:T(8,128)(2,1)S(1)} %collective-permute-done.1) | copy-start | bytes 1572868
  29.6 19.6 %collective-permute-start.7 = (bf16[256,1024]{1,0:T(8,128)(2,1)S(1)}, bf16[256,1024]{1,0:T(8,128)(2,1)S(1)}, u32[]{:S(2)}, u32[]{:S(2)}) collective-permute-start(bf16[256,1024]{1,0:T(8,128)(2,1)S(1)} %select_select_fusion.3), channel_id=1, source_target_pairs={{0,16},{1,17},{2,18},{3,19},{4,20},{5,21},{6,22},{7,23},{8,24},{9,... | collective-permute-start | bytes 1572872 | tf_op jit(solution)/shard_map/ppermute | solution.py:409
  32.3 17.0 %collective-permute-start.2 = (bf16[256,1024]{1,0:T(8,128)(2,1)}, bf16[256,1024]{1,0:T(8,128)(2,1)S(1)}, u32[]{:S(2)}, u32[]{:S(2)}) collective-permute-start(bf16[256,1024]{1,0:T(8,128)(2,1)} %collective-permute-done), channel_id=1, source_target_pairs={{0,8},{1,9},{2,10},{3,11},{4,0},{5,1},{6,2},{7,3},{8,12},{9,13},{1... | collective-permute-start | bytes 1572872 | tf_op jit(solution)/shard_map/ppermute | solution.py:409
  37.0 16.3 %collective-permute-start.8 = (bf16[256,1024]{1,0:T(8,128)(2,1)S(1)}, bf16[256,1024]{1,0:T(8,128)(2,1)S(1)}, u32[]{:S(2)}, u32[]{:S(2)}) collective-permute-start(bf16[256,1024]{1,0:T(8,128)(2,1)S(1)} %select_select_fusion.refs_0_), channel_id=1, source_target_pairs={{0,1},{1,0},{2,3},{3,2},{4,5},{5,4},{6,7},{7,6},{8,9},{9,8},{10,11... | collective-permute-start | bytes 1572872 | tf_op jit(solution)/shard_map/ppermute | solution.py:409
  37.1 16.3 %collective-permute-start.10 = (bf16[1024,256]{1,0:T(8,128)(2,1)S(1)}, bf16[1024,256]{1,0:T(8,128)(2,1)}, u32[]{:S(2)}, u32[]{:S(2)}) collective-permute-start(bf16[1024,256]{1,0:T(8,128)(2,1)S(1)} %collective-permute-done.4.refs_5_), channel_id=1, source_target_pairs={{0,2},{1,3},{2,0},{3,1},{4,6},{5,7},{6,4},{7,5},{8,10},{9,11},{10,... | collective-permute-start | bytes 1572872 | tf_op jit(solution)/shard_map/ppermute | solution.py:409
  38.7 10.8 %copy-start.12 = (bf16[256,1024]{1,0:T(8,128)(2,1)S(1)}, bf16[256,1024]{1,0:T(8,128)(2,1)}, u32[]{:S(2)}) copy-start(bf16[256,1024]{1,0:T(8,128)(2,1)} %copy-done.11) | copy-start | bytes 1572868
  49.3 4.1 %collective-permute-start.9 = (bf16[256,1024]{1,0:T(8,128)(2,1)S(1)}, bf16[256,1024]{1,0:T(8,128)(2,1)}, u32[]{:S(2)}, u32[]{:S(2)}) collective-permute-start(bf16[256,1024]{1,0:T(8,128)(2,1)S(1)} %collective-permute-done.7.refs_1_), channel_id=1, source_target_pairs={{0,1},{1,0},{2,3},{3,2},{4,5},{5,4},{6,7},{7,6},{8,9},{9,8},{10,11... | collective-permute-start | bytes 1572872 | tf_op jit(solution)/shard_map/ppermute | solution.py:409
  50.4 14.5 %collective-permute-start.6 = (bf16[256,1024]{1,0:T(8,128)(2,1)}, bf16[256,1024]{1,0:T(8,128)(2,1)}, u32[]{:S(2)}, u32[]{:S(2)}) collective-permute-start(bf16[256,1024]{1,0:T(8,128)(2,1)} %select_select_fusion.2), channel_id=1, source_target_pairs={{0,16},{1,17},{2,18},{3,19},{4,20},{5,21},{6,22},{7,23},{8,24},{9,... | collective-permute-start | bytes 1572872 | tf_op jit(solution)/shard_map/ppermute | solution.py:409
  53.2 19.7 %collective-permute-start.12 = (bf16[256,1024]{1,0:T(8,128)(2,1)S(1)}, bf16[256,1024]{1,0:T(8,128)(2,1)S(1)}, u32[]{:S(2)}, u32[]{:S(2)}) collective-permute-start(bf16[256,1024]{1,0:T(8,128)(2,1)S(1)} %select_select_fusion.1.refs_0_), channel_id=1, source_target_pairs={{0,1},{1,0},{2,3},{3,2},{4,5},{5,4},{6,7},{7,6},{8,9},{9,8},{10,11... | collective-permute-start | bytes 1572872 | tf_op jit(solution)/shard_map/ppermute | solution.py:409
  57.6 14.5 %collective-permute-start.11 = (bf16[512,512]{1,0:T(8,128)(2,1)}, bf16[512,512]{1,0:T(8,128)(2,1)S(1)}, u32[]{:S(2)}, u32[]{:S(2)}) collective-permute-start(bf16[512,512]{1,0:T(8,128)(2,1)} %long_range.2), channel_id=1, source_target_pairs={{0,2},{1,3},{2,0},{3,1},{4,6},{5,7},{6,4},{7,5},{8,10},{9,11},{10,... | collective-permute-start | bytes 1572872 | tf_op jit(solution)/shard_map/ppermute | solution.py:409
  65.0 8.0 %collective-permute-start.13 = (bf16[256,1024]{1,0:T(8,128)(2,1)}, bf16[256,1024]{1,0:T(8,128)(2,1)S(1)}, u32[]{:S(2)}, u32[]{:S(2)}) collective-permute-start(bf16[256,1024]{1,0:T(8,128)(2,1)} %collective-permute-done.6.refs_1_), channel_id=1, source_target_pairs={{0,1},{1,0},{2,3},{3,2},{4,5},{5,4},{6,7},{7,6},{8,9},{9,8},{10,11... | collective-permute-start | bytes 1572872 | tf_op jit(solution)/shard_map/ppermute | solution.py:409
  76.5 13.9 %collective-permute-start.14 = (bf16[512,512]{1,0:T(8,128)(2,1)}, bf16[512,512]{1,0:T(8,128)(2,1)}, u32[]{:S(2)}, u32[]{:S(2)}) collective-permute-start(bf16[512,512]{1,0:T(8,128)(2,1)} %long_range.3), channel_id=1, source_target_pairs={{0,2},{1,3},{2,0},{3,1},{4,6},{5,7},{6,4},{7,5},{8,10},{9,11},{10,... | collective-permute-start | bytes 1572872 | tf_op jit(solution)/shard_map/ppermute | solution.py:409
  (11 other events, 39.4 us)

commit v12 on v10

--- a/solution.py
+++ b/solution.py
@@ -22,8 +22,8 @@
 def short_kernel(
     half_ref, live_ref, sub_ref, meta_ref, basis_ref, decay_ref, *refs, share, subs, depth, width
 ):
-    items, scratch = refs[:-11], refs[-11:]
-    out_ref, basis, basis_f32, left, acc, made, dists, group_sub, cursor, basis_sem, out_sem = scratch
+    items, scratch = refs[:-10], refs[-10:]
+    out_ref, basis, left, acc, made, dists, group_sub, cursor, basis_sem, out_sem = scratch
     slots = share * len(items)
     row_count = out_ref.shape[0]
     mine = pl.ds(pl.multiple_of(half_ref[0] * row_count, row_count), row_count)
@@ -82,15 +82,17 @@
     tile = min(row_count, made.shape[1])
     decay = decay_ref[:, mine]
     basis_copy.wait()
-    basis_f32[...] = basis[...].astype(jnp.float32)
 
     def one_group(group, carry):
         s = group_sub[group]
-        damping = [jnp.exp(decay * -dists[group * GROUP_ITEMS + k]) for k in range(GROUP_ITEMS)]
+        damping = [
+            jnp.exp(decay * -dists[group * GROUP_ITEMS + k]).astype(basis.dtype)
+            for k in range(GROUP_ITEMS)
+        ]
         for t in range(0, row_count, tile):
             right = jnp.concatenate(
                 [
-                    (basis_f32[:, t : t + tile] * damping[k][:, t : t + tile]).astype(jnp.bfloat16)
+                    basis[:, t : t + tile] * damping[k][:, t : t + tile]
                     for k in range(GROUP_ITEMS)
                 ],
                 axis=0,
@@ -131,7 +133,6 @@
         out_specs=pl.BlockSpec(memory_space=pltpu.HBM),
         scratch_shapes=[
             pltpu.VMEM((depth, row_count), jnp.bfloat16),
-            pltpu.VMEM((depth, row_count), jnp.float32),
             pltpu.VMEM((groups, 2 * width, GROUP_ITEMS * depth), jnp.bfloat16),
             pltpu.VMEM((subs, 2 * width, row_count), jnp.float32),
             pltpu.VMEM((row_count // tile, tile, 2 * subs * width), jnp.float32),
@@ -214,11 +215,12 @@
     parts, (terms, made, part_sem, term_sem, out_sem) = scratch[:-5], scratch[-5:]
     parts = [parts.pop(0) if held else ref for held, ref in zip(stay, refs)]
     steps = pieces * blocks
-    windows = [pl.ds(pl.multiple_of(order_ref[n] * rows, rows), rows) for n in range(steps)]
+    windows = [pl.ds(pl.multiple_of(order_ref[n] * rows, rows), rows) for n in range(2 * steps)]
+    windows, sources = windows[:steps], windows[steps:]
     arriving = []
-    for n, window in enumerate(windows):
+    for n, source in enumerate(sources):
         arriving.append(
-            pltpu.make_async_copy(short_ref.at[window, :], terms.at[n], term_sem.at[n])
+            pltpu.make_async_copy(short_ref.at[source, :], terms.at[n], term_sem.at[n])
         )
         arriving[-1].start()
         piece = n // blocks
@@ -241,9 +243,8 @@
         copy.wait()
 
 
-def final_sum(order, pieces, short, earlier, rows):
+def final_sum(order, pieces, short, earlier, rows, row_count):
     columns = pieces[0].shape[1]
-    row_count = short.shape[0]
     count = len(pieces)
     blocks = pieces[0].shape[0] // rows
     steps = count * blocks
@@ -409,12 +410,13 @@
             value = jnp.where(wanted == k, block[window], value)
         return value
 
-    def numbers_of(n, s):
-        slab = here(lambda g, z: ring[(turn[z] - hops_of(g, z)[n]) % length] - g * home)
-        return [
-            (slab * breadth + (across - s) % breadth) * CORES + (core - t) % CORES
-            for t in range(CORES)
-        ]
+    slab_rows = rows * breadth * CORES
+
+    def slab_of(n):
+        return here(lambda g, z: ring[(turn[z] - hops_of(g, z)[n]) % length] - g * home)
+
+    def numbers_of(s):
+        return [(across - s) % breadth * CORES + (core - t) % CORES for t in range(CORES)]
 
     def with_cores(value):
         return [value] + [over_core(value, t) for t in range(1, CORES)]
@@ -423,9 +425,7 @@
     packed = jnp.concatenate([item_rows, slot_block(slots, item_rows)], axis=0)
     turned_x = to_plane(turned)
     factors = [[turned, turned_x]] + [[over_y(turned, s)] for s in range(1, breadth)]
-    items_x = to_plane(after(packed, *(pair[0] for pair in factors[1:]), turned_x, held[1]))
-    for s in range(1, breadth):
-        factors[s].append(over_y(turned_x, s))
+    items_x = to_plane(packed)
     units = [(n, 0, rows) for n in range(home)]
     mine = {}
     theirs = []
@@ -447,54 +447,49 @@
         theirs.append(pick(True, n, slice(first, first + count), *earlier))
         return to_plane(theirs[i])
 
-    moved = foreign(0, items_x, *(pair[1] for pair in factors[1:]))
-    begun = [theirs[0], held[1], held[length - 1]]
+    moved = foreign(0)
+    begun = [turned_x, items_x, *(pair[0] for pair in factors[1:])]
     for k in range(2, length // 2 + 1):
-        held[k] = along(after(held[k - 1], *begun), 1)
+        held[k] = along(after(held[k - 1], held[1], held[length - 1]), 1)
     for k in range(2, (length + 1) // 2):
-        held[length - k] = along(after(held[length - k + 1], *begun), -1)
+        held[length - k] = along(after(held[length - k + 1], held[1], held[length - 1]), -1)
+    for s in range(1, breadth):
+        factors[s].append(over_y(after(turned_x, theirs[0], *begun), s))
+
+    def short_of(n, *earlier):
+        slots_x = read_slots(after(items_x, *earlier), slots)
+        seen, sub_ids, live = jnp.concatenate([slots, slots_x], axis=1)
+        table = slot_table(image_dist, image_phase, seen)
+        which = jnp.reshape(group * home + slab_of(n), (1,)).astype(jnp.int32)
+        all_items = [packed, items_x]
+        return short_range(
+            which, live, sub_ids, table, aux_basis, aux_decay, all_items, slab_rows, subs
+        )
+
+    shorts = [short_of(0, theirs[0], *begun)]
     for i, (n, _, _) in enumerate(units):
         if i:
-            moved = foreign(i, theirs[i - 1], *(away[i - 2] if i > 1 else []))
-        mine[n] = with_cores(pick(False, n, slice(None), theirs[i]))
+            moved = foreign(i, theirs[i - 1], *(away[i - 2] if i > 1 else shorts))
         if i:
             multiply(i - 1)
-        crossed.append(with_cores(after(moved, *away[i - 1] if i else [])))
-    slots_x = read_slots(after(items_x, *(away[0] if away else [])), slots)
-    seen, sub_ids, live = jnp.concatenate([slots, slots_x], axis=1)
-    table = slot_table(image_dist, image_phase, seen)
-    short = short_range(
-        half, live, sub_ids, table, aux_basis, aux_decay, [packed, items_x], row_count, subs
-    )
+        earlier = away[i - 1] if i else begun
+        mine[n] = with_cores(pick(False, n, slice(None), theirs[i], *earlier))
+        crossed.append(with_cores(after(moved, *[mine[n][0], *away[i - 1]] if i else shorts)))
+        if i:
+            shorts.append(short_of(i, *away[i - 1]))
     last = len(units) - 1
 
-    def place_of(piece, i, s):
-        n, first, count = units[i]
-        return piece, [v * (rows // count) + first // count for v in numbers_of(n, s)]
-
-    calls = []
-    for i, (_, _, count) in enumerate(units[:-1]):
-        entries = [place_of(v, i, s) for s, v in enumerate([own[i], *arriving[i]])]
-        if calls and calls[-1][0] == count:
-            calls[-1][1].extend(entries)
-        else:
-            calls.append((count, entries))
-
-    def add_up(out, count, entries):
-        numbers = jnp.stack([v for _, each in entries for v in each]).astype(jnp.int32)
-        return final_sum(numbers, [piece for piece, _ in entries], short, out, count)
-
-    out = add_up(None, *calls.pop(0)) if calls else None
     multiply(last)
-    count = units[last][2]
-    calls.append((count, [place_of(own[last], last, 0)]))
-    if len(calls) > 1 and calls[-2][0] == count:
-        entries = calls.pop()[1]
-        calls[-1][1].extend(entries)
-    if breadth > 1:
-        calls.append((count, [place_of(v, last, s) for s, v in enumerate(arriving[last], 1)]))
-    for call in calls:
-        out = add_up(out, *call)
+    out = None
+    for n in range(home):
+        entries = [(own[n], 0)] + [(v, s) for s, v in enumerate(arriving[n], 1)]
+        for chosen in [entries] if n < last else [entries[:1], entries[1:]]:
+            if chosen:
+                inside = jnp.stack([v for _, s in chosen for v in numbers_of(s)])
+                order = jnp.concatenate([inside + slab_of(n) * breadth * CORES, inside])
+                pieces = [piece for piece, _ in chosen]
+                order = order.astype(jnp.int32)
+                out = final_sum(order, pieces, shorts[n], out, rows, row_count)
     return out
 
 

time: 90.8 us -> 85.9 us (0.946)
  waiting for transfers between devices: 31.5 us -> 25.2 us
  Pallas kernels: 28.1 us -> 32.8 us
  other arithmetic: 8.09 us -> 6.02 us
  starting transfers between devices: 18.5 us -> 17.2 us
    ppermute x15, waiting for transfers between devices: 31.5 us -> 25.2 us  [send(): return lax.ppermute(value, AXES, pairs)]
    pallas_call x1 -> x2, Pallas kernels: 9.68 us -> 14.3 us  [short_range(): pl.pallas_call(kernel, out_shape=pltpu.HBM((row_count, 2 * subs * width),...]
    select_n x4, other arithmetic: 5.37 us -> 3.24 us  [pick(): value = jnp.where(wanted == k, block[window], value)]
    ppermute x15, starting transfers between devices: 18.5 us -> 17.2 us  [send(): return lax.ppermute(value, AXES, pairs)]
    convert_element_type x1, other arithmetic: 1.45 us -> 0.41 us  [body(): weighted = (pairs * coul_weight[None, None, :]).astype(jnp.bfloat16)]
    unnamed x18 -> x28, local copies, waits for them, and re-layouts: 2.28 us -> 2.53 us
  transfers between devices with their start and end apart: 15 -> 15, of which waited for: 9 -> 6; matrix products, arithmetic and copies ran while one was open for 7% -> 9% of each run, Pallas kernels for 28% -> 35%
where the time goes in v12:
time: 85.9 us; the launch traced here: 85.4 us
  Pallas kernels  32.8 us (38%)
  waiting for transfers between devices  25.2 us (29%)
  starting transfers between devices  17.2 us (20%)
  other arithmetic  6.02 us (7%)
  local copies, waits for them, and re-layouts  3.26 us (4%)
  between operations  0.94 us (1%)
    ppermute x15, waiting for transfers between devices, send(): return lax.ppermute(value, AXES, pairs)  25.2 us
    ppermute x15, starting transfers between devices, send(): return lax.ppermute(value, AXES, pairs)  17.2 us
    pallas_call x2, Pallas kernels, short_range(): pl.pallas_call(kernel, out_shape=pltpu.HBM((row_count, 2 * subs * width),...  14.3 us
    pallas_call x3, Pallas kernels, final_sum(): pl.pallas_call(functools.partial(final_kernel, pieces=count, blocks=block...  9.64 us
    pallas_call x2, Pallas kernels, long_range(): pl.pallas_call(functools.partial(long_kernel, blocks=len(blocks), chains=...  8.8 us
    select_n x4, other arithmetic, pick(): value = jnp.where(wanted == k, block[window], value)  3.24 us
    unnamed x28, local copies, waits for them, and re-layouts  2.53 us
  transfers between devices with their start and end apart: 15, of which 6 were waited for; matrix products, arithmetic and copies ran while one was open for 9% of the time, Pallas kernels for 35%

profile of v12, /device:TPU:0, one launch (start us, length us, event | category | flops | bytes accessed | tf_op | source)
XLA Modules:
  0.0 85.4 jit_solution(16677964997442991988)
XLA Ops:
  0.0 1.2 %copy.18 = bf16[32,8,2,512]{3,1,2,0:T(8,128)(2,1)S(1)} copy(bf16[32,8,2,512]{3,2,1,0:T(2,128)(2,1)} %bitcast.56) | data formatting | bytes 1048576
  1.2 4.1 %collective-permute-start = (bf16[256,1024]{1,0:T(8,128)(2,1)S(1)}, bf16[256,1024]{1,0:T(8,128)(2,1)}, u32[]{:S(2)}, u32[]{:S(2)}) collective-permute-start(bf16[256,1024]{1,0:T(8,128)(2,1)S(1)} %bitcast.51), channel_id=1, source_target_pairs={{0,8},{1,9},{2,10},{3,11},{4,0},{5,1},{6,2},{7,3},{8,12},{9,13},{1... | collective-permute-start | bytes 1572872 | tf_op jit(solution)/shard_map/ppermute | solution.py:376
  6.0 1.3 %copy.16 = bf16[16,128,128]{1,2,0:T(8,128)(2,1)S(1)} copy(bf16[16,128,128]{2,1,0:T(8,128)(2,1)} %param.18) | data formatting | bytes 1048576 | tf_op args[7]
  7.4 1.6 %collective-permute-start.3 = (bf16[17,128,128]{2,1,0:T(8,128)(2,1)S(1)}, bf16[17,128,128]{2,1,0:T(8,128)(2,1)}, u32[]{:S(2)}, u32[]{:S(2)}) collective-permute-start(bf16[17,128,128]{2,1,0:T(8,128)(2,1)S(1)} %pad_maximum_fusion.refs_0_), channel_id=1, source_target_pairs={{0,16},{1,17},{2,18},{3,19},{4,20},{5,21},{6,22},{7,23},{8,24},{9,... | collective-permute-start | bytes 1671176 | tf_op jit(solution)/shard_map/ppermute | solution.py:376
  10.5 1.5 %collective-permute-start.5 = (bf16[1024,256]{1,0:T(8,128)(2,1)S(1)}, bf16[1024,256]{1,0:T(8,128)(2,1)S(1)}, u32[]{:S(2)}, u32[]{:S(2)}) collective-permute-start(bf16[1024,256]{1,0:T(8,128)(2,1)S(1)} %bitcast.46), channel_id=1, source_target_pairs={{0,2},{1,3},{2,0},{3,1},{4,6},{5,7},{6,4},{7,5},{8,10},{9,11},{10,... | collective-permute-start | bytes 1572872 | tf_op jit(solution)/shard_map/ppermute | solution.py:376
  12.2 5.5 %collective-permute-done = bf16[256,1024]{1,0:T(8,128)(2,1)} collective-permute-done((bf16[256,1024]{1,0:T(8,128)(2,1)S(1)}, bf16[256,1024]{1,0:T(8,128)(2,1)}, u32[]{:S(2)}, u32[]{:S(2)}) %collective-permute-start) | collective-permute-done | bytes 524320 | tf_op jit(solution)/shard_map/ppermute | solution.py:376
  17.7 11.8 %collective-permute-done.1 = bf16[256,1024]{1,0:T(8,128)(2,1)S(1)} collective-permute-done((bf16[256,1024]{1,0:T(8,128)(2,1)S(1)}, bf16[256,1024]{1,0:T(8,128)(2,1)S(1)}, u32[]{:S(2)}, u32[]{:S(2)}) %collective-permute-start.1) | collective-permute-done | bytes 524320 | tf_op jit(solution)/shard_map/ppermute | solution.py:376
  30.2 1.6 %collective-permute-start.6 = (bf16[256,1024]{1,0:T(8,128)(2,1)S(1)}, bf16[256,1024]{1,0:T(8,128)(2,1)}, u32[]{:S(2)}, u32[]{:S(2)}) collective-permute-start(bf16[256,1024]{1,0:T(8,128)(2,1)S(1)} %select_select_fusion.3), channel_id=1, source_target_pairs={{0,16},{1,17},{2,18},{3,19},{4,20},{5,21},{6,22},{7,23},{8,24},{9,... | collective-permute-start | bytes 1572872 | tf_op jit(solution)/shard_map/ppermute | solution.py:376
  31.8 1.5 %collective-permute-done.4.refs_5_ = bf16[1024,256]{1,0:T(8,128)(2,1)S(1)} collective-permute-done((bf16[1024,256]{1,0:T(8,128)(2,1)S(1)}, bf16[1024,256]{1,0:T(8,128)(2,1)S(1)}, u32[]{:S(2)}, u32[]{:S(2)}) %collective-permute-start.4) | collective-permute-done | bytes 524320 | tf_op jit(solution)/shard_map/ppermute | solution.py:376
  34.0 1.1 %select_select_fusion.1.refs_0_ = bf16[256,1024]{1,0:T(8,128)(2,1)S(1)} fusion(bf16[256,1024]{1,0:T(8,128)(2,1)} %bitcast.54, bf16[256,1024]{1,0:T(8,128)(2,1)} %collective-permute-done, bf16[256,1024]{1,0:T(8,128)(2,1)S(1)} %collective-permute-done.1, pred[]{:T(512)S(6)} %eq.81, pred[]{:T(512)S(6)} %eq.80), kind=kLoop, calls=%fused_computation.3 | loop fusion | flops 524288 | bytes 2097154 | tf_op jit(solution)/shard_map/jit(_where)/select_n | solution.py:410
  35.2 1.6 %collective-permute-start.9 = (bf16[1024,256]{1,0:T(8,128)(2,1)S(1)}, bf16[1024,256]{1,0:T(8,128)(2,1)S(1)}, u32[]{:S(2)}, u32[]{:S(2)}) collective-permute-start(bf16[1024,256]{1,0:T(8,128)(2,1)S(1)} %collective-permute-done.4.refs_5_), channel_id=1, source_target_pairs={{0,2},{1,3},{2,0},{3,1},{4,6},{5,7},{6,4},{7,5},{8,10},{9,11},{10,... | collective-permute-start | bytes 1572872 | tf_op jit(solution)/shard_map/ppermute | solution.py:376
  37.1 7.2 %short_range.2.refs_2_ = f32[1024,512]{1,0:T(8,128)} custom-call(s32[1]{0:T(128)} %bitcast.2.half_ref, s32[32]{0:T(128)S(1)} %get-tuple-element.60.live_ref, s32[32]{0:T(128)S(1)} %get-tuple-element.59.sub_ref, f32[3,32]{1,0:T(4,128)S(1)} %pad_maximum_fusion.1.meta_ref, bf16[128,4096]{1,0:T(8,128)(2,1)} %basis_ref.3, f32[1,4096]{1,0:T(1,128)S(1)} %bitcast.49, ...), custom_call_target="tpu_custom_call" | custom-call | flops 2147483648 | bytes 1 | tf_op jit(solution)/shard_map/short_range/pallas_call | solution.py:127
  45.3 2.3 %collective-permute-start.10 = (bf16[256,1024]{1,0:T(8,128)(2,1)}, bf16[256,1024]{1,0:T(8,128)(2,1)}, u32[]{:S(2)}, u32[]{:S(2)}) collective-permute-start(bf16[256,1024]{1,0:T(8,128)(2,1)} %select_select_fusion.2), channel_id=1, source_target_pairs={{0,16},{1,17},{2,18},{3,19},{4,20},{5,21},{6,22},{7,23},{8,24},{9,... | collective-permute-start | bytes 1572872 | tf_op jit(solution)/shard_map/ppermute | solution.py:376
  47.9 1.6 %collective-permute-done.9.refs_7_ = bf16[1024,256]{1,0:T(8,128)(2,1)S(1)} collective-permute-done((bf16[1024,256]{1,0:T(8,128)(2,1)S(1)}, bf16[1024,256]{1,0:T(8,128)(2,1)S(1)}, u32[]{:S(2)}, u32[]{:S(2)}) %collective-permute-start.9) | collective-permute-done | bytes 524320 | tf_op jit(solution)/shard_map/ppermute | solution.py:376
  49.6 4.5 %long_range.2 = (f32[512,512]{1,0:T(8,128)}, bf16[512,512]{1,0:T(8,128)(2,1)}) custom-call(bf16[256,1024]{1,0:T(8,128)(2,1)S(1)} %select_select_fusion.1.refs_0_, bf16[256,1024]{1,0:T(8,128)(2,1)} %collective-permute-done.6.refs_1_, bf16[256,1024]{1,0:T(8,128)(2,1)} %collective-permute-done.7.refs_2_, bf16[256,1024]{1,0:T(8,128)(2,1)} %collective-permute-done.8.refs_3_, ...), custom_call_target="tpu_custom_call" | custom-call | flops 1 | bytes 1 | tf_op jit(solution)/shard_map/long_range/pallas_call | solution.py:196
  54.1 1.6 %collective-permute-start.14 = (bf16[512,512]{1,0:T(8,128)(2,1)}, bf16[512,512]{1,0:T(8,128)(2,1)S(1)}, u32[]{:S(2)}, u32[]{:S(2)}) collective-permute-start(bf16[512,512]{1,0:T(8,128)(2,1)} %get-tuple-element.42), channel_id=1, source_target_pairs={{0,2},{1,3},{2,0},{3,1},{4,6},{5,7},{6,4},{7,5},{8,10},{9,11},{10,... | collective-permute-start | bytes 1572872 | tf_op jit(solution)/shard_map/ppermute | solution.py:376
  56.9 3.6 %collective-permute-done.10.refs_1_ = bf16[256,1024]{1,0:T(8,128)(2,1)} collective-permute-done((bf16[256,1024]{1,0:T(8,128)(2,1)}, bf16[256,1024]{1,0:T(8,128)(2,1)}, u32[]{:S(2)}, u32[]{:S(2)}) %collective-permute-start.10) | collective-permute-done | bytes 524320 | tf_op jit(solution)/shard_map/ppermute | solution.py:376
  61.5 1.2 %collective-permute-done.12.refs_3_ = bf16[256,1024]{1,0:T(8,128)(2,1)S(1)} collective-permute-done((bf16[256,1024]{1,0:T(8,128)(2,1)}, bf16[256,1024]{1,0:T(8,128)(2,1)S(1)}, u32[]{:S(2)}, u32[]{:S(2)}) %collective-permute-start.12) | collective-permute-done | bytes 524320 | tf_op jit(solution)/shard_map/ppermute | solution.py:376
  62.6 4.3 %long_range.3 = (f32[512,512]{1,0:T(8,128)}, bf16[512,512]{1,0:T(8,128)(2,1)}) custom-call(bf16[256,1024]{1,0:T(8,128)(2,1)S(1)} %select_select_fusion.refs_0_, bf16[256,1024]{1,0:T(8,128)(2,1)} %collective-permute-done.10.refs_1_, bf16[256,1024]{1,0:T(8,128)(2,1)S(1)} %collective-permute-done.11.refs_2_, ...), custom_call_target="tpu_custom_call" | custom-call | flops 1 | bytes 1 | tf_op jit(solution)/shard_map/long_range/pallas_call | solution.py:196
  66.9 1.6 %collective-permute-start.13 = (bf16[512,512]{1,0:T(8,128)(2,1)}, bf16[512,512]{1,0:T(8,128)(2,1)S(1)}, u32[]{:S(2)}, u32[]{:S(2)}) collective-permute-start(bf16[512,512]{1,0:T(8,128)(2,1)} %get-tuple-element.47), channel_id=1, source_target_pairs={{0,2},{1,3},{2,0},{3,1},{4,6},{5,7},{6,4},{7,5},{8,10},{9,11},{10,... | collective-permute-start | bytes 1572872 | tf_op jit(solution)/shard_map/ppermute | solution.py:376
  68.6 7.1 %short_range.3.refs_1_ = f32[1024,512]{1,0:T(8,128)} custom-call(s32[1]{0:T(128)} %bitcast.19.half_ref, s32[32]{0:T(128)S(1)} %get-tuple-element.57.live_ref, s32[32]{0:T(128)S(1)} %get-tuple-element.56.sub_ref, f32[3,32]{1,0:T(4,128)S(1)} %pad_maximum_fusion.2.meta_ref, bf16[128,4096]{1,0:T(8,128)(2,1)} %basis_ref.3, f32[1,4096]{1,0:T(1,128)S(1)} %bitcast.50, ...), custom_call_target="tpu_custom_call" | custom-call | flops 2147483648 | bytes 1 | tf_op jit(solution)/shard_map/short_range/pallas_call | solution.py:127
  75.7 3.8 %final_sum.3.refs_2_ = bf16[2048,2,256]{2,1,0:T(2,128)(2,1)} custom-call(s32[8]{0:T(128)S(1)} %concatenate.31.order_ref, f32[512,512]{1,0:T(8,128)} %get-tuple-element.50.refs_0_, bf16[512,512]{1,0:T(8,128)(2,1)S(1)} %collective-permute-done.14.refs_1_, f32[1024,512]{1,0:T(8,128)} %short_range.2.refs_2_), custom_call_target="tpu_custom_call" | custom-call | flops 1 | bytes 1 | tf_op jit(solution)/shard_map/final_sum/pallas_call | solution.py:253
  79.5 3.0 %final_sum.4.refs_2_ = bf16[2048,2,256]{2,1,0:T(2,128)(2,1)} custom-call(s32[4]{0:T(128)S(1)} %pad_add_fusion.4.order_ref, f32[512,512]{1,0:T(8,128)} %get-tuple-element.49.refs_0_, f32[1024,512]{1,0:T(8,128)} %short_range.3.refs_1_, bf16[2048,2,256]{2,1,0:T(2,128)(2,1)} %final_sum.3.refs_2_), custom_call_target="tpu_custom_call", output_to_operand_aliasing={{}: (3, {})} | custom-call | flops 1 | bytes 1 | tf_op jit(solution)/shard_map/final_sum/pallas_call | solution.py:253
  82.6 2.8 %final_sum.5 = bf16[2048,2,256]{2,1,0:T(2,128)(2,1)} custom-call(s32[4]{0:T(128)S(1)} %add_add_fusion.1.order_ref, bf16[512,512]{1,0:T(8,128)(2,1)S(1)} %collective-permute-done.13.refs_0_, f32[1024,512]{1,0:T(8,128)} %short_range.3.refs_1_, bf16[2048,2,256]{2,1,0:T(2,128)(2,1)} %final_sum.4.refs_2_), custom_call_target="tpu_custom_call", output_to_operand_aliasing={{}: (3, {})} | custom-call | flops 1 | bytes 1 | tf_op jit(solution)/shard_map/final_sum/pallas_call | solution.py:253
  (71 shorter events, 7.1 us)
Async XLA Ops:
  0.0 9.0 %copy-start.7 = (bf16[256,2,512]{2,1,0:T(2,128)(2,1)S(1)}, bf16[256,2,512]{2,1,0:T(2,128)(2,1)}, u32[]{:S(2)}) copy-start(bf16[256,2,512]{2,1,0:T(2,128)(2,1)} %param.11) | copy-start | bytes 1572868
  0.0 9.0 %copy-start.10 = (f32[512]{0:T(512)S(1)}, f32[512]{0:T(512)}, u32[]{:S(2)}) copy-start(f32[512]{0:T(512)} %param.13) | copy-start | bytes 6148
  1.2 28.9 %copy-start.4 = (bf16[32,8,2,512]{3,1,2,0:T(8,128)(2,1)}, bf16[32,8,2,512]{3,1,2,0:T(8,128)(2,1)S(1)}, u32[]{:S(2)}) copy-start(bf16[32,8,2,512]{3,1,2,0:T(8,128)(2,1)S(1)} %copy.18) | copy-start | bytes 1572868
  1.2 16.5 %collective-permute-start = (bf16[256,1024]{1,0:T(8,128)(2,1)S(1)}, bf16[256,1024]{1,0:T(8,128)(2,1)}, u32[]{:S(2)}, u32[]{:S(2)}) collective-permute-start(bf16[256,1024]{1,0:T(8,128)(2,1)S(1)} %bitcast.51), channel_id=1, source_target_pairs={{0,8},{1,9},{2,10},{3,11},{4,0},{5,1},{6,2},{7,3},{8,12},{9,13},{1... | collective-permute-start | bytes 1572872 | tf_op jit(solution)/shard_map/ppermute | solution.py:376
  5.3 24.2 %collective-permute-start.1 = (bf16[256,1024]{1,0:T(8,128)(2,1)S(1)}, bf16[256,1024]{1,0:T(8,128)(2,1)S(1)}, u32[]{:S(2)}, u32[]{:S(2)}) collective-permute-start(bf16[256,1024]{1,0:T(8,128)(2,1)S(1)} %bitcast.52), channel_id=1, source_target_pairs={{0,4},{1,5},{2,6},{3,7},{4,12},{5,13},{6,14},{7,15},{8,0},{9,1},{1... | collective-permute-start | bytes 1572872 | tf_op jit(solution)/shard_map/ppermute | solution.py:376
  7.4 25.8 %collective-permute-start.3 = (bf16[17,128,128]{2,1,0:T(8,128)(2,1)S(1)}, bf16[17,128,128]{2,1,0:T(8,128)(2,1)}, u32[]{:S(2)}, u32[]{:S(2)}) collective-permute-start(bf16[17,128,128]{2,1,0:T(8,128)(2,1)S(1)} %pad_maximum_fusion.refs_0_), channel_id=1, source_target_pairs={{0,16},{1,17},{2,18},{3,19},{4,20},{5,21},{6,22},{7,23},{8,24},{9,... | collective-permute-start | bytes 1671176 | tf_op jit(solution)/shard_map/ppermute | solution.py:376
  9.9 23.3 %collective-permute-start.4 = (bf16[1024,256]{1,0:T(8,128)(2,1)S(1)}, bf16[1024,256]{1,0:T(8,128)(2,1)S(1)}, u32[]{:S(2)}, u32[]{:S(2)}) collective-permute-start(bf16[1024,256]{1,0:T(8,128)(2,1)S(1)} %bitcast.45), channel_id=1, source_target_pairs={{0,16},{1,17},{2,18},{3,19},{4,20},{5,21},{6,22},{7,23},{8,24},{9,... | collective-permute-start | bytes 1572872 | tf_op jit(solution)/shard_map/ppermute | solution.py:376
  10.5 22.7 %collective-permute-start.5 = (bf16[1024,256]{1,0:T(8,128)(2,1)S(1)}, bf16[1024,256]{1,0:T(8,128)(2,1)S(1)}, u32[]{:S(2)}, u32[]{:S(2)}) collective-permute-start(bf16[1024,256]{1,0:T(8,128)(2,1)S(1)} %bitcast.46), channel_id=1, source_target_pairs={{0,2},{1,3},{2,0},{3,1},{4,6},{5,7},{6,4},{7,5},{8,10},{9,11},{10,... | collective-permute-start | bytes 1572872 | tf_op jit(solution)/shard_map/ppermute | solution.py:376
  12.2 24.6 %copy-start.11 = (f32[125]{0:T(128)S(1)}, f32[125]{0:T(128)}, u32[]{:S(2)}) copy-start(f32[125]{0:T(128)} %param.16) | copy-start | bytes 1504
  12.2 24.6 %copy-start.12 = (f32[125]{0:T(128)S(1)}, f32[125]{0:T(128)}, u32[]{:S(2)}) copy-start(f32[125]{0:T(128)} %param.17) | copy-start | bytes 1504
  12.2 24.8 %copy-start = (f32[4096]{0:T(1024)S(1)}, f32[4096]{0:T(1024)}, u32[]{:S(2)}) copy-start(f32[4096]{0:T(1024)} %param.15) | copy-start | bytes 49156
  29.5 14.8 %collective-permute-start.2 = (bf16[256,1024]{1,0:T(8,128)(2,1)}, bf16[256,1024]{1,0:T(8,128)(2,1)S(1)}, u32[]{:S(2)}, u32[]{:S(2)}) collective-permute-start(bf16[256,1024]{1,0:T(8,128)(2,1)} %collective-permute-done), channel_id=1, source_target_pairs={{0,8},{1,9},{2,10},{3,11},{4,0},{5,1},{6,2},{7,3},{8,12},{9,13},{1... | collective-permute-start | bytes 1572872 | tf_op jit(solution)/shard_map/ppermute | solution.py:376
  30.2 14.1 %collective-permute-start.6 = (bf16[256,1024]{1,0:T(8,128)(2,1)S(1)}, bf16[256,1024]{1,0:T(8,128)(2,1)}, u32[]{:S(2)}, u32[]{:S(2)}) collective-permute-start(bf16[256,1024]{1,0:T(8,128)(2,1)S(1)} %select_select_fusion.3), channel_id=1, source_target_pairs={{0,16},{1,17},{2,18},{3,19},{4,20},{5,21},{6,22},{7,23},{8,24},{9,... | collective-permute-start | bytes 1572872 | tf_op jit(solution)/shard_map/ppermute | solution.py:376
  35.1 12.8 %collective-permute-start.7 = (bf16[256,1024]{1,0:T(8,128)(2,1)S(1)}, bf16[256,1024]{1,0:T(8,128)(2,1)}, u32[]{:S(2)}, u32[]{:S(2)}) collective-permute-start(bf16[256,1024]{1,0:T(8,128)(2,1)S(1)} %select_select_fusion.1.refs_0_), channel_id=1, source_target_pairs={{0,1},{1,0},{2,3},{3,2},{4,5},{5,4},{6,7},{7,6},{8,9},{9,8},{10,11... | collective-permute-start | bytes 1572872 | tf_op jit(solution)/shard_map/ppermute | solution.py:376
  35.2 14.3 %collective-permute-start.9 = (bf16[1024,256]{1,0:T(8,128)(2,1)S(1)}, bf16[1024,256]{1,0:T(8,128)(2,1)S(1)}, u32[]{:S(2)}, u32[]{:S(2)}) collective-permute-start(bf16[1024,256]{1,0:T(8,128)(2,1)S(1)} %collective-permute-done.4.refs_5_), channel_id=1, source_target_pairs={{0,2},{1,3},{2,0},{3,1},{4,6},{5,7},{6,4},{7,5},{8,10},{9,11},{10,... | collective-permute-start | bytes 1572872 | tf_op jit(solution)/shard_map/ppermute | solution.py:376
  37.1 7.3 %copy-start.2 = (bf16[256,1024]{1,0:T(8,128)(2,1)S(1)}, bf16[256,1024]{1,0:T(8,128)(2,1)}, u32[]{:S(2)}) copy-start(bf16[256,1024]{1,0:T(8,128)(2,1)} %copy-done.1) | copy-start | bytes 1572868
  44.3 5.2 %collective-permute-start.8 = (bf16[256,1024]{1,0:T(8,128)(2,1)}, bf16[256,1024]{1,0:T(8,128)(2,1)}, u32[]{:S(2)}, u32[]{:S(2)}) collective-permute-start(bf16[256,1024]{1,0:T(8,128)(2,1)} %collective-permute-done.6.refs_1_), channel_id=1, source_target_pairs={{0,1},{1,0},{2,3},{3,2},{4,5},{5,4},{6,7},{7,6},{8,9},{9,8},{10,11... | collective-permute-start | bytes 1572872 | tf_op jit(solution)/shard_map/ppermute | solution.py:376
  45.3 15.2 %collective-permute-start.10 = (bf16[256,1024]{1,0:T(8,128)(2,1)}, bf16[256,1024]{1,0:T(8,128)(2,1)}, u32[]{:S(2)}, u32[]{:S(2)}) collective-permute-start(bf16[256,1024]{1,0:T(8,128)(2,1)} %select_select_fusion.2), channel_id=1, source_target_pairs={{0,16},{1,17},{2,18},{3,19},{4,20},{5,21},{6,22},{7,23},{8,24},{9,... | collective-permute-start | bytes 1572872 | tf_op jit(solution)/shard_map/ppermute | solution.py:376
  47.9 7.8 %copy-start.3 = (bf16[256,1024]{1,0:T(8,128)(2,1)S(1)}, bf16[256,1024]{1,0:T(8,128)(2,1)}, u32[]{:S(2)}) copy-start(bf16[256,1024]{1,0:T(8,128)(2,1)} %copy-done.1) | copy-start | bytes 1572868
  47.9 7.8 %copy-start.6 = (bf16[256,1024]{1,0:T(8,128)(2,1)S(1)}, bf16[256,1024]{1,0:T(8,128)(2,1)}, u32[]{:S(2)}) copy-start(bf16[256,1024]{1,0:T(8,128)(2,1)} %copy-done.5) | copy-start | bytes 1572868
  54.1 21.6 %collective-permute-start.14 = (bf16[512,512]{1,0:T(8,128)(2,1)}, bf16[512,512]{1,0:T(8,128)(2,1)S(1)}, u32[]{:S(2)}, u32[]{:S(2)}) collective-permute-start(bf16[512,512]{1,0:T(8,128)(2,1)} %get-tuple-element.42), channel_id=1, source_target_pairs={{0,2},{1,3},{2,0},{3,1},{4,6},{5,7},{6,4},{7,5},{8,10},{9,11},{10,... | collective-permute-start | bytes 1572872 | tf_op jit(solution)/shard_map/ppermute | solution.py:376
  56.8 4.7 %collective-permute-start.11 = (bf16[256,1024]{1,0:T(8,128)(2,1)S(1)}, bf16[256,1024]{1,0:T(8,128)(2,1)S(1)}, u32[]{:S(2)}, u32[]{:S(2)}) collective-permute-start(bf16[256,1024]{1,0:T(8,128)(2,1)S(1)} %select_select_fusion.refs_0_), channel_id=1, source_target_pairs={{0,1},{1,0},{2,3},{3,2},{4,5},{5,4},{6,7},{7,6},{8,9},{9,8},{10,11... | collective-permute-start | bytes 1572872 | tf_op jit(solution)/shard_map/ppermute | solution.py:376
  60.5 2.1 %collective-permute-start.12 = (bf16[256,1024]{1,0:T(8,128)(2,1)}, bf16[256,1024]{1,0:T(8,128)(2,1)S(1)}, u32[]{:S(2)}, u32[]{:S(2)}) collective-permute-start(bf16[256,1024]{1,0:T(8,128)(2,1)} %collective-permute-done.10.refs_1_), channel_id=1, source_target_pairs={{0,1},{1,0},{2,3},{3,2},{4,5},{5,4},{6,7},{7,6},{8,9},{9,8},{10,11... | collective-permute-start | bytes 1572872 | tf_op jit(solution)/shard_map/ppermute | solution.py:376
  66.9 15.7 %collective-permute-start.13 = (bf16[512,512]{1,0:T(8,128)(2,1)}, bf16[512,512]{1,0:T(8,128)(2,1)S(1)}, u32[]{:S(2)}, u32[]{:S(2)}) collective-permute-start(bf16[512,512]{1,0:T(8,128)(2,1)} %get-tuple-element.47), channel_id=1, source_target_pairs={{0,2},{1,3},{2,0},{3,1},{4,6},{5,7},{6,4},{7,5},{8,10},{9,11},{10,... | collective-permute-start | bytes 1572872 | tf_op jit(solution)/shard_map/ppermute | solution.py:376
  (4 other events, 21.2 us)

commit v13 on v11

--- a/solution.py
+++ b/solution.py
@@ -22,8 +22,8 @@
 def short_kernel(
     half_ref, live_ref, sub_ref, meta_ref, basis_ref, decay_ref, *refs, share, subs, depth, width
 ):
-    items, scratch = refs[:-11], refs[-11:]
-    out_ref, basis, basis_f32, left, acc, made, dists, group_sub, cursor, basis_sem, out_sem = scratch
+    items, scratch = refs[:-10], refs[-10:]
+    out_ref, basis, left, acc, made, dists, group_sub, cursor, basis_sem, out_sem = scratch
     slots = share * len(items)
     row_count = out_ref.shape[0]
     mine = pl.ds(pl.multiple_of(half_ref[0] * row_count, row_count), row_count)
@@ -82,15 +82,17 @@
     tile = min(row_count, made.shape[1])
     decay = decay_ref[:, mine]
     basis_copy.wait()
-    basis_f32[...] = basis[...].astype(jnp.float32)
 
     def one_group(group, carry):
         s = group_sub[group]
-        damping = [jnp.exp(decay * -dists[group * GROUP_ITEMS + k]) for k in range(GROUP_ITEMS)]
+        damping = [
+            jnp.exp(decay * -dists[group * GROUP_ITEMS + k]).astype(basis.dtype)
+            for k in range(GROUP_ITEMS)
+        ]
         for t in range(0, row_count, tile):
             right = jnp.concatenate(
                 [
-                    (basis_f32[:, t : t + tile] * damping[k][:, t : t + tile]).astype(jnp.bfloat16)
+                    basis[:, t : t + tile] * damping[k][:, t : t + tile]
                     for k in range(GROUP_ITEMS)
                 ],
                 axis=0,
@@ -131,7 +133,6 @@
         out_specs=pl.BlockSpec(memory_space=pltpu.HBM),
         scratch_shapes=[
             pltpu.VMEM((depth, row_count), jnp.bfloat16),
-            pltpu.VMEM((depth, row_count), jnp.float32),
             pltpu.VMEM((groups, 2 * width, GROUP_ITEMS * depth), jnp.bfloat16),
             pltpu.VMEM((subs, 2 * width, row_count), jnp.float32),
             pltpu.VMEM((row_count // tile, tile, 2 * subs * width), jnp.float32),
@@ -149,12 +150,12 @@
     )(half, live, sub_ids, meta, in_hbm(aux_basis), aux_decay.reshape(1, -1), *items)
 
 
-def long_kernel(*refs, blocks, chains, pieces):
+def long_kernel(*refs, blocks, chains, pieces, width):
     parts = refs[: blocks * chains]
     factors = refs[blocks * chains : (blocks + pieces) * chains]
     outs, scratch = refs[(blocks + pieces) * chains :][:pieces], refs[-pieces - 2 :]
     right, made, out_sem = scratch[0], scratch[1:-1], scratch[-1]
-    depth, width = factors[0].shape
+    depth = factors[0].shape[0]
     half = depth // 2
     count = parts[0].shape[0]
     copies = []
@@ -162,6 +163,9 @@
         for chain in range(chains):
             factor = factors[piece * chains + chain]
             top = chain * depth
+            if factor.shape[1] > width:
+                right[top : top + depth, :] = factor[...]
+                continue
             right[top : top + depth, 0:width] = factor[...]
             right[top : top + half, width:] = factor[half:, :]
             right[top + half : top + depth, width:] = -factor[0:half, :]
@@ -180,8 +184,8 @@
         copy.wait()
 
 
-def long_range(blocks, factors):
-    depth, width = factors[0][0].shape
+def long_range(blocks, factors, width):
+    depth = factors[0][0].shape[0]
     chains = len(factors[0])
     pieces = len(factors)
     count = blocks[0][0].shape[0]
@@ -189,7 +193,9 @@
     dtypes = [jnp.bfloat16] * pieces
     flat = [v for group in [*blocks, *factors] for v in group]
     return pl.pallas_call(
-        functools.partial(long_kernel, blocks=len(blocks), chains=chains, pieces=pieces),
+        functools.partial(
+            long_kernel, blocks=len(blocks), chains=chains, pieces=pieces, width=width
+        ),
         out_shape=[pltpu.HBM(shape, dtype) for dtype in dtypes],
         in_specs=[pl.BlockSpec(memory_space=pltpu.VMEM)] * len(flat),
         out_specs=[pl.BlockSpec(memory_space=pltpu.HBM)] * pieces,
@@ -319,6 +325,13 @@
     return jnp.stack([distance, jnp.cos(phase), jnp.sin(phase)])
 
 
+def both_parts(factor):
+    half = factor.shape[0] // 2
+    return jnp.concatenate(
+        [factor, jnp.concatenate([factor[half:], -factor[:half]], axis=0)], axis=1
+    )
+
+
 def slot_block(slots, items):
     digits = jnp.concatenate([slots // 128, slots % 128], axis=0).astype(items.dtype)
     fill = [(0, full - used) for full, used in zip(items.shape[1:], digits.shape)]
@@ -443,12 +456,11 @@
             value = jnp.where(wanted == k, block, value)
         return value
 
-    def numbers_of(n, s):
-        slab = here(lambda g, z: ring[(turn[z] - hops_of(g, z)[n]) % length] - g * home)
-        return [
-            (slab * breadth + (across - s) % breadth) * CORES + (core - t) % CORES
-            for t in range(CORES)
-        ]
+    def slab_of(n):
+        return here(lambda g, z: ring[(turn[z] - hops_of(g, z)[n]) % length] - g * home)
+
+    def number_of(n, s, t):
+        return (slab_of(n) * breadth + (across - s) % breadth) * CORES + (core - t) % CORES
 
     def with_cores(value):
         return [value] + [over_core(value, t) for t in range(1, CORES)]
@@ -458,32 +470,22 @@
     turned_x = to_plane(turned)
     factors = [[turned, turned_x]] + [[over_y(turned, s)] for s in range(1, breadth)]
     items_x = to_plane(packed)
-    mine = {}
+    mine = []
     theirs = []
     crossed = []
     away = []
     arriving = []
 
-    def blocks_of(i, *earlier):
-        return list(zip(mine[i], [after(crossed[i][0], *earlier), *crossed[i][1:]]))
-
-    def multiply(i):
-        earlier = arriving[i - 1] if i else []
-        away.append(long_range(blocks_of(i, *earlier), factors[1:]) if breadth > 1 else [])
-        arriving.append([over_y(v, s) for s, v in enumerate(away[i], 1)])
-
-    def shorts(*earlier):
-        slots_x = read_slots(after(items_x, *earlier), slots)
-        seen, sub_ids, live = jnp.concatenate([slots, slots_x], axis=1)
-        table = slot_table(image_dist, image_phase, seen)
-        all_items = [packed, items_x]
-        return short_range(
-            half, live, sub_ids, table, aux_basis, aux_decay, all_items, row_count, subs
-        )
-
     def foreign(n, *earlier):
         theirs.append(pick(True, n, *earlier))
         return to_plane(theirs[n])
+
+    def multiply(n, t, away_factors):
+        made = []
+        if breadth > 1:
+            made = long_range([(mine[n][t], crossed[n][t])], away_factors, local_rows)
+        away[n].extend(made)
+        arriving[n].append([over_y(v, s) for s, v in enumerate(made, 1)])
 
     moved = foreign(0)
     begun = [turned_x, items_x, *(pair[0] for pair in factors[1:])]
@@ -493,28 +495,43 @@
         held[length - k] = along(after(held[length - k + 1], held[1], held[length - 1]), -1)
     for s in range(1, breadth):
         factors[s].append(over_y(after(turned_x, theirs[0], *begun), s))
-    short = shorts(theirs[0], *begun)
-
+    slots_x = read_slots(after(items_x, theirs[0], *begun), slots)
+    seen, sub_ids, live = jnp.concatenate([slots, slots_x], axis=1)
+    table = slot_table(image_dist, image_phase, seen)
+    short = short_range(
+        half, live, sub_ids, table, aux_basis, aux_decay, [packed, items_x], row_count, subs
+    )
+
+    out = None
     for n in range(home):
         if n:
             moved = foreign(n, theirs[n - 1], *(away[n - 2] if n > 1 else [short]))
-        mine[n] = with_cores(pick(False, n, theirs[n], *begun))
+        away.append([])
+        arriving.append([])
+        mine.append(with_cores(pick(False, n, theirs[n], *(away[n - 1] if n else begun))))
+        away_factors = factors[1:]
         if n:
-            multiply(n - 1)
-        crossed.append(with_cores(after(moved, *away[n - 1] if n else [short])))
-    last = home - 1
-    multiply(last)
-
-    def order_of(n, places):
-        return jnp.stack([v for s in places for v in numbers_of(n, s)]).astype(jnp.int32)
-
-    out = None
+            away_factors = [[both_parts(after(v, *away[0])) for v in pair] for pair in factors[1:]]
+        crossed.append(with_cores(moved if n else after(moved, short)))
+        for t in range(CORES):
+            multiply(n, t, away_factors)
+        blocks = [
+            (after(mine[n][0], *away[n]), crossed[n][0]),
+            *zip(mine[n][1:], crossed[n][1:]),
+        ]
+        order = jnp.stack([number_of(n, 0, t) for t in range(CORES)]).astype(jnp.int32)
+        out = own_sum(order, blocks, factors[0], short, out)
+    calls = []
     for n in range(home):
-        blocks = blocks_of(n, *away[last])
-        out = own_sum(order_of(n, [0]), blocks, factors[0], short, out)
-    for n in range(home):
-        if breadth > 1:
-            out = final_sum(order_of(n, range(1, breadth)), arriving[n], short, out, rows)
+        calls += [
+            [(v, number_of(n, s, t)) for s, v in enumerate(arriving[n][t], 1)] for t in range(CORES)
+        ]
+        if n < home - 1:
+            calls[-CORES:] = [sum(calls[-CORES:], [])]
+    for entries in calls:
+        if entries:
+            order = jnp.stack([number for _, number in entries]).astype(jnp.int32)
+            out = final_sum(order, [piece for piece, _ in entries], short, out, rows)
     return out
 
 

time: 93.9 us -> 89.5 us (0.953)
  waiting for transfers between devices: 32 us -> 25.3 us
  local copies, waits for them, and re-layouts: 6.58 us -> 3.13 us
  Pallas kernels: 32.4 us -> 34.2 us
  starting transfers between devices: 16.3 us -> 18 us
  other arithmetic: 5.34 us -> 6.93 us
    ppermute x15 -> x17, waiting for transfers between devices: 32 us -> 25.3 us  [send(): return lax.ppermute(value, AXES, pairs)]
    unnamed x42 -> x34, local copies, waits for them, and re-layouts: 5.99 us -> 2.54 us
    ppermute x15 -> x17, starting transfers between devices: 16.3 us -> 18 us  [send(): return lax.ppermute(value, AXES, pairs)]
    pallas_call x2 -> x4, Pallas kernels: 6.71 us -> 8 us  [long_range(): pl.pallas_call(functools.partial(long_kernel, blocks=len(blocks), chains=...]
    pallas_call x2 -> x3, Pallas kernels: 5.99 us -> 7.11 us  [final_sum(): pl.pallas_call(functools.partial(final_kernel, pieces=count, blocks=block...]
  transfers between devices with their start and end apart: 15 -> 17, of which waited for: 5 -> 5; matrix products, arithmetic and copies ran while one was open for 8% -> 10% of each run, Pallas kernels for 27% -> 36%
where the time goes in v13:
time: 89.5 us; the launch traced here: 88.6 us
  Pallas kernels  34.2 us (38%)
  waiting for transfers between devices  25.3 us (28%)
  starting transfers between devices  18 us (20%)
  other arithmetic  6.93 us (8%)
  local copies, waits for them, and re-layouts  3.13 us (3%)
  between operations  0.98 us (1%)
    ppermute x17, waiting for transfers between devices, send(): return lax.ppermute(value, AXES, pairs)  25.3 us
    ppermute x17, starting transfers between devices, send(): return lax.ppermute(value, AXES, pairs)  18 us
    pallas_call x1, Pallas kernels, short_range(): pl.pallas_call(kernel, out_shape=pltpu.HBM((row_count, 2 * subs * width),...  9.78 us
    pallas_call x2, Pallas kernels, own_sum(): pl.pallas_call(functools.partial(own_kernel, blocks=count, chains=chains,...  9.32 us
    pallas_call x4, Pallas kernels, long_range(): pl.pallas_call(functools.partial(long_kernel, blocks=len(blocks), chains=...  8 us
    pallas_call x3, Pallas kernels, final_sum(): pl.pallas_call(functools.partial(final_kernel, pieces=count, blocks=block...  7.11 us
    select_n x4, other arithmetic, pick(): value = jnp.where(wanted == k, block, value)  4.22 us
    unnamed x34, local copies, waits for them, and re-layouts  2.54 us
  transfers between devices with their start and end apart: 17, of which 5 were waited for; matrix products, arithmetic and copies ran while one was open for 10% of the time, Pallas kernels for 36%

profile of v13, /device:TPU:0, one launch (start us, length us, event | category | flops | bytes accessed | tf_op | source)
XLA Modules:
  0.0 88.6 jit_solution(17216712770411005780)
XLA Ops:
  1.2 4.1 %collective-permute-start = (bf16[256,1024]{1,0:T(8,128)(2,1)S(1)}, bf16[256,1024]{1,0:T(8,128)(2,1)}, u32[]{:S(2)}, u32[]{:S(2)}) collective-permute-start(bf16[256,1024]{1,0:T(8,128)(2,1)S(1)} %bitcast.40), channel_id=1, source_target_pairs={{0,8},{1,9},{2,10},{3,11},{4,0},{5,1},{6,2},{7,3},{8,12},{9,13},{1... | collective-permute-start | bytes 1572872 | tf_op jit(solution)/shard_map/ppermute | solution.py:422
  6.0 1.3 %copy.18 = bf16[16,128,128]{1,2,0:T(8,128)(2,1)S(1)} copy(bf16[16,128,128]{2,1,0:T(8,128)(2,1)} %param.18) | data formatting | bytes 1048576 | tf_op args[7]
  8.2 1.5 %collective-permute-start.3 = (bf16[17,128,128]{2,1,0:T(8,128)(2,1)}, bf16[17,128,128]{2,1,0:T(8,128)(2,1)}, u32[]{:S(2)}, u32[]{:S(2)}) collective-permute-start(bf16[17,128,128]{2,1,0:T(8,128)(2,1)} %pad_maximum_fusion.refs_0_), channel_id=1, source_target_pairs={{0,16},{1,17},{2,18},{3,19},{4,20},{5,21},{6,22},{7,23},{8,24},{9,... | collective-permute-start | bytes 1671176 | tf_op jit(solution)/shard_map/ppermute | solution.py:422
  10.7 1.6 %collective-permute-start.5 = (bf16[1024,256]{1,0:T(8,128)(2,1)S(1)}, bf16[1024,256]{1,0:T(8,128)(2,1)S(1)}, u32[]{:S(2)}, u32[]{:S(2)}) collective-permute-start(bf16[1024,256]{1,0:T(8,128)(2,1)S(1)} %bitcast.35), channel_id=1, source_target_pairs={{0,2},{1,3},{2,0},{3,1},{4,6},{5,7},{6,4},{7,5},{8,10},{9,11},{10,... | collective-permute-start | bytes 1572872 | tf_op jit(solution)/shard_map/ppermute | solution.py:422
  12.8 4.9 %collective-permute-done = bf16[256,1024]{1,0:T(8,128)(2,1)} collective-permute-done((bf16[256,1024]{1,0:T(8,128)(2,1)S(1)}, bf16[256,1024]{1,0:T(8,128)(2,1)}, u32[]{:S(2)}, u32[]{:S(2)}) %collective-permute-start) | collective-permute-done | bytes 524320 | tf_op jit(solution)/shard_map/ppermute | solution.py:422
  17.7 11.8 %collective-permute-done.1 = bf16[256,1024]{1,0:T(8,128)(2,1)S(1)} collective-permute-done((bf16[256,1024]{1,0:T(8,128)(2,1)S(1)}, bf16[256,1024]{1,0:T(8,128)(2,1)S(1)}, u32[]{:S(2)}, u32[]{:S(2)}) %collective-permute-start.1) | collective-permute-done | bytes 524320 | tf_op jit(solution)/shard_map/ppermute | solution.py:422
  29.6 1.6 %collective-permute-start.6 = (bf16[256,1024]{1,0:T(8,128)(2,1)S(1)}, bf16[256,1024]{1,0:T(8,128)(2,1)S(1)}, u32[]{:S(2)}, u32[]{:S(2)}) collective-permute-start(bf16[256,1024]{1,0:T(8,128)(2,1)S(1)} %select_select_fusion.3), channel_id=1, source_target_pairs={{0,16},{1,17},{2,18},{3,19},{4,20},{5,21},{6,22},{7,23},{8,24},{9,... | collective-permute-start | bytes 1572872 | tf_op jit(solution)/shard_map/ppermute | solution.py:422
  31.2 1.8 %collective-permute-start.2 = (bf16[256,1024]{1,0:T(8,128)(2,1)}, bf16[256,1024]{1,0:T(8,128)(2,1)}, u32[]{:S(2)}, u32[]{:S(2)}) collective-permute-start(bf16[256,1024]{1,0:T(8,128)(2,1)} %collective-permute-done), channel_id=1, source_target_pairs={{0,8},{1,9},{2,10},{3,11},{4,0},{5,1},{6,2},{7,3},{8,12},{9,13},{1... | collective-permute-start | bytes 1572872 | tf_op jit(solution)/shard_map/ppermute | solution.py:422
  33.0 2.1 %collective-permute-done.4.refs_5_ = bf16[1024,256]{1,0:T(8,128)(2,1)S(1)} collective-permute-done((bf16[1024,256]{1,0:T(8,128)(2,1)S(1)}, bf16[1024,256]{1,0:T(8,128)(2,1)S(1)}, u32[]{:S(2)}, u32[]{:S(2)}) %collective-permute-start.4) | collective-permute-done | bytes 524320 | tf_op jit(solution)/shard_map/ppermute | solution.py:422
  37.4 1.6 %collective-permute-start.7 = (bf16[1024,256]{1,0:T(8,128)(2,1)S(1)}, bf16[1024,256]{1,0:T(8,128)(2,1)S(1)}, u32[]{:S(2)}, u32[]{:S(2)}) collective-permute-start(bf16[1024,256]{1,0:T(8,128)(2,1)S(1)} %collective-permute-done.4.refs_5_), channel_id=1, source_target_pairs={{0,2},{1,3},{2,0},{3,1},{4,6},{5,7},{6,4},{7,5},{8,10},{9,11},{10,... | collective-permute-start | bytes 1572872 | tf_op jit(solution)/shard_map/ppermute | solution.py:422
  39.0 9.8 %short_range.1.refs_6_.refs_2_.refs_1_ = f32[2048,512]{1,0:T(8,128)} custom-call(s32[1]{0:T(128)} %bitcast.1.half_ref, s32[32]{0:T(128)S(1)} %get-tuple-element.55.live_ref, s32[32]{0:T(128)S(1)} %get-tuple-element.54.sub_ref, f32[3,32]{1,0:T(4,128)S(1)} %pad_maximum_fusion.1.meta_ref, bf16[128,4096]{1,0:T(8,128)(2,1)} %basis_ref.1, f32[1,4096]{1,0:T(1,128)S(1)} %bitcast.39, ...), custom_call_target="tpu_custom_call" | custom-call | flops 4294967296 | bytes 1 | tf_op jit(solution)/shard_map/short_range/pallas_call | solution.py:127
  49.0 1.9 %select_select_fusion.2 = bf16[256,1024]{1,0:T(8,128)(2,1)} fusion(bf16[256,1024]{1,0:T(8,128)(2,1)} %collective-permute-done, bf16[256,1024]{1,0:T(8,128)(2,1)} %collective-permute-done.2, bf16[256,1024]{1,0:T(8,128)(2,1)} %copy-done.7, pred[]{:T(512)S(6)} %eq.71, pred[]{:T(512)S(6)} %eq.64), kind=kLoop, calls=%fused_computation.6 | loop fusion | flops 524288 | bytes 2097154 | tf_op jit(solution)/shard_map/jit(_where)/select_n | solution.py:456
  51.7 1.4 %long_range.4 = bf16[256,512]{1,0:T(8,128)(2,1)} custom-call(bf16[256,1024]{1,0:T(8,128)(2,1)S(1)} %select_select_fusion.1.refs_0_, bf16[256,1024]{1,0:T(8,128)(2,1)S(1)} %collective-permute-done.6.refs_1_, bf16[1024,256]{1,0:T(8,128)(2,1)S(1)} %collective-permute-done.5.refs_2_, bf16[1024,256]{1,0:T(8,128)(2,1)S(1)} %collective-permute-done.7.refs_3_), custom_call_target="tpu_custom_call" | custom-call | flops 1 | bytes 1 | tf_op jit(solution)/shard_map/long_range/pallas_call | solution.py:195
  53.1 1.6 %collective-permute-start.15 = (bf16[256,512]{1,0:T(8,128)(2,1)}, bf16[256,512]{1,0:T(8,128)(2,1)S(1)}, u32[]{:S(2)}, u32[]{:S(2)}) collective-permute-start(bf16[256,512]{1,0:T(8,128)(2,1)} %long_range.4), channel_id=1, source_target_pairs={{0,2},{1,3},{2,0},{3,1},{4,6},{5,7},{6,4},{7,5},{8,10},{9,11},{10,... | collective-permute-start | bytes 786440 | tf_op jit(solution)/shard_map/ppermute | solution.py:422
  54.7 2.6 %long_range.5 = bf16[256,512]{1,0:T(8,128)(2,1)} custom-call(bf16[256,1024]{1,0:T(8,128)(2,1)} %collective-permute-done.8.refs_0_.refs_2_, bf16[256,1024]{1,0:T(8,128)(2,1)} %collective-permute-done.9.refs_1_.refs_3_, bf16[1024,256]{1,0:T(8,128)(2,1)S(1)} %collective-permute-done.5.refs_2_, bf16[1024,256]{1,0:T(8,128)(2,1)S(1)} %collective-permute-done.7.refs_3_), custom_call_target="tpu_custom_call" | custom-call | flops 1 | bytes 1 | tf_op jit(solution)/shard_map/long_range/pallas_call | solution.py:195
  59.1 6.3 %collective-permute-done.11.refs_1_ = bf16[256,1024]{1,0:T(8,128)(2,1)} collective-permute-done((bf16[256,1024]{1,0:T(8,128)(2,1)}, bf16[256,1024]{1,0:T(8,128)(2,1)}, u32[]{:S(2)}, u32[]{:S(2)}) %collective-permute-start.11) | collective-permute-done | bytes 524320 | tf_op jit(solution)/shard_map/ppermute | solution.py:422
  65.6 2.5 %long_range.7 = bf16[256,512]{1,0:T(8,128)(2,1)} custom-call(bf16[256,1024]{1,0:T(8,128)(2,1)S(1)} %select_select_fusion.refs_0_, bf16[256,1024]{1,0:T(8,128)(2,1)} %collective-permute-done.11.refs_1_, bf16[1024,512]{1,0:T(8,128)(2,1)S(1)} %get-tuple-element.60.refs_2_, bf16[1024,512]{1,0:T(8,128)(2,1)S(1)} %get-tuple-element.61.refs_3_), custom_call_target="tpu_custom_call" | custom-call | flops 1 | bytes 1 | tf_op jit(solution)/shard_map/long_range/pallas_call | solution.py:195
  68.8 1.5 %long_range.6 = bf16[256,512]{1,0:T(8,128)(2,1)} custom-call(bf16[256,1024]{1,0:T(8,128)(2,1)S(1)} %collective-permute-done.10.refs_0_.refs_2_, bf16[256,1024]{1,0:T(8,128)(2,1)S(1)} %collective-permute-done.12.refs_1_.refs_3_, bf16[1024,512]{1,0:T(8,128)(2,1)S(1)} %get-tuple-element.60.refs_2_, bf16[1024,512]{1,0:T(8,128)(2,1)S(1)} %get-tuple-element.61.refs_3_), custom_call_target="tpu_custom_call" | custom-call | flops 1 | bytes 1 | tf_op jit(solution)/shard_map/long_range/pallas_call | solution.py:195
  70.2 1.6 %collective-permute-start.13 = (bf16[256,512]{1,0:T(8,128)(2,1)}, bf16[256,512]{1,0:T(8,128)(2,1)S(1)}, u32[]{:S(2)}, u32[]{:S(2)}) collective-permute-start(bf16[256,512]{1,0:T(8,128)(2,1)} %long_range.6), channel_id=1, source_target_pairs={{0,2},{1,3},{2,0},{3,1},{4,6},{5,7},{6,4},{7,5},{8,10},{9,11},{10,... | collective-permute-start | bytes 786440 | tf_op jit(solution)/shard_map/ppermute | solution.py:422
  72.0 4.8 %own_sum.2.refs_7_ = bf16[2048,2,256]{2,1,0:T(2,128)(2,1)} custom-call(s32[2]{0:T(128)S(1)} %pad_add_fusion.4.order_ref, bf16[256,1024]{1,0:T(8,128)(2,1)S(1)} %select_select_fusion.1.refs_0_, bf16[256,1024]{1,0:T(8,128)(2,1)S(1)} %copy-done.1, bf16[256,1024]{1,0:T(8,128)(2,1)} %collective-permute-done.8.refs_0_.refs_2_, ...), custom_call_target="tpu_custom_call" | custom-call | flops 1 | bytes 1 | tf_op jit(solution)/shard_map/own_sum/pallas_call | solution.py:251
  76.8 4.5 %own_sum.3.refs_3_ = bf16[2048,2,256]{2,1,0:T(2,128)(2,1)} custom-call(s32[2]{0:T(128)S(1)} %pad_add_fusion.3.order_ref, bf16[256,1024]{1,0:T(8,128)(2,1)S(1)} %select_select_fusion.refs_0_, bf16[256,1024]{1,0:T(8,128)(2,1)} %collective-permute-done.11.refs_1_, bf16[256,1024]{1,0:T(8,128)(2,1)S(1)} %copy-done.3, ...), custom_call_target="tpu_custom_call", output_to_operand_aliasing={{}: (8, {})} | custom-call | flops 1 | bytes 1 | tf_op jit(solution)/shard_map/own_sum/pallas_call | solution.py:251
  81.4 3.2 %final_sum.3.refs_2_ = bf16[2048,2,256]{2,1,0:T(2,128)(2,1)} custom-call(s32[2]{0:T(128)S(1)} %pad_add_fusion.2.order_ref, bf16[256,512]{1,0:T(8,128)(2,1)S(1)} %collective-permute-done.15.refs_0_, bf16[256,512]{1,0:T(8,128)(2,1)} %collective-permute-done.16.refs_1_, f32[2048,512]{1,0:T(8,128)} %short_range.1.refs_6_.refs_2_.refs_1_, ...), custom_call_target="tpu_custom_call", output_to_operand_aliasing={{}: (4, {})} | custom-call | flops 1 | bytes 1 | tf_op jit(solution)/shard_map/final_sum/pallas_call | solution.py:301
  84.6 2.0 %final_sum.4.refs_2_ = bf16[2048,2,256]{2,1,0:T(2,128)(2,1)} custom-call(s32[1]{0:T(128)} %bitcast.18.order_ref, bf16[256,512]{1,0:T(8,128)(2,1)S(1)} %collective-permute-done.14.refs_0_, f32[2048,512]{1,0:T(8,128)} %short_range.1.refs_6_.refs_2_.refs_1_, bf16[2048,2,256]{2,1,0:T(2,128)(2,1)} %final_sum.3.refs_2_), custom_call_target="tpu_custom_call", output_to_operand_aliasing={{}: (3, {})} | custom-call | flops 1 | bytes 1 | tf_op jit(solution)/shard_map/final_sum/pallas_call | solution.py:301
  86.6 2.0 %final_sum.5 = bf16[2048,2,256]{2,1,0:T(2,128)(2,1)} custom-call(s32[1]{0:T(128)} %bitcast.order_ref, bf16[256,512]{1,0:T(8,128)(2,1)S(1)} %collective-permute-done.13.refs_0_, f32[2048,512]{1,0:T(8,128)} %short_range.1.refs_6_.refs_2_.refs_1_, bf16[2048,2,256]{2,1,0:T(2,128)(2,1)} %final_sum.4.refs_2_), custom_call_target="tpu_custom_call", output_to_operand_aliasing={{}: (3, {})} | custom-call | flops 1 | bytes 1 | tf_op jit(solution)/shard_map/final_sum/pallas_call | solution.py:301
  (77 shorter events, 9.7 us)
Async XLA Ops:
  0.0 9.7 %copy-start.10 = (bf16[256,2,512]{2,1,0:T(2,128)(2,1)S(1)}, bf16[256,2,512]{2,1,0:T(2,128)(2,1)}, u32[]{:S(2)}) copy-start(bf16[256,2,512]{2,1,0:T(2,128)(2,1)} %param.11) | copy-start | bytes 1572868
  0.0 9.7 %copy-start.11 = (f32[512]{0:T(512)S(1)}, f32[512]{0:T(512)}, u32[]{:S(2)}) copy-start(f32[512]{0:T(512)} %param.13) | copy-start | bytes 6148
  1.2 28.3 %copy-start.9 = (bf16[32,8,2,512]{3,1,2,0:T(8,128)(2,1)}, bf16[32,8,2,512]{3,1,2,0:T(8,128)(2,1)S(1)}, u32[]{:S(2)}) copy-start(bf16[32,8,2,512]{3,1,2,0:T(8,128)(2,1)S(1)} %copy.20) | copy-start | bytes 1572868
  1.2 16.5 %collective-permute-start = (bf16[256,1024]{1,0:T(8,128)(2,1)S(1)}, bf16[256,1024]{1,0:T(8,128)(2,1)}, u32[]{:S(2)}, u32[]{:S(2)}) collective-permute-start(bf16[256,1024]{1,0:T(8,128)(2,1)S(1)} %bitcast.40), channel_id=1, source_target_pairs={{0,8},{1,9},{2,10},{3,11},{4,0},{5,1},{6,2},{7,3},{8,12},{9,13},{1... | collective-permute-start | bytes 1572872 | tf_op jit(solution)/shard_map/ppermute | solution.py:422
  5.3 24.2 %collective-permute-start.1 = (bf16[256,1024]{1,0:T(8,128)(2,1)S(1)}, bf16[256,1024]{1,0:T(8,128)(2,1)S(1)}, u32[]{:S(2)}, u32[]{:S(2)}) collective-permute-start(bf16[256,1024]{1,0:T(8,128)(2,1)S(1)} %bitcast.41), channel_id=1, source_target_pairs={{0,4},{1,5},{2,6},{3,7},{4,12},{5,13},{6,14},{7,15},{8,0},{9,1},{1... | collective-permute-start | bytes 1572872 | tf_op jit(solution)/shard_map/ppermute | solution.py:422
  8.2 27.7 %copy-start.14 = (f32[125]{0:T(128)S(1)}, f32[125]{0:T(128)}, u32[]{:S(2)}) copy-start(f32[125]{0:T(128)} %param.16) | copy-start | bytes 1504
  8.2 27.7 %copy-start.15 = (f32[125]{0:T(128)S(1)}, f32[125]{0:T(128)}, u32[]{:S(2)}) copy-start(f32[125]{0:T(128)} %param.17) | copy-start | bytes 1504
  8.2 26.9 %collective-permute-start.3 = (bf16[17,128,128]{2,1,0:T(8,128)(2,1)}, bf16[17,128,128]{2,1,0:T(8,128)(2,1)}, u32[]{:S(2)}, u32[]{:S(2)}) collective-permute-start(bf16[17,128,128]{2,1,0:T(8,128)(2,1)} %pad_maximum_fusion.refs_0_), channel_id=1, source_target_pairs={{0,16},{1,17},{2,18},{3,19},{4,20},{5,21},{6,22},{7,23},{8,24},{9,... | collective-permute-start | bytes 1671176 | tf_op jit(solution)/shard_map/ppermute | solution.py:422
  10.7 22.3 %collective-permute-start.5 = (bf16[1024,256]{1,0:T(8,128)(2,1)S(1)}, bf16[1024,256]{1,0:T(8,128)(2,1)S(1)}, u32[]{:S(2)}, u32[]{:S(2)}) collective-permute-start(bf16[1024,256]{1,0:T(8,128)(2,1)S(1)} %bitcast.35), channel_id=1, source_target_pairs={{0,2},{1,3},{2,0},{3,1},{4,6},{5,7},{6,4},{7,5},{8,10},{9,11},{10,... | collective-permute-start | bytes 1572872 | tf_op jit(solution)/shard_map/ppermute | solution.py:422
  12.2 22.9 %collective-permute-start.4 = (bf16[1024,256]{1,0:T(8,128)(2,1)S(1)}, bf16[1024,256]{1,0:T(8,128)(2,1)S(1)}, u32[]{:S(2)}, u32[]{:S(2)}) collective-permute-start(bf16[1024,256]{1,0:T(8,128)(2,1)S(1)} %bitcast.36), channel_id=1, source_target_pairs={{0,16},{1,17},{2,18},{3,19},{4,20},{5,21},{6,22},{7,23},{8,24},{9,... | collective-permute-start | bytes 1572872 | tf_op jit(solution)/shard_map/ppermute | solution.py:422
  12.8 26.2 %copy-start.6 = (f32[4096]{0:T(1024)S(1)}, f32[4096]{0:T(1024)}, u32[]{:S(2)}) copy-start(f32[4096]{0:T(1024)} %param.15) | copy-start | bytes 49156
  29.5 7.7 %copy-start.7 = (bf16[256,1024]{1,0:T(8,128)(2,1)}, bf16[256,1024]{1,0:T(8,128)(2,1)S(1)}, u32[]{:S(2)}) copy-start(bf16[256,1024]{1,0:T(8,128)(2,1)S(1)} %collective-permute-done.1) | copy-start | bytes 1572868
  29.6 19.2 %collective-permute-start.6 = (bf16[256,1024]{1,0:T(8,128)(2,1)S(1)}, bf16[256,1024]{1,0:T(8,128)(2,1)S(1)}, u32[]{:S(2)}, u32[]{:S(2)}) collective-permute-start(bf16[256,1024]{1,0:T(8,128)(2,1)S(1)} %select_select_fusion.3), channel_id=1, source_target_pairs={{0,16},{1,17},{2,18},{3,19},{4,20},{5,21},{6,22},{7,23},{8,24},{9,... | collective-permute-start | bytes 1572872 | tf_op jit(solution)/shard_map/ppermute | solution.py:422
  31.2 17.9 %collective-permute-start.2 = (bf16[256,1024]{1,0:T(8,128)(2,1)}, bf16[256,1024]{1,0:T(8,128)(2,1)}, u32[]{:S(2)}, u32[]{:S(2)}) collective-permute-start(bf16[256,1024]{1,0:T(8,128)(2,1)} %collective-permute-done), channel_id=1, source_target_pairs={{0,8},{1,9},{2,10},{3,11},{4,0},{5,1},{6,2},{7,3},{8,12},{9,13},{1... | collective-permute-start | bytes 1572872 | tf_op jit(solution)/shard_map/ppermute | solution.py:422
  37.3 17.5 %collective-permute-start.8 = (bf16[256,1024]{1,0:T(8,128)(2,1)S(1)}, bf16[256,1024]{1,0:T(8,128)(2,1)}, u32[]{:S(2)}, u32[]{:S(2)}) collective-permute-start(bf16[256,1024]{1,0:T(8,128)(2,1)S(1)} %select_select_fusion.1.refs_0_), channel_id=1, source_target_pairs={{0,1},{1,0},{2,3},{3,2},{4,5},{5,4},{6,7},{7,6},{8,9},{9,8},{10,11... | collective-permute-start | bytes 1572872 | tf_op jit(solution)/shard_map/ppermute | solution.py:422
  37.4 14.3 %collective-permute-start.7 = (bf16[1024,256]{1,0:T(8,128)(2,1)S(1)}, bf16[1024,256]{1,0:T(8,128)(2,1)S(1)}, u32[]{:S(2)}, u32[]{:S(2)}) collective-permute-start(bf16[1024,256]{1,0:T(8,128)(2,1)S(1)} %collective-permute-done.4.refs_5_), channel_id=1, source_target_pairs={{0,2},{1,3},{2,0},{3,1},{4,6},{5,7},{6,4},{7,5},{8,10},{9,11},{10,... | collective-permute-start | bytes 1572872 | tf_op jit(solution)/shard_map/ppermute | solution.py:422
  48.8 6.0 %collective-permute-start.9 = (bf16[256,1024]{1,0:T(8,128)(2,1)S(1)}, bf16[256,1024]{1,0:T(8,128)(2,1)}, u32[]{:S(2)}, u32[]{:S(2)}) collective-permute-start(bf16[256,1024]{1,0:T(8,128)(2,1)S(1)} %collective-permute-done.6.refs_1_), channel_id=1, source_target_pairs={{0,1},{1,0},{2,3},{3,2},{4,5},{5,4},{6,7},{7,6},{8,9},{9,8},{10,11... | collective-permute-start | bytes 1572872 | tf_op jit(solution)/shard_map/ppermute | solution.py:422
  50.9 14.5 %collective-permute-start.11 = (bf16[256,1024]{1,0:T(8,128)(2,1)}, bf16[256,1024]{1,0:T(8,128)(2,1)}, u32[]{:S(2)}, u32[]{:S(2)}) collective-permute-start(bf16[256,1024]{1,0:T(8,128)(2,1)} %select_select_fusion.2), channel_id=1, source_target_pairs={{0,16},{1,17},{2,18},{3,19},{4,20},{5,21},{6,22},{7,23},{8,24},{9,... | collective-permute-start | bytes 1572872 | tf_op jit(solution)/shard_map/ppermute | solution.py:422
  53.1 28.3 %collective-permute-start.15 = (bf16[256,512]{1,0:T(8,128)(2,1)}, bf16[256,512]{1,0:T(8,128)(2,1)S(1)}, u32[]{:S(2)}, u32[]{:S(2)}) collective-permute-start(bf16[256,512]{1,0:T(8,128)(2,1)} %long_range.4), channel_id=1, source_target_pairs={{0,2},{1,3},{2,0},{3,1},{4,6},{5,7},{6,4},{7,5},{8,10},{9,11},{10,... | collective-permute-start | bytes 786440 | tf_op jit(solution)/shard_map/ppermute | solution.py:422
  57.4 24.0 %collective-permute-start.16 = (bf16[256,512]{1,0:T(8,128)(2,1)}, bf16[256,512]{1,0:T(8,128)(2,1)}, u32[]{:S(2)}, u32[]{:S(2)}) collective-permute-start(bf16[256,512]{1,0:T(8,128)(2,1)} %long_range.5), channel_id=1, source_target_pairs={{0,2},{1,3},{2,0},{3,1},{4,6},{5,7},{6,4},{7,5},{8,10},{9,11},{10,... | collective-permute-start | bytes 786440 | tf_op jit(solution)/shard_map/ppermute | solution.py:422
  59.1 9.7 %collective-permute-start.10 = (bf16[256,1024]{1,0:T(8,128)(2,1)S(1)}, bf16[256,1024]{1,0:T(8,128)(2,1)S(1)}, u32[]{:S(2)}, u32[]{:S(2)}) collective-permute-start(bf16[256,1024]{1,0:T(8,128)(2,1)S(1)} %select_select_fusion.refs_0_), channel_id=1, source_target_pairs={{0,1},{1,0},{2,3},{3,2},{4,5},{5,4},{6,7},{7,6},{8,9},{9,8},{10,11... | collective-permute-start | bytes 1572872 | tf_op jit(solution)/shard_map/ppermute | solution.py:422
  65.4 3.3 %collective-permute-start.12 = (bf16[256,1024]{1,0:T(8,128)(2,1)}, bf16[256,1024]{1,0:T(8,128)(2,1)S(1)}, u32[]{:S(2)}, u32[]{:S(2)}) collective-permute-start(bf16[256,1024]{1,0:T(8,128)(2,1)} %collective-permute-done.11.refs_1_), channel_id=1, source_target_pairs={{0,1},{1,0},{2,3},{3,2},{4,5},{5,4},{6,7},{7,6},{8,9},{9,8},{10,11... | collective-permute-start | bytes 1572872 | tf_op jit(solution)/shard_map/ppermute | solution.py:422
  68.1 16.4 %collective-permute-start.14 = (bf16[256,512]{1,0:T(8,128)(2,1)}, bf16[256,512]{1,0:T(8,128)(2,1)S(1)}, u32[]{:S(2)}, u32[]{:S(2)}) collective-permute-start(bf16[256,512]{1,0:T(8,128)(2,1)} %long_range.7), channel_id=1, source_target_pairs={{0,2},{1,3},{2,0},{3,1},{4,6},{5,7},{6,4},{7,5},{8,10},{9,11},{10,... | collective-permute-start | bytes 786440 | tf_op jit(solution)/shard_map/ppermute | solution.py:422
  70.2 16.3 %collective-permute-start.13 = (bf16[256,512]{1,0:T(8,128)(2,1)}, bf16[256,512]{1,0:T(8,128)(2,1)S(1)}, u32[]{:S(2)}, u32[]{:S(2)}) collective-permute-start(bf16[256,512]{1,0:T(8,128)(2,1)} %long_range.6), channel_id=1, source_target_pairs={{0,2},{1,3},{2,0},{3,1},{4,6},{5,7},{6,4},{7,5},{8,10},{9,11},{10,... | collective-permute-start | bytes 786440 | tf_op jit(solution)/shard_map/ppermute | solution.py:422
  (9 other events, 43.4 us)

commit v14 on v13

--- a/solution.py
+++ b/solution.py
@@ -11,7 +11,7 @@
 CORES = 2
 SMALL_COST = pl.CostEstimate(flops=1, bytes_accessed=1, transcendentals=0)
 GROUP_ITEMS = 4
-SHORT_VMEM_BYTES = 20 * 1024 * 1024
+SHORT_VMEM_BYTES = 24 * 1024 * 1024
 VMEM_BYTES = 10 * 1024 * 1024
 
 
@@ -20,12 +20,21 @@
 
 
 def short_kernel(
-    half_ref, live_ref, sub_ref, meta_ref, basis_ref, decay_ref, *refs, share, subs, depth, width
+    half_ref, live_ref, sub_ref, meta_ref, basis_ref, decay_ref, *refs, share, subs, depth, width, adds
 ):
-    items, scratch = refs[:-10], refs[-10:]
+    if adds:
+        *refs, before, before_sem = refs
+    items, scratch = refs[: -10 - adds], refs[-10:]
     out_ref, basis, left, acc, made, dists, group_sub, cursor, basis_sem, out_sem = scratch
     slots = share * len(items)
     row_count = out_ref.shape[0]
+    tile = made.shape[1]
+    tiles = list(enumerate(range(0, row_count, tile)))
+    before_copies = []
+    for n, t in tiles if adds else []:
+        source = refs[-11].at[pl.ds(t, tile), :]
+        before_copies.append(pltpu.make_async_copy(source, before.at[n], before_sem.at[n]))
+        before_copies[-1].start()
     mine = pl.ds(pl.multiple_of(half_ref[0] * row_count, row_count), row_count)
     basis_copy = pltpu.make_async_copy(basis_ref.at[:, mine], basis, basis_sem)
     basis_copy.start()
@@ -79,7 +88,6 @@
 
         lax.fori_loop(0, share, place, 0)
 
-    tile = min(row_count, made.shape[1])
     decay = decay_ref[:, mine]
     basis_copy.wait()
 
@@ -104,32 +112,39 @@
 
     lax.fori_loop(0, first, one_group, 0)
     copies = []
-    for n, t in enumerate(range(0, row_count, tile)):
+    for n, t in tiles:
+        if adds:
+            before_copies[n].wait()
         for s in range(subs):
             for c in range(2):
                 column = (c * subs + s) * width
-                made[n, :, column : column + width] = acc[
-                    s, c * width : (c + 1) * width, t : t + tile
-                ].T
+                part = acc[s, c * width : (c + 1) * width, t : t + tile].T
+                if adds:
+                    part = part + before[n, :, column : column + width]
+                made[n, :, column : column + width] = part
         copies.append(pltpu.make_async_copy(made.at[n], out_ref.at[pl.ds(t, tile), :], out_sem.at[n]))
         copies[-1].start()
     for copy in copies:
         copy.wait()
 
 
-def short_range(half, live, sub_ids, meta, aux_basis, aux_decay, items, row_count, subs):
+def short_range(half, live, sub_ids, meta, aux_basis, aux_decay, items, row_count, subs, earlier=None):
+    adds = earlier is not None
     _, width, depth = items[0].shape
     slots = live.shape[0]
     share = slots // len(items)
     groups = slots // GROUP_ITEMS + subs
     tile = min(row_count, 512)
-    kernel = functools.partial(short_kernel, share=share, subs=subs, depth=depth, width=width)
+    kernel = functools.partial(
+        short_kernel, share=share, subs=subs, depth=depth, width=width, adds=adds
+    )
     return pl.pallas_call(
         kernel,
         out_shape=pltpu.HBM((row_count, 2 * subs * width), jnp.float32),
         in_specs=[pl.BlockSpec(memory_space=pltpu.SMEM)] * 4
         + [pl.BlockSpec(memory_space=pltpu.HBM)]
-        + [pl.BlockSpec(memory_space=pltpu.VMEM)] * (1 + len(items)),
+        + [pl.BlockSpec(memory_space=pltpu.VMEM)] * (1 + len(items))
+        + [pl.BlockSpec(memory_space=pltpu.HBM)] * adds,
         out_specs=pl.BlockSpec(memory_space=pltpu.HBM),
         scratch_shapes=[
             pltpu.VMEM((depth, row_count), jnp.bfloat16),
@@ -141,13 +156,26 @@
             pltpu.SMEM((subs,), jnp.int32),
             pltpu.SemaphoreType.DMA,
             pltpu.SemaphoreType.DMA((row_count // tile,)),
-        ],
+        ]
+        + [
+            pltpu.VMEM((row_count // tile, tile, 2 * subs * width), jnp.float32),
+            pltpu.SemaphoreType.DMA((row_count // tile,)),
+        ][: 2 * adds],
         compiler_params=pltpu.CompilerParams(vmem_limit_bytes=SHORT_VMEM_BYTES),
         cost_estimate=pl.CostEstimate(
             flops=4 * row_count * slots * depth * width, bytes_accessed=1, transcendentals=0
         ),
         name="short_range",
-    )(half, live, sub_ids, meta, in_hbm(aux_basis), aux_decay.reshape(1, -1), *items)
+    )(
+        half,
+        live,
+        sub_ids,
+        meta,
+        in_hbm(aux_basis),
+        aux_decay.reshape(1, -1),
+        *items,
+        *([in_hbm(earlier)] if adds else []),
+    )
 
 
 def long_kernel(*refs, blocks, chains, pieces, width):
@@ -376,7 +404,7 @@
     length = chips // breadth
 
     aux_flat = aux_ft.reshape(rows, 2 * local_g)
-    pairs = after(pair_ft, aux_flat).astype(jnp.float32)
+    pairs = pair_ft.astype(jnp.float32)
     weighted = (pairs * coul_weight[None, None, :]).astype(jnp.bfloat16)
     turned = weighted.reshape(local_rows, 2 * local_g).T
     item_rows = jnp.swapaxes(item_pair, 1, 2)
@@ -487,20 +515,25 @@
         away[n].extend(made)
         arriving[n].append([over_y(v, s) for s, v in enumerate(made, 1)])
 
-    moved = foreign(0)
+    def short_part(slots, items, earlier=None):
+        images, sub_ids, live = slots
+        table = slot_table(image_dist, image_phase, images)
+        return short_range(
+            half, live, sub_ids, table, aux_basis, aux_decay, [items], row_count, subs, earlier
+        )
+
+    short = short_part(slots, after(packed, *(pair[0] for pair in factors[1:])))
+
+    moved = foreign(0, short)
     begun = [turned_x, items_x, *(pair[0] for pair in factors[1:])]
     for k in range(2, length // 2 + 1):
-        held[k] = along(after(held[k - 1], held[1], held[length - 1]), 1)
+        held[k] = along(after(held[k - 1], held[1], held[length - 1], short), 1)
     for k in range(2, (length + 1) // 2):
-        held[length - k] = along(after(held[length - k + 1], held[1], held[length - 1]), -1)
+        held[length - k] = along(after(held[length - k + 1], held[1], held[length - 1], short), -1)
     for s in range(1, breadth):
         factors[s].append(over_y(after(turned_x, theirs[0], *begun), s))
-    slots_x = read_slots(after(items_x, theirs[0], *begun), slots)
-    seen, sub_ids, live = jnp.concatenate([slots, slots_x], axis=1)
-    table = slot_table(image_dist, image_phase, seen)
-    short = short_range(
-        half, live, sub_ids, table, aux_basis, aux_decay, [packed, items_x], row_count, subs
-    )
+
+    short = short_part(read_slots(after(items_x, theirs[0], *begun), slots), items_x, short)
 
     out = None
     for n in range(home):
@@ -508,7 +541,7 @@
             moved = foreign(n, theirs[n - 1], *(away[n - 2] if n > 1 else [short]))
         away.append([])
         arriving.append([])
-        mine.append(with_cores(pick(False, n, theirs[n], *(away[n - 1] if n else begun))))
+        mine.append(with_cores(pick(False, n, theirs[n], *([*away[n - 1], out] if n else begun))))
         away_factors = factors[1:]
         if n:
             away_factors = [[both_parts(after(v, *away[0])) for v in pair] for pair in factors[1:]]

time: 89.5 us -> 84.3 us (0.942)
  waiting for transfers between devices: 25.3 us -> 7.62 us
  Pallas kernels: 34.2 us -> 39 us
  starting transfers between devices: 18 us -> 22 us
  local copies, waits for them, and re-layouts: 3.13 us -> 6.01 us
    ppermute x17, waiting for transfers between devices: 25.3 us -> 7.62 us  [send(): return lax.ppermute(value, AXES, pairs)]
    pallas_call x1 -> x2, Pallas kernels: 9.78 us -> 15.1 us  [short_range(): pl.pallas_call(kernel, out_shape=pltpu.HBM((row_count, 2 * subs * width),...]
    ppermute x17, starting transfers between devices: 18 us -> 22 us  [send(): return lax.ppermute(value, AXES, pairs)]
    unnamed x34 -> x24, local copies, waits for them, and re-layouts: 2.54 us -> 5.38 us
    convert_element_type x1, other arithmetic: 0.41 us -> 1.45 us  [body(): weighted = (pairs * coul_weight[None, None, :]).astype(jnp.bfloat16)]
  transfers between devices with their start and end apart: 17 -> 17, of which waited for: 5 -> 2; matrix products, arithmetic and copies ran while one was open for 10% -> 11% of each run, Pallas kernels for 36% -> 44%
where the time goes in v14:
time: 84.3 us; the launch traced here: 83.6 us
  Pallas kernels  39 us (46%)
  starting transfers between devices  22 us (26%)
  waiting for transfers between devices  7.62 us (9%)
  other arithmetic  7.61 us (9%)
  local copies, waits for them, and re-layouts  6.01 us (7%)
  between operations  1.31 us (2%)
    ppermute x17, starting transfers between devices, send(): return lax.ppermute(value, AXES, pairs)  22 us
    pallas_call x2, Pallas kernels, short_range(): pl.pallas_call(kernel, out_shape=pltpu.HBM((row_count, 2 * subs * width),...  15.1 us
    pallas_call x2, Pallas kernels, own_sum(): pl.pallas_call(functools.partial(own_kernel, blocks=count, chains=chains,...  8.87 us
    pallas_call x4, Pallas kernels, long_range(): pl.pallas_call(functools.partial(long_kernel, blocks=len(blocks), chains=...  7.94 us
    ppermute x17, waiting for transfers between devices, send(): return lax.ppermute(value, AXES, pairs)  7.62 us
    pallas_call x3, Pallas kernels, final_sum(): pl.pallas_call(functools.partial(final_kernel, pieces=count, blocks=block...  7.11 us
    unnamed x24, local copies, waits for them, and re-layouts  5.38 us
    select_n x4, other arithmetic, pick(): value = jnp.where(wanted == k, block, value)  4.41 us
  transfers between devices with their start and end apart: 17, of which 2 were waited for; matrix products, arithmetic and copies ran while one was open for 11% of the time, Pallas kernels for 44%

profile of v14, /device:TPU:0, one launch (start us, length us, event | category | flops | bytes accessed | tf_op | source)
XLA Modules:
  0.0 83.6 jit_solution(11239786754895518404)
XLA Ops:
  0.0 1.9 %copy.20 = bf16[32,8,2,512]{3,1,2,0:T(8,128)(2,1)} copy(bf16[32,8,2,512]{3,2,1,0:T(2,128)(2,1)} %bitcast.47) | data formatting | bytes 1048576
  2.0 3.0 %collective-permute-start.1 = (bf16[256,1024]{1,0:T(8,128)(2,1)}, bf16[256,1024]{1,0:T(8,128)(2,1)S(1)}, u32[]{:S(2)}, u32[]{:S(2)}) collective-permute-start(bf16[256,1024]{1,0:T(8,128)(2,1)} %bitcast.28), channel_id=1, source_target_pairs={{0,4},{1,5},{2,6},{3,7},{4,12},{5,13},{6,14},{7,15},{8,0},{9,1},{1... | collective-permute-start | bytes 1572872 | tf_op jit(solution)/shard_map/ppermute | solution.py:450
  6.1 1.5 %multiply_convert_fusion = bf16[256,2,512]{2,1,0:T(2,128)(2,1)S(1)} fusion(bf16[256,2,512]{2,1,0:T(2,128)(2,1)} %param.11, f32[512]{0:T(512)} %param.13), kind=kLoop, calls=%fused_computation.2 | loop fusion | flops 786432 | bytes 1050624 | tf_op jit(solution)/shard_map/convert_element_type | solution.py:408
  8.1 1.8 %collective-permute-start.5 = (bf16[1024,256]{1,0:T(8,128)(2,1)S(1)}, bf16[1024,256]{1,0:T(8,128)(2,1)S(1)}, u32[]{:S(2)}, u32[]{:S(2)}) collective-permute-start(bf16[1024,256]{1,0:T(8,128)(2,1)S(1)} %bitcast.39), channel_id=1, source_target_pairs={{0,16},{1,17},{2,18},{3,19},{4,20},{5,21},{6,22},{7,23},{8,24},{9,... | collective-permute-start | bytes 1572872 | tf_op jit(solution)/shard_map/ppermute | solution.py:450
  9.9 1.5 %collective-permute-start.2 = (bf16[1024,256]{1,0:T(8,128)(2,1)S(1)}, bf16[1024,256]{1,0:T(8,128)(2,1)S(1)}, u32[]{:S(2)}, u32[]{:S(2)}) collective-permute-start(bf16[1024,256]{1,0:T(8,128)(2,1)S(1)} %bitcast.40), channel_id=1, source_target_pairs={{0,2},{1,3},{2,0},{3,1},{4,6},{5,7},{6,4},{7,5},{8,10},{9,11},{10,... | collective-permute-start | bytes 1572872 | tf_op jit(solution)/shard_map/ppermute | solution.py:450
  12.1 1.3 %copy.18 = bf16[16,128,128]{1,2,0:T(8,128)(2,1)S(1)} copy(bf16[16,128,128]{2,1,0:T(8,128)(2,1)} %param.18) | data formatting | bytes 1048576 | tf_op args[7]
  15.2 7.5 %collective-permute-done.2.refs_2_ = bf16[1024,256]{1,0:T(8,128)(2,1)S(1)} collective-permute-done((bf16[1024,256]{1,0:T(8,128)(2,1)S(1)}, bf16[1024,256]{1,0:T(8,128)(2,1)S(1)}, u32[]{:S(2)}, u32[]{:S(2)}) %collective-permute-start.2) | collective-permute-done | bytes 524320 | tf_op jit(solution)/shard_map/ppermute | solution.py:450
  22.7 6.7 %short_range.2.refs_1_ = f32[2048,512]{1,0:T(8,128)} custom-call(s32[1]{0:T(128)} %bitcast.1.half_ref, s32[16]{0:T(128)S(1)} %compare_convert_fusion.1.live_ref, s32[16]{0:T(128)S(1)} %copy-done.5, f32[3,16]{1,0:T(4,128)S(1)} %pad_maximum_fusion.1.meta_ref, bf16[128,4096]{1,0:T(8,128)(2,1)} %basis_ref.3, f32[1,4096]{1,0:T(1,128)S(1)} %bitcast.43, ...), custom_call_target="tpu_custom_call" | custom-call | flops 2147483648 | bytes 1 | tf_op jit(solution)/shard_map/short_range/pallas_call | solution.py:141
  29.6 2.7 %collective-permute-start.6 = (bf16[256,1024]{1,0:T(8,128)(2,1)S(1)}, bf16[256,1024]{1,0:T(8,128)(2,1)}, u32[]{:S(2)}, u32[]{:S(2)}) collective-permute-start(bf16[256,1024]{1,0:T(8,128)(2,1)S(1)} %select_select_fusion.3), channel_id=1, source_target_pairs={{0,16},{1,17},{2,18},{3,19},{4,20},{5,21},{6,22},{7,23},{8,24},{9,... | collective-permute-start | bytes 1572872 | tf_op jit(solution)/shard_map/ppermute | solution.py:450
  32.2 2.5 %collective-permute-start.3 = (bf16[256,1024]{1,0:T(8,128)(2,1)}, bf16[256,1024]{1,0:T(8,128)(2,1)}, u32[]{:S(2)}, u32[]{:S(2)}) collective-permute-start(bf16[256,1024]{1,0:T(8,128)(2,1)} %collective-permute-done), channel_id=1, source_target_pairs={{0,8},{1,9},{2,10},{3,11},{4,0},{5,1},{6,2},{7,3},{8,12},{9,13},{1... | collective-permute-start | bytes 1572872 | tf_op jit(solution)/shard_map/ppermute | solution.py:450
  34.9 1.3 %select_select_fusion.1.refs_0_ = bf16[256,1024]{1,0:T(8,128)(2,1)S(1)} fusion(bf16[256,1024]{1,0:T(8,128)(2,1)} %bitcast.28, bf16[256,1024]{1,0:T(8,128)(2,1)} %collective-permute-done, bf16[256,1024]{1,0:T(8,128)(2,1)} %copy-done.6, pred[]{:T(512)S(6)} %eq.82, pred[]{:T(512)S(6)} %eq.81), kind=kLoop, calls=%fused_computation.5 | loop fusion | flops 524288 | bytes 2097154 | tf_op jit(solution)/shard_map/jit(_where)/select_n | solution.py:484
  37.5 8.4 %short_range.3.refs_6_.refs_2_.refs_1_ = f32[2048,512]{1,0:T(8,128)} custom-call(s32[1]{0:T(128)} %bitcast.1.half_ref, s32[16]{0:T(128)S(1)} %get-tuple-element.57.live_ref, s32[16]{0:T(128)S(1)} %get-tuple-element.56.sub_ref, f32[3,16]{1,0:T(4,128)S(1)} %pad_maximum_fusion.2.meta_ref, bf16[128,4096]{1,0:T(8,128)(2,1)} %basis_ref.3, f32[1,4096]{1,0:T(1,128)S(1)} %bitcast.44, ...), custom_call_target="tpu_custom_call" | custom-call | flops 2147483648 | bytes 1 | tf_op jit(solution)/shard_map/short_range/pallas_call | solution.py:141
  46.1 1.9 %select_select_fusion.2 = bf16[256,1024]{1,0:T(8,128)(2,1)} fusion(bf16[256,1024]{1,0:T(8,128)(2,1)} %collective-permute-done, bf16[256,1024]{1,0:T(8,128)(2,1)} %collective-permute-done.3, bf16[256,1024]{1,0:T(8,128)(2,1)} %copy-done.6, pred[]{:T(512)S(6)} %eq.80, pred[]{:T(512)S(6)} %eq.73), kind=kLoop, calls=%fused_computation.6 | loop fusion | flops 524288 | bytes 2097154 | tf_op jit(solution)/shard_map/jit(_where)/select_n | solution.py:484
  48.0 2.8 %collective-permute-start.11 = (bf16[256,1024]{1,0:T(8,128)(2,1)}, bf16[256,1024]{1,0:T(8,128)(2,1)S(1)}, u32[]{:S(2)}, u32[]{:S(2)}) collective-permute-start(bf16[256,1024]{1,0:T(8,128)(2,1)} %select_select_fusion.2), channel_id=1, source_target_pairs={{0,16},{1,17},{2,18},{3,19},{4,20},{5,21},{6,22},{7,23},{8,24},{9,... | collective-permute-start | bytes 1572872 | tf_op jit(solution)/shard_map/ppermute | solution.py:450
  50.8 2.5 %long_range.4 = bf16[256,512]{1,0:T(8,128)(2,1)} custom-call(bf16[256,1024]{1,0:T(8,128)(2,1)S(1)} %select_select_fusion.1.refs_0_, bf16[256,1024]{1,0:T(8,128)(2,1)} %collective-permute-done.6.refs_1_, bf16[1024,256]{1,0:T(8,128)(2,1)S(1)} %collective-permute-done.2.refs_2_, bf16[1024,256]{1,0:T(8,128)(2,1)S(1)} %collective-permute-done.7.refs_3_), custom_call_target="tpu_custom_call" | custom-call | flops 1 | bytes 1 | tf_op jit(solution)/shard_map/long_range/pallas_call | solution.py:223
  54.2 2.6 %long_range.5 = bf16[256,512]{1,0:T(8,128)(2,1)} custom-call(bf16[256,1024]{1,0:T(8,128)(2,1)} %collective-permute-done.8.refs_0_.refs_2_, bf16[256,1024]{1,0:T(8,128)(2,1)} %collective-permute-done.9.refs_1_.refs_3_, bf16[1024,256]{1,0:T(8,128)(2,1)S(1)} %collective-permute-done.2.refs_2_, bf16[1024,256]{1,0:T(8,128)(2,1)S(1)} %collective-permute-done.7.refs_3_), custom_call_target="tpu_custom_call" | custom-call | flops 1 | bytes 1 | tf_op jit(solution)/shard_map/long_range/pallas_call | solution.py:223
  58.1 4.8 %own_sum.2.refs_7_ = bf16[2048,2,256]{2,1,0:T(2,128)(2,1)} custom-call(s32[2]{0:T(128)S(1)} %pad_add_fusion.1.order_ref, bf16[256,1024]{1,0:T(8,128)(2,1)S(1)} %select_select_fusion.1.refs_0_, bf16[256,1024]{1,0:T(8,128)(2,1)} %collective-permute-done.6.refs_1_, bf16[256,1024]{1,0:T(8,128)(2,1)} %collective-permute-done.8.refs_0_.refs_2_, ...), custom_call_target="tpu_custom_call" | custom-call | flops 1 | bytes 1 | tf_op jit(solution)/shard_map/own_sum/pallas_call | solution.py:279
  64.9 1.4 %long_range.7 = bf16[256,512]{1,0:T(8,128)(2,1)} custom-call(bf16[256,1024]{1,0:T(8,128)(2,1)S(1)} %select_select_fusion.refs_0_, bf16[256,1024]{1,0:T(8,128)(2,1)S(1)} %collective-permute-done.11.refs_1_, bf16[1024,512]{1,0:T(8,128)(2,1)S(1)} %get-tuple-element.64.refs_2_, bf16[1024,512]{1,0:T(8,128)(2,1)S(1)} %get-tuple-element.65.refs_3_), custom_call_target="tpu_custom_call" | custom-call | flops 1 | bytes 1 | tf_op jit(solution)/shard_map/long_range/pallas_call | solution.py:223
  67.3 1.4 %long_range.6 = bf16[256,512]{1,0:T(8,128)(2,1)} custom-call(bf16[256,1024]{1,0:T(8,128)(2,1)S(1)} %collective-permute-done.10.refs_0_.refs_2_, bf16[256,1024]{1,0:T(8,128)(2,1)S(1)} %collective-permute-done.12.refs_1_.refs_3_, bf16[1024,512]{1,0:T(8,128)(2,1)S(1)} %get-tuple-element.64.refs_2_, bf16[1024,512]{1,0:T(8,128)(2,1)S(1)} %get-tuple-element.65.refs_3_), custom_call_target="tpu_custom_call" | custom-call | flops 1 | bytes 1 | tf_op jit(solution)/shard_map/long_range/pallas_call | solution.py:223
  68.8 1.2 %collective-permute-start.13 = (bf16[256,512]{1,0:T(8,128)(2,1)}, bf16[256,512]{1,0:T(8,128)(2,1)S(1)}, u32[]{:S(2)}, u32[]{:S(2)}) collective-permute-start(bf16[256,512]{1,0:T(8,128)(2,1)} %long_range.6), channel_id=1, source_target_pairs={{0,2},{1,3},{2,0},{3,1},{4,6},{5,7},{6,4},{7,5},{8,10},{9,11},{10,... | collective-permute-start | bytes 786440 | tf_op jit(solution)/shard_map/ppermute | solution.py:450
  72.2 4.0 %own_sum.3.refs_3_ = bf16[2048,2,256]{2,1,0:T(2,128)(2,1)} custom-call(s32[2]{0:T(128)S(1)} %pad_add_fusion.3.order_ref, bf16[256,1024]{1,0:T(8,128)(2,1)S(1)} %select_select_fusion.refs_0_, bf16[256,1024]{1,0:T(8,128)(2,1)S(1)} %collective-permute-done.11.refs_1_, bf16[256,1024]{1,0:T(8,128)(2,1)S(1)} %copy-done.1, ...), custom_call_target="tpu_custom_call", output_to_operand_aliasing={{}: (8, {})} | custom-call | flops 1 | bytes 1 | tf_op jit(solution)/shard_map/own_sum/pallas_call | solution.py:279
  76.3 3.2 %final_sum.3.refs_2_ = bf16[2048,2,256]{2,1,0:T(2,128)(2,1)} custom-call(s32[2]{0:T(128)S(1)} %pad_add_fusion.2.order_ref, bf16[256,512]{1,0:T(8,128)(2,1)S(1)} %collective-permute-done.15.refs_0_, bf16[256,512]{1,0:T(8,128)(2,1)} %collective-permute-done.16.refs_1_, f32[2048,512]{1,0:T(8,128)} %short_range.3.refs_6_.refs_2_.refs_1_, ...), custom_call_target="tpu_custom_call", output_to_operand_aliasing={{}: (4, {})} | custom-call | flops 1 | bytes 1 | tf_op jit(solution)/shard_map/final_sum/pallas_call | solution.py:329
  79.5 2.0 %final_sum.4.refs_2_ = bf16[2048,2,256]{2,1,0:T(2,128)(2,1)} custom-call(s32[1]{0:T(128)} %bitcast.22.order_ref, bf16[256,512]{1,0:T(8,128)(2,1)S(1)} %collective-permute-done.14.refs_0_, f32[2048,512]{1,0:T(8,128)} %short_range.3.refs_6_.refs_2_.refs_1_, bf16[2048,2,256]{2,1,0:T(2,128)(2,1)} %final_sum.3.refs_2_), custom_call_target="tpu_custom_call", output_to_operand_aliasing={{}: (3, {})} | custom-call | flops 1 | bytes 1 | tf_op jit(solution)/shard_map/final_sum/pallas_call | solution.py:329
  81.5 2.0 %final_sum.5 = bf16[2048,2,256]{2,1,0:T(2,128)(2,1)} custom-call(s32[1]{0:T(128)} %bitcast.order_ref, bf16[256,512]{1,0:T(8,128)(2,1)S(1)} %collective-permute-done.13.refs_0_, f32[2048,512]{1,0:T(8,128)} %short_range.3.refs_6_.refs_2_.refs_1_, bf16[2048,2,256]{2,1,0:T(2,128)(2,1)} %final_sum.4.refs_2_), custom_call_target="tpu_custom_call", output_to_operand_aliasing={{}: (3, {})} | custom-call | flops 1 | bytes 1 | tf_op jit(solution)/shard_map/final_sum/pallas_call | solution.py:329
  (71 shorter events, 12.3 us)
Async XLA Ops:
  0.0 13.4 %copy-start.5 = (s32[16]{0:T(128)S(1)}, s32[16]{0:T(128)}, u32[]{:S(2)}) copy-start(s32[16]{0:T(128)} %sub_ref.1) | copy-start | bytes 196
  0.0 13.4 %copy-start.8 = (s32[16]{0:T(128)S(1)}, s32[16]{0:T(128)}, u32[]{:S(2)}) copy-start(s32[16]{0:T(128)} %param.19) | copy-start | bytes 196
  2.0 12.9 %copy-start.9 = (f32[125]{0:T(128)S(1)}, f32[125]{0:T(128)}, u32[]{:S(2)}) copy-start(f32[125]{0:T(128)} %param.16) | copy-start | bytes 1504
  2.0 12.9 %copy-start.10 = (f32[125]{0:T(128)S(1)}, f32[125]{0:T(128)}, u32[]{:S(2)}) copy-start(f32[125]{0:T(128)} %param.17) | copy-start | bytes 1504
  2.0 20.8 %copy-start.4 = (f32[4096]{0:T(1024)S(1)}, f32[4096]{0:T(1024)}, u32[]{:S(2)}) copy-start(f32[4096]{0:T(1024)} %param.15) | copy-start | bytes 49156
  2.0 27.5 %collective-permute-start.1 = (bf16[256,1024]{1,0:T(8,128)(2,1)}, bf16[256,1024]{1,0:T(8,128)(2,1)S(1)}, u32[]{:S(2)}, u32[]{:S(2)}) collective-permute-start(bf16[256,1024]{1,0:T(8,128)(2,1)} %bitcast.28), channel_id=1, source_target_pairs={{0,4},{1,5},{2,6},{3,7},{4,12},{5,13},{6,14},{7,15},{8,0},{9,1},{1... | collective-permute-start | bytes 1572872 | tf_op jit(solution)/shard_map/ppermute | solution.py:450
  5.0 24.5 %collective-permute-start = (bf16[256,1024]{1,0:T(8,128)(2,1)}, bf16[256,1024]{1,0:T(8,128)(2,1)}, u32[]{:S(2)}, u32[]{:S(2)}) collective-permute-start(bf16[256,1024]{1,0:T(8,128)(2,1)} %bitcast.28), channel_id=1, source_target_pairs={{0,8},{1,9},{2,10},{3,11},{4,0},{5,1},{6,2},{7,3},{8,12},{9,13},{1... | collective-permute-start | bytes 1572872 | tf_op jit(solution)/shard_map/ppermute | solution.py:450
  8.1 26.6 %collective-permute-start.5 = (bf16[1024,256]{1,0:T(8,128)(2,1)S(1)}, bf16[1024,256]{1,0:T(8,128)(2,1)S(1)}, u32[]{:S(2)}, u32[]{:S(2)}) collective-permute-start(bf16[1024,256]{1,0:T(8,128)(2,1)S(1)} %bitcast.39), channel_id=1, source_target_pairs={{0,16},{1,17},{2,18},{3,19},{4,20},{5,21},{6,22},{7,23},{8,24},{9,... | collective-permute-start | bytes 1572872 | tf_op jit(solution)/shard_map/ppermute | solution.py:450
  9.9 12.8 %collective-permute-start.2 = (bf16[1024,256]{1,0:T(8,128)(2,1)S(1)}, bf16[1024,256]{1,0:T(8,128)(2,1)S(1)}, u32[]{:S(2)}, u32[]{:S(2)}) collective-permute-start(bf16[1024,256]{1,0:T(8,128)(2,1)S(1)} %bitcast.40), channel_id=1, source_target_pairs={{0,2},{1,3},{2,0},{3,1},{4,6},{5,7},{6,4},{7,5},{8,10},{9,11},{10,... | collective-permute-start | bytes 1572872 | tf_op jit(solution)/shard_map/ppermute | solution.py:450
  14.3 20.4 %collective-permute-start.4 = (bf16[17,128,128]{2,1,0:T(8,128)(2,1)}, bf16[17,128,128]{2,1,0:T(8,128)(2,1)S(1)}, u32[]{:S(2)}, u32[]{:S(2)}) collective-permute-start(bf16[17,128,128]{2,1,0:T(8,128)(2,1)} %pad_maximum_fusion.refs_0_), channel_id=1, source_target_pairs={{0,16},{1,17},{2,18},{3,19},{4,20},{5,21},{6,22},{7,23},{8,24},{9,... | collective-permute-start | bytes 1671176 | tf_op jit(solution)/shard_map/ppermute | solution.py:450
  29.4 5.3 %copy-start.6 = (bf16[256,1024]{1,0:T(8,128)(2,1)}, bf16[256,1024]{1,0:T(8,128)(2,1)S(1)}, u32[]{:S(2)}) copy-start(bf16[256,1024]{1,0:T(8,128)(2,1)S(1)} %collective-permute-done.1) | copy-start | bytes 1572868
  29.6 16.3 %collective-permute-start.6 = (bf16[256,1024]{1,0:T(8,128)(2,1)S(1)}, bf16[256,1024]{1,0:T(8,128)(2,1)}, u32[]{:S(2)}, u32[]{:S(2)}) collective-permute-start(bf16[256,1024]{1,0:T(8,128)(2,1)S(1)} %select_select_fusion.3), channel_id=1, source_target_pairs={{0,16},{1,17},{2,18},{3,19},{4,20},{5,21},{6,22},{7,23},{8,24},{9,... | collective-permute-start | bytes 1572872 | tf_op jit(solution)/shard_map/ppermute | solution.py:450
  32.2 13.8 %collective-permute-start.3 = (bf16[256,1024]{1,0:T(8,128)(2,1)}, bf16[256,1024]{1,0:T(8,128)(2,1)}, u32[]{:S(2)}, u32[]{:S(2)}) collective-permute-start(bf16[256,1024]{1,0:T(8,128)(2,1)} %collective-permute-done), channel_id=1, source_target_pairs={{0,8},{1,9},{2,10},{3,11},{4,0},{5,1},{6,2},{7,3},{8,12},{9,13},{1... | collective-permute-start | bytes 1572872 | tf_op jit(solution)/shard_map/ppermute | solution.py:450
  36.2 18.0 %collective-permute-start.8 = (bf16[256,1024]{1,0:T(8,128)(2,1)S(1)}, bf16[256,1024]{1,0:T(8,128)(2,1)}, u32[]{:S(2)}, u32[]{:S(2)}) collective-permute-start(bf16[256,1024]{1,0:T(8,128)(2,1)S(1)} %select_select_fusion.1.refs_0_), channel_id=1, source_target_pairs={{0,1},{1,0},{2,3},{3,2},{4,5},{5,4},{6,7},{7,6},{8,9},{9,8},{10,11... | collective-permute-start | bytes 1572872 | tf_op jit(solution)/shard_map/ppermute | solution.py:450
  36.3 14.5 %collective-permute-start.7 = (bf16[1024,256]{1,0:T(8,128)(2,1)S(1)}, bf16[1024,256]{1,0:T(8,128)(2,1)S(1)}, u32[]{:S(2)}, u32[]{:S(2)}) collective-permute-start(bf16[1024,256]{1,0:T(8,128)(2,1)S(1)} %collective-permute-done.5.refs_5_), channel_id=1, source_target_pairs={{0,2},{1,3},{2,0},{3,1},{4,6},{5,7},{6,4},{7,5},{8,10},{9,11},{10,... | collective-permute-start | bytes 1572872 | tf_op jit(solution)/shard_map/ppermute | solution.py:450
  45.9 8.3 %collective-permute-start.9 = (bf16[256,1024]{1,0:T(8,128)(2,1)}, bf16[256,1024]{1,0:T(8,128)(2,1)}, u32[]{:S(2)}, u32[]{:S(2)}) collective-permute-start(bf16[256,1024]{1,0:T(8,128)(2,1)} %collective-permute-done.6.refs_1_), channel_id=1, source_target_pairs={{0,1},{1,0},{2,3},{3,2},{4,5},{5,4},{6,7},{7,6},{8,9},{9,8},{10,11... | collective-permute-start | bytes 1572872 | tf_op jit(solution)/shard_map/ppermute | solution.py:450
  48.0 16.2 %collective-permute-start.11 = (bf16[256,1024]{1,0:T(8,128)(2,1)}, bf16[256,1024]{1,0:T(8,128)(2,1)S(1)}, u32[]{:S(2)}, u32[]{:S(2)}) collective-permute-start(bf16[256,1024]{1,0:T(8,128)(2,1)} %select_select_fusion.2), channel_id=1, source_target_pairs={{0,16},{1,17},{2,18},{3,19},{4,20},{5,21},{6,22},{7,23},{8,24},{9,... | collective-permute-start | bytes 1572872 | tf_op jit(solution)/shard_map/ppermute | solution.py:450
  53.3 23.0 %collective-permute-start.15 = (bf16[256,512]{1,0:T(8,128)(2,1)}, bf16[256,512]{1,0:T(8,128)(2,1)S(1)}, u32[]{:S(2)}, u32[]{:S(2)}) collective-permute-start(bf16[256,512]{1,0:T(8,128)(2,1)} %long_range.4), channel_id=1, source_target_pairs={{0,2},{1,3},{2,0},{3,1},{4,6},{5,7},{6,4},{7,5},{8,10},{9,11},{10,... | collective-permute-start | bytes 786440 | tf_op jit(solution)/shard_map/ppermute | solution.py:450
  56.9 6.1 %copy-start.7 = (bf16[256,1024]{1,0:T(8,128)(2,1)S(1)}, bf16[256,1024]{1,0:T(8,128)(2,1)}, u32[]{:S(2)}) copy-start(bf16[256,1024]{1,0:T(8,128)(2,1)} %copy-done.6) | copy-start | bytes 1572868
  56.9 19.4 %collective-permute-start.16 = (bf16[256,512]{1,0:T(8,128)(2,1)}, bf16[256,512]{1,0:T(8,128)(2,1)}, u32[]{:S(2)}, u32[]{:S(2)}) collective-permute-start(bf16[256,512]{1,0:T(8,128)(2,1)} %long_range.5), channel_id=1, source_target_pairs={{0,2},{1,3},{2,0},{3,1},{4,6},{5,7},{6,4},{7,5},{8,10},{9,11},{10,... | collective-permute-start | bytes 786440 | tf_op jit(solution)/shard_map/ppermute | solution.py:450
  64.1 3.2 %collective-permute-start.10 = (bf16[256,1024]{1,0:T(8,128)(2,1)S(1)}, bf16[256,1024]{1,0:T(8,128)(2,1)S(1)}, u32[]{:S(2)}, u32[]{:S(2)}) collective-permute-start(bf16[256,1024]{1,0:T(8,128)(2,1)S(1)} %select_select_fusion.refs_0_), channel_id=1, source_target_pairs={{0,1},{1,0},{2,3},{3,2},{4,5},{5,4},{6,7},{7,6},{8,9},{9,8},{10,11... | collective-permute-start | bytes 1572872 | tf_op jit(solution)/shard_map/ppermute | solution.py:450
  64.2 3.1 %collective-permute-start.12 = (bf16[256,1024]{1,0:T(8,128)(2,1)S(1)}, bf16[256,1024]{1,0:T(8,128)(2,1)S(1)}, u32[]{:S(2)}, u32[]{:S(2)}) collective-permute-start(bf16[256,1024]{1,0:T(8,128)(2,1)S(1)} %collective-permute-done.11.refs_1_), channel_id=1, source_target_pairs={{0,1},{1,0},{2,3},{3,2},{4,5},{5,4},{6,7},{7,6},{8,9},{9,8},{10,11... | collective-permute-start | bytes 1572872 | tf_op jit(solution)/shard_map/ppermute | solution.py:450
  66.4 13.1 %collective-permute-start.14 = (bf16[256,512]{1,0:T(8,128)(2,1)}, bf16[256,512]{1,0:T(8,128)(2,1)S(1)}, u32[]{:S(2)}, u32[]{:S(2)}) collective-permute-start(bf16[256,512]{1,0:T(8,128)(2,1)} %long_range.7), channel_id=1, source_target_pairs={{0,2},{1,3},{2,0},{3,1},{4,6},{5,7},{6,4},{7,5},{8,10},{9,11},{10,... | collective-permute-start | bytes 786440 | tf_op jit(solution)/shard_map/ppermute | solution.py:450
  68.8 12.7 %collective-permute-start.13 = (bf16[256,512]{1,0:T(8,128)(2,1)}, bf16[256,512]{1,0:T(8,128)(2,1)S(1)}, u32[]{:S(2)}, u32[]{:S(2)}) collective-permute-start(bf16[256,512]{1,0:T(8,128)(2,1)} %long_range.6), channel_id=1, source_target_pairs={{0,2},{1,3},{2,0},{3,1},{4,6},{5,7},{6,4},{7,5},{8,10},{9,11},{10,... | collective-permute-start | bytes 786440 | tf_op jit(solution)/shard_map/ppermute | solution.py:450
  (4 other events, 5.0 us)

commit v15 on v14

--- a/solution.py
+++ b/solution.py
@@ -11,7 +11,7 @@
 CORES = 2
 SMALL_COST = pl.CostEstimate(flops=1, bytes_accessed=1, transcendentals=0)
 GROUP_ITEMS = 4
-SHORT_VMEM_BYTES = 24 * 1024 * 1024
+SHORT_VMEM_BYTES = 20 * 1024 * 1024
 VMEM_BYTES = 10 * 1024 * 1024
 
 
@@ -20,26 +20,22 @@
 
 
 def short_kernel(
-    half_ref, live_ref, sub_ref, meta_ref, basis_ref, decay_ref, *refs, share, subs, depth, width, adds
+    half_ref, live_ref, sub_ref, meta_ref, basis_ref, decay_ref, *refs, share, subs, depth, width, adds, finishes
 ):
-    if adds:
-        *refs, before, before_sem = refs
     items, scratch = refs[: -10 - adds], refs[-10:]
     out_ref, basis, left, acc, made, dists, group_sub, cursor, basis_sem, out_sem = scratch
     slots = share * len(items)
-    row_count = out_ref.shape[0]
+    row_count = acc.shape[2]
     tile = made.shape[1]
-    tiles = list(enumerate(range(0, row_count, tile)))
-    before_copies = []
-    for n, t in tiles if adds else []:
-        source = refs[-11].at[pl.ds(t, tile), :]
-        before_copies.append(pltpu.make_async_copy(source, before.at[n], before_sem.at[n]))
-        before_copies[-1].start()
+    if adds:
+        acc_copy = pltpu.make_async_copy(refs[-11], acc, out_sem.at[0])
+        acc_copy.start()
+    else:
+        acc[...] = jnp.zeros_like(acc)
     mine = pl.ds(pl.multiple_of(half_ref[0] * row_count, row_count), row_count)
     basis_copy = pltpu.make_async_copy(basis_ref.at[:, mine], basis, basis_sem)
     basis_copy.start()
     left[...] = jnp.zeros_like(left)
-    acc[...] = jnp.zeros_like(acc)
 
     for s in range(subs):
         cursor[s] = 0
@@ -90,6 +86,8 @@
 
     decay = decay_ref[:, mine]
     basis_copy.wait()
+    if adds:
+        acc_copy.wait()
 
     def one_group(group, carry):
         s = group_sub[group]
@@ -111,24 +109,26 @@
         return carry
 
     lax.fori_loop(0, first, one_group, 0)
+    if not finishes:
+        acc_copy = pltpu.make_async_copy(acc, out_ref, out_sem.at[0])
+        acc_copy.start()
+        acc_copy.wait()
+        return
     copies = []
-    for n, t in tiles:
-        if adds:
-            before_copies[n].wait()
+    for n, t in enumerate(range(0, row_count, tile)):
         for s in range(subs):
             for c in range(2):
                 column = (c * subs + s) * width
-                part = acc[s, c * width : (c + 1) * width, t : t + tile].T
-                if adds:
-                    part = part + before[n, :, column : column + width]
-                made[n, :, column : column + width] = part
+                made[n, :, column : column + width] = acc[
+                    s, c * width : (c + 1) * width, t : t + tile
+                ].T
         copies.append(pltpu.make_async_copy(made.at[n], out_ref.at[pl.ds(t, tile), :], out_sem.at[n]))
         copies[-1].start()
     for copy in copies:
         copy.wait()
 
 
-def short_range(half, live, sub_ids, meta, aux_basis, aux_decay, items, row_count, subs, earlier=None):
+def short_range(half, live, sub_ids, meta, aux_basis, aux_decay, items, row_count, subs, earlier=None, finishes=True):
     adds = earlier is not None
     _, width, depth = items[0].shape
     slots = live.shape[0]
@@ -136,11 +136,13 @@
     groups = slots // GROUP_ITEMS + subs
     tile = min(row_count, 512)
     kernel = functools.partial(
-        short_kernel, share=share, subs=subs, depth=depth, width=width, adds=adds
+        short_kernel, share=share, subs=subs, depth=depth, width=width, adds=adds, finishes=finishes
     )
     return pl.pallas_call(
         kernel,
-        out_shape=pltpu.HBM((row_count, 2 * subs * width), jnp.float32),
+        out_shape=pltpu.HBM(
+            (row_count, 2 * subs * width) if finishes else (subs, 2 * width, row_count), jnp.float32
+        ),
         in_specs=[pl.BlockSpec(memory_space=pltpu.SMEM)] * 4
         + [pl.BlockSpec(memory_space=pltpu.HBM)]
         + [pl.BlockSpec(memory_space=pltpu.VMEM)] * (1 + len(items))
@@ -156,11 +158,7 @@
             pltpu.SMEM((subs,), jnp.int32),
             pltpu.SemaphoreType.DMA,
             pltpu.SemaphoreType.DMA((row_count // tile,)),
-        ]
-        + [
-            pltpu.VMEM((row_count // tile, tile, 2 * subs * width), jnp.float32),
-            pltpu.SemaphoreType.DMA((row_count // tile,)),
-        ][: 2 * adds],
+        ],
         compiler_params=pltpu.CompilerParams(vmem_limit_bytes=SHORT_VMEM_BYTES),
         cost_estimate=pl.CostEstimate(
             flops=4 * row_count * slots * depth * width, bytes_accessed=1, transcendentals=0
@@ -515,14 +513,14 @@
         away[n].extend(made)
         arriving[n].append([over_y(v, s) for s, v in enumerate(made, 1)])
 
-    def short_part(slots, items, earlier=None):
+    def short_part(slots, items, *how):
         images, sub_ids, live = slots
         table = slot_table(image_dist, image_phase, images)
         return short_range(
-            half, live, sub_ids, table, aux_basis, aux_decay, [items], row_count, subs, earlier
+            half, live, sub_ids, table, aux_basis, aux_decay, [items], row_count, subs, *how
         )
 
-    short = short_part(slots, after(packed, *(pair[0] for pair in factors[1:])))
+    short = short_part(slots, packed, None, False)
 
     moved = foreign(0, short)
     begun = [turned_x, items_x, *(pair[0] for pair in factors[1:])]

time: 84.3 us -> 85.6 us (1.015)
  waiting for transfers between devices: 7.62 us -> 15 us
  starting transfers between devices: 22 us -> 18 us
  Pallas kernels: 39 us -> 37 us
    ppermute x17, waiting for transfers between devices: 7.62 us -> 15 us  [send(): return lax.ppermute(value, AXES, pairs)]
    ppermute x17, starting transfers between devices: 22 us -> 18 us  [send(): return lax.ppermute(value, AXES, pairs)]
    pallas_call x2, Pallas kernels: 15.1 us -> 13.1 us  [short_range(): pl.pallas_call(kernel, out_shape=pltpu.HBM((row_count, 2 * subs * width)...]
  transfers between devices with their start and end apart: 17 -> 17, of which waited for: 2 -> 4; matrix products, arithmetic and copies ran while one was open for 11% -> 11% of each run, Pallas kernels for 44% -> 41%
where the time goes in v15:
time: 85.6 us; the launch traced here: 84.8 us
  Pallas kernels  37 us (43%)
  starting transfers between devices  18 us (21%)
  waiting for transfers between devices  15 us (18%)
  other arithmetic  7.61 us (9%)
  local copies, waits for them, and re-layouts  6.01 us (7%)
  between operations  1.15 us (1%)
    ppermute x17, starting transfers between devices, send(): return lax.ppermute(value, AXES, pairs)  18 us
    ppermute x17, waiting for transfers between devices, send(): return lax.ppermute(value, AXES, pairs)  15 us
    pallas_call x2, Pallas kernels, short_range(): pl.pallas_call(kernel, out_shape=pltpu.HBM((row_count, 2 * subs * width)...  13.1 us
    pallas_call x2, Pallas kernels, own_sum(): pl.pallas_call(functools.partial(own_kernel, blocks=count, chains=chains,...  8.88 us
    pallas_call x4, Pallas kernels, long_range(): pl.pallas_call(functools.partial(long_kernel, blocks=len(blocks), chains=...  7.93 us
    pallas_call x3, Pallas kernels, final_sum(): pl.pallas_call(functools.partial(final_kernel, pieces=count, blocks=block...  7.11 us
    unnamed x24, local copies, waits for them, and re-layouts  5.38 us
    select_n x4, other arithmetic, pick(): value = jnp.where(wanted == k, block, value)  4.4 us
  transfers between devices with their start and end apart: 17, of which 4 were waited for; matrix products, arithmetic and copies ran while one was open for 11% of the time, Pallas kernels for 41%

profile of v15, /device:TPU:0, one launch (start us, length us, event | category | flops | bytes accessed | tf_op | source)
XLA Modules:
  0.0 84.8 jit_solution(10523259554777699560)
XLA Ops:
  0.0 1.9 %copy.20 = bf16[32,8,2,512]{3,1,2,0:T(8,128)(2,1)} copy(bf16[32,8,2,512]{3,2,1,0:T(2,128)(2,1)} %bitcast.47) | data formatting | bytes 1048576
  2.0 3.0 %collective-permute-start.1 = (bf16[256,1024]{1,0:T(8,128)(2,1)}, bf16[256,1024]{1,0:T(8,128)(2,1)S(1)}, u32[]{:S(2)}, u32[]{:S(2)}) collective-permute-start(bf16[256,1024]{1,0:T(8,128)(2,1)} %bitcast.28), channel_id=1, source_target_pairs={{0,4},{1,5},{2,6},{3,7},{4,12},{5,13},{6,14},{7,15},{8,0},{9,1},{1... | collective-permute-start | bytes 1572872 | tf_op jit(solution)/shard_map/ppermute | solution.py:448
  6.1 1.5 %multiply_convert_fusion = bf16[256,2,512]{2,1,0:T(2,128)(2,1)S(1)} fusion(bf16[256,2,512]{2,1,0:T(2,128)(2,1)} %param.11, f32[512]{0:T(512)} %param.13), kind=kLoop, calls=%fused_computation.2 | loop fusion | flops 786432 | bytes 1050624 | tf_op jit(solution)/shard_map/convert_element_type | solution.py:406
  8.1 1.9 %collective-permute-start.5 = (bf16[1024,256]{1,0:T(8,128)(2,1)S(1)}, bf16[1024,256]{1,0:T(8,128)(2,1)S(1)}, u32[]{:S(2)}, u32[]{:S(2)}) collective-permute-start(bf16[1024,256]{1,0:T(8,128)(2,1)S(1)} %bitcast.39), channel_id=1, source_target_pairs={{0,2},{1,3},{2,0},{3,1},{4,6},{5,7},{6,4},{7,5},{8,10},{9,11},{10,... | collective-permute-start | bytes 1572872 | tf_op jit(solution)/shard_map/ppermute | solution.py:448
  9.9 1.5 %collective-permute-start.4 = (bf16[1024,256]{1,0:T(8,128)(2,1)S(1)}, bf16[1024,256]{1,0:T(8,128)(2,1)S(1)}, u32[]{:S(2)}, u32[]{:S(2)}) collective-permute-start(bf16[1024,256]{1,0:T(8,128)(2,1)S(1)} %bitcast.40), channel_id=1, source_target_pairs={{0,16},{1,17},{2,18},{3,19},{4,20},{5,21},{6,22},{7,23},{8,24},{9,... | collective-permute-start | bytes 1572872 | tf_op jit(solution)/shard_map/ppermute | solution.py:448
  15.2 4.2 %short_range.2.refs_1_ = f32[2,256,2048]{2,1,0:T(8,128)} custom-call(s32[1]{0:T(128)} %bitcast.1.half_ref, s32[16]{0:T(128)S(1)} %compare_convert_fusion.1.live_ref, s32[16]{0:T(128)S(1)} %copy-done.5, f32[3,16]{1,0:T(4,128)S(1)} %pad_maximum_fusion.1.meta_ref, bf16[128,4096]{1,0:T(8,128)(2,1)} %basis_ref.3, f32[1,4096]{1,0:T(1,128)S(1)} %bitcast.43, ...), custom_call_target="tpu_custom_call" | custom-call | flops 2147483648 | bytes 1 | tf_op jit(solution)/shard_map/short_range/pallas_call | solution.py:141
  19.4 10.0 %collective-permute-done = bf16[256,1024]{1,0:T(8,128)(2,1)} collective-permute-done((bf16[256,1024]{1,0:T(8,128)(2,1)}, bf16[256,1024]{1,0:T(8,128)(2,1)}, u32[]{:S(2)}, u32[]{:S(2)}) %collective-permute-start) | collective-permute-done | bytes 524320 | tf_op jit(solution)/shard_map/ppermute | solution.py:448
  29.5 2.6 %collective-permute-start.6 = (bf16[256,1024]{1,0:T(8,128)(2,1)S(1)}, bf16[256,1024]{1,0:T(8,128)(2,1)}, u32[]{:S(2)}, u32[]{:S(2)}) collective-permute-start(bf16[256,1024]{1,0:T(8,128)(2,1)S(1)} %select_select_fusion.3), channel_id=1, source_target_pairs={{0,16},{1,17},{2,18},{3,19},{4,20},{5,21},{6,22},{7,23},{8,24},{9,... | collective-permute-start | bytes 1572872 | tf_op jit(solution)/shard_map/ppermute | solution.py:448
  32.2 1.7 %collective-permute-start.2 = (bf16[256,1024]{1,0:T(8,128)(2,1)}, bf16[256,1024]{1,0:T(8,128)(2,1)}, u32[]{:S(2)}, u32[]{:S(2)}) collective-permute-start(bf16[256,1024]{1,0:T(8,128)(2,1)} %collective-permute-done), channel_id=1, source_target_pairs={{0,8},{1,9},{2,10},{3,11},{4,0},{5,1},{6,2},{7,3},{8,12},{9,13},{1... | collective-permute-start | bytes 1572872 | tf_op jit(solution)/shard_map/ppermute | solution.py:448
  33.9 2.4 %collective-permute-done.3.refs_0_ = bf16[17,128,128]{2,1,0:T(8,128)(2,1)S(1)} collective-permute-done((bf16[17,128,128]{2,1,0:T(8,128)(2,1)}, bf16[17,128,128]{2,1,0:T(8,128)(2,1)S(1)}, u32[]{:S(2)}, u32[]{:S(2)}) %collective-permute-start.3) | collective-permute-done | bytes 557088 | tf_op jit(solution)/shard_map/ppermute | solution.py:448
  38.0 8.9 %short_range.3.refs_6_.refs_2_.refs_1_ = f32[2048,512]{1,0:T(8,128)} custom-call(s32[1]{0:T(128)} %bitcast.1.half_ref, s32[16]{0:T(128)S(1)} %get-tuple-element.55.live_ref, s32[16]{0:T(128)S(1)} %get-tuple-element.54.sub_ref, f32[3,16]{1,0:T(4,128)S(1)} %pad_maximum_fusion.2.meta_ref, bf16[128,4096]{1,0:T(8,128)(2,1)} %basis_ref.3, f32[1,4096]{1,0:T(1,128)S(1)} %bitcast.44, ...), custom_call_target="tpu_custom_call" | custom-call | flops 2147483648 | bytes 1 | tf_op jit(solution)/shard_map/short_range/pallas_call | solution.py:141
  47.0 1.9 %select_select_fusion.2 = bf16[256,1024]{1,0:T(8,128)(2,1)} fusion(bf16[256,1024]{1,0:T(8,128)(2,1)} %collective-permute-done, bf16[256,1024]{1,0:T(8,128)(2,1)} %collective-permute-done.2, bf16[256,1024]{1,0:T(8,128)(2,1)} %copy-done.6, pred[]{:T(512)S(6)} %eq.80, pred[]{:T(512)S(6)} %eq.73), kind=kLoop, calls=%fused_computation.6 | loop fusion | flops 524288 | bytes 2097154 | tf_op jit(solution)/shard_map/jit(_where)/select_n | solution.py:482
  49.7 2.5 %collective-permute-done.7.refs_3_ = bf16[1024,256]{1,0:T(8,128)(2,1)S(1)} collective-permute-done((bf16[1024,256]{1,0:T(8,128)(2,1)S(1)}, bf16[1024,256]{1,0:T(8,128)(2,1)S(1)}, u32[]{:S(2)}, u32[]{:S(2)}) %collective-permute-start.7) | collective-permute-done | bytes 524320 | tf_op jit(solution)/shard_map/ppermute | solution.py:448
  52.2 2.5 %long_range.4 = bf16[256,512]{1,0:T(8,128)(2,1)} custom-call(bf16[256,1024]{1,0:T(8,128)(2,1)S(1)} %select_select_fusion.1.refs_0_, bf16[256,1024]{1,0:T(8,128)(2,1)} %collective-permute-done.6.refs_1_, bf16[1024,256]{1,0:T(8,128)(2,1)S(1)} %collective-permute-done.5.refs_2_, bf16[1024,256]{1,0:T(8,128)(2,1)S(1)} %collective-permute-done.7.refs_3_), custom_call_target="tpu_custom_call" | custom-call | flops 1 | bytes 1 | tf_op jit(solution)/shard_map/long_range/pallas_call | solution.py:221
  55.0 2.6 %long_range.5 = bf16[256,512]{1,0:T(8,128)(2,1)} custom-call(bf16[256,1024]{1,0:T(8,128)(2,1)} %collective-permute-done.8.refs_0_.refs_2_, bf16[256,1024]{1,0:T(8,128)(2,1)} %collective-permute-done.9.refs_1_.refs_3_, bf16[1024,256]{1,0:T(8,128)(2,1)S(1)} %collective-permute-done.5.refs_2_, bf16[1024,256]{1,0:T(8,128)(2,1)S(1)} %collective-permute-done.7.refs_3_), custom_call_target="tpu_custom_call" | custom-call | flops 1 | bytes 1 | tf_op jit(solution)/shard_map/long_range/pallas_call | solution.py:221
  57.6 1.8 %collective-permute-start.16 = (bf16[256,512]{1,0:T(8,128)(2,1)}, bf16[256,512]{1,0:T(8,128)(2,1)}, u32[]{:S(2)}, u32[]{:S(2)}) collective-permute-start(bf16[256,512]{1,0:T(8,128)(2,1)} %long_range.5), channel_id=1, source_target_pairs={{0,2},{1,3},{2,0},{3,1},{4,6},{5,7},{6,4},{7,5},{8,10},{9,11},{10,... | collective-permute-start | bytes 786440 | tf_op jit(solution)/shard_map/ppermute | solution.py:448
  59.4 4.8 %own_sum.2.refs_7_ = bf16[2048,2,256]{2,1,0:T(2,128)(2,1)} custom-call(s32[2]{0:T(128)S(1)} %pad_add_fusion.1.order_ref, bf16[256,1024]{1,0:T(8,128)(2,1)S(1)} %select_select_fusion.1.refs_0_, bf16[256,1024]{1,0:T(8,128)(2,1)} %collective-permute-done.6.refs_1_, bf16[256,1024]{1,0:T(8,128)(2,1)} %collective-permute-done.8.refs_0_.refs_2_, ...), custom_call_target="tpu_custom_call" | custom-call | flops 1 | bytes 1 | tf_op jit(solution)/shard_map/own_sum/pallas_call | solution.py:277
  66.3 1.4 %long_range.7 = bf16[256,512]{1,0:T(8,128)(2,1)} custom-call(bf16[256,1024]{1,0:T(8,128)(2,1)S(1)} %select_select_fusion.refs_0_, bf16[256,1024]{1,0:T(8,128)(2,1)S(1)} %collective-permute-done.11.refs_1_, bf16[1024,512]{1,0:T(8,128)(2,1)S(1)} %get-tuple-element.62.refs_2_, bf16[1024,512]{1,0:T(8,128)(2,1)S(1)} %get-tuple-element.63.refs_3_), custom_call_target="tpu_custom_call" | custom-call | flops 1 | bytes 1 | tf_op jit(solution)/shard_map/long_range/pallas_call | solution.py:221
  68.1 1.4 %long_range.6 = bf16[256,512]{1,0:T(8,128)(2,1)} custom-call(bf16[256,1024]{1,0:T(8,128)(2,1)S(1)} %collective-permute-done.10.refs_0_.refs_2_, bf16[256,1024]{1,0:T(8,128)(2,1)S(1)} %collective-permute-done.12.refs_1_.refs_3_, bf16[1024,512]{1,0:T(8,128)(2,1)S(1)} %get-tuple-element.62.refs_2_, bf16[1024,512]{1,0:T(8,128)(2,1)S(1)} %get-tuple-element.63.refs_3_), custom_call_target="tpu_custom_call" | custom-call | flops 1 | bytes 1 | tf_op jit(solution)/shard_map/long_range/pallas_call | solution.py:221
  69.6 1.7 %collective-permute-start.13 = (bf16[256,512]{1,0:T(8,128)(2,1)}, bf16[256,512]{1,0:T(8,128)(2,1)S(1)}, u32[]{:S(2)}, u32[]{:S(2)}) collective-permute-start(bf16[256,512]{1,0:T(8,128)(2,1)} %long_range.6), channel_id=1, source_target_pairs={{0,2},{1,3},{2,0},{3,1},{4,6},{5,7},{6,4},{7,5},{8,10},{9,11},{10,... | collective-permute-start | bytes 786440 | tf_op jit(solution)/shard_map/ppermute | solution.py:448
  73.6 4.0 %own_sum.3.refs_3_ = bf16[2048,2,256]{2,1,0:T(2,128)(2,1)} custom-call(s32[2]{0:T(128)S(1)} %pad_add_fusion.3.order_ref, bf16[256,1024]{1,0:T(8,128)(2,1)S(1)} %select_select_fusion.refs_0_, bf16[256,1024]{1,0:T(8,128)(2,1)S(1)} %collective-permute-done.11.refs_1_, bf16[256,1024]{1,0:T(8,128)(2,1)S(1)} %copy-done.1, ...), custom_call_target="tpu_custom_call", output_to_operand_aliasing={{}: (8, {})} | custom-call | flops 1 | bytes 1 | tf_op jit(solution)/shard_map/own_sum/pallas_call | solution.py:277
  77.6 3.2 %final_sum.3.refs_2_ = bf16[2048,2,256]{2,1,0:T(2,128)(2,1)} custom-call(s32[2]{0:T(128)S(1)} %pad_add_fusion.2.order_ref, bf16[256,512]{1,0:T(8,128)(2,1)S(1)} %collective-permute-done.15.refs_0_, bf16[256,512]{1,0:T(8,128)(2,1)} %collective-permute-done.16.refs_1_, f32[2048,512]{1,0:T(8,128)} %short_range.3.refs_6_.refs_2_.refs_1_, ...), custom_call_target="tpu_custom_call", output_to_operand_aliasing={{}: (4, {})} | custom-call | flops 1 | bytes 1 | tf_op jit(solution)/shard_map/final_sum/pallas_call | solution.py:327
  80.8 2.0 %final_sum.4.refs_2_ = bf16[2048,2,256]{2,1,0:T(2,128)(2,1)} custom-call(s32[1]{0:T(128)} %bitcast.22.order_ref, bf16[256,512]{1,0:T(8,128)(2,1)S(1)} %collective-permute-done.14.refs_0_, f32[2048,512]{1,0:T(8,128)} %short_range.3.refs_6_.refs_2_.refs_1_, bf16[2048,2,256]{2,1,0:T(2,128)(2,1)} %final_sum.3.refs_2_), custom_call_target="tpu_custom_call", output_to_operand_aliasing={{}: (3, {})} | custom-call | flops 1 | bytes 1 | tf_op jit(solution)/shard_map/final_sum/pallas_call | solution.py:327
  82.8 2.0 %final_sum.5 = bf16[2048,2,256]{2,1,0:T(2,128)(2,1)} custom-call(s32[1]{0:T(128)} %bitcast.order_ref, bf16[256,512]{1,0:T(8,128)(2,1)S(1)} %collective-permute-done.13.refs_0_, f32[2048,512]{1,0:T(8,128)} %short_range.3.refs_6_.refs_2_.refs_1_, bf16[2048,2,256]{2,1,0:T(2,128)(2,1)} %final_sum.4.refs_2_), custom_call_target="tpu_custom_call", output_to_operand_aliasing={{}: (3, {})} | custom-call | flops 1 | bytes 1 | tf_op jit(solution)/shard_map/final_sum/pallas_call | solution.py:327
  (71 shorter events, 12.2 us)
Async XLA Ops:
  0.0 13.4 %copy-start.5 = (s32[16]{0:T(128)S(1)}, s32[16]{0:T(128)}, u32[]{:S(2)}) copy-start(s32[16]{0:T(128)} %sub_ref.1) | copy-start | bytes 196
  0.0 13.4 %copy-start.8 = (s32[16]{0:T(128)S(1)}, s32[16]{0:T(128)}, u32[]{:S(2)}) copy-start(s32[16]{0:T(128)} %param.19) | copy-start | bytes 196
  2.0 12.9 %copy-start.9 = (f32[125]{0:T(128)S(1)}, f32[125]{0:T(128)}, u32[]{:S(2)}) copy-start(f32[125]{0:T(128)} %param.16) | copy-start | bytes 1504
  2.0 12.9 %copy-start.10 = (f32[125]{0:T(128)S(1)}, f32[125]{0:T(128)}, u32[]{:S(2)}) copy-start(f32[125]{0:T(128)} %param.17) | copy-start | bytes 1504
  2.0 13.3 %copy-start.4 = (f32[4096]{0:T(1024)S(1)}, f32[4096]{0:T(1024)}, u32[]{:S(2)}) copy-start(f32[4096]{0:T(1024)} %param.15) | copy-start | bytes 49156
  2.0 17.4 %collective-permute-start.1 = (bf16[256,1024]{1,0:T(8,128)(2,1)}, bf16[256,1024]{1,0:T(8,128)(2,1)S(1)}, u32[]{:S(2)}, u32[]{:S(2)}) collective-permute-start(bf16[256,1024]{1,0:T(8,128)(2,1)} %bitcast.28), channel_id=1, source_target_pairs={{0,4},{1,5},{2,6},{3,7},{4,12},{5,13},{6,14},{7,15},{8,0},{9,1},{1... | collective-permute-start | bytes 1572872 | tf_op jit(solution)/shard_map/ppermute | solution.py:448
  5.0 24.5 %collective-permute-start = (bf16[256,1024]{1,0:T(8,128)(2,1)}, bf16[256,1024]{1,0:T(8,128)(2,1)}, u32[]{:S(2)}, u32[]{:S(2)}) collective-permute-start(bf16[256,1024]{1,0:T(8,128)(2,1)} %bitcast.28), channel_id=1, source_target_pairs={{0,8},{1,9},{2,10},{3,11},{4,0},{5,1},{6,2},{7,3},{8,12},{9,13},{1... | collective-permute-start | bytes 1572872 | tf_op jit(solution)/shard_map/ppermute | solution.py:448
  8.1 25.8 %collective-permute-start.5 = (bf16[1024,256]{1,0:T(8,128)(2,1)S(1)}, bf16[1024,256]{1,0:T(8,128)(2,1)S(1)}, u32[]{:S(2)}, u32[]{:S(2)}) collective-permute-start(bf16[1024,256]{1,0:T(8,128)(2,1)S(1)} %bitcast.39), channel_id=1, source_target_pairs={{0,2},{1,3},{2,0},{3,1},{4,6},{5,7},{6,4},{7,5},{8,10},{9,11},{10,... | collective-permute-start | bytes 1572872 | tf_op jit(solution)/shard_map/ppermute | solution.py:448
  9.9 24.0 %collective-permute-start.4 = (bf16[1024,256]{1,0:T(8,128)(2,1)S(1)}, bf16[1024,256]{1,0:T(8,128)(2,1)S(1)}, u32[]{:S(2)}, u32[]{:S(2)}) collective-permute-start(bf16[1024,256]{1,0:T(8,128)(2,1)S(1)} %bitcast.40), channel_id=1, source_target_pairs={{0,16},{1,17},{2,18},{3,19},{4,20},{5,21},{6,22},{7,23},{8,24},{9,... | collective-permute-start | bytes 1572872 | tf_op jit(solution)/shard_map/ppermute | solution.py:448
  14.3 21.9 %collective-permute-start.3 = (bf16[17,128,128]{2,1,0:T(8,128)(2,1)}, bf16[17,128,128]{2,1,0:T(8,128)(2,1)S(1)}, u32[]{:S(2)}, u32[]{:S(2)}) collective-permute-start(bf16[17,128,128]{2,1,0:T(8,128)(2,1)} %pad_maximum_fusion.refs_0_), channel_id=1, source_target_pairs={{0,16},{1,17},{2,18},{3,19},{4,20},{5,21},{6,22},{7,23},{8,24},{9,... | collective-permute-start | bytes 1671176 | tf_op jit(solution)/shard_map/ppermute | solution.py:448
  19.4 16.9 %copy-start.6 = (bf16[256,1024]{1,0:T(8,128)(2,1)}, bf16[256,1024]{1,0:T(8,128)(2,1)S(1)}, u32[]{:S(2)}) copy-start(bf16[256,1024]{1,0:T(8,128)(2,1)S(1)} %collective-permute-done.1) | copy-start | bytes 1572868
  29.5 17.3 %collective-permute-start.6 = (bf16[256,1024]{1,0:T(8,128)(2,1)S(1)}, bf16[256,1024]{1,0:T(8,128)(2,1)}, u32[]{:S(2)}, u32[]{:S(2)}) collective-permute-start(bf16[256,1024]{1,0:T(8,128)(2,1)S(1)} %select_select_fusion.3), channel_id=1, source_target_pairs={{0,16},{1,17},{2,18},{3,19},{4,20},{5,21},{6,22},{7,23},{8,24},{9,... | collective-permute-start | bytes 1572872 | tf_op jit(solution)/shard_map/ppermute | solution.py:448
  32.2 14.8 %collective-permute-start.2 = (bf16[256,1024]{1,0:T(8,128)(2,1)}, bf16[256,1024]{1,0:T(8,128)(2,1)}, u32[]{:S(2)}, u32[]{:S(2)}) collective-permute-start(bf16[256,1024]{1,0:T(8,128)(2,1)} %collective-permute-done), channel_id=1, source_target_pairs={{0,8},{1,9},{2,10},{3,11},{4,0},{5,1},{6,2},{7,3},{8,12},{9,13},{1... | collective-permute-start | bytes 1572872 | tf_op jit(solution)/shard_map/ppermute | solution.py:448
  37.7 17.2 %collective-permute-start.8 = (bf16[256,1024]{1,0:T(8,128)(2,1)S(1)}, bf16[256,1024]{1,0:T(8,128)(2,1)}, u32[]{:S(2)}, u32[]{:S(2)}) collective-permute-start(bf16[256,1024]{1,0:T(8,128)(2,1)S(1)} %select_select_fusion.1.refs_0_), channel_id=1, source_target_pairs={{0,1},{1,0},{2,3},{3,2},{4,5},{5,4},{6,7},{7,6},{8,9},{9,8},{10,11... | collective-permute-start | bytes 1572872 | tf_op jit(solution)/shard_map/ppermute | solution.py:448
  37.8 14.3 %collective-permute-start.7 = (bf16[1024,256]{1,0:T(8,128)(2,1)S(1)}, bf16[1024,256]{1,0:T(8,128)(2,1)S(1)}, u32[]{:S(2)}, u32[]{:S(2)}) collective-permute-start(bf16[1024,256]{1,0:T(8,128)(2,1)S(1)} %collective-permute-done.4.refs_5_), channel_id=1, source_target_pairs={{0,2},{1,3},{2,0},{3,1},{4,6},{5,7},{6,4},{7,5},{8,10},{9,11},{10,... | collective-permute-start | bytes 1572872 | tf_op jit(solution)/shard_map/ppermute | solution.py:448
  46.9 8.1 %collective-permute-start.9 = (bf16[256,1024]{1,0:T(8,128)(2,1)}, bf16[256,1024]{1,0:T(8,128)(2,1)}, u32[]{:S(2)}, u32[]{:S(2)}) collective-permute-start(bf16[256,1024]{1,0:T(8,128)(2,1)} %collective-permute-done.6.refs_1_), channel_id=1, source_target_pairs={{0,1},{1,0},{2,3},{3,2},{4,5},{5,4},{6,7},{7,6},{8,9},{9,8},{10,11... | collective-permute-start | bytes 1572872 | tf_op jit(solution)/shard_map/ppermute | solution.py:448
  48.9 16.6 %collective-permute-start.11 = (bf16[256,1024]{1,0:T(8,128)(2,1)}, bf16[256,1024]{1,0:T(8,128)(2,1)S(1)}, u32[]{:S(2)}, u32[]{:S(2)}) collective-permute-start(bf16[256,1024]{1,0:T(8,128)(2,1)} %select_select_fusion.2), channel_id=1, source_target_pairs={{0,16},{1,17},{2,18},{3,19},{4,20},{5,21},{6,22},{7,23},{8,24},{9,... | collective-permute-start | bytes 1572872 | tf_op jit(solution)/shard_map/ppermute | solution.py:448
  54.6 23.0 %collective-permute-start.15 = (bf16[256,512]{1,0:T(8,128)(2,1)}, bf16[256,512]{1,0:T(8,128)(2,1)S(1)}, u32[]{:S(2)}, u32[]{:S(2)}) collective-permute-start(bf16[256,512]{1,0:T(8,128)(2,1)} %long_range.4), channel_id=1, source_target_pairs={{0,2},{1,3},{2,0},{3,1},{4,6},{5,7},{6,4},{7,5},{8,10},{9,11},{10,... | collective-permute-start | bytes 786440 | tf_op jit(solution)/shard_map/ppermute | solution.py:448
  57.6 6.7 %copy-start.7 = (bf16[256,1024]{1,0:T(8,128)(2,1)S(1)}, bf16[256,1024]{1,0:T(8,128)(2,1)}, u32[]{:S(2)}) copy-start(bf16[256,1024]{1,0:T(8,128)(2,1)} %copy-done.6) | copy-start | bytes 1572868
  57.6 20.0 %collective-permute-start.16 = (bf16[256,512]{1,0:T(8,128)(2,1)}, bf16[256,512]{1,0:T(8,128)(2,1)}, u32[]{:S(2)}, u32[]{:S(2)}) collective-permute-start(bf16[256,512]{1,0:T(8,128)(2,1)} %long_range.5), channel_id=1, source_target_pairs={{0,2},{1,3},{2,0},{3,1},{4,6},{5,7},{6,4},{7,5},{8,10},{9,11},{10,... | collective-permute-start | bytes 786440 | tf_op jit(solution)/shard_map/ppermute | solution.py:448
  65.4 2.6 %collective-permute-start.10 = (bf16[256,1024]{1,0:T(8,128)(2,1)S(1)}, bf16[256,1024]{1,0:T(8,128)(2,1)S(1)}, u32[]{:S(2)}, u32[]{:S(2)}) collective-permute-start(bf16[256,1024]{1,0:T(8,128)(2,1)S(1)} %select_select_fusion.refs_0_), channel_id=1, source_target_pairs={{0,1},{1,0},{2,3},{3,2},{4,5},{5,4},{6,7},{7,6},{8,9},{9,8},{10,11... | collective-permute-start | bytes 1572872 | tf_op jit(solution)/shard_map/ppermute | solution.py:448
  65.5 2.6 %collective-permute-start.12 = (bf16[256,1024]{1,0:T(8,128)(2,1)S(1)}, bf16[256,1024]{1,0:T(8,128)(2,1)S(1)}, u32[]{:S(2)}, u32[]{:S(2)}) collective-permute-start(bf16[256,1024]{1,0:T(8,128)(2,1)S(1)} %collective-permute-done.11.refs_1_), channel_id=1, source_target_pairs={{0,1},{1,0},{2,3},{3,2},{4,5},{5,4},{6,7},{7,6},{8,9},{9,8},{10,11... | collective-permute-start | bytes 1572872 | tf_op jit(solution)/shard_map/ppermute | solution.py:448
  67.7 13.1 %collective-permute-start.14 = (bf16[256,512]{1,0:T(8,128)(2,1)}, bf16[256,512]{1,0:T(8,128)(2,1)S(1)}, u32[]{:S(2)}, u32[]{:S(2)}) collective-permute-start(bf16[256,512]{1,0:T(8,128)(2,1)} %long_range.7), channel_id=1, source_target_pairs={{0,2},{1,3},{2,0},{3,1},{4,6},{5,7},{6,4},{7,5},{8,10},{9,11},{10,... | collective-permute-start | bytes 786440 | tf_op jit(solution)/shard_map/ppermute | solution.py:448
  69.6 13.2 %collective-permute-start.13 = (bf16[256,512]{1,0:T(8,128)(2,1)}, bf16[256,512]{1,0:T(8,128)(2,1)S(1)}, u32[]{:S(2)}, u32[]{:S(2)}) collective-permute-start(bf16[256,512]{1,0:T(8,128)(2,1)} %long_range.6), channel_id=1, source_target_pairs={{0,2},{1,3},{2,0},{3,1},{4,6},{5,7},{6,4},{7,5},{8,10},{9,11},{10,... | collective-permute-start | bytes 786440 | tf_op jit(solution)/shard_map/ppermute | solution.py:448
  (4 other events, 5.1 us)

commit v16 on v15

--- a/solution.py
+++ b/solution.py
@@ -234,15 +234,16 @@
     )(*flat)
 
 
-def own_kernel(order_ref, *refs, blocks, chains, aliased):
+def own_kernel(order_ref, *refs, blocks, chains, pieces, aliased):
     parts = refs[: blocks * chains]
     factors = refs[blocks * chains : (blocks + 1) * chains]
-    short_ref = refs[(blocks + 1) * chains]
-    out_ref, right, terms, made, term_sem, out_sem = refs[(blocks + 1) * chains + 1 + aliased :]
+    arrived = refs[(blocks + 1) * chains :][:pieces]
+    short_ref = refs[(blocks + 1) * chains + pieces]
+    out_ref, right, terms, made, term_sem, out_sem = refs[(blocks + 1) * chains + pieces + 1 + aliased :]
     rows = terms.shape[1]
     depth, width = factors[0].shape
     half = depth // 2
-    windows = [pl.ds(pl.multiple_of(order_ref[n] * rows, rows), rows) for n in range(blocks)]
+    windows = [pl.ds(pl.multiple_of(order_ref[n] * rows, rows), rows) for n in range(blocks + pieces)]
     arriving = []
     for n, window in enumerate(windows):
         arriving.append(
@@ -256,8 +257,12 @@
         right[top + half : top + depth, width:] = -factor[0:half, :]
     leaving = []
     for n, window in enumerate(windows):
-        left = jnp.concatenate([parts[n * chains + chain][...] for chain in range(chains)], axis=1)
-        total = jnp.dot(left, right[...], preferred_element_type=jnp.float32)
+        if n < blocks:
+            left = [parts[n * chains + chain][...] for chain in range(chains)]
+            left = jnp.concatenate(left, axis=1)
+            total = jnp.dot(left, right[...], preferred_element_type=jnp.float32)
+        else:
+            total = arrived[n - blocks][...].astype(jnp.float32)
         arriving[n].wait()
         made[n] = (total + terms[n]).astype(made.dtype).reshape(made.shape[1:])
         leaving.append(pltpu.make_async_copy(made.at[n], out_ref.at[window], out_sem.at[n]))
@@ -266,16 +271,18 @@
         copy.wait()
 
 
-def own_sum(order, blocks, factors, short, earlier):
+def own_sum(order, blocks, factors, pieces, short, earlier):
     rows, depth = blocks[0][0].shape
     width = factors[0].shape[1]
     row_count, columns = short.shape
     chains = len(factors)
-    count = len(blocks)
+    count = len(blocks) + len(pieces)
     aliased = earlier is not None
-    flat = [v for group in [*blocks, factors] for v in group]
+    flat = [v for group in [*blocks, factors, pieces] for v in group]
     return pl.pallas_call(
-        functools.partial(own_kernel, blocks=count, chains=chains, aliased=aliased),
+        functools.partial(
+            own_kernel, blocks=len(blocks), chains=chains, pieces=len(pieces), aliased=aliased
+        ),
         out_shape=pltpu.HBM((row_count, 2, width), jnp.bfloat16),
         in_specs=[pl.BlockSpec(memory_space=pltpu.SMEM)]
         + [pl.BlockSpec(memory_space=pltpu.VMEM)] * len(flat)
@@ -523,7 +530,7 @@
     short = short_part(slots, packed, None, False)
 
     moved = foreign(0, short)
-    begun = [turned_x, items_x, *(pair[0] for pair in factors[1:])]
+    begun = [turned_x, *(pair[0] for pair in factors[1:])]
     for k in range(2, length // 2 + 1):
         held[k] = along(after(held[k - 1], held[1], held[length - 1], short), 1)
     for k in range(2, (length + 1) // 2):
@@ -532,6 +539,11 @@
         factors[s].append(over_y(after(turned_x, theirs[0], *begun), s))
 
     short = short_part(read_slots(after(items_x, theirs[0], *begun), slots), items_x, short)
+
+    def arrived_of(n):
+        return [
+            [(v, number_of(n, s, t)) for s, v in enumerate(arriving[n][t], 1)] for t in range(CORES)
+        ]
 
     out = None
     for n in range(home):
@@ -550,19 +562,17 @@
             (after(mine[n][0], *away[n]), crossed[n][0]),
             *zip(mine[n][1:], crossed[n][1:]),
         ]
-        order = jnp.stack([number_of(n, 0, t) for t in range(CORES)]).astype(jnp.int32)
-        out = own_sum(order, blocks, factors[0], short, out)
-    calls = []
-    for n in range(home):
-        calls += [
-            [(v, number_of(n, s, t)) for s, v in enumerate(arriving[n][t], 1)] for t in range(CORES)
-        ]
-        if n < home - 1:
-            calls[-CORES:] = [sum(calls[-CORES:], [])]
-    for entries in calls:
-        if entries:
-            order = jnp.stack([number for _, number in entries]).astype(jnp.int32)
-            out = final_sum(order, [piece for piece, _ in entries], short, out, rows)
+        numbers = [number_of(n, 0, t) for t in range(CORES)]
+        pieces = []
+        if n:
+            come = [(v, number) for entries in arrived_of(n - 1) for v, number in entries]
+            pieces = [v for v, _ in come]
+            numbers += [number for _, number in come]
+        out = own_sum(jnp.stack(numbers).astype(jnp.int32), blocks, factors[0], pieces, short, out)
+    entries = sum(arrived_of(home - 1), [])
+    if entries:
+        order = jnp.stack([number for _, number in entries]).astype(jnp.int32)
+        out = final_sum(order, [piece for piece, _ in entries], short, out, rows)
     return out
 
 

time: 85.6 us -> 82.6 us (0.965)
  Pallas kernels: 37 us -> 35 us
  waiting for transfers between devices: 15 us -> 13.3 us
  starting transfers between devices: 18 us -> 18.9 us
    pallas_call x3 -> x1, Pallas kernels: 7.11 us -> 2.74 us  [final_sum(): pl.pallas_call(functools.partial(final_kernel, pieces=count, blocks=block...]
    ppermute x17, waiting for transfers between devices: 15 us -> 13.3 us  [send(): return lax.ppermute(value, AXES, pairs)]
    pallas_call x2, Pallas kernels: 13.1 us -> 14.5 us  [short_range(): pl.pallas_call(kernel, out_shape=pltpu.HBM((row_count, 2 * subs * width)...]
    ppermute x17, starting transfers between devices: 18 us -> 18.9 us  [send(): return lax.ppermute(value, AXES, pairs)]
    pallas_call x2, Pallas kernels: 8.88 us -> 9.76 us  [own_sum(): pl.pallas_call(functools.partial(own_kernel, blocks=len(blocks), chains=c...]
  transfers between devices with their start and end apart: 17 -> 17, of which waited for: 4 -> 2; matrix products, arithmetic and copies ran while one was open for 11% -> 12% of each run, Pallas kernels for 41% -> 39%
where the time goes in v16:
time: 82.6 us; the launch traced here: 81.9 us
  Pallas kernels  35 us (42%)
  starting transfers between devices  18.9 us (23%)
  waiting for transfers between devices  13.3 us (16%)
  other arithmetic  7.6 us (9%)
  local copies, waits for them, and re-layouts  6.01 us (7%)
  between operations  1.11 us (1%)
    ppermute x17, starting transfers between devices, send(): return lax.ppermute(value, AXES, pairs)  18.9 us
    pallas_call x2, Pallas kernels, short_range(): pl.pallas_call(kernel, out_shape=pltpu.HBM((row_count, 2 * subs * width)...  14.5 us
    ppermute x17, waiting for transfers between devices, send(): return lax.ppermute(value, AXES, pairs)  13.3 us
    pallas_call x2, Pallas kernels, own_sum(): pl.pallas_call(functools.partial(own_kernel, blocks=len(blocks), chains=c...  9.76 us
    pallas_call x4, Pallas kernels, long_range(): pl.pallas_call(functools.partial(long_kernel, blocks=len(blocks), chains=...  7.94 us
    unnamed x24, local copies, waits for them, and re-layouts  5.38 us
    select_n x4, other arithmetic, pick(): value = jnp.where(wanted == k, block, value)  4.39 us
    pallas_call x1, Pallas kernels, final_sum(): pl.pallas_call(functools.partial(final_kernel, pieces=count, blocks=block...  2.74 us
  transfers between devices with their start and end apart: 17, of which 2 were waited for; matrix products, arithmetic and copies ran while one was open for 12% of the time, Pallas kernels for 39%

profile of v16, /device:TPU:0, one launch (start us, length us, event | category | flops | bytes accessed | tf_op | source)
XLA Modules:
  0.0 81.9 jit_solution(16339473555898316155)
XLA Ops:
  0.0 1.9 %copy.18 = bf16[32,8,2,512]{3,1,2,0:T(8,128)(2,1)} copy(bf16[32,8,2,512]{3,2,1,0:T(2,128)(2,1)} %bitcast.47) | data formatting | bytes 1048576
  2.0 4.0 %collective-permute-start = (bf16[256,1024]{1,0:T(8,128)(2,1)}, bf16[256,1024]{1,0:T(8,128)(2,1)}, u32[]{:S(2)}, u32[]{:S(2)}) collective-permute-start(bf16[256,1024]{1,0:T(8,128)(2,1)} %bitcast.28), channel_id=1, source_target_pairs={{0,8},{1,9},{2,10},{3,11},{4,0},{5,1},{6,2},{7,3},{8,12},{9,13},{1... | collective-permute-start | bytes 1572872 | tf_op jit(solution)/shard_map/ppermute | solution.py:455
  6.0 1.5 %multiply_convert_fusion = bf16[256,2,512]{2,1,0:T(2,128)(2,1)S(1)} fusion(bf16[256,2,512]{2,1,0:T(2,128)(2,1)} %param.11, f32[512]{0:T(512)} %param.13), kind=kLoop, calls=%fused_computation.2 | loop fusion | flops 786432 | bytes 1050624 | tf_op jit(solution)/shard_map/convert_element_type | solution.py:413
  8.0 1.6 %collective-permute-start.4 = (bf16[1024,256]{1,0:T(8,128)(2,1)S(1)}, bf16[1024,256]{1,0:T(8,128)(2,1)S(1)}, u32[]{:S(2)}, u32[]{:S(2)}) collective-permute-start(bf16[1024,256]{1,0:T(8,128)(2,1)S(1)} %bitcast.39), channel_id=1, source_target_pairs={{0,16},{1,17},{2,18},{3,19},{4,20},{5,21},{6,22},{7,23},{8,24},{9,... | collective-permute-start | bytes 1572872 | tf_op jit(solution)/shard_map/ppermute | solution.py:455
  9.6 1.5 %collective-permute-start.5 = (bf16[1024,256]{1,0:T(8,128)(2,1)S(1)}, bf16[1024,256]{1,0:T(8,128)(2,1)S(1)}, u32[]{:S(2)}, u32[]{:S(2)}) collective-permute-start(bf16[1024,256]{1,0:T(8,128)(2,1)S(1)} %bitcast.40), channel_id=1, source_target_pairs={{0,2},{1,3},{2,0},{3,1},{4,6},{5,7},{6,4},{7,5},{8,10},{9,11},{10,... | collective-permute-start | bytes 1572872 | tf_op jit(solution)/shard_map/ppermute | solution.py:455
  11.7 1.3 %copy.16 = bf16[16,128,128]{1,2,0:T(8,128)(2,1)S(1)} copy(bf16[16,128,128]{2,1,0:T(8,128)(2,1)} %param.18) | data formatting | bytes 1048576 | tf_op args[7]
  14.8 5.6 %short_range.2.refs_1_ = f32[2,256,2048]{2,1,0:T(8,128)} custom-call(s32[1]{0:T(128)} %bitcast.2.half_ref, s32[16]{0:T(128)S(1)} %compare_convert_fusion.1.live_ref, s32[16]{0:T(128)S(1)} %copy-done.5, f32[3,16]{1,0:T(4,128)S(1)} %pad_maximum_fusion.1.meta_ref, bf16[128,4096]{1,0:T(8,128)(2,1)} %basis_ref.3, f32[1,4096]{1,0:T(1,128)S(1)} %bitcast.43, ...), custom_call_target="tpu_custom_call" | custom-call | flops 2147483648 | bytes 1 | tf_op jit(solution)/shard_map/short_range/pallas_call | solution.py:141
  20.6 9.9 %collective-permute-done.1 = bf16[256,1024]{1,0:T(8,128)(2,1)S(1)} collective-permute-done((bf16[256,1024]{1,0:T(8,128)(2,1)}, bf16[256,1024]{1,0:T(8,128)(2,1)S(1)}, u32[]{:S(2)}, u32[]{:S(2)}) %collective-permute-start.1) | collective-permute-done | bytes 524320 | tf_op jit(solution)/shard_map/ppermute | solution.py:455
  31.1 2.6 %collective-permute-start.6 = (bf16[256,1024]{1,0:T(8,128)(2,1)S(1)}, bf16[256,1024]{1,0:T(8,128)(2,1)}, u32[]{:S(2)}, u32[]{:S(2)}) collective-permute-start(bf16[256,1024]{1,0:T(8,128)(2,1)S(1)} %select_select_fusion.3), channel_id=1, source_target_pairs={{0,16},{1,17},{2,18},{3,19},{4,20},{5,21},{6,22},{7,23},{8,24},{9,... | collective-permute-start | bytes 1572872 | tf_op jit(solution)/shard_map/ppermute | solution.py:455
  33.7 1.6 %collective-permute-start.7 = (bf16[1024,256]{1,0:T(8,128)(2,1)S(1)}, bf16[1024,256]{1,0:T(8,128)(2,1)S(1)}, u32[]{:S(2)}, u32[]{:S(2)}) collective-permute-start(bf16[1024,256]{1,0:T(8,128)(2,1)S(1)} %collective-permute-done.4.refs_5_), channel_id=1, source_target_pairs={{0,2},{1,3},{2,0},{3,1},{4,6},{5,7},{6,4},{7,5},{8,10},{9,11},{10,... | collective-permute-start | bytes 1572872 | tf_op jit(solution)/shard_map/ppermute | solution.py:455
  35.3 1.3 %select_select_fusion.1.refs_0_ = bf16[256,1024]{1,0:T(8,128)(2,1)S(1)} fusion(bf16[256,1024]{1,0:T(8,128)(2,1)} %bitcast.28, bf16[256,1024]{1,0:T(8,128)(2,1)} %collective-permute-done, bf16[256,1024]{1,0:T(8,128)(2,1)} %copy-done.6, pred[]{:T(512)S(6)} %eq.82, pred[]{:T(512)S(6)} %eq.81), kind=kLoop, calls=%fused_computation.5 | loop fusion | flops 524288 | bytes 2097154 | tf_op jit(solution)/shard_map/jit(_where)/select_n | solution.py:489
  37.0 8.9 %short_range.3.refs_6_.refs_8_.refs_2_ = f32[2048,512]{1,0:T(8,128)} custom-call(s32[1]{0:T(128)} %bitcast.2.half_ref, s32[16]{0:T(128)S(1)} %get-tuple-element.55.live_ref, s32[16]{0:T(128)S(1)} %get-tuple-element.54.sub_ref, f32[3,16]{1,0:T(4,128)S(1)} %pad_maximum_fusion.2.meta_ref, bf16[128,4096]{1,0:T(8,128)(2,1)} %basis_ref.3, f32[1,4096]{1,0:T(1,128)S(1)} %bitcast.44, ...), custom_call_target="tpu_custom_call" | custom-call | flops 2147483648 | bytes 1 | tf_op jit(solution)/shard_map/short_range/pallas_call | solution.py:141
  46.4 1.9 %select_select_fusion.2 = bf16[256,1024]{1,0:T(8,128)(2,1)} fusion(bf16[256,1024]{1,0:T(8,128)(2,1)} %collective-permute-done, bf16[256,1024]{1,0:T(8,128)(2,1)} %collective-permute-done.2, bf16[256,1024]{1,0:T(8,128)(2,1)} %copy-done.6, pred[]{:T(512)S(6)} %eq.80, pred[]{:T(512)S(6)} %eq.73), kind=kLoop, calls=%fused_computation.6 | loop fusion | flops 524288 | bytes 2097154 | tf_op jit(solution)/shard_map/jit(_where)/select_n | solution.py:489
  49.4 2.5 %long_range.4 = bf16[256,512]{1,0:T(8,128)(2,1)} custom-call(bf16[256,1024]{1,0:T(8,128)(2,1)S(1)} %select_select_fusion.1.refs_0_, bf16[256,1024]{1,0:T(8,128)(2,1)} %collective-permute-done.6.refs_1_, bf16[1024,256]{1,0:T(8,128)(2,1)S(1)} %collective-permute-done.5.refs_2_, bf16[1024,256]{1,0:T(8,128)(2,1)S(1)} %collective-permute-done.7.refs_3_), custom_call_target="tpu_custom_call" | custom-call | flops 1 | bytes 1 | tf_op jit(solution)/shard_map/long_range/pallas_call | solution.py:221
  51.9 1.6 %collective-permute-start.15 = (bf16[256,512]{1,0:T(8,128)(2,1)}, bf16[256,512]{1,0:T(8,128)(2,1)S(1)}, u32[]{:S(2)}, u32[]{:S(2)}) collective-permute-start(bf16[256,512]{1,0:T(8,128)(2,1)} %long_range.4), channel_id=1, source_target_pairs={{0,2},{1,3},{2,0},{3,1},{4,6},{5,7},{6,4},{7,5},{8,10},{9,11},{10,... | collective-permute-start | bytes 786440 | tf_op jit(solution)/shard_map/ppermute | solution.py:455
  53.5 2.6 %long_range.5 = bf16[256,512]{1,0:T(8,128)(2,1)} custom-call(bf16[256,1024]{1,0:T(8,128)(2,1)} %collective-permute-done.8.refs_0_.refs_2_, bf16[256,1024]{1,0:T(8,128)(2,1)} %collective-permute-done.9.refs_1_.refs_3_, bf16[1024,256]{1,0:T(8,128)(2,1)S(1)} %collective-permute-done.5.refs_2_, bf16[1024,256]{1,0:T(8,128)(2,1)S(1)} %collective-permute-done.7.refs_3_), custom_call_target="tpu_custom_call" | custom-call | flops 1 | bytes 1 | tf_op jit(solution)/shard_map/long_range/pallas_call | solution.py:221
  56.7 4.8 %own_sum.2.refs_9_ = bf16[2048,2,256]{2,1,0:T(2,128)(2,1)} custom-call(s32[2]{0:T(128)S(1)} %pad_add_fusion.2.order_ref, bf16[256,1024]{1,0:T(8,128)(2,1)S(1)} %select_select_fusion.1.refs_0_, bf16[256,1024]{1,0:T(8,128)(2,1)} %collective-permute-done.6.refs_1_, bf16[256,1024]{1,0:T(8,128)(2,1)} %collective-permute-done.8.refs_0_.refs_2_, ...), custom_call_target="tpu_custom_call" | custom-call | flops 1 | bytes 1 | tf_op jit(solution)/shard_map/own_sum/pallas_call | solution.py:282
  61.5 1.1 %select_select_fusion.refs_0_ = bf16[256,1024]{1,0:T(8,128)(2,1)S(1)} fusion(bf16[256,1024]{1,0:T(8,128)(2,1)} %collective-permute-done, bf16[256,1024]{1,0:T(8,128)(2,1)} %collective-permute-done.2, bf16[256,1024]{1,0:T(8,128)(2,1)S(1)} %copy-done.7, pred[]{:T(512)S(6)} %eq.83, pred[]{:T(512)S(6)} %eq.69), kind=kLoop, calls=%fused_computation.4 | loop fusion | flops 524288 | bytes 2097154 | tf_op jit(solution)/shard_map/jit(_where)/select_n | solution.py:489
  63.5 1.4 %long_range.6 = bf16[256,512]{1,0:T(8,128)(2,1)} custom-call(bf16[256,1024]{1,0:T(8,128)(2,1)S(1)} %select_select_fusion.refs_0_, bf16[256,1024]{1,0:T(8,128)(2,1)S(1)} %collective-permute-done.10.refs_1_, bf16[1024,512]{1,0:T(8,128)(2,1)S(1)} %get-tuple-element.62.refs_2_, bf16[1024,512]{1,0:T(8,128)(2,1)S(1)} %get-tuple-element.63.refs_3_), custom_call_target="tpu_custom_call" | custom-call | flops 1 | bytes 1 | tf_op jit(solution)/shard_map/long_range/pallas_call | solution.py:221
  64.9 1.6 %collective-permute-start.11 = (bf16[256,512]{1,0:T(8,128)(2,1)}, bf16[256,512]{1,0:T(8,128)(2,1)S(1)}, u32[]{:S(2)}, u32[]{:S(2)}) collective-permute-start(bf16[256,512]{1,0:T(8,128)(2,1)} %long_range.6), channel_id=1, source_target_pairs={{0,2},{1,3},{2,0},{3,1},{4,6},{5,7},{6,4},{7,5},{8,10},{9,11},{10,... | collective-permute-start | bytes 786440 | tf_op jit(solution)/shard_map/ppermute | solution.py:455
  66.6 1.4 %long_range.7 = bf16[256,512]{1,0:T(8,128)(2,1)} custom-call(bf16[256,1024]{1,0:T(8,128)(2,1)S(1)} %collective-permute-done.12.refs_0_.refs_2_, bf16[256,1024]{1,0:T(8,128)(2,1)S(1)} %collective-permute-done.13.refs_1_.refs_3_, bf16[1024,512]{1,0:T(8,128)(2,1)S(1)} %get-tuple-element.62.refs_2_, bf16[1024,512]{1,0:T(8,128)(2,1)S(1)} %get-tuple-element.63.refs_3_), custom_call_target="tpu_custom_call" | custom-call | flops 1 | bytes 1 | tf_op jit(solution)/shard_map/long_range/pallas_call | solution.py:221
  70.8 4.9 %own_sum.3.refs_3_ = bf16[2048,2,256]{2,1,0:T(2,128)(2,1)} custom-call(s32[4]{0:T(128)S(1)} %pad_add_fusion.3.order_ref, bf16[256,1024]{1,0:T(8,128)(2,1)S(1)} %select_select_fusion.refs_0_, bf16[256,1024]{1,0:T(8,128)(2,1)S(1)} %collective-permute-done.10.refs_1_, bf16[256,1024]{1,0:T(8,128)(2,1)S(1)} %copy-done.1, ...), custom_call_target="tpu_custom_call", output_to_operand_aliasing={{}: (10, {})} | custom-call | flops 1 | bytes 1 | tf_op jit(solution)/shard_map/own_sum/pallas_call | solution.py:282
  75.8 3.4 %collective-permute-done.14.refs_1_ = bf16[256,512]{1,0:T(8,128)(2,1)S(1)} collective-permute-done((bf16[256,512]{1,0:T(8,128)(2,1)}, bf16[256,512]{1,0:T(8,128)(2,1)S(1)}, u32[]{:S(2)}, u32[]{:S(2)}) %collective-permute-start.14) | collective-permute-done | bytes 262176 | tf_op jit(solution)/shard_map/ppermute | solution.py:455
  79.1 2.7 %final_sum.1 = bf16[2048,2,256]{2,1,0:T(2,128)(2,1)} custom-call(s32[2]{0:T(128)S(1)} %pad_add_fusion.1.order_ref, bf16[256,512]{1,0:T(8,128)(2,1)S(1)} %collective-permute-done.11.refs_0_, bf16[256,512]{1,0:T(8,128)(2,1)S(1)} %collective-permute-done.14.refs_1_, f32[2048,512]{1,0:T(8,128)} %short_range.3.refs_6_.refs_8_.refs_2_, ...), custom_call_target="tpu_custom_call", output_to_operand_aliasing={{}: (4, {})} | custom-call | flops 1 | bytes 1 | tf_op jit(solution)/shard_map/final_sum/pallas_call | solution.py:334
  (69 shorter events, 9.1 us)
Async XLA Ops:
  0.0 13.1 %copy-start.5 = (s32[16]{0:T(128)S(1)}, s32[16]{0:T(128)}, u32[]{:S(2)}) copy-start(s32[16]{0:T(128)} %sub_ref.1) | copy-start | bytes 196
  0.0 13.1 %copy-start.8 = (s32[16]{0:T(128)S(1)}, s32[16]{0:T(128)}, u32[]{:S(2)}) copy-start(s32[16]{0:T(128)} %param.19) | copy-start | bytes 196
  2.0 12.6 %copy-start.9 = (f32[125]{0:T(128)S(1)}, f32[125]{0:T(128)}, u32[]{:S(2)}) copy-start(f32[125]{0:T(128)} %param.16) | copy-start | bytes 1504
  2.0 12.6 %copy-start.10 = (f32[125]{0:T(128)S(1)}, f32[125]{0:T(128)}, u32[]{:S(2)}) copy-start(f32[125]{0:T(128)} %param.17) | copy-start | bytes 1504
  2.0 12.9 %copy-start.4 = (f32[4096]{0:T(1024)S(1)}, f32[4096]{0:T(1024)}, u32[]{:S(2)}) copy-start(f32[4096]{0:T(1024)} %param.15) | copy-start | bytes 49156
  2.0 18.6 %collective-permute-start = (bf16[256,1024]{1,0:T(8,128)(2,1)}, bf16[256,1024]{1,0:T(8,128)(2,1)}, u32[]{:S(2)}, u32[]{:S(2)}) collective-permute-start(bf16[256,1024]{1,0:T(8,128)(2,1)} %bitcast.28), channel_id=1, source_target_pairs={{0,8},{1,9},{2,10},{3,11},{4,0},{5,1},{6,2},{7,3},{8,12},{9,13},{1... | collective-permute-start | bytes 1572872 | tf_op jit(solution)/shard_map/ppermute | solution.py:455
  6.0 24.4 %collective-permute-start.1 = (bf16[256,1024]{1,0:T(8,128)(2,1)}, bf16[256,1024]{1,0:T(8,128)(2,1)S(1)}, u32[]{:S(2)}, u32[]{:S(2)}) collective-permute-start(bf16[256,1024]{1,0:T(8,128)(2,1)} %bitcast.28), channel_id=1, source_target_pairs={{0,4},{1,5},{2,6},{3,7},{4,12},{5,13},{6,14},{7,15},{8,0},{9,1},{1... | collective-permute-start | bytes 1572872 | tf_op jit(solution)/shard_map/ppermute | solution.py:455
  8.0 25.7 %collective-permute-start.4 = (bf16[1024,256]{1,0:T(8,128)(2,1)S(1)}, bf16[1024,256]{1,0:T(8,128)(2,1)S(1)}, u32[]{:S(2)}, u32[]{:S(2)}) collective-permute-start(bf16[1024,256]{1,0:T(8,128)(2,1)S(1)} %bitcast.39), channel_id=1, source_target_pairs={{0,16},{1,17},{2,18},{3,19},{4,20},{5,21},{6,22},{7,23},{8,24},{9,... | collective-permute-start | bytes 1572872 | tf_op jit(solution)/shard_map/ppermute | solution.py:455
  9.6 24.2 %collective-permute-start.5 = (bf16[1024,256]{1,0:T(8,128)(2,1)S(1)}, bf16[1024,256]{1,0:T(8,128)(2,1)S(1)}, u32[]{:S(2)}, u32[]{:S(2)}) collective-permute-start(bf16[1024,256]{1,0:T(8,128)(2,1)S(1)} %bitcast.40), channel_id=1, source_target_pairs={{0,2},{1,3},{2,0},{3,1},{4,6},{5,7},{6,4},{7,5},{8,10},{9,11},{10,... | collective-permute-start | bytes 1572872 | tf_op jit(solution)/shard_map/ppermute | solution.py:455
  14.0 22.7 %collective-permute-start.3 = (bf16[17,128,128]{2,1,0:T(8,128)(2,1)}, bf16[17,128,128]{2,1,0:T(8,128)(2,1)S(1)}, u32[]{:S(2)}, u32[]{:S(2)}) collective-permute-start(bf16[17,128,128]{2,1,0:T(8,128)(2,1)} %pad_maximum_fusion.refs_0_), channel_id=1, source_target_pairs={{0,16},{1,17},{2,18},{3,19},{4,20},{5,21},{6,22},{7,23},{8,24},{9,... | collective-permute-start | bytes 1671176 | tf_op jit(solution)/shard_map/ppermute | solution.py:455
  30.4 3.3 %copy-start.6 = (bf16[256,1024]{1,0:T(8,128)(2,1)}, bf16[256,1024]{1,0:T(8,128)(2,1)S(1)}, u32[]{:S(2)}) copy-start(bf16[256,1024]{1,0:T(8,128)(2,1)S(1)} %collective-permute-done.1) | copy-start | bytes 1572868
  30.4 16.0 %collective-permute-start.2 = (bf16[256,1024]{1,0:T(8,128)(2,1)}, bf16[256,1024]{1,0:T(8,128)(2,1)}, u32[]{:S(2)}, u32[]{:S(2)}) collective-permute-start(bf16[256,1024]{1,0:T(8,128)(2,1)} %collective-permute-done), channel_id=1, source_target_pairs={{0,8},{1,9},{2,10},{3,11},{4,0},{5,1},{6,2},{7,3},{8,12},{9,13},{1... | collective-permute-start | bytes 1572872 | tf_op jit(solution)/shard_map/ppermute | solution.py:455
  31.1 14.7 %collective-permute-start.6 = (bf16[256,1024]{1,0:T(8,128)(2,1)S(1)}, bf16[256,1024]{1,0:T(8,128)(2,1)}, u32[]{:S(2)}, u32[]{:S(2)}) collective-permute-start(bf16[256,1024]{1,0:T(8,128)(2,1)S(1)} %select_select_fusion.3), channel_id=1, source_target_pairs={{0,16},{1,17},{2,18},{3,19},{4,20},{5,21},{6,22},{7,23},{8,24},{9,... | collective-permute-start | bytes 1572872 | tf_op jit(solution)/shard_map/ppermute | solution.py:455
  33.7 15.7 %collective-permute-start.7 = (bf16[1024,256]{1,0:T(8,128)(2,1)S(1)}, bf16[1024,256]{1,0:T(8,128)(2,1)S(1)}, u32[]{:S(2)}, u32[]{:S(2)}) collective-permute-start(bf16[1024,256]{1,0:T(8,128)(2,1)S(1)} %collective-permute-done.4.refs_5_), channel_id=1, source_target_pairs={{0,2},{1,3},{2,0},{3,1},{4,6},{5,7},{6,4},{7,5},{8,10},{9,11},{10,... | collective-permute-start | bytes 1572872 | tf_op jit(solution)/shard_map/ppermute | solution.py:455
  36.6 16.9 %collective-permute-start.8 = (bf16[256,1024]{1,0:T(8,128)(2,1)S(1)}, bf16[256,1024]{1,0:T(8,128)(2,1)}, u32[]{:S(2)}, u32[]{:S(2)}) collective-permute-start(bf16[256,1024]{1,0:T(8,128)(2,1)S(1)} %select_select_fusion.1.refs_0_), channel_id=1, source_target_pairs={{0,1},{1,0},{2,3},{3,2},{4,5},{5,4},{6,7},{7,6},{8,9},{9,8},{10,11... | collective-permute-start | bytes 1572872 | tf_op jit(solution)/shard_map/ppermute | solution.py:455
  45.9 7.6 %collective-permute-start.9 = (bf16[256,1024]{1,0:T(8,128)(2,1)}, bf16[256,1024]{1,0:T(8,128)(2,1)}, u32[]{:S(2)}, u32[]{:S(2)}) collective-permute-start(bf16[256,1024]{1,0:T(8,128)(2,1)} %collective-permute-done.6.refs_1_), channel_id=1, source_target_pairs={{0,1},{1,0},{2,3},{3,2},{4,5},{5,4},{6,7},{7,6},{8,9},{9,8},{10,11... | collective-permute-start | bytes 1572872 | tf_op jit(solution)/shard_map/ppermute | solution.py:455
  48.3 14.4 %collective-permute-start.10 = (bf16[256,1024]{1,0:T(8,128)(2,1)}, bf16[256,1024]{1,0:T(8,128)(2,1)S(1)}, u32[]{:S(2)}, u32[]{:S(2)}) collective-permute-start(bf16[256,1024]{1,0:T(8,128)(2,1)} %select_select_fusion.2), channel_id=1, source_target_pairs={{0,16},{1,17},{2,18},{3,19},{4,20},{5,21},{6,22},{7,23},{8,24},{9,... | collective-permute-start | bytes 1572872 | tf_op jit(solution)/shard_map/ppermute | solution.py:455
  51.9 16.9 %collective-permute-start.15 = (bf16[256,512]{1,0:T(8,128)(2,1)}, bf16[256,512]{1,0:T(8,128)(2,1)S(1)}, u32[]{:S(2)}, u32[]{:S(2)}) collective-permute-start(bf16[256,512]{1,0:T(8,128)(2,1)} %long_range.4), channel_id=1, source_target_pairs={{0,2},{1,3},{2,0},{3,1},{4,6},{5,7},{6,4},{7,5},{8,10},{9,11},{10,... | collective-permute-start | bytes 786440 | tf_op jit(solution)/shard_map/ppermute | solution.py:455
  56.1 5.4 %copy-start.7 = (bf16[256,1024]{1,0:T(8,128)(2,1)S(1)}, bf16[256,1024]{1,0:T(8,128)(2,1)}, u32[]{:S(2)}) copy-start(bf16[256,1024]{1,0:T(8,128)(2,1)} %copy-done.6) | copy-start | bytes 1572868
  56.1 12.6 %collective-permute-start.16 = (bf16[256,512]{1,0:T(8,128)(2,1)}, bf16[256,512]{1,0:T(8,128)(2,1)}, u32[]{:S(2)}, u32[]{:S(2)}) collective-permute-start(bf16[256,512]{1,0:T(8,128)(2,1)} %long_range.5), channel_id=1, source_target_pairs={{0,2},{1,3},{2,0},{3,1},{4,6},{5,7},{6,4},{7,5},{8,10},{9,11},{10,... | collective-permute-start | bytes 786440 | tf_op jit(solution)/shard_map/ppermute | solution.py:455
  62.7 3.9 %collective-permute-start.12 = (bf16[256,1024]{1,0:T(8,128)(2,1)S(1)}, bf16[256,1024]{1,0:T(8,128)(2,1)S(1)}, u32[]{:S(2)}, u32[]{:S(2)}) collective-permute-start(bf16[256,1024]{1,0:T(8,128)(2,1)S(1)} %select_select_fusion.refs_0_), channel_id=1, source_target_pairs={{0,1},{1,0},{2,3},{3,2},{4,5},{5,4},{6,7},{7,6},{8,9},{9,8},{10,11... | collective-permute-start | bytes 1572872 | tf_op jit(solution)/shard_map/ppermute | solution.py:455
  62.8 3.8 %collective-permute-start.13 = (bf16[256,1024]{1,0:T(8,128)(2,1)S(1)}, bf16[256,1024]{1,0:T(8,128)(2,1)S(1)}, u32[]{:S(2)}, u32[]{:S(2)}) collective-permute-start(bf16[256,1024]{1,0:T(8,128)(2,1)S(1)} %collective-permute-done.10.refs_1_), channel_id=1, source_target_pairs={{0,1},{1,0},{2,3},{3,2},{4,5},{5,4},{6,7},{7,6},{8,9},{9,8},{10,11... | collective-permute-start | bytes 1572872 | tf_op jit(solution)/shard_map/ppermute | solution.py:455
  64.9 10.8 %collective-permute-start.11 = (bf16[256,512]{1,0:T(8,128)(2,1)}, bf16[256,512]{1,0:T(8,128)(2,1)S(1)}, u32[]{:S(2)}, u32[]{:S(2)}) collective-permute-start(bf16[256,512]{1,0:T(8,128)(2,1)} %long_range.6), channel_id=1, source_target_pairs={{0,2},{1,3},{2,0},{3,1},{4,6},{5,7},{6,4},{7,5},{8,10},{9,11},{10,... | collective-permute-start | bytes 786440 | tf_op jit(solution)/shard_map/ppermute | solution.py:455
  68.0 11.1 %collective-permute-start.14 = (bf16[256,512]{1,0:T(8,128)(2,1)}, bf16[256,512]{1,0:T(8,128)(2,1)S(1)}, u32[]{:S(2)}, u32[]{:S(2)}) collective-permute-start(bf16[256,512]{1,0:T(8,128)(2,1)} %long_range.7), channel_id=1, source_target_pairs={{0,2},{1,3},{2,0},{3,1},{4,6},{5,7},{6,4},{7,5},{8,10},{9,11},{10,... | collective-permute-start | bytes 786440 | tf_op jit(solution)/shard_map/ppermute | solution.py:455
  (4 other events, 5.0 us)

commit v17 on v16

--- a/solution.py
+++ b/solution.py
@@ -569,10 +569,10 @@
             pieces = [v for v, _ in come]
             numbers += [number for _, number in come]
         out = own_sum(jnp.stack(numbers).astype(jnp.int32), blocks, factors[0], pieces, short, out)
-    entries = sum(arrived_of(home - 1), [])
-    if entries:
-        order = jnp.stack([number for _, number in entries]).astype(jnp.int32)
-        out = final_sum(order, [piece for piece, _ in entries], short, out, rows)
+    for entries in arrived_of(home - 1):
+        if entries:
+            order = jnp.stack([number for _, number in entries]).astype(jnp.int32)
+            out = final_sum(order, [piece for piece, _ in entries], short, out, rows)
     return out
 
 

time: 82.6 us -> 84.4 us (1.022)
  waiting for transfers between devices: 13.3 us -> 14.4 us
    pallas_call x1 -> x2, Pallas kernels: 2.74 us -> 3.94 us  [final_sum(): pl.pallas_call(functools.partial(final_kernel, pieces=count, blocks=block...]
    ppermute x17, waiting for transfers between devices: 13.3 us -> 14.4 us  [send(): return lax.ppermute(value, AXES, pairs)]
  transfers between devices with their start and end apart: 17 -> 17, of which waited for: 2 -> 4; matrix products, arithmetic and copies ran while one was open for 12% -> 11% of each run, Pallas kernels for 39% -> 40%
where the time goes in v17:
time: 84.4 us; the launch traced here: 83.6 us
  Pallas kernels  35.4 us (42%)
  starting transfers between devices  19.2 us (23%)
  waiting for transfers between devices  14.4 us (17%)
  other arithmetic  7.53 us (9%)
  local copies, waits for them, and re-layouts  6 us (7%)
  between operations  1.09 us (1%)
    ppermute x17, starting transfers between devices, send(): return lax.ppermute(value, AXES, pairs)  19.2 us
    ppermute x17, waiting for transfers between devices, send(): return lax.ppermute(value, AXES, pairs)  14.4 us
    pallas_call x2, Pallas kernels, short_range(): pl.pallas_call(kernel, out_shape=pltpu.HBM((row_count, 2 * subs * width)...  13.8 us
    pallas_call x2, Pallas kernels, own_sum(): pl.pallas_call(functools.partial(own_kernel, blocks=len(blocks), chains=c...  9.76 us
    pallas_call x4, Pallas kernels, long_range(): pl.pallas_call(functools.partial(long_kernel, blocks=len(blocks), chains=...  7.93 us
    unnamed x24, local copies, waits for them, and re-layouts  5.37 us
    select_n x4, other arithmetic, pick(): value = jnp.where(wanted == k, block, value)  4.4 us
    pallas_call x2, Pallas kernels, final_sum(): pl.pallas_call(functools.partial(final_kernel, pieces=count, blocks=block...  3.94 us
  transfers between devices with their start and end apart: 17, of which 4 were waited for; matrix products, arithmetic and copies ran while one was open for 11% of the time, Pallas kernels for 40%

profile of v17, /device:TPU:0, one launch (start us, length us, event | category | flops | bytes accessed | tf_op | source)
XLA Modules:
  0.0 83.6 jit_solution(6041291024840503592)
XLA Ops:
  0.0 1.9 %copy.19 = bf16[32,8,2,512]{3,1,2,0:T(8,128)(2,1)} copy(bf16[32,8,2,512]{3,2,1,0:T(2,128)(2,1)} %bitcast.47) | data formatting | bytes 1048576
  1.9 3.0 %collective-permute-start.1 = (bf16[256,1024]{1,0:T(8,128)(2,1)}, bf16[256,1024]{1,0:T(8,128)(2,1)S(1)}, u32[]{:S(2)}, u32[]{:S(2)}) collective-permute-start(bf16[256,1024]{1,0:T(8,128)(2,1)} %bitcast.28), channel_id=1, source_target_pairs={{0,4},{1,5},{2,6},{3,7},{4,12},{5,13},{6,14},{7,15},{8,0},{9,1},{1... | collective-permute-start | bytes 1572872 | tf_op jit(solution)/shard_map/ppermute | solution.py:455
  6.0 1.5 %multiply_convert_fusion = bf16[256,2,512]{2,1,0:T(2,128)(2,1)S(1)} fusion(bf16[256,2,512]{2,1,0:T(2,128)(2,1)} %param.11, f32[512]{0:T(512)} %param.13), kind=kLoop, calls=%fused_computation.2 | loop fusion | flops 786432 | bytes 1050624 | tf_op jit(solution)/shard_map/convert_element_type | solution.py:413
  8.0 1.9 %collective-permute-start.5 = (bf16[1024,256]{1,0:T(8,128)(2,1)S(1)}, bf16[1024,256]{1,0:T(8,128)(2,1)S(1)}, u32[]{:S(2)}, u32[]{:S(2)}) collective-permute-start(bf16[1024,256]{1,0:T(8,128)(2,1)S(1)} %bitcast.39), channel_id=1, source_target_pairs={{0,2},{1,3},{2,0},{3,1},{4,6},{5,7},{6,4},{7,5},{8,10},{9,11},{10,... | collective-permute-start | bytes 1572872 | tf_op jit(solution)/shard_map/ppermute | solution.py:455
  9.9 1.5 %collective-permute-start.4 = (bf16[1024,256]{1,0:T(8,128)(2,1)S(1)}, bf16[1024,256]{1,0:T(8,128)(2,1)S(1)}, u32[]{:S(2)}, u32[]{:S(2)}) collective-permute-start(bf16[1024,256]{1,0:T(8,128)(2,1)S(1)} %bitcast.40), channel_id=1, source_target_pairs={{0,16},{1,17},{2,18},{3,19},{4,20},{5,21},{6,22},{7,23},{8,24},{9,... | collective-permute-start | bytes 1572872 | tf_op jit(solution)/shard_map/ppermute | solution.py:455
  15.1 4.9 %short_range.2.refs_1_ = f32[2,256,2048]{2,1,0:T(8,128)} custom-call(s32[1]{0:T(128)} %bitcast.1.half_ref, s32[16]{0:T(128)S(1)} %compare_convert_fusion.1.live_ref, s32[16]{0:T(128)S(1)} %copy-done.5, f32[3,16]{1,0:T(4,128)S(1)} %pad_maximum_fusion.1.meta_ref, bf16[128,4096]{1,0:T(8,128)(2,1)} %basis_ref.3, f32[1,4096]{1,0:T(1,128)S(1)} %bitcast.43, ...), custom_call_target="tpu_custom_call" | custom-call | flops 2147483648 | bytes 1 | tf_op jit(solution)/shard_map/short_range/pallas_call | solution.py:141
  20.2 9.3 %collective-permute-done = bf16[256,1024]{1,0:T(8,128)(2,1)} collective-permute-done((bf16[256,1024]{1,0:T(8,128)(2,1)}, bf16[256,1024]{1,0:T(8,128)(2,1)}, u32[]{:S(2)}, u32[]{:S(2)}) %collective-permute-start) | collective-permute-done | bytes 524320 | tf_op jit(solution)/shard_map/ppermute | solution.py:455
  29.5 2.6 %collective-permute-start.6 = (bf16[256,1024]{1,0:T(8,128)(2,1)S(1)}, bf16[256,1024]{1,0:T(8,128)(2,1)}, u32[]{:S(2)}, u32[]{:S(2)}) collective-permute-start(bf16[256,1024]{1,0:T(8,128)(2,1)S(1)} %select_select_fusion.3), channel_id=1, source_target_pairs={{0,16},{1,17},{2,18},{3,19},{4,20},{5,21},{6,22},{7,23},{8,24},{9,... | collective-permute-start | bytes 1572872 | tf_op jit(solution)/shard_map/ppermute | solution.py:455
  33.6 1.6 %collective-permute-start.7 = (bf16[1024,256]{1,0:T(8,128)(2,1)S(1)}, bf16[1024,256]{1,0:T(8,128)(2,1)S(1)}, u32[]{:S(2)}, u32[]{:S(2)}) collective-permute-start(bf16[1024,256]{1,0:T(8,128)(2,1)S(1)} %collective-permute-done.4.refs_5_), channel_id=1, source_target_pairs={{0,2},{1,3},{2,0},{3,1},{4,6},{5,7},{6,4},{7,5},{8,10},{9,11},{10,... | collective-permute-start | bytes 1572872 | tf_op jit(solution)/shard_map/ppermute | solution.py:455
  35.1 1.5 %collective-permute-start.2 = (bf16[256,1024]{1,0:T(8,128)(2,1)}, bf16[256,1024]{1,0:T(8,128)(2,1)}, u32[]{:S(2)}, u32[]{:S(2)}) collective-permute-start(bf16[256,1024]{1,0:T(8,128)(2,1)} %collective-permute-done), channel_id=1, source_target_pairs={{0,8},{1,9},{2,10},{3,11},{4,0},{5,1},{6,2},{7,3},{8,12},{9,13},{1... | collective-permute-start | bytes 1572872 | tf_op jit(solution)/shard_map/ppermute | solution.py:455
  36.9 8.9 %short_range.3.refs_6_.refs_8_.refs_1_ = f32[2048,512]{1,0:T(8,128)} custom-call(s32[1]{0:T(128)} %bitcast.1.half_ref, s32[16]{0:T(128)S(1)} %get-tuple-element.55.live_ref, s32[16]{0:T(128)S(1)} %get-tuple-element.54.sub_ref, f32[3,16]{1,0:T(4,128)S(1)} %pad_maximum_fusion.2.meta_ref, bf16[128,4096]{1,0:T(8,128)(2,1)} %basis_ref.3, f32[1,4096]{1,0:T(1,128)S(1)} %bitcast.44, ...), custom_call_target="tpu_custom_call" | custom-call | flops 2147483648 | bytes 1 | tf_op jit(solution)/shard_map/short_range/pallas_call | solution.py:141
  46.0 3.4 %collective-permute-done.2 = bf16[256,1024]{1,0:T(8,128)(2,1)} collective-permute-done((bf16[256,1024]{1,0:T(8,128)(2,1)}, bf16[256,1024]{1,0:T(8,128)(2,1)}, u32[]{:S(2)}, u32[]{:S(2)}) %collective-permute-start.2) | collective-permute-done | bytes 524320 | tf_op jit(solution)/shard_map/ppermute | solution.py:455
  49.5 1.9 %select_select_fusion.2 = bf16[256,1024]{1,0:T(8,128)(2,1)} fusion(bf16[256,1024]{1,0:T(8,128)(2,1)} %collective-permute-done, bf16[256,1024]{1,0:T(8,128)(2,1)} %collective-permute-done.2, bf16[256,1024]{1,0:T(8,128)(2,1)} %copy-done.6, pred[]{:T(512)S(6)} %eq.80, pred[]{:T(512)S(6)} %eq.73), kind=kLoop, calls=%fused_computation.6 | loop fusion | flops 524288 | bytes 2097154 | tf_op jit(solution)/shard_map/jit(_where)/select_n | solution.py:489
  51.9 2.5 %long_range.4 = bf16[256,512]{1,0:T(8,128)(2,1)} custom-call(bf16[256,1024]{1,0:T(8,128)(2,1)S(1)} %select_select_fusion.1.refs_0_, bf16[256,1024]{1,0:T(8,128)(2,1)} %collective-permute-done.6.refs_1_, bf16[1024,256]{1,0:T(8,128)(2,1)S(1)} %collective-permute-done.5.refs_2_, bf16[1024,256]{1,0:T(8,128)(2,1)S(1)} %collective-permute-done.7.refs_3_), custom_call_target="tpu_custom_call" | custom-call | flops 1 | bytes 1 | tf_op jit(solution)/shard_map/long_range/pallas_call | solution.py:221
  55.0 2.6 %long_range.5 = bf16[256,512]{1,0:T(8,128)(2,1)} custom-call(bf16[256,1024]{1,0:T(8,128)(2,1)} %collective-permute-done.8.refs_0_.refs_2_, bf16[256,1024]{1,0:T(8,128)(2,1)} %collective-permute-done.9.refs_1_.refs_3_, bf16[1024,256]{1,0:T(8,128)(2,1)S(1)} %collective-permute-done.5.refs_2_, bf16[1024,256]{1,0:T(8,128)(2,1)S(1)} %collective-permute-done.7.refs_3_), custom_call_target="tpu_custom_call" | custom-call | flops 1 | bytes 1 | tf_op jit(solution)/shard_map/long_range/pallas_call | solution.py:221
  57.6 1.6 %collective-permute-start.16 = (bf16[256,512]{1,0:T(8,128)(2,1)}, bf16[256,512]{1,0:T(8,128)(2,1)}, u32[]{:S(2)}, u32[]{:S(2)}) collective-permute-start(bf16[256,512]{1,0:T(8,128)(2,1)} %long_range.5), channel_id=1, source_target_pairs={{0,2},{1,3},{2,0},{3,1},{4,6},{5,7},{6,4},{7,5},{8,10},{9,11},{10,... | collective-permute-start | bytes 786440 | tf_op jit(solution)/shard_map/ppermute | solution.py:455
  59.2 4.9 %own_sum.2.refs_9_ = bf16[2048,2,256]{2,1,0:T(2,128)(2,1)} custom-call(s32[2]{0:T(128)S(1)} %pad_add_fusion.1.order_ref, bf16[256,1024]{1,0:T(8,128)(2,1)S(1)} %select_select_fusion.1.refs_0_, bf16[256,1024]{1,0:T(8,128)(2,1)} %collective-permute-done.6.refs_1_, bf16[256,1024]{1,0:T(8,128)(2,1)} %collective-permute-done.8.refs_0_.refs_2_, ...), custom_call_target="tpu_custom_call" | custom-call | flops 1 | bytes 1 | tf_op jit(solution)/shard_map/own_sum/pallas_call | solution.py:282
  66.0 1.4 %long_range.7 = bf16[256,512]{1,0:T(8,128)(2,1)} custom-call(bf16[256,1024]{1,0:T(8,128)(2,1)S(1)} %select_select_fusion.refs_0_, bf16[256,1024]{1,0:T(8,128)(2,1)S(1)} %collective-permute-done.11.refs_1_, bf16[1024,512]{1,0:T(8,128)(2,1)S(1)} %get-tuple-element.62.refs_2_, bf16[1024,512]{1,0:T(8,128)(2,1)S(1)} %get-tuple-element.63.refs_3_), custom_call_target="tpu_custom_call" | custom-call | flops 1 | bytes 1 | tf_op jit(solution)/shard_map/long_range/pallas_call | solution.py:221
  68.1 1.4 %long_range.6 = bf16[256,512]{1,0:T(8,128)(2,1)} custom-call(bf16[256,1024]{1,0:T(8,128)(2,1)S(1)} %collective-permute-done.10.refs_0_.refs_2_, bf16[256,1024]{1,0:T(8,128)(2,1)S(1)} %collective-permute-done.12.refs_1_.refs_3_, bf16[1024,512]{1,0:T(8,128)(2,1)S(1)} %get-tuple-element.62.refs_2_, bf16[1024,512]{1,0:T(8,128)(2,1)S(1)} %get-tuple-element.63.refs_3_), custom_call_target="tpu_custom_call" | custom-call | flops 1 | bytes 1 | tf_op jit(solution)/shard_map/long_range/pallas_call | solution.py:221
  69.5 1.6 %collective-permute-start.13 = (bf16[256,512]{1,0:T(8,128)(2,1)}, bf16[256,512]{1,0:T(8,128)(2,1)S(1)}, u32[]{:S(2)}, u32[]{:S(2)}) collective-permute-start(bf16[256,512]{1,0:T(8,128)(2,1)} %long_range.6), channel_id=1, source_target_pairs={{0,2},{1,3},{2,0},{3,1},{4,6},{5,7},{6,4},{7,5},{8,10},{9,11},{10,... | collective-permute-start | bytes 786440 | tf_op jit(solution)/shard_map/ppermute | solution.py:455
  73.3 4.9 %own_sum.3.refs_2_ = bf16[2048,2,256]{2,1,0:T(2,128)(2,1)} custom-call(s32[4]{0:T(128)S(1)} %pad_add_fusion.2.order_ref, bf16[256,1024]{1,0:T(8,128)(2,1)S(1)} %select_select_fusion.refs_0_, bf16[256,1024]{1,0:T(8,128)(2,1)S(1)} %collective-permute-done.11.refs_1_, bf16[256,1024]{1,0:T(8,128)(2,1)S(1)} %copy-done.1, ...), custom_call_target="tpu_custom_call", output_to_operand_aliasing={{}: (10, {})} | custom-call | flops 1 | bytes 1 | tf_op jit(solution)/shard_map/own_sum/pallas_call | solution.py:282
  78.2 2.0 %final_sum.2.refs_2_ = bf16[2048,2,256]{2,1,0:T(2,128)(2,1)} custom-call(s32[1]{0:T(128)} %bitcast.22.order_ref, bf16[256,512]{1,0:T(8,128)(2,1)S(1)} %collective-permute-done.14.refs_0_, f32[2048,512]{1,0:T(8,128)} %short_range.3.refs_6_.refs_8_.refs_1_, bf16[2048,2,256]{2,1,0:T(2,128)(2,1)} %own_sum.3.refs_2_), custom_call_target="tpu_custom_call", output_to_operand_aliasing={{}: (3, {})} | custom-call | flops 1 | bytes 1 | tf_op jit(solution)/shard_map/final_sum/pallas_call | solution.py:334
  80.2 1.5 %collective-permute-done.13.refs_0_ = bf16[256,512]{1,0:T(8,128)(2,1)S(1)} collective-permute-done((bf16[256,512]{1,0:T(8,128)(2,1)}, bf16[256,512]{1,0:T(8,128)(2,1)S(1)}, u32[]{:S(2)}, u32[]{:S(2)}) %collective-permute-start.13) | collective-permute-done | bytes 262176 | tf_op jit(solution)/shard_map/ppermute | solution.py:455
  81.7 2.0 %final_sum.3 = bf16[2048,2,256]{2,1,0:T(2,128)(2,1)} custom-call(s32[1]{0:T(128)} %bitcast.order_ref, bf16[256,512]{1,0:T(8,128)(2,1)S(1)} %collective-permute-done.13.refs_0_, f32[2048,512]{1,0:T(8,128)} %short_range.3.refs_6_.refs_8_.refs_1_, bf16[2048,2,256]{2,1,0:T(2,128)(2,1)} %final_sum.2.refs_2_), custom_call_target="tpu_custom_call", output_to_operand_aliasing={{}: (3, {})} | custom-call | flops 1 | bytes 1 | tf_op jit(solution)/shard_map/final_sum/pallas_call | solution.py:334
  (69 shorter events, 12.3 us)
Async XLA Ops:
  0.0 13.4 %copy-start.5 = (s32[16]{0:T(128)S(1)}, s32[16]{0:T(128)}, u32[]{:S(2)}) copy-start(s32[16]{0:T(128)} %sub_ref.1) | copy-start | bytes 196
  0.0 13.4 %copy-start.8 = (s32[16]{0:T(128)S(1)}, s32[16]{0:T(128)}, u32[]{:S(2)}) copy-start(s32[16]{0:T(128)} %param.19) | copy-start | bytes 196
  1.9 12.9 %copy-start.9 = (f32[125]{0:T(128)S(1)}, f32[125]{0:T(128)}, u32[]{:S(2)}) copy-start(f32[125]{0:T(128)} %param.16) | copy-start | bytes 1504
  1.9 12.9 %copy-start.10 = (f32[125]{0:T(128)S(1)}, f32[125]{0:T(128)}, u32[]{:S(2)}) copy-start(f32[125]{0:T(128)} %param.17) | copy-start | bytes 1504
  1.9 13.2 %copy-start.4 = (f32[4096]{0:T(1024)S(1)}, f32[4096]{0:T(1024)}, u32[]{:S(2)}) copy-start(f32[4096]{0:T(1024)} %param.15) | copy-start | bytes 49156
  1.9 18.2 %collective-permute-start.1 = (bf16[256,1024]{1,0:T(8,128)(2,1)}, bf16[256,1024]{1,0:T(8,128)(2,1)S(1)}, u32[]{:S(2)}, u32[]{:S(2)}) collective-permute-start(bf16[256,1024]{1,0:T(8,128)(2,1)} %bitcast.28), channel_id=1, source_target_pairs={{0,4},{1,5},{2,6},{3,7},{4,12},{5,13},{6,14},{7,15},{8,0},{9,1},{1... | collective-permute-start | bytes 1572872 | tf_op jit(solution)/shard_map/ppermute | solution.py:455
  5.0 24.5 %collective-permute-start = (bf16[256,1024]{1,0:T(8,128)(2,1)}, bf16[256,1024]{1,0:T(8,128)(2,1)}, u32[]{:S(2)}, u32[]{:S(2)}) collective-permute-start(bf16[256,1024]{1,0:T(8,128)(2,1)} %bitcast.28), channel_id=1, source_target_pairs={{0,8},{1,9},{2,10},{3,11},{4,0},{5,1},{6,2},{7,3},{8,12},{9,13},{1... | collective-permute-start | bytes 1572872 | tf_op jit(solution)/shard_map/ppermute | solution.py:455
  8.0 24.1 %collective-permute-start.5 = (bf16[1024,256]{1,0:T(8,128)(2,1)S(1)}, bf16[1024,256]{1,0:T(8,128)(2,1)S(1)}, u32[]{:S(2)}, u32[]{:S(2)}) collective-permute-start(bf16[1024,256]{1,0:T(8,128)(2,1)S(1)} %bitcast.39), channel_id=1, source_target_pairs={{0,2},{1,3},{2,0},{3,1},{4,6},{5,7},{6,4},{7,5},{8,10},{9,11},{10,... | collective-permute-start | bytes 1572872 | tf_op jit(solution)/shard_map/ppermute | solution.py:455
  9.9 22.3 %collective-permute-start.4 = (bf16[1024,256]{1,0:T(8,128)(2,1)S(1)}, bf16[1024,256]{1,0:T(8,128)(2,1)S(1)}, u32[]{:S(2)}, u32[]{:S(2)}) collective-permute-start(bf16[1024,256]{1,0:T(8,128)(2,1)S(1)} %bitcast.40), channel_id=1, source_target_pairs={{0,16},{1,17},{2,18},{3,19},{4,20},{5,21},{6,22},{7,23},{8,24},{9,... | collective-permute-start | bytes 1572872 | tf_op jit(solution)/shard_map/ppermute | solution.py:455
  14.3 22.4 %collective-permute-start.3 = (bf16[17,128,128]{2,1,0:T(8,128)(2,1)}, bf16[17,128,128]{2,1,0:T(8,128)(2,1)S(1)}, u32[]{:S(2)}, u32[]{:S(2)}) collective-permute-start(bf16[17,128,128]{2,1,0:T(8,128)(2,1)} %pad_maximum_fusion.refs_0_), channel_id=1, source_target_pairs={{0,16},{1,17},{2,18},{3,19},{4,20},{5,21},{6,22},{7,23},{8,24},{9,... | collective-permute-start | bytes 1671176 | tf_op jit(solution)/shard_map/ppermute | solution.py:455
  20.2 12.0 %copy-start.6 = (bf16[256,1024]{1,0:T(8,128)(2,1)}, bf16[256,1024]{1,0:T(8,128)(2,1)S(1)}, u32[]{:S(2)}) copy-start(bf16[256,1024]{1,0:T(8,128)(2,1)S(1)} %collective-permute-done.1) | copy-start | bytes 1572868
  29.5 16.5 %collective-permute-start.6 = (bf16[256,1024]{1,0:T(8,128)(2,1)S(1)}, bf16[256,1024]{1,0:T(8,128)(2,1)}, u32[]{:S(2)}, u32[]{:S(2)}) collective-permute-start(bf16[256,1024]{1,0:T(8,128)(2,1)S(1)} %select_select_fusion.3), channel_id=1, source_target_pairs={{0,16},{1,17},{2,18},{3,19},{4,20},{5,21},{6,22},{7,23},{8,24},{9,... | collective-permute-start | bytes 1572872 | tf_op jit(solution)/shard_map/ppermute | solution.py:455
  33.5 21.5 %collective-permute-start.8 = (bf16[256,1024]{1,0:T(8,128)(2,1)S(1)}, bf16[256,1024]{1,0:T(8,128)(2,1)}, u32[]{:S(2)}, u32[]{:S(2)}) collective-permute-start(bf16[256,1024]{1,0:T(8,128)(2,1)S(1)} %select_select_fusion.1.refs_0_), channel_id=1, source_target_pairs={{0,1},{1,0},{2,3},{3,2},{4,5},{5,4},{6,7},{7,6},{8,9},{9,8},{10,11... | collective-permute-start | bytes 1572872 | tf_op jit(solution)/shard_map/ppermute | solution.py:455
  33.6 18.4 %collective-permute-start.7 = (bf16[1024,256]{1,0:T(8,128)(2,1)S(1)}, bf16[1024,256]{1,0:T(8,128)(2,1)S(1)}, u32[]{:S(2)}, u32[]{:S(2)}) collective-permute-start(bf16[1024,256]{1,0:T(8,128)(2,1)S(1)} %collective-permute-done.4.refs_5_), channel_id=1, source_target_pairs={{0,2},{1,3},{2,0},{3,1},{4,6},{5,7},{6,4},{7,5},{8,10},{9,11},{10,... | collective-permute-start | bytes 1572872 | tf_op jit(solution)/shard_map/ppermute | solution.py:455
  35.1 14.3 %collective-permute-start.2 = (bf16[256,1024]{1,0:T(8,128)(2,1)}, bf16[256,1024]{1,0:T(8,128)(2,1)}, u32[]{:S(2)}, u32[]{:S(2)}) collective-permute-start(bf16[256,1024]{1,0:T(8,128)(2,1)} %collective-permute-done), channel_id=1, source_target_pairs={{0,8},{1,9},{2,10},{3,11},{4,0},{5,1},{6,2},{7,3},{8,12},{9,13},{1... | collective-permute-start | bytes 1572872 | tf_op jit(solution)/shard_map/ppermute | solution.py:455
  46.0 9.0 %collective-permute-start.9 = (bf16[256,1024]{1,0:T(8,128)(2,1)}, bf16[256,1024]{1,0:T(8,128)(2,1)}, u32[]{:S(2)}, u32[]{:S(2)}) collective-permute-start(bf16[256,1024]{1,0:T(8,128)(2,1)} %collective-permute-done.6.refs_1_), channel_id=1, source_target_pairs={{0,1},{1,0},{2,3},{3,2},{4,5},{5,4},{6,7},{7,6},{8,9},{9,8},{10,11... | collective-permute-start | bytes 1572872 | tf_op jit(solution)/shard_map/ppermute | solution.py:455
  51.4 13.9 %collective-permute-start.11 = (bf16[256,1024]{1,0:T(8,128)(2,1)}, bf16[256,1024]{1,0:T(8,128)(2,1)S(1)}, u32[]{:S(2)}, u32[]{:S(2)}) collective-permute-start(bf16[256,1024]{1,0:T(8,128)(2,1)} %select_select_fusion.2), channel_id=1, source_target_pairs={{0,16},{1,17},{2,18},{3,19},{4,20},{5,21},{6,22},{7,23},{8,24},{9,... | collective-permute-start | bytes 1572872 | tf_op jit(solution)/shard_map/ppermute | solution.py:455
  54.4 16.8 %collective-permute-start.15 = (bf16[256,512]{1,0:T(8,128)(2,1)}, bf16[256,512]{1,0:T(8,128)(2,1)S(1)}, u32[]{:S(2)}, u32[]{:S(2)}) collective-permute-start(bf16[256,512]{1,0:T(8,128)(2,1)} %long_range.4), channel_id=1, source_target_pairs={{0,2},{1,3},{2,0},{3,1},{4,6},{5,7},{6,4},{7,5},{8,10},{9,11},{10,... | collective-permute-start | bytes 786440 | tf_op jit(solution)/shard_map/ppermute | solution.py:455
  57.6 6.5 %copy-start.7 = (bf16[256,1024]{1,0:T(8,128)(2,1)S(1)}, bf16[256,1024]{1,0:T(8,128)(2,1)}, u32[]{:S(2)}) copy-start(bf16[256,1024]{1,0:T(8,128)(2,1)} %copy-done.6) | copy-start | bytes 1572868
  57.6 13.6 %collective-permute-start.16 = (bf16[256,512]{1,0:T(8,128)(2,1)}, bf16[256,512]{1,0:T(8,128)(2,1)}, u32[]{:S(2)}, u32[]{:S(2)}) collective-permute-start(bf16[256,512]{1,0:T(8,128)(2,1)} %long_range.5), channel_id=1, source_target_pairs={{0,2},{1,3},{2,0},{3,1},{4,6},{5,7},{6,4},{7,5},{8,10},{9,11},{10,... | collective-permute-start | bytes 786440 | tf_op jit(solution)/shard_map/ppermute | solution.py:455
  65.2 2.9 %collective-permute-start.10 = (bf16[256,1024]{1,0:T(8,128)(2,1)S(1)}, bf16[256,1024]{1,0:T(8,128)(2,1)S(1)}, u32[]{:S(2)}, u32[]{:S(2)}) collective-permute-start(bf16[256,1024]{1,0:T(8,128)(2,1)S(1)} %select_select_fusion.refs_0_), channel_id=1, source_target_pairs={{0,1},{1,0},{2,3},{3,2},{4,5},{5,4},{6,7},{7,6},{8,9},{9,8},{10,11... | collective-permute-start | bytes 1572872 | tf_op jit(solution)/shard_map/ppermute | solution.py:455
  65.3 2.8 %collective-permute-start.12 = (bf16[256,1024]{1,0:T(8,128)(2,1)S(1)}, bf16[256,1024]{1,0:T(8,128)(2,1)S(1)}, u32[]{:S(2)}, u32[]{:S(2)}) collective-permute-start(bf16[256,1024]{1,0:T(8,128)(2,1)S(1)} %collective-permute-done.11.refs_1_), channel_id=1, source_target_pairs={{0,1},{1,0},{2,3},{3,2},{4,5},{5,4},{6,7},{7,6},{8,9},{9,8},{10,11... | collective-permute-start | bytes 1572872 | tf_op jit(solution)/shard_map/ppermute | solution.py:455
  67.5 10.7 %collective-permute-start.14 = (bf16[256,512]{1,0:T(8,128)(2,1)}, bf16[256,512]{1,0:T(8,128)(2,1)S(1)}, u32[]{:S(2)}, u32[]{:S(2)}) collective-permute-start(bf16[256,512]{1,0:T(8,128)(2,1)} %long_range.7), channel_id=1, source_target_pairs={{0,2},{1,3},{2,0},{3,1},{4,6},{5,7},{6,4},{7,5},{8,10},{9,11},{10,... | collective-permute-start | bytes 786440 | tf_op jit(solution)/shard_map/ppermute | solution.py:455
  69.5 12.1 %collective-permute-start.13 = (bf16[256,512]{1,0:T(8,128)(2,1)}, bf16[256,512]{1,0:T(8,128)(2,1)S(1)}, u32[]{:S(2)}, u32[]{:S(2)}) collective-permute-start(bf16[256,512]{1,0:T(8,128)(2,1)} %long_range.6), channel_id=1, source_target_pairs={{0,2},{1,3},{2,0},{3,1},{4,6},{5,7},{6,4},{7,5},{8,10},{9,11},{10,... | collective-permute-start | bytes 786440 | tf_op jit(solution)/shard_map/ppermute | solution.py:455
  (4 other events, 5.0 us)

commit v18 on v17

--- a/solution.py
+++ b/solution.py
@@ -555,7 +555,7 @@
         away_factors = factors[1:]
         if n:
             away_factors = [[both_parts(after(v, *away[0])) for v in pair] for pair in factors[1:]]
-        crossed.append(with_cores(moved if n else after(moved, short)))
+        crossed.append(with_cores(moved if n else after(moved, short, held[length // 2])))
         for t in range(CORES):
             multiply(n, t, away_factors)
         blocks = [

time: 84.4 us -> 81.9 us (0.970)
  waiting for transfers between devices: 14.4 us -> 10.8 us
  Pallas kernels: 35.4 us -> 36.3 us
    ppermute x17, waiting for transfers between devices: 14.4 us -> 10.8 us  [send(): return lax.ppermute(value, AXES, pairs)]
    pallas_call x2, Pallas kernels: 13.8 us -> 14.7 us  [short_range(): pl.pallas_call(kernel, out_shape=pltpu.HBM((row_count, 2 * subs * width)...]
  transfers between devices with their start and end apart: 17 -> 17, of which waited for: 4 -> 4; matrix products, arithmetic and copies ran while one was open for 11% -> 12% of each run, Pallas kernels for 40% -> 42%
where the time goes in v18:
time: 81.9 us; the launch traced here: 81.1 us
  Pallas kernels  36.3 us (44%)
  starting transfers between devices  19.3 us (24%)
  waiting for transfers between devices  10.8 us (13%)
  other arithmetic  7.52 us (9%)
  local copies, waits for them, and re-layouts  6.01 us (7%)
  between operations  1.1 us (1%)
    ppermute x17, starting transfers between devices, send(): return lax.ppermute(value, AXES, pairs)  19.3 us
    pallas_call x2, Pallas kernels, short_range(): pl.pallas_call(kernel, out_shape=pltpu.HBM((row_count, 2 * subs * width)...  14.7 us
    ppermute x17, waiting for transfers between devices, send(): return lax.ppermute(value, AXES, pairs)  10.8 us
    pallas_call x2, Pallas kernels, own_sum(): pl.pallas_call(functools.partial(own_kernel, blocks=len(blocks), chains=c...  9.77 us
    pallas_call x4, Pallas kernels, long_range(): pl.pallas_call(functools.partial(long_kernel, blocks=len(blocks), chains=...  7.94 us
    unnamed x24, local copies, waits for them, and re-layouts  5.38 us
    select_n x4, other arithmetic, pick(): value = jnp.where(wanted == k, block, value)  4.39 us
    pallas_call x2, Pallas kernels, final_sum(): pl.pallas_call(functools.partial(final_kernel, pieces=count, blocks=block...  3.94 us
  transfers between devices with their start and end apart: 17, of which 4 were waited for; matrix products, arithmetic and copies ran while one was open for 12% of the time, Pallas kernels for 42%

profile of v18, /device:TPU:0, one launch (start us, length us, event | category | flops | bytes accessed | tf_op | source)
XLA Modules:
  0.0 81.1 jit_solution(11472172818209923792)
XLA Ops:
  0.0 1.9 %copy.19 = bf16[32,8,2,512]{3,1,2,0:T(8,128)(2,1)} copy(bf16[32,8,2,512]{3,2,1,0:T(2,128)(2,1)} %bitcast.47) | data formatting | bytes 1048576
  2.0 4.0 %collective-permute-start = (bf16[256,1024]{1,0:T(8,128)(2,1)}, bf16[256,1024]{1,0:T(8,128)(2,1)}, u32[]{:S(2)}, u32[]{:S(2)}) collective-permute-start(bf16[256,1024]{1,0:T(8,128)(2,1)} %bitcast.28), channel_id=1, source_target_pairs={{0,8},{1,9},{2,10},{3,11},{4,0},{5,1},{6,2},{7,3},{8,12},{9,13},{1... | collective-permute-start | bytes 1572872 | tf_op jit(solution)/shard_map/ppermute | solution.py:455
  6.0 1.5 %multiply_convert_fusion = bf16[256,2,512]{2,1,0:T(2,128)(2,1)S(1)} fusion(bf16[256,2,512]{2,1,0:T(2,128)(2,1)} %param.11, f32[512]{0:T(512)} %param.13), kind=kLoop, calls=%fused_computation.2 | loop fusion | flops 786432 | bytes 1050624 | tf_op jit(solution)/shard_map/convert_element_type | solution.py:413
  8.0 1.6 %collective-permute-start.4 = (bf16[1024,256]{1,0:T(8,128)(2,1)S(1)}, bf16[1024,256]{1,0:T(8,128)(2,1)S(1)}, u32[]{:S(2)}, u32[]{:S(2)}) collective-permute-start(bf16[1024,256]{1,0:T(8,128)(2,1)S(1)} %bitcast.39), channel_id=1, source_target_pairs={{0,16},{1,17},{2,18},{3,19},{4,20},{5,21},{6,22},{7,23},{8,24},{9,... | collective-permute-start | bytes 1572872 | tf_op jit(solution)/shard_map/ppermute | solution.py:455
  9.6 1.5 %collective-permute-start.5 = (bf16[1024,256]{1,0:T(8,128)(2,1)S(1)}, bf16[1024,256]{1,0:T(8,128)(2,1)S(1)}, u32[]{:S(2)}, u32[]{:S(2)}) collective-permute-start(bf16[1024,256]{1,0:T(8,128)(2,1)S(1)} %bitcast.40), channel_id=1, source_target_pairs={{0,2},{1,3},{2,0},{3,1},{4,6},{5,7},{6,4},{7,5},{8,10},{9,11},{10,... | collective-permute-start | bytes 1572872 | tf_op jit(solution)/shard_map/ppermute | solution.py:455
  11.7 1.3 %copy.17 = bf16[16,128,128]{1,2,0:T(8,128)(2,1)S(1)} copy(bf16[16,128,128]{2,1,0:T(8,128)(2,1)} %param.18) | data formatting | bytes 1048576 | tf_op args[7]
  14.8 8.0 %short_range.2.refs_1_ = f32[2,256,2048]{2,1,0:T(8,128)} custom-call(s32[1]{0:T(128)} %bitcast.1.half_ref, s32[16]{0:T(128)S(1)} %compare_convert_fusion.1.live_ref, s32[16]{0:T(128)S(1)} %copy-done.5, f32[3,16]{1,0:T(4,128)S(1)} %pad_maximum_fusion.1.meta_ref, bf16[128,4096]{1,0:T(8,128)(2,1)} %basis_ref.3, f32[1,4096]{1,0:T(1,128)S(1)} %bitcast.43, ...), custom_call_target="tpu_custom_call" | custom-call | flops 2147483648 | bytes 1 | tf_op jit(solution)/shard_map/short_range/pallas_call | solution.py:141
  23.0 7.5 %collective-permute-done.1 = bf16[256,1024]{1,0:T(8,128)(2,1)S(1)} collective-permute-done((bf16[256,1024]{1,0:T(8,128)(2,1)}, bf16[256,1024]{1,0:T(8,128)(2,1)S(1)}, u32[]{:S(2)}, u32[]{:S(2)}) %collective-permute-start.1) | collective-permute-done | bytes 524320 | tf_op jit(solution)/shard_map/ppermute | solution.py:455
  31.1 2.6 %collective-permute-start.6 = (bf16[256,1024]{1,0:T(8,128)(2,1)S(1)}, bf16[256,1024]{1,0:T(8,128)(2,1)}, u32[]{:S(2)}, u32[]{:S(2)}) collective-permute-start(bf16[256,1024]{1,0:T(8,128)(2,1)S(1)} %select_select_fusion.3), channel_id=1, source_target_pairs={{0,16},{1,17},{2,18},{3,19},{4,20},{5,21},{6,22},{7,23},{8,24},{9,... | collective-permute-start | bytes 1572872 | tf_op jit(solution)/shard_map/ppermute | solution.py:455
  33.7 1.6 %collective-permute-start.7 = (bf16[1024,256]{1,0:T(8,128)(2,1)S(1)}, bf16[1024,256]{1,0:T(8,128)(2,1)S(1)}, u32[]{:S(2)}, u32[]{:S(2)}) collective-permute-start(bf16[1024,256]{1,0:T(8,128)(2,1)S(1)} %collective-permute-done.4.refs_5_), channel_id=1, source_target_pairs={{0,2},{1,3},{2,0},{3,1},{4,6},{5,7},{6,4},{7,5},{8,10},{9,11},{10,... | collective-permute-start | bytes 1572872 | tf_op jit(solution)/shard_map/ppermute | solution.py:455
  37.0 6.7 %short_range.3.refs_6_.refs_8_.refs_1_ = f32[2048,512]{1,0:T(8,128)} custom-call(s32[1]{0:T(128)} %bitcast.1.half_ref, s32[16]{0:T(128)S(1)} %get-tuple-element.55.live_ref, s32[16]{0:T(128)S(1)} %get-tuple-element.54.sub_ref, f32[3,16]{1,0:T(4,128)S(1)} %pad_maximum_fusion.2.meta_ref, bf16[128,4096]{1,0:T(8,128)(2,1)} %basis_ref.3, f32[1,4096]{1,0:T(1,128)S(1)} %bitcast.44, ...), custom_call_target="tpu_custom_call" | custom-call | flops 2147483648 | bytes 1 | tf_op jit(solution)/shard_map/short_range/pallas_call | solution.py:141
  45.5 1.9 %select_select_fusion.2 = bf16[256,1024]{1,0:T(8,128)(2,1)} fusion(bf16[256,1024]{1,0:T(8,128)(2,1)} %collective-permute-done, bf16[256,1024]{1,0:T(8,128)(2,1)} %collective-permute-done.2, bf16[256,1024]{1,0:T(8,128)(2,1)} %copy-done.6, pred[]{:T(512)S(6)} %eq.80, pred[]{:T(512)S(6)} %eq.73), kind=kLoop, calls=%fused_computation.6 | loop fusion | flops 524288 | bytes 2097154 | tf_op jit(solution)/shard_map/jit(_where)/select_n | solution.py:489
  47.4 1.9 %collective-permute-start.11 = (bf16[256,1024]{1,0:T(8,128)(2,1)}, bf16[256,1024]{1,0:T(8,128)(2,1)S(1)}, u32[]{:S(2)}, u32[]{:S(2)}) collective-permute-start(bf16[256,1024]{1,0:T(8,128)(2,1)} %select_select_fusion.2), channel_id=1, source_target_pairs={{0,16},{1,17},{2,18},{3,19},{4,20},{5,21},{6,22},{7,23},{8,24},{9,... | collective-permute-start | bytes 1572872 | tf_op jit(solution)/shard_map/ppermute | solution.py:455
  49.4 2.5 %long_range.4 = bf16[256,512]{1,0:T(8,128)(2,1)} custom-call(bf16[256,1024]{1,0:T(8,128)(2,1)S(1)} %select_select_fusion.1.refs_0_, bf16[256,1024]{1,0:T(8,128)(2,1)} %collective-permute-done.6.refs_1_, bf16[1024,256]{1,0:T(8,128)(2,1)S(1)} %collective-permute-done.5.refs_2_, bf16[1024,256]{1,0:T(8,128)(2,1)S(1)} %collective-permute-done.7.refs_3_), custom_call_target="tpu_custom_call" | custom-call | flops 1 | bytes 1 | tf_op jit(solution)/shard_map/long_range/pallas_call | solution.py:221
  51.9 1.6 %collective-permute-start.15 = (bf16[256,512]{1,0:T(8,128)(2,1)}, bf16[256,512]{1,0:T(8,128)(2,1)S(1)}, u32[]{:S(2)}, u32[]{:S(2)}) collective-permute-start(bf16[256,512]{1,0:T(8,128)(2,1)} %long_range.4), channel_id=1, source_target_pairs={{0,2},{1,3},{2,0},{3,1},{4,6},{5,7},{6,4},{7,5},{8,10},{9,11},{10,... | collective-permute-start | bytes 786440 | tf_op jit(solution)/shard_map/ppermute | solution.py:455
  53.5 2.6 %long_range.5 = bf16[256,512]{1,0:T(8,128)(2,1)} custom-call(bf16[256,1024]{1,0:T(8,128)(2,1)} %collective-permute-done.8.refs_0_.refs_2_, bf16[256,1024]{1,0:T(8,128)(2,1)} %collective-permute-done.9.refs_1_.refs_3_, bf16[1024,256]{1,0:T(8,128)(2,1)S(1)} %collective-permute-done.5.refs_2_, bf16[1024,256]{1,0:T(8,128)(2,1)S(1)} %collective-permute-done.7.refs_3_), custom_call_target="tpu_custom_call" | custom-call | flops 1 | bytes 1 | tf_op jit(solution)/shard_map/long_range/pallas_call | solution.py:221
  56.7 4.9 %own_sum.2.refs_9_ = bf16[2048,2,256]{2,1,0:T(2,128)(2,1)} custom-call(s32[2]{0:T(128)S(1)} %pad_add_fusion.1.order_ref, bf16[256,1024]{1,0:T(8,128)(2,1)S(1)} %select_select_fusion.1.refs_0_, bf16[256,1024]{1,0:T(8,128)(2,1)} %collective-permute-done.6.refs_1_, bf16[256,1024]{1,0:T(8,128)(2,1)} %collective-permute-done.8.refs_0_.refs_2_, ...), custom_call_target="tpu_custom_call" | custom-call | flops 1 | bytes 1 | tf_op jit(solution)/shard_map/own_sum/pallas_call | solution.py:282
  63.5 1.4 %long_range.7 = bf16[256,512]{1,0:T(8,128)(2,1)} custom-call(bf16[256,1024]{1,0:T(8,128)(2,1)S(1)} %select_select_fusion.refs_0_, bf16[256,1024]{1,0:T(8,128)(2,1)S(1)} %collective-permute-done.11.refs_1_, bf16[1024,512]{1,0:T(8,128)(2,1)S(1)} %get-tuple-element.62.refs_2_, bf16[1024,512]{1,0:T(8,128)(2,1)S(1)} %get-tuple-element.63.refs_3_), custom_call_target="tpu_custom_call" | custom-call | flops 1 | bytes 1 | tf_op jit(solution)/shard_map/long_range/pallas_call | solution.py:221
  64.9 1.6 %collective-permute-start.14 = (bf16[256,512]{1,0:T(8,128)(2,1)}, bf16[256,512]{1,0:T(8,128)(2,1)S(1)}, u32[]{:S(2)}, u32[]{:S(2)}) collective-permute-start(bf16[256,512]{1,0:T(8,128)(2,1)} %long_range.7), channel_id=1, source_target_pairs={{0,2},{1,3},{2,0},{3,1},{4,6},{5,7},{6,4},{7,5},{8,10},{9,11},{10,... | collective-permute-start | bytes 786440 | tf_op jit(solution)/shard_map/ppermute | solution.py:455
  66.5 1.4 %long_range.6 = bf16[256,512]{1,0:T(8,128)(2,1)} custom-call(bf16[256,1024]{1,0:T(8,128)(2,1)S(1)} %collective-permute-done.10.refs_0_.refs_2_, bf16[256,1024]{1,0:T(8,128)(2,1)S(1)} %collective-permute-done.12.refs_1_.refs_3_, bf16[1024,512]{1,0:T(8,128)(2,1)S(1)} %get-tuple-element.62.refs_2_, bf16[1024,512]{1,0:T(8,128)(2,1)S(1)} %get-tuple-element.63.refs_3_), custom_call_target="tpu_custom_call" | custom-call | flops 1 | bytes 1 | tf_op jit(solution)/shard_map/long_range/pallas_call | solution.py:221
  70.8 4.9 %own_sum.3.refs_2_ = bf16[2048,2,256]{2,1,0:T(2,128)(2,1)} custom-call(s32[4]{0:T(128)S(1)} %pad_add_fusion.2.order_ref, bf16[256,1024]{1,0:T(8,128)(2,1)S(1)} %select_select_fusion.refs_0_, bf16[256,1024]{1,0:T(8,128)(2,1)S(1)} %collective-permute-done.11.refs_1_, bf16[256,1024]{1,0:T(8,128)(2,1)S(1)} %copy-done.1, ...), custom_call_target="tpu_custom_call", output_to_operand_aliasing={{}: (10, {})} | custom-call | flops 1 | bytes 1 | tf_op jit(solution)/shard_map/own_sum/pallas_call | solution.py:282
  75.7 2.0 %final_sum.2.refs_2_ = bf16[2048,2,256]{2,1,0:T(2,128)(2,1)} custom-call(s32[1]{0:T(128)} %bitcast.22.order_ref, bf16[256,512]{1,0:T(8,128)(2,1)S(1)} %collective-permute-done.14.refs_0_, f32[2048,512]{1,0:T(8,128)} %short_range.3.refs_6_.refs_8_.refs_1_, bf16[2048,2,256]{2,1,0:T(2,128)(2,1)} %own_sum.3.refs_2_), custom_call_target="tpu_custom_call", output_to_operand_aliasing={{}: (3, {})} | custom-call | flops 1 | bytes 1 | tf_op jit(solution)/shard_map/final_sum/pallas_call | solution.py:334
  77.7 1.5 %collective-permute-done.13.refs_0_ = bf16[256,512]{1,0:T(8,128)(2,1)S(1)} collective-permute-done((bf16[256,512]{1,0:T(8,128)(2,1)}, bf16[256,512]{1,0:T(8,128)(2,1)S(1)}, u32[]{:S(2)}, u32[]{:S(2)}) %collective-permute-start.13) | collective-permute-done | bytes 262176 | tf_op jit(solution)/shard_map/ppermute | solution.py:455
  79.1 2.0 %final_sum.3 = bf16[2048,2,256]{2,1,0:T(2,128)(2,1)} custom-call(s32[1]{0:T(128)} %bitcast.order_ref, bf16[256,512]{1,0:T(8,128)(2,1)S(1)} %collective-permute-done.13.refs_0_, f32[2048,512]{1,0:T(8,128)} %short_range.3.refs_6_.refs_8_.refs_1_, bf16[2048,2,256]{2,1,0:T(2,128)(2,1)} %final_sum.2.refs_2_), custom_call_target="tpu_custom_call", output_to_operand_aliasing={{}: (3, {})} | custom-call | flops 1 | bytes 1 | tf_op jit(solution)/shard_map/final_sum/pallas_call | solution.py:334
  (69 shorter events, 11.7 us)
Async XLA Ops:
  0.0 13.1 %copy-start.5 = (s32[16]{0:T(128)S(1)}, s32[16]{0:T(128)}, u32[]{:S(2)}) copy-start(s32[16]{0:T(128)} %sub_ref.1) | copy-start | bytes 196
  0.0 13.1 %copy-start.8 = (s32[16]{0:T(128)S(1)}, s32[16]{0:T(128)}, u32[]{:S(2)}) copy-start(s32[16]{0:T(128)} %param.19) | copy-start | bytes 196
  2.0 12.6 %copy-start.9 = (f32[125]{0:T(128)S(1)}, f32[125]{0:T(128)}, u32[]{:S(2)}) copy-start(f32[125]{0:T(128)} %param.16) | copy-start | bytes 1504
  2.0 12.6 %copy-start.10 = (f32[125]{0:T(128)S(1)}, f32[125]{0:T(128)}, u32[]{:S(2)}) copy-start(f32[125]{0:T(128)} %param.17) | copy-start | bytes 1504
  2.0 12.9 %copy-start.4 = (f32[4096]{0:T(1024)S(1)}, f32[4096]{0:T(1024)}, u32[]{:S(2)}) copy-start(f32[4096]{0:T(1024)} %param.15) | copy-start | bytes 49156
  2.0 21.0 %collective-permute-start = (bf16[256,1024]{1,0:T(8,128)(2,1)}, bf16[256,1024]{1,0:T(8,128)(2,1)}, u32[]{:S(2)}, u32[]{:S(2)}) collective-permute-start(bf16[256,1024]{1,0:T(8,128)(2,1)} %bitcast.28), channel_id=1, source_target_pairs={{0,8},{1,9},{2,10},{3,11},{4,0},{5,1},{6,2},{7,3},{8,12},{9,13},{1... | collective-permute-start | bytes 1572872 | tf_op jit(solution)/shard_map/ppermute | solution.py:455
  6.0 24.4 %collective-permute-start.1 = (bf16[256,1024]{1,0:T(8,128)(2,1)}, bf16[256,1024]{1,0:T(8,128)(2,1)S(1)}, u32[]{:S(2)}, u32[]{:S(2)}) collective-permute-start(bf16[256,1024]{1,0:T(8,128)(2,1)} %bitcast.28), channel_id=1, source_target_pairs={{0,4},{1,5},{2,6},{3,7},{4,12},{5,13},{6,14},{7,15},{8,0},{9,1},{1... | collective-permute-start | bytes 1572872 | tf_op jit(solution)/shard_map/ppermute | solution.py:455
  8.0 25.7 %collective-permute-start.4 = (bf16[1024,256]{1,0:T(8,128)(2,1)S(1)}, bf16[1024,256]{1,0:T(8,128)(2,1)S(1)}, u32[]{:S(2)}, u32[]{:S(2)}) collective-permute-start(bf16[1024,256]{1,0:T(8,128)(2,1)S(1)} %bitcast.39), channel_id=1, source_target_pairs={{0,16},{1,17},{2,18},{3,19},{4,20},{5,21},{6,22},{7,23},{8,24},{9,... | collective-permute-start | bytes 1572872 | tf_op jit(solution)/shard_map/ppermute | solution.py:455
  9.6 24.2 %collective-permute-start.5 = (bf16[1024,256]{1,0:T(8,128)(2,1)S(1)}, bf16[1024,256]{1,0:T(8,128)(2,1)S(1)}, u32[]{:S(2)}, u32[]{:S(2)}) collective-permute-start(bf16[1024,256]{1,0:T(8,128)(2,1)S(1)} %bitcast.40), channel_id=1, source_target_pairs={{0,2},{1,3},{2,0},{3,1},{4,6},{5,7},{6,4},{7,5},{8,10},{9,11},{10,... | collective-permute-start | bytes 1572872 | tf_op jit(solution)/shard_map/ppermute | solution.py:455
  14.0 22.7 %collective-permute-start.3 = (bf16[17,128,128]{2,1,0:T(8,128)(2,1)}, bf16[17,128,128]{2,1,0:T(8,128)(2,1)S(1)}, u32[]{:S(2)}, u32[]{:S(2)}) collective-permute-start(bf16[17,128,128]{2,1,0:T(8,128)(2,1)} %pad_maximum_fusion.refs_0_), channel_id=1, source_target_pairs={{0,16},{1,17},{2,18},{3,19},{4,20},{5,21},{6,22},{7,23},{8,24},{9,... | collective-permute-start | bytes 1671176 | tf_op jit(solution)/shard_map/ppermute | solution.py:455
  30.4 3.3 %copy-start.6 = (bf16[256,1024]{1,0:T(8,128)(2,1)}, bf16[256,1024]{1,0:T(8,128)(2,1)S(1)}, u32[]{:S(2)}) copy-start(bf16[256,1024]{1,0:T(8,128)(2,1)S(1)} %collective-permute-done.1) | copy-start | bytes 1572868
  30.4 14.2 %collective-permute-start.2 = (bf16[256,1024]{1,0:T(8,128)(2,1)}, bf16[256,1024]{1,0:T(8,128)(2,1)}, u32[]{:S(2)}, u32[]{:S(2)}) collective-permute-start(bf16[256,1024]{1,0:T(8,128)(2,1)} %collective-permute-done), channel_id=1, source_target_pairs={{0,8},{1,9},{2,10},{3,11},{4,0},{5,1},{6,2},{7,3},{8,12},{9,13},{1... | collective-permute-start | bytes 1572872 | tf_op jit(solution)/shard_map/ppermute | solution.py:455
  31.1 14.4 %collective-permute-start.6 = (bf16[256,1024]{1,0:T(8,128)(2,1)S(1)}, bf16[256,1024]{1,0:T(8,128)(2,1)}, u32[]{:S(2)}, u32[]{:S(2)}) collective-permute-start(bf16[256,1024]{1,0:T(8,128)(2,1)S(1)} %select_select_fusion.3), channel_id=1, source_target_pairs={{0,16},{1,17},{2,18},{3,19},{4,20},{5,21},{6,22},{7,23},{8,24},{9,... | collective-permute-start | bytes 1572872 | tf_op jit(solution)/shard_map/ppermute | solution.py:455
  33.7 15.7 %collective-permute-start.7 = (bf16[1024,256]{1,0:T(8,128)(2,1)S(1)}, bf16[1024,256]{1,0:T(8,128)(2,1)S(1)}, u32[]{:S(2)}, u32[]{:S(2)}) collective-permute-start(bf16[1024,256]{1,0:T(8,128)(2,1)S(1)} %collective-permute-done.4.refs_5_), channel_id=1, source_target_pairs={{0,2},{1,3},{2,0},{3,1},{4,6},{5,7},{6,4},{7,5},{8,10},{9,11},{10,... | collective-permute-start | bytes 1572872 | tf_op jit(solution)/shard_map/ppermute | solution.py:455
  36.6 16.9 %collective-permute-start.8 = (bf16[256,1024]{1,0:T(8,128)(2,1)S(1)}, bf16[256,1024]{1,0:T(8,128)(2,1)}, u32[]{:S(2)}, u32[]{:S(2)}) collective-permute-start(bf16[256,1024]{1,0:T(8,128)(2,1)S(1)} %select_select_fusion.1.refs_0_), channel_id=1, source_target_pairs={{0,1},{1,0},{2,3},{3,2},{4,5},{5,4},{6,7},{7,6},{8,9},{9,8},{10,11... | collective-permute-start | bytes 1572872 | tf_op jit(solution)/shard_map/ppermute | solution.py:455
  45.5 8.0 %collective-permute-start.9 = (bf16[256,1024]{1,0:T(8,128)(2,1)}, bf16[256,1024]{1,0:T(8,128)(2,1)}, u32[]{:S(2)}, u32[]{:S(2)}) collective-permute-start(bf16[256,1024]{1,0:T(8,128)(2,1)} %collective-permute-done.6.refs_1_), channel_id=1, source_target_pairs={{0,1},{1,0},{2,3},{3,2},{4,5},{5,4},{6,7},{7,6},{8,9},{9,8},{10,11... | collective-permute-start | bytes 1572872 | tf_op jit(solution)/shard_map/ppermute | solution.py:455
  47.4 15.3 %collective-permute-start.11 = (bf16[256,1024]{1,0:T(8,128)(2,1)}, bf16[256,1024]{1,0:T(8,128)(2,1)S(1)}, u32[]{:S(2)}, u32[]{:S(2)}) collective-permute-start(bf16[256,1024]{1,0:T(8,128)(2,1)} %select_select_fusion.2), channel_id=1, source_target_pairs={{0,16},{1,17},{2,18},{3,19},{4,20},{5,21},{6,22},{7,23},{8,24},{9,... | collective-permute-start | bytes 1572872 | tf_op jit(solution)/shard_map/ppermute | solution.py:455
  51.9 16.8 %collective-permute-start.15 = (bf16[256,512]{1,0:T(8,128)(2,1)}, bf16[256,512]{1,0:T(8,128)(2,1)S(1)}, u32[]{:S(2)}, u32[]{:S(2)}) collective-permute-start(bf16[256,512]{1,0:T(8,128)(2,1)} %long_range.4), channel_id=1, source_target_pairs={{0,2},{1,3},{2,0},{3,1},{4,6},{5,7},{6,4},{7,5},{8,10},{9,11},{10,... | collective-permute-start | bytes 786440 | tf_op jit(solution)/shard_map/ppermute | solution.py:455
  56.1 5.4 %copy-start.7 = (bf16[256,1024]{1,0:T(8,128)(2,1)S(1)}, bf16[256,1024]{1,0:T(8,128)(2,1)}, u32[]{:S(2)}) copy-start(bf16[256,1024]{1,0:T(8,128)(2,1)} %copy-done.6) | copy-start | bytes 1572868
  56.1 12.6 %collective-permute-start.16 = (bf16[256,512]{1,0:T(8,128)(2,1)}, bf16[256,512]{1,0:T(8,128)(2,1)}, u32[]{:S(2)}, u32[]{:S(2)}) collective-permute-start(bf16[256,512]{1,0:T(8,128)(2,1)} %long_range.5), channel_id=1, source_target_pairs={{0,2},{1,3},{2,0},{3,1},{4,6},{5,7},{6,4},{7,5},{8,10},{9,11},{10,... | collective-permute-start | bytes 786440 | tf_op jit(solution)/shard_map/ppermute | solution.py:455
  62.7 3.9 %collective-permute-start.10 = (bf16[256,1024]{1,0:T(8,128)(2,1)S(1)}, bf16[256,1024]{1,0:T(8,128)(2,1)S(1)}, u32[]{:S(2)}, u32[]{:S(2)}) collective-permute-start(bf16[256,1024]{1,0:T(8,128)(2,1)S(1)} %select_select_fusion.refs_0_), channel_id=1, source_target_pairs={{0,1},{1,0},{2,3},{3,2},{4,5},{5,4},{6,7},{7,6},{8,9},{9,8},{10,11... | collective-permute-start | bytes 1572872 | tf_op jit(solution)/shard_map/ppermute | solution.py:455
  62.8 3.8 %collective-permute-start.12 = (bf16[256,1024]{1,0:T(8,128)(2,1)S(1)}, bf16[256,1024]{1,0:T(8,128)(2,1)S(1)}, u32[]{:S(2)}, u32[]{:S(2)}) collective-permute-start(bf16[256,1024]{1,0:T(8,128)(2,1)S(1)} %collective-permute-done.11.refs_1_), channel_id=1, source_target_pairs={{0,1},{1,0},{2,3},{3,2},{4,5},{5,4},{6,7},{7,6},{8,9},{9,8},{10,11... | collective-permute-start | bytes 1572872 | tf_op jit(solution)/shard_map/ppermute | solution.py:455
  64.9 10.7 %collective-permute-start.14 = (bf16[256,512]{1,0:T(8,128)(2,1)}, bf16[256,512]{1,0:T(8,128)(2,1)S(1)}, u32[]{:S(2)}, u32[]{:S(2)}) collective-permute-start(bf16[256,512]{1,0:T(8,128)(2,1)} %long_range.7), channel_id=1, source_target_pairs={{0,2},{1,3},{2,0},{3,1},{4,6},{5,7},{6,4},{7,5},{8,10},{9,11},{10,... | collective-permute-start | bytes 786440 | tf_op jit(solution)/shard_map/ppermute | solution.py:455
  68.0 11.1 %collective-permute-start.13 = (bf16[256,512]{1,0:T(8,128)(2,1)}, bf16[256,512]{1,0:T(8,128)(2,1)S(1)}, u32[]{:S(2)}, u32[]{:S(2)}) collective-permute-start(bf16[256,512]{1,0:T(8,128)(2,1)} %long_range.6), channel_id=1, source_target_pairs={{0,2},{1,3},{2,0},{3,1},{4,6},{5,7},{6,4},{7,5},{8,10},{9,11},{10,... | collective-permute-start | bytes 786440 | tf_op jit(solution)/shard_map/ppermute | solution.py:455
  (4 other events, 5.0 us)

commit v19 on v18

--- a/solution.py
+++ b/solution.py
@@ -239,10 +239,17 @@
     factors = refs[blocks * chains : (blocks + 1) * chains]
     arrived = refs[(blocks + 1) * chains :][:pieces]
     short_ref = refs[(blocks + 1) * chains + pieces]
-    out_ref, right, terms, made, term_sem, out_sem = refs[(blocks + 1) * chains + pieces + 1 + aliased :]
+    out_ref, right, terms, made, right_sem, term_sem, out_sem = refs[
+        (blocks + 1) * chains + pieces + 1 + aliased :
+    ]
     rows = terms.shape[1]
     depth, width = factors[0].shape
     half = depth // 2
+    right_copies = []
+    for chain, factor in enumerate(factors):
+        target = right.at[pl.ds(chain * depth, depth), pl.ds(0, width)]
+        right_copies.append(pltpu.make_async_copy(factor, target, right_sem.at[chain]))
+        right_copies[-1].start()
     windows = [pl.ds(pl.multiple_of(order_ref[n] * rows, rows), rows) for n in range(blocks + pieces)]
     arriving = []
     for n, window in enumerate(windows):
@@ -250,11 +257,11 @@
             pltpu.make_async_copy(short_ref.at[window, :], terms.at[n], term_sem.at[n])
         )
         arriving[-1].start()
-    for chain, factor in enumerate(factors):
+    for chain, copy in enumerate(right_copies):
+        copy.wait()
         top = chain * depth
-        right[top : top + depth, 0:width] = factor[...]
-        right[top : top + half, width:] = factor[half:, :]
-        right[top + half : top + depth, width:] = -factor[0:half, :]
+        right[top : top + half, width:] = right[top + half : top + depth, 0:width]
+        right[top + half : top + depth, width:] = -right[top : top + half, 0:width]
     leaving = []
     for n, window in enumerate(windows):
         if n < blocks:
@@ -278,20 +285,23 @@
     chains = len(factors)
     count = len(blocks) + len(pieces)
     aliased = earlier is not None
-    flat = [v for group in [*blocks, factors, pieces] for v in group]
+    flat = [v for group in blocks for v in group] + [in_hbm(v) for v in factors] + pieces
     return pl.pallas_call(
         functools.partial(
             own_kernel, blocks=len(blocks), chains=chains, pieces=len(pieces), aliased=aliased
         ),
         out_shape=pltpu.HBM((row_count, 2, width), jnp.bfloat16),
         in_specs=[pl.BlockSpec(memory_space=pltpu.SMEM)]
-        + [pl.BlockSpec(memory_space=pltpu.VMEM)] * len(flat)
+        + [pl.BlockSpec(memory_space=pltpu.VMEM)] * (chains * len(blocks))
+        + [pl.BlockSpec(memory_space=pltpu.HBM)] * chains
+        + [pl.BlockSpec(memory_space=pltpu.VMEM)] * len(pieces)
         + [pl.BlockSpec(memory_space=pltpu.HBM)] * (1 + aliased),
         out_specs=pl.BlockSpec(memory_space=pltpu.HBM),
         scratch_shapes=[
             pltpu.VMEM((chains * depth, 2 * width), jnp.bfloat16),
             pltpu.VMEM((count, rows, columns), jnp.float32),
             pltpu.VMEM((count, rows, 2, width), jnp.bfloat16),
+            pltpu.SemaphoreType.DMA((chains,)),
             pltpu.SemaphoreType.DMA((count,)),
             pltpu.SemaphoreType.DMA((count,)),
         ],

time: 81.9 us -> 81.4 us (level)
  waiting for transfers between devices: 10.8 us -> 16.2 us
  starting transfers between devices: 19.3 us -> 16 us
  local copies, waits for them, and re-layouts: 6.01 us -> 3.96 us
  Pallas kernels: 36.3 us -> 35.2 us
    ppermute x17, waiting for transfers between devices: 10.8 us -> 16.2 us  [send(): return lax.ppermute(value, AXES, pairs)]
    ppermute x17, starting transfers between devices: 19.3 us -> 16 us  [send(): return lax.ppermute(value, AXES, pairs)]
    unnamed x24, local copies, waits for them, and re-layouts: 5.38 us -> 3.32 us
    pallas_call x4, Pallas kernels: 7.94 us -> 6.77 us  [long_range(): pl.pallas_call(functools.partial(long_kernel, blocks=len(blocks), chains=...]
    pallas_call x2, Pallas kernels: 9.77 us -> 10.8 us  [own_sum(): pl.pallas_call(functools.partial(own_kernel, blocks=len(blocks), chains=c...]
    pallas_call x2, Pallas kernels: 14.7 us -> 13.7 us  [short_range(): pl.pallas_call(kernel, out_shape=pltpu.HBM((row_count, 2 * subs * width)...]
  transfers between devices with their start and end apart: 17 -> 17, of which waited for: 4 -> 4; matrix products, arithmetic and copies ran while one was open for 12% -> 12% of each run, Pallas kernels for 42% -> 41%
where the time goes in v19:
time: 81.4 us; the launch traced here: 80.7 us
  Pallas kernels  35.2 us (43%)
  waiting for transfers between devices  16.2 us (20%)
  starting transfers between devices  16 us (20%)
  other arithmetic  8.03 us (10%)
  local copies, waits for them, and re-layouts  3.96 us (5%)
  between operations  1.3 us (2%)
    ppermute x17, waiting for transfers between devices, send(): return lax.ppermute(value, AXES, pairs)  16.2 us
    ppermute x17, starting transfers between devices, send(): return lax.ppermute(value, AXES, pairs)  16 us
    pallas_call x2, Pallas kernels, short_range(): pl.pallas_call(kernel, out_shape=pltpu.HBM((row_count, 2 * subs * width)...  13.7 us
    pallas_call x2, Pallas kernels, own_sum(): pl.pallas_call(functools.partial(own_kernel, blocks=len(blocks), chains=c...  10.8 us
    pallas_call x4, Pallas kernels, long_range(): pl.pallas_call(functools.partial(long_kernel, blocks=len(blocks), chains=...  6.77 us
    select_n x4, other arithmetic, pick(): value = jnp.where(wanted == k, block, value)  4.23 us
    pallas_call x2, Pallas kernels, final_sum(): pl.pallas_call(functools.partial(final_kernel, pieces=count, blocks=block...  3.94 us
    unnamed x24, local copies, waits for them, and re-layouts  3.32 us
  transfers between devices with their start and end apart: 17, of which 4 were waited for; matrix products, arithmetic and copies ran while one was open for 12% of the time, Pallas kernels for 41%

profile of v19, /device:TPU:0, one launch (start us, length us, event | category | flops | bytes accessed | tf_op | source)
XLA Modules:
  0.0 80.7 jit_solution(14749224938874789258)
XLA Ops:
  0.0 1.1 %copy.19 = bf16[32,8,2,512]{3,1,2,0:T(8,128)(2,1)S(1)} copy(bf16[32,8,2,512]{3,2,1,0:T(2,128)(2,1)} %bitcast.51) | data formatting | bytes 1048576
  1.2 4.1 %collective-permute-start = (bf16[256,1024]{1,0:T(8,128)(2,1)S(1)}, bf16[256,1024]{1,0:T(8,128)(2,1)}, u32[]{:S(2)}, u32[]{:S(2)}) collective-permute-start(bf16[256,1024]{1,0:T(8,128)(2,1)S(1)} %bitcast.46), channel_id=1, source_target_pairs={{0,8},{1,9},{2,10},{3,11},{4,0},{5,1},{6,2},{7,3},{8,12},{9,13},{1... | collective-permute-start | bytes 1572872 | tf_op jit(solution)/shard_map/ppermute | solution.py:465
  5.3 1.5 %multiply_convert_fusion = bf16[256,2,512]{2,1,0:T(2,128)(2,1)S(1)} fusion(bf16[256,2,512]{2,1,0:T(2,128)(2,1)} %param.11, f32[512]{0:T(512)} %param.13), kind=kLoop, calls=%fused_computation.2 | loop fusion | flops 786432 | bytes 1050624 | tf_op jit(solution)/shard_map/convert_element_type | solution.py:423
  7.3 1.6 %collective-permute-start.4 = (bf16[1024,256]{1,0:T(8,128)(2,1)S(1)}, bf16[1024,256]{1,0:T(8,128)(2,1)}, u32[]{:S(2)}, u32[]{:S(2)}) collective-permute-start(bf16[1024,256]{1,0:T(8,128)(2,1)S(1)} %bitcast.42), channel_id=1, source_target_pairs={{0,16},{1,17},{2,18},{3,19},{4,20},{5,21},{6,22},{7,23},{8,24},{9,... | collective-permute-start | bytes 1572872 | tf_op jit(solution)/shard_map/ppermute | solution.py:465
  8.9 1.5 %collective-permute-start.5 = (bf16[1024,256]{1,0:T(8,128)(2,1)S(1)}, bf16[1024,256]{1,0:T(8,128)(2,1)S(1)}, u32[]{:S(2)}, u32[]{:S(2)}) collective-permute-start(bf16[1024,256]{1,0:T(8,128)(2,1)S(1)} %bitcast.43), channel_id=1, source_target_pairs={{0,2},{1,3},{2,0},{3,1},{4,6},{5,7},{6,4},{7,5},{8,10},{9,11},{10,... | collective-permute-start | bytes 1572872 | tf_op jit(solution)/shard_map/ppermute | solution.py:465
  11.0 1.4 %copy.17 = bf16[16,128,128]{1,2,0:T(8,128)(2,1)S(1)} copy(bf16[16,128,128]{2,1,0:T(8,128)(2,1)} %param.18) | data formatting | bytes 1048576 | tf_op args[7]
  14.2 4.2 %short_range.2.refs_1_ = f32[2,256,2048]{2,1,0:T(8,128)} custom-call(s32[1]{0:T(128)} %bitcast.1.half_ref, s32[16]{0:T(128)S(1)} %compare_convert_fusion.1.live_ref, s32[16]{0:T(128)S(1)} %copy-done.1, f32[3,16]{1,0:T(4,128)S(1)} %pad_maximum_fusion.1.meta_ref, bf16[128,4096]{1,0:T(8,128)(2,1)} %basis_ref.3, f32[1,4096]{1,0:T(1,128)S(1)} %bitcast.39, ...), custom_call_target="tpu_custom_call" | custom-call | flops 2147483648 | bytes 1 | tf_op jit(solution)/shard_map/short_range/pallas_call | solution.py:141
  18.4 11.1 %collective-permute-done.1 = bf16[256,1024]{1,0:T(8,128)(2,1)S(1)} collective-permute-done((bf16[256,1024]{1,0:T(8,128)(2,1)S(1)}, bf16[256,1024]{1,0:T(8,128)(2,1)S(1)}, u32[]{:S(2)}, u32[]{:S(2)}) %collective-permute-start.1) | collective-permute-done | bytes 524320 | tf_op jit(solution)/shard_map/ppermute | solution.py:465
  30.2 1.6 %collective-permute-start.6 = (bf16[256,1024]{1,0:T(8,128)(2,1)S(1)}, bf16[256,1024]{1,0:T(8,128)(2,1)S(1)}, u32[]{:S(2)}, u32[]{:S(2)}) collective-permute-start(bf16[256,1024]{1,0:T(8,128)(2,1)S(1)} %select_select_fusion.3), channel_id=1, source_target_pairs={{0,16},{1,17},{2,18},{3,19},{4,20},{5,21},{6,22},{7,23},{8,24},{9,... | collective-permute-start | bytes 1572872 | tf_op jit(solution)/shard_map/ppermute | solution.py:465
  31.8 1.5 %collective-permute-start.7 = (bf16[1024,256]{1,0:T(8,128)(2,1)}, bf16[1024,256]{1,0:T(8,128)(2,1)S(1)}, u32[]{:S(2)}, u32[]{:S(2)}) collective-permute-start(bf16[1024,256]{1,0:T(8,128)(2,1)} %collective-permute-done.4.refs_5_), channel_id=1, source_target_pairs={{0,2},{1,3},{2,0},{3,1},{4,6},{5,7},{6,4},{7,5},{8,10},{9,11},{10,... | collective-permute-start | bytes 1572872 | tf_op jit(solution)/shard_map/ppermute | solution.py:465
  35.4 9.6 %short_range.3.refs_6_.refs_8_.refs_1_ = f32[2048,512]{1,0:T(8,128)} custom-call(s32[1]{0:T(128)} %bitcast.1.half_ref, s32[16]{0:T(128)S(1)} %get-tuple-element.55.live_ref, s32[16]{0:T(128)S(1)} %get-tuple-element.54.sub_ref, f32[3,16]{1,0:T(4,128)S(1)} %pad_maximum_fusion.2.meta_ref, bf16[128,4096]{1,0:T(8,128)(2,1)} %basis_ref.3, f32[1,4096]{1,0:T(1,128)S(1)} %bitcast.40, ...), custom_call_target="tpu_custom_call" | custom-call | flops 2147483648 | bytes 1 | tf_op jit(solution)/shard_map/short_range/pallas_call | solution.py:141
  45.8 1.9 %select_select_fusion.2 = bf16[256,1024]{1,0:T(8,128)(2,1)} fusion(bf16[256,1024]{1,0:T(8,128)(2,1)} %collective-permute-done, bf16[256,1024]{1,0:T(8,128)(2,1)} %copy-done.6, bf16[256,1024]{1,0:T(8,128)(2,1)} %copy-done.2, pred[]{:T(512)S(6)} %eq.80, pred[]{:T(512)S(6)} %eq.73), kind=kLoop, calls=%fused_computation.6 | loop fusion | flops 524288 | bytes 2097154 | tf_op jit(solution)/shard_map/jit(_where)/select_n | solution.py:499
  48.0 1.4 %long_range.4 = bf16[256,512]{1,0:T(8,128)(2,1)} custom-call(bf16[256,1024]{1,0:T(8,128)(2,1)S(1)} %select_select_fusion.1.refs_0_, bf16[256,1024]{1,0:T(8,128)(2,1)S(1)} %collective-permute-done.6.refs_1_, bf16[1024,256]{1,0:T(8,128)(2,1)S(1)} %collective-permute-done.5.refs_2_, bf16[1024,256]{1,0:T(8,128)(2,1)S(1)} %collective-permute-done.7.refs_3_), custom_call_target="tpu_custom_call" | custom-call | flops 1 | bytes 1 | tf_op jit(solution)/shard_map/long_range/pallas_call | solution.py:221
  49.4 1.6 %collective-permute-start.15 = (bf16[256,512]{1,0:T(8,128)(2,1)}, bf16[256,512]{1,0:T(8,128)(2,1)S(1)}, u32[]{:S(2)}, u32[]{:S(2)}) collective-permute-start(bf16[256,512]{1,0:T(8,128)(2,1)} %long_range.4), channel_id=1, source_target_pairs={{0,2},{1,3},{2,0},{3,1},{4,6},{5,7},{6,4},{7,5},{8,10},{9,11},{10,... | collective-permute-start | bytes 786440 | tf_op jit(solution)/shard_map/ppermute | solution.py:465
  51.0 2.5 %long_range.5 = bf16[256,512]{1,0:T(8,128)(2,1)} custom-call(bf16[256,1024]{1,0:T(8,128)(2,1)S(1)} %collective-permute-done.8.refs_0_.refs_2_, bf16[256,1024]{1,0:T(8,128)(2,1)} %collective-permute-done.9.refs_1_.refs_3_, bf16[1024,256]{1,0:T(8,128)(2,1)S(1)} %collective-permute-done.5.refs_2_, bf16[1024,256]{1,0:T(8,128)(2,1)S(1)} %collective-permute-done.7.refs_3_), custom_call_target="tpu_custom_call" | custom-call | flops 1 | bytes 1 | tf_op jit(solution)/shard_map/long_range/pallas_call | solution.py:221
  54.1 5.0 %own_sum.2.refs_9_ = bf16[2048,2,256]{2,1,0:T(2,128)(2,1)} custom-call(s32[2]{0:T(128)S(1)} %pad_add_fusion.1.order_ref, bf16[256,1024]{1,0:T(8,128)(2,1)S(1)} %select_select_fusion.1.refs_0_, bf16[256,1024]{1,0:T(8,128)(2,1)S(1)} %collective-permute-done.6.refs_1_, bf16[256,1024]{1,0:T(8,128)(2,1)S(1)} %collective-permute-done.8.refs_0_.refs_2_, ...), custom_call_target="tpu_custom_call" | custom-call | flops 1 | bytes 1 | tf_op jit(solution)/shard_map/own_sum/pallas_call | solution.py:289
  60.3 2.0 %collective-permute-done.11.refs_1_ = bf16[256,1024]{1,0:T(8,128)(2,1)S(1)} collective-permute-done((bf16[256,1024]{1,0:T(8,128)(2,1)}, bf16[256,1024]{1,0:T(8,128)(2,1)S(1)}, u32[]{:S(2)}, u32[]{:S(2)}) %collective-permute-start.11) | collective-permute-done | bytes 524320 | tf_op jit(solution)/shard_map/ppermute | solution.py:465
  62.5 1.4 %long_range.7 = bf16[256,512]{1,0:T(8,128)(2,1)} custom-call(bf16[256,1024]{1,0:T(8,128)(2,1)S(1)} %select_select_fusion.refs_0_, bf16[256,1024]{1,0:T(8,128)(2,1)S(1)} %collective-permute-done.11.refs_1_, bf16[1024,512]{1,0:T(8,128)(2,1)S(1)} %get-tuple-element.62.refs_2_, bf16[1024,512]{1,0:T(8,128)(2,1)S(1)} %get-tuple-element.63.refs_3_), custom_call_target="tpu_custom_call" | custom-call | flops 1 | bytes 1 | tf_op jit(solution)/shard_map/long_range/pallas_call | solution.py:221
  64.2 1.4 %long_range.6 = bf16[256,512]{1,0:T(8,128)(2,1)} custom-call(bf16[256,1024]{1,0:T(8,128)(2,1)S(1)} %collective-permute-done.10.refs_0_.refs_2_, bf16[256,1024]{1,0:T(8,128)(2,1)S(1)} %collective-permute-done.12.refs_1_.refs_3_, bf16[1024,512]{1,0:T(8,128)(2,1)S(1)} %get-tuple-element.62.refs_2_, bf16[1024,512]{1,0:T(8,128)(2,1)S(1)} %get-tuple-element.63.refs_3_), custom_call_target="tpu_custom_call" | custom-call | flops 1 | bytes 1 | tf_op jit(solution)/shard_map/long_range/pallas_call | solution.py:221
  65.6 1.9 %collective-permute-start.13 = (bf16[256,512]{1,0:T(8,128)(2,1)}, bf16[256,512]{1,0:T(8,128)(2,1)S(1)}, u32[]{:S(2)}, u32[]{:S(2)}) collective-permute-start(bf16[256,512]{1,0:T(8,128)(2,1)} %long_range.6), channel_id=1, source_target_pairs={{0,2},{1,3},{2,0},{3,1},{4,6},{5,7},{6,4},{7,5},{8,10},{9,11},{10,... | collective-permute-start | bytes 786440 | tf_op jit(solution)/shard_map/ppermute | solution.py:465
  67.7 5.8 %own_sum.3.refs_2_ = bf16[2048,2,256]{2,1,0:T(2,128)(2,1)} custom-call(s32[4]{0:T(128)S(1)} %pad_add_fusion.2.order_ref, bf16[256,1024]{1,0:T(8,128)(2,1)S(1)} %select_select_fusion.refs_0_, bf16[256,1024]{1,0:T(8,128)(2,1)S(1)} %collective-permute-done.11.refs_1_, ...), custom_call_target="tpu_custom_call", output_to_operand_aliasing={{}: (10, {})} | custom-call | flops 1 | bytes 1 | tf_op jit(solution)/shard_map/own_sum/pallas_call | solution.py:289
  73.5 2.0 %final_sum.2.refs_2_ = bf16[2048,2,256]{2,1,0:T(2,128)(2,1)} custom-call(s32[1]{0:T(128)} %bitcast.22.order_ref, bf16[256,512]{1,0:T(8,128)(2,1)S(1)} %collective-permute-done.14.refs_0_, f32[2048,512]{1,0:T(8,128)} %short_range.3.refs_6_.refs_8_.refs_1_, bf16[2048,2,256]{2,1,0:T(2,128)(2,1)} %own_sum.3.refs_2_), custom_call_target="tpu_custom_call", output_to_operand_aliasing={{}: (3, {})} | custom-call | flops 1 | bytes 1 | tf_op jit(solution)/shard_map/final_sum/pallas_call | solution.py:344
  75.5 3.1 %collective-permute-done.13.refs_0_ = bf16[256,512]{1,0:T(8,128)(2,1)S(1)} collective-permute-done((bf16[256,512]{1,0:T(8,128)(2,1)}, bf16[256,512]{1,0:T(8,128)(2,1)S(1)}, u32[]{:S(2)}, u32[]{:S(2)}) %collective-permute-start.13) | collective-permute-done | bytes 262176 | tf_op jit(solution)/shard_map/ppermute | solution.py:465
  78.6 2.0 %final_sum.3 = bf16[2048,2,256]{2,1,0:T(2,128)(2,1)} custom-call(s32[1]{0:T(128)} %bitcast.order_ref, bf16[256,512]{1,0:T(8,128)(2,1)S(1)} %collective-permute-done.13.refs_0_, f32[2048,512]{1,0:T(8,128)} %short_range.3.refs_6_.refs_8_.refs_1_, bf16[2048,2,256]{2,1,0:T(2,128)(2,1)} %final_sum.2.refs_2_), custom_call_target="tpu_custom_call", output_to_operand_aliasing={{}: (3, {})} | custom-call | flops 1 | bytes 1 | tf_op jit(solution)/shard_map/final_sum/pallas_call | solution.py:344
  (69 shorter events, 8.4 us)
Async XLA Ops:
  0.0 12.4 %copy-start.1 = (s32[16]{0:T(128)S(1)}, s32[16]{0:T(128)}, u32[]{:S(2)}) copy-start(s32[16]{0:T(128)} %sub_ref.1) | copy-start | bytes 196
  0.0 12.4 %copy-start.8 = (s32[16]{0:T(128)S(1)}, s32[16]{0:T(128)}, u32[]{:S(2)}) copy-start(s32[16]{0:T(128)} %param.19) | copy-start | bytes 196
  1.1 29.0 %copy-start.5 = (bf16[32,8,2,512]{3,1,2,0:T(8,128)(2,1)}, bf16[32,8,2,512]{3,1,2,0:T(8,128)(2,1)S(1)}, u32[]{:S(2)}) copy-start(bf16[32,8,2,512]{3,1,2,0:T(8,128)(2,1)S(1)} %copy.19) | copy-start | bytes 1572868
  1.2 12.7 %copy-start.9 = (f32[125]{0:T(128)S(1)}, f32[125]{0:T(128)}, u32[]{:S(2)}) copy-start(f32[125]{0:T(128)} %param.16) | copy-start | bytes 1504
  1.2 12.7 %copy-start.10 = (f32[125]{0:T(128)S(1)}, f32[125]{0:T(128)}, u32[]{:S(2)}) copy-start(f32[125]{0:T(128)} %param.17) | copy-start | bytes 1504
  1.2 13.0 %copy-start = (f32[4096]{0:T(1024)S(1)}, f32[4096]{0:T(1024)}, u32[]{:S(2)}) copy-start(f32[4096]{0:T(1024)} %param.15) | copy-start | bytes 49156
  1.2 17.2 %collective-permute-start = (bf16[256,1024]{1,0:T(8,128)(2,1)S(1)}, bf16[256,1024]{1,0:T(8,128)(2,1)}, u32[]{:S(2)}, u32[]{:S(2)}) collective-permute-start(bf16[256,1024]{1,0:T(8,128)(2,1)S(1)} %bitcast.46), channel_id=1, source_target_pairs={{0,8},{1,9},{2,10},{3,11},{4,0},{5,1},{6,2},{7,3},{8,12},{9,13},{1... | collective-permute-start | bytes 1572872 | tf_op jit(solution)/shard_map/ppermute | solution.py:465
  5.3 24.2 %collective-permute-start.1 = (bf16[256,1024]{1,0:T(8,128)(2,1)S(1)}, bf16[256,1024]{1,0:T(8,128)(2,1)S(1)}, u32[]{:S(2)}, u32[]{:S(2)}) collective-permute-start(bf16[256,1024]{1,0:T(8,128)(2,1)S(1)} %bitcast.47), channel_id=1, source_target_pairs={{0,4},{1,5},{2,6},{3,7},{4,12},{5,13},{6,14},{7,15},{8,0},{9,1},{1... | collective-permute-start | bytes 1572872 | tf_op jit(solution)/shard_map/ppermute | solution.py:465
  7.3 11.0 %copy-start.4 = (bf16[256,2,512]{0,2,1:T(8,128)(2,1)}, bf16[256,2,512]{0,2,1:T(8,128)(2,1)S(1)}, u32[]{:S(2)}) copy-start(bf16[256,2,512]{0,2,1:T(8,128)(2,1)S(1)} %copy.18) | copy-start | bytes 1572868
  7.3 24.5 %collective-permute-start.4 = (bf16[1024,256]{1,0:T(8,128)(2,1)S(1)}, bf16[1024,256]{1,0:T(8,128)(2,1)}, u32[]{:S(2)}, u32[]{:S(2)}) collective-permute-start(bf16[1024,256]{1,0:T(8,128)(2,1)S(1)} %bitcast.42), channel_id=1, source_target_pairs={{0,16},{1,17},{2,18},{3,19},{4,20},{5,21},{6,22},{7,23},{8,24},{9,... | collective-permute-start | bytes 1572872 | tf_op jit(solution)/shard_map/ppermute | solution.py:465
  8.9 22.9 %collective-permute-start.5 = (bf16[1024,256]{1,0:T(8,128)(2,1)S(1)}, bf16[1024,256]{1,0:T(8,128)(2,1)S(1)}, u32[]{:S(2)}, u32[]{:S(2)}) collective-permute-start(bf16[1024,256]{1,0:T(8,128)(2,1)S(1)} %bitcast.43), channel_id=1, source_target_pairs={{0,2},{1,3},{2,0},{3,1},{4,6},{5,7},{6,4},{7,5},{8,10},{9,11},{10,... | collective-permute-start | bytes 1572872 | tf_op jit(solution)/shard_map/ppermute | solution.py:465
  13.3 21.2 %collective-permute-start.3 = (bf16[17,128,128]{2,1,0:T(8,128)(2,1)}, bf16[17,128,128]{2,1,0:T(8,128)(2,1)}, u32[]{:S(2)}, u32[]{:S(2)}) collective-permute-start(bf16[17,128,128]{2,1,0:T(8,128)(2,1)} %pad_maximum_fusion.refs_0_), channel_id=1, source_target_pairs={{0,16},{1,17},{2,18},{3,19},{4,20},{5,21},{6,22},{7,23},{8,24},{9,... | collective-permute-start | bytes 1671176 | tf_op jit(solution)/shard_map/ppermute | solution.py:465
  29.5 15.5 %collective-permute-start.2 = (bf16[256,1024]{1,0:T(8,128)(2,1)}, bf16[256,1024]{1,0:T(8,128)(2,1)S(1)}, u32[]{:S(2)}, u32[]{:S(2)}) collective-permute-start(bf16[256,1024]{1,0:T(8,128)(2,1)} %collective-permute-done), channel_id=1, source_target_pairs={{0,8},{1,9},{2,10},{3,11},{4,0},{5,1},{6,2},{7,3},{8,12},{9,13},{1... | collective-permute-start | bytes 1572872 | tf_op jit(solution)/shard_map/ppermute | solution.py:465
  30.2 14.8 %collective-permute-start.6 = (bf16[256,1024]{1,0:T(8,128)(2,1)S(1)}, bf16[256,1024]{1,0:T(8,128)(2,1)S(1)}, u32[]{:S(2)}, u32[]{:S(2)}) collective-permute-start(bf16[256,1024]{1,0:T(8,128)(2,1)S(1)} %select_select_fusion.3), channel_id=1, source_target_pairs={{0,16},{1,17},{2,18},{3,19},{4,20},{5,21},{6,22},{7,23},{8,24},{9,... | collective-permute-start | bytes 1572872 | tf_op jit(solution)/shard_map/ppermute | solution.py:465
  31.8 16.3 %collective-permute-start.7 = (bf16[1024,256]{1,0:T(8,128)(2,1)}, bf16[1024,256]{1,0:T(8,128)(2,1)S(1)}, u32[]{:S(2)}, u32[]{:S(2)}) collective-permute-start(bf16[1024,256]{1,0:T(8,128)(2,1)} %collective-permute-done.4.refs_5_), channel_id=1, source_target_pairs={{0,2},{1,3},{2,0},{3,1},{4,6},{5,7},{6,4},{7,5},{8,10},{9,11},{10,... | collective-permute-start | bytes 1572872 | tf_op jit(solution)/shard_map/ppermute | solution.py:465
  34.4 16.6 %collective-permute-start.8 = (bf16[256,1024]{1,0:T(8,128)(2,1)S(1)}, bf16[256,1024]{1,0:T(8,128)(2,1)S(1)}, u32[]{:S(2)}, u32[]{:S(2)}) collective-permute-start(bf16[256,1024]{1,0:T(8,128)(2,1)S(1)} %select_select_fusion.1.refs_0_), channel_id=1, source_target_pairs={{0,1},{1,0},{2,3},{3,2},{4,5},{5,4},{6,7},{7,6},{8,9},{9,8},{10,11... | collective-permute-start | bytes 1572872 | tf_op jit(solution)/shard_map/ppermute | solution.py:465
  45.8 5.2 %collective-permute-start.9 = (bf16[256,1024]{1,0:T(8,128)(2,1)S(1)}, bf16[256,1024]{1,0:T(8,128)(2,1)}, u32[]{:S(2)}, u32[]{:S(2)}) collective-permute-start(bf16[256,1024]{1,0:T(8,128)(2,1)S(1)} %collective-permute-done.6.refs_1_), channel_id=1, source_target_pairs={{0,1},{1,0},{2,3},{3,2},{4,5},{5,4},{6,7},{7,6},{8,9},{9,8},{10,11... | collective-permute-start | bytes 1572872 | tf_op jit(solution)/shard_map/ppermute | solution.py:465
  47.7 14.5 %collective-permute-start.11 = (bf16[256,1024]{1,0:T(8,128)(2,1)}, bf16[256,1024]{1,0:T(8,128)(2,1)S(1)}, u32[]{:S(2)}, u32[]{:S(2)}) collective-permute-start(bf16[256,1024]{1,0:T(8,128)(2,1)} %select_select_fusion.2), channel_id=1, source_target_pairs={{0,16},{1,17},{2,18},{3,19},{4,20},{5,21},{6,22},{7,23},{8,24},{9,... | collective-permute-start | bytes 1572872 | tf_op jit(solution)/shard_map/ppermute | solution.py:465
  49.4 18.2 %collective-permute-start.15 = (bf16[256,512]{1,0:T(8,128)(2,1)}, bf16[256,512]{1,0:T(8,128)(2,1)S(1)}, u32[]{:S(2)}, u32[]{:S(2)}) collective-permute-start(bf16[256,512]{1,0:T(8,128)(2,1)} %long_range.4), channel_id=1, source_target_pairs={{0,2},{1,3},{2,0},{3,1},{4,6},{5,7},{6,4},{7,5},{8,10},{9,11},{10,... | collective-permute-start | bytes 786440 | tf_op jit(solution)/shard_map/ppermute | solution.py:465
  53.5 14.2 %collective-permute-start.16 = (bf16[256,512]{1,0:T(8,128)(2,1)}, bf16[256,512]{1,0:T(8,128)(2,1)}, u32[]{:S(2)}, u32[]{:S(2)}) collective-permute-start(bf16[256,512]{1,0:T(8,128)(2,1)} %long_range.5), channel_id=1, source_target_pairs={{0,2},{1,3},{2,0},{3,1},{4,6},{5,7},{6,4},{7,5},{8,10},{9,11},{10,... | collective-permute-start | bytes 786440 | tf_op jit(solution)/shard_map/ppermute | solution.py:465
  60.2 3.9 %collective-permute-start.10 = (bf16[256,1024]{1,0:T(8,128)(2,1)S(1)}, bf16[256,1024]{1,0:T(8,128)(2,1)S(1)}, u32[]{:S(2)}, u32[]{:S(2)}) collective-permute-start(bf16[256,1024]{1,0:T(8,128)(2,1)S(1)} %select_select_fusion.refs_0_), channel_id=1, source_target_pairs={{0,1},{1,0},{2,3},{3,2},{4,5},{5,4},{6,7},{7,6},{8,9},{9,8},{10,11... | collective-permute-start | bytes 1572872 | tf_op jit(solution)/shard_map/ppermute | solution.py:465
  62.3 1.9 %collective-permute-start.12 = (bf16[256,1024]{1,0:T(8,128)(2,1)S(1)}, bf16[256,1024]{1,0:T(8,128)(2,1)S(1)}, u32[]{:S(2)}, u32[]{:S(2)}) collective-permute-start(bf16[256,1024]{1,0:T(8,128)(2,1)S(1)} %collective-permute-done.11.refs_1_), channel_id=1, source_target_pairs={{0,1},{1,0},{2,3},{3,2},{4,5},{5,4},{6,7},{7,6},{8,9},{9,8},{10,11... | collective-permute-start | bytes 1572872 | tf_op jit(solution)/shard_map/ppermute | solution.py:465
  64.0 9.5 %collective-permute-start.14 = (bf16[256,512]{1,0:T(8,128)(2,1)}, bf16[256,512]{1,0:T(8,128)(2,1)S(1)}, u32[]{:S(2)}, u32[]{:S(2)}) collective-permute-start(bf16[256,512]{1,0:T(8,128)(2,1)} %long_range.7), channel_id=1, source_target_pairs={{0,2},{1,3},{2,0},{3,1},{4,6},{5,7},{6,4},{7,5},{8,10},{9,11},{10,... | collective-permute-start | bytes 786440 | tf_op jit(solution)/shard_map/ppermute | solution.py:465
  65.6 12.9 %collective-permute-start.13 = (bf16[256,512]{1,0:T(8,128)(2,1)}, bf16[256,512]{1,0:T(8,128)(2,1)S(1)}, u32[]{:S(2)}, u32[]{:S(2)}) collective-permute-start(bf16[256,512]{1,0:T(8,128)(2,1)} %long_range.6), channel_id=1, source_target_pairs={{0,2},{1,3},{2,0},{3,1},{4,6},{5,7},{6,4},{7,5},{8,10},{9,11},{10,... | collective-permute-start | bytes 786440 | tf_op jit(solution)/shard_map/ppermute | solution.py:465
  (4 other events, 15.7 us)

commit v20 on v19

--- a/solution.py
+++ b/solution.py
@@ -11,7 +11,7 @@
 CORES = 2
 SMALL_COST = pl.CostEstimate(flops=1, bytes_accessed=1, transcendentals=0)
 GROUP_ITEMS = 4
-SHORT_VMEM_BYTES = 20 * 1024 * 1024
+SHORT_VMEM_BYTES = 15 * 1024 * 1024
 VMEM_BYTES = 10 * 1024 * 1024
 
 
@@ -20,13 +20,12 @@
 
 
 def short_kernel(
-    half_ref, live_ref, sub_ref, meta_ref, basis_ref, decay_ref, *refs, share, subs, depth, width, adds, finishes
+    half_ref, live_ref, sub_ref, meta_ref, basis_ref, decay_ref, *refs, share, subs, depth, width, adds, finishes, tile
 ):
     items, scratch = refs[: -10 - adds], refs[-10:]
     out_ref, basis, left, acc, made, dists, group_sub, cursor, basis_sem, out_sem = scratch
     slots = share * len(items)
     row_count = acc.shape[2]
-    tile = made.shape[1]
     if adds:
         acc_copy = pltpu.make_async_copy(refs[-11], acc, out_sem.at[0])
         acc_copy.start()
@@ -136,7 +135,7 @@
     groups = slots // GROUP_ITEMS + subs
     tile = min(row_count, 512)
     kernel = functools.partial(
-        short_kernel, share=share, subs=subs, depth=depth, width=width, adds=adds, finishes=finishes
+        short_kernel, share=share, subs=subs, depth=depth, width=width, adds=adds, finishes=finishes, tile=tile
     )
     return pl.pallas_call(
         kernel,
@@ -152,14 +151,14 @@
             pltpu.VMEM((depth, row_count), jnp.bfloat16),
             pltpu.VMEM((groups, 2 * width, GROUP_ITEMS * depth), jnp.bfloat16),
             pltpu.VMEM((subs, 2 * width, row_count), jnp.float32),
-            pltpu.VMEM((row_count // tile, tile, 2 * subs * width), jnp.float32),
+            pltpu.VMEM((row_count // tile, tile if finishes else 8, 2 * subs * width), jnp.float32),
             pltpu.SMEM((groups * GROUP_ITEMS,), jnp.float32),
             pltpu.SMEM((groups,), jnp.int32),
             pltpu.SMEM((subs,), jnp.int32),
             pltpu.SemaphoreType.DMA,
             pltpu.SemaphoreType.DMA((row_count // tile,)),
         ],
-        compiler_params=pltpu.CompilerParams(vmem_limit_bytes=SHORT_VMEM_BYTES),
+        compiler_params=pltpu.CompilerParams(vmem_limit_bytes=SHORT_VMEM_BYTES if finishes else VMEM_BYTES),
         cost_estimate=pl.CostEstimate(
             flops=4 * row_count * slots * depth * width, bytes_accessed=1, transcendentals=0
         ),

time: 81.4 us -> 81.4 us (level)
  waiting for transfers between devices: 16.2 us -> 14.4 us
  starting transfers between devices: 16 us -> 17.1 us
    ppermute x17, waiting for transfers between devices: 16.2 us -> 14.4 us  [send(): return lax.ppermute(value, AXES, pairs)]
    ppermute x17, starting transfers between devices: 16 us -> 17.1 us  [send(): return lax.ppermute(value, AXES, pairs)]
  transfers between devices with their start and end apart: 17 -> 17, of which waited for: 4 -> 3; matrix products, arithmetic and copies ran while one was open for 12% -> 12% of each run, Pallas kernels for 41% -> 42%
where the time goes in v20:
time: 81.4 us; the launch traced here: 80.7 us
  Pallas kernels  36 us (44%)
  starting transfers between devices  17.1 us (21%)
  waiting for transfers between devices  14.4 us (18%)
  other arithmetic  8.03 us (10%)
  local copies, waits for them, and re-layouts  3.96 us (5%)
  between operations  1.3 us (2%)
    ppermute x17, starting transfers between devices, send(): return lax.ppermute(value, AXES, pairs)  17.1 us
    pallas_call x2, Pallas kernels, short_range(): pl.pallas_call(kernel, out_shape=pltpu.HBM((row_count, 2 * subs * width)...  14.5 us
    ppermute x17, waiting for transfers between devices, send(): return lax.ppermute(value, AXES, pairs)  14.4 us
    pallas_call x2, Pallas kernels, own_sum(): pl.pallas_call(functools.partial(own_kernel, blocks=len(blocks), chains=c...  10.8 us
    pallas_call x4, Pallas kernels, long_range(): pl.pallas_call(functools.partial(long_kernel, blocks=len(blocks), chains=...  6.77 us
    select_n x4, other arithmetic, pick(): value = jnp.where(wanted == k, block, value)  4.22 us
    pallas_call x2, Pallas kernels, final_sum(): pl.pallas_call(functools.partial(final_kernel, pieces=count, blocks=block...  3.94 us
    unnamed x24, local copies, waits for them, and re-layouts  3.32 us
  transfers between devices with their start and end apart: 17, of which 3 were waited for; matrix products, arithmetic and copies ran while one was open for 12% of the time, Pallas kernels for 42%

profile of v20, /device:TPU:0, one launch (start us, length us, event | category | flops | bytes accessed | tf_op | source)
XLA Modules:
  0.0 80.7 jit_solution(3245101731564602089)
XLA Ops:
  1.2 4.1 %collective-permute-start = (bf16[256,1024]{1,0:T(8,128)(2,1)S(1)}, bf16[256,1024]{1,0:T(8,128)(2,1)}, u32[]{:S(2)}, u32[]{:S(2)}) collective-permute-start(bf16[256,1024]{1,0:T(8,128)(2,1)S(1)} %bitcast.46), channel_id=1, source_target_pairs={{0,8},{1,9},{2,10},{3,11},{4,0},{5,1},{6,2},{7,3},{8,12},{9,13},{1... | collective-permute-start | bytes 1572872 | tf_op jit(solution)/shard_map/ppermute | solution.py:464
  5.3 1.5 %multiply_convert_fusion = bf16[256,2,512]{2,1,0:T(2,128)(2,1)S(1)} fusion(bf16[256,2,512]{2,1,0:T(2,128)(2,1)} %param.11, f32[512]{0:T(512)} %param.13), kind=kLoop, calls=%fused_computation.2 | loop fusion | flops 786432 | bytes 1050624 | tf_op jit(solution)/shard_map/convert_element_type | solution.py:422
  7.3 1.6 %collective-permute-start.4 = (bf16[1024,256]{1,0:T(8,128)(2,1)S(1)}, bf16[1024,256]{1,0:T(8,128)(2,1)}, u32[]{:S(2)}, u32[]{:S(2)}) collective-permute-start(bf16[1024,256]{1,0:T(8,128)(2,1)S(1)} %bitcast.42), channel_id=1, source_target_pairs={{0,16},{1,17},{2,18},{3,19},{4,20},{5,21},{6,22},{7,23},{8,24},{9,... | collective-permute-start | bytes 1572872 | tf_op jit(solution)/shard_map/ppermute | solution.py:464
  8.9 1.5 %collective-permute-start.5 = (bf16[1024,256]{1,0:T(8,128)(2,1)S(1)}, bf16[1024,256]{1,0:T(8,128)(2,1)S(1)}, u32[]{:S(2)}, u32[]{:S(2)}) collective-permute-start(bf16[1024,256]{1,0:T(8,128)(2,1)S(1)} %bitcast.43), channel_id=1, source_target_pairs={{0,2},{1,3},{2,0},{3,1},{4,6},{5,7},{6,4},{7,5},{8,10},{9,11},{10,... | collective-permute-start | bytes 1572872 | tf_op jit(solution)/shard_map/ppermute | solution.py:464
  11.0 1.4 %copy.17 = bf16[16,128,128]{1,2,0:T(8,128)(2,1)S(1)} copy(bf16[16,128,128]{2,1,0:T(8,128)(2,1)} %param.18) | data formatting | bytes 1048576 | tf_op args[7]
  14.2 5.6 %short_range.2.refs_1_ = f32[2,256,2048]{2,1,0:T(8,128)} custom-call(s32[1]{0:T(128)} %bitcast.1.half_ref, s32[16]{0:T(128)S(1)} %compare_convert_fusion.1.live_ref, s32[16]{0:T(128)S(1)} %copy-done.1, f32[3,16]{1,0:T(4,128)S(1)} %pad_maximum_fusion.1.meta_ref, bf16[128,4096]{1,0:T(8,128)(2,1)} %basis_ref.3, f32[1,4096]{1,0:T(1,128)S(1)} %bitcast.39, ...), custom_call_target="tpu_custom_call" | custom-call | flops 2147483648 | bytes 1 | tf_op jit(solution)/shard_map/short_range/pallas_call | solution.py:140
  19.9 9.6 %collective-permute-done.1 = bf16[256,1024]{1,0:T(8,128)(2,1)S(1)} collective-permute-done((bf16[256,1024]{1,0:T(8,128)(2,1)S(1)}, bf16[256,1024]{1,0:T(8,128)(2,1)S(1)}, u32[]{:S(2)}, u32[]{:S(2)}) %collective-permute-start.1) | collective-permute-done | bytes 524320 | tf_op jit(solution)/shard_map/ppermute | solution.py:464
  30.2 1.6 %collective-permute-start.6 = (bf16[256,1024]{1,0:T(8,128)(2,1)S(1)}, bf16[256,1024]{1,0:T(8,128)(2,1)S(1)}, u32[]{:S(2)}, u32[]{:S(2)}) collective-permute-start(bf16[256,1024]{1,0:T(8,128)(2,1)S(1)} %select_select_fusion.3), channel_id=1, source_target_pairs={{0,16},{1,17},{2,18},{3,19},{4,20},{5,21},{6,22},{7,23},{8,24},{9,... | collective-permute-start | bytes 1572872 | tf_op jit(solution)/shard_map/ppermute | solution.py:464
  31.8 1.5 %collective-permute-start.7 = (bf16[1024,256]{1,0:T(8,128)(2,1)}, bf16[1024,256]{1,0:T(8,128)(2,1)S(1)}, u32[]{:S(2)}, u32[]{:S(2)}) collective-permute-start(bf16[1024,256]{1,0:T(8,128)(2,1)} %collective-permute-done.4.refs_5_), channel_id=1, source_target_pairs={{0,2},{1,3},{2,0},{3,1},{4,6},{5,7},{6,4},{7,5},{8,10},{9,11},{10,... | collective-permute-start | bytes 1572872 | tf_op jit(solution)/shard_map/ppermute | solution.py:464
  35.4 8.8 %short_range.3.refs_6_.refs_8_.refs_1_ = f32[2048,512]{1,0:T(8,128)} custom-call(s32[1]{0:T(128)} %bitcast.1.half_ref, s32[16]{0:T(128)S(1)} %get-tuple-element.55.live_ref, s32[16]{0:T(128)S(1)} %get-tuple-element.54.sub_ref, f32[3,16]{1,0:T(4,128)S(1)} %pad_maximum_fusion.2.meta_ref, bf16[128,4096]{1,0:T(8,128)(2,1)} %basis_ref.3, f32[1,4096]{1,0:T(1,128)S(1)} %bitcast.40, ...), custom_call_target="tpu_custom_call" | custom-call | flops 2147483648 | bytes 1 | tf_op jit(solution)/shard_map/short_range/pallas_call | solution.py:140
  45.1 1.2 %collective-permute-start.9 = (bf16[256,1024]{1,0:T(8,128)(2,1)S(1)}, bf16[256,1024]{1,0:T(8,128)(2,1)}, u32[]{:S(2)}, u32[]{:S(2)}) collective-permute-start(bf16[256,1024]{1,0:T(8,128)(2,1)S(1)} %collective-permute-done.6.refs_1_), channel_id=1, source_target_pairs={{0,1},{1,0},{2,3},{3,2},{4,5},{5,4},{6,7},{7,6},{8,9},{9,8},{10,11... | collective-permute-start | bytes 1572872 | tf_op jit(solution)/shard_map/ppermute | solution.py:464
  46.3 1.9 %select_select_fusion.2 = bf16[256,1024]{1,0:T(8,128)(2,1)} fusion(bf16[256,1024]{1,0:T(8,128)(2,1)} %collective-permute-done, bf16[256,1024]{1,0:T(8,128)(2,1)} %copy-done.6, bf16[256,1024]{1,0:T(8,128)(2,1)} %copy-done.2, pred[]{:T(512)S(6)} %eq.80, pred[]{:T(512)S(6)} %eq.73), kind=kLoop, calls=%fused_computation.6 | loop fusion | flops 524288 | bytes 2097154 | tf_op jit(solution)/shard_map/jit(_where)/select_n | solution.py:498
  48.3 1.4 %long_range.4 = bf16[256,512]{1,0:T(8,128)(2,1)} custom-call(bf16[256,1024]{1,0:T(8,128)(2,1)S(1)} %select_select_fusion.1.refs_0_, bf16[256,1024]{1,0:T(8,128)(2,1)S(1)} %collective-permute-done.6.refs_1_, bf16[1024,256]{1,0:T(8,128)(2,1)S(1)} %collective-permute-done.5.refs_2_, bf16[1024,256]{1,0:T(8,128)(2,1)S(1)} %collective-permute-done.7.refs_3_), custom_call_target="tpu_custom_call" | custom-call | flops 1 | bytes 1 | tf_op jit(solution)/shard_map/long_range/pallas_call | solution.py:220
  49.7 1.4 %collective-permute-start.15 = (bf16[256,512]{1,0:T(8,128)(2,1)}, bf16[256,512]{1,0:T(8,128)(2,1)S(1)}, u32[]{:S(2)}, u32[]{:S(2)}) collective-permute-start(bf16[256,512]{1,0:T(8,128)(2,1)} %long_range.4), channel_id=1, source_target_pairs={{0,2},{1,3},{2,0},{3,1},{4,6},{5,7},{6,4},{7,5},{8,10},{9,11},{10,... | collective-permute-start | bytes 786440 | tf_op jit(solution)/shard_map/ppermute | solution.py:464
  51.1 2.5 %long_range.5 = bf16[256,512]{1,0:T(8,128)(2,1)} custom-call(bf16[256,1024]{1,0:T(8,128)(2,1)S(1)} %collective-permute-done.8.refs_0_.refs_2_, bf16[256,1024]{1,0:T(8,128)(2,1)} %collective-permute-done.9.refs_1_.refs_3_, bf16[1024,256]{1,0:T(8,128)(2,1)S(1)} %collective-permute-done.5.refs_2_, bf16[1024,256]{1,0:T(8,128)(2,1)S(1)} %collective-permute-done.7.refs_3_), custom_call_target="tpu_custom_call" | custom-call | flops 1 | bytes 1 | tf_op jit(solution)/shard_map/long_range/pallas_call | solution.py:220
  54.4 5.0 %own_sum.2.refs_9_ = bf16[2048,2,256]{2,1,0:T(2,128)(2,1)} custom-call(s32[2]{0:T(128)S(1)} %pad_add_fusion.1.order_ref, bf16[256,1024]{1,0:T(8,128)(2,1)S(1)} %select_select_fusion.1.refs_0_, bf16[256,1024]{1,0:T(8,128)(2,1)S(1)} %collective-permute-done.6.refs_1_, bf16[256,1024]{1,0:T(8,128)(2,1)S(1)} %collective-permute-done.8.refs_0_.refs_2_, ...), custom_call_target="tpu_custom_call" | custom-call | flops 1 | bytes 1 | tf_op jit(solution)/shard_map/own_sum/pallas_call | solution.py:288
  60.6 1.7 %collective-permute-done.11.refs_1_ = bf16[256,1024]{1,0:T(8,128)(2,1)S(1)} collective-permute-done((bf16[256,1024]{1,0:T(8,128)(2,1)}, bf16[256,1024]{1,0:T(8,128)(2,1)S(1)}, u32[]{:S(2)}, u32[]{:S(2)}) %collective-permute-start.11) | collective-permute-done | bytes 524320 | tf_op jit(solution)/shard_map/ppermute | solution.py:464
  62.5 1.4 %long_range.7 = bf16[256,512]{1,0:T(8,128)(2,1)} custom-call(bf16[256,1024]{1,0:T(8,128)(2,1)S(1)} %select_select_fusion.refs_0_, bf16[256,1024]{1,0:T(8,128)(2,1)S(1)} %collective-permute-done.11.refs_1_, bf16[1024,512]{1,0:T(8,128)(2,1)S(1)} %get-tuple-element.62.refs_2_, bf16[1024,512]{1,0:T(8,128)(2,1)S(1)} %get-tuple-element.63.refs_3_), custom_call_target="tpu_custom_call" | custom-call | flops 1 | bytes 1 | tf_op jit(solution)/shard_map/long_range/pallas_call | solution.py:220
  64.5 1.4 %long_range.6 = bf16[256,512]{1,0:T(8,128)(2,1)} custom-call(bf16[256,1024]{1,0:T(8,128)(2,1)S(1)} %collective-permute-done.10.refs_0_.refs_2_, bf16[256,1024]{1,0:T(8,128)(2,1)S(1)} %collective-permute-done.12.refs_1_.refs_3_, bf16[1024,512]{1,0:T(8,128)(2,1)S(1)} %get-tuple-element.62.refs_2_, bf16[1024,512]{1,0:T(8,128)(2,1)S(1)} %get-tuple-element.63.refs_3_), custom_call_target="tpu_custom_call" | custom-call | flops 1 | bytes 1 | tf_op jit(solution)/shard_map/long_range/pallas_call | solution.py:220
  66.0 1.6 %collective-permute-start.13 = (bf16[256,512]{1,0:T(8,128)(2,1)}, bf16[256,512]{1,0:T(8,128)(2,1)S(1)}, u32[]{:S(2)}, u32[]{:S(2)}) collective-permute-start(bf16[256,512]{1,0:T(8,128)(2,1)} %long_range.6), channel_id=1, source_target_pairs={{0,2},{1,3},{2,0},{3,1},{4,6},{5,7},{6,4},{7,5},{8,10},{9,11},{10,... | collective-permute-start | bytes 786440 | tf_op jit(solution)/shard_map/ppermute | solution.py:464
  67.7 5.8 %own_sum.3.refs_2_ = bf16[2048,2,256]{2,1,0:T(2,128)(2,1)} custom-call(s32[4]{0:T(128)S(1)} %pad_add_fusion.2.order_ref, bf16[256,1024]{1,0:T(8,128)(2,1)S(1)} %select_select_fusion.refs_0_, bf16[256,1024]{1,0:T(8,128)(2,1)S(1)} %collective-permute-done.11.refs_1_, ...), custom_call_target="tpu_custom_call", output_to_operand_aliasing={{}: (10, {})} | custom-call | flops 1 | bytes 1 | tf_op jit(solution)/shard_map/own_sum/pallas_call | solution.py:288
  73.5 2.0 %final_sum.2.refs_2_ = bf16[2048,2,256]{2,1,0:T(2,128)(2,1)} custom-call(s32[1]{0:T(128)} %bitcast.22.order_ref, bf16[256,512]{1,0:T(8,128)(2,1)S(1)} %collective-permute-done.14.refs_0_, f32[2048,512]{1,0:T(8,128)} %short_range.3.refs_6_.refs_8_.refs_1_, bf16[2048,2,256]{2,1,0:T(2,128)(2,1)} %own_sum.3.refs_2_), custom_call_target="tpu_custom_call", output_to_operand_aliasing={{}: (3, {})} | custom-call | flops 1 | bytes 1 | tf_op jit(solution)/shard_map/final_sum/pallas_call | solution.py:343
  75.5 3.1 %collective-permute-done.13.refs_0_ = bf16[256,512]{1,0:T(8,128)(2,1)S(1)} collective-permute-done((bf16[256,512]{1,0:T(8,128)(2,1)}, bf16[256,512]{1,0:T(8,128)(2,1)S(1)}, u32[]{:S(2)}, u32[]{:S(2)}) %collective-permute-start.13) | collective-permute-done | bytes 262176 | tf_op jit(solution)/shard_map/ppermute | solution.py:464
  78.6 2.0 %final_sum.3 = bf16[2048,2,256]{2,1,0:T(2,128)(2,1)} custom-call(s32[1]{0:T(128)} %bitcast.order_ref, bf16[256,512]{1,0:T(8,128)(2,1)S(1)} %collective-permute-done.13.refs_0_, f32[2048,512]{1,0:T(8,128)} %short_range.3.refs_6_.refs_8_.refs_1_, bf16[2048,2,256]{2,1,0:T(2,128)(2,1)} %final_sum.2.refs_2_), custom_call_target="tpu_custom_call", output_to_operand_aliasing={{}: (3, {})} | custom-call | flops 1 | bytes 1 | tf_op jit(solution)/shard_map/final_sum/pallas_call | solution.py:343
  (69 shorter events, 9.9 us)
Async XLA Ops:
  0.0 12.4 %copy-start.1 = (s32[16]{0:T(128)S(1)}, s32[16]{0:T(128)}, u32[]{:S(2)}) copy-start(s32[16]{0:T(128)} %sub_ref.1) | copy-start | bytes 196
  0.0 12.4 %copy-start.8 = (s32[16]{0:T(128)S(1)}, s32[16]{0:T(128)}, u32[]{:S(2)}) copy-start(s32[16]{0:T(128)} %param.19) | copy-start | bytes 196
  1.1 29.0 %copy-start.5 = (bf16[32,8,2,512]{3,1,2,0:T(8,128)(2,1)}, bf16[32,8,2,512]{3,1,2,0:T(8,128)(2,1)S(1)}, u32[]{:S(2)}) copy-start(bf16[32,8,2,512]{3,1,2,0:T(8,128)(2,1)S(1)} %copy.19) | copy-start | bytes 1572868
  1.2 12.7 %copy-start.9 = (f32[125]{0:T(128)S(1)}, f32[125]{0:T(128)}, u32[]{:S(2)}) copy-start(f32[125]{0:T(128)} %param.16) | copy-start | bytes 1504
  1.2 12.7 %copy-start.10 = (f32[125]{0:T(128)S(1)}, f32[125]{0:T(128)}, u32[]{:S(2)}) copy-start(f32[125]{0:T(128)} %param.17) | copy-start | bytes 1504
  1.2 13.0 %copy-start = (f32[4096]{0:T(1024)S(1)}, f32[4096]{0:T(1024)}, u32[]{:S(2)}) copy-start(f32[4096]{0:T(1024)} %param.15) | copy-start | bytes 49156
  1.2 18.7 %collective-permute-start = (bf16[256,1024]{1,0:T(8,128)(2,1)S(1)}, bf16[256,1024]{1,0:T(8,128)(2,1)}, u32[]{:S(2)}, u32[]{:S(2)}) collective-permute-start(bf16[256,1024]{1,0:T(8,128)(2,1)S(1)} %bitcast.46), channel_id=1, source_target_pairs={{0,8},{1,9},{2,10},{3,11},{4,0},{5,1},{6,2},{7,3},{8,12},{9,13},{1... | collective-permute-start | bytes 1572872 | tf_op jit(solution)/shard_map/ppermute | solution.py:464
  5.3 24.2 %collective-permute-start.1 = (bf16[256,1024]{1,0:T(8,128)(2,1)S(1)}, bf16[256,1024]{1,0:T(8,128)(2,1)S(1)}, u32[]{:S(2)}, u32[]{:S(2)}) collective-permute-start(bf16[256,1024]{1,0:T(8,128)(2,1)S(1)} %bitcast.47), channel_id=1, source_target_pairs={{0,4},{1,5},{2,6},{3,7},{4,12},{5,13},{6,14},{7,15},{8,0},{9,1},{1... | collective-permute-start | bytes 1572872 | tf_op jit(solution)/shard_map/ppermute | solution.py:464
  7.3 12.5 %copy-start.4 = (bf16[256,2,512]{0,2,1:T(8,128)(2,1)}, bf16[256,2,512]{0,2,1:T(8,128)(2,1)S(1)}, u32[]{:S(2)}) copy-start(bf16[256,2,512]{0,2,1:T(8,128)(2,1)S(1)} %copy.18) | copy-start | bytes 1572868
  7.3 24.5 %collective-permute-start.4 = (bf16[1024,256]{1,0:T(8,128)(2,1)S(1)}, bf16[1024,256]{1,0:T(8,128)(2,1)}, u32[]{:S(2)}, u32[]{:S(2)}) collective-permute-start(bf16[1024,256]{1,0:T(8,128)(2,1)S(1)} %bitcast.42), channel_id=1, source_target_pairs={{0,16},{1,17},{2,18},{3,19},{4,20},{5,21},{6,22},{7,23},{8,24},{9,... | collective-permute-start | bytes 1572872 | tf_op jit(solution)/shard_map/ppermute | solution.py:464
  8.9 22.9 %collective-permute-start.5 = (bf16[1024,256]{1,0:T(8,128)(2,1)S(1)}, bf16[1024,256]{1,0:T(8,128)(2,1)S(1)}, u32[]{:S(2)}, u32[]{:S(2)}) collective-permute-start(bf16[1024,256]{1,0:T(8,128)(2,1)S(1)} %bitcast.43), channel_id=1, source_target_pairs={{0,2},{1,3},{2,0},{3,1},{4,6},{5,7},{6,4},{7,5},{8,10},{9,11},{10,... | collective-permute-start | bytes 1572872 | tf_op jit(solution)/shard_map/ppermute | solution.py:464
  13.3 21.2 %collective-permute-start.3 = (bf16[17,128,128]{2,1,0:T(8,128)(2,1)}, bf16[17,128,128]{2,1,0:T(8,128)(2,1)}, u32[]{:S(2)}, u32[]{:S(2)}) collective-permute-start(bf16[17,128,128]{2,1,0:T(8,128)(2,1)} %pad_maximum_fusion.refs_0_), channel_id=1, source_target_pairs={{0,16},{1,17},{2,18},{3,19},{4,20},{5,21},{6,22},{7,23},{8,24},{9,... | collective-permute-start | bytes 1671176 | tf_op jit(solution)/shard_map/ppermute | solution.py:464
  29.5 14.8 %collective-permute-start.2 = (bf16[256,1024]{1,0:T(8,128)(2,1)}, bf16[256,1024]{1,0:T(8,128)(2,1)S(1)}, u32[]{:S(2)}, u32[]{:S(2)}) collective-permute-start(bf16[256,1024]{1,0:T(8,128)(2,1)} %collective-permute-done), channel_id=1, source_target_pairs={{0,8},{1,9},{2,10},{3,11},{4,0},{5,1},{6,2},{7,3},{8,12},{9,13},{1... | collective-permute-start | bytes 1572872 | tf_op jit(solution)/shard_map/ppermute | solution.py:464
  30.2 14.1 %collective-permute-start.6 = (bf16[256,1024]{1,0:T(8,128)(2,1)S(1)}, bf16[256,1024]{1,0:T(8,128)(2,1)S(1)}, u32[]{:S(2)}, u32[]{:S(2)}) collective-permute-start(bf16[256,1024]{1,0:T(8,128)(2,1)S(1)} %select_select_fusion.3), channel_id=1, source_target_pairs={{0,16},{1,17},{2,18},{3,19},{4,20},{5,21},{6,22},{7,23},{8,24},{9,... | collective-permute-start | bytes 1572872 | tf_op jit(solution)/shard_map/ppermute | solution.py:464
  31.8 16.5 %collective-permute-start.7 = (bf16[1024,256]{1,0:T(8,128)(2,1)}, bf16[1024,256]{1,0:T(8,128)(2,1)S(1)}, u32[]{:S(2)}, u32[]{:S(2)}) collective-permute-start(bf16[1024,256]{1,0:T(8,128)(2,1)} %collective-permute-done.4.refs_5_), channel_id=1, source_target_pairs={{0,2},{1,3},{2,0},{3,1},{4,6},{5,7},{6,4},{7,5},{8,10},{9,11},{10,... | collective-permute-start | bytes 1572872 | tf_op jit(solution)/shard_map/ppermute | solution.py:464
  34.4 16.7 %collective-permute-start.8 = (bf16[256,1024]{1,0:T(8,128)(2,1)S(1)}, bf16[256,1024]{1,0:T(8,128)(2,1)S(1)}, u32[]{:S(2)}, u32[]{:S(2)}) collective-permute-start(bf16[256,1024]{1,0:T(8,128)(2,1)S(1)} %select_select_fusion.1.refs_0_), channel_id=1, source_target_pairs={{0,1},{1,0},{2,3},{3,2},{4,5},{5,4},{6,7},{7,6},{8,9},{9,8},{10,11... | collective-permute-start | bytes 1572872 | tf_op jit(solution)/shard_map/ppermute | solution.py:464
  45.1 6.0 %collective-permute-start.9 = (bf16[256,1024]{1,0:T(8,128)(2,1)S(1)}, bf16[256,1024]{1,0:T(8,128)(2,1)}, u32[]{:S(2)}, u32[]{:S(2)}) collective-permute-start(bf16[256,1024]{1,0:T(8,128)(2,1)S(1)} %collective-permute-done.6.refs_1_), channel_id=1, source_target_pairs={{0,1},{1,0},{2,3},{3,2},{4,5},{5,4},{6,7},{7,6},{8,9},{9,8},{10,11... | collective-permute-start | bytes 1572872 | tf_op jit(solution)/shard_map/ppermute | solution.py:464
  48.2 14.0 %collective-permute-start.11 = (bf16[256,1024]{1,0:T(8,128)(2,1)}, bf16[256,1024]{1,0:T(8,128)(2,1)S(1)}, u32[]{:S(2)}, u32[]{:S(2)}) collective-permute-start(bf16[256,1024]{1,0:T(8,128)(2,1)} %select_select_fusion.2), channel_id=1, source_target_pairs={{0,16},{1,17},{2,18},{3,19},{4,20},{5,21},{6,22},{7,23},{8,24},{9,... | collective-permute-start | bytes 1572872 | tf_op jit(solution)/shard_map/ppermute | solution.py:464
  49.7 17.9 %collective-permute-start.15 = (bf16[256,512]{1,0:T(8,128)(2,1)}, bf16[256,512]{1,0:T(8,128)(2,1)S(1)}, u32[]{:S(2)}, u32[]{:S(2)}) collective-permute-start(bf16[256,512]{1,0:T(8,128)(2,1)} %long_range.4), channel_id=1, source_target_pairs={{0,2},{1,3},{2,0},{3,1},{4,6},{5,7},{6,4},{7,5},{8,10},{9,11},{10,... | collective-permute-start | bytes 786440 | tf_op jit(solution)/shard_map/ppermute | solution.py:464
  53.6 14.0 %collective-permute-start.16 = (bf16[256,512]{1,0:T(8,128)(2,1)}, bf16[256,512]{1,0:T(8,128)(2,1)}, u32[]{:S(2)}, u32[]{:S(2)}) collective-permute-start(bf16[256,512]{1,0:T(8,128)(2,1)} %long_range.5), channel_id=1, source_target_pairs={{0,2},{1,3},{2,0},{3,1},{4,6},{5,7},{6,4},{7,5},{8,10},{9,11},{10,... | collective-permute-start | bytes 786440 | tf_op jit(solution)/shard_map/ppermute | solution.py:464
  60.5 4.0 %collective-permute-start.10 = (bf16[256,1024]{1,0:T(8,128)(2,1)S(1)}, bf16[256,1024]{1,0:T(8,128)(2,1)S(1)}, u32[]{:S(2)}, u32[]{:S(2)}) collective-permute-start(bf16[256,1024]{1,0:T(8,128)(2,1)S(1)} %select_select_fusion.refs_0_), channel_id=1, source_target_pairs={{0,1},{1,0},{2,3},{3,2},{4,5},{5,4},{6,7},{7,6},{8,9},{9,8},{10,11... | collective-permute-start | bytes 1572872 | tf_op jit(solution)/shard_map/ppermute | solution.py:464
  62.3 2.3 %collective-permute-start.12 = (bf16[256,1024]{1,0:T(8,128)(2,1)S(1)}, bf16[256,1024]{1,0:T(8,128)(2,1)S(1)}, u32[]{:S(2)}, u32[]{:S(2)}) collective-permute-start(bf16[256,1024]{1,0:T(8,128)(2,1)S(1)} %collective-permute-done.11.refs_1_), channel_id=1, source_target_pairs={{0,1},{1,0},{2,3},{3,2},{4,5},{5,4},{6,7},{7,6},{8,9},{9,8},{10,11... | collective-permute-start | bytes 1572872 | tf_op jit(solution)/shard_map/ppermute | solution.py:464
  64.0 9.5 %collective-permute-start.14 = (bf16[256,512]{1,0:T(8,128)(2,1)}, bf16[256,512]{1,0:T(8,128)(2,1)S(1)}, u32[]{:S(2)}, u32[]{:S(2)}) collective-permute-start(bf16[256,512]{1,0:T(8,128)(2,1)} %long_range.7), channel_id=1, source_target_pairs={{0,2},{1,3},{2,0},{3,1},{4,6},{5,7},{6,4},{7,5},{8,10},{9,11},{10,... | collective-permute-start | bytes 786440 | tf_op jit(solution)/shard_map/ppermute | solution.py:464
  66.0 12.6 %collective-permute-start.13 = (bf16[256,512]{1,0:T(8,128)(2,1)}, bf16[256,512]{1,0:T(8,128)(2,1)S(1)}, u32[]{:S(2)}, u32[]{:S(2)}) collective-permute-start(bf16[256,512]{1,0:T(8,128)(2,1)} %long_range.6), channel_id=1, source_target_pairs={{0,2},{1,3},{2,0},{3,1},{4,6},{5,7},{6,4},{7,5},{8,10},{9,11},{10,... | collective-permute-start | bytes 786440 | tf_op jit(solution)/shard_map/ppermute | solution.py:464
  (4 other events, 16.1 us)

commit v21 on v19

--- a/solution.py
+++ b/solution.py
@@ -10,7 +10,7 @@
 AXES = ("grp", "dev")
 CORES = 2
 SMALL_COST = pl.CostEstimate(flops=1, bytes_accessed=1, transcendentals=0)
-GROUP_ITEMS = 4
+GROUP_ITEMS = 8
 SHORT_VMEM_BYTES = 20 * 1024 * 1024
 VMEM_BYTES = 10 * 1024 * 1024
 

time: 81.4 us -> 81 us (level)
  waiting for transfers between devices: 16.2 us -> 13.3 us
  Pallas kernels: 35.2 us -> 38 us
    ppermute x17, waiting for transfers between devices: 16.2 us -> 13.3 us  [send(): return lax.ppermute(value, AXES, pairs)]
    pallas_call x2, Pallas kernels: 13.7 us -> 16.5 us  [short_range(): pl.pallas_call(kernel, out_shape=pltpu.HBM((row_count, 2 * subs * width)...]
  transfers between devices with their start and end apart: 17 -> 17, of which waited for: 4 -> 3; matrix products, arithmetic and copies ran while one was open for 12% -> 12% of each run, Pallas kernels for 41% -> 45%
where the time goes in v21:
time: 81 us; the launch traced here: 80.9 us
  Pallas kernels  38 us (47%)
  starting transfers between devices  16.3 us (20%)
  waiting for transfers between devices  13.3 us (16%)
  other arithmetic  8.03 us (10%)
  local copies, waits for them, and re-layouts  3.96 us (5%)
  between operations  1.3 us (2%)
    pallas_call x2, Pallas kernels, short_range(): pl.pallas_call(kernel, out_shape=pltpu.HBM((row_count, 2 * subs * width)...  16.5 us
    ppermute x17, starting transfers between devices, send(): return lax.ppermute(value, AXES, pairs)  16.3 us
    ppermute x17, waiting for transfers between devices, send(): return lax.ppermute(value, AXES, pairs)  13.3 us
    pallas_call x2, Pallas kernels, own_sum(): pl.pallas_call(functools.partial(own_kernel, blocks=len(blocks), chains=c...  10.8 us
    pallas_call x4, Pallas kernels, long_range(): pl.pallas_call(functools.partial(long_kernel, blocks=len(blocks), chains=...  6.77 us
    select_n x4, other arithmetic, pick(): value = jnp.where(wanted == k, block, value)  4.22 us
    pallas_call x2, Pallas kernels, final_sum(): pl.pallas_call(functools.partial(final_kernel, pieces=count, blocks=block...  3.94 us
    unnamed x24, local copies, waits for them, and re-layouts  3.32 us
  transfers between devices with their start and end apart: 17, of which 3 were waited for; matrix products, arithmetic and copies ran while one was open for 12% of the time, Pallas kernels for 45%

profile of v21, /device:TPU:0, one launch (start us, length us, event | category | flops | bytes accessed | tf_op | source)
XLA Modules:
  0.0 80.9 jit_solution(15697125277294999931)
XLA Ops:
  0.0 1.1 %copy.19 = bf16[32,8,2,512]{3,1,2,0:T(8,128)(2,1)S(1)} copy(bf16[32,8,2,512]{3,2,1,0:T(2,128)(2,1)} %bitcast.51) | data formatting | bytes 1048576
  1.2 4.1 %collective-permute-start = (bf16[256,1024]{1,0:T(8,128)(2,1)S(1)}, bf16[256,1024]{1,0:T(8,128)(2,1)}, u32[]{:S(2)}, u32[]{:S(2)}) collective-permute-start(bf16[256,1024]{1,0:T(8,128)(2,1)S(1)} %bitcast.46), channel_id=1, source_target_pairs={{0,8},{1,9},{2,10},{3,11},{4,0},{5,1},{6,2},{7,3},{8,12},{9,13},{1... | collective-permute-start | bytes 1572872 | tf_op jit(solution)/shard_map/ppermute | solution.py:465
  5.3 1.5 %multiply_convert_fusion = bf16[256,2,512]{2,1,0:T(2,128)(2,1)S(1)} fusion(bf16[256,2,512]{2,1,0:T(2,128)(2,1)} %param.11, f32[512]{0:T(512)} %param.13), kind=kLoop, calls=%fused_computation.2 | loop fusion | flops 786432 | bytes 1050624 | tf_op jit(solution)/shard_map/convert_element_type | solution.py:423
  7.3 1.6 %collective-permute-start.4 = (bf16[1024,256]{1,0:T(8,128)(2,1)S(1)}, bf16[1024,256]{1,0:T(8,128)(2,1)}, u32[]{:S(2)}, u32[]{:S(2)}) collective-permute-start(bf16[1024,256]{1,0:T(8,128)(2,1)S(1)} %bitcast.42), channel_id=1, source_target_pairs={{0,16},{1,17},{2,18},{3,19},{4,20},{5,21},{6,22},{7,23},{8,24},{9,... | collective-permute-start | bytes 1572872 | tf_op jit(solution)/shard_map/ppermute | solution.py:465
  8.9 1.5 %collective-permute-start.5 = (bf16[1024,256]{1,0:T(8,128)(2,1)S(1)}, bf16[1024,256]{1,0:T(8,128)(2,1)S(1)}, u32[]{:S(2)}, u32[]{:S(2)}) collective-permute-start(bf16[1024,256]{1,0:T(8,128)(2,1)S(1)} %bitcast.43), channel_id=1, source_target_pairs={{0,2},{1,3},{2,0},{3,1},{4,6},{5,7},{6,4},{7,5},{8,10},{9,11},{10,... | collective-permute-start | bytes 1572872 | tf_op jit(solution)/shard_map/ppermute | solution.py:465
  11.0 1.4 %copy.17 = bf16[16,128,128]{1,2,0:T(8,128)(2,1)S(1)} copy(bf16[16,128,128]{2,1,0:T(8,128)(2,1)} %param.18) | data formatting | bytes 1048576 | tf_op args[7]
  14.2 6.7 %short_range.2.refs_1_ = f32[2,256,2048]{2,1,0:T(8,128)} custom-call(s32[1]{0:T(128)} %bitcast.1.half_ref, s32[16]{0:T(128)S(1)} %compare_convert_fusion.1.live_ref, s32[16]{0:T(128)S(1)} %copy-done.1, f32[3,16]{1,0:T(4,128)S(1)} %pad_maximum_fusion.1.meta_ref, bf16[128,4096]{1,0:T(8,128)(2,1)} %basis_ref.3, f32[1,4096]{1,0:T(1,128)S(1)} %bitcast.39, ...), custom_call_target="tpu_custom_call" | custom-call | flops 2147483648 | bytes 1 | tf_op jit(solution)/shard_map/short_range/pallas_call | solution.py:141
  21.0 8.5 %collective-permute-done.1 = bf16[256,1024]{1,0:T(8,128)(2,1)S(1)} collective-permute-done((bf16[256,1024]{1,0:T(8,128)(2,1)S(1)}, bf16[256,1024]{1,0:T(8,128)(2,1)S(1)}, u32[]{:S(2)}, u32[]{:S(2)}) %collective-permute-start.1) | collective-permute-done | bytes 524320 | tf_op jit(solution)/shard_map/ppermute | solution.py:465
  30.2 1.6 %collective-permute-start.6 = (bf16[256,1024]{1,0:T(8,128)(2,1)S(1)}, bf16[256,1024]{1,0:T(8,128)(2,1)S(1)}, u32[]{:S(2)}, u32[]{:S(2)}) collective-permute-start(bf16[256,1024]{1,0:T(8,128)(2,1)S(1)} %select_select_fusion.3), channel_id=1, source_target_pairs={{0,16},{1,17},{2,18},{3,19},{4,20},{5,21},{6,22},{7,23},{8,24},{9,... | collective-permute-start | bytes 1572872 | tf_op jit(solution)/shard_map/ppermute | solution.py:465
  31.8 1.5 %collective-permute-start.7 = (bf16[1024,256]{1,0:T(8,128)(2,1)}, bf16[1024,256]{1,0:T(8,128)(2,1)S(1)}, u32[]{:S(2)}, u32[]{:S(2)}) collective-permute-start(bf16[1024,256]{1,0:T(8,128)(2,1)} %collective-permute-done.4.refs_5_), channel_id=1, source_target_pairs={{0,2},{1,3},{2,0},{3,1},{4,6},{5,7},{6,4},{7,5},{8,10},{9,11},{10,... | collective-permute-start | bytes 1572872 | tf_op jit(solution)/shard_map/ppermute | solution.py:465
  35.4 9.7 %short_range.3.refs_6_.refs_8_.refs_1_ = f32[2048,512]{1,0:T(8,128)} custom-call(s32[1]{0:T(128)} %bitcast.1.half_ref, s32[16]{0:T(128)S(1)} %get-tuple-element.55.live_ref, s32[16]{0:T(128)S(1)} %get-tuple-element.54.sub_ref, f32[3,16]{1,0:T(4,128)S(1)} %pad_maximum_fusion.2.meta_ref, bf16[128,4096]{1,0:T(8,128)(2,1)} %basis_ref.3, f32[1,4096]{1,0:T(1,128)S(1)} %bitcast.40, ...), custom_call_target="tpu_custom_call" | custom-call | flops 2147483648 | bytes 1 | tf_op jit(solution)/shard_map/short_range/pallas_call | solution.py:141
  46.5 1.9 %select_select_fusion.2 = bf16[256,1024]{1,0:T(8,128)(2,1)} fusion(bf16[256,1024]{1,0:T(8,128)(2,1)} %collective-permute-done, bf16[256,1024]{1,0:T(8,128)(2,1)} %copy-done.6, bf16[256,1024]{1,0:T(8,128)(2,1)} %copy-done.2, pred[]{:T(512)S(6)} %eq.80, pred[]{:T(512)S(6)} %eq.73), kind=kLoop, calls=%fused_computation.6 | loop fusion | flops 524288 | bytes 2097154 | tf_op jit(solution)/shard_map/jit(_where)/select_n | solution.py:499
  48.5 1.4 %long_range.4 = bf16[256,512]{1,0:T(8,128)(2,1)} custom-call(bf16[256,1024]{1,0:T(8,128)(2,1)S(1)} %select_select_fusion.1.refs_0_, bf16[256,1024]{1,0:T(8,128)(2,1)S(1)} %collective-permute-done.6.refs_1_, bf16[1024,256]{1,0:T(8,128)(2,1)S(1)} %collective-permute-done.5.refs_2_, bf16[1024,256]{1,0:T(8,128)(2,1)S(1)} %collective-permute-done.7.refs_3_), custom_call_target="tpu_custom_call" | custom-call | flops 1 | bytes 1 | tf_op jit(solution)/shard_map/long_range/pallas_call | solution.py:221
  49.9 1.4 %collective-permute-start.15 = (bf16[256,512]{1,0:T(8,128)(2,1)}, bf16[256,512]{1,0:T(8,128)(2,1)S(1)}, u32[]{:S(2)}, u32[]{:S(2)}) collective-permute-start(bf16[256,512]{1,0:T(8,128)(2,1)} %long_range.4), channel_id=1, source_target_pairs={{0,2},{1,3},{2,0},{3,1},{4,6},{5,7},{6,4},{7,5},{8,10},{9,11},{10,... | collective-permute-start | bytes 786440 | tf_op jit(solution)/shard_map/ppermute | solution.py:465
  51.3 2.5 %long_range.5 = bf16[256,512]{1,0:T(8,128)(2,1)} custom-call(bf16[256,1024]{1,0:T(8,128)(2,1)S(1)} %collective-permute-done.8.refs_0_.refs_2_, bf16[256,1024]{1,0:T(8,128)(2,1)} %collective-permute-done.9.refs_1_.refs_3_, bf16[1024,256]{1,0:T(8,128)(2,1)S(1)} %collective-permute-done.5.refs_2_, bf16[1024,256]{1,0:T(8,128)(2,1)S(1)} %collective-permute-done.7.refs_3_), custom_call_target="tpu_custom_call" | custom-call | flops 1 | bytes 1 | tf_op jit(solution)/shard_map/long_range/pallas_call | solution.py:221
  54.6 5.0 %own_sum.2.refs_9_ = bf16[2048,2,256]{2,1,0:T(2,128)(2,1)} custom-call(s32[2]{0:T(128)S(1)} %pad_add_fusion.1.order_ref, bf16[256,1024]{1,0:T(8,128)(2,1)S(1)} %select_select_fusion.1.refs_0_, bf16[256,1024]{1,0:T(8,128)(2,1)S(1)} %collective-permute-done.6.refs_1_, bf16[256,1024]{1,0:T(8,128)(2,1)S(1)} %collective-permute-done.8.refs_0_.refs_2_, ...), custom_call_target="tpu_custom_call" | custom-call | flops 1 | bytes 1 | tf_op jit(solution)/shard_map/own_sum/pallas_call | solution.py:289
  60.8 1.7 %collective-permute-done.11.refs_1_ = bf16[256,1024]{1,0:T(8,128)(2,1)S(1)} collective-permute-done((bf16[256,1024]{1,0:T(8,128)(2,1)}, bf16[256,1024]{1,0:T(8,128)(2,1)S(1)}, u32[]{:S(2)}, u32[]{:S(2)}) %collective-permute-start.11) | collective-permute-done | bytes 524320 | tf_op jit(solution)/shard_map/ppermute | solution.py:465
  62.7 1.4 %long_range.7 = bf16[256,512]{1,0:T(8,128)(2,1)} custom-call(bf16[256,1024]{1,0:T(8,128)(2,1)S(1)} %select_select_fusion.refs_0_, bf16[256,1024]{1,0:T(8,128)(2,1)S(1)} %collective-permute-done.11.refs_1_, bf16[1024,512]{1,0:T(8,128)(2,1)S(1)} %get-tuple-element.62.refs_2_, bf16[1024,512]{1,0:T(8,128)(2,1)S(1)} %get-tuple-element.63.refs_3_), custom_call_target="tpu_custom_call" | custom-call | flops 1 | bytes 1 | tf_op jit(solution)/shard_map/long_range/pallas_call | solution.py:221
  64.4 1.4 %long_range.6 = bf16[256,512]{1,0:T(8,128)(2,1)} custom-call(bf16[256,1024]{1,0:T(8,128)(2,1)S(1)} %collective-permute-done.10.refs_0_.refs_2_, bf16[256,1024]{1,0:T(8,128)(2,1)S(1)} %collective-permute-done.12.refs_1_.refs_3_, bf16[1024,512]{1,0:T(8,128)(2,1)S(1)} %get-tuple-element.62.refs_2_, bf16[1024,512]{1,0:T(8,128)(2,1)S(1)} %get-tuple-element.63.refs_3_), custom_call_target="tpu_custom_call" | custom-call | flops 1 | bytes 1 | tf_op jit(solution)/shard_map/long_range/pallas_call | solution.py:221
  65.8 1.9 %collective-permute-start.13 = (bf16[256,512]{1,0:T(8,128)(2,1)}, bf16[256,512]{1,0:T(8,128)(2,1)S(1)}, u32[]{:S(2)}, u32[]{:S(2)}) collective-permute-start(bf16[256,512]{1,0:T(8,128)(2,1)} %long_range.6), channel_id=1, source_target_pairs={{0,2},{1,3},{2,0},{3,1},{4,6},{5,7},{6,4},{7,5},{8,10},{9,11},{10,... | collective-permute-start | bytes 786440 | tf_op jit(solution)/shard_map/ppermute | solution.py:465
  67.8 5.8 %own_sum.3.refs_2_ = bf16[2048,2,256]{2,1,0:T(2,128)(2,1)} custom-call(s32[4]{0:T(128)S(1)} %pad_add_fusion.2.order_ref, bf16[256,1024]{1,0:T(8,128)(2,1)S(1)} %select_select_fusion.refs_0_, bf16[256,1024]{1,0:T(8,128)(2,1)S(1)} %collective-permute-done.11.refs_1_, ...), custom_call_target="tpu_custom_call", output_to_operand_aliasing={{}: (10, {})} | custom-call | flops 1 | bytes 1 | tf_op jit(solution)/shard_map/own_sum/pallas_call | solution.py:289
  73.7 2.0 %final_sum.2.refs_2_ = bf16[2048,2,256]{2,1,0:T(2,128)(2,1)} custom-call(s32[1]{0:T(128)} %bitcast.22.order_ref, bf16[256,512]{1,0:T(8,128)(2,1)S(1)} %collective-permute-done.14.refs_0_, f32[2048,512]{1,0:T(8,128)} %short_range.3.refs_6_.refs_8_.refs_1_, bf16[2048,2,256]{2,1,0:T(2,128)(2,1)} %own_sum.3.refs_2_), custom_call_target="tpu_custom_call", output_to_operand_aliasing={{}: (3, {})} | custom-call | flops 1 | bytes 1 | tf_op jit(solution)/shard_map/final_sum/pallas_call | solution.py:344
  75.7 3.1 %collective-permute-done.13.refs_0_ = bf16[256,512]{1,0:T(8,128)(2,1)S(1)} collective-permute-done((bf16[256,512]{1,0:T(8,128)(2,1)}, bf16[256,512]{1,0:T(8,128)(2,1)S(1)}, u32[]{:S(2)}, u32[]{:S(2)}) %collective-permute-start.13) | collective-permute-done | bytes 262176 | tf_op jit(solution)/shard_map/ppermute | solution.py:465
  78.7 2.0 %final_sum.3 = bf16[2048,2,256]{2,1,0:T(2,128)(2,1)} custom-call(s32[1]{0:T(128)} %bitcast.order_ref, bf16[256,512]{1,0:T(8,128)(2,1)S(1)} %collective-permute-done.13.refs_0_, f32[2048,512]{1,0:T(8,128)} %short_range.3.refs_6_.refs_8_.refs_1_, bf16[2048,2,256]{2,1,0:T(2,128)(2,1)} %final_sum.2.refs_2_), custom_call_target="tpu_custom_call", output_to_operand_aliasing={{}: (3, {})} | custom-call | flops 1 | bytes 1 | tf_op jit(solution)/shard_map/final_sum/pallas_call | solution.py:344
  (69 shorter events, 8.9 us)
Async XLA Ops:
  0.0 12.4 %copy-start.1 = (s32[16]{0:T(128)S(1)}, s32[16]{0:T(128)}, u32[]{:S(2)}) copy-start(s32[16]{0:T(128)} %sub_ref.1) | copy-start | bytes 196
  0.0 12.4 %copy-start.8 = (s32[16]{0:T(128)S(1)}, s32[16]{0:T(128)}, u32[]{:S(2)}) copy-start(s32[16]{0:T(128)} %param.19) | copy-start | bytes 196
  1.1 29.0 %copy-start.5 = (bf16[32,8,2,512]{3,1,2,0:T(8,128)(2,1)}, bf16[32,8,2,512]{3,1,2,0:T(8,128)(2,1)S(1)}, u32[]{:S(2)}) copy-start(bf16[32,8,2,512]{3,1,2,0:T(8,128)(2,1)S(1)} %copy.19) | copy-start | bytes 1572868
  1.2 12.7 %copy-start.9 = (f32[125]{0:T(128)S(1)}, f32[125]{0:T(128)}, u32[]{:S(2)}) copy-start(f32[125]{0:T(128)} %param.16) | copy-start | bytes 1504
  1.2 12.7 %copy-start.10 = (f32[125]{0:T(128)S(1)}, f32[125]{0:T(128)}, u32[]{:S(2)}) copy-start(f32[125]{0:T(128)} %param.17) | copy-start | bytes 1504
  1.2 13.0 %copy-start = (f32[4096]{0:T(1024)S(1)}, f32[4096]{0:T(1024)}, u32[]{:S(2)}) copy-start(f32[4096]{0:T(1024)} %param.15) | copy-start | bytes 49156
  1.2 19.8 %collective-permute-start = (bf16[256,1024]{1,0:T(8,128)(2,1)S(1)}, bf16[256,1024]{1,0:T(8,128)(2,1)}, u32[]{:S(2)}, u32[]{:S(2)}) collective-permute-start(bf16[256,1024]{1,0:T(8,128)(2,1)S(1)} %bitcast.46), channel_id=1, source_target_pairs={{0,8},{1,9},{2,10},{3,11},{4,0},{5,1},{6,2},{7,3},{8,12},{9,13},{1... | collective-permute-start | bytes 1572872 | tf_op jit(solution)/shard_map/ppermute | solution.py:465
  5.3 24.2 %collective-permute-start.1 = (bf16[256,1024]{1,0:T(8,128)(2,1)S(1)}, bf16[256,1024]{1,0:T(8,128)(2,1)S(1)}, u32[]{:S(2)}, u32[]{:S(2)}) collective-permute-start(bf16[256,1024]{1,0:T(8,128)(2,1)S(1)} %bitcast.47), channel_id=1, source_target_pairs={{0,4},{1,5},{2,6},{3,7},{4,12},{5,13},{6,14},{7,15},{8,0},{9,1},{1... | collective-permute-start | bytes 1572872 | tf_op jit(solution)/shard_map/ppermute | solution.py:465
  7.3 13.6 %copy-start.4 = (bf16[256,2,512]{0,2,1:T(8,128)(2,1)}, bf16[256,2,512]{0,2,1:T(8,128)(2,1)S(1)}, u32[]{:S(2)}) copy-start(bf16[256,2,512]{0,2,1:T(8,128)(2,1)S(1)} %copy.18) | copy-start | bytes 1572868
  7.3 24.5 %collective-permute-start.4 = (bf16[1024,256]{1,0:T(8,128)(2,1)S(1)}, bf16[1024,256]{1,0:T(8,128)(2,1)}, u32[]{:S(2)}, u32[]{:S(2)}) collective-permute-start(bf16[1024,256]{1,0:T(8,128)(2,1)S(1)} %bitcast.42), channel_id=1, source_target_pairs={{0,16},{1,17},{2,18},{3,19},{4,20},{5,21},{6,22},{7,23},{8,24},{9,... | collective-permute-start | bytes 1572872 | tf_op jit(solution)/shard_map/ppermute | solution.py:465
  8.9 22.9 %collective-permute-start.5 = (bf16[1024,256]{1,0:T(8,128)(2,1)S(1)}, bf16[1024,256]{1,0:T(8,128)(2,1)S(1)}, u32[]{:S(2)}, u32[]{:S(2)}) collective-permute-start(bf16[1024,256]{1,0:T(8,128)(2,1)S(1)} %bitcast.43), channel_id=1, source_target_pairs={{0,2},{1,3},{2,0},{3,1},{4,6},{5,7},{6,4},{7,5},{8,10},{9,11},{10,... | collective-permute-start | bytes 1572872 | tf_op jit(solution)/shard_map/ppermute | solution.py:465
  13.3 21.2 %collective-permute-start.3 = (bf16[17,128,128]{2,1,0:T(8,128)(2,1)}, bf16[17,128,128]{2,1,0:T(8,128)(2,1)}, u32[]{:S(2)}, u32[]{:S(2)}) collective-permute-start(bf16[17,128,128]{2,1,0:T(8,128)(2,1)} %pad_maximum_fusion.refs_0_), channel_id=1, source_target_pairs={{0,16},{1,17},{2,18},{3,19},{4,20},{5,21},{6,22},{7,23},{8,24},{9,... | collective-permute-start | bytes 1671176 | tf_op jit(solution)/shard_map/ppermute | solution.py:465
  29.5 15.7 %collective-permute-start.2 = (bf16[256,1024]{1,0:T(8,128)(2,1)}, bf16[256,1024]{1,0:T(8,128)(2,1)S(1)}, u32[]{:S(2)}, u32[]{:S(2)}) collective-permute-start(bf16[256,1024]{1,0:T(8,128)(2,1)} %collective-permute-done), channel_id=1, source_target_pairs={{0,8},{1,9},{2,10},{3,11},{4,0},{5,1},{6,2},{7,3},{8,12},{9,13},{1... | collective-permute-start | bytes 1572872 | tf_op jit(solution)/shard_map/ppermute | solution.py:465
  30.2 15.0 %collective-permute-start.6 = (bf16[256,1024]{1,0:T(8,128)(2,1)S(1)}, bf16[256,1024]{1,0:T(8,128)(2,1)S(1)}, u32[]{:S(2)}, u32[]{:S(2)}) collective-permute-start(bf16[256,1024]{1,0:T(8,128)(2,1)S(1)} %select_select_fusion.3), channel_id=1, source_target_pairs={{0,16},{1,17},{2,18},{3,19},{4,20},{5,21},{6,22},{7,23},{8,24},{9,... | collective-permute-start | bytes 1572872 | tf_op jit(solution)/shard_map/ppermute | solution.py:465
  31.8 16.7 %collective-permute-start.7 = (bf16[1024,256]{1,0:T(8,128)(2,1)}, bf16[1024,256]{1,0:T(8,128)(2,1)S(1)}, u32[]{:S(2)}, u32[]{:S(2)}) collective-permute-start(bf16[1024,256]{1,0:T(8,128)(2,1)} %collective-permute-done.4.refs_5_), channel_id=1, source_target_pairs={{0,2},{1,3},{2,0},{3,1},{4,6},{5,7},{6,4},{7,5},{8,10},{9,11},{10,... | collective-permute-start | bytes 1572872 | tf_op jit(solution)/shard_map/ppermute | solution.py:465
  34.4 16.9 %collective-permute-start.8 = (bf16[256,1024]{1,0:T(8,128)(2,1)S(1)}, bf16[256,1024]{1,0:T(8,128)(2,1)S(1)}, u32[]{:S(2)}, u32[]{:S(2)}) collective-permute-start(bf16[256,1024]{1,0:T(8,128)(2,1)S(1)} %select_select_fusion.1.refs_0_), channel_id=1, source_target_pairs={{0,1},{1,0},{2,3},{3,2},{4,5},{5,4},{6,7},{7,6},{8,9},{9,8},{10,11... | collective-permute-start | bytes 1572872 | tf_op jit(solution)/shard_map/ppermute | solution.py:465
  46.0 5.3 %collective-permute-start.9 = (bf16[256,1024]{1,0:T(8,128)(2,1)S(1)}, bf16[256,1024]{1,0:T(8,128)(2,1)}, u32[]{:S(2)}, u32[]{:S(2)}) collective-permute-start(bf16[256,1024]{1,0:T(8,128)(2,1)S(1)} %collective-permute-done.6.refs_1_), channel_id=1, source_target_pairs={{0,1},{1,0},{2,3},{3,2},{4,5},{5,4},{6,7},{7,6},{8,9},{9,8},{10,11... | collective-permute-start | bytes 1572872 | tf_op jit(solution)/shard_map/ppermute | solution.py:465
  48.4 14.1 %collective-permute-start.11 = (bf16[256,1024]{1,0:T(8,128)(2,1)}, bf16[256,1024]{1,0:T(8,128)(2,1)S(1)}, u32[]{:S(2)}, u32[]{:S(2)}) collective-permute-start(bf16[256,1024]{1,0:T(8,128)(2,1)} %select_select_fusion.2), channel_id=1, source_target_pairs={{0,16},{1,17},{2,18},{3,19},{4,20},{5,21},{6,22},{7,23},{8,24},{9,... | collective-permute-start | bytes 1572872 | tf_op jit(solution)/shard_map/ppermute | solution.py:465
  49.9 18.0 %collective-permute-start.15 = (bf16[256,512]{1,0:T(8,128)(2,1)}, bf16[256,512]{1,0:T(8,128)(2,1)S(1)}, u32[]{:S(2)}, u32[]{:S(2)}) collective-permute-start(bf16[256,512]{1,0:T(8,128)(2,1)} %long_range.4), channel_id=1, source_target_pairs={{0,2},{1,3},{2,0},{3,1},{4,6},{5,7},{6,4},{7,5},{8,10},{9,11},{10,... | collective-permute-start | bytes 786440 | tf_op jit(solution)/shard_map/ppermute | solution.py:465
  53.8 14.1 %collective-permute-start.16 = (bf16[256,512]{1,0:T(8,128)(2,1)}, bf16[256,512]{1,0:T(8,128)(2,1)}, u32[]{:S(2)}, u32[]{:S(2)}) collective-permute-start(bf16[256,512]{1,0:T(8,128)(2,1)} %long_range.5), channel_id=1, source_target_pairs={{0,2},{1,3},{2,0},{3,1},{4,6},{5,7},{6,4},{7,5},{8,10},{9,11},{10,... | collective-permute-start | bytes 786440 | tf_op jit(solution)/shard_map/ppermute | solution.py:465
  60.7 3.7 %collective-permute-start.10 = (bf16[256,1024]{1,0:T(8,128)(2,1)S(1)}, bf16[256,1024]{1,0:T(8,128)(2,1)S(1)}, u32[]{:S(2)}, u32[]{:S(2)}) collective-permute-start(bf16[256,1024]{1,0:T(8,128)(2,1)S(1)} %select_select_fusion.refs_0_), channel_id=1, source_target_pairs={{0,1},{1,0},{2,3},{3,2},{4,5},{5,4},{6,7},{7,6},{8,9},{9,8},{10,11... | collective-permute-start | bytes 1572872 | tf_op jit(solution)/shard_map/ppermute | solution.py:465
  62.4 1.9 %collective-permute-start.12 = (bf16[256,1024]{1,0:T(8,128)(2,1)S(1)}, bf16[256,1024]{1,0:T(8,128)(2,1)S(1)}, u32[]{:S(2)}, u32[]{:S(2)}) collective-permute-start(bf16[256,1024]{1,0:T(8,128)(2,1)S(1)} %collective-permute-done.11.refs_1_), channel_id=1, source_target_pairs={{0,1},{1,0},{2,3},{3,2},{4,5},{5,4},{6,7},{7,6},{8,9},{9,8},{10,11... | collective-permute-start | bytes 1572872 | tf_op jit(solution)/shard_map/ppermute | solution.py:465
  64.1 9.6 %collective-permute-start.14 = (bf16[256,512]{1,0:T(8,128)(2,1)}, bf16[256,512]{1,0:T(8,128)(2,1)S(1)}, u32[]{:S(2)}, u32[]{:S(2)}) collective-permute-start(bf16[256,512]{1,0:T(8,128)(2,1)} %long_range.7), channel_id=1, source_target_pairs={{0,2},{1,3},{2,0},{3,1},{4,6},{5,7},{6,4},{7,5},{8,10},{9,11},{10,... | collective-permute-start | bytes 786440 | tf_op jit(solution)/shard_map/ppermute | solution.py:465
  65.8 12.9 %collective-permute-start.13 = (bf16[256,512]{1,0:T(8,128)(2,1)}, bf16[256,512]{1,0:T(8,128)(2,1)S(1)}, u32[]{:S(2)}, u32[]{:S(2)}) collective-permute-start(bf16[256,512]{1,0:T(8,128)(2,1)} %long_range.6), channel_id=1, source_target_pairs={{0,2},{1,3},{2,0},{3,1},{4,6},{5,7},{6,4},{7,5},{8,10},{9,11},{10,... | collective-permute-start | bytes 786440 | tf_op jit(solution)/shard_map/ppermute | solution.py:465
  (4 other events, 16.1 us)

commit v22 on v20

--- a/solution.py
+++ b/solution.py
@@ -13,6 +13,7 @@
 GROUP_ITEMS = 4
 SHORT_VMEM_BYTES = 15 * 1024 * 1024
 VMEM_BYTES = 10 * 1024 * 1024
+SMALL_VMEM_BYTES = 6 * 1024 * 1024
 
 
 def in_hbm(value):
@@ -227,7 +228,7 @@
         scratch_shapes=[pltpu.VMEM((chains * depth, 2 * width), jnp.bfloat16)]
         + [pltpu.VMEM((len(blocks), count, 2 * width), dtype) for dtype in dtypes]
         + [pltpu.SemaphoreType.DMA((pieces, len(blocks)))],
-        compiler_params=pltpu.CompilerParams(vmem_limit_bytes=VMEM_BYTES),
+        compiler_params=pltpu.CompilerParams(vmem_limit_bytes=SMALL_VMEM_BYTES),
         cost_estimate=SMALL_COST,
         name="long_range",
     )(*flat)
@@ -354,7 +355,7 @@
             pltpu.SemaphoreType.DMA((steps,)),
         ],
         input_output_aliases={count + 2: 0},
-        compiler_params=pltpu.CompilerParams(vmem_limit_bytes=VMEM_BYTES),
+        compiler_params=pltpu.CompilerParams(vmem_limit_bytes=SMALL_VMEM_BYTES),
         cost_estimate=SMALL_COST,
         name="final_sum",
     )(order, *pieces, in_hbm(short), earlier)

time: 81.4 us -> 81.4 us (level)
  waiting for transfers between devices: 14.4 us -> 13.1 us
  Pallas kernels: 36 us -> 36.9 us
    ppermute x17, waiting for transfers between devices: 14.4 us -> 13.1 us  [send(): return lax.ppermute(value, AXES, pairs)]
    pallas_call x2, Pallas kernels: 14.5 us -> 15.4 us  [short_range(): pl.pallas_call(kernel, out_shape=pltpu.HBM((row_count, 2 * subs * width)...]
  transfers between devices with their start and end apart: 17 -> 17, of which waited for: 3 -> 5; matrix products, arithmetic and copies ran while one was open for 12% -> 12% of each run, Pallas kernels for 42% -> 43%
where the time goes in v22:
time: 81.4 us; the launch traced here: 80.7 us
  Pallas kernels  36.9 us (45%)
  starting transfers between devices  17.8 us (22%)
  waiting for transfers between devices  13.1 us (16%)
  other arithmetic  8.03 us (10%)
  local copies, waits for them, and re-layouts  3.62 us (4%)
  between operations  1.28 us (2%)
    ppermute x17, starting transfers between devices, send(): return lax.ppermute(value, AXES, pairs)  17.8 us
    pallas_call x2, Pallas kernels, short_range(): pl.pallas_call(kernel, out_shape=pltpu.HBM((row_count, 2 * subs * width)...  15.4 us
    ppermute x17, waiting for transfers between devices, send(): return lax.ppermute(value, AXES, pairs)  13.1 us
    pallas_call x2, Pallas kernels, own_sum(): pl.pallas_call(functools.partial(own_kernel, blocks=len(blocks), chains=c...  10.8 us
    pallas_call x4, Pallas kernels, long_range(): pl.pallas_call(functools.partial(long_kernel, blocks=len(blocks), chains=...  6.77 us
    select_n x4, other arithmetic, pick(): value = jnp.where(wanted == k, block, value)  4.22 us
    pallas_call x2, Pallas kernels, final_sum(): pl.pallas_call(functools.partial(final_kernel, pieces=count, blocks=block...  3.94 us
    unnamed x24, local copies, waits for them, and re-layouts  2.98 us
  transfers between devices with their start and end apart: 17, of which 5 were waited for; matrix products, arithmetic and copies ran while one was open for 12% of the time, Pallas kernels for 43%

profile of v22, /device:TPU:0, one launch (start us, length us, event | category | flops | bytes accessed | tf_op | source)
XLA Modules:
  0.0 80.7 jit_solution(3245101731564602089)
XLA Ops:
  1.2 4.1 %collective-permute-start = (bf16[256,1024]{1,0:T(8,128)(2,1)S(1)}, bf16[256,1024]{1,0:T(8,128)(2,1)}, u32[]{:S(2)}, u32[]{:S(2)}) collective-permute-start(bf16[256,1024]{1,0:T(8,128)(2,1)S(1)} %bitcast.46), channel_id=1, source_target_pairs={{0,8},{1,9},{2,10},{3,11},{4,0},{5,1},{6,2},{7,3},{8,12},{9,13},{1... | collective-permute-start | bytes 1572872 | tf_op jit(solution)/shard_map/ppermute | solution.py:465
  5.3 1.5 %multiply_convert_fusion = bf16[256,2,512]{2,1,0:T(2,128)(2,1)S(1)} fusion(bf16[256,2,512]{2,1,0:T(2,128)(2,1)} %param.11, f32[512]{0:T(512)} %param.13), kind=kLoop, calls=%fused_computation.2 | loop fusion | flops 786432 | bytes 1050624 | tf_op jit(solution)/shard_map/convert_element_type | solution.py:423
  7.3 1.6 %collective-permute-start.4 = (bf16[1024,256]{1,0:T(8,128)(2,1)S(1)}, bf16[1024,256]{1,0:T(8,128)(2,1)}, u32[]{:S(2)}, u32[]{:S(2)}) collective-permute-start(bf16[1024,256]{1,0:T(8,128)(2,1)S(1)} %bitcast.42), channel_id=1, source_target_pairs={{0,16},{1,17},{2,18},{3,19},{4,20},{5,21},{6,22},{7,23},{8,24},{9,... | collective-permute-start | bytes 1572872 | tf_op jit(solution)/shard_map/ppermute | solution.py:465
  8.9 1.5 %collective-permute-start.5 = (bf16[1024,256]{1,0:T(8,128)(2,1)S(1)}, bf16[1024,256]{1,0:T(8,128)(2,1)S(1)}, u32[]{:S(2)}, u32[]{:S(2)}) collective-permute-start(bf16[1024,256]{1,0:T(8,128)(2,1)S(1)} %bitcast.43), channel_id=1, source_target_pairs={{0,2},{1,3},{2,0},{3,1},{4,6},{5,7},{6,4},{7,5},{8,10},{9,11},{10,... | collective-permute-start | bytes 1572872 | tf_op jit(solution)/shard_map/ppermute | solution.py:465
  11.0 1.4 %copy.17 = bf16[16,128,128]{1,2,0:T(8,128)(2,1)S(1)} copy(bf16[16,128,128]{2,1,0:T(8,128)(2,1)} %param.18) | data formatting | bytes 1048576 | tf_op args[7]
  14.2 8.0 %short_range.2.refs_1_ = f32[2,256,2048]{2,1,0:T(8,128)} custom-call(s32[1]{0:T(128)} %bitcast.1.half_ref, s32[16]{0:T(128)S(1)} %compare_convert_fusion.1.live_ref, s32[16]{0:T(128)S(1)} %copy-done.1, f32[3,16]{1,0:T(4,128)S(1)} %pad_maximum_fusion.1.meta_ref, bf16[128,4096]{1,0:T(8,128)(2,1)} %basis_ref.3, f32[1,4096]{1,0:T(1,128)S(1)} %bitcast.39, ...), custom_call_target="tpu_custom_call" | custom-call | flops 2147483648 | bytes 1 | tf_op jit(solution)/shard_map/short_range/pallas_call | solution.py:141
  22.3 7.2 %collective-permute-done.1 = bf16[256,1024]{1,0:T(8,128)(2,1)S(1)} collective-permute-done((bf16[256,1024]{1,0:T(8,128)(2,1)S(1)}, bf16[256,1024]{1,0:T(8,128)(2,1)S(1)}, u32[]{:S(2)}, u32[]{:S(2)}) %collective-permute-start.1) | collective-permute-done | bytes 524320 | tf_op jit(solution)/shard_map/ppermute | solution.py:465
  30.2 1.6 %collective-permute-start.6 = (bf16[256,1024]{1,0:T(8,128)(2,1)S(1)}, bf16[256,1024]{1,0:T(8,128)(2,1)S(1)}, u32[]{:S(2)}, u32[]{:S(2)}) collective-permute-start(bf16[256,1024]{1,0:T(8,128)(2,1)S(1)} %select_select_fusion.3), channel_id=1, source_target_pairs={{0,16},{1,17},{2,18},{3,19},{4,20},{5,21},{6,22},{7,23},{8,24},{9,... | collective-permute-start | bytes 1572872 | tf_op jit(solution)/shard_map/ppermute | solution.py:465
  31.8 1.5 %collective-permute-start.7 = (bf16[1024,256]{1,0:T(8,128)(2,1)}, bf16[1024,256]{1,0:T(8,128)(2,1)S(1)}, u32[]{:S(2)}, u32[]{:S(2)}) collective-permute-start(bf16[1024,256]{1,0:T(8,128)(2,1)} %collective-permute-done.4.refs_5_), channel_id=1, source_target_pairs={{0,2},{1,3},{2,0},{3,1},{4,6},{5,7},{6,4},{7,5},{8,10},{9,11},{10,... | collective-permute-start | bytes 1572872 | tf_op jit(solution)/shard_map/ppermute | solution.py:465
  35.4 7.3 %short_range.3.refs_6_.refs_8_.refs_1_ = f32[2048,512]{1,0:T(8,128)} custom-call(s32[1]{0:T(128)} %bitcast.1.half_ref, s32[16]{0:T(128)S(1)} %get-tuple-element.55.live_ref, s32[16]{0:T(128)S(1)} %get-tuple-element.54.sub_ref, f32[3,16]{1,0:T(4,128)S(1)} %pad_maximum_fusion.2.meta_ref, bf16[128,4096]{1,0:T(8,128)(2,1)} %basis_ref.3, f32[1,4096]{1,0:T(1,128)S(1)} %bitcast.40, ...), custom_call_target="tpu_custom_call" | custom-call | flops 2147483648 | bytes 1 | tf_op jit(solution)/shard_map/short_range/pallas_call | solution.py:141
  44.4 1.9 %collective-permute-start.9 = (bf16[256,1024]{1,0:T(8,128)(2,1)S(1)}, bf16[256,1024]{1,0:T(8,128)(2,1)}, u32[]{:S(2)}, u32[]{:S(2)}) collective-permute-start(bf16[256,1024]{1,0:T(8,128)(2,1)S(1)} %collective-permute-done.6.refs_1_), channel_id=1, source_target_pairs={{0,1},{1,0},{2,3},{3,2},{4,5},{5,4},{6,7},{7,6},{8,9},{9,8},{10,11... | collective-permute-start | bytes 1572872 | tf_op jit(solution)/shard_map/ppermute | solution.py:465
  46.3 1.9 %select_select_fusion.2 = bf16[256,1024]{1,0:T(8,128)(2,1)} fusion(bf16[256,1024]{1,0:T(8,128)(2,1)} %collective-permute-done, bf16[256,1024]{1,0:T(8,128)(2,1)} %copy-done.6, bf16[256,1024]{1,0:T(8,128)(2,1)} %copy-done.2, pred[]{:T(512)S(6)} %eq.80, pred[]{:T(512)S(6)} %eq.73), kind=kLoop, calls=%fused_computation.6 | loop fusion | flops 524288 | bytes 2097154 | tf_op jit(solution)/shard_map/jit(_where)/select_n | solution.py:499
  48.3 1.4 %long_range.4 = bf16[256,512]{1,0:T(8,128)(2,1)} custom-call(bf16[256,1024]{1,0:T(8,128)(2,1)S(1)} %select_select_fusion.1.refs_0_, bf16[256,1024]{1,0:T(8,128)(2,1)S(1)} %collective-permute-done.6.refs_1_, bf16[1024,256]{1,0:T(8,128)(2,1)S(1)} %collective-permute-done.5.refs_2_, bf16[1024,256]{1,0:T(8,128)(2,1)S(1)} %collective-permute-done.7.refs_3_), custom_call_target="tpu_custom_call" | custom-call | flops 1 | bytes 1 | tf_op jit(solution)/shard_map/long_range/pallas_call | solution.py:221
  49.7 1.4 %collective-permute-start.15 = (bf16[256,512]{1,0:T(8,128)(2,1)}, bf16[256,512]{1,0:T(8,128)(2,1)S(1)}, u32[]{:S(2)}, u32[]{:S(2)}) collective-permute-start(bf16[256,512]{1,0:T(8,128)(2,1)} %long_range.4), channel_id=1, source_target_pairs={{0,2},{1,3},{2,0},{3,1},{4,6},{5,7},{6,4},{7,5},{8,10},{9,11},{10,... | collective-permute-start | bytes 786440 | tf_op jit(solution)/shard_map/ppermute | solution.py:465
  51.1 2.5 %long_range.5 = bf16[256,512]{1,0:T(8,128)(2,1)} custom-call(bf16[256,1024]{1,0:T(8,128)(2,1)S(1)} %collective-permute-done.8.refs_0_.refs_2_, bf16[256,1024]{1,0:T(8,128)(2,1)} %collective-permute-done.9.refs_1_.refs_3_, bf16[1024,256]{1,0:T(8,128)(2,1)S(1)} %collective-permute-done.5.refs_2_, bf16[1024,256]{1,0:T(8,128)(2,1)S(1)} %collective-permute-done.7.refs_3_), custom_call_target="tpu_custom_call" | custom-call | flops 1 | bytes 1 | tf_op jit(solution)/shard_map/long_range/pallas_call | solution.py:221
  54.4 5.0 %own_sum.2.refs_9_ = bf16[2048,2,256]{2,1,0:T(2,128)(2,1)} custom-call(s32[2]{0:T(128)S(1)} %pad_add_fusion.1.order_ref, bf16[256,1024]{1,0:T(8,128)(2,1)S(1)} %select_select_fusion.1.refs_0_, bf16[256,1024]{1,0:T(8,128)(2,1)S(1)} %collective-permute-done.6.refs_1_, bf16[256,1024]{1,0:T(8,128)(2,1)S(1)} %collective-permute-done.8.refs_0_.refs_2_, ...), custom_call_target="tpu_custom_call" | custom-call | flops 1 | bytes 1 | tf_op jit(solution)/shard_map/own_sum/pallas_call | solution.py:289
  60.6 1.7 %collective-permute-done.11.refs_1_ = bf16[256,1024]{1,0:T(8,128)(2,1)S(1)} collective-permute-done((bf16[256,1024]{1,0:T(8,128)(2,1)}, bf16[256,1024]{1,0:T(8,128)(2,1)S(1)}, u32[]{:S(2)}, u32[]{:S(2)}) %collective-permute-start.11) | collective-permute-done | bytes 524320 | tf_op jit(solution)/shard_map/ppermute | solution.py:465
  62.5 1.4 %long_range.7 = bf16[256,512]{1,0:T(8,128)(2,1)} custom-call(bf16[256,1024]{1,0:T(8,128)(2,1)S(1)} %select_select_fusion.refs_0_, bf16[256,1024]{1,0:T(8,128)(2,1)S(1)} %collective-permute-done.11.refs_1_, bf16[1024,512]{1,0:T(8,128)(2,1)S(1)} %get-tuple-element.62.refs_2_, bf16[1024,512]{1,0:T(8,128)(2,1)S(1)} %get-tuple-element.63.refs_3_), custom_call_target="tpu_custom_call" | custom-call | flops 1 | bytes 1 | tf_op jit(solution)/shard_map/long_range/pallas_call | solution.py:221
  64.2 1.4 %long_range.6 = bf16[256,512]{1,0:T(8,128)(2,1)} custom-call(bf16[256,1024]{1,0:T(8,128)(2,1)S(1)} %collective-permute-done.10.refs_0_.refs_2_, bf16[256,1024]{1,0:T(8,128)(2,1)S(1)} %collective-permute-done.12.refs_1_.refs_3_, bf16[1024,512]{1,0:T(8,128)(2,1)S(1)} %get-tuple-element.62.refs_2_, bf16[1024,512]{1,0:T(8,128)(2,1)S(1)} %get-tuple-element.63.refs_3_), custom_call_target="tpu_custom_call" | custom-call | flops 1 | bytes 1 | tf_op jit(solution)/shard_map/long_range/pallas_call | solution.py:221
  65.6 1.9 %collective-permute-start.13 = (bf16[256,512]{1,0:T(8,128)(2,1)}, bf16[256,512]{1,0:T(8,128)(2,1)S(1)}, u32[]{:S(2)}, u32[]{:S(2)}) collective-permute-start(bf16[256,512]{1,0:T(8,128)(2,1)} %long_range.6), channel_id=1, source_target_pairs={{0,2},{1,3},{2,0},{3,1},{4,6},{5,7},{6,4},{7,5},{8,10},{9,11},{10,... | collective-permute-start | bytes 786440 | tf_op jit(solution)/shard_map/ppermute | solution.py:465
  67.7 5.8 %own_sum.3.refs_2_ = bf16[2048,2,256]{2,1,0:T(2,128)(2,1)} custom-call(s32[4]{0:T(128)S(1)} %pad_add_fusion.2.order_ref, bf16[256,1024]{1,0:T(8,128)(2,1)S(1)} %select_select_fusion.refs_0_, bf16[256,1024]{1,0:T(8,128)(2,1)S(1)} %collective-permute-done.11.refs_1_, ...), custom_call_target="tpu_custom_call", output_to_operand_aliasing={{}: (10, {})} | custom-call | flops 1 | bytes 1 | tf_op jit(solution)/shard_map/own_sum/pallas_call | solution.py:289
  73.5 2.0 %final_sum.2.refs_2_ = bf16[2048,2,256]{2,1,0:T(2,128)(2,1)} custom-call(s32[1]{0:T(128)} %bitcast.22.order_ref, bf16[256,512]{1,0:T(8,128)(2,1)S(1)} %collective-permute-done.14.refs_0_, f32[2048,512]{1,0:T(8,128)} %short_range.3.refs_6_.refs_8_.refs_1_, bf16[2048,2,256]{2,1,0:T(2,128)(2,1)} %own_sum.3.refs_2_), custom_call_target="tpu_custom_call", output_to_operand_aliasing={{}: (3, {})} | custom-call | flops 1 | bytes 1 | tf_op jit(solution)/shard_map/final_sum/pallas_call | solution.py:344
  75.5 3.1 %collective-permute-done.13.refs_0_ = bf16[256,512]{1,0:T(8,128)(2,1)S(1)} collective-permute-done((bf16[256,512]{1,0:T(8,128)(2,1)}, bf16[256,512]{1,0:T(8,128)(2,1)S(1)}, u32[]{:S(2)}, u32[]{:S(2)}) %collective-permute-start.13) | collective-permute-done | bytes 262176 | tf_op jit(solution)/shard_map/ppermute | solution.py:465
  78.6 2.0 %final_sum.3 = bf16[2048,2,256]{2,1,0:T(2,128)(2,1)} custom-call(s32[1]{0:T(128)} %bitcast.order_ref, bf16[256,512]{1,0:T(8,128)(2,1)S(1)} %collective-permute-done.13.refs_0_, f32[2048,512]{1,0:T(8,128)} %short_range.3.refs_6_.refs_8_.refs_1_, bf16[2048,2,256]{2,1,0:T(2,128)(2,1)} %final_sum.2.refs_2_), custom_call_target="tpu_custom_call", output_to_operand_aliasing={{}: (3, {})} | custom-call | flops 1 | bytes 1 | tf_op jit(solution)/shard_map/final_sum/pallas_call | solution.py:344
  (69 shorter events, 10.4 us)
Async XLA Ops:
  0.0 12.4 %copy-start.1 = (s32[16]{0:T(128)S(1)}, s32[16]{0:T(128)}, u32[]{:S(2)}) copy-start(s32[16]{0:T(128)} %sub_ref.1) | copy-start | bytes 196
  0.0 12.4 %copy-start.8 = (s32[16]{0:T(128)S(1)}, s32[16]{0:T(128)}, u32[]{:S(2)}) copy-start(s32[16]{0:T(128)} %param.19) | copy-start | bytes 196
  1.1 29.0 %copy-start.5 = (bf16[32,8,2,512]{3,1,2,0:T(8,128)(2,1)}, bf16[32,8,2,512]{3,1,2,0:T(8,128)(2,1)S(1)}, u32[]{:S(2)}) copy-start(bf16[32,8,2,512]{3,1,2,0:T(8,128)(2,1)S(1)} %copy.19) | copy-start | bytes 1572868
  1.2 12.7 %copy-start.9 = (f32[125]{0:T(128)S(1)}, f32[125]{0:T(128)}, u32[]{:S(2)}) copy-start(f32[125]{0:T(128)} %param.16) | copy-start | bytes 1504
  1.2 12.7 %copy-start.10 = (f32[125]{0:T(128)S(1)}, f32[125]{0:T(128)}, u32[]{:S(2)}) copy-start(f32[125]{0:T(128)} %param.17) | copy-start | bytes 1504
  1.2 13.0 %copy-start = (f32[4096]{0:T(1024)S(1)}, f32[4096]{0:T(1024)}, u32[]{:S(2)}) copy-start(f32[4096]{0:T(1024)} %param.15) | copy-start | bytes 49156
  1.2 21.1 %collective-permute-start = (bf16[256,1024]{1,0:T(8,128)(2,1)S(1)}, bf16[256,1024]{1,0:T(8,128)(2,1)}, u32[]{:S(2)}, u32[]{:S(2)}) collective-permute-start(bf16[256,1024]{1,0:T(8,128)(2,1)S(1)} %bitcast.46), channel_id=1, source_target_pairs={{0,8},{1,9},{2,10},{3,11},{4,0},{5,1},{6,2},{7,3},{8,12},{9,13},{1... | collective-permute-start | bytes 1572872 | tf_op jit(solution)/shard_map/ppermute | solution.py:465
  5.3 24.2 %collective-permute-start.1 = (bf16[256,1024]{1,0:T(8,128)(2,1)S(1)}, bf16[256,1024]{1,0:T(8,128)(2,1)S(1)}, u32[]{:S(2)}, u32[]{:S(2)}) collective-permute-start(bf16[256,1024]{1,0:T(8,128)(2,1)S(1)} %bitcast.47), channel_id=1, source_target_pairs={{0,4},{1,5},{2,6},{3,7},{4,12},{5,13},{6,14},{7,15},{8,0},{9,1},{1... | collective-permute-start | bytes 1572872 | tf_op jit(solution)/shard_map/ppermute | solution.py:465
  7.3 14.9 %copy-start.4 = (bf16[256,2,512]{0,2,1:T(8,128)(2,1)}, bf16[256,2,512]{0,2,1:T(8,128)(2,1)S(1)}, u32[]{:S(2)}) copy-start(bf16[256,2,512]{0,2,1:T(8,128)(2,1)S(1)} %copy.18) | copy-start | bytes 1572868
  7.3 24.5 %collective-permute-start.4 = (bf16[1024,256]{1,0:T(8,128)(2,1)S(1)}, bf16[1024,256]{1,0:T(8,128)(2,1)}, u32[]{:S(2)}, u32[]{:S(2)}) collective-permute-start(bf16[1024,256]{1,0:T(8,128)(2,1)S(1)} %bitcast.42), channel_id=1, source_target_pairs={{0,16},{1,17},{2,18},{3,19},{4,20},{5,21},{6,22},{7,23},{8,24},{9,... | collective-permute-start | bytes 1572872 | tf_op jit(solution)/shard_map/ppermute | solution.py:465
  8.9 22.9 %collective-permute-start.5 = (bf16[1024,256]{1,0:T(8,128)(2,1)S(1)}, bf16[1024,256]{1,0:T(8,128)(2,1)S(1)}, u32[]{:S(2)}, u32[]{:S(2)}) collective-permute-start(bf16[1024,256]{1,0:T(8,128)(2,1)S(1)} %bitcast.43), channel_id=1, source_target_pairs={{0,2},{1,3},{2,0},{3,1},{4,6},{5,7},{6,4},{7,5},{8,10},{9,11},{10,... | collective-permute-start | bytes 1572872 | tf_op jit(solution)/shard_map/ppermute | solution.py:465
  13.3 21.2 %collective-permute-start.3 = (bf16[17,128,128]{2,1,0:T(8,128)(2,1)}, bf16[17,128,128]{2,1,0:T(8,128)(2,1)}, u32[]{:S(2)}, u32[]{:S(2)}) collective-permute-start(bf16[17,128,128]{2,1,0:T(8,128)(2,1)} %pad_maximum_fusion.refs_0_), channel_id=1, source_target_pairs={{0,16},{1,17},{2,18},{3,19},{4,20},{5,21},{6,22},{7,23},{8,24},{9,... | collective-permute-start | bytes 1671176 | tf_op jit(solution)/shard_map/ppermute | solution.py:465
  29.5 14.1 %collective-permute-start.2 = (bf16[256,1024]{1,0:T(8,128)(2,1)}, bf16[256,1024]{1,0:T(8,128)(2,1)S(1)}, u32[]{:S(2)}, u32[]{:S(2)}) collective-permute-start(bf16[256,1024]{1,0:T(8,128)(2,1)} %collective-permute-done), channel_id=1, source_target_pairs={{0,8},{1,9},{2,10},{3,11},{4,0},{5,1},{6,2},{7,3},{8,12},{9,13},{1... | collective-permute-start | bytes 1572872 | tf_op jit(solution)/shard_map/ppermute | solution.py:465
  30.2 13.7 %collective-permute-start.6 = (bf16[256,1024]{1,0:T(8,128)(2,1)S(1)}, bf16[256,1024]{1,0:T(8,128)(2,1)S(1)}, u32[]{:S(2)}, u32[]{:S(2)}) collective-permute-start(bf16[256,1024]{1,0:T(8,128)(2,1)S(1)} %select_select_fusion.3), channel_id=1, source_target_pairs={{0,16},{1,17},{2,18},{3,19},{4,20},{5,21},{6,22},{7,23},{8,24},{9,... | collective-permute-start | bytes 1572872 | tf_op jit(solution)/shard_map/ppermute | solution.py:465
  31.8 16.5 %collective-permute-start.7 = (bf16[1024,256]{1,0:T(8,128)(2,1)}, bf16[1024,256]{1,0:T(8,128)(2,1)S(1)}, u32[]{:S(2)}, u32[]{:S(2)}) collective-permute-start(bf16[1024,256]{1,0:T(8,128)(2,1)} %collective-permute-done.4.refs_5_), channel_id=1, source_target_pairs={{0,2},{1,3},{2,0},{3,1},{4,6},{5,7},{6,4},{7,5},{8,10},{9,11},{10,... | collective-permute-start | bytes 1572872 | tf_op jit(solution)/shard_map/ppermute | solution.py:465
  34.4 16.7 %collective-permute-start.8 = (bf16[256,1024]{1,0:T(8,128)(2,1)S(1)}, bf16[256,1024]{1,0:T(8,128)(2,1)S(1)}, u32[]{:S(2)}, u32[]{:S(2)}) collective-permute-start(bf16[256,1024]{1,0:T(8,128)(2,1)S(1)} %select_select_fusion.1.refs_0_), channel_id=1, source_target_pairs={{0,1},{1,0},{2,3},{3,2},{4,5},{5,4},{6,7},{7,6},{8,9},{9,8},{10,11... | collective-permute-start | bytes 1572872 | tf_op jit(solution)/shard_map/ppermute | solution.py:465
  44.4 6.8 %collective-permute-start.9 = (bf16[256,1024]{1,0:T(8,128)(2,1)S(1)}, bf16[256,1024]{1,0:T(8,128)(2,1)}, u32[]{:S(2)}, u32[]{:S(2)}) collective-permute-start(bf16[256,1024]{1,0:T(8,128)(2,1)S(1)} %collective-permute-done.6.refs_1_), channel_id=1, source_target_pairs={{0,1},{1,0},{2,3},{3,2},{4,5},{5,4},{6,7},{7,6},{8,9},{9,8},{10,11... | collective-permute-start | bytes 1572872 | tf_op jit(solution)/shard_map/ppermute | solution.py:465
  48.2 14.0 %collective-permute-start.11 = (bf16[256,1024]{1,0:T(8,128)(2,1)}, bf16[256,1024]{1,0:T(8,128)(2,1)S(1)}, u32[]{:S(2)}, u32[]{:S(2)}) collective-permute-start(bf16[256,1024]{1,0:T(8,128)(2,1)} %select_select_fusion.2), channel_id=1, source_target_pairs={{0,16},{1,17},{2,18},{3,19},{4,20},{5,21},{6,22},{7,23},{8,24},{9,... | collective-permute-start | bytes 1572872 | tf_op jit(solution)/shard_map/ppermute | solution.py:465
  49.7 17.9 %collective-permute-start.15 = (bf16[256,512]{1,0:T(8,128)(2,1)}, bf16[256,512]{1,0:T(8,128)(2,1)S(1)}, u32[]{:S(2)}, u32[]{:S(2)}) collective-permute-start(bf16[256,512]{1,0:T(8,128)(2,1)} %long_range.4), channel_id=1, source_target_pairs={{0,2},{1,3},{2,0},{3,1},{4,6},{5,7},{6,4},{7,5},{8,10},{9,11},{10,... | collective-permute-start | bytes 786440 | tf_op jit(solution)/shard_map/ppermute | solution.py:465
  53.6 14.0 %collective-permute-start.16 = (bf16[256,512]{1,0:T(8,128)(2,1)}, bf16[256,512]{1,0:T(8,128)(2,1)}, u32[]{:S(2)}, u32[]{:S(2)}) collective-permute-start(bf16[256,512]{1,0:T(8,128)(2,1)} %long_range.5), channel_id=1, source_target_pairs={{0,2},{1,3},{2,0},{3,1},{4,6},{5,7},{6,4},{7,5},{8,10},{9,11},{10,... | collective-permute-start | bytes 786440 | tf_op jit(solution)/shard_map/ppermute | solution.py:465
  60.5 3.7 %collective-permute-start.10 = (bf16[256,1024]{1,0:T(8,128)(2,1)S(1)}, bf16[256,1024]{1,0:T(8,128)(2,1)S(1)}, u32[]{:S(2)}, u32[]{:S(2)}) collective-permute-start(bf16[256,1024]{1,0:T(8,128)(2,1)S(1)} %select_select_fusion.refs_0_), channel_id=1, source_target_pairs={{0,1},{1,0},{2,3},{3,2},{4,5},{5,4},{6,7},{7,6},{8,9},{9,8},{10,11... | collective-permute-start | bytes 1572872 | tf_op jit(solution)/shard_map/ppermute | solution.py:465
  62.3 1.9 %collective-permute-start.12 = (bf16[256,1024]{1,0:T(8,128)(2,1)S(1)}, bf16[256,1024]{1,0:T(8,128)(2,1)S(1)}, u32[]{:S(2)}, u32[]{:S(2)}) collective-permute-start(bf16[256,1024]{1,0:T(8,128)(2,1)S(1)} %collective-permute-done.11.refs_1_), channel_id=1, source_target_pairs={{0,1},{1,0},{2,3},{3,2},{4,5},{5,4},{6,7},{7,6},{8,9},{9,8},{10,11... | collective-permute-start | bytes 1572872 | tf_op jit(solution)/shard_map/ppermute | solution.py:465
  64.0 9.5 %collective-permute-start.14 = (bf16[256,512]{1,0:T(8,128)(2,1)}, bf16[256,512]{1,0:T(8,128)(2,1)S(1)}, u32[]{:S(2)}, u32[]{:S(2)}) collective-permute-start(bf16[256,512]{1,0:T(8,128)(2,1)} %long_range.7), channel_id=1, source_target_pairs={{0,2},{1,3},{2,0},{3,1},{4,6},{5,7},{6,4},{7,5},{8,10},{9,11},{10,... | collective-permute-start | bytes 786440 | tf_op jit(solution)/shard_map/ppermute | solution.py:465
  65.6 12.9 %collective-permute-start.13 = (bf16[256,512]{1,0:T(8,128)(2,1)}, bf16[256,512]{1,0:T(8,128)(2,1)S(1)}, u32[]{:S(2)}, u32[]{:S(2)}) collective-permute-start(bf16[256,512]{1,0:T(8,128)(2,1)} %long_range.6), channel_id=1, source_target_pairs={{0,2},{1,3},{2,0},{3,1},{4,6},{5,7},{6,4},{7,5},{8,10},{9,11},{10,... | collective-permute-start | bytes 786440 | tf_op jit(solution)/shard_map/ppermute | solution.py:465
  (4 other events, 16.1 us)

commit v23 on v19

--- a/solution.py
+++ b/solution.py
@@ -565,8 +565,10 @@
         away_factors = factors[1:]
         if n:
             away_factors = [[both_parts(after(v, *away[0])) for v in pair] for pair in factors[1:]]
-        crossed.append(with_cores(moved if n else after(moved, short, held[length // 2])))
+        crossed.append(with_cores(moved) if n else [after(moved, short, held[length // 2])])
         for t in range(CORES):
+            if t == len(crossed[n]):
+                crossed[n].append(over_core(after(crossed[n][0], *away[n]), t))
             multiply(n, t, away_factors)
         blocks = [
             (after(mine[n][0], *away[n]), crossed[n][0]),

time: 81.4 us -> 82.6 us (1.015)
  waiting for transfers between devices: 16.2 us -> 17.7 us
    ppermute x17, waiting for transfers between devices: 16.2 us -> 17.7 us  [send(): return lax.ppermute(value, AXES, pairs)]
    ppermute x17, starting transfers between devices: 16 us -> 16.8 us  [send(): return lax.ppermute(value, AXES, pairs)]
    unnamed x24 -> x26, local copies, waits for them, and re-layouts: 3.32 us -> 2.55 us
  transfers between devices with their start and end apart: 17 -> 17, of which waited for: 4 -> 6; matrix products, arithmetic and copies ran while one was open for 12% -> 12% of each run, Pallas kernels for 41% -> 40%
where the time goes in v23:
time: 82.6 us; the launch traced here: 81.5 us
  Pallas kernels  34.5 us (42%)
  waiting for transfers between devices  17.7 us (21%)
  starting transfers between devices  16.8 us (20%)
  other arithmetic  8.03 us (10%)
  local copies, waits for them, and re-layouts  3.18 us (4%)
  between operations  1.28 us (2%)
    ppermute x17, waiting for transfers between devices, send(): return lax.ppermute(value, AXES, pairs)  17.7 us
    ppermute x17, starting transfers between devices, send(): return lax.ppermute(value, AXES, pairs)  16.8 us
    pallas_call x2, Pallas kernels, short_range(): pl.pallas_call(kernel, out_shape=pltpu.HBM((row_count, 2 * subs * width)...  13 us
    pallas_call x2, Pallas kernels, own_sum(): pl.pallas_call(functools.partial(own_kernel, blocks=len(blocks), chains=c...  10.8 us
    pallas_call x4, Pallas kernels, long_range(): pl.pallas_call(functools.partial(long_kernel, blocks=len(blocks), chains=...  6.77 us
    select_n x4, other arithmetic, pick(): value = jnp.where(wanted == k, block, value)  4.23 us
    pallas_call x2, Pallas kernels, final_sum(): pl.pallas_call(functools.partial(final_kernel, pieces=count, blocks=block...  3.94 us
    unnamed x26, local copies, waits for them, and re-layouts  2.55 us
  transfers between devices with their start and end apart: 17, of which 6 were waited for; matrix products, arithmetic and copies ran while one was open for 12% of the time, Pallas kernels for 40%

profile of v23, /device:TPU:0, one launch (start us, length us, event | category | flops | bytes accessed | tf_op | source)
XLA Modules:
  0.0 81.5 jit_solution(479761443570134153)
XLA Ops:
  1.2 4.1 %collective-permute-start = (bf16[256,1024]{1,0:T(8,128)(2,1)S(1)}, bf16[256,1024]{1,0:T(8,128)(2,1)}, u32[]{:S(2)}, u32[]{:S(2)}) collective-permute-start(bf16[256,1024]{1,0:T(8,128)(2,1)S(1)} %bitcast.46), channel_id=1, source_target_pairs={{0,8},{1,9},{2,10},{3,11},{4,0},{5,1},{6,2},{7,3},{8,12},{9,13},{1... | collective-permute-start | bytes 1572872 | tf_op jit(solution)/shard_map/ppermute | solution.py:465
  5.3 1.5 %multiply_convert_fusion = bf16[256,2,512]{2,1,0:T(2,128)(2,1)S(1)} fusion(bf16[256,2,512]{2,1,0:T(2,128)(2,1)} %param.11, f32[512]{0:T(512)} %param.13), kind=kLoop, calls=%fused_computation.2 | loop fusion | flops 786432 | bytes 1050624 | tf_op jit(solution)/shard_map/convert_element_type | solution.py:423
  7.3 1.6 %collective-permute-start.4 = (bf16[1024,256]{1,0:T(8,128)(2,1)S(1)}, bf16[1024,256]{1,0:T(8,128)(2,1)}, u32[]{:S(2)}, u32[]{:S(2)}) collective-permute-start(bf16[1024,256]{1,0:T(8,128)(2,1)S(1)} %bitcast.42), channel_id=1, source_target_pairs={{0,16},{1,17},{2,18},{3,19},{4,20},{5,21},{6,22},{7,23},{8,24},{9,... | collective-permute-start | bytes 1572872 | tf_op jit(solution)/shard_map/ppermute | solution.py:465
  8.9 1.5 %collective-permute-start.5 = (bf16[1024,256]{1,0:T(8,128)(2,1)S(1)}, bf16[1024,256]{1,0:T(8,128)(2,1)S(1)}, u32[]{:S(2)}, u32[]{:S(2)}) collective-permute-start(bf16[1024,256]{1,0:T(8,128)(2,1)S(1)} %bitcast.43), channel_id=1, source_target_pairs={{0,2},{1,3},{2,0},{3,1},{4,6},{5,7},{6,4},{7,5},{8,10},{9,11},{10,... | collective-permute-start | bytes 1572872 | tf_op jit(solution)/shard_map/ppermute | solution.py:465
  11.0 1.4 %copy.17 = bf16[16,128,128]{1,2,0:T(8,128)(2,1)S(1)} copy(bf16[16,128,128]{2,1,0:T(8,128)(2,1)} %param.18) | data formatting | bytes 1048576 | tf_op args[7]
  14.2 7.3 %short_range.2.refs_1_ = f32[2,256,2048]{2,1,0:T(8,128)} custom-call(s32[1]{0:T(128)} %bitcast.1.half_ref, s32[16]{0:T(128)S(1)} %compare_convert_fusion.1.live_ref, s32[16]{0:T(128)S(1)} %copy-done.1, f32[3,16]{1,0:T(4,128)S(1)} %pad_maximum_fusion.1.meta_ref, bf16[128,4096]{1,0:T(8,128)(2,1)} %basis_ref.3, f32[1,4096]{1,0:T(1,128)S(1)} %bitcast.39, ...), custom_call_target="tpu_custom_call" | custom-call | flops 2147483648 | bytes 1 | tf_op jit(solution)/shard_map/short_range/pallas_call | solution.py:141
  21.5 8.0 %collective-permute-done.1 = bf16[256,1024]{1,0:T(8,128)(2,1)S(1)} collective-permute-done((bf16[256,1024]{1,0:T(8,128)(2,1)S(1)}, bf16[256,1024]{1,0:T(8,128)(2,1)S(1)}, u32[]{:S(2)}, u32[]{:S(2)}) %collective-permute-start.1) | collective-permute-done | bytes 524320 | tf_op jit(solution)/shard_map/ppermute | solution.py:465
  30.2 1.6 %collective-permute-start.6 = (bf16[256,1024]{1,0:T(8,128)(2,1)S(1)}, bf16[256,1024]{1,0:T(8,128)(2,1)S(1)}, u32[]{:S(2)}, u32[]{:S(2)}) collective-permute-start(bf16[256,1024]{1,0:T(8,128)(2,1)S(1)} %select_select_fusion.3), channel_id=1, source_target_pairs={{0,16},{1,17},{2,18},{3,19},{4,20},{5,21},{6,22},{7,23},{8,24},{9,... | collective-permute-start | bytes 1572872 | tf_op jit(solution)/shard_map/ppermute | solution.py:465
  31.8 1.5 %collective-permute-start.7 = (bf16[1024,256]{1,0:T(8,128)(2,1)}, bf16[1024,256]{1,0:T(8,128)(2,1)S(1)}, u32[]{:S(2)}, u32[]{:S(2)}) collective-permute-start(bf16[1024,256]{1,0:T(8,128)(2,1)} %collective-permute-done.4.refs_5_), channel_id=1, source_target_pairs={{0,2},{1,3},{2,0},{3,1},{4,6},{5,7},{6,4},{7,5},{8,10},{9,11},{10,... | collective-permute-start | bytes 1572872 | tf_op jit(solution)/shard_map/ppermute | solution.py:465
  35.4 5.7 %short_range.3.refs_6_.refs_8_.refs_1_ = f32[2048,512]{1,0:T(8,128)} custom-call(s32[1]{0:T(128)} %bitcast.1.half_ref, s32[16]{0:T(128)S(1)} %get-tuple-element.57.live_ref, s32[16]{0:T(128)S(1)} %get-tuple-element.56.sub_ref, f32[3,16]{1,0:T(4,128)S(1)} %pad_maximum_fusion.2.meta_ref, bf16[128,4096]{1,0:T(8,128)(2,1)} %basis_ref.3, f32[1,4096]{1,0:T(1,128)S(1)} %bitcast.40, ...), custom_call_target="tpu_custom_call" | custom-call | flops 2147483648 | bytes 1 | tf_op jit(solution)/shard_map/short_range/pallas_call | solution.py:141
  41.1 2.4 %collective-permute-done.2 = bf16[256,1024]{1,0:T(8,128)(2,1)S(1)} collective-permute-done((bf16[256,1024]{1,0:T(8,128)(2,1)}, bf16[256,1024]{1,0:T(8,128)(2,1)S(1)}, u32[]{:S(2)}, u32[]{:S(2)}) %collective-permute-start.2) | collective-permute-done | bytes 524320 | tf_op jit(solution)/shard_map/ppermute | solution.py:465
  44.9 1.4 %long_range.4 = bf16[256,512]{1,0:T(8,128)(2,1)} custom-call(bf16[256,1024]{1,0:T(8,128)(2,1)S(1)} %select_select_fusion.1.refs_0_, bf16[256,1024]{1,0:T(8,128)(2,1)S(1)} %collective-permute-done.6.refs_1_, bf16[1024,256]{1,0:T(8,128)(2,1)S(1)} %collective-permute-done.5.refs_2_, bf16[1024,256]{1,0:T(8,128)(2,1)S(1)} %collective-permute-done.7.refs_3_), custom_call_target="tpu_custom_call" | custom-call | flops 1 | bytes 1 | tf_op jit(solution)/shard_map/long_range/pallas_call | solution.py:221
  47.1 1.9 %select_select_fusion.2 = bf16[256,1024]{1,0:T(8,128)(2,1)} fusion(bf16[256,1024]{1,0:T(8,128)(2,1)} %collective-permute-done, bf16[256,1024]{1,0:T(8,128)(2,1)} %copy-done.7, bf16[256,1024]{1,0:T(8,128)(2,1)S(1)} %copy-done.3, pred[]{:T(512)S(6)} %eq.80, pred[]{:T(512)S(6)} %eq.73), kind=kLoop, calls=%fused_computation.6 | loop fusion | flops 524288 | bytes 2097154 | tf_op jit(solution)/shard_map/jit(_where)/select_n | solution.py:499
  49.4 1.6 %collective-permute-start.15 = (bf16[256,512]{1,0:T(8,128)(2,1)}, bf16[256,512]{1,0:T(8,128)(2,1)S(1)}, u32[]{:S(2)}, u32[]{:S(2)}) collective-permute-start(bf16[256,512]{1,0:T(8,128)(2,1)} %long_range.4), channel_id=1, source_target_pairs={{0,2},{1,3},{2,0},{3,1},{4,6},{5,7},{6,4},{7,5},{8,10},{9,11},{10,... | collective-permute-start | bytes 786440 | tf_op jit(solution)/shard_map/ppermute | solution.py:465
  51.0 2.5 %long_range.5 = bf16[256,512]{1,0:T(8,128)(2,1)} custom-call(bf16[256,1024]{1,0:T(8,128)(2,1)S(1)} %collective-permute-done.8.refs_0_.refs_2_, bf16[256,1024]{1,0:T(8,128)(2,1)} %collective-permute-done.9.refs_1_.refs_3_, bf16[1024,256]{1,0:T(8,128)(2,1)S(1)} %collective-permute-done.5.refs_2_, bf16[1024,256]{1,0:T(8,128)(2,1)S(1)} %collective-permute-done.7.refs_3_), custom_call_target="tpu_custom_call" | custom-call | flops 1 | bytes 1 | tf_op jit(solution)/shard_map/long_range/pallas_call | solution.py:221
  54.0 5.0 %own_sum.2.refs_9_ = bf16[2048,2,256]{2,1,0:T(2,128)(2,1)} custom-call(s32[2]{0:T(128)S(1)} %pad_add_fusion.1.order_ref, bf16[256,1024]{1,0:T(8,128)(2,1)S(1)} %select_select_fusion.1.refs_0_, bf16[256,1024]{1,0:T(8,128)(2,1)S(1)} %collective-permute-done.6.refs_1_, bf16[256,1024]{1,0:T(8,128)(2,1)S(1)} %collective-permute-done.8.refs_0_.refs_2_, ...), custom_call_target="tpu_custom_call" | custom-call | flops 1 | bytes 1 | tf_op jit(solution)/shard_map/own_sum/pallas_call | solution.py:289
  60.2 2.9 %collective-permute-done.11.refs_1_ = bf16[256,1024]{1,0:T(8,128)(2,1)S(1)} collective-permute-done((bf16[256,1024]{1,0:T(8,128)(2,1)}, bf16[256,1024]{1,0:T(8,128)(2,1)S(1)}, u32[]{:S(2)}, u32[]{:S(2)}) %collective-permute-start.11) | collective-permute-done | bytes 524320 | tf_op jit(solution)/shard_map/ppermute | solution.py:465
  63.3 1.4 %long_range.7 = bf16[256,512]{1,0:T(8,128)(2,1)} custom-call(bf16[256,1024]{1,0:T(8,128)(2,1)S(1)} %select_select_fusion.refs_0_, bf16[256,1024]{1,0:T(8,128)(2,1)S(1)} %collective-permute-done.11.refs_1_, bf16[1024,512]{1,0:T(8,128)(2,1)S(1)} %get-tuple-element.64.refs_2_, bf16[1024,512]{1,0:T(8,128)(2,1)S(1)} %get-tuple-element.65.refs_3_), custom_call_target="tpu_custom_call" | custom-call | flops 1 | bytes 1 | tf_op jit(solution)/shard_map/long_range/pallas_call | solution.py:221
  64.8 1.4 %collective-permute-start.14 = (bf16[256,512]{1,0:T(8,128)(2,1)}, bf16[256,512]{1,0:T(8,128)(2,1)S(1)}, u32[]{:S(2)}, u32[]{:S(2)}) collective-permute-start(bf16[256,512]{1,0:T(8,128)(2,1)} %long_range.7), channel_id=1, source_target_pairs={{0,2},{1,3},{2,0},{3,1},{4,6},{5,7},{6,4},{7,5},{8,10},{9,11},{10,... | collective-permute-start | bytes 786440 | tf_op jit(solution)/shard_map/ppermute | solution.py:465
  66.2 1.4 %long_range.6 = bf16[256,512]{1,0:T(8,128)(2,1)} custom-call(bf16[256,1024]{1,0:T(8,128)(2,1)S(1)} %collective-permute-done.10.refs_0_.refs_2_, bf16[256,1024]{1,0:T(8,128)(2,1)S(1)} %collective-permute-done.12.refs_1_.refs_3_, bf16[1024,512]{1,0:T(8,128)(2,1)S(1)} %get-tuple-element.64.refs_2_, bf16[1024,512]{1,0:T(8,128)(2,1)S(1)} %get-tuple-element.65.refs_3_), custom_call_target="tpu_custom_call" | custom-call | flops 1 | bytes 1 | tf_op jit(solution)/shard_map/long_range/pallas_call | solution.py:221
  68.5 5.8 %own_sum.3.refs_2_ = bf16[2048,2,256]{2,1,0:T(2,128)(2,1)} custom-call(s32[4]{0:T(128)S(1)} %pad_add_fusion.2.order_ref, bf16[256,1024]{1,0:T(8,128)(2,1)S(1)} %select_select_fusion.refs_0_, bf16[256,1024]{1,0:T(8,128)(2,1)S(1)} %collective-permute-done.11.refs_1_, ...), custom_call_target="tpu_custom_call", output_to_operand_aliasing={{}: (10, {})} | custom-call | flops 1 | bytes 1 | tf_op jit(solution)/shard_map/own_sum/pallas_call | solution.py:289
  74.3 2.0 %final_sum.2.refs_2_ = bf16[2048,2,256]{2,1,0:T(2,128)(2,1)} custom-call(s32[1]{0:T(128)} %bitcast.22.order_ref, bf16[256,512]{1,0:T(8,128)(2,1)S(1)} %collective-permute-done.14.refs_0_, f32[2048,512]{1,0:T(8,128)} %short_range.3.refs_6_.refs_8_.refs_1_, bf16[2048,2,256]{2,1,0:T(2,128)(2,1)} %own_sum.3.refs_2_), custom_call_target="tpu_custom_call", output_to_operand_aliasing={{}: (3, {})} | custom-call | flops 1 | bytes 1 | tf_op jit(solution)/shard_map/final_sum/pallas_call | solution.py:344
  76.3 3.1 %collective-permute-done.13.refs_0_ = bf16[256,512]{1,0:T(8,128)(2,1)S(1)} collective-permute-done((bf16[256,512]{1,0:T(8,128)(2,1)}, bf16[256,512]{1,0:T(8,128)(2,1)S(1)}, u32[]{:S(2)}, u32[]{:S(2)}) %collective-permute-start.13) | collective-permute-done | bytes 262176 | tf_op jit(solution)/shard_map/ppermute | solution.py:465
  79.4 2.0 %final_sum.3 = bf16[2048,2,256]{2,1,0:T(2,128)(2,1)} custom-call(s32[1]{0:T(128)} %bitcast.order_ref, bf16[256,512]{1,0:T(8,128)(2,1)S(1)} %collective-permute-done.13.refs_0_, f32[2048,512]{1,0:T(8,128)} %short_range.3.refs_6_.refs_8_.refs_1_, bf16[2048,2,256]{2,1,0:T(2,128)(2,1)} %final_sum.2.refs_2_), custom_call_target="tpu_custom_call", output_to_operand_aliasing={{}: (3, {})} | custom-call | flops 1 | bytes 1 | tf_op jit(solution)/shard_map/final_sum/pallas_call | solution.py:344
  (71 shorter events, 11.5 us)
Async XLA Ops:
  0.0 12.4 %copy-start.1 = (s32[16]{0:T(128)S(1)}, s32[16]{0:T(128)}, u32[]{:S(2)}) copy-start(s32[16]{0:T(128)} %sub_ref.1) | copy-start | bytes 196
  0.0 12.4 %copy-start.9 = (s32[16]{0:T(128)S(1)}, s32[16]{0:T(128)}, u32[]{:S(2)}) copy-start(s32[16]{0:T(128)} %param.19) | copy-start | bytes 196
  1.1 29.0 %copy-start.6 = (bf16[32,8,2,512]{3,1,2,0:T(8,128)(2,1)}, bf16[32,8,2,512]{3,1,2,0:T(8,128)(2,1)S(1)}, u32[]{:S(2)}) copy-start(bf16[32,8,2,512]{3,1,2,0:T(8,128)(2,1)S(1)} %copy.19) | copy-start | bytes 1572868
  1.2 12.7 %copy-start.10 = (f32[125]{0:T(128)S(1)}, f32[125]{0:T(128)}, u32[]{:S(2)}) copy-start(f32[125]{0:T(128)} %param.16) | copy-start | bytes 1504
  1.2 12.7 %copy-start.11 = (f32[125]{0:T(128)S(1)}, f32[125]{0:T(128)}, u32[]{:S(2)}) copy-start(f32[125]{0:T(128)} %param.17) | copy-start | bytes 1504
  1.2 13.0 %copy-start = (f32[4096]{0:T(1024)S(1)}, f32[4096]{0:T(1024)}, u32[]{:S(2)}) copy-start(f32[4096]{0:T(1024)} %param.15) | copy-start | bytes 49156
  1.2 20.3 %collective-permute-start = (bf16[256,1024]{1,0:T(8,128)(2,1)S(1)}, bf16[256,1024]{1,0:T(8,128)(2,1)}, u32[]{:S(2)}, u32[]{:S(2)}) collective-permute-start(bf16[256,1024]{1,0:T(8,128)(2,1)S(1)} %bitcast.46), channel_id=1, source_target_pairs={{0,8},{1,9},{2,10},{3,11},{4,0},{5,1},{6,2},{7,3},{8,12},{9,13},{1... | collective-permute-start | bytes 1572872 | tf_op jit(solution)/shard_map/ppermute | solution.py:465
  5.3 24.2 %collective-permute-start.1 = (bf16[256,1024]{1,0:T(8,128)(2,1)S(1)}, bf16[256,1024]{1,0:T(8,128)(2,1)S(1)}, u32[]{:S(2)}, u32[]{:S(2)}) collective-permute-start(bf16[256,1024]{1,0:T(8,128)(2,1)S(1)} %bitcast.47), channel_id=1, source_target_pairs={{0,4},{1,5},{2,6},{3,7},{4,12},{5,13},{6,14},{7,15},{8,0},{9,1},{1... | collective-permute-start | bytes 1572872 | tf_op jit(solution)/shard_map/ppermute | solution.py:465
  7.3 14.1 %copy-start.5 = (bf16[256,2,512]{0,2,1:T(8,128)(2,1)}, bf16[256,2,512]{0,2,1:T(8,128)(2,1)S(1)}, u32[]{:S(2)}) copy-start(bf16[256,2,512]{0,2,1:T(8,128)(2,1)S(1)} %copy.18) | copy-start | bytes 1572868
  7.3 24.5 %collective-permute-start.4 = (bf16[1024,256]{1,0:T(8,128)(2,1)S(1)}, bf16[1024,256]{1,0:T(8,128)(2,1)}, u32[]{:S(2)}, u32[]{:S(2)}) collective-permute-start(bf16[1024,256]{1,0:T(8,128)(2,1)S(1)} %bitcast.42), channel_id=1, source_target_pairs={{0,16},{1,17},{2,18},{3,19},{4,20},{5,21},{6,22},{7,23},{8,24},{9,... | collective-permute-start | bytes 1572872 | tf_op jit(solution)/shard_map/ppermute | solution.py:465
  8.9 22.9 %collective-permute-start.5 = (bf16[1024,256]{1,0:T(8,128)(2,1)S(1)}, bf16[1024,256]{1,0:T(8,128)(2,1)S(1)}, u32[]{:S(2)}, u32[]{:S(2)}) collective-permute-start(bf16[1024,256]{1,0:T(8,128)(2,1)S(1)} %bitcast.43), channel_id=1, source_target_pairs={{0,2},{1,3},{2,0},{3,1},{4,6},{5,7},{6,4},{7,5},{8,10},{9,11},{10,... | collective-permute-start | bytes 1572872 | tf_op jit(solution)/shard_map/ppermute | solution.py:465
  13.3 21.2 %collective-permute-start.3 = (bf16[17,128,128]{2,1,0:T(8,128)(2,1)}, bf16[17,128,128]{2,1,0:T(8,128)(2,1)}, u32[]{:S(2)}, u32[]{:S(2)}) collective-permute-start(bf16[17,128,128]{2,1,0:T(8,128)(2,1)} %pad_maximum_fusion.refs_0_), channel_id=1, source_target_pairs={{0,16},{1,17},{2,18},{3,19},{4,20},{5,21},{6,22},{7,23},{8,24},{9,... | collective-permute-start | bytes 1671176 | tf_op jit(solution)/shard_map/ppermute | solution.py:465
  29.5 14.1 %collective-permute-start.2 = (bf16[256,1024]{1,0:T(8,128)(2,1)}, bf16[256,1024]{1,0:T(8,128)(2,1)S(1)}, u32[]{:S(2)}, u32[]{:S(2)}) collective-permute-start(bf16[256,1024]{1,0:T(8,128)(2,1)} %collective-permute-done), channel_id=1, source_target_pairs={{0,8},{1,9},{2,10},{3,11},{4,0},{5,1},{6,2},{7,3},{8,12},{9,13},{1... | collective-permute-start | bytes 1572872 | tf_op jit(solution)/shard_map/ppermute | solution.py:465
  30.2 13.7 %collective-permute-start.6 = (bf16[256,1024]{1,0:T(8,128)(2,1)S(1)}, bf16[256,1024]{1,0:T(8,128)(2,1)S(1)}, u32[]{:S(2)}, u32[]{:S(2)}) collective-permute-start(bf16[256,1024]{1,0:T(8,128)(2,1)S(1)} %select_select_fusion.3), channel_id=1, source_target_pairs={{0,16},{1,17},{2,18},{3,19},{4,20},{5,21},{6,22},{7,23},{8,24},{9,... | collective-permute-start | bytes 1572872 | tf_op jit(solution)/shard_map/ppermute | solution.py:465
  31.8 13.2 %collective-permute-start.7 = (bf16[1024,256]{1,0:T(8,128)(2,1)}, bf16[1024,256]{1,0:T(8,128)(2,1)S(1)}, u32[]{:S(2)}, u32[]{:S(2)}) collective-permute-start(bf16[1024,256]{1,0:T(8,128)(2,1)} %collective-permute-done.4.refs_5_), channel_id=1, source_target_pairs={{0,2},{1,3},{2,0},{3,1},{4,6},{5,7},{6,4},{7,5},{8,10},{9,11},{10,... | collective-permute-start | bytes 1572872 | tf_op jit(solution)/shard_map/ppermute | solution.py:465
  34.4 16.6 %collective-permute-start.8 = (bf16[256,1024]{1,0:T(8,128)(2,1)S(1)}, bf16[256,1024]{1,0:T(8,128)(2,1)S(1)}, u32[]{:S(2)}, u32[]{:S(2)}) collective-permute-start(bf16[256,1024]{1,0:T(8,128)(2,1)S(1)} %select_select_fusion.1.refs_0_), channel_id=1, source_target_pairs={{0,1},{1,0},{2,3},{3,2},{4,5},{5,4},{6,7},{7,6},{8,9},{9,8},{10,11... | collective-permute-start | bytes 1572872 | tf_op jit(solution)/shard_map/ppermute | solution.py:465
  46.4 4.7 %collective-permute-start.9 = (bf16[256,1024]{1,0:T(8,128)(2,1)S(1)}, bf16[256,1024]{1,0:T(8,128)(2,1)}, u32[]{:S(2)}, u32[]{:S(2)}) collective-permute-start(bf16[256,1024]{1,0:T(8,128)(2,1)S(1)} %collective-permute-done.6.refs_1_), channel_id=1, source_target_pairs={{0,1},{1,0},{2,3},{3,2},{4,5},{5,4},{6,7},{7,6},{8,9},{9,8},{10,11... | collective-permute-start | bytes 1572872 | tf_op jit(solution)/shard_map/ppermute | solution.py:465
  49.0 14.1 %collective-permute-start.11 = (bf16[256,1024]{1,0:T(8,128)(2,1)}, bf16[256,1024]{1,0:T(8,128)(2,1)S(1)}, u32[]{:S(2)}, u32[]{:S(2)}) collective-permute-start(bf16[256,1024]{1,0:T(8,128)(2,1)} %select_select_fusion.2), channel_id=1, source_target_pairs={{0,16},{1,17},{2,18},{3,19},{4,20},{5,21},{6,22},{7,23},{8,24},{9,... | collective-permute-start | bytes 1572872 | tf_op jit(solution)/shard_map/ppermute | solution.py:465
  49.4 19.1 %collective-permute-start.15 = (bf16[256,512]{1,0:T(8,128)(2,1)}, bf16[256,512]{1,0:T(8,128)(2,1)S(1)}, u32[]{:S(2)}, u32[]{:S(2)}) collective-permute-start(bf16[256,512]{1,0:T(8,128)(2,1)} %long_range.4), channel_id=1, source_target_pairs={{0,2},{1,3},{2,0},{3,1},{4,6},{5,7},{6,4},{7,5},{8,10},{9,11},{10,... | collective-permute-start | bytes 786440 | tf_op jit(solution)/shard_map/ppermute | solution.py:465
  53.5 15.0 %collective-permute-start.16 = (bf16[256,512]{1,0:T(8,128)(2,1)}, bf16[256,512]{1,0:T(8,128)(2,1)}, u32[]{:S(2)}, u32[]{:S(2)}) collective-permute-start(bf16[256,512]{1,0:T(8,128)(2,1)} %long_range.5), channel_id=1, source_target_pairs={{0,2},{1,3},{2,0},{3,1},{4,6},{5,7},{6,4},{7,5},{8,10},{9,11},{10,... | collective-permute-start | bytes 786440 | tf_op jit(solution)/shard_map/ppermute | solution.py:465
  60.1 6.1 %collective-permute-start.10 = (bf16[256,1024]{1,0:T(8,128)(2,1)S(1)}, bf16[256,1024]{1,0:T(8,128)(2,1)S(1)}, u32[]{:S(2)}, u32[]{:S(2)}) collective-permute-start(bf16[256,1024]{1,0:T(8,128)(2,1)S(1)} %select_select_fusion.refs_0_), channel_id=1, source_target_pairs={{0,1},{1,0},{2,3},{3,2},{4,5},{5,4},{6,7},{7,6},{8,9},{9,8},{10,11... | collective-permute-start | bytes 1572872 | tf_op jit(solution)/shard_map/ppermute | solution.py:465
  63.1 3.1 %collective-permute-start.12 = (bf16[256,1024]{1,0:T(8,128)(2,1)S(1)}, bf16[256,1024]{1,0:T(8,128)(2,1)S(1)}, u32[]{:S(2)}, u32[]{:S(2)}) collective-permute-start(bf16[256,1024]{1,0:T(8,128)(2,1)S(1)} %collective-permute-done.11.refs_1_), channel_id=1, source_target_pairs={{0,1},{1,0},{2,3},{3,2},{4,5},{5,4},{6,7},{7,6},{8,9},{9,8},{10,11... | collective-permute-start | bytes 1572872 | tf_op jit(solution)/shard_map/ppermute | solution.py:465
  64.8 9.5 %collective-permute-start.14 = (bf16[256,512]{1,0:T(8,128)(2,1)}, bf16[256,512]{1,0:T(8,128)(2,1)S(1)}, u32[]{:S(2)}, u32[]{:S(2)}) collective-permute-start(bf16[256,512]{1,0:T(8,128)(2,1)} %long_range.7), channel_id=1, source_target_pairs={{0,2},{1,3},{2,0},{3,1},{4,6},{5,7},{6,4},{7,5},{8,10},{9,11},{10,... | collective-permute-start | bytes 786440 | tf_op jit(solution)/shard_map/ppermute | solution.py:465
  67.6 11.8 %collective-permute-start.13 = (bf16[256,512]{1,0:T(8,128)(2,1)}, bf16[256,512]{1,0:T(8,128)(2,1)S(1)}, u32[]{:S(2)}, u32[]{:S(2)}) collective-permute-start(bf16[256,512]{1,0:T(8,128)(2,1)} %long_range.6), channel_id=1, source_target_pairs={{0,2},{1,3},{2,0},{3,1},{4,6},{5,7},{6,4},{7,5},{8,10},{9,11},{10,... | collective-permute-start | bytes 786440 | tf_op jit(solution)/shard_map/ppermute | solution.py:465
  (5 other events, 22.1 us)
